TPU v7x, 32 devices: a whole 2x2x4 slice. The times are simulated.
32 devices in a mesh: tm: 16 (over z, y, core), plane: 2 (over x).
Axes of the slice: x: 2, y: 2, z: 4, core: 2. Of those that a mesh axis runs over, the one named last changes fastest.
Arguments:
- frames: bfloat16 [32, 2, 512, 1024], P('tm', 'plane'), may hold values from -6 to 6
- template: bfloat16 [32, 2, 128, 128], P('tm', 'plane'), may hold values from -6 to 6
- shift_codes: int32 [32, 2, 32], P('tm'), may hold values from -128 to 127
Outputs:
- correlation: float32 [32, 32, 256], P('tm', 'plane')
- new_template: float32 [32, 2, 128, 128], P('tm', 'plane')
Inputs may be any that keep to these rules, and one draw needn't show every extreme that they name: shift_codes is 16 times the shift in pixels, its integer part at most 8 pixels either way; every plane of a volume shares it.
All inputs are finite; a program needn't handle non-finite values.
Results may differ from a plain program's by a relative error of at most 0.0065.
Values may be sent and summed in bfloat16 or wider, within the bound.
No kernel may reach another device: no remote copies, remote signals or barrier semaphores. Data moves between devices by JAX's collectives and lax.ppermute only.
A program may use at most 128 MiB of HBM per device.

v0:
```python
import functools
import math

import jax
import jax.numpy as jnp
import numpy as np
from jax import lax
from jax.experimental import pallas as pl
from jax.experimental.pallas import tpu as pltpu
from jax.sharding import PartitionSpec as P

SHIFT = 8
WIN = 16
TAPS = 8
SUB = 16
EDGE = 16
LANES = 128
MIB = 1024 * 1024

full_turn = 2.0 * math.pi


def dft_constants(block_size):
    positions = np.arange(block_size)
    angles = full_turn * (np.outer(positions, positions) % block_size) / block_size
    cosine = np.cos(angles)
    sine = -np.sin(angles)
    half = block_size // 2 + 1
    rows = -(-half // 8) * 8
    row_table = np.concatenate([cosine, sine], axis=1)
    col_table = np.zeros((2 * rows, 2 * block_size))
    col_table[:half] = np.concatenate([cosine[:half], -sine[:half]], axis=1)
    col_table[rows : rows + half] = np.concatenate([sine[:half], cosine[:half]], axis=1)
    weights = np.zeros((rows,))
    weights[:half] = 2.0
    weights[0] = weights[half - 1] = 1.0
    starts = 2 * SHIFT
    lag_table = np.zeros((starts, 2 * WIN, 2 * rows))
    for start in range(starts):
        lags = start - SHIFT - WIN // 2 + np.arange(WIN)
        turns = full_turn * (np.outer(lags, positions[:half]) % block_size) / block_size
        lag_cos = np.cos(turns) * weights[:half]
        lag_sin = np.sin(turns) * weights[:half]
        lag_table[start, :WIN, :half] = lag_cos
        lag_table[start, :WIN, rows : rows + half] = -lag_sin
        lag_table[start, WIN:, :half] = lag_sin
        lag_table[start, WIN:, rows : rows + half] = lag_cos
    span = starts + WIN
    lags = np.arange(span) - SHIFT - WIN // 2
    turns = full_turn * (np.outer(positions, lags) % block_size) / block_size
    span_table = np.zeros((2 * block_size, LANES))
    span_table[:block_size, :span] = np.cos(turns)
    span_table[block_size:, :span] = -np.sin(turns)
    return tuple(
        jnp.asarray(table, jnp.bfloat16) for table in (row_table, col_table, lag_table, span_table)
    ) + (jnp.asarray(np.broadcast_to(weights[:, None], (rows, LANES)), jnp.float32),)


def tap_constants(width):
    offsets = np.arange(TAPS) - (TAPS // 2 - 1)
    spots = offsets[None, :] - np.arange(SUB)[:, None] / SUB
    raw_taps = np.sinc(spots) * np.sinc(spots / (TAPS // 2))
    taps = raw_taps / raw_taps.sum(axis=-1, keepdims=True)
    table = np.zeros((SUB, EDGE, width))
    for row in range(EDGE):
        table[:, row, row : row + TAPS] = taps
    return jnp.asarray(table, jnp.float32)


def band_matrix(head, start, size):
    width = head.shape[1]
    head = pltpu.roll(head, start, 1).astype(jnp.bfloat16)
    groups = [head]
    for step in range(EDGE, size, EDGE):
        groups.append(jnp.concatenate([head[:, width - step :], head[:, : width - step]], axis=1))
    return jnp.concatenate(groups, axis=0)


def warp_kernel(vols, down, across, block, codes_ref, taps_ref, frames_ref, out_ref, padded, sems):
    rows, cols = down * block, across * block
    copies = [
        pltpu.make_async_copy(
            frames_ref.at[v],
            padded.at[v, pl.ds(EDGE, rows), pl.ds(block, cols)],
            sems.at[v],
        )
        for v in range(vols)
    ]
    for copy in copies:
        copy.start()
    zero_rows = jnp.zeros((EDGE, cols + 2 * block), jnp.bfloat16)
    zero_cols = jnp.zeros((rows, block), jnp.bfloat16)
    for v in range(vols):
        padded[v, :EDGE, :] = zero_rows
        padded[v, EDGE + rows :, :] = zero_rows
        padded[v, EDGE : EDGE + rows, :block] = zero_cols
        padded[v, EDGE : EDGE + rows, block + cols :] = zero_cols
    for copy in copies:
        copy.wait()
    tall = block + 2 * EDGE
    lane = lax.broadcasted_iota(jnp.int32, (tall, block), 1)
    width = 2 * block
    before = TAPS // 2 - 1

    def one_block(index, _):
        row = pl.multiple_of((index // across) * block, block)
        col = pl.multiple_of((index % across) * block, block)
        total = jnp.zeros((block, block), jnp.float32)
        for v in range(vols):
            row_code = codes_ref[v, 0, index]
            col_code = codes_ref[v, 1, index]
            row_start = (row_code >> 4) + (EDGE - before)
            col_start = (col_code >> 4) + (width - before)
            row_band = band_matrix(taps_ref[row_code & (SUB - 1)], row_start, block)
            col_band = band_matrix(taps_ref[col_code & (SUB - 1)], col_start, block)
            left = padded[v, pl.ds(row, tall), pl.ds(col, block)]
            middle = padded[v, pl.ds(row, tall), pl.ds(col + block, block)]
            right = padded[v, pl.ds(row, tall), pl.ds(col + 2 * block, block)]
            sides = jnp.where(lane < block // 2, right, left)
            region = jnp.concatenate([middle, sides], axis=1)
            partial = lax.dot_general(
                region,
                col_band,
                (((1,), (1,)), ((), ())),
                preferred_element_type=jnp.float32,
            ).astype(jnp.bfloat16)
            total += jnp.dot(row_band[:, :tall], partial, preferred_element_type=jnp.float32)
        out_ref[index] = total.astype(jnp.bfloat16)
        return 0

    lax.fori_loop(0, down * across, one_block, 0, unroll=2)


def warp_sums(frames, codes, block):
    vols, rows, cols = frames.shape
    down, across = rows // block, cols // block
    taps = tap_constants(2 * block)
    return pl.pallas_call(
        functools.partial(warp_kernel, vols, down, across, block),
        out_shape=jax.ShapeDtypeStruct((down * across, block, block), jnp.bfloat16),
        in_specs=[
            pl.BlockSpec(memory_space=pltpu.SMEM),
            pl.BlockSpec(memory_space=pltpu.VMEM),
            pl.BlockSpec(memory_space=pl.ANY),
        ],
        out_specs=pl.BlockSpec(memory_space=pltpu.VMEM),
        scratch_shapes=[
            pltpu.VMEM((vols, rows + 2 * EDGE, cols + 2 * block), jnp.bfloat16),
            pltpu.SemaphoreType.DMA((vols,)),
        ],
        compiler_params=pltpu.CompilerParams(vmem_limit_bytes=32 * MIB),
        cost_estimate=pl.CostEstimate(
            flops=2 * vols * rows * cols * block * 4,
            bytes_accessed=vols * rows * cols * 2 + rows * cols * 2,
            transcendentals=0,
        ),
        name="warp",
    )(codes, taps, frames)


def spectrum_kernel(
    vols,
    across,
    block,
    codes_ref,
    row_ref,
    col_ref,
    lag_ref,
    span_ref,
    weight_ref,
    frames_ref,
    template_ref,
    out_ref,
    found,
):
    band = pl.program_id(0)
    half = weight_ref.shape[0]
    row_table = row_ref[...]
    col_table = col_ref[...]
    span_table = span_ref[...]
    weights = weight_ref[...]
    count = vols + 1

    def one_pair(pair, _):
        col = pl.multiple_of(pair * 2 * block, 2 * block)
        parts = [template_ref[2 * pair], template_ref[2 * pair + 1]]
        for v in range(vols):
            both = frames_ref[v, :, pl.ds(col, 2 * block)]
            parts += [both[:, :block], both[:, block:]]
        rows = jnp.dot(
            jnp.concatenate(parts, axis=0), row_table, preferred_element_type=jnp.float32
        ).astype(jnp.bfloat16)
        spectra = []
        for at in range(count):
            stacks = []
            for side in range(2):
                one = rows[(2 * at + side) * block : (2 * at + side + 1) * block]
                stacks.append(jnp.concatenate([one[:, :block], one[:, block:]], axis=0))
            spectra.append(
                jnp.dot(
                    col_table,
                    jnp.concatenate(stacks, axis=1),
                    preferred_element_type=jnp.float32,
                )
            )
        temp = spectra[0].astype(jnp.bfloat16).astype(jnp.float32)
        lag_sums = []
        for v in range(vols):
            for side in range(2):
                lanes = slice(side * block, (side + 1) * block)
                temp_real, temp_imag = temp[:half, lanes], temp[half:, lanes]
                real, imag = spectra[v + 1][:half, lanes], spectra[v + 1][half:, lanes]
                cross_real = real * temp_real + imag * temp_imag
                cross_imag = imag * temp_real - real * temp_imag
                power = cross_real * cross_real + cross_imag * cross_imag
                magnitude = power * lax.rsqrt(jnp.maximum(power, 1e-36))
                mean = jnp.sum(magnitude * weights) * (1.0 / (block * block)) + 1e-06
                scale = 1.0 / (magnitude + mean)
                norm = jnp.concatenate(
                    [
                        (cross_real * scale).astype(jnp.bfloat16),
                        (cross_imag * scale).astype(jnp.bfloat16),
                    ],
                    axis=0,
                )
                index = band * across + 2 * pair + side
                row_shift = codes_ref[v, 0, index] >> 4
                lag_rows = jnp.dot(
                    lag_ref[row_shift + SHIFT], norm, preferred_element_type=jnp.float32
                ).astype(jnp.bfloat16)
                lag_sums.append(jnp.concatenate([lag_rows[:WIN], lag_rows[WIN:]], axis=1))
        lags = jnp.dot(
            jnp.concatenate(lag_sums, axis=0), span_table, preferred_element_type=jnp.float32
        )
        for v in range(vols):
            for side in range(2):
                index = band * across + 2 * pair + side
                col_shift = codes_ref[v, 1, index] >> 4
                at = 2 * v + side
                one = lags[at * WIN : (at + 1) * WIN]
                one = pltpu.roll(one, LANES - SHIFT - col_shift, 1)
                start = pl.multiple_of((2 * pair + side) * WIN, WIN)
                found[v, pl.ds(start, WIN), :] = one
        return 0

    lax.fori_loop(0, across // 2, one_pair, 0)

    per_tile = LANES // WIN
    lane = lax.broadcasted_iota(jnp.int32, (across, LANES), 1) // WIN
    for v in range(vols):
        for tile in range(WIN // per_tile):
            total = jnp.zeros((across, LANES), jnp.float32)
            for part in range(per_tile):
                one = found[v, pl.ds(tile * per_tile + part, across, stride=WIN), :]
                if part:
                    one = pltpu.roll(one, part * WIN, 1)
                total = jnp.where(lane == part, one, total)
            out_ref[v, :, tile * LANES : (tile + 1) * LANES] = total * (1.0 / block)


def lag_windows(frames, template, codes):
    vols, rows, cols = frames.shape
    block = template.shape[-1]
    down, across = rows // block, cols // block
    tables = dft_constants(block)
    whole = [
        pl.BlockSpec(table.shape, functools.partial(lambda dims, band: (0,) * dims, table.ndim))
        for table in tables
    ]
    return pl.pallas_call(
        functools.partial(spectrum_kernel, vols, across, block),
        grid=(down,),
        out_shape=jax.ShapeDtypeStruct((vols, down * across, WIN * WIN), jnp.float32),
        in_specs=[
            pl.BlockSpec(memory_space=pltpu.SMEM),
            *whole,
            pl.BlockSpec((vols, block, cols), lambda band: (0, band, 0)),
            pl.BlockSpec((across, block, block), lambda band: (band, 0, 0)),
        ],
        out_specs=pl.BlockSpec((vols, across, WIN * WIN), lambda band: (0, band, 0)),
        scratch_shapes=[pltpu.VMEM((vols, across * WIN, LANES), jnp.float32)],
        compiler_params=pltpu.CompilerParams(vmem_limit_bytes=32 * MIB),
        cost_estimate=pl.CostEstimate(
            flops=2 * 3 * rows * cols * block * 4,
            bytes_accessed=vols * rows * cols * 2 + rows * cols * 2,
            transcendentals=0,
        ),
        name="lag_windows",
    )(codes, *tables, frames, template)


def on_device(frames, template, shift_codes):
    vol_dev, pl_dev, img_rows, img_cols = frames.shape
    block = template.shape[-1]
    tm_size = lax.axis_size("tm")
    plane_size = lax.axis_size("plane")
    own = template.shape[0]
    total = own * tm_size
    gathered = lax.all_gather(template, "tm", axis=0, tiled=True)
    warped = jnp.stack(
        [warp_sums(frames[:, p], shift_codes, block) for p in range(pl_dev)], axis=1
    )
    moved = lax.all_to_all(
        warped.reshape(tm_size, own, pl_dev, block, block), "tm", 0, 0, tiled=True
    )
    window = lag_windows(frames[:, 0], gathered[:, 0], shift_codes)
    for p in range(1, pl_dev):
        window = window + lag_windows(frames[:, p], gathered[:, p], shift_codes)
    me = lax.axis_index("plane")
    share = total // plane_size
    pieces = window.reshape(vol_dev, plane_size, share, WIN * WIN)
    correlation = lax.dynamic_index_in_dim(pieces, me, 1, keepdims=False)
    for step in range(1, plane_size):
        there = lax.rem(me + step, plane_size)
        sent = lax.dynamic_index_in_dim(pieces, there, 1, keepdims=False)
        correlation = correlation + lax.ppermute(
            sent, "plane", [(j, (j + step) % plane_size) for j in range(plane_size)]
        )
    volumes = vol_dev * tm_size
    new_template = jnp.sum(moved.astype(jnp.float32), axis=0) * (1.0 / volumes)
    return (correlation, new_template)


def solution(mesh):
    in_specs = (P("tm", "plane", None, None), P("tm", "plane", None, None), P("tm", None, None))
    out_specs = (P("tm", "plane", None), P("tm", "plane", None, None))
    return jax.shard_map(
        on_device, mesh=mesh, in_specs=in_specs, out_specs=out_specs, check_vma=False
    )
```

profile of v0, /device:TPU:0, one launch (start us, length us, event | category | flops | bytes accessed | tf_op | source)
XLA Modules:
  0.0 86.8 jit_solution(1181791822531993367)
XLA Ops:
  7.2 0.0 all-gather.2.cloned.1.call-start
  7.2 0.7 all-gather.2.cloned.1.call-update
  7.9 1.6 %copy-done = bf16[2,1,512,1024]{3,2,1,0:T(8,128)(2,1)S(1)} copy-done((bf16[2,1,512,1024]{3,2,1,0:T(8,128)(2,1)S(1)}, bf16[2,1,512,1024]{3,2,1,0:T(8,128)(2,1)}, u32[]{:S(2)}) %copy-start) | copy-done | bytes 2097176
  9.5 0.7 copy-done.3
  10.2 0.9 %copy-done.6 = f32[16,16,256]{2,1,0:T(8,128)S(1)} copy-done((f32[16,16,256]{2,1,0:T(8,128)S(1)}, f32[16,16,256]{2,1,0:T(8,128)}, u32[]{:S(2)}) %copy-start.6) | copy-done | bytes 262168
  11.1 0.0 copy-start.8
  11.1 0.0 copy-start.9
  11.2 0.0 copy-start.10
  11.2 12.7 %warp.1 = bf16[32,128,128]{2,1,0:T(8,128)(2,1)} custom-call(s32[2,2,32]{2,1,0:T(2,128)S(1)} %copy-done.3, f32[16,16,256]{2,1,0:T(8,128)S(1)} %copy-done.6, bf16[2,512,1024]{2,1,0:T(8,128)(2,1)S(1)} %bitcast.14), custom_call_target="tpu_custom_call" | custom-call | flops 1073741824 | bytes 3145728 | tf_op jit(solution)/shard_map/warp/pallas_call | solution.py:138
  23.9 7.4 %all-to-all-start = ((bf16[16,2,1,128,128]{4,3,1,2,0:T(8,128)(2,1)}), bf16[16,2,1,128,128]{4,3,1,2,0:T(8,128)(2,1)}, u32[]{:S(2)}, u32[]{:S(2)}) async-start(bf16[16,2,1,128,128]{4,3,1,2,0:T(8,128)(2,1)} %bitcast.6), calls=%async_computation | async-start | bytes 2097152 | tf_op jit(solution)/shard_map/all_to_all | solution.py:303
  31.4 25.4 %all-gather.2.cloned.1.call-done = bf16[32,1,128,128]{3,2,1,0:T(8,128)(2,1)} async-done(((bf16[2,1,128,128]{3,2,1,0:T(8,128)(2,1)}), bf16[32,1,128,128]{3,2,1,0:T(8,128)(2,1)}) %all-gather.2.cloned.1.call-update) | async-done | bytes 1048592 | tf_op jit(solution)/shard_map/all_gather | solution.py:299
  56.7 0.0 copy-done.1
  56.8 0.0 copy-done.8
  56.8 0.0 copy-done.9
  56.8 0.0 copy-done.10
  56.8 0.0 copy-start.2
  56.8 1.2 %copy-done.2 = bf16[32,1,128,128]{3,2,1,0:T(8,128)(2,1)S(1)} copy-done((bf16[32,1,128,128]{3,2,1,0:T(8,128)(2,1)S(1)}, bf16[32,1,128,128]{3,2,1,0:T(8,128)(2,1)}, u32[]{:S(2)}) %copy-start.2) | copy-done | bytes 1048600
  58.0 17.4 %lag_windows.1 = f32[2,32,256]{2,1,0:T(8,128)S(1)} custom-call(s32[2,2,32]{2,1,0:T(2,128)S(1)} %copy-done.4, bf16[128,256]{1,0:T(8,128)(2,1)S(1)} %copy-done.9, bf16[144,256]{1,0:T(8,128)(2,1)S(1)} %copy-done.7, bf16[16,32,144]{2,1,0:T(8,128)(2,1)S(1)} %copy-done.5, bf16[256,128]{1,0:T(8,128)(2,1)S(1)} %copy-done.8, f32[72,128]{1,0:T(8,128)S(1)} %copy-done.10, ...), custom_call_target="tpu_custom_call" | custom-call | flops 1610612736 | bytes 3145728 | tf_op jit(solution)/shard_map/lag_windows/pallas_call | solution.py:270
  75.4 1.5 %collective-permute-start = (f32[2,16,256]{2,1,0:T(8,128)S(1)}, f32[2,16,256]{2,1,0:T(8,128)S(1)}, u32[]{:S(2)}, u32[]{:S(2)}) collective-permute-start(f32[2,16,256]{2,1,0:T(8,128)S(1)} %dynamic-slice_bitcast_fusion), channel_id=1, source_target_pairs={{0,1},{1,0},{2,3},{3,2},{4,5},{5,4},{6,7},{7,6},{8,9},{9,8},{10,11... | collective-permute-start | bytes 98312 | tf_op jit(solution)/shard_map/ppermute | solution.py:316
  76.9 0.0 all-to-all-done
  76.9 1.4 %convert_reduce_fusion = f32[2,128,128]{2,1,0:T(8,128)S(1)} fusion(bf16[16,2,1,128,128]{4,3,1,2,0:T(8,128)(2,1)} %all-to-all-done), kind=kLoop, calls=%fused_computation | loop fusion | flops 1015808 | bytes 1179648 | tf_op jit(solution)/shard_map/reduce_sum | solution.py:320
  78.3 0.7 multiply_bitcast_fusion
  79.0 0.4 collective-permute-done
  79.4 0.6 bitcast_add_fusion
  (11 shorter events, 0.0 us)
Async XLA Ops:
  7.2 49.6 %all-gather.2.cloned.1.call-start = ((), (), s32[]{:S(2)}) async-start(), calls=%async_computation.1 | async-start | bytes 1114112 | tf_op jit(solution)/shard_map/all_gather | solution.py:299
  7.9 1.6 %copy-start = (bf16[2,1,512,1024]{3,2,1,0:T(8,128)(2,1)S(1)}, bf16[2,1,512,1024]{3,2,1,0:T(8,128)(2,1)}, u32[]{:S(2)}) copy-start(bf16[2,1,512,1024]{3,2,1,0:T(8,128)(2,1)} %param.9) | copy-start | bytes 6291460
  9.5 0.7 copy-start.3
  10.2 0.9 %copy-start.6 = (f32[16,16,256]{2,1,0:T(8,128)S(1)}, f32[16,16,256]{2,1,0:T(8,128)}, u32[]{:S(2)}) copy-start(f32[16,16,256]{2,1,0:T(8,128)} %constant.33.clone.taps_ref) | copy-start | bytes 786436
  11.1 45.6 %copy-start.1 = (bf16[2,1,512,1024]{3,2,1,0:T(8,128)(2,1)S(1)}, bf16[2,1,512,1024]{3,2,1,0:T(8,128)(2,1)}, u32[]{:S(2)}) copy-start(bf16[2,1,512,1024]{3,2,1,0:T(8,128)(2,1)} %param.9) | copy-start | bytes 6291460
  11.1 45.6 %copy-start.4 = (s32[2,2,32]{2,1,0:T(2,128)S(1)}, s32[2,2,32]{2,1,0:T(2,128)}, u32[]{:S(2)}) copy-start(s32[2,2,32]{2,1,0:T(2,128)} %codes_ref.3) | copy-start | bytes 1540
  11.1 45.6 %copy-start.5 = (bf16[16,32,144]{2,1,0:T(8,128)(2,1)S(1)}, bf16[16,32,144]{2,1,0:T(8,128)(2,1)}, u32[]{:S(2)}) copy-start(bf16[16,32,144]{2,1,0:T(8,128)(2,1)} %constant.36.clone.lag_ref) | copy-start | bytes 442372
  11.1 45.6 %copy-start.7 = (bf16[144,256]{1,0:T(8,128)(2,1)S(1)}, bf16[144,256]{1,0:T(8,128)(2,1)}, u32[]{:S(2)}) copy-start(bf16[144,256]{1,0:T(8,128)(2,1)} %constant.35.clone.col_ref) | copy-start | bytes 221188
  11.1 45.6 %copy-start.8 = (bf16[256,128]{1,0:T(8,128)(2,1)S(1)}, bf16[256,128]{1,0:T(8,128)(2,1)}, u32[]{:S(2)}) copy-start(bf16[256,128]{1,0:T(8,128)(2,1)} %constant.37.clone.span_ref) | copy-start | bytes 196612
  11.1 45.6 %copy-start.9 = (bf16[128,256]{1,0:T(8,128)(2,1)S(1)}, bf16[128,256]{1,0:T(8,128)(2,1)}, u32[]{:S(2)}) copy-start(bf16[128,256]{1,0:T(8,128)(2,1)} %constant.34.clone.row_ref) | copy-start | bytes 196612
  11.2 45.6 %copy-start.10 = (f32[72,128]{1,0:T(8,128)S(1)}, f32[72,128]{1,0:T(8,128)}, u32[]{:S(2)}) copy-start(f32[72,128]{1,0:T(8,128)} %constant.38.clone.weight_ref) | copy-start | bytes 110596
  23.9 53.0 %all-to-all-start = ((bf16[16,2,1,128,128]{4,3,1,2,0:T(8,128)(2,1)}), bf16[16,2,1,128,128]{4,3,1,2,0:T(8,128)(2,1)}, u32[]{:S(2)}, u32[]{:S(2)}) async-start(bf16[16,2,1,128,128]{4,3,1,2,0:T(8,128)(2,1)} %bitcast.6), calls=%async_computation | async-start | bytes 2097152 | tf_op jit(solution)/shard_map/all_to_all | solution.py:303
  56.8 1.2 %copy-start.2 = (bf16[32,1,128,128]{3,2,1,0:T(8,128)(2,1)S(1)}, bf16[32,1,128,128]{3,2,1,0:T(8,128)(2,1)}, u32[]{:S(2)}) copy-start(bf16[32,1,128,128]{3,2,1,0:T(8,128)(2,1)} %all-gather.2.cloned.1.call-done) | copy-start | bytes 3145732
  75.4 4.0 %collective-permute-start = (f32[2,16,256]{2,1,0:T(8,128)S(1)}, f32[2,16,256]{2,1,0:T(8,128)S(1)}, u32[]{:S(2)}, u32[]{:S(2)}) collective-permute-start(f32[2,16,256]{2,1,0:T(8,128)S(1)} %dynamic-slice_bitcast_fusion), channel_id=1, source_target_pairs={{0,1},{1,0},{2,3},{3,2},{4,5},{5,4},{6,7},{7,6},{8,9},{9,8},{10,11... | collective-permute-start | bytes 98312 | tf_op jit(solution)/shard_map/ppermute | solution.py:316
Sparse Core Ops, SparseCore 0:
  10.2 46.5 all-gather.1
where the time goes:
time: 87.2 us; the launch traced here: 86.8 us
  Pallas kernels  30.1 us (35%)
  waiting for transfers between devices  26.4 us (30%)
  between operations  14.1 us (16%)
  starting transfers between devices  9.02 us (10%)
  local copies, waits for them, and re-layouts  4.48 us (5%)
  other arithmetic  2.67 us (3%)
    all_gather x1, waiting for transfers between devices, on_device(): gathered = lax.all_gather(template, 'tm', axis=0, tiled=True)  25.4 us
    pallas_call x1, Pallas kernels, lag_windows(): pl.pallas_call(functools.partial(spectrum_kernel, vols, across, block), g...  17.4 us
    pallas_call x1, Pallas kernels, warp_sums(): pl.pallas_call(functools.partial(warp_kernel, vols, down, across, block),...  12.7 us
    all_to_all x1, starting transfers between devices, on_device(): lax.all_to_all(warped.reshape(tm_size, own, pl_dev, block, block), 'tm',...  7.45 us
    unnamed x22, local copies, waits for them, and re-layouts  4.47 us
  transfers between devices with their start and end apart: 3, of which 2 were waited for; matrix products, arithmetic and copies ran while one was open for 2% of the time, Pallas kernels for 35%

commit v1 on v0

v1 whole, which is shorter than its diff:
```python
import functools
import math

import jax
import jax.numpy as jnp
import numpy as np
from jax import lax
from jax.experimental import pallas as pl
from jax.experimental.pallas import tpu as pltpu
from jax.sharding import PartitionSpec as P

SHIFT = 8
WIN = 16
TAPS = 8
SUB = 16
EDGE = 16
LANES = 128
VMEM_LIMIT = 56 * 1024 * 1024

full_turn = 2.0 * math.pi


def dft_constants(block_size):
    positions = np.arange(block_size)
    angles = full_turn * (np.outer(positions, positions) % block_size) / block_size
    cosine = np.cos(angles)
    sine = -np.sin(angles)
    half = block_size // 2 + 1
    rows = -(-half // 8) * 8
    row_table = np.concatenate([cosine, sine], axis=1)
    col_table = np.zeros((2 * rows, 2 * block_size))
    col_table[:half] = np.concatenate([cosine[:half], -sine[:half]], axis=1)
    col_table[rows : rows + half] = np.concatenate([sine[:half], cosine[:half]], axis=1)
    weights = np.zeros((rows,))
    weights[:half] = 2.0
    weights[0] = weights[half - 1] = 1.0
    starts = 2 * SHIFT
    lag_table = np.zeros((starts, 2 * WIN, 2 * rows))
    for start in range(starts):
        lags = start - SHIFT - WIN // 2 + np.arange(WIN)
        turns = full_turn * (np.outer(lags, positions[:half]) % block_size) / block_size
        lag_cos = np.cos(turns) * weights[:half]
        lag_sin = np.sin(turns) * weights[:half]
        lag_table[start, :WIN, :half] = lag_cos
        lag_table[start, :WIN, rows : rows + half] = -lag_sin
        lag_table[start, WIN:, :half] = lag_sin
        lag_table[start, WIN:, rows : rows + half] = lag_cos
    span = starts + WIN
    lags = np.arange(span) - SHIFT - WIN // 2
    turns = full_turn * (np.outer(positions, lags) % block_size) / block_size
    span_table = np.zeros((2 * block_size, LANES))
    span_table[:block_size, :span] = np.cos(turns)
    span_table[block_size:, :span] = -np.sin(turns)
    return tuple(
        jnp.asarray(table, jnp.bfloat16) for table in (row_table, col_table, lag_table, span_table)
    )


def tap_constants():
    offsets = np.arange(TAPS) - (TAPS // 2 - 1)
    spots = offsets[None, :] - np.arange(SUB)[:, None] / SUB
    raw_taps = np.sinc(spots) * np.sinc(spots / (TAPS // 2))
    taps = raw_taps / raw_taps.sum(axis=-1, keepdims=True)
    table = np.zeros((SUB, EDGE, LANES))
    for row in range(EDGE):
        table[:, row, row : row + TAPS] = taps
    return jnp.asarray(table, jnp.float32)


def band_groups(head, shift, lane):
    start = shift + (LANES - (TAPS // 2 - 1))
    head = pltpu.roll(head, start, 1).astype(jnp.bfloat16)
    groups = [head] + [pltpu.roll(head, step, 1) for step in range(EDGE, LANES, EDGE)]
    zero = jnp.zeros_like(head)
    low = lane < LANES // 2
    before, after = jnp.where(low, zero, groups[0]), jnp.where(low, groups[-1], zero)
    middle = [jnp.where(low, groups[0], zero), *groups[1:-1], jnp.where(low, zero, groups[-1])]
    return middle, before, after


def warp_kernel(vols, down, across, block, codes_ref, taps_ref, mid_ref, above_ref, below_ref, out_ref):
    band = pl.program_id(0)
    lane = lax.broadcasted_iota(jnp.int32, (EDGE, LANES), 1)
    tall_lane = lax.broadcasted_iota(jnp.int32, (block + 2 * EDGE, LANES), 1)
    zero = jnp.zeros((EDGE, LANES), jnp.bfloat16)
    no_tile = jnp.zeros((block + 2 * EDGE, block), jnp.bfloat16)

    def tile(v, at):
        if at < 0 or at >= across:
            return no_tile
        lanes = slice(at * block, (at + 1) * block)
        above = jnp.where(band > 0, above_ref[v, :, lanes], zero)
        below = jnp.where(band < down - 1, below_ref[v, :, lanes], zero)
        return jnp.concatenate([mid_ref[v, :, lanes], below, above], axis=0)

    for at in range(across):
        index = band * across + at
        row_tiles, first_edge, last_edge = [], [], []
        partials, edges = [], []
        for v in range(vols):
            row_code = codes_ref[v, 0, index]
            col_code = codes_ref[v, 1, index]
            middle, before, after = band_groups(taps_ref[col_code & (SUB - 1)], col_code >> 4, lane)
            col_band = jnp.concatenate(
                [
                    jnp.concatenate(middle, axis=0),
                    jnp.concatenate([before] + [zero] * (block // EDGE - 2) + [after], axis=0),
                ],
                axis=1,
            )
            sides = jnp.where(tall_lane < LANES // 2, tile(v, at + 1), tile(v, at - 1))
            partial = lax.dot_general(
                jnp.concatenate([tile(v, at), sides], axis=1),
                col_band,
                (((1,), (1,)), ((), ())),
                preferred_element_type=jnp.float32,
            ).astype(jnp.bfloat16)
            partials.append(partial[:block])
            edges.append(partial[block:])
            middle, before, after = band_groups(taps_ref[row_code & (SUB - 1)], row_code >> 4, lane)
            row_tiles.append(jnp.concatenate(middle, axis=0))
            place = 2 * EDGE * v % LANES
            first_edge.append(pltpu.roll(before, (place + 2 * EDGE) % LANES, 1))
            last_edge.append(pltpu.roll(after, place, 1) if place else after)
        per_tile = LANES // (2 * EDGE)
        for v in range(0, vols, per_tile):
            first, last = first_edge[v], last_edge[v]
            for more in range(v + 1, min(v + per_tile, vols)):
                first, last = first + first_edge[more], last + last_edge[more]
            row_tiles.append(
                jnp.concatenate([first] + [zero] * (block // EDGE - 2) + [last], axis=0)
            )
        depth = vols * (block + 2 * EDGE)
        total = jnp.dot(
            jnp.concatenate(row_tiles, axis=1)[:, :depth],
            jnp.concatenate(partials + edges, axis=0),
            preferred_element_type=jnp.float32,
        )
        out_ref[at] = total.astype(jnp.bfloat16)


def warp_sums(frames, codes, block):
    vols, rows, cols = frames.shape
    down, across = rows // block, cols // block
    steps = block // EDGE
    taps = tap_constants()
    return pl.pallas_call(
        functools.partial(warp_kernel, vols, down, across, block),
        grid=(down,),
        out_shape=jax.ShapeDtypeStruct((down * across, block, block), jnp.bfloat16),
        in_specs=[
            pl.BlockSpec(memory_space=pltpu.SMEM),
            pl.BlockSpec(taps.shape, lambda band: (0, 0, 0)),
            pl.BlockSpec((vols, block, cols), lambda band: (0, band, 0)),
            pl.BlockSpec((vols, EDGE, cols), lambda band: (0, jnp.maximum(band * steps - 1, 0), 0)),
            pl.BlockSpec(
                (vols, EDGE, cols),
                lambda band: (0, jnp.minimum((band + 1) * steps, down * steps - 1), 0),
            ),
        ],
        out_specs=pl.BlockSpec((across, block, block), lambda band: (band, 0, 0)),
        compiler_params=pltpu.CompilerParams(vmem_limit_bytes=VMEM_LIMIT),
        cost_estimate=pl.CostEstimate(
            flops=2 * vols * rows * cols * block * 4,
            bytes_accessed=vols * rows * cols * 2 + rows * cols * 2,
            transcendentals=0,
        ),
        name="warp",
    )(codes, taps, frames, frames, frames)


def spectrum_kernel(
    vols,
    across,
    block,
    codes_ref,
    here_ref,
    row_ref,
    col_ref,
    lag_ref,
    span_ref,
    frames_ref,
    template_ref,
    out_ref,
    cross,
    sums,
    found,
):
    band = pl.program_id(0)
    own = template_ref.shape[1]
    row_table = row_ref[...]
    col_table = col_ref[...]
    half = col_table.shape[0] // 2
    top = lax.broadcasted_iota(jnp.int32, (8, LANES), 0) == 0

    for pair in range(across // 2):
        parts = []
        for side in range(2):
            index = band * across + 2 * pair + side
            parts.append(template_ref[(index // own) ^ here_ref[0], index % own])
        for v in range(vols):
            for side in range(2):
                at = 2 * pair + side
                parts.append(frames_ref[v, :, at * block : (at + 1) * block])
        rows = jnp.dot(
            jnp.concatenate(parts, axis=0), row_table, preferred_element_type=jnp.float32
        ).astype(jnp.bfloat16)
        spectra = []
        for source in range(vols + 1):
            stacks = []
            for side in range(2):
                at = (2 * source + side) * block
                one = rows[at : at + block]
                stacks.append(jnp.concatenate([one[:, :block], one[:, block:]], axis=0))
            spectra.append(
                jnp.dot(
                    col_table, jnp.concatenate(stacks, axis=1), preferred_element_type=jnp.float32
                )
            )
        temp = spectra[0].astype(jnp.bfloat16).astype(jnp.float32)
        for v in range(vols):
            for side in range(2):
                lanes = slice(side * block, (side + 1) * block)
                one = (2 * pair + side) * vols + v
                total = jnp.zeros((8, LANES), jnp.float32)
                for row in range(0, half, 8):
                    temp_real = temp[row : row + 8, lanes]
                    temp_imag = temp[half + row : half + row + 8, lanes]
                    real = spectra[v + 1][row : row + 8, lanes]
                    imag = spectra[v + 1][half + row : half + row + 8, lanes]
                    cross_real = real * temp_real + imag * temp_imag
                    cross_imag = imag * temp_real - real * temp_imag
                    power = cross_real * cross_real + cross_imag * cross_imag
                    magnitude = power * lax.rsqrt(jnp.maximum(power, 1e-36))
                    cross[one, row : row + 8, :] = cross_real
                    cross[one, half + row : half + row + 8, :] = cross_imag
                    cross[one, 2 * half + row : 2 * half + row + 8, :] = magnitude
                    if row == 0:
                        total = jnp.where(top, magnitude, 2.0 * magnitude)
                    elif row == block // 2:
                        total += magnitude
                    else:
                        total += 2.0 * magnitude
                sums[one] = jnp.sum(total, axis=0, keepdims=True)

    means = jnp.sum(sums[...], axis=2, keepdims=True) * (1.0 / (block * block)) + 1e-06
    lag_sums = []
    for one in range(across * vols):
        at, v = one // vols, one % vols
        mean = means[one]
        norms = []
        scales = []
        for row in range(0, half, 16):
            size = min(16, half - row)
            magnitude = cross[one, 2 * half + row : 2 * half + row + size, :]
            scales.append(pl.reciprocal(magnitude + mean, approx=True))
        scale = jnp.concatenate(scales, axis=0)
        norm = jnp.concatenate(
            [
                (cross[one, :half, :] * scale).astype(jnp.bfloat16),
                (cross[one, half : 2 * half, :] * scale).astype(jnp.bfloat16),
            ],
            axis=0,
        )
        row_shift = codes_ref[v, 0, band * across + at] >> 4
        lag_rows = jnp.dot(
            lag_ref[row_shift + SHIFT], norm, preferred_element_type=jnp.float32
        ).astype(jnp.bfloat16)
        lag_sums.append(jnp.concatenate([lag_rows[:WIN], lag_rows[WIN:]], axis=1))
    lags = jnp.dot(
        jnp.concatenate(lag_sums, axis=0), span_ref[...], preferred_element_type=jnp.float32
    )
    for one in range(across * vols):
        at, v = one // vols, one % vols
        col_shift = codes_ref[v, 1, band * across + at] >> 4
        found[v, at * WIN : (at + 1) * WIN, :] = pltpu.roll(
            lags[one * WIN : (one + 1) * WIN], LANES - SHIFT - col_shift, 1
        )

    per_tile = LANES // WIN
    lane = lax.broadcasted_iota(jnp.int32, (across, LANES), 1) // WIN
    for v in range(vols):
        for tile in range(WIN // per_tile):
            total = jnp.zeros((across, LANES), jnp.float32)
            for part in range(per_tile):
                one = found[v, pl.ds(tile * per_tile + part, across, stride=WIN), :]
                if part:
                    one = pltpu.roll(one, part * WIN, 1)
                total = jnp.where(lane == part, one, total)
            out_ref[v, :, tile * LANES : (tile + 1) * LANES] = total * (1.0 / block)


def lag_windows(frames, template, codes, here):
    vols, rows, cols = frames.shape
    block = template.shape[-1]
    down, across = rows // block, cols // block
    tables = dft_constants(block)
    half = tables[1].shape[0] // 2
    whole = [
        pl.BlockSpec(table.shape, functools.partial(lambda dims, band: (0,) * dims, table.ndim))
        for table in tables
    ]
    return pl.pallas_call(
        functools.partial(spectrum_kernel, vols, across, block),
        grid=(down,),
        out_shape=jax.ShapeDtypeStruct((vols, down * across, WIN * WIN), jnp.float32),
        in_specs=[
            pl.BlockSpec(memory_space=pltpu.SMEM),
            pl.BlockSpec(memory_space=pltpu.SMEM),
            *whole,
            pl.BlockSpec((vols, block, cols), lambda band: (0, band, 0)),
            pl.BlockSpec(template.shape, lambda band: (0, 0, 0, 0)),
        ],
        out_specs=pl.BlockSpec((vols, across, WIN * WIN), lambda band: (0, band, 0)),
        scratch_shapes=[
            pltpu.VMEM((vols * across, 3 * half, LANES), jnp.float32),
            pltpu.VMEM((vols * across, 1, LANES), jnp.float32),
            pltpu.VMEM((vols, across * WIN, LANES), jnp.float32),
        ],
        compiler_params=pltpu.CompilerParams(vmem_limit_bytes=VMEM_LIMIT),
        cost_estimate=pl.CostEstimate(
            flops=2 * 3 * rows * cols * block * 4,
            bytes_accessed=vols * rows * cols * 2 + rows * cols * 2,
            transcendentals=0,
        ),
        name="lag_windows",
    )(codes, here.reshape(1), *tables, frames, template)


def on_device(frames, template, shift_codes):
    vol_dev, pl_dev, img_rows, img_cols = frames.shape
    block = template.shape[-1]
    tm_size = lax.axis_size("tm")
    plane_size = lax.axis_size("plane")
    own = template.shape[0]
    total = own * tm_size
    here = lax.axis_index("tm")
    everyone = range(tm_size)
    same = [template[:, 0]]
    for step in range(2, tm_size, 2):
        same.append(lax.ppermute(template[:, 0], "tm", [(t, t ^ step) for t in everyone]))
    same = jnp.stack(same)
    other = lax.ppermute(same, "tm", [(t, t ^ 1) for t in everyone])
    gathered = jnp.stack([same, other], axis=1).reshape(tm_size, own, block, block)
    warped = jnp.stack(
        [warp_sums(frames[:, p], shift_codes, block) for p in range(pl_dev)], axis=1
    )
    moved = lax.all_to_all(
        warped.reshape(tm_size, own, pl_dev, block, block), "tm", 0, 0, tiled=True
    )
    window = lag_windows(frames[:, 0], gathered, shift_codes, here)
    me = lax.axis_index("plane")
    share = total // plane_size
    pieces = window.reshape(vol_dev, plane_size, share, WIN * WIN)
    correlation = lax.dynamic_index_in_dim(pieces, me, 1, keepdims=False)
    for step in range(1, plane_size):
        there = lax.rem(me + step, plane_size)
        sent = lax.dynamic_index_in_dim(pieces, there, 1, keepdims=False)
        correlation = correlation + lax.ppermute(
            sent, "plane", [(j, (j + step) % plane_size) for j in range(plane_size)]
        )
    volumes = vol_dev * tm_size
    new_template = jnp.sum(moved.astype(jnp.float32), axis=0) * (1.0 / volumes)
    return (correlation, new_template)


def solution(mesh):
    in_specs = (P("tm", "plane", None, None), P("tm", "plane", None, None), P("tm", None, None))
    out_specs = (P("tm", "plane", None), P("tm", "plane", None, None))
    return jax.shard_map(
        on_device, mesh=mesh, in_specs=in_specs, out_specs=out_specs, check_vma=False
    )
```

time: 87.2 us -> 74.1 us (0.85)
  starting transfers between devices: 9.02 us -> 22.8 us
  between operations: 14.1 us -> 0.75 us
  Pallas kernels: 30.1 us -> 21 us
  local copies, waits for them, and re-layouts: 4.48 us -> 1.96 us
  waiting for transfers between devices: 26.4 us -> 24.8 us
    all_gather x1 -> x0, waiting for transfers between devices: 25.4 us -> none  [on_device(): gathered = lax.all_gather(template, 'tm', axis=0, tiled=True)]
    ppermute x0 -> x8, waiting for transfers between devices: none -> 22.4 us  [the longest x7 20.5 us: on_device(): lax.ppermute(template[:, 0], 'tm', [(t, t ^ step) for t in everyone])]
    ppermute x0 -> x8, starting transfers between devices: none -> 16.2 us  [the longest x7 16.2 us: on_device(): lax.ppermute(template[:, 0], 'tm', [(t, t ^ step) for t in everyone])]
    pallas_call x1, Pallas kernels: 17.4 us -> 11.1 us  [lag_windows(): pl.pallas_call(functools.partial(spectrum_kernel, vols, across, block), g...]
    unnamed x22 -> x9, local copies, waits for them, and re-layouts: 4.47 us -> 0.09 us
    pallas_call x1, Pallas kernels: 12.7 us -> 9.91 us  [warp_sums(): pl.pallas_call(functools.partial(warp_kernel, vols, down, across, block),...]
    all_to_all x1, starting transfers between devices: 7.45 us -> 5.11 us  [on_device(): lax.all_to_all(warped.reshape(tm_size, own, pl_dev, block, block), 'tm',...]
    ppermute x1, waiting for transfers between devices: 0.4 us -> 2.43 us  [on_device(): lax.ppermute(sent, 'plane', [(j, (j + step) % plane_size) for j in range(...]
  transfers between devices with their start and end apart: 3 -> 10, of which waited for: 2 -> 4; matrix products, arithmetic and copies ran while one was open for 2% -> 5% of each run, Pallas kernels for 35% -> 28%
where the time goes in v1:
time: 74.1 us; the launch traced here: 73.7 us
  waiting for transfers between devices  24.8 us (33%)
  starting transfers between devices  22.8 us (31%)
  Pallas kernels  21 us (28%)
  other arithmetic  2.29 us (3%)
  local copies, waits for them, and re-layouts  1.96 us (3%)
  between operations  0.75 us (1%)
    ppermute x7, waiting for transfers between devices, on_device(): lax.ppermute(template[:, 0], 'tm', [(t, t ^ step) for t in everyone])  20.5 us
    ppermute x7, starting transfers between devices, on_device(): lax.ppermute(template[:, 0], 'tm', [(t, t ^ step) for t in everyone])  16.2 us
    pallas_call x1, Pallas kernels, lag_windows(): pl.pallas_call(functools.partial(spectrum_kernel, vols, across, block), g...  11.1 us
    pallas_call x1, Pallas kernels, warp_sums(): pl.pallas_call(functools.partial(warp_kernel, vols, down, across, block),...  9.91 us
    all_to_all x1, starting transfers between devices, on_device(): lax.all_to_all(warped.reshape(tm_size, own, pl_dev, block, block), 'tm',...  5.11 us
    ppermute x1, waiting for transfers between devices, on_device(): lax.ppermute(sent, 'plane', [(j, (j + step) % plane_size) for j in range(...  2.43 us
    ppermute x1, waiting for transfers between devices, on_device(): other = lax.ppermute(same, 'tm', [(t, t ^ 1) for t in everyone])  1.89 us
    ppermute x1, starting transfers between devices, on_device(): lax.ppermute(sent, 'plane', [(j, (j + step) % plane_size) for j in range(...  1.49 us
  transfers between devices with their start and end apart: 10, of which 4 were waited for; matrix products, arithmetic and copies ran while one was open for 5% of the time, Pallas kernels for 28%

profile of v1, /device:TPU:0, one launch (start us, length us, event | category | flops | bytes accessed | tf_op | source)
XLA Modules:
  0.0 73.7 jit_solution(18124667043258101043)
XLA Ops:
  0.6 6.1 %collective-permute-start.6 = (bf16[2,128,128]{2,1,0:T(8,128)(2,1)}, bf16[2,128,128]{2,1,0:T(8,128)(2,1)S(1)}, u32[]{:S(2)}, u32[]{:S(2)}) collective-permute-start(bf16[2,128,128]{2,1,0:T(8,128)(2,1)} %bitcast.42), channel_id=1, source_target_pairs={{0,28},{2,30},{4,24},{6,26},{8,20},{10,22},{12,16},{14,18},{16,12}... | collective-permute-start | bytes 196616 | tf_op jit(solution)/shard_map/ppermute | solution.py:341
  6.7 0.2 collective-permute-start.5
  6.9 0.7 collective-permute-start.4
  7.7 2.0 %collective-permute-start.3 = (bf16[2,128,128]{2,1,0:T(8,128)(2,1)}, bf16[2,128,128]{2,1,0:T(8,128)(2,1)S(1)}, u32[]{:S(2)}, u32[]{:S(2)}) collective-permute-start(bf16[2,128,128]{2,1,0:T(8,128)(2,1)} %bitcast.45), channel_id=1, source_target_pairs={{0,16},{2,18},{4,20},{6,22},{8,24},{10,26},{12,28},{14,30},{16,0},... | collective-permute-start | bytes 196616 | tf_op jit(solution)/shard_map/ppermute | solution.py:341
  9.7 1.6 %collective-permute-start = (bf16[2,128,128]{2,1,0:T(8,128)(2,1)}, bf16[2,128,128]{2,1,0:T(8,128)(2,1)S(1)}, u32[]{:S(2)}, u32[]{:S(2)}) collective-permute-start(bf16[2,128,128]{2,1,0:T(8,128)(2,1)} %bitcast.46), channel_id=1, source_target_pairs={{0,4},{2,6},{4,0},{6,2},{8,12},{10,14},{12,8},{14,10},{16,20},{18,... | collective-permute-start | bytes 196616 | tf_op jit(solution)/shard_map/ppermute | solution.py:341
  11.3 9.9 %warp.1 = bf16[32,128,128]{2,1,0:T(8,128)(2,1)} custom-call(s32[2,2,32]{2,1,0:T(2,128)} %codes_ref.3, f32[16,16,128]{2,1,0:T(8,128)} %constant.35.clone.taps_ref, bf16[2,512,1024]{2,1,0:T(8,128)(2,1)} %bitcast.32, bf16[2,512,1024]{2,1,0:T(8,128)(2,1)} %bitcast.33, bf16[2,512,1024]{2,1,0:T(8,128)(2,1)} %bitcast.34), custom_call_target="tpu_custom_call" | custom-call | flops 1073741824 | bytes 3145728 | tf_op jit(solution)/shard_map/warp/pallas_call | solution.py:147
  21.2 5.1 %all-to-all-start = ((bf16[16,2,1,128,128]{4,3,1,2,0:T(8,128)(2,1)}), bf16[16,2,1,128,128]{4,3,1,2,0:T(8,128)(2,1)S(1)}, u32[]{:S(2)}, u32[]{:S(2)}) async-start(bf16[16,2,1,128,128]{4,3,1,2,0:T(8,128)(2,1)} %bitcast.36), calls=%async_computation | async-start | bytes 2097152 | tf_op jit(solution)/shard_map/all_to_all | solution.py:348
  26.4 0.0 collective-permute-done
  26.4 2.0 %collective-permute-start.1 = (bf16[2,128,128]{2,1,0:T(8,128)(2,1)S(1)}, bf16[2,128,128]{2,1,0:T(8,128)(2,1)S(1)}, u32[]{:S(2)}, u32[]{:S(2)}) collective-permute-start(bf16[2,128,128]{2,1,0:T(8,128)(2,1)S(1)} %bitcast.47), channel_id=1, source_target_pairs={{0,8},{2,10},{4,12},{6,14},{8,0},{10,2},{12,4},{14,6},{16,24},{18,... | collective-permute-start | bytes 196616 | tf_op jit(solution)/shard_map/ppermute | solution.py:341
  28.4 17.4 %collective-permute-done.1 = bf16[2,128,128]{2,1,0:T(8,128)(2,1)S(1)} collective-permute-done((bf16[2,128,128]{2,1,0:T(8,128)(2,1)S(1)}, bf16[2,128,128]{2,1,0:T(8,128)(2,1)S(1)}, u32[]{:S(2)}, u32[]{:S(2)}) %collective-permute-start.1) | collective-permute-done | bytes 65568 | tf_op jit(solution)/shard_map/ppermute | solution.py:341
  45.8 3.5 %collective-permute-start.2 = (bf16[2,128,128]{2,1,0:T(8,128)(2,1)S(1)}, bf16[2,128,128]{2,1,0:T(8,128)(2,1)S(1)}, u32[]{:S(2)}, u32[]{:S(2)}) collective-permute-start(bf16[2,128,128]{2,1,0:T(8,128)(2,1)S(1)} %bitcast.48), channel_id=1, source_target_pairs={{0,12},{2,14},{4,8},{6,10},{8,4},{10,6},{12,0},{14,2},{16,28},{18,... | collective-permute-start | bytes 196616 | tf_op jit(solution)/shard_map/ppermute | solution.py:341
  49.3 3.1 %collective-permute-done.2 = bf16[2,128,128]{2,1,0:T(8,128)(2,1)S(1)} collective-permute-done((bf16[2,128,128]{2,1,0:T(8,128)(2,1)S(1)}, bf16[2,128,128]{2,1,0:T(8,128)(2,1)S(1)}, u32[]{:S(2)}, u32[]{:S(2)}) %collective-permute-start.2) | collective-permute-done | bytes 65568 | tf_op jit(solution)/shard_map/ppermute | solution.py:341
  52.4 0.0 collective-permute-done.3
  52.5 0.1 collective-permute-start.7
  52.6 1.9 %collective-permute-done.7 = bf16[8,2,128,128]{3,2,1,0:T(8,128)(2,1)S(1)} collective-permute-done((bf16[8,2,128,128]{3,2,1,0:T(8,128)(2,1)S(1)}, bf16[8,2,128,128]{3,2,1,0:T(8,128)(2,1)S(1)}, u32[]{:S(2)}, u32[]{:S(2)}) %collective-permute-start.7) | collective-permute-done | bytes 524320 | tf_op jit(solution)/shard_map/ppermute | solution.py:343
  54.5 0.1 pad_maximum_fusion
  54.6 1.1 %copy.11 = bf16[8,2,2,128,128]{4,3,2,1,0:T(8,128)(2,1)} copy(bf16[8,2,2,128,128]{4,3,2,0,1:T(8,128)(2,1)S(1)} %pad_maximum_fusion) | data formatting | bytes 2097152 | tf_op jit(solution)/shard_map/stack | solution.py:344
  55.7 11.1 %lag_windows.1 = f32[2,32,256]{2,1,0:T(8,128)} custom-call(s32[2,2,32]{2,1,0:T(2,128)} %codes_ref.3, s32[1]{0:T(128)} %bitcast.here_ref, bf16[128,256]{1,0:T(8,128)(2,1)} %constant.36.clone.row_ref, bf16[144,256]{1,0:T(8,128)(2,1)} %constant.37.clone.col_ref, bf16[16,32,144]{2,1,0:T(8,128)(2,1)} %constant.38.clone.lag_ref, ...), custom_call_target="tpu_custom_call" | custom-call | flops 1610612736 | bytes 3145728 | tf_op jit(solution)/shard_map/lag_windows/pallas_call | solution.py:303
  66.8 0.8 %dynamic-slice_bitcast_fusion = f32[2,16,256]{2,1,0:T(8,128)S(1)} fusion(f32[2,2,16,256]{3,2,1,0:T(8,128)} %bitcast.40, s32[]{:T(128)S(6)} %select_n.8), kind=kLoop, calls=%fused_computation.12 | loop fusion | bytes 65540 | tf_op jit(solution)/shard_map/jit(dynamic_index_in_dim)/squeeze | solution.py:358
  67.6 1.5 %collective-permute-start.8 = (f32[2,16,256]{2,1,0:T(8,128)S(1)}, f32[2,16,256]{2,1,0:T(8,128)S(1)}, u32[]{:S(2)}, u32[]{:S(2)}) collective-permute-start(f32[2,16,256]{2,1,0:T(8,128)S(1)} %dynamic-slice_bitcast_fusion), channel_id=1, source_target_pairs={{0,1},{1,0},{2,3},{3,2},{4,5},{5,4},{6,7},{7,6},{8,9},{9,8},{10,11... | collective-permute-start | bytes 98312 | tf_op jit(solution)/shard_map/ppermute | solution.py:359
  69.0 2.4 %collective-permute-done.8 = f32[2,16,256]{2,1,0:T(8,128)S(1)} collective-permute-done((f32[2,16,256]{2,1,0:T(8,128)S(1)}, f32[2,16,256]{2,1,0:T(8,128)S(1)}, u32[]{:S(2)}, u32[]{:S(2)}) %collective-permute-start.8) | collective-permute-done | bytes 32800 | tf_op jit(solution)/shard_map/ppermute | solution.py:359
  71.5 1.4 %bitcast_add_fusion = f32[2,16,256]{2,1,0:T(8,128)} fusion(f32[2,16,256]{2,1,0:T(8,128)S(1)} %collective-permute-done.8, f32[2,2,16,256]{3,2,1,0:T(8,128)} %bitcast.41, s32[]{:T(128)S(6)} %select_n.7), kind=kLoop, calls=%fused_computation.11 | loop fusion | flops 8192 | bytes 98308 | tf_op jit(solution)/shard_map/add | solution.py:359
  72.9 0.1 convert_reduce_fusion
  73.0 0.7 multiply_bitcast_fusion
  (14 shorter events, 0.1 us)
Async XLA Ops:
  0.6 51.9 %collective-permute-start.6 = (bf16[2,128,128]{2,1,0:T(8,128)(2,1)}, bf16[2,128,128]{2,1,0:T(8,128)(2,1)S(1)}, u32[]{:S(2)}, u32[]{:S(2)}) collective-permute-start(bf16[2,128,128]{2,1,0:T(8,128)(2,1)} %bitcast.42), channel_id=1, source_target_pairs={{0,28},{2,30},{4,24},{6,26},{8,20},{10,22},{12,16},{14,18},{16,12}... | collective-permute-start | bytes 196616 | tf_op jit(solution)/shard_map/ppermute | solution.py:341
  6.7 45.8 %collective-permute-start.5 = (bf16[2,128,128]{2,1,0:T(8,128)(2,1)}, bf16[2,128,128]{2,1,0:T(8,128)(2,1)S(1)}, u32[]{:S(2)}, u32[]{:S(2)}) collective-permute-start(bf16[2,128,128]{2,1,0:T(8,128)(2,1)} %bitcast.43), channel_id=1, source_target_pairs={{0,24},{2,26},{4,28},{6,30},{8,16},{10,18},{12,20},{14,22},{16,8},... | collective-permute-start | bytes 196616 | tf_op jit(solution)/shard_map/ppermute | solution.py:341
  6.9 45.5 %collective-permute-start.4 = (bf16[2,128,128]{2,1,0:T(8,128)(2,1)}, bf16[2,128,128]{2,1,0:T(8,128)(2,1)S(1)}, u32[]{:S(2)}, u32[]{:S(2)}) collective-permute-start(bf16[2,128,128]{2,1,0:T(8,128)(2,1)} %bitcast.44), channel_id=1, source_target_pairs={{0,20},{2,22},{4,16},{6,18},{8,28},{10,30},{12,24},{14,26},{16,4},... | collective-permute-start | bytes 196616 | tf_op jit(solution)/shard_map/ppermute | solution.py:341
  7.7 44.8 %collective-permute-start.3 = (bf16[2,128,128]{2,1,0:T(8,128)(2,1)}, bf16[2,128,128]{2,1,0:T(8,128)(2,1)S(1)}, u32[]{:S(2)}, u32[]{:S(2)}) collective-permute-start(bf16[2,128,128]{2,1,0:T(8,128)(2,1)} %bitcast.45), channel_id=1, source_target_pairs={{0,16},{2,18},{4,20},{6,22},{8,24},{10,26},{12,28},{14,30},{16,0},... | collective-permute-start | bytes 196616 | tf_op jit(solution)/shard_map/ppermute | solution.py:341
  9.7 16.7 %collective-permute-start = (bf16[2,128,128]{2,1,0:T(8,128)(2,1)}, bf16[2,128,128]{2,1,0:T(8,128)(2,1)S(1)}, u32[]{:S(2)}, u32[]{:S(2)}) collective-permute-start(bf16[2,128,128]{2,1,0:T(8,128)(2,1)} %bitcast.46), channel_id=1, source_target_pairs={{0,4},{2,6},{4,0},{6,2},{8,12},{10,14},{12,8},{14,10},{16,20},{18,... | collective-permute-start | bytes 196616 | tf_op jit(solution)/shard_map/ppermute | solution.py:341
  21.2 5.1 %copy-start = (bf16[2,1,128,128]{3,2,1,0:T(8,128)(2,1)S(1)}, bf16[2,1,128,128]{3,2,1,0:T(8,128)(2,1)}, u32[]{:S(2)}) copy-start(bf16[2,1,128,128]{3,2,1,0:T(8,128)(2,1)} %param.9) | copy-start | bytes 196612
  21.2 51.6 %all-to-all-start = ((bf16[16,2,1,128,128]{4,3,1,2,0:T(8,128)(2,1)}), bf16[16,2,1,128,128]{4,3,1,2,0:T(8,128)(2,1)S(1)}, u32[]{:S(2)}, u32[]{:S(2)}) async-start(bf16[16,2,1,128,128]{4,3,1,2,0:T(8,128)(2,1)} %bitcast.36), calls=%async_computation | async-start | bytes 2097152 | tf_op jit(solution)/shard_map/all_to_all | solution.py:348
  26.4 19.4 %collective-permute-start.1 = (bf16[2,128,128]{2,1,0:T(8,128)(2,1)S(1)}, bf16[2,128,128]{2,1,0:T(8,128)(2,1)S(1)}, u32[]{:S(2)}, u32[]{:S(2)}) collective-permute-start(bf16[2,128,128]{2,1,0:T(8,128)(2,1)S(1)} %bitcast.47), channel_id=1, source_target_pairs={{0,8},{2,10},{4,12},{6,14},{8,0},{10,2},{12,4},{14,6},{16,24},{18,... | collective-permute-start | bytes 196616 | tf_op jit(solution)/shard_map/ppermute | solution.py:341
  45.8 6.6 %collective-permute-start.2 = (bf16[2,128,128]{2,1,0:T(8,128)(2,1)S(1)}, bf16[2,128,128]{2,1,0:T(8,128)(2,1)S(1)}, u32[]{:S(2)}, u32[]{:S(2)}) collective-permute-start(bf16[2,128,128]{2,1,0:T(8,128)(2,1)S(1)} %bitcast.48), channel_id=1, source_target_pairs={{0,12},{2,14},{4,8},{6,10},{8,4},{10,6},{12,0},{14,2},{16,28},{18,... | collective-permute-start | bytes 196616 | tf_op jit(solution)/shard_map/ppermute | solution.py:341
  52.5 2.0 %collective-permute-start.7 = (bf16[8,2,128,128]{3,2,1,0:T(8,128)(2,1)S(1)}, bf16[8,2,128,128]{3,2,1,0:T(8,128)(2,1)S(1)}, u32[]{:S(2)}, u32[]{:S(2)}) collective-permute-start(bf16[8,2,128,128]{3,2,1,0:T(8,128)(2,1)S(1)} %bitcast_dynamic-update-slice_fusion), channel_id=1, source_target_pairs={{0,2},{2,0},{4,6},{6,4},{8,10},{10,8},{12,14},{14,12},{16,18},{18,... | collective-permute-start | bytes 1572872 | tf_op jit(solution)/shard_map/ppermute | solution.py:343
  67.6 3.9 %collective-permute-start.8 = (f32[2,16,256]{2,1,0:T(8,128)S(1)}, f32[2,16,256]{2,1,0:T(8,128)S(1)}, u32[]{:S(2)}, u32[]{:S(2)}) collective-permute-start(f32[2,16,256]{2,1,0:T(8,128)S(1)} %dynamic-slice_bitcast_fusion), channel_id=1, source_target_pairs={{0,1},{1,0},{2,3},{3,2},{4,5},{5,4},{6,7},{7,6},{8,9},{9,8},{10,11... | collective-permute-start | bytes 98312 | tf_op jit(solution)/shard_map/ppermute | solution.py:359

commit v2 on v1

v2 whole, which is shorter than its diff:
```python
import functools
import math

import jax
import jax.numpy as jnp
import numpy as np
from jax import lax
from jax.experimental import pallas as pl
from jax.experimental.pallas import tpu as pltpu
from jax.sharding import PartitionSpec as P

SHIFT = 8
WIN = 16
TAPS = 8
SUB = 16
EDGE = 16
LANES = 128
VMEM_LIMIT = 56 * 1024 * 1024

full_turn = 2.0 * math.pi


def dft_constants(block_size):
    positions = np.arange(block_size)
    angles = full_turn * (np.outer(positions, positions) % block_size) / block_size
    cosine = np.cos(angles)
    sine = -np.sin(angles)
    half = block_size // 2 + 1
    rows = -(-half // 8) * 8
    row_table = np.concatenate([cosine, sine], axis=1)
    col_table = np.zeros((2 * rows, 2 * block_size))
    col_table[:half] = np.concatenate([cosine[:half], -sine[:half]], axis=1)
    col_table[rows : rows + half] = np.concatenate([sine[:half], cosine[:half]], axis=1)
    weights = np.zeros((rows,))
    weights[:half] = 2.0
    weights[0] = weights[half - 1] = 1.0
    starts = 2 * SHIFT
    lag_table = np.zeros((starts, 2 * WIN, 2 * rows))
    for start in range(starts):
        lags = start - SHIFT - WIN // 2 + np.arange(WIN)
        turns = full_turn * (np.outer(lags, positions[:half]) % block_size) / block_size
        lag_cos = np.cos(turns) * weights[:half]
        lag_sin = np.sin(turns) * weights[:half]
        lag_table[start, :WIN, :half] = lag_cos
        lag_table[start, :WIN, rows : rows + half] = -lag_sin
        lag_table[start, WIN:, :half] = lag_sin
        lag_table[start, WIN:, rows : rows + half] = lag_cos
    span = starts + WIN
    lags = np.arange(span) - SHIFT - WIN // 2
    turns = full_turn * (np.outer(positions, lags) % block_size) / block_size
    span_table = np.zeros((2 * block_size, LANES))
    span_table[:block_size, :span] = np.cos(turns)
    span_table[block_size:, :span] = -np.sin(turns)
    return tuple(
        jnp.asarray(table, jnp.bfloat16) for table in (row_table, col_table, lag_table, span_table)
    )


def tap_constants():
    offsets = np.arange(TAPS) - (TAPS // 2 - 1)
    spots = offsets[None, :] - np.arange(SUB)[:, None] / SUB
    raw_taps = np.sinc(spots) * np.sinc(spots / (TAPS // 2))
    taps = raw_taps / raw_taps.sum(axis=-1, keepdims=True)
    table = np.zeros((SUB, EDGE, LANES))
    for row in range(EDGE):
        table[:, row, row : row + TAPS] = taps
    return jnp.asarray(table, jnp.float32)


def band_groups(head, shift, lane):
    start = shift + (LANES - (TAPS // 2 - 1))
    head = pltpu.roll(head, start, 1).astype(jnp.bfloat16)
    groups = [head] + [pltpu.roll(head, step, 1) for step in range(EDGE, LANES, EDGE)]
    zero = jnp.zeros_like(head)
    low = lane < LANES // 2
    before, after = jnp.where(low, zero, groups[0]), jnp.where(low, groups[-1], zero)
    middle = [jnp.where(low, groups[0], zero), *groups[1:-1], jnp.where(low, zero, groups[-1])]
    return middle, before, after


def warp_kernel(
    vols,
    down,
    across,
    block,
    own,
    core_ref,
    codes_ref,
    other_codes_ref,
    taps_ref,
    mid_ref,
    above_ref,
    below_ref,
    other_mid_ref,
    other_above_ref,
    other_below_ref,
    out_ref,
):
    band = pl.program_id(0)
    lane = lax.broadcasted_iota(jnp.int32, (EDGE, LANES), 1)
    tall_lane = lax.broadcasted_iota(jnp.int32, (block + 2 * EDGE, LANES), 1)
    zero = jnp.zeros((EDGE, LANES), jnp.bfloat16)
    no_tile = jnp.zeros((block + 2 * EDGE, block), jnp.bfloat16)
    volumes = [(codes_ref, mid_ref, above_ref, below_ref, v) for v in range(vols)]
    volumes += [
        (other_codes_ref, other_mid_ref, other_above_ref, other_below_ref, v) for v in range(vols)
    ]

    def tile(volume, at):
        _, mid, above, below, v = volume
        lanes = pl.ds(pl.multiple_of(at * block, block), block)
        above = jnp.where(band > 0, above[v, :, lanes], zero)
        below = jnp.where(band < down - 1, below[v, :, lanes], zero)
        return jnp.concatenate([mid[v, :, lanes], below, above], axis=0)

    for count in range(across // 2):
        at = (2 * (count // own) + core_ref[0]) * own + count % own
        index = band * across + at
        row_tiles, first_edge, last_edge = [], [], []
        partials, edges = [], []
        for order, volume in enumerate(volumes):
            codes, v = volume[0], volume[-1]
            row_code = codes[v, 0, index]
            col_code = codes[v, 1, index]
            middle, before, after = band_groups(taps_ref[col_code & (SUB - 1)], col_code >> 4, lane)
            col_band = jnp.concatenate(
                [
                    jnp.concatenate(middle, axis=0),
                    jnp.concatenate([before] + [zero] * (block // EDGE - 2) + [after], axis=0),
                ],
                axis=1,
            )
            left = jnp.where(at > 0, tile(volume, jnp.maximum(at - 1, 0)), no_tile)
            right = jnp.where(
                at < across - 1, tile(volume, jnp.minimum(at + 1, across - 1)), no_tile
            )
            sides = jnp.where(tall_lane < LANES // 2, right, left)
            partial = lax.dot_general(
                jnp.concatenate([tile(volume, at), sides], axis=1),
                col_band,
                (((1,), (1,)), ((), ())),
                preferred_element_type=jnp.float32,
            ).astype(jnp.bfloat16)
            partials.append(partial[:block])
            edges.append(partial[block:])
            middle, before, after = band_groups(taps_ref[row_code & (SUB - 1)], row_code >> 4, lane)
            row_tiles.append(jnp.concatenate(middle, axis=0))
            place = 2 * EDGE * order % LANES
            first_edge.append(pltpu.roll(before, (place + 2 * EDGE) % LANES, 1))
            last_edge.append(pltpu.roll(after, place, 1) if place else after)
        per_tile = LANES // (2 * EDGE)
        for first_order in range(0, 2 * vols, per_tile):
            first, last = first_edge[first_order], last_edge[first_order]
            for more in range(first_order + 1, min(first_order + per_tile, 2 * vols)):
                first, last = first + first_edge[more], last + last_edge[more]
            row_tiles.append(
                jnp.concatenate([first] + [zero] * (block // EDGE - 2) + [last], axis=0)
            )
        depth = 2 * vols * (block + 2 * EDGE)
        total = jnp.dot(
            jnp.concatenate(row_tiles, axis=1)[:, :depth],
            jnp.concatenate(partials + edges, axis=0),
            preferred_element_type=jnp.float32,
        )
        out_ref[count] = total.astype(jnp.bfloat16)


def warp_sums(core, codes, other_codes, frames, other_frames, block, own):
    vols, rows, cols = frames.shape
    down, across = rows // block, cols // block
    steps = block // EDGE
    taps = tap_constants()
    smem = pl.BlockSpec(memory_space=pltpu.SMEM)
    frame_specs = [
        pl.BlockSpec((vols, block, cols), lambda band: (0, band, 0)),
        pl.BlockSpec((vols, EDGE, cols), lambda band: (0, jnp.maximum(band * steps - 1, 0), 0)),
        pl.BlockSpec(
            (vols, EDGE, cols),
            lambda band: (0, jnp.minimum((band + 1) * steps, down * steps - 1), 0),
        ),
    ]
    return pl.pallas_call(
        functools.partial(warp_kernel, vols, down, across, block, own),
        grid=(down,),
        out_shape=jax.ShapeDtypeStruct((down * across // 2, block, block), jnp.bfloat16),
        in_specs=[
            smem,
            smem,
            smem,
            pl.BlockSpec(taps.shape, lambda band: (0, 0, 0)),
            *frame_specs,
            *frame_specs,
        ],
        out_specs=pl.BlockSpec((across // 2, block, block), lambda band: (band, 0, 0)),
        compiler_params=pltpu.CompilerParams(vmem_limit_bytes=VMEM_LIMIT),
        cost_estimate=pl.CostEstimate(
            flops=2 * vols * rows * cols * block * 4,
            bytes_accessed=vols * rows * cols * 4 + rows * cols,
            transcendentals=0,
        ),
        name="warp",
    )(core, codes, other_codes, taps, *([frames] * 3), *([other_frames] * 3))


def spectrum_kernel(
    vols,
    down,
    across,
    block,
    own,
    planes,
    core_ref,
    codes_ref,
    other_codes_ref,
    row_ref,
    col_ref,
    lag_ref,
    span_ref,
    frames_ref,
    other_frames_ref,
    template_ref,
    out_ref,
    cross,
    sums,
    found,
):
    band = pl.program_id(0)
    core = core_ref[0]
    row_table = row_ref[...]
    col_table = col_ref[...]
    half = col_table.shape[0] // 2
    top = lax.broadcasted_iota(jnp.int32, (8, LANES), 0) == 0
    volumes = [(codes_ref, frames_ref, v) for v in range(vols)]
    volumes += [(other_codes_ref, other_frames_ref, v) for v in range(vols)]
    many = len(volumes)
    local = across // 2
    places = [(2 * (count // own) + core) * own + count % own for count in range(local)]

    for pair in range(local // 2):
        pair_places = places[2 * pair : 2 * pair + 2]
        parts = [template_ref[2 * pair], template_ref[2 * pair + 1]]
        for _, frames, v in volumes:
            for at in pair_places:
                parts.append(frames[v, :, pl.ds(pl.multiple_of(at * block, block), block)])
        rows = jnp.dot(
            jnp.concatenate(parts, axis=0), row_table, preferred_element_type=jnp.float32
        ).astype(jnp.bfloat16)
        spectra = []
        for source in range(many + 1):
            stacks = []
            for side in range(2):
                at = (2 * source + side) * block
                one = rows[at : at + block]
                stacks.append(jnp.concatenate([one[:, :block], one[:, block:]], axis=0))
            spectra.append(
                jnp.dot(
                    col_table, jnp.concatenate(stacks, axis=1), preferred_element_type=jnp.float32
                )
            )
        temp = spectra[0].astype(jnp.bfloat16).astype(jnp.float32)
        for order in range(many):
            for side in range(2):
                lanes = slice(side * block, (side + 1) * block)
                one = (2 * pair + side) * many + order
                total = jnp.zeros((8, LANES), jnp.float32)
                for row in range(0, half, 8):
                    temp_real = temp[row : row + 8, lanes]
                    temp_imag = temp[half + row : half + row + 8, lanes]
                    real = spectra[order + 1][row : row + 8, lanes]
                    imag = spectra[order + 1][half + row : half + row + 8, lanes]
                    cross_real = real * temp_real + imag * temp_imag
                    cross_imag = imag * temp_real - real * temp_imag
                    power = cross_real * cross_real + cross_imag * cross_imag
                    magnitude = power * lax.rsqrt(jnp.maximum(power, 1e-36))
                    cross[one, row : row + 8, :] = cross_real
                    cross[one, half + row : half + row + 8, :] = cross_imag
                    cross[one, 2 * half + row : 2 * half + row + 8, :] = magnitude
                    if row == 0:
                        total = jnp.where(top, magnitude, 2.0 * magnitude)
                    elif row == block // 2:
                        total += magnitude
                    else:
                        total += 2.0 * magnitude
                sums[one] = jnp.sum(total, axis=0, keepdims=True)

    means = jnp.sum(sums[...], axis=2, keepdims=True) * (1.0 / (block * block)) + 1e-06
    lag_sums = []
    for one in range(local * many):
        codes, _, v = volumes[one % many]
        index = band * across + places[one // many]
        scale = pl.reciprocal(cross[one, 2 * half :, :] + means[one], approx=True)
        norm = jnp.concatenate(
            [
                (cross[one, :half, :] * scale).astype(jnp.bfloat16),
                (cross[one, half : 2 * half, :] * scale).astype(jnp.bfloat16),
            ],
            axis=0,
        )
        row_shift = codes[v, 0, index] >> 4
        lag_rows = jnp.dot(
            lag_ref[row_shift + SHIFT], norm, preferred_element_type=jnp.float32
        ).astype(jnp.bfloat16)
        lag_sums.append(jnp.concatenate([lag_rows[:WIN], lag_rows[WIN:]], axis=1))
    lags = jnp.dot(
        jnp.concatenate(lag_sums, axis=0), span_ref[...], preferred_element_type=jnp.float32
    )
    for one in range(local * many):
        codes, _, v = volumes[one % many]
        index = band * across + places[one // many]
        col_shift = codes[v, 1, index] >> 4
        start = pl.multiple_of((band * local + one // many) * WIN, WIN)
        found[one % many, pl.ds(start, WIN), :] = pltpu.roll(
            lags[one * WIN : (one + 1) * WIN], LANES - SHIFT - col_shift, 1
        )

    @pl.when(band == down - 1)
    def _():
        share = down * local // planes
        per_tile = LANES // WIN
        lane = lax.broadcasted_iota(jnp.int32, (share, LANES), 1) // WIN
        for order in range(many):
            owner = core if order < vols else 1 - core
            for plane in range(planes):
                for tile in range(WIN // per_tile):
                    total = jnp.zeros((share, LANES), jnp.float32)
                    for part in range(per_tile):
                        start = plane * share * WIN + tile * per_tile + part
                        one = found[order, pl.ds(start, share, stride=WIN), :]
                        if part:
                            one = pltpu.roll(one, part * WIN, 1)
                        total = jnp.where(lane == part, one, total)
                    lanes = slice(tile * LANES, (tile + 1) * LANES)
                    out_ref[owner * planes + plane, order % vols, :, lanes] = total * (1.0 / block)


def lag_windows(core, codes, other_codes, frames, other_frames, template, planes, own):
    vols, rows, cols = frames.shape
    block = template.shape[-1]
    down, across = rows // block, cols // block
    tables = dft_constants(block)
    half = tables[1].shape[0] // 2
    whole = [
        pl.BlockSpec(table.shape, functools.partial(lambda dims, band: (0,) * dims, table.ndim))
        for table in tables
    ]
    smem = pl.BlockSpec(memory_space=pltpu.SMEM)
    frame_spec = pl.BlockSpec((vols, block, cols), lambda band: (0, band, 0))
    local = down * across // 2
    out_dims = (2 * planes, vols, local // planes, WIN * WIN)
    return pl.pallas_call(
        functools.partial(spectrum_kernel, vols, down, across, block, own, planes),
        grid=(down,),
        out_shape=jax.ShapeDtypeStruct(out_dims, jnp.float32),
        in_specs=[
            smem,
            smem,
            smem,
            *whole,
            frame_spec,
            frame_spec,
            pl.BlockSpec((across // 2, block, block), lambda band: (band, 0, 0)),
        ],
        out_specs=pl.BlockSpec(out_dims, lambda band: (0, 0, 0, 0)),
        scratch_shapes=[
            pltpu.VMEM((vols * across, 3 * half, LANES), jnp.float32),
            pltpu.VMEM((vols * across, 1, LANES), jnp.float32),
            pltpu.VMEM((2 * vols, local * WIN, LANES), jnp.float32),
        ],
        compiler_params=pltpu.CompilerParams(vmem_limit_bytes=VMEM_LIMIT),
        cost_estimate=pl.CostEstimate(
            flops=2 * 3 * rows * cols * block * 4,
            bytes_accessed=vols * rows * cols * 4 + rows * cols,
            transcendentals=0,
        ),
        name="lag_windows",
    )(core, codes, other_codes, *tables, frames, other_frames, template)


def on_device(frames, template, shift_codes):
    vol_dev, pl_dev, img_rows, img_cols = frames.shape
    own, block = template.shape[0], template.shape[-1]
    chips = lax.axis_size("chip")
    planes = lax.axis_size("plane")
    share = 2 * chips * own // planes
    core = lax.axis_index("core").reshape(1)
    swap = [(0, 1), (1, 0)]
    other_frames = lax.ppermute(frames, "core", swap)
    other_codes = lax.ppermute(shift_codes, "core", swap)
    copies = jnp.broadcast_to(template[None], (chips, *template.shape))
    gathered = lax.all_to_all(copies, "chip", 0, 0, tiled=True)
    gathered = gathered.reshape(chips * own, pl_dev, block, block)
    moved, window = [], 0.0
    for p in range(pl_dev):
        work = (core, shift_codes, other_codes, frames[:, p], other_frames[:, p])
        warped = warp_sums(*work, block, own).reshape(chips, own, block, block)
        moved.append(lax.all_to_all(warped, "chip", 0, 0, tiled=True))
        window = window + lag_windows(*work, gathered[:, p], planes, own)
    window = lax.all_to_all(window, ("core", "plane"), 0, 0, tiled=True)
    window = window.reshape(2, planes, vol_dev, share // (2 * own), own, WIN * WIN)
    window = jnp.sum(window, axis=1)
    correlation = window.transpose(1, 2, 0, 3, 4).reshape(vol_dev, share, WIN * WIN)
    volumes = vol_dev * chips * 2
    sums = [jnp.sum(one.astype(jnp.float32), axis=0) for one in moved]
    new_template = jnp.stack(sums, axis=1) * (1.0 / volumes)
    return (correlation, new_template)


def solution(mesh):
    devices = mesh.devices.reshape(-1, 2, mesh.shape["plane"])
    split = jax.sharding.Mesh(devices, ("chip", "core", "plane"))
    vols = ("chip", "core")
    in_specs = (P(vols, "plane", None, None), P(vols, "plane", None, None), P(vols, None, None))
    out_specs = (P(vols, "plane", None), P(vols, "plane", None, None))
    return jax.shard_map(
        on_device, mesh=split, in_specs=in_specs, out_specs=out_specs, check_vma=False
    )
```

time: 74.1 us -> 66.6 us (0.90)
  starting transfers between devices: 22.8 us -> 14.5 us
  waiting for transfers between devices: 24.8 us -> 29.4 us
  Pallas kernels: 21 us -> 16.9 us
  local copies, waits for them, and re-layouts: 1.96 us -> 3.89 us
  other arithmetic: 2.29 us -> 0.77 us
    all_to_all x1 -> x3, waiting for transfers between devices: 0.01 us -> 28.2 us  [the longest x1 14.4 us: on_device(): moved.append(lax.all_to_all(warped, 'chip', 0, 0, tiled=True))]
    ppermute x9 -> x2, waiting for transfers between devices: 24.8 us -> 1.16 us  [the longest x1 1.15 us: on_device(): other_codes = lax.ppermute(shift_codes, 'core', swap)]
    ppermute x9 -> x2, starting transfers between devices: 17.7 us -> 0.73 us  [the longest x1 0.52 us: on_device(): other_frames = lax.ppermute(frames, 'core', swap)]
    all_to_all x1 -> x3, starting transfers between devices: 5.11 us -> 13.8 us  [the longest x1 6.85 us: on_device(): gathered = lax.all_to_all(copies, 'chip', 0, 0, tiled=True)]
    pallas_call x2, Pallas kernels: 21 us -> 16.9 us  [the longest x1 8.87 us: lag_windows(): pl.pallas_call(functools.partial(spectrum_kernel, vols, down, across, blo...]
    unnamed x9 -> x7, local copies, waits for them, and re-layouts: 0.09 us -> 2.11 us
    broadcast_in_dim x0 -> x1, local copies, waits for them, and re-layouts: none -> 1.73 us  [on_device(): copies = jnp.broadcast_to(template[None], (chips, *template.shape))]
    add x1 -> x0, other arithmetic: 1.38 us -> none  [on_device(): correlation + lax.ppermute(sent, 'plane', [(j, (j + step) % plane_size) f...]
  transfers between devices with their start and end apart: 10 -> 5, of which waited for: 4 -> 3; matrix products, arithmetic and copies ran while one was open for 5% -> 4% of each run, Pallas kernels for 28% -> 12%
where the time goes in v2:
time: 66.6 us; the launch traced here: 66.1 us
  waiting for transfers between devices  29.4 us (44%)
  Pallas kernels  16.9 us (25%)
  starting transfers between devices  14.5 us (22%)
  local copies, waits for them, and re-layouts  3.89 us (6%)
  other arithmetic  0.77 us (1%)
  between operations  0.67 us (1%)
    all_to_all x1, waiting for transfers between devices, on_device(): moved.append(lax.all_to_all(warped, 'chip', 0, 0, tiled=True))  14.4 us
    all_to_all x1, waiting for transfers between devices, on_device(): gathered = lax.all_to_all(copies, 'chip', 0, 0, tiled=True)  13.8 us
    pallas_call x1, Pallas kernels, lag_windows(): pl.pallas_call(functools.partial(spectrum_kernel, vols, down, across, blo...  8.87 us
    pallas_call x1, Pallas kernels, warp_sums(): pl.pallas_call(functools.partial(warp_kernel, vols, down, across, block,...  8.05 us
    all_to_all x1, starting transfers between devices, on_device(): gathered = lax.all_to_all(copies, 'chip', 0, 0, tiled=True)  6.85 us
    all_to_all x1, starting transfers between devices, on_device(): moved.append(lax.all_to_all(warped, 'chip', 0, 0, tiled=True))  3.65 us
    all_to_all x1, starting transfers between devices, on_device(): window = lax.all_to_all(window, ('core', 'plane'), 0, 0, tiled=True)  3.28 us
    unnamed x7, local copies, waits for them, and re-layouts  2.11 us
  transfers between devices with their start and end apart: 5, of which 3 were waited for; matrix products, arithmetic and copies ran while one was open for 4% of the time, Pallas kernels for 12%

profile of v2, /device:TPU:0, one launch (start us, length us, event | category | flops | bytes accessed | tf_op | source)
XLA Modules:
  0.0 66.1 jit_solution(3562530524971988608)
XLA Ops:
  0.6 0.5 collective-permute-start.1
  1.1 1.7 %broadcast_in_dim.9 = bf16[8,2,1,128,128]{4,3,1,2,0:T(8,128)(2,1)} broadcast(bf16[2,128,128]{2,1,0:T(8,128)(2,1)} %bitcast.26), dimensions={1,3,4} | broadcast | bytes 589824 | tf_op jit(solution)/shard_map/broadcast_in_dim | solution.py:389
  2.9 6.8 %all-to-all-start = ((bf16[8,2,1,128,128]{4,3,1,2,0:T(8,128)(2,1)}), bf16[8,2,1,128,128]{4,3,1,2,0:T(8,128)(2,1)S(1)}, u32[]{:S(2)}, u32[]{:S(2)}) async-start(bf16[8,2,1,128,128]{4,3,1,2,0:T(8,128)(2,1)} %broadcast_in_dim.9), calls=%async_computation | async-start | bytes 1048576 | tf_op jit(solution)/shard_map/all_to_all | solution.py:390
  9.7 0.2 collective-permute-start
  9.9 1.2 %collective-permute-done.other_codes_ref = s32[2,2,32]{2,1,0:T(2,128)S(1)} collective-permute-done((s32[2,2,32]{2,1,0:T(2,128)}, s32[2,2,32]{2,1,0:T(2,128)S(1)}, u32[]{:S(2)}, u32[]{:S(2)}) %collective-permute-start) | collective-permute-done | bytes 544 | tf_op jit(solution)/shard_map/ppermute | solution.py:388
  11.1 0.0 copy-start.2
  11.1 13.8 %all-to-all-done = bf16[8,2,1,128,128]{4,3,1,2,0:T(8,128)(2,1)S(1)} async-done(((bf16[8,2,1,128,128]{4,3,1,2,0:T(8,128)(2,1)}), bf16[8,2,1,128,128]{4,3,1,2,0:T(8,128)(2,1)S(1)}, u32[]{:S(2)}, u32[]{:S(2)}) %all-to-all-start) | async-done | bytes 524320 | tf_op jit(solution)/shard_map/all_to_all | solution.py:390
  24.9 0.0 copy-start.1
  24.9 0.0 collective-permute-done.1
  24.9 0.0 copy-start
  24.9 0.0 copy-done.2
  24.9 0.8 %copy-done.1 = bf16[8,2,1,128,128]{4,3,1,2,0:T(8,128)(2,1)} copy-done((bf16[8,2,1,128,128]{4,3,1,2,0:T(8,128)(2,1)}, bf16[8,2,1,128,128]{4,3,1,2,0:T(8,128)(2,1)S(1)}, u32[]{:S(2)}) %copy-start.1) | copy-done | bytes 524312
  25.7 0.7 %copy-done = bf16[2,1,512,1024]{3,2,0,1:T(8,128)(2,1)} copy-done((bf16[2,1,512,1024]{3,2,0,1:T(8,128)(2,1)}, bf16[2,1,512,1024]{3,2,0,1:T(8,128)(2,1)S(1)}, u32[]{:S(2)}) %copy-start) | copy-done | bytes 2097176
  26.4 8.9 %lag_windows.1 = f32[4,2,8,256]{3,2,1,0:T(8,128)} custom-call(s32[1]{0:T(128)} %bitcast.core_ref, s32[2,2,32]{2,1,0:T(2,128)} %codes_ref.3, s32[2,2,32]{2,1,0:T(2,128)} %copy-done.2, bf16[128,256]{1,0:T(8,128)(2,1)} %constant.19.clone.row_ref, bf16[144,256]{1,0:T(8,128)(2,1)} %constant.20.clone.col_ref, bf16[16,32,144]{2,1,0:T(8,128)(2,1)} %constant.21.clone.lag_ref, ...), custom_call_target="tpu_custom_call" | custom-call | flops 1610612736 | bytes 4718592 | tf_op jit(solution)/shard_map/lag_windows/pallas_call | solution.py:350
  35.2 3.3 %all-to-all-start.1 = ((f32[4,2,8,256]{3,2,1,0:T(8,128)}), f32[4,2,8,256]{3,2,1,0:T(8,128)S(1)}, u32[]{:S(2)}, u32[]{:S(2)}) async-start(f32[4,2,8,256]{3,2,1,0:T(8,128)} %lag_windows.1), calls=%async_computation.1 | async-start | bytes 131072 | tf_op jit(solution)/shard_map/all_to_all | solution.py:398
  38.5 8.0 %warp.1 = bf16[16,128,128]{2,1,0:T(8,128)(2,1)} custom-call(s32[1]{0:T(128)} %bitcast.core_ref, s32[2,2,32]{2,1,0:T(2,128)} %codes_ref.3, s32[2,2,32]{2,1,0:T(2,128)} %copy-done.2, f32[16,16,128]{2,1,0:T(8,128)} %constant.18.clone.taps_ref, bf16[2,512,1024]{2,1,0:T(8,128)(2,1)} %bitcast.15, bf16[2,512,1024]{2,1,0:T(8,128)(2,1)} %bitcast.16, ...), custom_call_target="tpu_custom_call" | custom-call | flops 1073741824 | bytes 4718592 | tf_op jit(solution)/shard_map/warp/pallas_call | solution.py:182
  46.6 0.0 all-to-all-done.1
  46.6 3.6 %all-to-all-start.2 = ((bf16[8,2,128,128]{3,2,1,0:T(8,128)(2,1)}), bf16[8,2,128,128]{3,2,1,0:T(8,128)(2,1)S(1)}, u32[]{:S(2)}, u32[]{:S(2)}) async-start(bf16[8,2,128,128]{3,2,1,0:T(8,128)(2,1)} %bitcast.22), calls=%async_computation.2 | async-start | bytes 1048576 | tf_op jit(solution)/shard_map/all_to_all | solution.py:396
  50.3 0.6 copy.14
  51.0 14.4 %all-to-all-done.2 = bf16[8,2,128,128]{3,2,1,0:T(8,128)(2,1)S(1)} async-done(((bf16[8,2,128,128]{3,2,1,0:T(8,128)(2,1)}), bf16[8,2,128,128]{3,2,1,0:T(8,128)(2,1)S(1)}, u32[]{:S(2)}, u32[]{:S(2)}) %all-to-all-start.2) | async-done | bytes 524320 | tf_op jit(solution)/shard_map/all_to_all | solution.py:396
  65.4 0.1 convert_reduce_fusion
  65.5 0.7 %multiply_bitcast_fusion = f32[2,1,128,128]{3,2,1,0:T(8,128)} fusion(f32[2,128,128]{2,1,0:T(8,128)S(1)} %convert_reduce_fusion), kind=kLoop, calls=%fused_computation.1 | loop fusion | flops 32768 | bytes 262144 | tf_op jit(solution)/shard_map/mul | solution.py:404
  (3 shorter events, 0.1 us)
Async XLA Ops:
  0.6 24.2 %collective-permute-start.1 = (bf16[2,1,512,1024]{3,2,0,1:T(8,128)(2,1)}, bf16[2,1,512,1024]{3,2,0,1:T(8,128)(2,1)S(1)}, u32[]{:S(2)}, u32[]{:S(2)}) collective-permute-start(bf16[2,1,512,1024]{3,2,0,1:T(8,128)(2,1)} %bitcast.13), channel_id=1, source_target_pairs={{0,2},{2,0},{1,3},{3,1},{4,6},{6,4},{5,7},{7,5},{8,10},{10,8},{9,1... | collective-permute-start | bytes 6291464 | tf_op jit(solution)/shard_map/ppermute | solution.py:387
  2.9 22.0 %all-to-all-start = ((bf16[8,2,1,128,128]{4,3,1,2,0:T(8,128)(2,1)}), bf16[8,2,1,128,128]{4,3,1,2,0:T(8,128)(2,1)S(1)}, u32[]{:S(2)}, u32[]{:S(2)}) async-start(bf16[8,2,1,128,128]{4,3,1,2,0:T(8,128)(2,1)} %broadcast_in_dim.9), calls=%async_computation | async-start | bytes 1048576 | tf_op jit(solution)/shard_map/all_to_all | solution.py:390
  9.7 1.4 %collective-permute-start = (s32[2,2,32]{2,1,0:T(2,128)}, s32[2,2,32]{2,1,0:T(2,128)S(1)}, u32[]{:S(2)}, u32[]{:S(2)}) collective-permute-start(s32[2,2,32]{2,1,0:T(2,128)} %codes_ref.3), channel_id=1, source_target_pairs={{0,2},{2,0},{1,3},{3,1},{4,6},{6,4},{5,7},{7,5},{8,10},{10,8},{9,1... | collective-permute-start | bytes 1544 | tf_op jit(solution)/shard_map/ppermute | solution.py:388
  11.1 13.8 %copy-start.2 = (s32[2,2,32]{2,1,0:T(2,128)}, s32[2,2,32]{2,1,0:T(2,128)S(1)}, u32[]{:S(2)}) copy-start(s32[2,2,32]{2,1,0:T(2,128)S(1)} %collective-permute-done.other_codes_ref) | copy-start | bytes 1540
  24.9 0.8 %copy-start.1 = (bf16[8,2,1,128,128]{4,3,1,2,0:T(8,128)(2,1)}, bf16[8,2,1,128,128]{4,3,1,2,0:T(8,128)(2,1)S(1)}, u32[]{:S(2)}) copy-start(bf16[8,2,1,128,128]{4,3,1,2,0:T(8,128)(2,1)S(1)} %all-to-all-done) | copy-start | bytes 1572868
  24.9 1.5 %copy-start = (bf16[2,1,512,1024]{3,2,0,1:T(8,128)(2,1)}, bf16[2,1,512,1024]{3,2,0,1:T(8,128)(2,1)S(1)}, u32[]{:S(2)}) copy-start(bf16[2,1,512,1024]{3,2,0,1:T(8,128)(2,1)S(1)} %collective-permute-done.1) | copy-start | bytes 6291460
  35.2 11.3 %all-to-all-start.1 = ((f32[4,2,8,256]{3,2,1,0:T(8,128)}), f32[4,2,8,256]{3,2,1,0:T(8,128)S(1)}, u32[]{:S(2)}, u32[]{:S(2)}) async-start(f32[4,2,8,256]{3,2,1,0:T(8,128)} %lag_windows.1), calls=%async_computation.1 | async-start | bytes 131072 | tf_op jit(solution)/shard_map/all_to_all | solution.py:398
  46.6 18.8 %all-to-all-start.2 = ((bf16[8,2,128,128]{3,2,1,0:T(8,128)(2,1)}), bf16[8,2,128,128]{3,2,1,0:T(8,128)(2,1)S(1)}, u32[]{:S(2)}, u32[]{:S(2)}) async-start(bf16[8,2,128,128]{3,2,1,0:T(8,128)(2,1)} %bitcast.22), calls=%async_computation.2 | async-start | bytes 1048576 | tf_op jit(solution)/shard_map/all_to_all | solution.py:396

commit v3 on v2

--- a/solution.py
+++ b/solution.py
@@ -78,13 +78,21 @@
     return middle, before, after
 
 
+def local_places(band, across, own, core, row):
+    return [
+        (2 * (2 * group + row) + core) * own + one
+        for group in range(across // (4 * own))
+        for one in range(own)
+    ]
+
+
 def warp_kernel(
     vols,
     down,
     across,
     block,
     own,
-    core_ref,
+    place_ref,
     codes_ref,
     other_codes_ref,
     taps_ref,
@@ -94,6 +102,7 @@
     other_mid_ref,
     other_above_ref,
     other_below_ref,
+    after_ref,
     out_ref,
 ):
     band = pl.program_id(0)
@@ -113,8 +122,7 @@
         below = jnp.where(band < down - 1, below[v, :, lanes], zero)
         return jnp.concatenate([mid[v, :, lanes], below, above], axis=0)
 
-    for count in range(across // 2):
-        at = (2 * (count // own) + core_ref[0]) * own + count % own
+    for count, at in enumerate(local_places(band, across, own, place_ref[0], place_ref[1])):
         index = band * across + at
         row_tiles, first_edge, last_edge = [], [], []
         partials, edges = [], []
@@ -165,7 +173,7 @@
         out_ref[count] = total.astype(jnp.bfloat16)
 
 
-def warp_sums(core, codes, other_codes, frames, other_frames, block, own):
+def warp_sums(place, codes, other_codes, frames, other_frames, after, block, own):
     vols, rows, cols = frames.shape
     down, across = rows // block, cols // block
     steps = block // EDGE
@@ -182,7 +190,7 @@
     return pl.pallas_call(
         functools.partial(warp_kernel, vols, down, across, block, own),
         grid=(down,),
-        out_shape=jax.ShapeDtypeStruct((down * across // 2, block, block), jnp.bfloat16),
+        out_shape=jax.ShapeDtypeStruct((down * across // 4, block, block), jnp.bfloat16),
         in_specs=[
             smem,
             smem,
@@ -190,16 +198,17 @@
             pl.BlockSpec(taps.shape, lambda band: (0, 0, 0)),
             *frame_specs,
             *frame_specs,
+            pl.BlockSpec(memory_space=pl.ANY),
         ],
-        out_specs=pl.BlockSpec((across // 2, block, block), lambda band: (band, 0, 0)),
+        out_specs=pl.BlockSpec((across // 4, block, block), lambda band: (band, 0, 0)),
         compiler_params=pltpu.CompilerParams(vmem_limit_bytes=VMEM_LIMIT),
         cost_estimate=pl.CostEstimate(
-            flops=2 * vols * rows * cols * block * 4,
-            bytes_accessed=vols * rows * cols * 4 + rows * cols,
+            flops=2 * vols * rows * cols * block * 2,
+            bytes_accessed=vols * rows * cols * 4 + rows * cols // 2,
             transcendentals=0,
         ),
         name="warp",
-    )(core, codes, other_codes, taps, *([frames] * 3), *([other_frames] * 3))
+    )(place, codes, other_codes, taps, *([frames] * 3), *([other_frames] * 3), after)
 
 
 def spectrum_kernel(
@@ -209,7 +218,7 @@
     block,
     own,
     planes,
-    core_ref,
+    place_ref,
     codes_ref,
     other_codes_ref,
     row_ref,
@@ -219,13 +228,14 @@
     frames_ref,
     other_frames_ref,
     template_ref,
+    after_ref,
     out_ref,
     cross,
     sums,
     found,
 ):
     band = pl.program_id(0)
-    core = core_ref[0]
+    core = place_ref[0]
     row_table = row_ref[...]
     col_table = col_ref[...]
     half = col_table.shape[0] // 2
@@ -233,8 +243,8 @@
     volumes = [(codes_ref, frames_ref, v) for v in range(vols)]
     volumes += [(other_codes_ref, other_frames_ref, v) for v in range(vols)]
     many = len(volumes)
-    local = across // 2
-    places = [(2 * (count // own) + core) * own + count % own for count in range(local)]
+    local = across // 4
+    places = local_places(band, across, own, core, place_ref[1])
 
     for pair in range(local // 2):
         pair_places = places[2 * pair : 2 * pair + 2]
@@ -333,7 +343,7 @@
                     out_ref[owner * planes + plane, order % vols, :, lanes] = total * (1.0 / block)
 
 
-def lag_windows(core, codes, other_codes, frames, other_frames, template, planes, own):
+def lag_windows(place, codes, other_codes, frames, other_frames, template, after, planes, own):
     vols, rows, cols = frames.shape
     block = template.shape[-1]
     down, across = rows // block, cols // block
@@ -345,7 +355,7 @@
     ]
     smem = pl.BlockSpec(memory_space=pltpu.SMEM)
     frame_spec = pl.BlockSpec((vols, block, cols), lambda band: (0, band, 0))
-    local = down * across // 2
+    local = down * across // 4
     out_dims = (2 * planes, vols, local // planes, WIN * WIN)
     return pl.pallas_call(
         functools.partial(spectrum_kernel, vols, down, across, block, own, planes),
@@ -358,12 +368,13 @@
             *whole,
             frame_spec,
             frame_spec,
-            pl.BlockSpec((across // 2, block, block), lambda band: (band, 0, 0)),
+            pl.BlockSpec((across // 4, block, block), lambda band: (band, 0, 0)),
+            pl.BlockSpec(memory_space=pl.ANY),
         ],
         out_specs=pl.BlockSpec(out_dims, lambda band: (0, 0, 0, 0)),
         scratch_shapes=[
-            pltpu.VMEM((vols * across, 3 * half, LANES), jnp.float32),
-            pltpu.VMEM((vols * across, 1, LANES), jnp.float32),
+            pltpu.VMEM((vols * across // 2, 3 * half, LANES), jnp.float32),
+            pltpu.VMEM((vols * across // 2, 1, LANES), jnp.float32),
             pltpu.VMEM((2 * vols, local * WIN, LANES), jnp.float32),
         ],
         compiler_params=pltpu.CompilerParams(vmem_limit_bytes=VMEM_LIMIT),
@@ -373,42 +384,52 @@
             transcendentals=0,
         ),
         name="lag_windows",
-    )(core, codes, other_codes, *tables, frames, other_frames, template)
+    )(place, codes, other_codes, *tables, frames, other_frames, template, after)
 
 
 def on_device(frames, template, shift_codes):
     vol_dev, pl_dev, img_rows, img_cols = frames.shape
     own, block = template.shape[0], template.shape[-1]
-    chips = lax.axis_size("chip")
+    depth = lax.axis_size("z")
     planes = lax.axis_size("plane")
-    share = 2 * chips * own // planes
-    core = lax.axis_index("core").reshape(1)
+    share = 4 * depth * own // planes
+    core, row = lax.axis_index("core"), lax.axis_index("y")
+    here, there = jnp.stack([core, row]), jnp.stack([core, 1 - row])
     swap = [(0, 1), (1, 0)]
     other_frames = lax.ppermute(frames, "core", swap)
     other_codes = lax.ppermute(shift_codes, "core", swap)
-    copies = jnp.broadcast_to(template[None], (chips, *template.shape))
-    gathered = lax.all_to_all(copies, "chip", 0, 0, tiled=True)
-    gathered = gathered.reshape(chips * own, pl_dev, block, block)
+    copies = jnp.broadcast_to(template[None], (depth, *template.shape))
+    near = lax.all_to_all(copies, "z", 0, 0, tiled=True)
+    far = lax.ppermute(near, "y", swap)
+    near = near.reshape(depth * own, pl_dev, block, block)
+    far = far.reshape(depth * own, pl_dev, block, block)
     moved, window = [], 0.0
     for p in range(pl_dev):
-        work = (core, shift_codes, other_codes, frames[:, p], other_frames[:, p])
-        warped = warp_sums(*work, block, own).reshape(chips, own, block, block)
-        moved.append(lax.all_to_all(warped, "chip", 0, 0, tiled=True))
-        window = window + lag_windows(*work, gathered[:, p], planes, own)
+        work = (shift_codes, other_codes, frames[:, p], other_frames[:, p])
+        far_sums = warp_sums(there, *work, template, block, own)
+        taken = lax.ppermute(far_sums, "y", swap)
+        near_sums = warp_sums(here, *work, far_sums, block, own)
+        sums = near_sums.astype(jnp.float32) + taken.astype(jnp.float32)
+        sums = sums.astype(jnp.bfloat16).reshape(depth, own, block, block)
+        moved.append(lax.all_to_all(sums, "z", 0, 0, tiled=True))
+        near_window = lag_windows(here, *work, near[:, p], sums, planes, own)
+        far_window = lag_windows(there, *work, far[:, p], near_window, planes, own)
+        window = window + jnp.stack([near_window, far_window], axis=1)
     window = lax.all_to_all(window, ("core", "plane"), 0, 0, tiled=True)
-    window = window.reshape(2, planes, vol_dev, share // (2 * own), own, WIN * WIN)
+    window = window.reshape(2, planes, 2, vol_dev, depth // planes, own, WIN * WIN)
     window = jnp.sum(window, axis=1)
-    correlation = window.transpose(1, 2, 0, 3, 4).reshape(vol_dev, share, WIN * WIN)
-    volumes = vol_dev * chips * 2
+    window = jnp.where(row == 0, window, window[:, ::-1])
+    correlation = window.transpose(2, 3, 1, 0, 4, 5).reshape(vol_dev, share, WIN * WIN)
+    volumes = vol_dev * depth * 4
     sums = [jnp.sum(one.astype(jnp.float32), axis=0) for one in moved]
     new_template = jnp.stack(sums, axis=1) * (1.0 / volumes)
     return (correlation, new_template)
 
 
 def solution(mesh):
-    devices = mesh.devices.reshape(-1, 2, mesh.shape["plane"])
-    split = jax.sharding.Mesh(devices, ("chip", "core", "plane"))
-    vols = ("chip", "core")
+    devices = mesh.devices.reshape(-1, 2, 2, mesh.shape["plane"])
+    split = jax.sharding.Mesh(devices, ("z", "y", "core", "plane"))
+    vols = ("z", "y", "core")
     in_specs = (P(vols, "plane", None, None), P(vols, "plane", None, None), P(vols, None, None))
     out_specs = (P(vols, "plane", None), P(vols, "plane", None, None))
     return jax.shard_map(

time: 66.6 us -> 65.7 us (0.986)
  waiting for transfers between devices: 29.4 us -> 9.07 us
  Pallas kernels: 16.9 us -> 25.9 us
  blocking collectives: 0 us -> 6.69 us
  other arithmetic: 0.77 us -> 4.49 us
  starting transfers between devices: 14.5 us -> 13.7 us
    all_to_all x3 -> x2, waiting for transfers between devices: 28.2 us -> 7.91 us  [the longest x1 7.91 us: on_device(): moved.append(lax.all_to_all(sums, 'z', 0, 0, tiled=True))]
    all_to_all x0 -> x1, blocking collectives: none -> 6.69 us  [on_device(): window = lax.all_to_all(window, ('core', 'plane'), 0, 0, tiled=True)]
    pallas_call x1 -> x2, Pallas kernels: 8.87 us -> 13.8 us  [lag_windows(): pl.pallas_call(functools.partial(spectrum_kernel, vols, down, across, blo...]
    pallas_call x1 -> x2, Pallas kernels: 8.05 us -> 12.1 us  [warp_sums(): pl.pallas_call(functools.partial(warp_kernel, vols, down, across, block,...]
    all_to_all x3 -> x2, starting transfers between devices: 13.8 us -> 11 us  [the longest x1 5.88 us: on_device(): near = lax.all_to_all(copies, 'z', 0, 0, tiled=True)]
    ppermute x0 -> x2, starting transfers between devices: none -> 2.03 us  [the longest x1 1.51 us: on_device(): taken = lax.ppermute(far_sums, 'y', swap)]
    another operation x0 -> x3, other arithmetic: none -> 2.02 us  [the longest x2 1.24 us: on_device(): here, there = (jnp.stack([core, row]), jnp.stack([core, 1 - row]))]
    convert_element_type x0 -> x1, other arithmetic: none -> 1.72 us  [on_device(): sums = sums.astype(jnp.bfloat16).reshape(depth, own, block, block)]
  transfers between devices with their start and end apart: 5 -> 6, of which waited for: 3 -> 3; matrix products, arithmetic and copies ran while one was open for 4% -> 8% of each run, Pallas kernels for 12% -> 29%
where the time goes in v3:
time: 65.7 us; the launch traced here: 64.9 us
  Pallas kernels  25.9 us (39%)
  starting transfers between devices  13.7 us (21%)
  waiting for transfers between devices  9.07 us (14%)
  blocking collectives  6.69 us (10%)
  other arithmetic  4.49 us (7%)
  local copies, waits for them, and re-layouts  4.31 us (7%)
  between operations  0.7 us (1%)
    pallas_call x2, Pallas kernels, lag_windows(): pl.pallas_call(functools.partial(spectrum_kernel, vols, down, across, blo...  13.8 us
    pallas_call x2, Pallas kernels, warp_sums(): pl.pallas_call(functools.partial(warp_kernel, vols, down, across, block,...  12.1 us
    all_to_all x1, waiting for transfers between devices, on_device(): moved.append(lax.all_to_all(sums, 'z', 0, 0, tiled=True))  7.91 us
    all_to_all x1, blocking collectives, on_device(): window = lax.all_to_all(window, ('core', 'plane'), 0, 0, tiled=True)  6.69 us
    all_to_all x1, starting transfers between devices, on_device(): near = lax.all_to_all(copies, 'z', 0, 0, tiled=True)  5.88 us
    all_to_all x1, starting transfers between devices, on_device(): moved.append(lax.all_to_all(sums, 'z', 0, 0, tiled=True))  5.09 us
    unnamed x12, local copies, waits for them, and re-layouts  2.67 us
    convert_element_type x1, other arithmetic, on_device(): sums = sums.astype(jnp.bfloat16).reshape(depth, own, block, block)  1.72 us
  transfers between devices with their start and end apart: 6, of which 3 were waited for; matrix products, arithmetic and copies ran while one was open for 8% of the time, Pallas kernels for 29%

profile of v3, /device:TPU:0, one launch (start us, length us, event | category | flops | bytes accessed | tf_op | source)
XLA Modules:
  0.0 64.9 jit_solution(7681676550159606329)
XLA Ops:
  0.6 0.5 collective-permute-start.1
  1.1 1.6 %broadcast_in_dim.9 = bf16[4,2,1,128,128]{4,3,1,2,0:T(8,128)(2,1)} broadcast(bf16[2,128,128]{2,1,0:T(8,128)(2,1)} %bitcast.34), dimensions={1,3,4} | broadcast | bytes 327680 | tf_op jit(solution)/shard_map/broadcast_in_dim | solution.py:401
  2.7 5.9 %all-to-all-start = ((bf16[4,2,1,128,128]{4,3,1,2,0:T(8,128)(2,1)}), bf16[4,2,1,128,128]{4,3,1,2,0:T(8,128)(2,1)S(1)}, u32[]{:S(2)}, u32[]{:S(2)}) async-start(bf16[4,2,1,128,128]{4,3,1,2,0:T(8,128)(2,1)} %broadcast_in_dim.9), calls=%async_computation | async-start | bytes 524288 | tf_op jit(solution)/shard_map/all_to_all | solution.py:402
  8.6 0.2 collective-permute-start
  8.8 0.6 pad_add_fusion.1.place_ref
  9.4 0.6 collective-permute-done.other_codes_ref
  10.0 0.6 copy-done.3
  10.5 0.8 %copy-done = bf16[2,1,512,1024]{3,2,0,1:T(8,128)(2,1)} copy-done((bf16[2,1,512,1024]{3,2,0,1:T(8,128)(2,1)}, bf16[2,1,512,1024]{3,2,0,1:T(8,128)(2,1)S(1)}, u32[]{:S(2)}) %copy-start) | copy-done | bytes 2097176
  11.3 6.1 %warp.2.after_ref = bf16[8,128,128]{2,1,0:T(8,128)(2,1)} custom-call(s32[2]{0:T(128)} %pad_add_fusion.1.place_ref, s32[2,2,32]{2,1,0:T(2,128)} %codes_ref.7, s32[2,2,32]{2,1,0:T(2,128)} %copy-done.3, f32[16,16,128]{2,1,0:T(8,128)} %constant.26.clone.taps_ref, bf16[2,512,1024]{2,1,0:T(8,128)(2,1)} %bitcast.18, bf16[2,512,1024]{2,1,0:T(8,128)(2,1)} %bitcast.19, ...), custom_call_target="tpu_custom_call" | custom-call | flops 536870912 | bytes 4456448 | tf_op jit(solution)/shard_map/warp/pallas_call | solution.py:190
  17.4 1.5 %collective-permute-start.2 = (bf16[8,128,128]{2,1,0:T(8,128)(2,1)}, bf16[8,128,128]{2,1,0:T(8,128)(2,1)S(1)}, u32[]{:S(2)}, u32[]{:S(2)}) collective-permute-start(bf16[8,128,128]{2,1,0:T(8,128)(2,1)} %warp.2.after_ref), channel_id=1, source_target_pairs={{0,4},{4,0},{1,5},{5,1},{2,6},{6,2},{3,7},{7,3},{8,12},{12,8},{9,1... | collective-permute-start | bytes 786440 | tf_op jit(solution)/shard_map/ppermute | solution.py:410
  18.9 0.7 %pad_add_fusion.place_ref = s32[2]{0:T(128)} fusion(s32[1]{0:T(128)} %bitcast.1, s32[1]{0:T(128)} %bitcast), kind=kLoop, calls=%fused_computation.6 | loop fusion | flops 2 | bytes 16 | tf_op jit(solution)/shard_map/stack | solution.py:397
  19.6 0.5 collective-permute-start.3
  20.1 6.1 %warp.3 = bf16[8,128,128]{2,1,0:T(8,128)(2,1)} custom-call(s32[2]{0:T(128)} %pad_add_fusion.place_ref, s32[2,2,32]{2,1,0:T(2,128)} %codes_ref.7, s32[2,2,32]{2,1,0:T(2,128)} %copy-done.3, f32[16,16,128]{2,1,0:T(8,128)} %constant.26.clone.taps_ref, bf16[2,512,1024]{2,1,0:T(8,128)(2,1)} %bitcast.21, bf16[2,512,1024]{2,1,0:T(8,128)(2,1)} %bitcast.22, ...), custom_call_target="tpu_custom_call" | custom-call | flops 536870912 | bytes 4456448 | tf_op jit(solution)/shard_map/warp/pallas_call | solution.py:190
  26.2 0.6 collective-permute-done.2
  26.7 1.7 %add_convert_fusion = bf16[8,128,128]{2,1,0:T(8,128)(2,1)} fusion(bf16[8,128,128]{2,1,0:T(8,128)(2,1)S(1)} %collective-permute-done.2, bf16[8,128,128]{2,1,0:T(8,128)(2,1)} %warp.3), kind=kLoop, calls=%fused_computation.1 | loop fusion | flops 524288 | bytes 786432 | tf_op jit(solution)/shard_map/convert_element_type | solution.py:413
  28.5 6.9 %lag_windows.2.after_ref = f32[4,2,4,256]{3,2,1,0:T(4,128)} custom-call(s32[2]{0:T(128)} %pad_add_fusion.place_ref, s32[2,2,32]{2,1,0:T(2,128)} %codes_ref.7, s32[2,2,32]{2,1,0:T(2,128)} %copy-done.3, bf16[128,256]{1,0:T(8,128)(2,1)} %constant.27.clone.row_ref, bf16[144,256]{1,0:T(8,128)(2,1)} %constant.28.clone.col_ref, ...), custom_call_target="tpu_custom_call" | custom-call | flops 1610612736 | bytes 4718592 | tf_op jit(solution)/shard_map/lag_windows/pallas_call | solution.py:360
  35.4 0.7 %copy-done.4 = bf16[4,2,1,128,128]{4,3,1,2,0:T(8,128)(2,1)} copy-done((bf16[4,2,1,128,128]{4,3,1,2,0:T(8,128)(2,1)}, bf16[4,2,1,128,128]{4,3,1,2,0:T(8,128)(2,1)S(1)}, u32[]{:S(2)}) %copy-start.4) | copy-done | bytes 262168
  36.1 6.9 %lag_windows.3 = f32[4,2,4,256]{3,2,1,0:T(4,128)} custom-call(s32[2]{0:T(128)} %pad_add_fusion.1.place_ref, s32[2,2,32]{2,1,0:T(2,128)} %codes_ref.7, s32[2,2,32]{2,1,0:T(2,128)} %copy-done.3, bf16[128,256]{1,0:T(8,128)(2,1)} %constant.27.clone.row_ref, bf16[144,256]{1,0:T(8,128)(2,1)} %constant.28.clone.col_ref, ...), custom_call_target="tpu_custom_call" | custom-call | flops 1610612736 | bytes 4718592 | tf_op jit(solution)/shard_map/lag_windows/pallas_call | solution.py:360
  43.0 0.8 %pad_maximum_fusion = f32[4,2,2,4,256]{4,3,2,0,1:T(4,128)S(1)} fusion(f32[4,1,2,4,256]{4,3,2,0,1:T(4,128)} %bitcast.38, f32[4,1,2,4,256]{4,3,2,0,1:T(4,128)S(1)} %bitcast.37), kind=kLoop, calls=%fused_computation.3 | loop fusion | flops 16384 | bytes 131072 | tf_op jit(solution)/shard_map/stack | solution.py:417
  43.8 6.7 %all_to_all.15 = f32[4,2,2,4,256]{4,3,2,1,0:T(4,128)S(1)} all-to-all(f32[4,2,2,4,256]{4,3,2,1,0:T(4,128)S(1)} %copy.20), channel_id=1, replica_groups=mesh['z'=4,'y'=2,'core'=2,'plane'=2] {'core','plane'}, dimensions={0} | all-to-all | bytes 131072 | tf_op jit(solution)/shard_map/all_to_all | solution.py:418
  50.5 5.1 %all-to-all-start.2 = ((bf16[4,2,128,128]{3,2,1,0:T(8,128)(2,1)}), bf16[4,2,128,128]{3,2,1,0:T(8,128)(2,1)S(1)}, u32[]{:S(2)}, u32[]{:S(2)}) async-start(bf16[4,2,128,128]{3,2,1,0:T(8,128)(2,1)} %bitcast.8.after_ref), calls=%async_computation.2 | async-start | bytes 524288 | tf_op jit(solution)/shard_map/all_to_all | solution.py:414
  55.7 0.6 copy.23
  56.3 7.9 %all-to-all-done.2 = bf16[4,2,128,128]{3,2,1,0:T(8,128)(2,1)S(1)} async-done(((bf16[4,2,128,128]{3,2,1,0:T(8,128)(2,1)}), bf16[4,2,128,128]{3,2,1,0:T(8,128)(2,1)S(1)}, u32[]{:S(2)}, u32[]{:S(2)}) %all-to-all-start.2) | async-done | bytes 262176 | tf_op jit(solution)/shard_map/all_to_all | solution.py:414
  64.3 0.7 %multiply_bitcast_fusion = f32[2,1,128,128]{3,2,1,0:T(8,128)} fusion(f32[2,128,128]{2,1,0:T(8,128)S(1)} %convert_reduce_fusion), kind=kLoop, calls=%fused_computation.2 | loop fusion | flops 32768 | bytes 262144 | tf_op jit(solution)/shard_map/mul | solution.py:425
  (17 shorter events, 0.2 us)
Async XLA Ops:
  0.6 9.3 %collective-permute-start.1 = (bf16[2,1,512,1024]{3,2,0,1:T(8,128)(2,1)}, bf16[2,1,512,1024]{3,2,0,1:T(8,128)(2,1)S(1)}, u32[]{:S(2)}, u32[]{:S(2)}) collective-permute-start(bf16[2,1,512,1024]{3,2,0,1:T(8,128)(2,1)} %bitcast.17), channel_id=1, source_target_pairs={{0,2},{2,0},{1,3},{3,1},{4,6},{6,4},{5,7},{7,5},{8,10},{10,8},{9,1... | collective-permute-start | bytes 6291464 | tf_op jit(solution)/shard_map/ppermute | solution.py:399
  2.7 16.9 %all-to-all-start = ((bf16[4,2,1,128,128]{4,3,1,2,0:T(8,128)(2,1)}), bf16[4,2,1,128,128]{4,3,1,2,0:T(8,128)(2,1)S(1)}, u32[]{:S(2)}, u32[]{:S(2)}) async-start(bf16[4,2,1,128,128]{4,3,1,2,0:T(8,128)(2,1)} %broadcast_in_dim.9), calls=%async_computation | async-start | bytes 524288 | tf_op jit(solution)/shard_map/all_to_all | solution.py:402
  8.6 1.4 %collective-permute-start = (s32[2,2,32]{2,1,0:T(2,128)}, s32[2,2,32]{2,1,0:T(2,128)S(1)}, u32[]{:S(2)}, u32[]{:S(2)}) collective-permute-start(s32[2,2,32]{2,1,0:T(2,128)} %codes_ref.7), channel_id=1, source_target_pairs={{0,2},{2,0},{1,3},{3,1},{4,6},{6,4},{5,7},{7,5},{8,10},{10,8},{9,1... | collective-permute-start | bytes 1544 | tf_op jit(solution)/shard_map/ppermute | solution.py:400
  10.0 0.6 copy-start.3
  10.0 1.4 %copy-start = (bf16[2,1,512,1024]{3,2,0,1:T(8,128)(2,1)}, bf16[2,1,512,1024]{3,2,0,1:T(8,128)(2,1)S(1)}, u32[]{:S(2)}) copy-start(bf16[2,1,512,1024]{3,2,0,1:T(8,128)(2,1)S(1)} %collective-permute-done.1) | copy-start | bytes 6291460
  17.4 9.3 %collective-permute-start.2 = (bf16[8,128,128]{2,1,0:T(8,128)(2,1)}, bf16[8,128,128]{2,1,0:T(8,128)(2,1)S(1)}, u32[]{:S(2)}, u32[]{:S(2)}) collective-permute-start(bf16[8,128,128]{2,1,0:T(8,128)(2,1)} %warp.2.after_ref), channel_id=1, source_target_pairs={{0,4},{4,0},{1,5},{5,1},{2,6},{6,2},{3,7},{7,3},{8,12},{12,8},{9,1... | collective-permute-start | bytes 786440 | tf_op jit(solution)/shard_map/ppermute | solution.py:410
  19.6 6.6 %copy-start.1 = (bf16[4,2,1,128,128]{4,3,1,2,0:T(8,128)(2,1)}, bf16[4,2,1,128,128]{4,3,1,2,0:T(8,128)(2,1)S(1)}, u32[]{:S(2)}) copy-start(bf16[4,2,1,128,128]{4,3,1,2,0:T(8,128)(2,1)S(1)} %all-to-all-done) | copy-start | bytes 786436
  19.6 15.8 %collective-permute-start.3 = (bf16[4,2,1,128,128]{4,3,1,2,0:T(8,128)(2,1)S(1)}, bf16[4,2,1,128,128]{4,3,1,2,0:T(8,128)(2,1)S(1)}, u32[]{:S(2)}, u32[]{:S(2)}) collective-permute-start(bf16[4,2,1,128,128]{4,3,1,2,0:T(8,128)(2,1)S(1)} %all-to-all-done), channel_id=1, source_target_pairs={{0,4},{4,0},{1,5},{5,1},{2,6},{6,2},{3,7},{7,3},{8,12},{12,8},{9,1... | collective-permute-start | bytes 786440 | tf_op jit(solution)/shard_map/ppermute | solution.py:403
  35.4 0.7 %copy-start.4 = (bf16[4,2,1,128,128]{4,3,1,2,0:T(8,128)(2,1)}, bf16[4,2,1,128,128]{4,3,1,2,0:T(8,128)(2,1)S(1)}, u32[]{:S(2)}) copy-start(bf16[4,2,1,128,128]{4,3,1,2,0:T(8,128)(2,1)S(1)} %collective-permute-done.3) | copy-start | bytes 786436
  36.1 6.9 %copy-start.2 = (f32[4,2,4,256]{3,2,1,0:T(4,128)S(1)}, f32[4,2,4,256]{3,2,1,0:T(4,128)}, u32[]{:S(2)}) copy-start(f32[4,2,4,256]{3,2,1,0:T(4,128)} %lag_windows.2.after_ref) | copy-start | bytes 98308
  50.5 13.8 %all-to-all-start.2 = ((bf16[4,2,128,128]{3,2,1,0:T(8,128)(2,1)}), bf16[4,2,128,128]{3,2,1,0:T(8,128)(2,1)S(1)}, u32[]{:S(2)}, u32[]{:S(2)}) async-start(bf16[4,2,128,128]{3,2,1,0:T(8,128)(2,1)} %bitcast.8.after_ref), calls=%async_computation.2 | async-start | bytes 524288 | tf_op jit(solution)/shard_map/all_to_all | solution.py:414

commit v4 on v2

--- a/solution.py
+++ b/solution.py
@@ -15,7 +15,7 @@
 SUB = 16
 EDGE = 16
 LANES = 128
-VMEM_LIMIT = 56 * 1024 * 1024
+VMEM_LIMIT = 24 * 1024 * 1024
 
 full_turn = 2.0 * math.pi
 
@@ -78,13 +78,27 @@
     return middle, before, after
 
 
+def step_places(place_ref, across, own):
+    z = place_ref[0] ^ pl.program_id(0)
+    places = []
+    for other in range(2):
+        for one in range(own):
+            index = ((2 * z + (place_ref[1] ^ other)) * 2 + place_ref[2]) * own + one
+            places.append((index, index % across))
+    return places
+
+
+def step_band(place_ref, step, across, own):
+    return (place_ref[0] ^ step) * (4 * own) // across
+
+
 def warp_kernel(
     vols,
     down,
     across,
     block,
     own,
-    core_ref,
+    place_ref,
     codes_ref,
     other_codes_ref,
     taps_ref,
@@ -94,13 +108,15 @@
     other_mid_ref,
     other_above_ref,
     other_below_ref,
-    out_ref,
+    *out_refs,
 ):
-    band = pl.program_id(0)
+    step = pl.program_id(0)
+    band = step_band(place_ref, step, across, own)
     lane = lax.broadcasted_iota(jnp.int32, (EDGE, LANES), 1)
     tall_lane = lax.broadcasted_iota(jnp.int32, (block + 2 * EDGE, LANES), 1)
     zero = jnp.zeros((EDGE, LANES), jnp.bfloat16)
     no_tile = jnp.zeros((block + 2 * EDGE, block), jnp.bfloat16)
+    *out_refs, sums = out_refs
     volumes = [(codes_ref, mid_ref, above_ref, below_ref, v) for v in range(vols)]
     volumes += [
         (other_codes_ref, other_mid_ref, other_above_ref, other_below_ref, v) for v in range(vols)
@@ -113,9 +129,7 @@
         below = jnp.where(band < down - 1, below[v, :, lanes], zero)
         return jnp.concatenate([mid[v, :, lanes], below, above], axis=0)
 
-    for count in range(across // 2):
-        at = (2 * (count // own) + core_ref[0]) * own + count % own
-        index = band * across + at
+    for count, (index, at) in enumerate(step_places(place_ref, across, own)):
         row_tiles, first_edge, last_edge = [], [], []
         partials, edges = [], []
         for order, volume in enumerate(volumes):
@@ -162,36 +176,52 @@
             jnp.concatenate(partials + edges, axis=0),
             preferred_element_type=jnp.float32,
         )
-        out_ref[count] = total.astype(jnp.bfloat16)
-
-
-def warp_sums(core, codes, other_codes, frames, other_frames, block, own):
+        sums[count] = total.astype(jnp.bfloat16)
+    for at_step, out_ref in enumerate(out_refs):
+
+        @pl.when(step == at_step)
+        def _():
+            out_ref[...] = sums[...]
+
+
+def warp_sums(place, codes, other_codes, frames, other_frames, depth, block, own):
     vols, rows, cols = frames.shape
     down, across = rows // block, cols // block
     steps = block // EDGE
     taps = tap_constants()
     smem = pl.BlockSpec(memory_space=pltpu.SMEM)
+
+    def above(step, place):
+        return (0, jnp.maximum(step_band(place, step, across, own) * steps - 1, 0), 0)
+
+    def below(step, place):
+        last = down * steps - 1
+        return (0, jnp.minimum((step_band(place, step, across, own) + 1) * steps, last), 0)
+
     frame_specs = [
-        pl.BlockSpec((vols, block, cols), lambda band: (0, band, 0)),
-        pl.BlockSpec((vols, EDGE, cols), lambda band: (0, jnp.maximum(band * steps - 1, 0), 0)),
         pl.BlockSpec(
-            (vols, EDGE, cols),
-            lambda band: (0, jnp.minimum((band + 1) * steps, down * steps - 1), 0),
+            (vols, block, cols), lambda step, place: (0, step_band(place, step, across, own), 0)
         ),
+        pl.BlockSpec((vols, EDGE, cols), above),
+        pl.BlockSpec((vols, EDGE, cols), below),
     ]
+    out = (2 * own, block, block)
     return pl.pallas_call(
         functools.partial(warp_kernel, vols, down, across, block, own),
-        grid=(down,),
-        out_shape=jax.ShapeDtypeStruct((down * across // 2, block, block), jnp.bfloat16),
-        in_specs=[
-            smem,
-            smem,
-            smem,
-            pl.BlockSpec(taps.shape, lambda band: (0, 0, 0)),
-            *frame_specs,
-            *frame_specs,
-        ],
-        out_specs=pl.BlockSpec((across // 2, block, block), lambda band: (band, 0, 0)),
+        grid_spec=pltpu.PrefetchScalarGridSpec(
+            num_scalar_prefetch=1,
+            grid=(depth,),
+            in_specs=[
+                smem,
+                smem,
+                pl.BlockSpec(taps.shape, lambda step, place: (0, 0, 0)),
+                *frame_specs,
+                *frame_specs,
+            ],
+            out_specs=[pl.BlockSpec(out, lambda step, place: (0, 0, 0))] * depth,
+            scratch_shapes=[pltpu.VMEM(out, jnp.bfloat16)],
+        ),
+        out_shape=[jax.ShapeDtypeStruct(out, jnp.bfloat16)] * depth,
         compiler_params=pltpu.CompilerParams(vmem_limit_bytes=VMEM_LIMIT),
         cost_estimate=pl.CostEstimate(
             flops=2 * vols * rows * cols * block * 4,
@@ -199,17 +229,17 @@
             transcendentals=0,
         ),
         name="warp",
-    )(core, codes, other_codes, taps, *([frames] * 3), *([other_frames] * 3))
+    )(place, codes, other_codes, taps, *([frames] * 3), *([other_frames] * 3))
 
 
 def spectrum_kernel(
     vols,
-    down,
     across,
     block,
     own,
     planes,
-    core_ref,
+    depth,
+    place_ref,
     codes_ref,
     other_codes_ref,
     row_ref,
@@ -218,14 +248,23 @@
     span_ref,
     frames_ref,
     other_frames_ref,
-    template_ref,
-    out_ref,
-    cross,
-    sums,
-    found,
+    *refs,
 ):
-    band = pl.program_id(0)
-    core = core_ref[0]
+    template_refs, out_refs = refs[:depth], refs[depth + 1 : depth + 1 + 2 * planes]
+    templates, cross, sums, found, sems = refs[depth + 1 + 2 * planes :]
+    step = pl.program_id(0)
+
+    @pl.when(step == 0)
+    def _():
+        copies = [
+            pltpu.make_async_copy(template_ref, templates.at[at], sems.at[at])
+            for at, template_ref in enumerate(template_refs)
+        ]
+        for copy in copies:
+            copy.start()
+        for copy in copies:
+            copy.wait()
+
     row_table = row_ref[...]
     col_table = col_ref[...]
     half = col_table.shape[0] // 2
@@ -233,14 +272,14 @@
     volumes = [(codes_ref, frames_ref, v) for v in range(vols)]
     volumes += [(other_codes_ref, other_frames_ref, v) for v in range(vols)]
     many = len(volumes)
-    local = across // 2
-    places = [(2 * (count // own) + core) * own + count % own for count in range(local)]
+    places = step_places(place_ref, across, own)
+    local = len(places)
 
     for pair in range(local // 2):
         pair_places = places[2 * pair : 2 * pair + 2]
-        parts = [template_ref[2 * pair], template_ref[2 * pair + 1]]
+        parts = [templates[step, 2 * pair], templates[step, 2 * pair + 1]]
         for _, frames, v in volumes:
-            for at in pair_places:
+            for _, at in pair_places:
                 parts.append(frames[v, :, pl.ds(pl.multiple_of(at * block, block), block)])
         rows = jnp.dot(
             jnp.concatenate(parts, axis=0), row_table, preferred_element_type=jnp.float32
@@ -287,7 +326,7 @@
     lag_sums = []
     for one in range(local * many):
         codes, _, v = volumes[one % many]
-        index = band * across + places[one // many]
+        index, _ = places[one // many]
         scale = pl.reciprocal(cross[one, 2 * half :, :] + means[one], approx=True)
         norm = jnp.concatenate(
             [
@@ -306,21 +345,22 @@
     )
     for one in range(local * many):
         codes, _, v = volumes[one % many]
-        index = band * across + places[one // many]
+        index, _ = places[one // many]
         col_shift = codes[v, 1, index] >> 4
-        start = pl.multiple_of((band * local + one // many) * WIN, WIN)
-        found[one % many, pl.ds(start, WIN), :] = pltpu.roll(
+        order = index // (2 * own) * own + one // many % own
+        found[one % many, pl.ds(pl.multiple_of(order * WIN, WIN), WIN), :] = pltpu.roll(
             lags[one * WIN : (one + 1) * WIN], LANES - SHIFT - col_shift, 1
         )
 
-    @pl.when(band == down - 1)
+    @pl.when(step == depth - 1)
     def _():
-        share = down * local // planes
+        share = depth * local // planes
         per_tile = LANES // WIN
         lane = lax.broadcasted_iota(jnp.int32, (share, LANES), 1) // WIN
-        for order in range(many):
-            owner = core if order < vols else 1 - core
-            for plane in range(planes):
+        for turn, out_ref in enumerate(out_refs):
+            plane = place_ref[3] ^ (turn % planes)
+            for v in range(vols):
+                order = turn // planes * vols + v
                 for tile in range(WIN // per_tile):
                     total = jnp.zeros((share, LANES), jnp.float32)
                     for part in range(per_tile):
@@ -329,43 +369,46 @@
                         if part:
                             one = pltpu.roll(one, part * WIN, 1)
                         total = jnp.where(lane == part, one, total)
-                    lanes = slice(tile * LANES, (tile + 1) * LANES)
-                    out_ref[owner * planes + plane, order % vols, :, lanes] = total * (1.0 / block)
-
-
-def lag_windows(core, codes, other_codes, frames, other_frames, template, planes, own):
+                    out_ref[v, :, tile * LANES : (tile + 1) * LANES] = total * (1.0 / block)
+
+
+def lag_windows(place, codes, other_codes, frames, other_frames, templates, after, planes, own):
     vols, rows, cols = frames.shape
-    block = template.shape[-1]
+    block = templates[0].shape[-1]
     down, across = rows // block, cols // block
+    depth = len(templates)
     tables = dft_constants(block)
     half = tables[1].shape[0] // 2
     whole = [
-        pl.BlockSpec(table.shape, functools.partial(lambda dims, band: (0,) * dims, table.ndim))
+        pl.BlockSpec(
+            table.shape, functools.partial(lambda dims, step, place: (0,) * dims, table.ndim)
+        )
         for table in tables
     ]
     smem = pl.BlockSpec(memory_space=pltpu.SMEM)
-    frame_spec = pl.BlockSpec((vols, block, cols), lambda band: (0, band, 0))
-    local = down * across // 2
-    out_dims = (2 * planes, vols, local // planes, WIN * WIN)
+    frame_spec = pl.BlockSpec(
+        (vols, block, cols), lambda step, place: (0, step_band(place, step, across, own), 0)
+    )
+    local = depth * 2 * own
+    many = 2 * vols * 2 * own
+    out = (vols, local // planes, WIN * WIN)
     return pl.pallas_call(
-        functools.partial(spectrum_kernel, vols, down, across, block, own, planes),
-        grid=(down,),
-        out_shape=jax.ShapeDtypeStruct(out_dims, jnp.float32),
-        in_specs=[
-            smem,
-            smem,
-            smem,
-            *whole,
-            frame_spec,
-            frame_spec,
-            pl.BlockSpec((across // 2, block, block), lambda band: (band, 0, 0)),
-        ],
-        out_specs=pl.BlockSpec(out_dims, lambda band: (0, 0, 0, 0)),
-        scratch_shapes=[
-            pltpu.VMEM((vols * across, 3 * half, LANES), jnp.float32),
-            pltpu.VMEM((vols * across, 1, LANES), jnp.float32),
-            pltpu.VMEM((2 * vols, local * WIN, LANES), jnp.float32),
-        ],
+        functools.partial(spectrum_kernel, vols, across, block, own, planes, depth),
+        grid_spec=pltpu.PrefetchScalarGridSpec(
+            num_scalar_prefetch=1,
+            grid=(depth,),
+            in_specs=[smem, smem, *whole, frame_spec, frame_spec]
+            + [pl.BlockSpec(memory_space=pl.ANY)] * (depth + 1),
+            out_specs=[pl.BlockSpec(out, lambda step, place: (0, 0, 0))] * (2 * planes),
+            scratch_shapes=[
+                pltpu.VMEM((depth, 2 * own, block, block), jnp.bfloat16),
+                pltpu.VMEM((many, 3 * half, LANES), jnp.float32),
+                pltpu.VMEM((many, 1, LANES), jnp.float32),
+                pltpu.VMEM((2 * vols, local * WIN, LANES), jnp.float32),
+                pltpu.SemaphoreType.DMA((depth,)),
+            ],
+        ),
+        out_shape=[jax.ShapeDtypeStruct(out, jnp.float32)] * (2 * planes),
         compiler_params=pltpu.CompilerParams(vmem_limit_bytes=VMEM_LIMIT),
         cost_estimate=pl.CostEstimate(
             flops=2 * 3 * rows * cols * block * 4,
@@ -373,42 +416,53 @@
             transcendentals=0,
         ),
         name="lag_windows",
-    )(core, codes, other_codes, *tables, frames, other_frames, template)
+    )(place, codes, other_codes, *tables, frames, other_frames, *templates, after)
+
+
+def exchange(value, axes, size, turn):
+    return lax.ppermute(value, axes, [(at, at ^ turn) for at in range(size)])
 
 
 def on_device(frames, template, shift_codes):
     vol_dev, pl_dev, img_rows, img_cols = frames.shape
     own, block = template.shape[0], template.shape[-1]
-    chips = lax.axis_size("chip")
+    depth = lax.axis_size("z")
     planes = lax.axis_size("plane")
-    share = 2 * chips * own // planes
-    core = lax.axis_index("core").reshape(1)
-    swap = [(0, 1), (1, 0)]
-    other_frames = lax.ppermute(frames, "core", swap)
-    other_codes = lax.ppermute(shift_codes, "core", swap)
-    copies = jnp.broadcast_to(template[None], (chips, *template.shape))
-    gathered = lax.all_to_all(copies, "chip", 0, 0, tiled=True)
-    gathered = gathered.reshape(chips * own, pl_dev, block, block)
-    moved, window = [], 0.0
+    share = 4 * depth * own // planes
+    place = jnp.stack([lax.axis_index(axis) for axis in ("z", "y", "core", "plane")])
+    other_frames = exchange(frames, "core", 2, 1)
+    other_codes = exchange(shift_codes, "core", 2, 1)
+    templates = [jnp.concatenate([template, exchange(template, "y", 2, 1)], axis=0)]
+    for turn in range(1, depth):
+        templates.append(exchange(templates[0], "z", depth, turn))
+    averages, window = [], [0.0, 0.0]
+    volumes = vol_dev * depth * 4
     for p in range(pl_dev):
-        work = (core, shift_codes, other_codes, frames[:, p], other_frames[:, p])
-        warped = warp_sums(*work, block, own).reshape(chips, own, block, block)
-        moved.append(lax.all_to_all(warped, "chip", 0, 0, tiled=True))
-        window = window + lag_windows(*work, gathered[:, p], planes, own)
-    window = lax.all_to_all(window, ("core", "plane"), 0, 0, tiled=True)
-    window = window.reshape(2, planes, vol_dev, share // (2 * own), own, WIN * WIN)
-    window = jnp.sum(window, axis=1)
-    correlation = window.transpose(1, 2, 0, 3, 4).reshape(vol_dev, share, WIN * WIN)
-    volumes = vol_dev * chips * 2
-    sums = [jnp.sum(one.astype(jnp.float32), axis=0) for one in moved]
-    new_template = jnp.stack(sums, axis=1) * (1.0 / volumes)
-    return (correlation, new_template)
+        work = (place, shift_codes, other_codes, frames[:, p], other_frames[:, p])
+        warped = warp_sums(*work, depth, block, own)
+        chosen = [one[:, p] for one in templates]
+        found = lag_windows(*work, chosen, warped[0], planes, own)
+        warped = [warped[0]] + [
+            exchange(warped[turn], "z", depth, turn) for turn in range(1, depth)
+        ]
+        sums = [sum(one[at : at + own].astype(jnp.float32) for one in warped) for at in (0, own)]
+        taken = exchange(sums[1].astype(jnp.bfloat16), "y", 2, 1)
+        averages.append((sums[0] + taken.astype(jnp.float32)) * (1.0 / volumes))
+        for turn, one in enumerate(found):
+            if turn:
+                one = exchange(one, ("core", "plane"), 2 * planes, turn)
+            window[turn // planes] += one
+    core = place[2]
+    window = [jnp.where(core == 0, *window), jnp.where(core == 0, *window[::-1])]
+    window = [one.reshape(vol_dev, share // (2 * own), 1, own, WIN * WIN) for one in window]
+    correlation = jnp.concatenate(window, axis=2).reshape(vol_dev, share, WIN * WIN)
+    return (correlation, jnp.stack(averages, axis=1))
 
 
 def solution(mesh):
-    devices = mesh.devices.reshape(-1, 2, mesh.shape["plane"])
-    split = jax.sharding.Mesh(devices, ("chip", "core", "plane"))
-    vols = ("chip", "core")
+    devices = mesh.devices.reshape(-1, 2, 2, mesh.shape["plane"])
+    split = jax.sharding.Mesh(devices, ("z", "y", "core", "plane"))
+    vols = ("z", "y", "core")
     in_specs = (P(vols, "plane", None, None), P(vols, "plane", None, None), P(vols, None, None))
     out_specs = (P(vols, "plane", None), P(vols, "plane", None, None))
     return jax.shard_map(

time: 66.6 us -> 53.4 us (0.80)
  waiting for transfers between devices: 29.4 us -> 14.1 us
  starting transfers between devices: 14.5 us -> 15.7 us
  other arithmetic: 0.77 us -> 1.7 us
    all_to_all x3 -> x0, waiting for transfers between devices: 28.2 us -> none  [the longest x1 14.4 us: on_device(): moved.append(lax.all_to_all(warped, 'chip', 0, 0, tiled=True))]
    ppermute x2 -> x13, starting transfers between devices: 0.73 us -> 15.7 us  [exchange(): return lax.ppermute(value, axes, [(at, at ^ turn) for at in range(size)])]
    all_to_all x3 -> x0, starting transfers between devices: 13.8 us -> none  [the longest x1 6.85 us: on_device(): gathered = lax.all_to_all(copies, 'chip', 0, 0, tiled=True)]
    ppermute x2 -> x13, waiting for transfers between devices: 1.16 us -> 14.1 us  [exchange(): return lax.ppermute(value, axes, [(at, at ^ turn) for at in range(size)])]
    broadcast_in_dim x1 -> x0, local copies, waits for them, and re-layouts: 1.73 us -> none  [on_device(): copies = jnp.broadcast_to(template[None], (chips, *template.shape))]
    unnamed x7 -> x16, local copies, waits for them, and re-layouts: 2.11 us -> 3.2 us
    concatenate x0 -> x2, other arithmetic: none -> 0.87 us  [the longest x1 0.86 us: on_device(): jnp.concatenate([template, exchange(template, 'y', 2, 1)], axis=0)]
    unnamed x0 -> x1, other arithmetic: none -> 0.7 us
  transfers between devices with their start and end apart: 5 -> 13, of which waited for: 3 -> 4; matrix products, arithmetic and copies ran while one was open for 4% -> 3% of each run, Pallas kernels for 12% -> 15%
where the time goes in v4:
time: 53.4 us; the launch traced here: 53.2 us
  Pallas kernels  17.1 us (32%)
  starting transfers between devices  15.7 us (29%)
  waiting for transfers between devices  14.1 us (26%)
  local copies, waits for them, and re-layouts  3.87 us (7%)
  other arithmetic  1.7 us (3%)
  between operations  0.79 us (1%)
    ppermute x13, starting transfers between devices, exchange(): return lax.ppermute(value, axes, [(at, at ^ turn) for at in range(size)])  15.7 us
    ppermute x13, waiting for transfers between devices, exchange(): return lax.ppermute(value, axes, [(at, at ^ turn) for at in range(size)])  14.1 us
    pallas_call x1, Pallas kernels, lag_windows(): pl.pallas_call(functools.partial(spectrum_kernel, vols, across, block, ow...  9.26 us
    pallas_call x1, Pallas kernels, warp_sums(): pl.pallas_call(functools.partial(warp_kernel, vols, down, across, block,...  7.84 us
    unnamed x16, local copies, waits for them, and re-layouts  3.2 us
  transfers between devices with their start and end apart: 13, of which 4 were waited for; matrix products, arithmetic and copies ran while one was open for 3% of the time, Pallas kernels for 15%

profile of v4, /device:TPU:0, one launch (start us, length us, event | category | flops | bytes accessed | tf_op | source)
XLA Modules:
  0.0 53.2 jit_solution(3417118950155445073)
XLA Ops:
  0.6 0.5 collective-permute-start.1
  1.1 2.6 %collective-permute-start.2 = (bf16[2,1,128,128]{3,2,0,1:T(8,128)(2,1)}, bf16[2,1,128,128]{3,2,0,1:T(8,128)(2,1)S(1)}, u32[]{:S(2)}, u32[]{:S(2)}) collective-permute-start(bf16[2,1,128,128]{3,2,0,1:T(8,128)(2,1)} %bitcast.29), channel_id=1, source_target_pairs={{0,4},{4,0},{1,5},{5,1},{2,6},{6,2},{3,7},{7,3},{8,12},{12,8},{9,1... | collective-permute-start | bytes 196616 | tf_op jit(solution)/shard_map/ppermute | solution.py:423
  3.7 0.2 collective-permute-start
  3.9 2.7 %collective-permute-done.2 = bf16[2,1,128,128]{3,2,0,1:T(8,128)(2,1)S(1)} collective-permute-done((bf16[2,1,128,128]{3,2,0,1:T(8,128)(2,1)}, bf16[2,1,128,128]{3,2,0,1:T(8,128)(2,1)S(1)}, u32[]{:S(2)}, u32[]{:S(2)}) %collective-permute-start.2) | collective-permute-done | bytes 65568 | tf_op jit(solution)/shard_map/ppermute | solution.py:423
  6.6 0.9 %pad_maximum_fusion = (bf16[4,1,128,128]{3,2,0,1:T(8,128)(2,1)S(1)}, bf16[4,128,128]{2,1,0:T(8,128)(2,1)S(1)}) fusion(bf16[2,1,128,128]{3,2,0,1:T(8,128)(2,1)S(1)} %collective-permute-done.2, bf16[2,1,128,128]{3,2,0,1:T(8,128)(2,1)} %bitcast.30), kind=kLoop, calls=%fused_computation | loop fusion | flops 65536 | bytes 393216 | tf_op jit(solution)/shard_map/concatenate | solution.py:435
  7.5 2.9 %collective-permute-start.4 = (bf16[4,1,128,128]{3,2,0,1:T(8,128)(2,1)S(1)}, bf16[4,1,128,128]{3,2,0,1:T(8,128)(2,1)S(1)}, u32[]{:S(2)}, u32[]{:S(2)}) collective-permute-start(bf16[4,1,128,128]{3,2,0,1:T(8,128)(2,1)S(1)} %get-tuple-element.20), channel_id=1, source_target_pairs={{0,16},{8,24},{16,0},{24,8},{1,17},{9,25},{17,1},{25,9},{2,18},{10... | collective-permute-start | bytes 393224 | tf_op jit(solution)/shard_map/ppermute | solution.py:423
  10.4 1.3 %collective-permute-start.5 = (bf16[4,1,128,128]{3,2,0,1:T(8,128)(2,1)S(1)}, bf16[4,1,128,128]{3,2,0,1:T(8,128)(2,1)S(1)}, u32[]{:S(2)}, u32[]{:S(2)}) collective-permute-start(bf16[4,1,128,128]{3,2,0,1:T(8,128)(2,1)S(1)} %get-tuple-element.20), channel_id=1, source_target_pairs={{0,24},{8,16},{16,8},{24,0},{1,25},{9,17},{17,9},{25,1},{2,26},{10... | collective-permute-start | bytes 393224 | tf_op jit(solution)/shard_map/ppermute | solution.py:423
  11.7 0.2 collective-permute-start.3
  12.0 0.1 pad_add_fusion.place_ref
  12.1 1.6 %copy-done = bf16[2,1,512,1024]{3,2,1,0:T(8,128)(2,1)S(1)} copy-done((bf16[2,1,512,1024]{3,2,1,0:T(8,128)(2,1)S(1)}, bf16[2,1,512,1024]{3,2,1,0:T(8,128)(2,1)}, u32[]{:S(2)}) %copy-start) | copy-done | bytes 2097176
  13.7 0.9 %copy-done.2 = f32[16,16,128]{2,1,0:T(8,128)S(1)} copy-done((f32[16,16,128]{2,1,0:T(8,128)S(1)}, f32[16,16,128]{2,1,0:T(8,128)}, u32[]{:S(2)}) %copy-start.2) | copy-done | bytes 131096
  14.6 0.7 %copy-done.3 = s32[2,2,32]{2,1,0:T(2,128)S(1)} copy-done((s32[2,2,32]{2,1,0:T(2,128)S(1)}, s32[2,2,32]{2,1,0:T(2,128)}, u32[]{:S(2)}) %copy-start.3) | copy-done | bytes 536
  15.3 7.8 %warp.1 = (bf16[4,128,128]{2,1,0:T(8,128)(2,1)S(1)}, bf16[4,128,128]{2,1,0:T(8,128)(2,1)S(1)}, bf16[4,128,128]{2,1,0:T(8,128)(2,1)S(1)}, bf16[4,128,128]{2,1,0:T(8,128)(2,1)S(1)}) custom-call(s32[4]{0:T(128)S(1)} %pad_add_fusion.place_ref, s32[2,2,32]{2,1,0:T(2,128)S(1)} %copy-done.3, s32[2,2,32]{2,1,0:T(2,128)S(1)} %collective-permute-done.other_codes_ref, ...), custom_call_target="tpu_custom_call" | custom-call | flops 1073741824 | bytes 4718592 | tf_op jit(solution)/shard_map/warp/pallas_call | solution.py:209
  23.2 9.3 %lag_windows.1 = (f32[2,8,256]{2,1,0:T(8,128)S(1)}, f32[2,8,256]{2,1,0:T(8,128)S(1)}, f32[2,8,256]{2,1,0:T(8,128)S(1)}, f32[2,8,256]{2,1,0:T(8,128)S(1)}) custom-call(s32[4]{0:T(128)S(1)} %pad_add_fusion.place_ref, s32[2,2,32]{2,1,0:T(2,128)S(1)} %copy-done.3, s32[2,2,32]{2,1,0:T(2,128)S(1)} %collective-permute-done.other_codes_ref, ...), custom_call_target="tpu_custom_call" | custom-call | flops 1610612736 | bytes 4718592 | tf_op jit(solution)/shard_map/lag_windows/pallas_call | solution.py:395
  32.5 1.6 %collective-permute-start.6 = (f32[2,8,256]{2,1,0:T(8,128)S(1)}, f32[2,8,256]{2,1,0:T(8,128)S(1)}, u32[]{:S(2)}, u32[]{:S(2)}) collective-permute-start(f32[2,8,256]{2,1,0:T(8,128)S(1)} %get-tuple-element.12), channel_id=1, source_target_pairs={{0,1},{1,0},{2,3},{3,2},{4,5},{5,4},{6,7},{7,6},{8,9},{9,8},{10,11... | collective-permute-start | bytes 49160 | tf_op jit(solution)/shard_map/ppermute | solution.py:423
  34.0 0.6 %collective-permute-start.8 = (f32[2,8,256]{2,1,0:T(8,128)S(1)}, f32[2,8,256]{2,1,0:T(8,128)S(1)}, u32[]{:S(2)}, u32[]{:S(2)}) collective-permute-start(f32[2,8,256]{2,1,0:T(8,128)S(1)} %get-tuple-element.14), channel_id=1, source_target_pairs={{0,3},{1,2},{2,1},{3,0},{4,7},{5,6},{6,5},{7,4},{8,11},{9,10},{10,... | collective-permute-start | bytes 49160 | tf_op jit(solution)/shard_map/ppermute | solution.py:423
  34.7 2.8 %collective-permute-start.10 = (bf16[4,128,128]{2,1,0:T(8,128)(2,1)S(1)}, bf16[4,128,128]{2,1,0:T(8,128)(2,1)S(1)}, u32[]{:S(2)}, u32[]{:S(2)}) collective-permute-start(bf16[4,128,128]{2,1,0:T(8,128)(2,1)S(1)} %get-tuple-element.16), channel_id=1, source_target_pairs={{0,16},{8,24},{16,0},{24,8},{1,17},{9,25},{17,1},{25,9},{2,18},{10... | collective-permute-start | bytes 393224 | tf_op jit(solution)/shard_map/ppermute | solution.py:423
  37.5 1.3 %collective-permute-start.11 = (bf16[4,128,128]{2,1,0:T(8,128)(2,1)S(1)}, bf16[4,128,128]{2,1,0:T(8,128)(2,1)S(1)}, u32[]{:S(2)}, u32[]{:S(2)}) collective-permute-start(bf16[4,128,128]{2,1,0:T(8,128)(2,1)S(1)} %get-tuple-element.17), channel_id=1, source_target_pairs={{0,24},{8,16},{16,8},{24,0},{1,25},{9,17},{17,9},{25,1},{2,26},{10... | collective-permute-start | bytes 393224 | tf_op jit(solution)/shard_map/ppermute | solution.py:423
  38.9 8.7 %collective-permute-done.10 = bf16[4,128,128]{2,1,0:T(8,128)(2,1)S(1)} collective-permute-done((bf16[4,128,128]{2,1,0:T(8,128)(2,1)S(1)}, bf16[4,128,128]{2,1,0:T(8,128)(2,1)S(1)}, u32[]{:S(2)}, u32[]{:S(2)}) %collective-permute-start.10) | collective-permute-done | bytes 131104 | tf_op jit(solution)/shard_map/ppermute | solution.py:423
  47.6 0.6 %collective-permute-done.9 = bf16[4,128,128]{2,1,0:T(8,128)(2,1)S(1)} collective-permute-done((bf16[4,128,128]{2,1,0:T(8,128)(2,1)S(1)}, bf16[4,128,128]{2,1,0:T(8,128)(2,1)S(1)}, u32[]{:S(2)}, u32[]{:S(2)}) %collective-permute-start.9) | collective-permute-done | bytes 131104 | tf_op jit(solution)/shard_map/ppermute | solution.py:423
  48.2 1.6 %collective-permute-start.12 = (bf16[2,128,128]{2,1,0:T(8,128)(2,1)S(1)}, bf16[2,128,128]{2,1,0:T(8,128)(2,1)S(1)}, u32[]{:S(2)}, u32[]{:S(2)}) collective-permute-start(bf16[2,128,128]{2,1,0:T(8,128)(2,1)S(1)} %add_convert_fusion), channel_id=1, source_target_pairs={{0,4},{4,0},{1,5},{5,1},{2,6},{6,2},{3,7},{7,3},{8,12},{12,8},{9,1... | collective-permute-start | bytes 196616 | tf_op jit(solution)/shard_map/ppermute | solution.py:423
  49.8 0.6 %reshape.15 = f32[2,16,256]{2,1,0:T(8,128)} reshape(f32[2,4,2,2,256]{4,3,2,1,0:T(2,128)S(1)} %copy.13) | data formatting | bytes 65536 | tf_op jit(solution)/shard_map/reshape | solution.py:458
  50.4 2.1 %collective-permute-done.12 = bf16[2,128,128]{2,1,0:T(8,128)(2,1)S(1)} collective-permute-done((bf16[2,128,128]{2,1,0:T(8,128)(2,1)S(1)}, bf16[2,128,128]{2,1,0:T(8,128)(2,1)S(1)}, u32[]{:S(2)}, u32[]{:S(2)}) %collective-permute-start.12) | collective-permute-done | bytes 65568 | tf_op jit(solution)/shard_map/ppermute | solution.py:423
  52.5 0.7 %multiply_bitcast_fusion = f32[2,1,128,128]{3,2,1,0:T(8,128)} fusion(bf16[2,128,128]{2,1,0:T(8,128)(2,1)S(1)} %collective-permute-done.12, bf16[4,128,128]{2,1,0:T(8,128)(2,1)S(1)} %collective-permute-done.11, bf16[4,128,128]{2,1,0:T(8,128)(2,1)S(1)} %collective-permute-done.10, bf16[4,128,128]{2,1,0:T(8,128)(2,1)S(1)} %collective-permute-done.9, ...), kind=kLoop, calls=%fused_computation.1 | loop fusion | flops 327680 | bytes 458752
  (30 shorter events, 0.2 us)
Async XLA Ops:
  0.6 11.4 %collective-permute-start.1 = (bf16[2,1,512,1024]{3,2,0,1:T(8,128)(2,1)}, bf16[2,1,512,1024]{3,2,0,1:T(8,128)(2,1)S(1)}, u32[]{:S(2)}, u32[]{:S(2)}) collective-permute-start(bf16[2,1,512,1024]{3,2,0,1:T(8,128)(2,1)} %bitcast.17), channel_id=1, source_target_pairs={{0,2},{2,0},{1,3},{3,1},{4,6},{6,4},{5,7},{7,5},{8,10},{10,8},{9,1... | collective-permute-start | bytes 6291464 | tf_op jit(solution)/shard_map/ppermute | solution.py:423
  1.1 5.5 %collective-permute-start.2 = (bf16[2,1,128,128]{3,2,0,1:T(8,128)(2,1)}, bf16[2,1,128,128]{3,2,0,1:T(8,128)(2,1)S(1)}, u32[]{:S(2)}, u32[]{:S(2)}) collective-permute-start(bf16[2,1,128,128]{3,2,0,1:T(8,128)(2,1)} %bitcast.29), channel_id=1, source_target_pairs={{0,4},{4,0},{1,5},{5,1},{2,6},{6,2},{3,7},{7,3},{8,12},{12,8},{9,1... | collective-permute-start | bytes 196616 | tf_op jit(solution)/shard_map/ppermute | solution.py:423
  3.7 8.3 %collective-permute-start = (s32[2,2,32]{2,1,0:T(2,128)}, s32[2,2,32]{2,1,0:T(2,128)S(1)}, u32[]{:S(2)}, u32[]{:S(2)}) collective-permute-start(s32[2,2,32]{2,1,0:T(2,128)} %codes_ref.3), channel_id=1, source_target_pairs={{0,2},{2,0},{1,3},{3,1},{4,6},{6,4},{5,7},{7,5},{8,10},{10,8},{9,1... | collective-permute-start | bytes 1544 | tf_op jit(solution)/shard_map/ppermute | solution.py:423
  7.5 15.6 %collective-permute-start.4 = (bf16[4,1,128,128]{3,2,0,1:T(8,128)(2,1)S(1)}, bf16[4,1,128,128]{3,2,0,1:T(8,128)(2,1)S(1)}, u32[]{:S(2)}, u32[]{:S(2)}) collective-permute-start(bf16[4,1,128,128]{3,2,0,1:T(8,128)(2,1)S(1)} %get-tuple-element.20), channel_id=1, source_target_pairs={{0,16},{8,24},{16,0},{24,8},{1,17},{9,25},{17,1},{25,9},{2,18},{10... | collective-permute-start | bytes 393224 | tf_op jit(solution)/shard_map/ppermute | solution.py:423
  10.4 12.7 %collective-permute-start.5 = (bf16[4,1,128,128]{3,2,0,1:T(8,128)(2,1)S(1)}, bf16[4,1,128,128]{3,2,0,1:T(8,128)(2,1)S(1)}, u32[]{:S(2)}, u32[]{:S(2)}) collective-permute-start(bf16[4,1,128,128]{3,2,0,1:T(8,128)(2,1)S(1)} %get-tuple-element.20), channel_id=1, source_target_pairs={{0,24},{8,16},{16,8},{24,0},{1,25},{9,17},{17,9},{25,1},{2,26},{10... | collective-permute-start | bytes 393224 | tf_op jit(solution)/shard_map/ppermute | solution.py:423
  11.7 11.4 %collective-permute-start.3 = (bf16[4,1,128,128]{3,2,0,1:T(8,128)(2,1)S(1)}, bf16[4,1,128,128]{3,2,0,1:T(8,128)(2,1)S(1)}, u32[]{:S(2)}, u32[]{:S(2)}) collective-permute-start(bf16[4,1,128,128]{3,2,0,1:T(8,128)(2,1)S(1)} %get-tuple-element.20), channel_id=1, source_target_pairs={{0,8},{8,0},{16,24},{24,16},{1,9},{9,1},{17,25},{25,17},{2,10},{10... | collective-permute-start | bytes 393224 | tf_op jit(solution)/shard_map/ppermute | solution.py:423
  12.1 1.6 %copy-start = (bf16[2,1,512,1024]{3,2,1,0:T(8,128)(2,1)S(1)}, bf16[2,1,512,1024]{3,2,1,0:T(8,128)(2,1)}, u32[]{:S(2)}) copy-start(bf16[2,1,512,1024]{3,2,1,0:T(8,128)(2,1)} %param.8) | copy-start | bytes 6291460
  13.6 0.9 %copy-start.2 = (f32[16,16,128]{2,1,0:T(8,128)S(1)}, f32[16,16,128]{2,1,0:T(8,128)}, u32[]{:S(2)}) copy-start(f32[16,16,128]{2,1,0:T(8,128)} %constant.28.clone.taps_ref) | copy-start | bytes 393220
  14.6 0.7 %copy-start.3 = (s32[2,2,32]{2,1,0:T(2,128)S(1)}, s32[2,2,32]{2,1,0:T(2,128)}, u32[]{:S(2)}) copy-start(s32[2,2,32]{2,1,0:T(2,128)} %codes_ref.3) | copy-start | bytes 1540
  15.2 7.9 %copy-start.1 = (bf16[2,1,512,1024]{3,2,1,0:T(8,128)(2,1)S(1)}, bf16[2,1,512,1024]{3,2,1,0:T(8,128)(2,1)}, u32[]{:S(2)}) copy-start(bf16[2,1,512,1024]{3,2,1,0:T(8,128)(2,1)} %param.8) | copy-start | bytes 6291460
  15.2 7.9 %copy-start.4 = (bf16[16,32,144]{2,1,0:T(8,128)(2,1)S(1)}, bf16[16,32,144]{2,1,0:T(8,128)(2,1)}, u32[]{:S(2)}) copy-start(bf16[16,32,144]{2,1,0:T(8,128)(2,1)} %constant.31.clone.lag_ref) | copy-start | bytes 442372
  15.2 7.9 %copy-start.5 = (bf16[144,256]{1,0:T(8,128)(2,1)S(1)}, bf16[144,256]{1,0:T(8,128)(2,1)}, u32[]{:S(2)}) copy-start(bf16[144,256]{1,0:T(8,128)(2,1)} %constant.30.clone.col_ref) | copy-start | bytes 221188
  15.2 7.9 %copy-start.6 = (bf16[128,256]{1,0:T(8,128)(2,1)S(1)}, bf16[128,256]{1,0:T(8,128)(2,1)}, u32[]{:S(2)}) copy-start(bf16[128,256]{1,0:T(8,128)(2,1)} %constant.29.clone.row_ref) | copy-start | bytes 196612
  15.2 7.9 %copy-start.7 = (bf16[256,128]{1,0:T(8,128)(2,1)S(1)}, bf16[256,128]{1,0:T(8,128)(2,1)}, u32[]{:S(2)}) copy-start(bf16[256,128]{1,0:T(8,128)(2,1)} %constant.32.clone.span_ref) | copy-start | bytes 196612
  32.5 6.4 %collective-permute-start.6 = (f32[2,8,256]{2,1,0:T(8,128)S(1)}, f32[2,8,256]{2,1,0:T(8,128)S(1)}, u32[]{:S(2)}, u32[]{:S(2)}) collective-permute-start(f32[2,8,256]{2,1,0:T(8,128)S(1)} %get-tuple-element.12), channel_id=1, source_target_pairs={{0,1},{1,0},{2,3},{3,2},{4,5},{5,4},{6,7},{7,6},{8,9},{9,8},{10,11... | collective-permute-start | bytes 49160 | tf_op jit(solution)/shard_map/ppermute | solution.py:423
  34.0 4.8 %collective-permute-start.7 = (f32[2,8,256]{2,1,0:T(8,128)S(1)}, f32[2,8,256]{2,1,0:T(8,128)S(1)}, u32[]{:S(2)}, u32[]{:S(2)}) collective-permute-start(f32[2,8,256]{2,1,0:T(8,128)S(1)} %get-tuple-element.13), channel_id=1, source_target_pairs={{0,2},{1,3},{2,0},{3,1},{4,6},{5,7},{6,4},{7,5},{8,10},{9,11},{10,... | collective-permute-start | bytes 49160 | tf_op jit(solution)/shard_map/ppermute | solution.py:423
  34.0 4.8 %collective-permute-start.8 = (f32[2,8,256]{2,1,0:T(8,128)S(1)}, f32[2,8,256]{2,1,0:T(8,128)S(1)}, u32[]{:S(2)}, u32[]{:S(2)}) collective-permute-start(f32[2,8,256]{2,1,0:T(8,128)S(1)} %get-tuple-element.14), channel_id=1, source_target_pairs={{0,3},{1,2},{2,1},{3,0},{4,7},{5,6},{6,5},{7,4},{8,11},{9,10},{10,... | collective-permute-start | bytes 49160 | tf_op jit(solution)/shard_map/ppermute | solution.py:423
  34.7 12.9 %collective-permute-start.10 = (bf16[4,128,128]{2,1,0:T(8,128)(2,1)S(1)}, bf16[4,128,128]{2,1,0:T(8,128)(2,1)S(1)}, u32[]{:S(2)}, u32[]{:S(2)}) collective-permute-start(bf16[4,128,128]{2,1,0:T(8,128)(2,1)S(1)} %get-tuple-element.16), channel_id=1, source_target_pairs={{0,16},{8,24},{16,0},{24,8},{1,17},{9,25},{17,1},{25,9},{2,18},{10... | collective-permute-start | bytes 393224 | tf_op jit(solution)/shard_map/ppermute | solution.py:423
  37.5 10.1 %collective-permute-start.11 = (bf16[4,128,128]{2,1,0:T(8,128)(2,1)S(1)}, bf16[4,128,128]{2,1,0:T(8,128)(2,1)S(1)}, u32[]{:S(2)}, u32[]{:S(2)}) collective-permute-start(bf16[4,128,128]{2,1,0:T(8,128)(2,1)S(1)} %get-tuple-element.17), channel_id=1, source_target_pairs={{0,24},{8,16},{16,8},{24,0},{1,25},{9,17},{17,9},{25,1},{2,26},{10... | collective-permute-start | bytes 393224 | tf_op jit(solution)/shard_map/ppermute | solution.py:423
  38.8 9.3 %collective-permute-start.9 = (bf16[4,128,128]{2,1,0:T(8,128)(2,1)S(1)}, bf16[4,128,128]{2,1,0:T(8,128)(2,1)S(1)}, u32[]{:S(2)}, u32[]{:S(2)}) collective-permute-start(bf16[4,128,128]{2,1,0:T(8,128)(2,1)S(1)} %get-tuple-element.15), channel_id=1, source_target_pairs={{0,8},{8,0},{16,24},{24,16},{1,9},{9,1},{17,25},{25,17},{2,10},{10... | collective-permute-start | bytes 393224 | tf_op jit(solution)/shard_map/ppermute | solution.py:423
  48.2 4.3 %collective-permute-start.12 = (bf16[2,128,128]{2,1,0:T(8,128)(2,1)S(1)}, bf16[2,128,128]{2,1,0:T(8,128)(2,1)S(1)}, u32[]{:S(2)}, u32[]{:S(2)}) collective-permute-start(bf16[2,128,128]{2,1,0:T(8,128)(2,1)S(1)} %add_convert_fusion), channel_id=1, source_target_pairs={{0,4},{4,0},{1,5},{5,1},{2,6},{6,2},{3,7},{7,3},{8,12},{12,8},{9,1... | collective-permute-start | bytes 196616 | tf_op jit(solution)/shard_map/ppermute | solution.py:423

commit v5 on v4

v5 whole, which is shorter than its diff:
```python
import functools
import math

import jax
import jax.numpy as jnp
import numpy as np
from jax import lax
from jax.experimental import pallas as pl
from jax.experimental.pallas import tpu as pltpu
from jax.sharding import PartitionSpec as P

SHIFT = 8
WIN = 16
TAPS = 8
SUB = 16
EDGE = 16
LANES = 128
VMEM_LIMIT = 24 * 1024 * 1024

full_turn = 2.0 * math.pi


def dft_constants(block_size):
    positions = np.arange(block_size)
    angles = full_turn * (np.outer(positions, positions) % block_size) / block_size
    cosine = np.cos(angles)
    sine = -np.sin(angles)
    half = block_size // 2 + 1
    rows = -(-half // 8) * 8
    row_table = np.concatenate([cosine, sine], axis=1)
    col_table = np.zeros((2 * rows, 2 * block_size))
    col_table[:half] = np.concatenate([cosine[:half], -sine[:half]], axis=1)
    col_table[rows : rows + half] = np.concatenate([sine[:half], cosine[:half]], axis=1)
    weights = np.zeros((rows,))
    weights[:half] = 2.0
    weights[0] = weights[half - 1] = 1.0
    starts = 2 * SHIFT
    lag_table = np.zeros((starts, 2 * WIN, 2 * rows))
    for start in range(starts):
        lags = start - SHIFT - WIN // 2 + np.arange(WIN)
        turns = full_turn * (np.outer(lags, positions[:half]) % block_size) / block_size
        lag_cos = np.cos(turns) * weights[:half]
        lag_sin = np.sin(turns) * weights[:half]
        lag_table[start, :WIN, :half] = lag_cos
        lag_table[start, :WIN, rows : rows + half] = -lag_sin
        lag_table[start, WIN:, :half] = lag_sin
        lag_table[start, WIN:, rows : rows + half] = lag_cos
    span = starts + WIN
    lags = np.arange(span) - SHIFT - WIN // 2
    turns = full_turn * (np.outer(positions, lags) % block_size) / block_size
    span_table = np.zeros((2 * block_size, LANES))
    span_table[:block_size, :span] = np.cos(turns)
    span_table[block_size:, :span] = -np.sin(turns)
    return tuple(
        jnp.asarray(table, jnp.bfloat16) for table in (row_table, col_table, lag_table, span_table)
    )


def tap_constants():
    offsets = np.arange(TAPS) - (TAPS // 2 - 1)
    spots = offsets[None, :] - np.arange(SUB)[:, None] / SUB
    raw_taps = np.sinc(spots) * np.sinc(spots / (TAPS // 2))
    taps = raw_taps / raw_taps.sum(axis=-1, keepdims=True)
    table = np.zeros((2, SUB, EDGE, LANES))
    for row in range(EDGE):
        table[0, :, row, row : row + TAPS] = taps
        table[1, :, row, row : row + TAPS] = taps[:, ::-1]
    return jnp.asarray(table, jnp.float32)


def band_groups(head, start, lane):
    head = pltpu.roll(head, start + LANES, 1).astype(jnp.bfloat16)
    groups = [head] + [pltpu.roll(head, step, 1) for step in range(EDGE, LANES, EDGE)]
    zero = jnp.zeros_like(head)
    low = lane < LANES // 2
    before, after = jnp.where(low, zero, groups[0]), jnp.where(low, groups[-1], zero)
    middle = [jnp.where(low, groups[0], zero), *groups[1:-1], jnp.where(low, zero, groups[-1])]
    return middle, before, after


def step_places(place_ref, step, across, own):
    z = place_ref[0] ^ step
    places = []
    for other in range(2):
        for one in range(own):
            index = ((2 * z + (place_ref[1] ^ other)) * 2 + place_ref[2]) * own + one
            places.append((index, index % across))
    return places


def step_band(place_ref, step, across, own):
    return (place_ref[0] ^ step) * (4 * own) // across


def warp_kernel(vols, down, across, block, own, depth, *refs):
    place_ref, codes_hbm, other_codes_hbm, taps_hbm, frames_hbm, other_frames_ref = refs[:6]
    out_refs = refs[6 : 6 + depth]
    codes_ref, other_codes_ref, taps_ref, frames_ref, sums, sems = refs[6 + depth :]
    moves = [
        (frames_hbm, frames_ref),
        (codes_hbm, codes_ref),
        (other_codes_hbm, other_codes_ref),
        (taps_hbm, taps_ref),
    ]
    copies = [
        pltpu.make_async_copy(source, target, sems.at[at])
        for at, (source, target) in enumerate(moves)
    ]
    for copy in copies:
        copy.start()
    for copy in copies:
        copy.wait()
    lane = lax.broadcasted_iota(jnp.int32, (EDGE, LANES), 1)
    tall_lane = lax.broadcasted_iota(jnp.int32, (block + 2 * EDGE, LANES), 1)
    zero = jnp.zeros((EDGE, LANES), jnp.bfloat16)
    gap = jnp.zeros((block - 2 * EDGE, LANES), jnp.bfloat16)
    no_tile = jnp.zeros((block + 2 * EDGE, block), jnp.bfloat16)
    volumes = [(codes_ref, frames_ref, v) for v in range(vols)]
    volumes += [(other_codes_ref, other_frames_ref, v) for v in range(vols)]
    before_taps = TAPS // 2 - 1
    after_taps = TAPS // 2

    def one_step(step, _):
        band = step_band(place_ref, step, across, own)
        row = pl.multiple_of(band * block, block)
        row_above = pl.multiple_of(jnp.maximum(row - EDGE, 0), EDGE)
        row_below = pl.multiple_of(jnp.minimum(row + block, down * block - EDGE), EDGE)

        def tile(volume, at):
            _, frames, v = volume
            lanes = pl.ds(pl.multiple_of(at * block, block), block)
            above = jnp.where(band > 0, frames[v, pl.ds(row_above, EDGE), lanes], zero)
            below = jnp.where(band < down - 1, frames[v, pl.ds(row_below, EDGE), lanes], zero)
            return jnp.concatenate([frames[v, pl.ds(row, block), lanes], below, above], axis=0)

        for count, (index, at) in enumerate(step_places(place_ref, step, across, own)):
            row_tiles, first_edge, last_edge = [], [], []
            partials, edges = [], []
            for order, volume in enumerate(volumes):
                codes, _, v = volume
                row_code = codes[v, 0, index]
                col_code = codes[v, 1, index]
                middle, before, after = band_groups(
                    taps_ref[1, col_code & (SUB - 1)], -after_taps - (col_code >> 4), lane
                )
                left = jnp.where(at > 0, tile(volume, jnp.maximum(at - 1, 0)), no_tile)
                right = jnp.where(
                    at < across - 1, tile(volume, jnp.minimum(at + 1, across - 1)), no_tile
                )
                sides = jnp.where(tall_lane < LANES // 2, right, left)
                partial = jnp.dot(
                    jnp.concatenate([tile(volume, at), sides], axis=1),
                    jnp.concatenate([*middle, before, gap, after], axis=0),
                    preferred_element_type=jnp.float32,
                ).astype(jnp.bfloat16)
                partials.append(partial[:block])
                edges.append(partial[block:])
                middle, before, after = band_groups(
                    taps_ref[0, row_code & (SUB - 1)], (row_code >> 4) - before_taps, lane
                )
                row_tiles.append(jnp.concatenate(middle, axis=0))
                place = 2 * EDGE * order % LANES
                first_edge.append(pltpu.roll(before, (place + 2 * EDGE) % LANES, 1))
                last_edge.append(pltpu.roll(after, place, 1) if place else after)
            per_tile = LANES // (2 * EDGE)
            for start in range(0, 2 * vols, per_tile):
                first, last = first_edge[start], last_edge[start]
                for more in range(start + 1, min(start + per_tile, 2 * vols)):
                    first, last = first + first_edge[more], last + last_edge[more]
                row_tiles.append(jnp.concatenate([first, gap, last], axis=0))
            deep = 2 * vols * (block + 2 * EDGE)
            total = jnp.dot(
                jnp.concatenate(row_tiles, axis=1)[:, :deep],
                jnp.concatenate(partials + edges, axis=0),
                preferred_element_type=jnp.float32,
            )
            sums[count] = total.astype(jnp.bfloat16)
        for at_step, out_ref in enumerate(out_refs):

            @pl.when(step == at_step)
            def _():
                out_ref[...] = sums[...]

        return 0

    lax.fori_loop(0, depth, one_step, 0)


def warp_sums(place, codes, other_codes, frames, other_frames, depth, block, own):
    vols, rows, cols = frames.shape
    down, across = rows // block, cols // block
    taps = tap_constants()
    out = (2 * own, block, block)
    hbm = pl.BlockSpec(memory_space=pltpu.HBM)
    kept = [
        pltpu.with_memory_space_constraint(one, pltpu.HBM)
        for one in (codes, other_codes, taps, frames)
    ]
    vmem = pl.BlockSpec(memory_space=pltpu.VMEM)
    return pl.pallas_call(
        functools.partial(warp_kernel, vols, down, across, block, own, depth),
        out_shape=[jax.ShapeDtypeStruct(out, jnp.bfloat16)] * depth,
        in_specs=[pl.BlockSpec(memory_space=pltpu.SMEM), hbm, hbm, hbm, hbm, vmem],
        out_specs=[vmem] * depth,
        scratch_shapes=[
            pltpu.SMEM(codes.shape, jnp.int32),
            pltpu.SMEM(codes.shape, jnp.int32),
            pltpu.VMEM(taps.shape, jnp.float32),
            pltpu.VMEM(frames.shape, jnp.bfloat16),
            pltpu.VMEM(out, jnp.bfloat16),
            pltpu.SemaphoreType.DMA((4,)),
        ],
        compiler_params=pltpu.CompilerParams(vmem_limit_bytes=VMEM_LIMIT),
        cost_estimate=pl.CostEstimate(
            flops=2 * vols * rows * cols * block * 16,
            bytes_accessed=vols * rows * cols * 4 + rows * cols,
            transcendentals=0,
        ),
        name="warp",
    )(place, *kept, other_frames)


def spectrum_kernel(vols, across, block, own, planes, depth, *refs):
    place_ref, codes_ref, other_codes_ref, row_ref, col_ref, lag_ref, span_ref = refs[:7]
    frames_ref, other_frames_ref = refs[7:9]
    template_refs, out_refs = refs[9 : 9 + depth], refs[10 + depth : 10 + depth + 2 * planes]
    templates, cross, sums, found = refs[10 + depth + 2 * planes :]
    for at, template_ref in enumerate(template_refs):
        templates[at] = template_ref[...]

    row_table = row_ref[...]
    col_table = col_ref[...]
    half = col_table.shape[0] // 2
    top = lax.broadcasted_iota(jnp.int32, (8, LANES), 0) == 0
    volumes = [(codes_ref, frames_ref, v) for v in range(vols)]
    volumes += [(other_codes_ref, other_frames_ref, v) for v in range(vols)]
    many = len(volumes)
    local = 2 * own
    def one_step(step, _):
        places = step_places(place_ref, step, across, own)
        band = step_band(place_ref, step, across, own)
        band_rows = pl.ds(pl.multiple_of(band * block, block), block)

        for pair in range(local // 2):
            pair_places = places[2 * pair : 2 * pair + 2]
            parts = [templates[step, 2 * pair], templates[step, 2 * pair + 1]]
            for _, frames, v in volumes:
                for _, at in pair_places:
                    parts.append(frames[v, band_rows, pl.ds(pl.multiple_of(at * block, block), block)])
            rows = jnp.dot(
                jnp.concatenate(parts, axis=0), row_table, preferred_element_type=jnp.float32
            ).astype(jnp.bfloat16)
            spectra = []
            for source in range(many + 1):
                stacks = []
                for side in range(2):
                    at = (2 * source + side) * block
                    one = rows[at : at + block]
                    stacks.append(jnp.concatenate([one[:, :block], one[:, block:]], axis=0))
                spectra.append(
                    jnp.dot(
                        col_table, jnp.concatenate(stacks, axis=1), preferred_element_type=jnp.float32
                    )
                )
            temp = spectra[0].astype(jnp.bfloat16).astype(jnp.float32)
            for order in range(many):
                for side in range(2):
                    lanes = slice(side * block, (side + 1) * block)
                    one = (2 * pair + side) * many + order
                    total = jnp.zeros((8, LANES), jnp.float32)
                    for row in range(0, half, 8):
                        temp_real = temp[row : row + 8, lanes]
                        temp_imag = temp[half + row : half + row + 8, lanes]
                        real = spectra[order + 1][row : row + 8, lanes]
                        imag = spectra[order + 1][half + row : half + row + 8, lanes]
                        cross_real = real * temp_real + imag * temp_imag
                        cross_imag = imag * temp_real - real * temp_imag
                        power = cross_real * cross_real + cross_imag * cross_imag
                        magnitude = power * lax.rsqrt(jnp.maximum(power, 1e-36))
                        cross[one, row : row + 8, :] = cross_real
                        cross[one, half + row : half + row + 8, :] = cross_imag
                        cross[one, 2 * half + row : 2 * half + row + 8, :] = magnitude
                        if row == 0:
                            total = jnp.where(top, magnitude, 2.0 * magnitude)
                        elif row == block // 2:
                            total += magnitude
                        else:
                            total += 2.0 * magnitude
                    sums[one] = jnp.sum(total, axis=0, keepdims=True)

        means = jnp.sum(sums[...], axis=2, keepdims=True) * (1.0 / (block * block)) + 1e-06
        lag_sums = []
        for one in range(local * many):
            codes, _, v = volumes[one % many]
            index, _ = places[one // many]
            scale = pl.reciprocal(cross[one, 2 * half :, :] + means[one], approx=True)
            norm = jnp.concatenate(
                [
                    (cross[one, :half, :] * scale).astype(jnp.bfloat16),
                    (cross[one, half : 2 * half, :] * scale).astype(jnp.bfloat16),
                ],
                axis=0,
            )
            row_shift = codes[v, 0, index] >> 4
            lag_rows = jnp.dot(
                lag_ref[row_shift + SHIFT], norm, preferred_element_type=jnp.float32
            ).astype(jnp.bfloat16)
            lag_sums.append(jnp.concatenate([lag_rows[:WIN], lag_rows[WIN:]], axis=1))
        lags = jnp.dot(
            jnp.concatenate(lag_sums, axis=0), span_ref[...], preferred_element_type=jnp.float32
        )
        for one in range(local * many):
            codes, _, v = volumes[one % many]
            index, _ = places[one // many]
            col_shift = codes[v, 1, index] >> 4
            order = index // (2 * own) * own + one // many % own
            found[one % many, pl.ds(pl.multiple_of(order * WIN, WIN), WIN), :] = pltpu.roll(
                lags[one * WIN : (one + 1) * WIN], LANES - SHIFT - col_shift, 1
            )
        return 0

    lax.fori_loop(0, depth, one_step, 0)

    share = depth * local // planes
    per_tile = LANES // WIN
    lane = lax.broadcasted_iota(jnp.int32, (share, LANES), 1) // WIN
    for turn, out_ref in enumerate(out_refs):
        plane = place_ref[3] ^ (turn % planes)
        for v in range(vols):
            order = turn // planes * vols + v
            for tile in range(WIN // per_tile):
                total = jnp.zeros((share, LANES), jnp.float32)
                for part in range(per_tile):
                    start = plane * share * WIN + tile * per_tile + part
                    one = found[order, pl.ds(start, share, stride=WIN), :]
                    if part:
                        one = pltpu.roll(one, part * WIN, 1)
                    total = jnp.where(lane == part, one, total)
                out_ref[v, :, tile * LANES : (tile + 1) * LANES] = total * (1.0 / block)


def lag_windows(place, codes, other_codes, frames, other_frames, templates, after, planes, own):
    vols, rows, cols = frames.shape
    block = templates[0].shape[-1]
    down, across = rows // block, cols // block
    depth = len(templates)
    tables = dft_constants(block)
    half = tables[1].shape[0] // 2
    smem = pl.BlockSpec(memory_space=pltpu.SMEM)
    vmem = pl.BlockSpec(memory_space=pltpu.VMEM)
    local = depth * 2 * own
    many = 2 * vols * 2 * own
    out = (vols, local // planes, WIN * WIN)
    return pl.pallas_call(
        functools.partial(spectrum_kernel, vols, across, block, own, planes, depth),
        out_shape=[jax.ShapeDtypeStruct(out, jnp.float32)] * (2 * planes),
        in_specs=[smem] * 3
        + [vmem] * (len(tables) + 2 + depth)
        + [pl.BlockSpec(memory_space=pl.ANY)],
        out_specs=[vmem] * (2 * planes),
        scratch_shapes=[
            pltpu.VMEM((depth, 2 * own, block, block), jnp.bfloat16),
            pltpu.VMEM((many, 3 * half, LANES), jnp.float32),
            pltpu.VMEM((many, 1, LANES), jnp.float32),
            pltpu.VMEM((2 * vols, local * WIN, LANES), jnp.float32),
        ],
        compiler_params=pltpu.CompilerParams(vmem_limit_bytes=VMEM_LIMIT),
        cost_estimate=pl.CostEstimate(
            flops=2 * 3 * rows * cols * block * 16,
            bytes_accessed=vols * rows * cols * 4 + rows * cols,
            transcendentals=0,
        ),
        name="lag_windows",
    )(place, codes, other_codes, *tables, frames, other_frames, *templates, after)


def exchange(value, axes, size, turn):
    return lax.ppermute(value, axes, [(at, at ^ turn) for at in range(size)])


def on_device(frames, template, shift_codes):
    vol_dev, pl_dev, img_rows, img_cols = frames.shape
    own, block = template.shape[0], template.shape[-1]
    depth = lax.axis_size("z")
    planes = lax.axis_size("plane")
    share = 4 * depth * own // planes
    place = jnp.stack([lax.axis_index(axis) for axis in ("z", "y", "core", "plane")])
    other_codes = exchange(shift_codes, "core", 2, 1)
    other_template = exchange(template, "y", 2, 1)
    later_frames, other_template = lax.optimization_barrier((frames, other_template))
    other_frames = exchange(later_frames, "core", 2, 1)
    templates = [jnp.concatenate([template, other_template], axis=0)]
    for turn in range(1, depth):
        templates.append(exchange(templates[0], "z", depth, turn))
    averages, window = [], [0.0, 0.0]
    volumes = vol_dev * depth * 4
    for p in range(pl_dev):
        work = (place, shift_codes, other_codes, frames[:, p], other_frames[:, p])
        warped = warp_sums(*work, depth, block, own)
        chosen = [one[:, p] for one in templates]
        found = lag_windows(*work, chosen, warped[0], planes, own)
        warped = [warped[0]] + [
            exchange(warped[turn], "z", depth, turn) for turn in range(1, depth)
        ]
        sums = [sum(one[at : at + own].astype(jnp.float32) for one in warped) for at in (0, own)]
        found, sums = lax.optimization_barrier((found, sums))
        taken = exchange(sums[1].astype(jnp.bfloat16), "y", 2, 1)
        averages.append((sums[0] + taken.astype(jnp.float32)) * (1.0 / volumes))
        for turn, one in enumerate(found):
            if turn:
                one = exchange(one, ("core", "plane"), 2 * planes, turn)
            window[turn // planes] += one
    core = place[2]
    window = [jnp.where(core == 0, *window), jnp.where(core == 0, *window[::-1])]
    window = [one.reshape(vol_dev, share // (2 * own), 1, own, WIN * WIN) for one in window]
    correlation = jnp.concatenate(window, axis=2).reshape(vol_dev, share, WIN * WIN)
    return (correlation, jnp.stack(averages, axis=1))


def solution(mesh):
    devices = mesh.devices.reshape(-1, 2, 2, mesh.shape["plane"])
    split = jax.sharding.Mesh(devices, ("z", "y", "core", "plane"))
    vols = ("z", "y", "core")
    in_specs = (P(vols, "plane", None, None), P(vols, "plane", None, None), P(vols, None, None))
    out_specs = (P(vols, "plane", None), P(vols, "plane", None, None))
    return jax.shard_map(
        on_device, mesh=split, in_specs=in_specs, out_specs=out_specs, check_vma=False
    )
```

time: 53.4 us -> 42.5 us (0.80)
  waiting for transfers between devices: 14.1 us -> 5.92 us
  local copies, waits for them, and re-layouts: 3.87 us -> 1.95 us
  Pallas kernels: 17.1 us -> 15.4 us
  starting transfers between devices: 15.7 us -> 16.5 us
    ppermute x13, waiting for transfers between devices: 14.1 us -> 5.92 us  [exchange(): return lax.ppermute(value, axes, [(at, at ^ turn) for at in range(size)])]
    unnamed x16, local copies, waits for them, and re-layouts: 3.2 us -> 1.28 us
    pallas_call x1, Pallas kernels: 9.26 us -> 7.49 us  [lag_windows(): pl.pallas_call(functools.partial(spectrum_kernel, vols, across, block, ow...]
    ppermute x13, starting transfers between devices: 15.7 us -> 16.5 us  [exchange(): return lax.ppermute(value, axes, [(at, at ^ turn) for at in range(size)])]
  transfers between devices with their start and end apart: 13 -> 13, of which waited for: 4 -> 4; matrix products, arithmetic and copies ran while one was open for 3% -> 4% of each run, Pallas kernels for 15% -> 36%
where the time goes in v5:
time: 42.5 us; the launch traced here: 42.3 us
  starting transfers between devices  16.5 us (39%)
  Pallas kernels  15.4 us (36%)
  waiting for transfers between devices  5.92 us (14%)
  local copies, waits for them, and re-layouts  1.95 us (5%)
  other arithmetic  1.71 us (4%)
  between operations  0.79 us (2%)
    ppermute x13, starting transfers between devices, exchange(): return lax.ppermute(value, axes, [(at, at ^ turn) for at in range(size)])  16.5 us
    pallas_call x1, Pallas kernels, warp_sums(): pl.pallas_call(functools.partial(warp_kernel, vols, down, across, block,...  7.95 us
    pallas_call x1, Pallas kernels, lag_windows(): pl.pallas_call(functools.partial(spectrum_kernel, vols, across, block, ow...  7.49 us
    ppermute x13, waiting for transfers between devices, exchange(): return lax.ppermute(value, axes, [(at, at ^ turn) for at in range(size)])  5.92 us
    unnamed x16, local copies, waits for them, and re-layouts  1.28 us
    concatenate x1, other arithmetic, on_device(): templates = [jnp.concatenate([template, other_template], axis=0)]  0.86 us
  transfers between devices with their start and end apart: 13, of which 4 were waited for; matrix products, arithmetic and copies ran while one was open for 4% of the time, Pallas kernels for 36%

profile of v5, /device:TPU:0, one launch (start us, length us, event | category | flops | bytes accessed | tf_op | source)
XLA Modules:
  0.0 42.3 jit_solution(9359885486379762337)
XLA Ops:
  0.6 3.0 %collective-permute-start.1 = (bf16[2,1,128,128]{3,2,0,1:T(8,128)(2,1)}, bf16[2,1,128,128]{3,2,0,1:T(8,128)(2,1)S(1)}, u32[]{:S(2)}, u32[]{:S(2)}) collective-permute-start(bf16[2,1,128,128]{3,2,0,1:T(8,128)(2,1)} %bitcast.25), channel_id=1, source_target_pairs={{0,4},{4,0},{1,5},{5,1},{2,6},{6,2},{3,7},{7,3},{8,12},{12,8},{9,1... | collective-permute-start | bytes 196616 | tf_op jit(solution)/shard_map/ppermute | solution.py:378
  3.7 2.5 %collective-permute-done.1 = bf16[2,1,128,128]{3,2,0,1:T(8,128)(2,1)S(1)} collective-permute-done((bf16[2,1,128,128]{3,2,0,1:T(8,128)(2,1)}, bf16[2,1,128,128]{3,2,0,1:T(8,128)(2,1)S(1)}, u32[]{:S(2)}, u32[]{:S(2)}) %collective-permute-start.1) | collective-permute-done | bytes 65568 | tf_op jit(solution)/shard_map/ppermute | solution.py:378
  6.1 0.5 %collective-permute-start = (s32[2,2,32]{2,1,0:T(2,128)}, s32[2,2,32]{2,1,0:T(2,128)S(1)}, u32[]{:S(2)}, u32[]{:S(2)}) collective-permute-start(s32[2,2,32]{2,1,0:T(2,128)} %refs_1_.3), channel_id=1, source_target_pairs={{0,2},{2,0},{1,3},{3,1},{4,6},{6,4},{5,7},{7,5},{8,10},{10,8},{9,1... | collective-permute-start | bytes 1544 | tf_op jit(solution)/shard_map/ppermute | solution.py:378
  6.6 0.1 pad_add_fusion.refs_0_
  6.7 0.9 %pad_maximum_fusion = (bf16[4,1,128,128]{3,2,0,1:T(8,128)(2,1)S(1)}, bf16[4,128,128]{2,1,0:T(8,128)(2,1)S(1)}) fusion(bf16[2,1,128,128]{3,2,0,1:T(8,128)(2,1)S(1)} %collective-permute-done.1, bf16[2,1,128,128]{3,2,0,1:T(8,128)(2,1)} %bitcast.26), kind=kLoop, calls=%fused_computation | loop fusion | flops 65536 | bytes 393216 | tf_op jit(solution)/shard_map/concatenate | solution.py:392
  7.6 3.2 %collective-permute-start.4 = (bf16[4,1,128,128]{3,2,0,1:T(8,128)(2,1)S(1)}, bf16[4,1,128,128]{3,2,0,1:T(8,128)(2,1)S(1)}, u32[]{:S(2)}, u32[]{:S(2)}) collective-permute-start(bf16[4,1,128,128]{3,2,0,1:T(8,128)(2,1)S(1)} %get-tuple-element.36), channel_id=1, source_target_pairs={{0,16},{8,24},{16,0},{24,8},{1,17},{9,25},{17,1},{25,9},{2,18},{10... | collective-permute-start | bytes 393224 | tf_op jit(solution)/shard_map/ppermute | solution.py:378
  10.7 1.3 %collective-permute-start.5 = (bf16[4,1,128,128]{3,2,0,1:T(8,128)(2,1)S(1)}, bf16[4,1,128,128]{3,2,0,1:T(8,128)(2,1)S(1)}, u32[]{:S(2)}, u32[]{:S(2)}) collective-permute-start(bf16[4,1,128,128]{3,2,0,1:T(8,128)(2,1)S(1)} %get-tuple-element.36), channel_id=1, source_target_pairs={{0,24},{8,16},{16,8},{24,0},{1,25},{9,17},{17,9},{25,1},{2,26},{10... | collective-permute-start | bytes 393224 | tf_op jit(solution)/shard_map/ppermute | solution.py:378
  12.1 0.2 collective-permute-start.3
  12.3 0.6 %copy-done.2 = s32[2,2,32]{2,1,0:T(2,128)} copy-done((s32[2,2,32]{2,1,0:T(2,128)}, s32[2,2,32]{2,1,0:T(2,128)S(1)}, u32[]{:S(2)}) %copy-start.2) | copy-done | bytes 536
  12.9 7.9 %warp.1 = (bf16[4,128,128]{2,1,0:T(8,128)(2,1)S(1)}, bf16[4,128,128]{2,1,0:T(8,128)(2,1)S(1)}, bf16[4,128,128]{2,1,0:T(8,128)(2,1)S(1)}, bf16[4,128,128]{2,1,0:T(8,128)(2,1)S(1)}) custom-call(s32[4]{0:T(128)S(1)} %pad_add_fusion.refs_0_, s32[2,2,32]{2,1,0:T(2,128)} %refs_1_.3, s32[2,2,32]{2,1,0:T(2,128)} %copy-done.2, ...), custom_call_target="tpu_custom_call" | custom-call | flops 4294967296 | bytes 4718592 | tf_op jit(solution)/shard_map/warp/pallas_call | solution.py:200
  20.9 1.9 %collective-permute-start.6 = (bf16[4,128,128]{2,1,0:T(8,128)(2,1)S(1)}, bf16[4,128,128]{2,1,0:T(8,128)(2,1)S(1)}, u32[]{:S(2)}, u32[]{:S(2)}) collective-permute-start(bf16[4,128,128]{2,1,0:T(8,128)(2,1)S(1)} %get-tuple-element.25), channel_id=1, source_target_pairs={{0,8},{8,0},{16,24},{24,16},{1,9},{9,1},{17,25},{25,17},{2,10},{10... | collective-permute-start | bytes 393224 | tf_op jit(solution)/shard_map/ppermute | solution.py:378
  22.7 1.7 %collective-permute-start.7 = (bf16[4,128,128]{2,1,0:T(8,128)(2,1)S(1)}, bf16[4,128,128]{2,1,0:T(8,128)(2,1)S(1)}, u32[]{:S(2)}, u32[]{:S(2)}) collective-permute-start(bf16[4,128,128]{2,1,0:T(8,128)(2,1)S(1)} %get-tuple-element.26), channel_id=1, source_target_pairs={{0,16},{8,24},{16,0},{24,8},{1,17},{9,25},{17,1},{25,9},{2,18},{10... | collective-permute-start | bytes 393224 | tf_op jit(solution)/shard_map/ppermute | solution.py:378
  24.4 0.9 %collective-permute-start.8 = (bf16[4,128,128]{2,1,0:T(8,128)(2,1)S(1)}, bf16[4,128,128]{2,1,0:T(8,128)(2,1)S(1)}, u32[]{:S(2)}, u32[]{:S(2)}) collective-permute-start(bf16[4,128,128]{2,1,0:T(8,128)(2,1)S(1)} %get-tuple-element.27), channel_id=1, source_target_pairs={{0,24},{8,16},{16,8},{24,0},{1,25},{9,17},{17,9},{25,1},{2,26},{10... | collective-permute-start | bytes 393224 | tf_op jit(solution)/shard_map/ppermute | solution.py:378
  25.4 0.7 %copy-done.3 = s32[2,2,32]{2,1,0:T(2,128)S(1)} copy-done((s32[2,2,32]{2,1,0:T(2,128)S(1)}, s32[2,2,32]{2,1,0:T(2,128)}, u32[]{:S(2)}) %copy-start.3) | copy-done | bytes 536
  26.1 7.5 %lag_windows.1 = (f32[2,8,256]{2,1,0:T(8,128)S(1)}, f32[2,8,256]{2,1,0:T(8,128)S(1)}, f32[2,8,256]{2,1,0:T(8,128)S(1)}, f32[2,8,256]{2,1,0:T(8,128)S(1)}) custom-call(s32[4]{0:T(128)S(1)} %pad_add_fusion.refs_0_, s32[2,2,32]{2,1,0:T(2,128)S(1)} %copy-done.1, s32[2,2,32]{2,1,0:T(2,128)S(1)} %copy-done.3, bf16[128,256]{1,0:T(8,128)(2,1)S(1)} %copy-done.6, ...), custom_call_target="tpu_custom_call" | custom-call | flops 6442450944 | bytes 4718592 | tf_op jit(solution)/shard_map/lag_windows/pallas_call | solution.py:354
  33.6 1.4 %collective-permute-done.7 = bf16[4,128,128]{2,1,0:T(8,128)(2,1)S(1)} collective-permute-done((bf16[4,128,128]{2,1,0:T(8,128)(2,1)S(1)}, bf16[4,128,128]{2,1,0:T(8,128)(2,1)S(1)}, u32[]{:S(2)}, u32[]{:S(2)}) %collective-permute-start.7) | collective-permute-done | bytes 131104 | tf_op jit(solution)/shard_map/ppermute | solution.py:378
  35.1 0.1 collective-permute-start.10
  35.2 1.6 %collective-permute-start.11 = (f32[2,8,256]{2,1,0:T(8,128)S(1)}, f32[2,8,256]{2,1,0:T(8,128)S(1)}, u32[]{:S(2)}, u32[]{:S(2)}) collective-permute-start(f32[2,8,256]{2,1,0:T(8,128)S(1)} %get-tuple-element.31), channel_id=1, source_target_pairs={{0,3},{1,2},{2,1},{3,0},{4,7},{5,6},{6,5},{7,4},{8,11},{9,10},{10,... | collective-permute-start | bytes 49160 | tf_op jit(solution)/shard_map/ppermute | solution.py:378
  36.8 0.5 %collective-permute-start.9 = (f32[2,8,256]{2,1,0:T(8,128)S(1)}, f32[2,8,256]{2,1,0:T(8,128)S(1)}, u32[]{:S(2)}, u32[]{:S(2)}) collective-permute-start(f32[2,8,256]{2,1,0:T(8,128)S(1)} %get-tuple-element.29), channel_id=1, source_target_pairs={{0,1},{1,0},{2,3},{3,2},{4,5},{5,4},{6,7},{7,6},{8,9},{9,8},{10,11... | collective-permute-start | bytes 49160 | tf_op jit(solution)/shard_map/ppermute | solution.py:378
  37.3 1.5 %collective-permute-start.12 = (bf16[2,128,128]{2,1,0:T(8,128)(2,1)S(1)}, bf16[2,128,128]{2,1,0:T(8,128)(2,1)S(1)}, u32[]{:S(2)}, u32[]{:S(2)}) collective-permute-start(bf16[2,128,128]{2,1,0:T(8,128)(2,1)S(1)} %convert_add_fusion), channel_id=1, source_target_pairs={{0,4},{4,0},{1,5},{5,1},{2,6},{6,2},{3,7},{7,3},{8,12},{12,8},{9,1... | collective-permute-start | bytes 196616 | tf_op jit(solution)/shard_map/ppermute | solution.py:378
  38.8 1.7 %collective-permute-done.9 = f32[2,8,256]{2,1,0:T(8,128)S(1)} collective-permute-done((f32[2,8,256]{2,1,0:T(8,128)S(1)}, f32[2,8,256]{2,1,0:T(8,128)S(1)}, u32[]{:S(2)}, u32[]{:S(2)}) %collective-permute-start.9) | collective-permute-done | bytes 16416 | tf_op jit(solution)/shard_map/ppermute | solution.py:378
  40.6 0.6 %reshape.15 = f32[2,16,256]{2,1,0:T(8,128)} reshape(f32[2,4,2,2,256]{4,3,2,1,0:T(2,128)S(1)} %copy.13) | data formatting | bytes 65536 | tf_op jit(solution)/shard_map/reshape | solution.py:416
  41.2 0.3 collective-permute-done.12
  41.6 0.7 %multiply_bitcast_fusion = f32[2,1,128,128]{3,2,1,0:T(8,128)} fusion(f32[2,128,128]{2,1,0:T(8,128)S(1)} %convert_add_fusion.1, bf16[2,128,128]{2,1,0:T(8,128)(2,1)S(1)} %collective-permute-done.12), kind=kLoop, calls=%fused_computation.1 | loop fusion | flops 98304 | bytes 327680
  (31 shorter events, 0.2 us)
Async XLA Ops:
  0.6 5.5 %collective-permute-start.1 = (bf16[2,1,128,128]{3,2,0,1:T(8,128)(2,1)}, bf16[2,1,128,128]{3,2,0,1:T(8,128)(2,1)S(1)}, u32[]{:S(2)}, u32[]{:S(2)}) collective-permute-start(bf16[2,1,128,128]{3,2,0,1:T(8,128)(2,1)} %bitcast.25), channel_id=1, source_target_pairs={{0,4},{4,0},{1,5},{5,1},{2,6},{6,2},{3,7},{7,3},{8,12},{12,8},{9,1... | collective-permute-start | bytes 196616 | tf_op jit(solution)/shard_map/ppermute | solution.py:378
  6.1 6.2 %collective-permute-start.2 = (bf16[2,1,512,1024]{3,2,0,1:T(8,128)(2,1)}, bf16[2,1,512,1024]{3,2,0,1:T(8,128)(2,1)S(1)}, u32[]{:S(2)}, u32[]{:S(2)}) collective-permute-start(bf16[2,1,512,1024]{3,2,0,1:T(8,128)(2,1)} %bitcast.17), channel_id=1, source_target_pairs={{0,2},{2,0},{1,3},{3,1},{4,6},{6,4},{5,7},{7,5},{8,10},{10,8},{9,1... | collective-permute-start | bytes 6291464 | tf_op jit(solution)/shard_map/ppermute | solution.py:378
  6.1 6.2 %collective-permute-start = (s32[2,2,32]{2,1,0:T(2,128)}, s32[2,2,32]{2,1,0:T(2,128)S(1)}, u32[]{:S(2)}, u32[]{:S(2)}) collective-permute-start(s32[2,2,32]{2,1,0:T(2,128)} %refs_1_.3), channel_id=1, source_target_pairs={{0,2},{2,0},{1,3},{3,1},{4,6},{6,4},{5,7},{7,5},{8,10},{10,8},{9,1... | collective-permute-start | bytes 1544 | tf_op jit(solution)/shard_map/ppermute | solution.py:378
  7.6 16.9 %collective-permute-start.4 = (bf16[4,1,128,128]{3,2,0,1:T(8,128)(2,1)S(1)}, bf16[4,1,128,128]{3,2,0,1:T(8,128)(2,1)S(1)}, u32[]{:S(2)}, u32[]{:S(2)}) collective-permute-start(bf16[4,1,128,128]{3,2,0,1:T(8,128)(2,1)S(1)} %get-tuple-element.36), channel_id=1, source_target_pairs={{0,16},{8,24},{16,0},{24,8},{1,17},{9,25},{17,1},{25,9},{2,18},{10... | collective-permute-start | bytes 393224 | tf_op jit(solution)/shard_map/ppermute | solution.py:378
  10.7 14.6 %collective-permute-start.5 = (bf16[4,1,128,128]{3,2,0,1:T(8,128)(2,1)S(1)}, bf16[4,1,128,128]{3,2,0,1:T(8,128)(2,1)S(1)}, u32[]{:S(2)}, u32[]{:S(2)}) collective-permute-start(bf16[4,1,128,128]{3,2,0,1:T(8,128)(2,1)S(1)} %get-tuple-element.36), channel_id=1, source_target_pairs={{0,24},{8,16},{16,8},{24,0},{1,25},{9,17},{17,9},{25,1},{2,26},{10... | collective-permute-start | bytes 393224 | tf_op jit(solution)/shard_map/ppermute | solution.py:378
  12.1 13.3 %collective-permute-start.3 = (bf16[4,1,128,128]{3,2,0,1:T(8,128)(2,1)S(1)}, bf16[4,1,128,128]{3,2,0,1:T(8,128)(2,1)S(1)}, u32[]{:S(2)}, u32[]{:S(2)}) collective-permute-start(bf16[4,1,128,128]{3,2,0,1:T(8,128)(2,1)S(1)} %get-tuple-element.36), channel_id=1, source_target_pairs={{0,8},{8,0},{16,24},{24,16},{1,9},{9,1},{17,25},{25,17},{2,10},{10... | collective-permute-start | bytes 393224 | tf_op jit(solution)/shard_map/ppermute | solution.py:378
  12.3 0.6 %copy-start.2 = (s32[2,2,32]{2,1,0:T(2,128)}, s32[2,2,32]{2,1,0:T(2,128)S(1)}, u32[]{:S(2)}) copy-start(s32[2,2,32]{2,1,0:T(2,128)S(1)} %collective-permute-done.refs_2_) | copy-start | bytes 1540
  12.9 12.5 %copy-start = (bf16[2,1,512,1024]{3,2,1,0:T(8,128)(2,1)S(1)}, bf16[2,1,512,1024]{3,2,1,0:T(8,128)(2,1)}, u32[]{:S(2)}) copy-start(bf16[2,1,512,1024]{3,2,1,0:T(8,128)(2,1)} %param.8) | copy-start | bytes 6291460
  12.9 12.5 %copy-start.1 = (s32[2,2,32]{2,1,0:T(2,128)S(1)}, s32[2,2,32]{2,1,0:T(2,128)}, u32[]{:S(2)}) copy-start(s32[2,2,32]{2,1,0:T(2,128)} %refs_1_.3) | copy-start | bytes 1540
  12.9 12.5 %copy-start.4 = (bf16[16,32,144]{2,1,0:T(8,128)(2,1)S(1)}, bf16[16,32,144]{2,1,0:T(8,128)(2,1)}, u32[]{:S(2)}) copy-start(bf16[16,32,144]{2,1,0:T(8,128)(2,1)} %constant.31.clone.refs_5_) | copy-start | bytes 442372
  12.9 12.5 %copy-start.5 = (bf16[144,256]{1,0:T(8,128)(2,1)S(1)}, bf16[144,256]{1,0:T(8,128)(2,1)}, u32[]{:S(2)}) copy-start(bf16[144,256]{1,0:T(8,128)(2,1)} %constant.30.clone.refs_4_) | copy-start | bytes 221188
  12.9 12.5 %copy-start.6 = (bf16[128,256]{1,0:T(8,128)(2,1)S(1)}, bf16[128,256]{1,0:T(8,128)(2,1)}, u32[]{:S(2)}) copy-start(bf16[128,256]{1,0:T(8,128)(2,1)} %constant.29.clone.refs_3_) | copy-start | bytes 196612
  12.9 12.5 %copy-start.7 = (bf16[256,128]{1,0:T(8,128)(2,1)S(1)}, bf16[256,128]{1,0:T(8,128)(2,1)}, u32[]{:S(2)}) copy-start(bf16[256,128]{1,0:T(8,128)(2,1)} %constant.32.clone.refs_6_) | copy-start | bytes 196612
  20.9 12.7 %collective-permute-start.6 = (bf16[4,128,128]{2,1,0:T(8,128)(2,1)S(1)}, bf16[4,128,128]{2,1,0:T(8,128)(2,1)S(1)}, u32[]{:S(2)}, u32[]{:S(2)}) collective-permute-start(bf16[4,128,128]{2,1,0:T(8,128)(2,1)S(1)} %get-tuple-element.25), channel_id=1, source_target_pairs={{0,8},{8,0},{16,24},{24,16},{1,9},{9,1},{17,25},{25,17},{2,10},{10... | collective-permute-start | bytes 393224 | tf_op jit(solution)/shard_map/ppermute | solution.py:378
  22.7 12.3 %collective-permute-start.7 = (bf16[4,128,128]{2,1,0:T(8,128)(2,1)S(1)}, bf16[4,128,128]{2,1,0:T(8,128)(2,1)S(1)}, u32[]{:S(2)}, u32[]{:S(2)}) collective-permute-start(bf16[4,128,128]{2,1,0:T(8,128)(2,1)S(1)} %get-tuple-element.26), channel_id=1, source_target_pairs={{0,16},{8,24},{16,0},{24,8},{1,17},{9,25},{17,1},{25,9},{2,18},{10... | collective-permute-start | bytes 393224 | tf_op jit(solution)/shard_map/ppermute | solution.py:378
  24.4 10.6 %collective-permute-start.8 = (bf16[4,128,128]{2,1,0:T(8,128)(2,1)S(1)}, bf16[4,128,128]{2,1,0:T(8,128)(2,1)S(1)}, u32[]{:S(2)}, u32[]{:S(2)}) collective-permute-start(bf16[4,128,128]{2,1,0:T(8,128)(2,1)S(1)} %get-tuple-element.27), channel_id=1, source_target_pairs={{0,24},{8,16},{16,8},{24,0},{1,25},{9,17},{17,9},{25,1},{2,26},{10... | collective-permute-start | bytes 393224 | tf_op jit(solution)/shard_map/ppermute | solution.py:378
  25.4 0.7 %copy-start.3 = (s32[2,2,32]{2,1,0:T(2,128)S(1)}, s32[2,2,32]{2,1,0:T(2,128)}, u32[]{:S(2)}) copy-start(s32[2,2,32]{2,1,0:T(2,128)} %copy-done.2) | copy-start | bytes 1540
  35.1 3.7 %collective-permute-start.10 = (f32[2,8,256]{2,1,0:T(8,128)S(1)}, f32[2,8,256]{2,1,0:T(8,128)S(1)}, u32[]{:S(2)}, u32[]{:S(2)}) collective-permute-start(f32[2,8,256]{2,1,0:T(8,128)S(1)} %get-tuple-element.30), channel_id=1, source_target_pairs={{0,2},{1,3},{2,0},{3,1},{4,6},{5,7},{6,4},{7,5},{8,10},{9,11},{10,... | collective-permute-start | bytes 49160 | tf_op jit(solution)/shard_map/ppermute | solution.py:378
  35.2 3.7 %collective-permute-start.11 = (f32[2,8,256]{2,1,0:T(8,128)S(1)}, f32[2,8,256]{2,1,0:T(8,128)S(1)}, u32[]{:S(2)}, u32[]{:S(2)}) collective-permute-start(f32[2,8,256]{2,1,0:T(8,128)S(1)} %get-tuple-element.31), channel_id=1, source_target_pairs={{0,3},{1,2},{2,1},{3,0},{4,7},{5,6},{6,5},{7,4},{8,11},{9,10},{10,... | collective-permute-start | bytes 49160 | tf_op jit(solution)/shard_map/ppermute | solution.py:378
  36.8 3.7 %collective-permute-start.9 = (f32[2,8,256]{2,1,0:T(8,128)S(1)}, f32[2,8,256]{2,1,0:T(8,128)S(1)}, u32[]{:S(2)}, u32[]{:S(2)}) collective-permute-start(f32[2,8,256]{2,1,0:T(8,128)S(1)} %get-tuple-element.29), channel_id=1, source_target_pairs={{0,1},{1,0},{2,3},{3,2},{4,5},{5,4},{6,7},{7,6},{8,9},{9,8},{10,11... | collective-permute-start | bytes 49160 | tf_op jit(solution)/shard_map/ppermute | solution.py:378
  37.3 4.3 %collective-permute-start.12 = (bf16[2,128,128]{2,1,0:T(8,128)(2,1)S(1)}, bf16[2,128,128]{2,1,0:T(8,128)(2,1)S(1)}, u32[]{:S(2)}, u32[]{:S(2)}) collective-permute-start(bf16[2,128,128]{2,1,0:T(8,128)(2,1)S(1)} %convert_add_fusion), channel_id=1, source_target_pairs={{0,4},{4,0},{1,5},{5,1},{2,6},{6,2},{3,7},{7,3},{8,12},{12,8},{9,1... | collective-permute-start | bytes 196616 | tf_op jit(solution)/shard_map/ppermute | solution.py:378

commit v6 on v5

--- a/solution.py
+++ b/solution.py
@@ -26,31 +26,25 @@
     cosine = np.cos(angles)
     sine = -np.sin(angles)
     half = block_size // 2 + 1
-    rows = -(-half // 8) * 8
-    row_table = np.concatenate([cosine, sine], axis=1)
-    col_table = np.zeros((2 * rows, 2 * block_size))
-    col_table[:half] = np.concatenate([cosine[:half], -sine[:half]], axis=1)
-    col_table[rows : rows + half] = np.concatenate([sine[:half], cosine[:half]], axis=1)
-    weights = np.zeros((rows,))
-    weights[:half] = 2.0
+    rows = -(-half // 16) * 16
+    row_table = np.zeros((2 * rows, block_size))
+    row_table[:half] = cosine[:half]
+    row_table[rows : rows + half] = sine[:half]
+    col_table = np.block([[cosine, sine], [-sine, cosine]])
+    weights = np.full((half,), 2.0)
     weights[0] = weights[half - 1] = 1.0
-    starts = 2 * SHIFT
-    lag_table = np.zeros((starts, 2 * WIN, 2 * rows))
-    for start in range(starts):
-        lags = start - SHIFT - WIN // 2 + np.arange(WIN)
-        turns = full_turn * (np.outer(lags, positions[:half]) % block_size) / block_size
-        lag_cos = np.cos(turns) * weights[:half]
-        lag_sin = np.sin(turns) * weights[:half]
-        lag_table[start, :WIN, :half] = lag_cos
-        lag_table[start, :WIN, rows : rows + half] = -lag_sin
-        lag_table[start, WIN:, :half] = lag_sin
-        lag_table[start, WIN:, rows : rows + half] = lag_cos
-    span = starts + WIN
+    span = 2 * SHIFT + WIN
     lags = np.arange(span) - SHIFT - WIN // 2
-    turns = full_turn * (np.outer(positions, lags) % block_size) / block_size
+    turns = full_turn * (np.outer(lags, positions) % block_size) / block_size
+    lag_cos, lag_sin = np.cos(turns), np.sin(turns)
+    lag_table = np.zeros((2 * span, 2 * rows))
+    lag_table[:span, :half] = lag_cos[:, :half] * weights
+    lag_table[:span, rows : rows + half] = -lag_sin[:, :half] * weights
+    lag_table[span:, :half] = lag_sin[:, :half] * weights
+    lag_table[span:, rows : rows + half] = lag_cos[:, :half] * weights
     span_table = np.zeros((2 * block_size, LANES))
-    span_table[:block_size, :span] = np.cos(turns)
-    span_table[block_size:, :span] = -np.sin(turns)
+    span_table[:block_size, :span] = lag_cos.T
+    span_table[block_size:, :span] = -lag_sin.T
     return tuple(
         jnp.asarray(table, jnp.bfloat16) for table in (row_table, col_table, lag_table, span_table)
     )
@@ -61,11 +55,10 @@
     spots = offsets[None, :] - np.arange(SUB)[:, None] / SUB
     raw_taps = np.sinc(spots) * np.sinc(spots / (TAPS // 2))
     taps = raw_taps / raw_taps.sum(axis=-1, keepdims=True)
-    table = np.zeros((2, SUB, EDGE, LANES))
+    heads = np.zeros((SUB, EDGE, LANES))
     for row in range(EDGE):
-        table[0, :, row, row : row + TAPS] = taps
-        table[1, :, row, row : row + TAPS] = taps[:, ::-1]
-    return jnp.asarray(table, jnp.float32)
+        heads[:, row, row : row + TAPS] = taps[:, ::-1]
+    return jnp.asarray(taps, jnp.float32), jnp.asarray(heads, jnp.float32)
 
 
 def band_groups(head, start, lane):
@@ -93,14 +86,15 @@
 
 
 def warp_kernel(vols, down, across, block, own, depth, *refs):
-    place_ref, codes_hbm, other_codes_hbm, taps_hbm, frames_hbm, other_frames_ref = refs[:6]
-    out_refs = refs[6 : 6 + depth]
-    codes_ref, other_codes_ref, taps_ref, frames_ref, sums, sems = refs[6 + depth :]
+    place_ref, codes_hbm, other_codes_hbm, taps_hbm, heads_hbm, frames_hbm = refs[:6]
+    other_frames_ref, out_refs = refs[6], refs[7 : 7 + depth]
+    codes_ref, other_codes_ref, taps_ref, heads_ref, frames_ref, columns, sums, sems = refs[7 + depth :]
     moves = [
         (frames_hbm, frames_ref),
         (codes_hbm, codes_ref),
         (other_codes_hbm, other_codes_ref),
         (taps_hbm, taps_ref),
+        (heads_hbm, heads_ref),
     ]
     copies = [
         pltpu.make_async_copy(source, target, sems.at[at])
@@ -131,49 +125,34 @@
             lanes = pl.ds(pl.multiple_of(at * block, block), block)
             above = jnp.where(band > 0, frames[v, pl.ds(row_above, EDGE), lanes], zero)
             below = jnp.where(band < down - 1, frames[v, pl.ds(row_below, EDGE), lanes], zero)
-            return jnp.concatenate([frames[v, pl.ds(row, block), lanes], below, above], axis=0)
-
-        for count, (index, at) in enumerate(step_places(place_ref, step, across, own)):
-            row_tiles, first_edge, last_edge = [], [], []
-            partials, edges = [], []
+            return jnp.concatenate([above, frames[v, pl.ds(row, block), lanes], below], axis=0)
+
+        places = step_places(place_ref, step, across, own)
+        for count, (index, at) in enumerate(places):
             for order, volume in enumerate(volumes):
                 codes, _, v = volume
-                row_code = codes[v, 0, index]
                 col_code = codes[v, 1, index]
                 middle, before, after = band_groups(
-                    taps_ref[1, col_code & (SUB - 1)], -after_taps - (col_code >> 4), lane
+                    heads_ref[col_code & (SUB - 1)], -after_taps - (col_code >> 4), lane
                 )
                 left = jnp.where(at > 0, tile(volume, jnp.maximum(at - 1, 0)), no_tile)
                 right = jnp.where(
                     at < across - 1, tile(volume, jnp.minimum(at + 1, across - 1)), no_tile
                 )
                 sides = jnp.where(tall_lane < LANES // 2, right, left)
-                partial = jnp.dot(
+                columns[count * 2 * vols + order] = jnp.dot(
                     jnp.concatenate([tile(volume, at), sides], axis=1),
                     jnp.concatenate([*middle, before, gap, after], axis=0),
                     preferred_element_type=jnp.float32,
-                ).astype(jnp.bfloat16)
-                partials.append(partial[:block])
-                edges.append(partial[block:])
-                middle, before, after = band_groups(
-                    taps_ref[0, row_code & (SUB - 1)], (row_code >> 4) - before_taps, lane
                 )
-                row_tiles.append(jnp.concatenate(middle, axis=0))
-                place = 2 * EDGE * order % LANES
-                first_edge.append(pltpu.roll(before, (place + 2 * EDGE) % LANES, 1))
-                last_edge.append(pltpu.roll(after, place, 1) if place else after)
-            per_tile = LANES // (2 * EDGE)
-            for start in range(0, 2 * vols, per_tile):
-                first, last = first_edge[start], last_edge[start]
-                for more in range(start + 1, min(start + per_tile, 2 * vols)):
-                    first, last = first + first_edge[more], last + last_edge[more]
-                row_tiles.append(jnp.concatenate([first, gap, last], axis=0))
-            deep = 2 * vols * (block + 2 * EDGE)
-            total = jnp.dot(
-                jnp.concatenate(row_tiles, axis=1)[:, :deep],
-                jnp.concatenate(partials + edges, axis=0),
-                preferred_element_type=jnp.float32,
-            )
+        for count, (index, _) in enumerate(places):
+            total = jnp.zeros((block, block), jnp.float32)
+            for order, (codes, _, v) in enumerate(volumes):
+                row_code = codes[v, 0, index]
+                start = EDGE - before_taps + (row_code >> 4)
+                for tap in range(TAPS):
+                    part = columns[count * 2 * vols + order, pl.ds(start + tap, block), :]
+                    total += taps_ref[row_code & (SUB - 1), tap] * part
             sums[count] = total.astype(jnp.bfloat16)
         for at_step, out_ref in enumerate(out_refs):
 
@@ -189,26 +168,28 @@
 def warp_sums(place, codes, other_codes, frames, other_frames, depth, block, own):
     vols, rows, cols = frames.shape
     down, across = rows // block, cols // block
-    taps = tap_constants()
+    taps, heads = tap_constants()
     out = (2 * own, block, block)
     hbm = pl.BlockSpec(memory_space=pltpu.HBM)
     kept = [
         pltpu.with_memory_space_constraint(one, pltpu.HBM)
-        for one in (codes, other_codes, taps, frames)
+        for one in (codes, other_codes, taps, heads, frames)
     ]
     vmem = pl.BlockSpec(memory_space=pltpu.VMEM)
     return pl.pallas_call(
         functools.partial(warp_kernel, vols, down, across, block, own, depth),
         out_shape=[jax.ShapeDtypeStruct(out, jnp.bfloat16)] * depth,
-        in_specs=[pl.BlockSpec(memory_space=pltpu.SMEM), hbm, hbm, hbm, hbm, vmem],
+        in_specs=[pl.BlockSpec(memory_space=pltpu.SMEM)] + [hbm] * 5 + [vmem],
         out_specs=[vmem] * depth,
         scratch_shapes=[
             pltpu.SMEM(codes.shape, jnp.int32),
             pltpu.SMEM(codes.shape, jnp.int32),
-            pltpu.VMEM(taps.shape, jnp.float32),
+            pltpu.SMEM(taps.shape, jnp.float32),
+            pltpu.VMEM(heads.shape, jnp.float32),
             pltpu.VMEM(frames.shape, jnp.bfloat16),
+            pltpu.VMEM((2 * vols * 2 * own, block + 2 * EDGE, block), jnp.float32),
             pltpu.VMEM(out, jnp.bfloat16),
-            pltpu.SemaphoreType.DMA((4,)),
+            pltpu.SemaphoreType.DMA((5,)),
         ],
         compiler_params=pltpu.CompilerParams(vmem_limit_bytes=VMEM_LIMIT),
         cost_estimate=pl.CostEstimate(
@@ -230,12 +211,17 @@
 
     row_table = row_ref[...]
     col_table = col_ref[...]
-    half = col_table.shape[0] // 2
+    lag_table = lag_ref[...]
+    half = row_table.shape[0] // 2
+    kept = -(-(block // 2 + 1) // 8) * 8
+    span = lag_table.shape[0] // 2
     top = lax.broadcasted_iota(jnp.int32, (8, LANES), 0) == 0
     volumes = [(codes_ref, frames_ref, v) for v in range(vols)]
     volumes += [(other_codes_ref, other_frames_ref, v) for v in range(vols)]
     many = len(volumes)
     local = 2 * own
+    no_rows = jnp.zeros((half - kept, LANES), jnp.float32)
+
     def one_step(step, _):
         places = step_places(place_ref, step, across, own)
         band = step_band(place_ref, step, across, own)
@@ -243,43 +229,46 @@
 
         for pair in range(local // 2):
             pair_places = places[2 * pair : 2 * pair + 2]
-            parts = [templates[step, 2 * pair], templates[step, 2 * pair + 1]]
+            sources = [[templates[step, 2 * pair], templates[step, 2 * pair + 1]]]
             for _, frames, v in volumes:
-                for _, at in pair_places:
-                    parts.append(frames[v, band_rows, pl.ds(pl.multiple_of(at * block, block), block)])
-            rows = jnp.dot(
-                jnp.concatenate(parts, axis=0), row_table, preferred_element_type=jnp.float32
-            ).astype(jnp.bfloat16)
-            spectra = []
-            for source in range(many + 1):
-                stacks = []
+                sources.append(
+                    [
+                        frames[v, band_rows, pl.ds(pl.multiple_of(at * block, block), block)]
+                        for _, at in pair_places
+                    ]
+                )
+            parts = []
+            for source in sources:
+                rows = jnp.dot(
+                    row_table,
+                    jnp.concatenate(source, axis=1),
+                    preferred_element_type=jnp.float32,
+                ).astype(jnp.bfloat16)
                 for side in range(2):
-                    at = (2 * source + side) * block
-                    one = rows[at : at + block]
-                    stacks.append(jnp.concatenate([one[:, :block], one[:, block:]], axis=0))
-                spectra.append(
-                    jnp.dot(
-                        col_table, jnp.concatenate(stacks, axis=1), preferred_element_type=jnp.float32
-                    )
-                )
-            temp = spectra[0].astype(jnp.bfloat16).astype(jnp.float32)
+                    lanes = slice(side * block, (side + 1) * block)
+                    parts.append(jnp.concatenate([rows[:half, lanes], rows[half:, lanes]], axis=1))
+            spectra = jnp.dot(
+                jnp.concatenate(parts, axis=0), col_table, preferred_element_type=jnp.float32
+            )
+            temp = spectra[: 2 * half].astype(jnp.bfloat16).astype(jnp.float32)
             for order in range(many):
                 for side in range(2):
-                    lanes = slice(side * block, (side + 1) * block)
                     one = (2 * pair + side) * many + order
+                    base = (2 * (order + 1) + side) * half
                     total = jnp.zeros((8, LANES), jnp.float32)
-                    for row in range(0, half, 8):
-                        temp_real = temp[row : row + 8, lanes]
-                        temp_imag = temp[half + row : half + row + 8, lanes]
-                        real = spectra[order + 1][row : row + 8, lanes]
-                        imag = spectra[order + 1][half + row : half + row + 8, lanes]
+                    for row in range(0, kept, 8):
+                        at = side * half + row
+                        temp_real = temp[at : at + 8, :block]
+                        temp_imag = temp[at : at + 8, block:]
+                        real = spectra[base + row : base + row + 8, :block]
+                        imag = spectra[base + row : base + row + 8, block:]
                         cross_real = real * temp_real + imag * temp_imag
                         cross_imag = imag * temp_real - real * temp_imag
                         power = cross_real * cross_real + cross_imag * cross_imag
                         magnitude = power * lax.rsqrt(jnp.maximum(power, 1e-36))
                         cross[one, row : row + 8, :] = cross_real
-                        cross[one, half + row : half + row + 8, :] = cross_imag
-                        cross[one, 2 * half + row : 2 * half + row + 8, :] = magnitude
+                        cross[one, kept + row : kept + row + 8, :] = cross_imag
+                        cross[one, 2 * kept + row : 2 * kept + row + 8, :] = magnitude
                         if row == 0:
                             total = jnp.where(top, magnitude, 2.0 * magnitude)
                         elif row == block // 2:
@@ -290,33 +279,47 @@
 
         means = jnp.sum(sums[...], axis=2, keepdims=True) * (1.0 / (block * block)) + 1e-06
         lag_sums = []
-        for one in range(local * many):
-            codes, _, v = volumes[one % many]
-            index, _ = places[one // many]
-            scale = pl.reciprocal(cross[one, 2 * half :, :] + means[one], approx=True)
-            norm = jnp.concatenate(
-                [
-                    (cross[one, :half, :] * scale).astype(jnp.bfloat16),
-                    (cross[one, half : 2 * half, :] * scale).astype(jnp.bfloat16),
-                ],
-                axis=0,
-            )
-            row_shift = codes[v, 0, index] >> 4
-            lag_rows = jnp.dot(
-                lag_ref[row_shift + SHIFT], norm, preferred_element_type=jnp.float32
-            ).astype(jnp.bfloat16)
-            lag_sums.append(jnp.concatenate([lag_rows[:WIN], lag_rows[WIN:]], axis=1))
+        for pair in range(local // 2):
+            for order in range(many):
+                norms = []
+                for side in range(2):
+                    one = (2 * pair + side) * many + order
+                    scale = pl.reciprocal(cross[one, 2 * kept :, :] + means[one], approx=True)
+                    norms.append(
+                        jnp.concatenate(
+                            [
+                                cross[one, :kept, :] * scale,
+                                no_rows,
+                                cross[one, kept : 2 * kept, :] * scale,
+                                no_rows,
+                            ],
+                            axis=0,
+                        ).astype(jnp.bfloat16)
+                    )
+                lag_rows = jnp.dot(
+                    lag_table, jnp.concatenate(norms, axis=1), preferred_element_type=jnp.float32
+                ).astype(jnp.bfloat16)
+                for side in range(2):
+                    lanes = slice(side * block, (side + 1) * block)
+                    lag_sums.append(
+                        jnp.concatenate([lag_rows[:span, lanes], lag_rows[span:, lanes]], axis=1)
+                    )
         lags = jnp.dot(
             jnp.concatenate(lag_sums, axis=0), span_ref[...], preferred_element_type=jnp.float32
         )
-        for one in range(local * many):
-            codes, _, v = volumes[one % many]
-            index, _ = places[one // many]
-            col_shift = codes[v, 1, index] >> 4
-            order = index // (2 * own) * own + one // many % own
-            found[one % many, pl.ds(pl.multiple_of(order * WIN, WIN), WIN), :] = pltpu.roll(
-                lags[one * WIN : (one + 1) * WIN], LANES - SHIFT - col_shift, 1
-            )
+        for pair in range(local // 2):
+            for order, (codes, _, v) in enumerate(volumes):
+                for side in range(2):
+                    index, _ = places[2 * pair + side]
+                    row_shift = codes[v, 0, index] >> 4
+                    col_shift = codes[v, 1, index] >> 4
+                    at = (pair * many + order) * 2 + side
+                    one = lags[at * span : (at + 1) * span]
+                    one = pltpu.roll(one, span - SHIFT - row_shift, 0)[:WIN]
+                    place = index // (2 * own) * own + (2 * pair + side) % own
+                    found[order, pl.ds(pl.multiple_of(place * WIN, WIN), WIN), :] = pltpu.roll(
+                        one, LANES - SHIFT - col_shift, 1
+                    )
         return 0
 
     lax.fori_loop(0, depth, one_step, 0)
@@ -345,7 +348,7 @@
     down, across = rows // block, cols // block
     depth = len(templates)
     tables = dft_constants(block)
-    half = tables[1].shape[0] // 2
+    kept = -(-(block // 2 + 1) // 8) * 8
     smem = pl.BlockSpec(memory_space=pltpu.SMEM)
     vmem = pl.BlockSpec(memory_space=pltpu.VMEM)
     local = depth * 2 * own
@@ -360,7 +363,7 @@
         out_specs=[vmem] * (2 * planes),
         scratch_shapes=[
             pltpu.VMEM((depth, 2 * own, block, block), jnp.bfloat16),
-            pltpu.VMEM((many, 3 * half, LANES), jnp.float32),
+            pltpu.VMEM((many, 3 * kept, LANES), jnp.float32),
             pltpu.VMEM((many, 1, LANES), jnp.float32),
             pltpu.VMEM((2 * vols, local * WIN, LANES), jnp.float32),
         ],

time: 42.5 us -> 42.8 us (level)
  waiting for transfers between devices: 5.92 us -> 7.5 us
  Pallas kernels: 15.4 us -> 14.2 us
    pallas_call x1, Pallas kernels: 7.49 us -> 5.91 us  [lag_windows(): pl.pallas_call(functools.partial(spectrum_kernel, vols, across, block, ow...]
    ppermute x13, waiting for transfers between devices: 5.92 us -> 7.5 us  [exchange(): return lax.ppermute(value, axes, [(at, at ^ turn) for at in range(size)])]
  transfers between devices with their start and end apart: 13 -> 13, of which waited for: 4 -> 4; matrix products, arithmetic and copies ran while one was open for 4% -> 4% of each run, Pallas kernels for 36% -> 33%
where the time goes in v6:
time: 42.8 us; the launch traced here: 42.6 us
  starting transfers between devices  16.5 us (39%)
  Pallas kernels  14.2 us (33%)
  waiting for transfers between devices  7.5 us (18%)
  local copies, waits for them, and re-layouts  1.95 us (5%)
  other arithmetic  1.71 us (4%)
  between operations  0.79 us (2%)
    ppermute x13, starting transfers between devices, exchange(): return lax.ppermute(value, axes, [(at, at ^ turn) for at in range(size)])  16.5 us
    pallas_call x1, Pallas kernels, warp_sums(): pl.pallas_call(functools.partial(warp_kernel, vols, down, across, block,...  8.27 us
    ppermute x13, waiting for transfers between devices, exchange(): return lax.ppermute(value, axes, [(at, at ^ turn) for at in range(size)])  7.5 us
    pallas_call x1, Pallas kernels, lag_windows(): pl.pallas_call(functools.partial(spectrum_kernel, vols, across, block, ow...  5.91 us
    unnamed x16, local copies, waits for them, and re-layouts  1.28 us
    concatenate x1, other arithmetic, on_device(): templates = [jnp.concatenate([template, other_template], axis=0)]  0.86 us
  transfers between devices with their start and end apart: 13, of which 4 were waited for; matrix products, arithmetic and copies ran while one was open for 4% of the time, Pallas kernels for 33%

profile of v6, /device:TPU:0, one launch (start us, length us, event | category | flops | bytes accessed | tf_op | source)
XLA Modules:
  0.0 42.6 jit_solution(11236230650771302921)
XLA Ops:
  0.6 3.0 %collective-permute-start.1 = (bf16[2,1,128,128]{3,2,0,1:T(8,128)(2,1)}, bf16[2,1,128,128]{3,2,0,1:T(8,128)(2,1)S(1)}, u32[]{:S(2)}, u32[]{:S(2)}) collective-permute-start(bf16[2,1,128,128]{3,2,0,1:T(8,128)(2,1)} %bitcast.25), channel_id=1, source_target_pairs={{0,4},{4,0},{1,5},{5,1},{2,6},{6,2},{3,7},{7,3},{8,12},{12,8},{9,1... | collective-permute-start | bytes 196616 | tf_op jit(solution)/shard_map/ppermute | solution.py:381
  3.7 2.5 %collective-permute-done.1 = bf16[2,1,128,128]{3,2,0,1:T(8,128)(2,1)S(1)} collective-permute-done((bf16[2,1,128,128]{3,2,0,1:T(8,128)(2,1)}, bf16[2,1,128,128]{3,2,0,1:T(8,128)(2,1)S(1)}, u32[]{:S(2)}, u32[]{:S(2)}) %collective-permute-start.1) | collective-permute-done | bytes 65568 | tf_op jit(solution)/shard_map/ppermute | solution.py:381
  6.1 0.5 %collective-permute-start = (s32[2,2,32]{2,1,0:T(2,128)}, s32[2,2,32]{2,1,0:T(2,128)S(1)}, u32[]{:S(2)}, u32[]{:S(2)}) collective-permute-start(s32[2,2,32]{2,1,0:T(2,128)} %refs_1_.3), channel_id=1, source_target_pairs={{0,2},{2,0},{1,3},{3,1},{4,6},{6,4},{5,7},{7,5},{8,10},{10,8},{9,1... | collective-permute-start | bytes 1544 | tf_op jit(solution)/shard_map/ppermute | solution.py:381
  6.6 0.1 pad_add_fusion.refs_0_
  6.7 0.9 %pad_maximum_fusion = (bf16[4,1,128,128]{3,2,0,1:T(8,128)(2,1)S(1)}, bf16[4,128,128]{2,1,0:T(8,128)(2,1)S(1)}) fusion(bf16[2,1,128,128]{3,2,0,1:T(8,128)(2,1)S(1)} %collective-permute-done.1, bf16[2,1,128,128]{3,2,0,1:T(8,128)(2,1)} %bitcast.26), kind=kLoop, calls=%fused_computation | loop fusion | flops 65536 | bytes 393216 | tf_op jit(solution)/shard_map/concatenate | solution.py:395
  7.6 3.2 %collective-permute-start.4 = (bf16[4,1,128,128]{3,2,0,1:T(8,128)(2,1)S(1)}, bf16[4,1,128,128]{3,2,0,1:T(8,128)(2,1)S(1)}, u32[]{:S(2)}, u32[]{:S(2)}) collective-permute-start(bf16[4,1,128,128]{3,2,0,1:T(8,128)(2,1)S(1)} %get-tuple-element.36), channel_id=1, source_target_pairs={{0,16},{8,24},{16,0},{24,8},{1,17},{9,25},{17,1},{25,9},{2,18},{10... | collective-permute-start | bytes 393224 | tf_op jit(solution)/shard_map/ppermute | solution.py:381
  10.7 1.3 %collective-permute-start.5 = (bf16[4,1,128,128]{3,2,0,1:T(8,128)(2,1)S(1)}, bf16[4,1,128,128]{3,2,0,1:T(8,128)(2,1)S(1)}, u32[]{:S(2)}, u32[]{:S(2)}) collective-permute-start(bf16[4,1,128,128]{3,2,0,1:T(8,128)(2,1)S(1)} %get-tuple-element.36), channel_id=1, source_target_pairs={{0,24},{8,16},{16,8},{24,0},{1,25},{9,17},{17,9},{25,1},{2,26},{10... | collective-permute-start | bytes 393224 | tf_op jit(solution)/shard_map/ppermute | solution.py:381
  12.1 0.2 collective-permute-start.3
  12.3 0.6 %copy-done.2 = s32[2,2,32]{2,1,0:T(2,128)} copy-done((s32[2,2,32]{2,1,0:T(2,128)}, s32[2,2,32]{2,1,0:T(2,128)S(1)}, u32[]{:S(2)}) %copy-start.2) | copy-done | bytes 536
  12.9 8.3 %warp.1 = (bf16[4,128,128]{2,1,0:T(8,128)(2,1)S(1)}, bf16[4,128,128]{2,1,0:T(8,128)(2,1)S(1)}, bf16[4,128,128]{2,1,0:T(8,128)(2,1)S(1)}, bf16[4,128,128]{2,1,0:T(8,128)(2,1)S(1)}) custom-call(s32[4]{0:T(128)S(1)} %pad_add_fusion.refs_0_, s32[2,2,32]{2,1,0:T(2,128)} %refs_1_.3, s32[2,2,32]{2,1,0:T(2,128)} %copy-done.2, f32[16,8]{1,0:T(8,128)} %constant.30.clone.refs_3_, ...), custom_call_target="tpu_custom_call" | custom-call | flops 4294967296 | bytes 4718592 | tf_op jit(solution)/shard_map/warp/pallas_call | solution.py:179
  21.2 1.9 %collective-permute-start.6 = (bf16[4,128,128]{2,1,0:T(8,128)(2,1)S(1)}, bf16[4,128,128]{2,1,0:T(8,128)(2,1)S(1)}, u32[]{:S(2)}, u32[]{:S(2)}) collective-permute-start(bf16[4,128,128]{2,1,0:T(8,128)(2,1)S(1)} %get-tuple-element.25), channel_id=1, source_target_pairs={{0,8},{8,0},{16,24},{24,16},{1,9},{9,1},{17,25},{25,17},{2,10},{10... | collective-permute-start | bytes 393224 | tf_op jit(solution)/shard_map/ppermute | solution.py:381
  23.1 1.7 %collective-permute-start.7 = (bf16[4,128,128]{2,1,0:T(8,128)(2,1)S(1)}, bf16[4,128,128]{2,1,0:T(8,128)(2,1)S(1)}, u32[]{:S(2)}, u32[]{:S(2)}) collective-permute-start(bf16[4,128,128]{2,1,0:T(8,128)(2,1)S(1)} %get-tuple-element.26), channel_id=1, source_target_pairs={{0,16},{8,24},{16,0},{24,8},{1,17},{9,25},{17,1},{25,9},{2,18},{10... | collective-permute-start | bytes 393224 | tf_op jit(solution)/shard_map/ppermute | solution.py:381
  24.8 0.9 %collective-permute-start.8 = (bf16[4,128,128]{2,1,0:T(8,128)(2,1)S(1)}, bf16[4,128,128]{2,1,0:T(8,128)(2,1)S(1)}, u32[]{:S(2)}, u32[]{:S(2)}) collective-permute-start(bf16[4,128,128]{2,1,0:T(8,128)(2,1)S(1)} %get-tuple-element.27), channel_id=1, source_target_pairs={{0,24},{8,16},{16,8},{24,0},{1,25},{9,17},{17,9},{25,1},{2,26},{10... | collective-permute-start | bytes 393224 | tf_op jit(solution)/shard_map/ppermute | solution.py:381
  25.7 0.7 %copy-done.3 = s32[2,2,32]{2,1,0:T(2,128)S(1)} copy-done((s32[2,2,32]{2,1,0:T(2,128)S(1)}, s32[2,2,32]{2,1,0:T(2,128)}, u32[]{:S(2)}) %copy-start.3) | copy-done | bytes 536
  26.4 5.9 %lag_windows.1 = (f32[2,8,256]{2,1,0:T(8,128)S(1)}, f32[2,8,256]{2,1,0:T(8,128)S(1)}, f32[2,8,256]{2,1,0:T(8,128)S(1)}, f32[2,8,256]{2,1,0:T(8,128)S(1)}) custom-call(s32[4]{0:T(128)S(1)} %pad_add_fusion.refs_0_, s32[2,2,32]{2,1,0:T(2,128)S(1)} %copy-done.1, s32[2,2,32]{2,1,0:T(2,128)S(1)} %copy-done.3, bf16[160,128]{1,0:T(8,128)(2,1)S(1)} %copy-done.6, ...), custom_call_target="tpu_custom_call" | custom-call | flops 6442450944 | bytes 4718592 | tf_op jit(solution)/shard_map/lag_windows/pallas_call | solution.py:357
  32.3 3.0 %collective-permute-done.7 = bf16[4,128,128]{2,1,0:T(8,128)(2,1)S(1)} collective-permute-done((bf16[4,128,128]{2,1,0:T(8,128)(2,1)S(1)}, bf16[4,128,128]{2,1,0:T(8,128)(2,1)S(1)}, u32[]{:S(2)}, u32[]{:S(2)}) %collective-permute-start.7) | collective-permute-done | bytes 131104 | tf_op jit(solution)/shard_map/ppermute | solution.py:381
  35.4 0.1 collective-permute-start.10
  35.5 1.6 %collective-permute-start.11 = (f32[2,8,256]{2,1,0:T(8,128)S(1)}, f32[2,8,256]{2,1,0:T(8,128)S(1)}, u32[]{:S(2)}, u32[]{:S(2)}) collective-permute-start(f32[2,8,256]{2,1,0:T(8,128)S(1)} %get-tuple-element.31), channel_id=1, source_target_pairs={{0,3},{1,2},{2,1},{3,0},{4,7},{5,6},{6,5},{7,4},{8,11},{9,10},{10,... | collective-permute-start | bytes 49160 | tf_op jit(solution)/shard_map/ppermute | solution.py:381
  37.1 0.5 %collective-permute-start.9 = (f32[2,8,256]{2,1,0:T(8,128)S(1)}, f32[2,8,256]{2,1,0:T(8,128)S(1)}, u32[]{:S(2)}, u32[]{:S(2)}) collective-permute-start(f32[2,8,256]{2,1,0:T(8,128)S(1)} %get-tuple-element.29), channel_id=1, source_target_pairs={{0,1},{1,0},{2,3},{3,2},{4,5},{5,4},{6,7},{7,6},{8,9},{9,8},{10,11... | collective-permute-start | bytes 49160 | tf_op jit(solution)/shard_map/ppermute | solution.py:381
  37.7 1.5 %collective-permute-start.12 = (bf16[2,128,128]{2,1,0:T(8,128)(2,1)S(1)}, bf16[2,128,128]{2,1,0:T(8,128)(2,1)S(1)}, u32[]{:S(2)}, u32[]{:S(2)}) collective-permute-start(bf16[2,128,128]{2,1,0:T(8,128)(2,1)S(1)} %convert_add_fusion), channel_id=1, source_target_pairs={{0,4},{4,0},{1,5},{5,1},{2,6},{6,2},{3,7},{7,3},{8,12},{12,8},{9,1... | collective-permute-start | bytes 196616 | tf_op jit(solution)/shard_map/ppermute | solution.py:381
  39.2 1.7 %collective-permute-done.9 = f32[2,8,256]{2,1,0:T(8,128)S(1)} collective-permute-done((f32[2,8,256]{2,1,0:T(8,128)S(1)}, f32[2,8,256]{2,1,0:T(8,128)S(1)}, u32[]{:S(2)}, u32[]{:S(2)}) %collective-permute-start.9) | collective-permute-done | bytes 16416 | tf_op jit(solution)/shard_map/ppermute | solution.py:381
  40.9 0.6 %reshape.15 = f32[2,16,256]{2,1,0:T(8,128)} reshape(f32[2,4,2,2,256]{4,3,2,1,0:T(2,128)S(1)} %copy.14) | data formatting | bytes 65536 | tf_op jit(solution)/shard_map/reshape | solution.py:419
  41.6 0.3 collective-permute-done.12
  41.9 0.7 %multiply_bitcast_fusion = f32[2,1,128,128]{3,2,1,0:T(8,128)} fusion(f32[2,128,128]{2,1,0:T(8,128)S(1)} %convert_add_fusion.1, bf16[2,128,128]{2,1,0:T(8,128)(2,1)S(1)} %collective-permute-done.12), kind=kLoop, calls=%fused_computation.1 | loop fusion | flops 98304 | bytes 327680
  (31 shorter events, 0.2 us)
Async XLA Ops:
  0.6 5.5 %collective-permute-start.1 = (bf16[2,1,128,128]{3,2,0,1:T(8,128)(2,1)}, bf16[2,1,128,128]{3,2,0,1:T(8,128)(2,1)S(1)}, u32[]{:S(2)}, u32[]{:S(2)}) collective-permute-start(bf16[2,1,128,128]{3,2,0,1:T(8,128)(2,1)} %bitcast.25), channel_id=1, source_target_pairs={{0,4},{4,0},{1,5},{5,1},{2,6},{6,2},{3,7},{7,3},{8,12},{12,8},{9,1... | collective-permute-start | bytes 196616 | tf_op jit(solution)/shard_map/ppermute | solution.py:381
  6.1 6.2 %collective-permute-start.2 = (bf16[2,1,512,1024]{3,2,0,1:T(8,128)(2,1)}, bf16[2,1,512,1024]{3,2,0,1:T(8,128)(2,1)S(1)}, u32[]{:S(2)}, u32[]{:S(2)}) collective-permute-start(bf16[2,1,512,1024]{3,2,0,1:T(8,128)(2,1)} %bitcast.17), channel_id=1, source_target_pairs={{0,2},{2,0},{1,3},{3,1},{4,6},{6,4},{5,7},{7,5},{8,10},{10,8},{9,1... | collective-permute-start | bytes 6291464 | tf_op jit(solution)/shard_map/ppermute | solution.py:381
  6.1 6.2 %collective-permute-start = (s32[2,2,32]{2,1,0:T(2,128)}, s32[2,2,32]{2,1,0:T(2,128)S(1)}, u32[]{:S(2)}, u32[]{:S(2)}) collective-permute-start(s32[2,2,32]{2,1,0:T(2,128)} %refs_1_.3), channel_id=1, source_target_pairs={{0,2},{2,0},{1,3},{3,1},{4,6},{6,4},{5,7},{7,5},{8,10},{10,8},{9,1... | collective-permute-start | bytes 1544 | tf_op jit(solution)/shard_map/ppermute | solution.py:381
  7.6 17.2 %collective-permute-start.4 = (bf16[4,1,128,128]{3,2,0,1:T(8,128)(2,1)S(1)}, bf16[4,1,128,128]{3,2,0,1:T(8,128)(2,1)S(1)}, u32[]{:S(2)}, u32[]{:S(2)}) collective-permute-start(bf16[4,1,128,128]{3,2,0,1:T(8,128)(2,1)S(1)} %get-tuple-element.36), channel_id=1, source_target_pairs={{0,16},{8,24},{16,0},{24,8},{1,17},{9,25},{17,1},{25,9},{2,18},{10... | collective-permute-start | bytes 393224 | tf_op jit(solution)/shard_map/ppermute | solution.py:381
  10.7 14.9 %collective-permute-start.5 = (bf16[4,1,128,128]{3,2,0,1:T(8,128)(2,1)S(1)}, bf16[4,1,128,128]{3,2,0,1:T(8,128)(2,1)S(1)}, u32[]{:S(2)}, u32[]{:S(2)}) collective-permute-start(bf16[4,1,128,128]{3,2,0,1:T(8,128)(2,1)S(1)} %get-tuple-element.36), channel_id=1, source_target_pairs={{0,24},{8,16},{16,8},{24,0},{1,25},{9,17},{17,9},{25,1},{2,26},{10... | collective-permute-start | bytes 393224 | tf_op jit(solution)/shard_map/ppermute | solution.py:381
  12.1 13.6 %collective-permute-start.3 = (bf16[4,1,128,128]{3,2,0,1:T(8,128)(2,1)S(1)}, bf16[4,1,128,128]{3,2,0,1:T(8,128)(2,1)S(1)}, u32[]{:S(2)}, u32[]{:S(2)}) collective-permute-start(bf16[4,1,128,128]{3,2,0,1:T(8,128)(2,1)S(1)} %get-tuple-element.36), channel_id=1, source_target_pairs={{0,8},{8,0},{16,24},{24,16},{1,9},{9,1},{17,25},{25,17},{2,10},{10... | collective-permute-start | bytes 393224 | tf_op jit(solution)/shard_map/ppermute | solution.py:381
  12.3 0.6 %copy-start.2 = (s32[2,2,32]{2,1,0:T(2,128)}, s32[2,2,32]{2,1,0:T(2,128)S(1)}, u32[]{:S(2)}) copy-start(s32[2,2,32]{2,1,0:T(2,128)S(1)} %collective-permute-done.refs_2_) | copy-start | bytes 1540
  12.9 12.8 %copy-start = (bf16[2,1,512,1024]{3,2,1,0:T(8,128)(2,1)S(1)}, bf16[2,1,512,1024]{3,2,1,0:T(8,128)(2,1)}, u32[]{:S(2)}) copy-start(bf16[2,1,512,1024]{3,2,1,0:T(8,128)(2,1)} %param.9) | copy-start | bytes 6291460
  12.9 12.8 %copy-start.1 = (s32[2,2,32]{2,1,0:T(2,128)S(1)}, s32[2,2,32]{2,1,0:T(2,128)}, u32[]{:S(2)}) copy-start(s32[2,2,32]{2,1,0:T(2,128)} %refs_1_.3) | copy-start | bytes 1540
  12.9 12.8 %copy-start.4 = (bf16[256,256]{1,0:T(8,128)(2,1)S(1)}, bf16[256,256]{1,0:T(8,128)(2,1)}, u32[]{:S(2)}) copy-start(bf16[256,256]{1,0:T(8,128)(2,1)} %constant.33.clone.refs_4_) | copy-start | bytes 393220
  12.9 12.8 %copy-start.5 = (bf16[256,128]{1,0:T(8,128)(2,1)S(1)}, bf16[256,128]{1,0:T(8,128)(2,1)}, u32[]{:S(2)}) copy-start(bf16[256,128]{1,0:T(8,128)(2,1)} %constant.35.clone.refs_6_) | copy-start | bytes 196612
  12.9 12.8 %copy-start.6 = (bf16[160,128]{1,0:T(8,128)(2,1)S(1)}, bf16[160,128]{1,0:T(8,128)(2,1)}, u32[]{:S(2)}) copy-start(bf16[160,128]{1,0:T(8,128)(2,1)} %constant.32.clone.refs_3_) | copy-start | bytes 122884
  12.9 12.8 %copy-start.7 = (bf16[64,160]{1,0:T(8,128)(2,1)S(1)}, bf16[64,160]{1,0:T(8,128)(2,1)}, u32[]{:S(2)}) copy-start(bf16[64,160]{1,0:T(8,128)(2,1)} %constant.34.clone.refs_5_) | copy-start | bytes 61444
  21.2 11.1 %collective-permute-start.6 = (bf16[4,128,128]{2,1,0:T(8,128)(2,1)S(1)}, bf16[4,128,128]{2,1,0:T(8,128)(2,1)S(1)}, u32[]{:S(2)}, u32[]{:S(2)}) collective-permute-start(bf16[4,128,128]{2,1,0:T(8,128)(2,1)S(1)} %get-tuple-element.25), channel_id=1, source_target_pairs={{0,8},{8,0},{16,24},{24,16},{1,9},{9,1},{17,25},{25,17},{2,10},{10... | collective-permute-start | bytes 393224 | tf_op jit(solution)/shard_map/ppermute | solution.py:381
  23.1 12.3 %collective-permute-start.7 = (bf16[4,128,128]{2,1,0:T(8,128)(2,1)S(1)}, bf16[4,128,128]{2,1,0:T(8,128)(2,1)S(1)}, u32[]{:S(2)}, u32[]{:S(2)}) collective-permute-start(bf16[4,128,128]{2,1,0:T(8,128)(2,1)S(1)} %get-tuple-element.26), channel_id=1, source_target_pairs={{0,16},{8,24},{16,0},{24,8},{1,17},{9,25},{17,1},{25,9},{2,18},{10... | collective-permute-start | bytes 393224 | tf_op jit(solution)/shard_map/ppermute | solution.py:381
  24.8 10.6 %collective-permute-start.8 = (bf16[4,128,128]{2,1,0:T(8,128)(2,1)S(1)}, bf16[4,128,128]{2,1,0:T(8,128)(2,1)S(1)}, u32[]{:S(2)}, u32[]{:S(2)}) collective-permute-start(bf16[4,128,128]{2,1,0:T(8,128)(2,1)S(1)} %get-tuple-element.27), channel_id=1, source_target_pairs={{0,24},{8,16},{16,8},{24,0},{1,25},{9,17},{17,9},{25,1},{2,26},{10... | collective-permute-start | bytes 393224 | tf_op jit(solution)/shard_map/ppermute | solution.py:381
  25.7 0.7 %copy-start.3 = (s32[2,2,32]{2,1,0:T(2,128)S(1)}, s32[2,2,32]{2,1,0:T(2,128)}, u32[]{:S(2)}) copy-start(s32[2,2,32]{2,1,0:T(2,128)} %copy-done.2) | copy-start | bytes 1540
  35.4 3.8 %collective-permute-start.10 = (f32[2,8,256]{2,1,0:T(8,128)S(1)}, f32[2,8,256]{2,1,0:T(8,128)S(1)}, u32[]{:S(2)}, u32[]{:S(2)}) collective-permute-start(f32[2,8,256]{2,1,0:T(8,128)S(1)} %get-tuple-element.30), channel_id=1, source_target_pairs={{0,2},{1,3},{2,0},{3,1},{4,6},{5,7},{6,4},{7,5},{8,10},{9,11},{10,... | collective-permute-start | bytes 49160 | tf_op jit(solution)/shard_map/ppermute | solution.py:381
  35.5 3.7 %collective-permute-start.11 = (f32[2,8,256]{2,1,0:T(8,128)S(1)}, f32[2,8,256]{2,1,0:T(8,128)S(1)}, u32[]{:S(2)}, u32[]{:S(2)}) collective-permute-start(f32[2,8,256]{2,1,0:T(8,128)S(1)} %get-tuple-element.31), channel_id=1, source_target_pairs={{0,3},{1,2},{2,1},{3,0},{4,7},{5,6},{6,5},{7,4},{8,11},{9,10},{10,... | collective-permute-start | bytes 49160 | tf_op jit(solution)/shard_map/ppermute | solution.py:381
  37.1 3.7 %collective-permute-start.9 = (f32[2,8,256]{2,1,0:T(8,128)S(1)}, f32[2,8,256]{2,1,0:T(8,128)S(1)}, u32[]{:S(2)}, u32[]{:S(2)}) collective-permute-start(f32[2,8,256]{2,1,0:T(8,128)S(1)} %get-tuple-element.29), channel_id=1, source_target_pairs={{0,1},{1,0},{2,3},{3,2},{4,5},{5,4},{6,7},{7,6},{8,9},{9,8},{10,11... | collective-permute-start | bytes 49160 | tf_op jit(solution)/shard_map/ppermute | solution.py:381
  37.7 4.3 %collective-permute-start.12 = (bf16[2,128,128]{2,1,0:T(8,128)(2,1)S(1)}, bf16[2,128,128]{2,1,0:T(8,128)(2,1)S(1)}, u32[]{:S(2)}, u32[]{:S(2)}) collective-permute-start(bf16[2,128,128]{2,1,0:T(8,128)(2,1)S(1)} %convert_add_fusion), channel_id=1, source_target_pairs={{0,4},{4,0},{1,5},{5,1},{2,6},{6,2},{3,7},{7,3},{8,12},{12,8},{9,1... | collective-permute-start | bytes 196616 | tf_op jit(solution)/shard_map/ppermute | solution.py:381

commit v7 on v6

--- a/solution.py
+++ b/solution.py
@@ -55,10 +55,11 @@
     spots = offsets[None, :] - np.arange(SUB)[:, None] / SUB
     raw_taps = np.sinc(spots) * np.sinc(spots / (TAPS // 2))
     taps = raw_taps / raw_taps.sum(axis=-1, keepdims=True)
-    heads = np.zeros((SUB, EDGE, LANES))
+    table = np.zeros((2, SUB, EDGE, LANES))
     for row in range(EDGE):
-        heads[:, row, row : row + TAPS] = taps[:, ::-1]
-    return jnp.asarray(taps, jnp.float32), jnp.asarray(heads, jnp.float32)
+        table[0, :, row, row : row + TAPS] = taps
+        table[1, :, row, row : row + TAPS] = taps[:, ::-1]
+    return jnp.asarray(table, jnp.float32)
 
 
 def band_groups(head, start, lane):
@@ -85,111 +86,161 @@
     return (place_ref[0] ^ step) * (4 * own) // across
 
 
-def warp_kernel(vols, down, across, block, own, depth, *refs):
-    place_ref, codes_hbm, other_codes_hbm, taps_hbm, heads_hbm, frames_hbm = refs[:6]
-    other_frames_ref, out_refs = refs[6], refs[7 : 7 + depth]
-    codes_ref, other_codes_ref, taps_ref, heads_ref, frames_ref, columns, sums, sems = refs[7 + depth :]
-    moves = [
-        (frames_hbm, frames_ref),
-        (codes_hbm, codes_ref),
-        (other_codes_hbm, other_codes_ref),
-        (taps_hbm, taps_ref),
-        (heads_hbm, heads_ref),
+def band_kernel(
+    vols, across, own, depth, place_ref, codes_ref, other_codes_ref, heads_ref, *out_refs
+):
+    cols_ref, rows_ref, edges_ref = out_refs
+    lane = lax.broadcasted_iota(jnp.int32, (EDGE, LANES), 1)
+    volumes = [(codes_ref, v) for v in range(vols)] + [(other_codes_ref, v) for v in range(vols)]
+    many = len(volumes)
+    per_tile = LANES // (2 * EDGE)
+
+    def one_step(step, _):
+        for count, (index, _) in enumerate(step_places(place_ref, step, across, own)):
+            block_at = step * (2 * own) + count
+            edges = []
+            for order, (codes, v) in enumerate(volumes):
+                row_code = codes[v, 0, index]
+                col_code = codes[v, 1, index]
+                middle, before, after = band_groups(
+                    heads_ref[1, col_code & (SUB - 1)], -(TAPS // 2) - (col_code >> 4), lane
+                )
+                one = block_at * many + order
+                cols_ref[one] = jnp.concatenate([*middle, before, after], axis=0)
+                middle, before, after = band_groups(
+                    heads_ref[0, row_code & (SUB - 1)], (row_code >> 4) - (TAPS // 2 - 1), lane
+                )
+                rows_ref[one] = jnp.concatenate(middle, axis=0)
+                place = 2 * EDGE * order % LANES
+                first = pltpu.roll(before, (place + 2 * EDGE) % LANES, 1)
+                last = pltpu.roll(after, place, 1) if place else after
+                if order % per_tile:
+                    first, last = edges[-1][0] + first, edges[-1][1] + last
+                    edges.pop()
+                edges.append((first, last))
+            for at, (first, last) in enumerate(edges):
+                edges_ref[block_at * len(edges) + at] = jnp.concatenate([first, last], axis=0)
+        return 0
+
+    lax.fori_loop(0, depth, one_step, 0)
+
+
+def warp_bands(place, codes, other_codes, across, depth, block, own):
+    vols = codes.shape[0]
+    heads = tap_constants()
+    smem = pl.BlockSpec(memory_space=pltpu.SMEM)
+    vmem = pl.BlockSpec(memory_space=pltpu.VMEM)
+    blocks = depth * 2 * own
+    tiles = -(-2 * vols * 2 * EDGE // LANES)
+    shapes = [
+        (blocks * 2 * vols, block + 2 * EDGE, block),
+        (blocks * 2 * vols, block, block),
+        (blocks * tiles, 2 * EDGE, LANES),
     ]
-    copies = [
-        pltpu.make_async_copy(source, target, sems.at[at])
-        for at, (source, target) in enumerate(moves)
-    ]
-    for copy in copies:
-        copy.start()
-    for copy in copies:
-        copy.wait()
-    lane = lax.broadcasted_iota(jnp.int32, (EDGE, LANES), 1)
-    tall_lane = lax.broadcasted_iota(jnp.int32, (block + 2 * EDGE, LANES), 1)
+    return pl.pallas_call(
+        functools.partial(band_kernel, vols, across, own, depth),
+        out_shape=[jax.ShapeDtypeStruct(shape, jnp.bfloat16) for shape in shapes],
+        in_specs=[smem] * 3 + [vmem],
+        out_specs=[vmem] * 3,
+        compiler_params=pltpu.CompilerParams(vmem_limit_bytes=VMEM_LIMIT),
+        cost_estimate=pl.CostEstimate(
+            flops=blocks * vols * block * block * 128, bytes_accessed=0, transcendentals=0
+        ),
+        name="bands",
+    )(place, codes, other_codes, heads)
+
+
+def warp_step(place_ref, step, frame_refs, band_refs, down, across, block, own):
+    cols_ref, rows_ref, edges_ref = band_refs
+    band = step_band(place_ref, step, across, own)
+    row = pl.multiple_of(band * block, block)
+    row_above = pl.multiple_of(jnp.maximum(row - EDGE, 0), EDGE)
+    row_below = pl.multiple_of(jnp.minimum(row + block, down * block - EDGE), EDGE)
     zero = jnp.zeros((EDGE, LANES), jnp.bfloat16)
     gap = jnp.zeros((block - 2 * EDGE, LANES), jnp.bfloat16)
     no_tile = jnp.zeros((block + 2 * EDGE, block), jnp.bfloat16)
-    volumes = [(codes_ref, frames_ref, v) for v in range(vols)]
-    volumes += [(other_codes_ref, other_frames_ref, v) for v in range(vols)]
-    before_taps = TAPS // 2 - 1
-    after_taps = TAPS // 2
+    volumes = [(frames, v) for frames in frame_refs for v in range(frames.shape[0])]
+    many = len(volumes)
+    tiles = -(-many * 2 * EDGE // LANES)
+
+    def tile(frames, v, at):
+        lanes = pl.ds(pl.multiple_of(at * block, block), block)
+        above = jnp.where(band > 0, frames[v, pl.ds(row_above, EDGE), lanes], zero)
+        below = jnp.where(band < down - 1, frames[v, pl.ds(row_below, EDGE), lanes], zero)
+        return jnp.concatenate([frames[v, pl.ds(row, block), lanes], below, above], axis=0)
+
+    totals = []
+    for count, (_, at) in enumerate(step_places(place_ref, step, across, own)):
+        block_at = step * (2 * own) + count
+        row_tiles, partials, edges = [], [], []
+        for order, (frames, v) in enumerate(volumes):
+            one = block_at * many + order
+            left = jnp.where(at > 0, tile(frames, v, jnp.maximum(at - 1, 0)), no_tile)
+            right = jnp.where(
+                at < across - 1, tile(frames, v, jnp.minimum(at + 1, across - 1)), no_tile
+            )
+            sides = jnp.concatenate([right[:, : block // 2], left[:, block // 2 :]], axis=1)
+            cols = cols_ref[one]
+            partial = jnp.dot(
+                jnp.concatenate([tile(frames, v, at), sides], axis=1),
+                jnp.concatenate([cols[: block + EDGE], gap, cols[block + EDGE :]], axis=0),
+                preferred_element_type=jnp.float32,
+            ).astype(jnp.bfloat16)
+            partials.append(partial[:block])
+            edges.append(partial[block:])
+            row_tiles.append(rows_ref[one])
+        for at_tile in range(tiles):
+            both = edges_ref[block_at * tiles + at_tile]
+            row_tiles.append(jnp.concatenate([both[:EDGE], gap, both[EDGE:]], axis=0))
+        deep = many * (block + 2 * EDGE)
+        total = jnp.dot(
+            jnp.concatenate(row_tiles, axis=1)[:, :deep],
+            jnp.concatenate(partials + edges, axis=0),
+            preferred_element_type=jnp.float32,
+        )
+        totals.append(total.astype(jnp.bfloat16))
+    return totals
+
+
+def warp_kernel(down, across, block, own, depth, *refs):
+    place_ref, frames_hbm, other_frames_ref, *band_refs = refs[:6]
+    out_refs = refs[6 : 5 + depth]
+    frames_ref, sums, sem = refs[5 + depth :]
+    copy = pltpu.make_async_copy(frames_hbm, frames_ref, sem)
+    copy.start()
+    copy.wait()
+    frame_refs = (frames_ref, other_frames_ref)
 
     def one_step(step, _):
-        band = step_band(place_ref, step, across, own)
-        row = pl.multiple_of(band * block, block)
-        row_above = pl.multiple_of(jnp.maximum(row - EDGE, 0), EDGE)
-        row_below = pl.multiple_of(jnp.minimum(row + block, down * block - EDGE), EDGE)
-
-        def tile(volume, at):
-            _, frames, v = volume
-            lanes = pl.ds(pl.multiple_of(at * block, block), block)
-            above = jnp.where(band > 0, frames[v, pl.ds(row_above, EDGE), lanes], zero)
-            below = jnp.where(band < down - 1, frames[v, pl.ds(row_below, EDGE), lanes], zero)
-            return jnp.concatenate([above, frames[v, pl.ds(row, block), lanes], below], axis=0)
-
-        places = step_places(place_ref, step, across, own)
-        for count, (index, at) in enumerate(places):
-            for order, volume in enumerate(volumes):
-                codes, _, v = volume
-                col_code = codes[v, 1, index]
-                middle, before, after = band_groups(
-                    heads_ref[col_code & (SUB - 1)], -after_taps - (col_code >> 4), lane
-                )
-                left = jnp.where(at > 0, tile(volume, jnp.maximum(at - 1, 0)), no_tile)
-                right = jnp.where(
-                    at < across - 1, tile(volume, jnp.minimum(at + 1, across - 1)), no_tile
-                )
-                sides = jnp.where(tall_lane < LANES // 2, right, left)
-                columns[count * 2 * vols + order] = jnp.dot(
-                    jnp.concatenate([tile(volume, at), sides], axis=1),
-                    jnp.concatenate([*middle, before, gap, after], axis=0),
-                    preferred_element_type=jnp.float32,
-                )
-        for count, (index, _) in enumerate(places):
-            total = jnp.zeros((block, block), jnp.float32)
-            for order, (codes, _, v) in enumerate(volumes):
-                row_code = codes[v, 0, index]
-                start = EDGE - before_taps + (row_code >> 4)
-                for tap in range(TAPS):
-                    part = columns[count * 2 * vols + order, pl.ds(start + tap, block), :]
-                    total += taps_ref[row_code & (SUB - 1), tap] * part
-            sums[count] = total.astype(jnp.bfloat16)
-        for at_step, out_ref in enumerate(out_refs):
-
-            @pl.when(step == at_step)
+        totals = warp_step(place_ref, step, frame_refs, band_refs, down, across, block, own)
+        for count, total in enumerate(totals):
+            sums[count] = total
+        for at, out_ref in enumerate(out_refs):
+
+            @pl.when(step == at + 1)
             def _():
                 out_ref[...] = sums[...]
 
         return 0
 
-    lax.fori_loop(0, depth, one_step, 0)
-
-
-def warp_sums(place, codes, other_codes, frames, other_frames, depth, block, own):
+    lax.fori_loop(1, depth, one_step, 0)
+
+
+def warp_sums(place, frames, other_frames, bands, depth, block, own):
     vols, rows, cols = frames.shape
     down, across = rows // block, cols // block
-    taps, heads = tap_constants()
     out = (2 * own, block, block)
     hbm = pl.BlockSpec(memory_space=pltpu.HBM)
-    kept = [
-        pltpu.with_memory_space_constraint(one, pltpu.HBM)
-        for one in (codes, other_codes, taps, heads, frames)
-    ]
     vmem = pl.BlockSpec(memory_space=pltpu.VMEM)
     return pl.pallas_call(
-        functools.partial(warp_kernel, vols, down, across, block, own, depth),
-        out_shape=[jax.ShapeDtypeStruct(out, jnp.bfloat16)] * depth,
-        in_specs=[pl.BlockSpec(memory_space=pltpu.SMEM)] + [hbm] * 5 + [vmem],
-        out_specs=[vmem] * depth,
+        functools.partial(warp_kernel, down, across, block, own, depth),
+        out_shape=[jax.ShapeDtypeStruct(out, jnp.bfloat16)] * (depth - 1),
+        in_specs=[pl.BlockSpec(memory_space=pltpu.SMEM), hbm] + [vmem] * 4,
+        out_specs=[vmem] * (depth - 1),
         scratch_shapes=[
-            pltpu.SMEM(codes.shape, jnp.int32),
-            pltpu.SMEM(codes.shape, jnp.int32),
-            pltpu.SMEM(taps.shape, jnp.float32),
-            pltpu.VMEM(heads.shape, jnp.float32),
             pltpu.VMEM(frames.shape, jnp.bfloat16),
-            pltpu.VMEM((2 * vols * 2 * own, block + 2 * EDGE, block), jnp.float32),
             pltpu.VMEM(out, jnp.bfloat16),
-            pltpu.SemaphoreType.DMA((5,)),
+            pltpu.SemaphoreType.DMA,
         ],
         compiler_params=pltpu.CompilerParams(vmem_limit_bytes=VMEM_LIMIT),
         cost_estimate=pl.CostEstimate(
@@ -198,16 +249,18 @@
             transcendentals=0,
         ),
         name="warp",
-    )(place, *kept, other_frames)
-
-
-def spectrum_kernel(vols, across, block, own, planes, depth, *refs):
+    )(place, pltpu.with_memory_space_constraint(frames, pltpu.HBM), other_frames, *bands)
+
+
+def spectrum_kernel(vols, down, across, block, own, planes, depth, *refs):
     place_ref, codes_ref, other_codes_ref, row_ref, col_ref, lag_ref, span_ref = refs[:7]
-    frames_ref, other_frames_ref = refs[7:9]
-    template_refs, out_refs = refs[9 : 9 + depth], refs[10 + depth : 10 + depth + 2 * planes]
-    templates, cross, sums, found = refs[10 + depth + 2 * planes :]
-    for at, template_ref in enumerate(template_refs):
-        templates[at] = template_ref[...]
+    frames_ref, other_frames_ref, near_ref, far_ref, *band_refs = refs[7:14]
+    out_refs, sums_ref = refs[15 : 15 + 2 * planes], refs[15 + 2 * planes]
+    cross, sums, found = refs[16 + 2 * planes :]
+    frame_refs = (frames_ref, other_frames_ref)
+    totals = warp_step(place_ref, 0, frame_refs, band_refs, down, across, block, own)
+    for count, total in enumerate(totals):
+        sums_ref[count] = total
 
     row_table = row_ref[...]
     col_table = col_ref[...]
@@ -229,7 +282,10 @@
 
         for pair in range(local // 2):
             pair_places = places[2 * pair : 2 * pair + 2]
-            sources = [[templates[step, 2 * pair], templates[step, 2 * pair + 1]]]
+            counts = (2 * pair, 2 * pair + 1)
+            sources = [
+                [(far_ref if count // own else near_ref)[step * own + count % own] for count in counts]
+            ]
             for _, frames, v in volumes:
                 sources.append(
                     [
@@ -342,11 +398,12 @@
                 out_ref[v, :, tile * LANES : (tile + 1) * LANES] = total * (1.0 / block)
 
 
-def lag_windows(place, codes, other_codes, frames, other_frames, templates, after, planes, own):
+def lag_windows(
+    place, codes, other_codes, frames, other_frames, templates, bands, after, planes, depth, own
+):
     vols, rows, cols = frames.shape
     block = templates[0].shape[-1]
     down, across = rows // block, cols // block
-    depth = len(templates)
     tables = dft_constants(block)
     kept = -(-(block // 2 + 1) // 8) * 8
     smem = pl.BlockSpec(memory_space=pltpu.SMEM)
@@ -354,15 +411,16 @@
     local = depth * 2 * own
     many = 2 * vols * 2 * own
     out = (vols, local // planes, WIN * WIN)
+    kept_sums = (2 * own, block, block)
     return pl.pallas_call(
-        functools.partial(spectrum_kernel, vols, across, block, own, planes, depth),
-        out_shape=[jax.ShapeDtypeStruct(out, jnp.float32)] * (2 * planes),
+        functools.partial(spectrum_kernel, vols, down, across, block, own, planes, depth),
+        out_shape=[jax.ShapeDtypeStruct(out, jnp.float32)] * (2 * planes)
+        + [jax.ShapeDtypeStruct(kept_sums, jnp.bfloat16)],
         in_specs=[smem] * 3
-        + [vmem] * (len(tables) + 2 + depth)
+        + [vmem] * (len(tables) + 4 + len(bands))
         + [pl.BlockSpec(memory_space=pl.ANY)],
-        out_specs=[vmem] * (2 * planes),
+        out_specs=[vmem] * (2 * planes + 1),
         scratch_shapes=[
-            pltpu.VMEM((depth, 2 * own, block, block), jnp.bfloat16),
             pltpu.VMEM((many, 3 * kept, LANES), jnp.float32),
             pltpu.VMEM((many, 1, LANES), jnp.float32),
             pltpu.VMEM((2 * vols, local * WIN, LANES), jnp.float32),
@@ -374,7 +432,7 @@
             transcendentals=0,
         ),
         name="lag_windows",
-    )(place, codes, other_codes, *tables, frames, other_frames, *templates, after)
+    )(place, codes, other_codes, *tables, frames, other_frames, *templates, *bands, after)
 
 
 def exchange(value, axes, size, turn):
@@ -389,24 +447,25 @@
     share = 4 * depth * own // planes
     place = jnp.stack([lax.axis_index(axis) for axis in ("z", "y", "core", "plane")])
     other_codes = exchange(shift_codes, "core", 2, 1)
-    other_template = exchange(template, "y", 2, 1)
-    later_frames, other_template = lax.optimization_barrier((frames, other_template))
-    other_frames = exchange(later_frames, "core", 2, 1)
-    templates = [jnp.concatenate([template, other_template], axis=0)]
-    for turn in range(1, depth):
-        templates.append(exchange(templates[0], "z", depth, turn))
+    other_frames = exchange(frames, "core", 2, 1)
+    near = jnp.concatenate(
+        [template] + [exchange(template, "z", depth, turn) for turn in range(1, depth)], axis=0
+    )
+    far = exchange(near, "y", 2, 1)
+    bands = warp_bands(place, shift_codes, other_codes, img_cols // block, depth, block, own)
     averages, window = [], [0.0, 0.0]
     volumes = vol_dev * depth * 4
     for p in range(pl_dev):
-        work = (place, shift_codes, other_codes, frames[:, p], other_frames[:, p])
-        warped = warp_sums(*work, depth, block, own)
-        chosen = [one[:, p] for one in templates]
-        found = lag_windows(*work, chosen, warped[0], planes, own)
-        warped = [warped[0]] + [
-            exchange(warped[turn], "z", depth, turn) for turn in range(1, depth)
-        ]
+        work = (frames[:, p], other_frames[:, p])
+        warped = warp_sums(place, *work, bands, depth, block, own)
+        templates = (near[:, p], far[:, p])
+        *found, kept = lag_windows(
+            place, shift_codes, other_codes, *work, templates, bands, warped[0], planes, depth, own
+        )
+        warped = [exchange(one, "z", depth, turn + 1) for turn, one in enumerate(warped)]
+        found, warped[0] = lax.optimization_barrier((found, warped[0]))
+        warped.append(kept)
         sums = [sum(one[at : at + own].astype(jnp.float32) for one in warped) for at in (0, own)]
-        found, sums = lax.optimization_barrier((found, sums))
         taken = exchange(sums[1].astype(jnp.bfloat16), "y", 2, 1)
         averages.append((sums[0] + taken.astype(jnp.float32)) * (1.0 / volumes))
         for turn, one in enumerate(found):

time: 42.8 us -> 45.2 us (1.056)
  Pallas kernels: 14.2 us -> 19.3 us
  starting transfers between devices: 16.5 us -> 14.4 us
  waiting for transfers between devices: 7.5 us -> 6.43 us
    pallas_call x2 -> x3, Pallas kernels: 14.2 us -> 19.3 us  [the longest x1 7.03 us: lag_windows(): pl.pallas_call(functools.partial(spectrum_kernel, vols, down, across, blo...]
    ppermute x13, starting transfers between devices: 16.5 us -> 14.4 us  [exchange(): return lax.ppermute(value, axes, [(at, at ^ turn) for at in range(size)])]
    ppermute x13, waiting for transfers between devices: 7.5 us -> 6.43 us  [exchange(): return lax.ppermute(value, axes, [(at, at ^ turn) for at in range(size)])]
  transfers between devices with their start and end apart: 13 -> 13, of which waited for: 4 -> 5; matrix products, arithmetic and copies ran while one was open for 4% -> 4% of each run, Pallas kernels for 33% -> 43%
where the time goes in v7:
time: 45.2 us; the launch traced here: 45 us
  Pallas kernels  19.3 us (43%)
  starting transfers between devices  14.4 us (32%)
  waiting for transfers between devices  6.43 us (14%)
  local copies, waits for them, and re-layouts  2.34 us (5%)
  other arithmetic  1.73 us (4%)
  between operations  0.79 us (2%)
    ppermute x13, starting transfers between devices, exchange(): return lax.ppermute(value, axes, [(at, at ^ turn) for at in range(size)])  14.4 us
    pallas_call x1, Pallas kernels, lag_windows(): pl.pallas_call(functools.partial(spectrum_kernel, vols, down, across, blo...  7.03 us
    ppermute x13, waiting for transfers between devices, exchange(): return lax.ppermute(value, axes, [(at, at ^ turn) for at in range(size)])  6.43 us
    pallas_call x1, Pallas kernels, warp_bands(): pl.pallas_call(functools.partial(band_kernel, vols, across, own, depth),...  6.32 us
    pallas_call x1, Pallas kernels, warp_sums(): pl.pallas_call(functools.partial(warp_kernel, down, across, block, own, d...  5.97 us
    unnamed x16, local copies, waits for them, and re-layouts  1.66 us
  transfers between devices with their start and end apart: 13, of which 5 were waited for; matrix products, arithmetic and copies ran while one was open for 4% of the time, Pallas kernels for 43%

profile of v7, /device:TPU:0, one launch (start us, length us, event | category | flops | bytes accessed | tf_op | source)
XLA Modules:
  0.0 45.0 jit_solution(3748180074004660475)
XLA Ops:
  0.6 0.5 %collective-permute-start.1 = (bf16[2,1,512,1024]{3,2,0,1:T(8,128)(2,1)}, bf16[2,1,512,1024]{3,2,0,1:T(8,128)(2,1)S(1)}, u32[]{:S(2)}, u32[]{:S(2)}) collective-permute-start(bf16[2,1,512,1024]{3,2,0,1:T(8,128)(2,1)} %bitcast.15), channel_id=1, source_target_pairs={{0,2},{2,0},{1,3},{3,1},{4,6},{6,4},{5,7},{7,5},{8,10},{10,8},{9,1... | collective-permute-start | bytes 6291464 | tf_op jit(solution)/shard_map/ppermute | solution.py:439
  1.1 4.7 %collective-permute-start.4 = (bf16[2,1,128,128]{3,2,0,1:T(8,128)(2,1)}, bf16[2,1,128,128]{3,2,0,1:T(8,128)(2,1)S(1)}, u32[]{:S(2)}, u32[]{:S(2)}) collective-permute-start(bf16[2,1,128,128]{3,2,0,1:T(8,128)(2,1)} %bitcast.21), channel_id=1, source_target_pairs={{0,24},{8,16},{16,8},{24,0},{1,25},{9,17},{17,9},{25,1},{2,26},{10... | collective-permute-start | bytes 196616 | tf_op jit(solution)/shard_map/ppermute | solution.py:439
  5.8 0.6 %collective-permute-start.2 = (bf16[2,1,128,128]{3,2,0,1:T(8,128)(2,1)}, bf16[2,1,128,128]{3,2,0,1:T(8,128)(2,1)S(1)}, u32[]{:S(2)}, u32[]{:S(2)}) collective-permute-start(bf16[2,1,128,128]{3,2,0,1:T(8,128)(2,1)} %bitcast.23), channel_id=1, source_target_pairs={{0,8},{8,0},{16,24},{24,16},{1,9},{9,1},{17,25},{25,17},{2,10},{10... | collective-permute-start | bytes 196616 | tf_op jit(solution)/shard_map/ppermute | solution.py:439
  6.5 0.1 pad_add_fusion.place_ref.refs_0_
  6.5 1.3 %collective-permute-done.other_codes_ref.refs_2_ = s32[2,2,32]{2,1,0:T(2,128)S(1)} collective-permute-done((s32[2,2,32]{2,1,0:T(2,128)}, s32[2,2,32]{2,1,0:T(2,128)S(1)}, u32[]{:S(2)}, u32[]{:S(2)}) %collective-permute-start) | collective-permute-done | bytes 544 | tf_op jit(solution)/shard_map/ppermute | solution.py:439
  7.8 0.9 %copy-done = f32[2,16,16,128]{3,2,1,0:T(8,128)S(1)} copy-done((f32[2,16,16,128]{3,2,1,0:T(8,128)S(1)}, f32[2,16,16,128]{3,2,1,0:T(8,128)}, u32[]{:S(2)}) %copy-start) | copy-done | bytes 262168
  8.8 0.7 %copy-done.1 = s32[2,2,32]{2,1,0:T(2,128)S(1)} copy-done((s32[2,2,32]{2,1,0:T(2,128)S(1)}, s32[2,2,32]{2,1,0:T(2,128)}, u32[]{:S(2)}) %copy-start.1) | copy-done | bytes 536
  9.5 6.3 %bands.1 = (bf16[64,160,128]{2,1,0:T(8,128)(2,1)S(1)}, bf16[64,128,128]{2,1,0:T(8,128)(2,1)S(1)}, bf16[16,32,128]{2,1,0:T(8,128)(2,1)S(1)}) custom-call(s32[4]{0:T(128)S(1)} %pad_add_fusion.place_ref.refs_0_, s32[2,2,32]{2,1,0:T(2,128)S(1)} %copy-done.1, s32[2,2,32]{2,1,0:T(2,128)S(1)} %collective-permute-done.other_codes_ref.refs_2_, ...), custom_call_target="tpu_custom_call" | custom-call | flops 67108864 | tf_op jit(solution)/shard_map/bands/pallas_call | solution.py:140
  15.8 0.9 %pad_maximum_fusion = (bf16[8,1,128,128]{3,2,0,1:T(8,128)(2,1)S(1)}, bf16[8,128,128]{2,1,0:T(8,128)(2,1)S(1)}) fusion(bf16[2,1,128,128]{3,2,0,1:T(8,128)(2,1)S(1)} %collective-permute-done.4, bf16[2,1,128,128]{3,2,0,1:T(8,128)(2,1)S(1)} %collective-permute-done.3, bf16[2,1,128,128]{3,2,0,1:T(8,128)(2,1)S(1)} %collective-permute-done.2, ...), kind=kLoop, calls=%fused_computation | loop fusion | flops 393216 | bytes 786432 | tf_op jit(solution)/shard_map/concatenate | solution.py:451
  16.7 1.7 %collective-permute-start.5 = (bf16[8,1,128,128]{3,2,0,1:T(8,128)(2,1)S(1)}, bf16[8,1,128,128]{3,2,0,1:T(8,128)(2,1)S(1)}, u32[]{:S(2)}, u32[]{:S(2)}) collective-permute-start(bf16[8,1,128,128]{3,2,0,1:T(8,128)(2,1)S(1)} %get-tuple-element.36), channel_id=1, source_target_pairs={{0,4},{4,0},{1,5},{5,1},{2,6},{6,2},{3,7},{7,3},{8,12},{12,8},{9,1... | collective-permute-start | bytes 786440 | tf_op jit(solution)/shard_map/ppermute | solution.py:439
  18.5 6.0 %warp.1 = (bf16[4,128,128]{2,1,0:T(8,128)(2,1)S(1)}, bf16[4,128,128]{2,1,0:T(8,128)(2,1)S(1)}, bf16[4,128,128]{2,1,0:T(8,128)(2,1)S(1)}) custom-call(s32[4]{0:T(128)S(1)} %pad_add_fusion.place_ref.refs_0_, bf16[2,512,1024]{2,1,0:T(8,128)(2,1)} %bitcast.16, bf16[2,512,1024]{2,1,0:T(8,128)(2,1)S(1)} %bitcast.18, ...), custom_call_target="tpu_custom_call" | custom-call | flops 4294967296 | bytes 4718592 | tf_op jit(solution)/shard_map/warp/pallas_call | solution.py:235
  24.5 2.2 %collective-permute-start.10 = (bf16[4,128,128]{2,1,0:T(8,128)(2,1)S(1)}, bf16[4,128,128]{2,1,0:T(8,128)(2,1)S(1)}, u32[]{:S(2)}, u32[]{:S(2)}) collective-permute-start(bf16[4,128,128]{2,1,0:T(8,128)(2,1)S(1)} %get-tuple-element.31), channel_id=1, source_target_pairs={{0,16},{8,24},{16,0},{24,8},{1,17},{9,25},{17,1},{25,9},{2,18},{10... | collective-permute-start | bytes 393224 | tf_op jit(solution)/shard_map/ppermute | solution.py:439
  26.7 1.5 %collective-permute-start.11 = (bf16[4,128,128]{2,1,0:T(8,128)(2,1)S(1)}, bf16[4,128,128]{2,1,0:T(8,128)(2,1)S(1)}, u32[]{:S(2)}, u32[]{:S(2)}) collective-permute-start(bf16[4,128,128]{2,1,0:T(8,128)(2,1)S(1)} %get-tuple-element.32), channel_id=1, source_target_pairs={{0,24},{8,16},{16,8},{24,0},{1,25},{9,17},{17,9},{25,1},{2,26},{10... | collective-permute-start | bytes 393224 | tf_op jit(solution)/shard_map/ppermute | solution.py:439
  28.2 0.5 %collective-permute-start.6 = (bf16[4,128,128]{2,1,0:T(8,128)(2,1)S(1)}, bf16[4,128,128]{2,1,0:T(8,128)(2,1)S(1)}, u32[]{:S(2)}, u32[]{:S(2)}) collective-permute-start(bf16[4,128,128]{2,1,0:T(8,128)(2,1)S(1)} %get-tuple-element.21.refs_14_), channel_id=1, source_target_pairs={{0,8},{8,0},{16,24},{24,16},{1,9},{9,1},{17,25},{25,17},{2,10},{10... | collective-permute-start | bytes 393224 | tf_op jit(solution)/shard_map/ppermute | solution.py:439
  28.8 7.0 %lag_windows.1 = (f32[2,8,256]{2,1,0:T(8,128)S(1)}, f32[2,8,256]{2,1,0:T(8,128)S(1)}, f32[2,8,256]{2,1,0:T(8,128)S(1)}, f32[2,8,256]{2,1,0:T(8,128)S(1)}, bf16[4,128,128]{2,1,0:T(8,128)(2,1)S(1)}) custom-call(s32[4]{0:T(128)S(1)} %pad_add_fusion.place_ref.refs_0_, s32[2,2,32]{2,1,0:T(2,128)S(1)} %copy-done.2, ...), custom_call_target="tpu_custom_call" | custom-call | flops 6442450944 | bytes 4718592 | tf_op jit(solution)/shard_map/lag_windows/pallas_call | solution.py:415
  35.8 2.0 %collective-permute-done.6 = bf16[4,128,128]{2,1,0:T(8,128)(2,1)S(1)} collective-permute-done((bf16[4,128,128]{2,1,0:T(8,128)(2,1)S(1)}, bf16[4,128,128]{2,1,0:T(8,128)(2,1)S(1)}, u32[]{:S(2)}, u32[]{:S(2)}) %collective-permute-start.6) | collective-permute-done | bytes 131104 | tf_op jit(solution)/shard_map/ppermute | solution.py:439
  37.8 1.5 %collective-permute-start.7 = (f32[2,8,256]{2,1,0:T(8,128)S(1)}, f32[2,8,256]{2,1,0:T(8,128)S(1)}, u32[]{:S(2)}, u32[]{:S(2)}) collective-permute-start(f32[2,8,256]{2,1,0:T(8,128)S(1)} %get-tuple-element.27), channel_id=1, source_target_pairs={{0,1},{1,0},{2,3},{3,2},{4,5},{5,4},{6,7},{7,6},{8,9},{9,8},{10,11... | collective-permute-start | bytes 49160 | tf_op jit(solution)/shard_map/ppermute | solution.py:439
  39.3 0.6 %collective-permute-start.9 = (f32[2,8,256]{2,1,0:T(8,128)S(1)}, f32[2,8,256]{2,1,0:T(8,128)S(1)}, u32[]{:S(2)}, u32[]{:S(2)}) collective-permute-start(f32[2,8,256]{2,1,0:T(8,128)S(1)} %get-tuple-element.29), channel_id=1, source_target_pairs={{0,3},{1,2},{2,1},{3,0},{4,7},{5,6},{6,5},{7,4},{8,11},{9,10},{10,... | collective-permute-start | bytes 49160 | tf_op jit(solution)/shard_map/ppermute | solution.py:439
  40.0 0.5 %collective-permute-start.12 = (bf16[2,128,128]{2,1,0:T(8,128)(2,1)S(1)}, bf16[2,128,128]{2,1,0:T(8,128)(2,1)S(1)}, u32[]{:S(2)}, u32[]{:S(2)}) collective-permute-start(bf16[2,128,128]{2,1,0:T(8,128)(2,1)S(1)} %add_convert_fusion), channel_id=1, source_target_pairs={{0,4},{4,0},{1,5},{5,1},{2,6},{6,2},{3,7},{7,3},{8,12},{12,8},{9,1... | collective-permute-start | bytes 196616 | tf_op jit(solution)/shard_map/ppermute | solution.py:439
  40.4 1.1 %collective-permute-done.7 = f32[2,8,256]{2,1,0:T(8,128)S(1)} collective-permute-done((f32[2,8,256]{2,1,0:T(8,128)S(1)}, f32[2,8,256]{2,1,0:T(8,128)S(1)}, u32[]{:S(2)}, u32[]{:S(2)}) %collective-permute-start.7) | collective-permute-done | bytes 16416 | tf_op jit(solution)/shard_map/ppermute | solution.py:439
  41.5 0.9 %collective-permute-done.9 = f32[2,8,256]{2,1,0:T(8,128)S(1)} collective-permute-done((f32[2,8,256]{2,1,0:T(8,128)S(1)}, f32[2,8,256]{2,1,0:T(8,128)S(1)}, u32[]{:S(2)}, u32[]{:S(2)}) %collective-permute-start.9) | collective-permute-done | bytes 16416 | tf_op jit(solution)/shard_map/ppermute | solution.py:439
  42.5 0.6 %reshape.15 = f32[2,16,256]{2,1,0:T(8,128)} reshape(f32[2,4,2,2,256]{4,3,2,1,0:T(2,128)S(1)} %copy.15) | data formatting | bytes 65536 | tf_op jit(solution)/shard_map/reshape | solution.py:478
  43.2 1.1 %collective-permute-done.12 = bf16[2,128,128]{2,1,0:T(8,128)(2,1)S(1)} collective-permute-done((bf16[2,128,128]{2,1,0:T(8,128)(2,1)S(1)}, bf16[2,128,128]{2,1,0:T(8,128)(2,1)S(1)}, u32[]{:S(2)}, u32[]{:S(2)}) %collective-permute-start.12) | collective-permute-done | bytes 65568 | tf_op jit(solution)/shard_map/ppermute | solution.py:439
  44.3 0.7 %multiply_bitcast_fusion = f32[2,1,128,128]{3,2,1,0:T(8,128)} fusion(bf16[2,128,128]{2,1,0:T(8,128)(2,1)S(1)} %collective-permute-done.12, bf16[4,128,128]{2,1,0:T(8,128)(2,1)S(1)} %collective-permute-done.11, bf16[4,128,128]{2,1,0:T(8,128)(2,1)S(1)} %collective-permute-done.10, bf16[4,128,128]{2,1,0:T(8,128)(2,1)S(1)} %get-tuple-element.33, ...), kind=kLoop, calls=%fused_computation.1 | loop fusion | flops 327680 | bytes 458752
  (31 shorter events, 0.2 us)
Async XLA Ops:
  0.6 17.8 %collective-permute-start.1 = (bf16[2,1,512,1024]{3,2,0,1:T(8,128)(2,1)}, bf16[2,1,512,1024]{3,2,0,1:T(8,128)(2,1)S(1)}, u32[]{:S(2)}, u32[]{:S(2)}) collective-permute-start(bf16[2,1,512,1024]{3,2,0,1:T(8,128)(2,1)} %bitcast.15), channel_id=1, source_target_pairs={{0,2},{2,0},{1,3},{3,1},{4,6},{6,4},{5,7},{7,5},{8,10},{10,8},{9,1... | collective-permute-start | bytes 6291464 | tf_op jit(solution)/shard_map/ppermute | solution.py:439
  1.1 14.7 %collective-permute-start.4 = (bf16[2,1,128,128]{3,2,0,1:T(8,128)(2,1)}, bf16[2,1,128,128]{3,2,0,1:T(8,128)(2,1)S(1)}, u32[]{:S(2)}, u32[]{:S(2)}) collective-permute-start(bf16[2,1,128,128]{3,2,0,1:T(8,128)(2,1)} %bitcast.21), channel_id=1, source_target_pairs={{0,24},{8,16},{16,8},{24,0},{1,25},{9,17},{17,9},{25,1},{2,26},{10... | collective-permute-start | bytes 196616 | tf_op jit(solution)/shard_map/ppermute | solution.py:439
  5.8 10.0 %collective-permute-start.3 = (bf16[2,1,128,128]{3,2,0,1:T(8,128)(2,1)}, bf16[2,1,128,128]{3,2,0,1:T(8,128)(2,1)S(1)}, u32[]{:S(2)}, u32[]{:S(2)}) collective-permute-start(bf16[2,1,128,128]{3,2,0,1:T(8,128)(2,1)} %bitcast.22), channel_id=1, source_target_pairs={{0,16},{8,24},{16,0},{24,8},{1,17},{9,25},{17,1},{25,9},{2,18},{10... | collective-permute-start | bytes 196616 | tf_op jit(solution)/shard_map/ppermute | solution.py:439
  5.8 10.0 %collective-permute-start.2 = (bf16[2,1,128,128]{3,2,0,1:T(8,128)(2,1)}, bf16[2,1,128,128]{3,2,0,1:T(8,128)(2,1)S(1)}, u32[]{:S(2)}, u32[]{:S(2)}) collective-permute-start(bf16[2,1,128,128]{3,2,0,1:T(8,128)(2,1)} %bitcast.23), channel_id=1, source_target_pairs={{0,8},{8,0},{16,24},{24,16},{1,9},{9,1},{17,25},{25,17},{2,10},{10... | collective-permute-start | bytes 196616 | tf_op jit(solution)/shard_map/ppermute | solution.py:439
  6.5 1.4 %collective-permute-start = (s32[2,2,32]{2,1,0:T(2,128)}, s32[2,2,32]{2,1,0:T(2,128)S(1)}, u32[]{:S(2)}, u32[]{:S(2)}) collective-permute-start(s32[2,2,32]{2,1,0:T(2,128)} %refs_1_.1), channel_id=1, source_target_pairs={{0,2},{2,0},{1,3},{3,1},{4,6},{6,4},{5,7},{7,5},{8,10},{10,8},{9,1... | collective-permute-start | bytes 1544 | tf_op jit(solution)/shard_map/ppermute | solution.py:439
  7.8 1.0 %copy-start = (f32[2,16,16,128]{3,2,1,0:T(8,128)S(1)}, f32[2,16,16,128]{3,2,1,0:T(8,128)}, u32[]{:S(2)}) copy-start(f32[2,16,16,128]{3,2,1,0:T(8,128)} %constant.28.clone.heads_ref) | copy-start | bytes 786436
  8.8 0.7 %copy-start.1 = (s32[2,2,32]{2,1,0:T(2,128)S(1)}, s32[2,2,32]{2,1,0:T(2,128)}, u32[]{:S(2)}) copy-start(s32[2,2,32]{2,1,0:T(2,128)} %refs_1_.1) | copy-start | bytes 1540
  16.7 12.0 %collective-permute-start.5 = (bf16[8,1,128,128]{3,2,0,1:T(8,128)(2,1)S(1)}, bf16[8,1,128,128]{3,2,0,1:T(8,128)(2,1)S(1)}, u32[]{:S(2)}, u32[]{:S(2)}) collective-permute-start(bf16[8,1,128,128]{3,2,0,1:T(8,128)(2,1)S(1)} %get-tuple-element.36), channel_id=1, source_target_pairs={{0,4},{4,0},{1,5},{5,1},{2,6},{6,2},{3,7},{7,3},{8,12},{12,8},{9,1... | collective-permute-start | bytes 786440 | tf_op jit(solution)/shard_map/ppermute | solution.py:439
  18.5 10.3 %copy-start.2 = (s32[2,2,32]{2,1,0:T(2,128)S(1)}, s32[2,2,32]{2,1,0:T(2,128)}, u32[]{:S(2)}) copy-start(s32[2,2,32]{2,1,0:T(2,128)} %refs_1_.1) | copy-start | bytes 1540
  18.5 10.3 %copy-start.3 = (bf16[2,1,512,1024]{3,2,1,0:T(8,128)(2,1)S(1)}, bf16[2,1,512,1024]{3,2,1,0:T(8,128)(2,1)}, u32[]{:S(2)}) copy-start(bf16[2,1,512,1024]{3,2,1,0:T(8,128)(2,1)} %param.8) | copy-start | bytes 6291460
  18.5 10.3 %copy-start.4 = (bf16[256,256]{1,0:T(8,128)(2,1)S(1)}, bf16[256,256]{1,0:T(8,128)(2,1)}, u32[]{:S(2)}) copy-start(bf16[256,256]{1,0:T(8,128)(2,1)} %constant.30.clone.refs_4_) | copy-start | bytes 393220
  18.5 10.3 %copy-start.5 = (bf16[256,128]{1,0:T(8,128)(2,1)S(1)}, bf16[256,128]{1,0:T(8,128)(2,1)}, u32[]{:S(2)}) copy-start(bf16[256,128]{1,0:T(8,128)(2,1)} %constant.32.clone.refs_6_) | copy-start | bytes 196612
  18.5 10.3 %copy-start.6 = (bf16[160,128]{1,0:T(8,128)(2,1)S(1)}, bf16[160,128]{1,0:T(8,128)(2,1)}, u32[]{:S(2)}) copy-start(bf16[160,128]{1,0:T(8,128)(2,1)} %constant.29.clone.refs_3_) | copy-start | bytes 122884
  18.5 10.3 %copy-start.7 = (bf16[64,160]{1,0:T(8,128)(2,1)S(1)}, bf16[64,160]{1,0:T(8,128)(2,1)}, u32[]{:S(2)}) copy-start(bf16[64,160]{1,0:T(8,128)(2,1)} %constant.31.clone.refs_5_) | copy-start | bytes 61444
  24.5 15.4 %collective-permute-start.10 = (bf16[4,128,128]{2,1,0:T(8,128)(2,1)S(1)}, bf16[4,128,128]{2,1,0:T(8,128)(2,1)S(1)}, u32[]{:S(2)}, u32[]{:S(2)}) collective-permute-start(bf16[4,128,128]{2,1,0:T(8,128)(2,1)S(1)} %get-tuple-element.31), channel_id=1, source_target_pairs={{0,16},{8,24},{16,0},{24,8},{1,17},{9,25},{17,1},{25,9},{2,18},{10... | collective-permute-start | bytes 393224 | tf_op jit(solution)/shard_map/ppermute | solution.py:439
  26.7 13.2 %collective-permute-start.11 = (bf16[4,128,128]{2,1,0:T(8,128)(2,1)S(1)}, bf16[4,128,128]{2,1,0:T(8,128)(2,1)S(1)}, u32[]{:S(2)}, u32[]{:S(2)}) collective-permute-start(bf16[4,128,128]{2,1,0:T(8,128)(2,1)S(1)} %get-tuple-element.32), channel_id=1, source_target_pairs={{0,24},{8,16},{16,8},{24,0},{1,25},{9,17},{17,9},{25,1},{2,26},{10... | collective-permute-start | bytes 393224 | tf_op jit(solution)/shard_map/ppermute | solution.py:439
  28.2 9.5 %collective-permute-start.6 = (bf16[4,128,128]{2,1,0:T(8,128)(2,1)S(1)}, bf16[4,128,128]{2,1,0:T(8,128)(2,1)S(1)}, u32[]{:S(2)}, u32[]{:S(2)}) collective-permute-start(bf16[4,128,128]{2,1,0:T(8,128)(2,1)S(1)} %get-tuple-element.21.refs_14_), channel_id=1, source_target_pairs={{0,8},{8,0},{16,24},{24,16},{1,9},{9,1},{17,25},{25,17},{2,10},{10... | collective-permute-start | bytes 393224 | tf_op jit(solution)/shard_map/ppermute | solution.py:439
  37.8 3.7 %collective-permute-start.7 = (f32[2,8,256]{2,1,0:T(8,128)S(1)}, f32[2,8,256]{2,1,0:T(8,128)S(1)}, u32[]{:S(2)}, u32[]{:S(2)}) collective-permute-start(f32[2,8,256]{2,1,0:T(8,128)S(1)} %get-tuple-element.27), channel_id=1, source_target_pairs={{0,1},{1,0},{2,3},{3,2},{4,5},{5,4},{6,7},{7,6},{8,9},{9,8},{10,11... | collective-permute-start | bytes 49160 | tf_op jit(solution)/shard_map/ppermute | solution.py:439
  39.3 2.2 %collective-permute-start.8 = (f32[2,8,256]{2,1,0:T(8,128)S(1)}, f32[2,8,256]{2,1,0:T(8,128)S(1)}, u32[]{:S(2)}, u32[]{:S(2)}) collective-permute-start(f32[2,8,256]{2,1,0:T(8,128)S(1)} %get-tuple-element.28), channel_id=1, source_target_pairs={{0,2},{1,3},{2,0},{3,1},{4,6},{5,7},{6,4},{7,5},{8,10},{9,11},{10,... | collective-permute-start | bytes 49160 | tf_op jit(solution)/shard_map/ppermute | solution.py:439
  39.3 3.2 %collective-permute-start.9 = (f32[2,8,256]{2,1,0:T(8,128)S(1)}, f32[2,8,256]{2,1,0:T(8,128)S(1)}, u32[]{:S(2)}, u32[]{:S(2)}) collective-permute-start(f32[2,8,256]{2,1,0:T(8,128)S(1)} %get-tuple-element.29), channel_id=1, source_target_pairs={{0,3},{1,2},{2,1},{3,0},{4,7},{5,6},{6,5},{7,4},{8,11},{9,10},{10,... | collective-permute-start | bytes 49160 | tf_op jit(solution)/shard_map/ppermute | solution.py:439
  40.0 4.3 %collective-permute-start.12 = (bf16[2,128,128]{2,1,0:T(8,128)(2,1)S(1)}, bf16[2,128,128]{2,1,0:T(8,128)(2,1)S(1)}, u32[]{:S(2)}, u32[]{:S(2)}) collective-permute-start(bf16[2,128,128]{2,1,0:T(8,128)(2,1)S(1)} %add_convert_fusion), channel_id=1, source_target_pairs={{0,4},{4,0},{1,5},{5,1},{2,6},{6,2},{3,7},{7,3},{8,12},{12,8},{9,1... | collective-permute-start | bytes 196616 | tf_op jit(solution)/shard_map/ppermute | solution.py:439

commit v8 on v7

--- a/solution.py
+++ b/solution.py
@@ -50,26 +50,24 @@
     )
 
 
-def tap_constants():
+def tap_constants(block_size):
     offsets = np.arange(TAPS) - (TAPS // 2 - 1)
     spots = offsets[None, :] - np.arange(SUB)[:, None] / SUB
     raw_taps = np.sinc(spots) * np.sinc(spots / (TAPS // 2))
     taps = raw_taps / raw_taps.sum(axis=-1, keepdims=True)
-    table = np.zeros((2, SUB, EDGE, LANES))
-    for row in range(EDGE):
-        table[0, :, row, row : row + TAPS] = taps
-        table[1, :, row, row : row + TAPS] = taps[:, ::-1]
-    return jnp.asarray(table, jnp.float32)
-
-
-def band_groups(head, start, lane):
-    head = pltpu.roll(head, start + LANES, 1).astype(jnp.bfloat16)
-    groups = [head] + [pltpu.roll(head, step, 1) for step in range(EDGE, LANES, EDGE)]
-    zero = jnp.zeros_like(head)
-    low = lane < LANES // 2
-    before, after = jnp.where(low, zero, groups[0]), jnp.where(low, groups[-1], zero)
-    middle = [jnp.where(low, groups[0], zero), *groups[1:-1], jnp.where(low, zero, groups[-1])]
-    return middle, before, after
+
+    def band(inputs, outputs):
+        at = inputs - outputs + TAPS // 2 - 1
+        return np.where((at >= 0) & (at < TAPS), taps[:, np.clip(at, 0, TAPS - 1)], 0.0)
+
+    lanes = np.arange(block_size)[None, :]
+    inputs = np.arange(block_size + 3 * EDGE)[:, None] - EDGE - SHIFT
+    outputs = np.arange(block_size + EDGE)[:, None] - SHIFT
+    spare = np.arange(LANES)[None, :] % (2 * EDGE)
+    first = band(spare - 2 * EDGE, outputs[: 2 * EDGE]) * (spare >= EDGE)
+    last = band(spare + EDGE, outputs[: 2 * EDGE]) * (spare < EDGE)
+    tables = band(inputs, lanes), band(lanes, outputs), np.stack([first, last], axis=1)
+    return [jnp.asarray(table, jnp.float32) for table in tables]
 
 
 def step_places(place_ref, step, across, own):
@@ -86,71 +84,34 @@
     return (place_ref[0] ^ step) * (4 * own) // across
 
 
-def band_kernel(
-    vols, across, own, depth, place_ref, codes_ref, other_codes_ref, heads_ref, *out_refs
-):
-    cols_ref, rows_ref, edges_ref = out_refs
-    lane = lax.broadcasted_iota(jnp.int32, (EDGE, LANES), 1)
-    volumes = [(codes_ref, v) for v in range(vols)] + [(other_codes_ref, v) for v in range(vols)]
-    many = len(volumes)
-    per_tile = LANES // (2 * EDGE)
-
-    def one_step(step, _):
-        for count, (index, _) in enumerate(step_places(place_ref, step, across, own)):
-            block_at = step * (2 * own) + count
-            edges = []
-            for order, (codes, v) in enumerate(volumes):
-                row_code = codes[v, 0, index]
-                col_code = codes[v, 1, index]
-                middle, before, after = band_groups(
-                    heads_ref[1, col_code & (SUB - 1)], -(TAPS // 2) - (col_code >> 4), lane
-                )
-                one = block_at * many + order
-                cols_ref[one] = jnp.concatenate([*middle, before, after], axis=0)
-                middle, before, after = band_groups(
-                    heads_ref[0, row_code & (SUB - 1)], (row_code >> 4) - (TAPS // 2 - 1), lane
-                )
-                rows_ref[one] = jnp.concatenate(middle, axis=0)
-                place = 2 * EDGE * order % LANES
-                first = pltpu.roll(before, (place + 2 * EDGE) % LANES, 1)
-                last = pltpu.roll(after, place, 1) if place else after
-                if order % per_tile:
-                    first, last = edges[-1][0] + first, edges[-1][1] + last
-                    edges.pop()
-                edges.append((first, last))
-            for at, (first, last) in enumerate(edges):
-                edges_ref[block_at * len(edges) + at] = jnp.concatenate([first, last], axis=0)
-        return 0
-
-    lax.fori_loop(0, depth, one_step, 0)
-
-
-def warp_bands(place, codes, other_codes, across, depth, block, own):
-    vols = codes.shape[0]
-    heads = tap_constants()
-    smem = pl.BlockSpec(memory_space=pltpu.SMEM)
-    vmem = pl.BlockSpec(memory_space=pltpu.VMEM)
-    blocks = depth * 2 * own
-    tiles = -(-2 * vols * 2 * EDGE // LANES)
-    shapes = [
-        (blocks * 2 * vols, block + 2 * EDGE, block),
-        (blocks * 2 * vols, block, block),
-        (blocks * tiles, 2 * EDGE, LANES),
+def stage_kernel(count, *refs):
+    sources, targets, sems = refs[:count], refs[count + 1 : 2 * count + 1], refs[-1]
+    copies = [
+        pltpu.make_async_copy(source, target, sems.at[at])
+        for at, (source, target) in enumerate(zip(sources, targets))
     ]
+    for copy in copies:
+        copy.start()
+    for copy in copies:
+        copy.wait()
+
+
+def stage(arrays, after):
+    kept = [pltpu.with_memory_space_constraint(one, pltpu.HBM) for one in arrays]
+    count = len(arrays)
     return pl.pallas_call(
-        functools.partial(band_kernel, vols, across, own, depth),
-        out_shape=[jax.ShapeDtypeStruct(shape, jnp.bfloat16) for shape in shapes],
-        in_specs=[smem] * 3 + [vmem],
-        out_specs=[vmem] * 3,
+        functools.partial(stage_kernel, count),
+        out_shape=[jax.ShapeDtypeStruct(one.shape, one.dtype) for one in arrays],
+        in_specs=[pl.BlockSpec(memory_space=pltpu.HBM)] * count
+        + [pl.BlockSpec(memory_space=pl.ANY)],
+        out_specs=[pl.BlockSpec(memory_space=pltpu.VMEM)] * count,
+        scratch_shapes=[pltpu.SemaphoreType.DMA((count,))],
         compiler_params=pltpu.CompilerParams(vmem_limit_bytes=VMEM_LIMIT),
-        cost_estimate=pl.CostEstimate(
-            flops=blocks * vols * block * block * 128, bytes_accessed=0, transcendentals=0
-        ),
-        name="bands",
-    )(place, codes, other_codes, heads)
-
-
-def warp_step(place_ref, step, frame_refs, band_refs, down, across, block, own):
+        name="stage",
+    )(*kept, after)
+
+
+def warp_step(place_ref, step, code_refs, frame_refs, band_refs, down, across, block, own):
     cols_ref, rows_ref, edges_ref = band_refs
     band = step_band(place_ref, step, across, own)
     row = pl.multiple_of(band * block, block)
@@ -159,9 +120,14 @@
     zero = jnp.zeros((EDGE, LANES), jnp.bfloat16)
     gap = jnp.zeros((block - 2 * EDGE, LANES), jnp.bfloat16)
     no_tile = jnp.zeros((block + 2 * EDGE, block), jnp.bfloat16)
-    volumes = [(frames, v) for frames in frame_refs for v in range(frames.shape[0])]
+    volumes = [
+        (codes, frames, v)
+        for codes, frames in zip(code_refs, frame_refs)
+        for v in range(frames.shape[0])
+    ]
     many = len(volumes)
-    tiles = -(-many * 2 * EDGE // LANES)
+    per_tile = LANES // (2 * EDGE)
+    lane = lax.broadcasted_iota(jnp.int32, (EDGE, LANES), 1) // (2 * EDGE)
 
     def tile(frames, v, at):
         lanes = pl.ds(pl.multiple_of(at * block, block), block)
@@ -169,50 +135,69 @@
         below = jnp.where(band < down - 1, frames[v, pl.ds(row_below, EDGE), lanes], zero)
         return jnp.concatenate([frames[v, pl.ds(row, block), lanes], below, above], axis=0)
 
+    places = step_places(place_ref, step, across, own)
     totals = []
-    for count, (_, at) in enumerate(step_places(place_ref, step, across, own)):
-        block_at = step * (2 * own) + count
-        row_tiles, partials, edges = [], [], []
-        for order, (frames, v) in enumerate(volumes):
-            one = block_at * many + order
-            left = jnp.where(at > 0, tile(frames, v, jnp.maximum(at - 1, 0)), no_tile)
+    for group in range(0, len(places), own):
+        start = places[group][1]
+        tiles = []
+        for _, frames, v in volumes:
+            left = jnp.where(start > 0, tile(frames, v, jnp.maximum(start - 1, 0)), no_tile)
             right = jnp.where(
-                at < across - 1, tile(frames, v, jnp.minimum(at + 1, across - 1)), no_tile
+                start + own < across,
+                tile(frames, v, jnp.minimum(start + own, across - 1)),
+                no_tile,
             )
-            sides = jnp.concatenate([right[:, : block // 2], left[:, block // 2 :]], axis=1)
-            cols = cols_ref[one]
-            partial = jnp.dot(
-                jnp.concatenate([tile(frames, v, at), sides], axis=1),
-                jnp.concatenate([cols[: block + EDGE], gap, cols[block + EDGE :]], axis=0),
+            tiles.append([left] + [tile(frames, v, start + one) for one in range(own)] + [right])
+        for one in range(own):
+            index = places[group + one][0]
+            row_tiles, partials, edges = [], [], []
+            firsts, lasts = [], []
+            for order, (codes, _, v) in enumerate(volumes):
+                row_code, col_code = codes[v, 0, index], codes[v, 1, index]
+                left, middle, right = tiles[order][one : one + 3]
+                sides = jnp.concatenate([right[:, : block // 2], left[:, block // 2 :]], axis=1)
+                col_start = SHIFT - (col_code >> 4)
+                cols = cols_ref[col_code & (SUB - 1), pl.ds(col_start, block + 2 * EDGE), :]
+                cols = cols.astype(jnp.bfloat16)
+                partial = jnp.dot(
+                    jnp.concatenate([middle, sides], axis=1),
+                    jnp.concatenate([cols[EDGE:], gap, cols[:EDGE]], axis=0),
+                    preferred_element_type=jnp.float32,
+                ).astype(jnp.bfloat16)
+                partials.append(partial[:block])
+                edges.append(partial[block:])
+                row_start = SHIFT + (row_code >> 4)
+                step_at = row_code & (SUB - 1)
+                row_tiles.append(rows_ref[step_at, pl.ds(row_start, block), :].astype(jnp.bfloat16))
+                first = edges_ref[step_at, 0, pl.ds(row_start, EDGE), :]
+                last = edges_ref[step_at, 1, pl.ds(row_start, EDGE), :]
+                if order % per_tile:
+                    first = jnp.where(lane == order % per_tile, first, firsts.pop())
+                    last = jnp.where(lane == order % per_tile, last, lasts.pop())
+                firsts.append(first)
+                lasts.append(last)
+            for first, last in zip(firsts, lasts):
+                both = [first.astype(jnp.bfloat16), gap, last.astype(jnp.bfloat16)]
+                row_tiles.append(jnp.concatenate(both, axis=0))
+            deep = many * (block + 2 * EDGE)
+            total = jnp.dot(
+                jnp.concatenate(row_tiles, axis=1)[:, :deep],
+                jnp.concatenate(partials + edges, axis=0),
                 preferred_element_type=jnp.float32,
-            ).astype(jnp.bfloat16)
-            partials.append(partial[:block])
-            edges.append(partial[block:])
-            row_tiles.append(rows_ref[one])
-        for at_tile in range(tiles):
-            both = edges_ref[block_at * tiles + at_tile]
-            row_tiles.append(jnp.concatenate([both[:EDGE], gap, both[EDGE:]], axis=0))
-        deep = many * (block + 2 * EDGE)
-        total = jnp.dot(
-            jnp.concatenate(row_tiles, axis=1)[:, :deep],
-            jnp.concatenate(partials + edges, axis=0),
-            preferred_element_type=jnp.float32,
+            )
+            totals.append(total.astype(jnp.bfloat16))
+    return totals
+
+
+def warp_kernel(down, across, block, own, depth, *refs):
+    place_ref, *code_refs = refs[:3]
+    frame_refs, band_refs = refs[3:5], refs[5:8]
+    out_refs, sums = refs[8 : 7 + depth], refs[7 + depth]
+
+    def one_step(step, _):
+        totals = warp_step(
+            place_ref, step, code_refs, frame_refs, band_refs, down, across, block, own
         )
-        totals.append(total.astype(jnp.bfloat16))
-    return totals
-
-
-def warp_kernel(down, across, block, own, depth, *refs):
-    place_ref, frames_hbm, other_frames_ref, *band_refs = refs[:6]
-    out_refs = refs[6 : 5 + depth]
-    frames_ref, sums, sem = refs[5 + depth :]
-    copy = pltpu.make_async_copy(frames_hbm, frames_ref, sem)
-    copy.start()
-    copy.wait()
-    frame_refs = (frames_ref, other_frames_ref)
-
-    def one_step(step, _):
-        totals = warp_step(place_ref, step, frame_refs, band_refs, down, across, block, own)
         for count, total in enumerate(totals):
             sums[count] = total
         for at, out_ref in enumerate(out_refs):
@@ -226,22 +211,18 @@
     lax.fori_loop(1, depth, one_step, 0)
 
 
-def warp_sums(place, frames, other_frames, bands, depth, block, own):
+def warp_sums(place, codes, other_codes, frames, other_frames, bands, depth, block, own):
     vols, rows, cols = frames.shape
     down, across = rows // block, cols // block
     out = (2 * own, block, block)
-    hbm = pl.BlockSpec(memory_space=pltpu.HBM)
+    smem = pl.BlockSpec(memory_space=pltpu.SMEM)
     vmem = pl.BlockSpec(memory_space=pltpu.VMEM)
     return pl.pallas_call(
         functools.partial(warp_kernel, down, across, block, own, depth),
         out_shape=[jax.ShapeDtypeStruct(out, jnp.bfloat16)] * (depth - 1),
-        in_specs=[pl.BlockSpec(memory_space=pltpu.SMEM), hbm] + [vmem] * 4,
+        in_specs=[smem] * 3 + [vmem] * 5,
         out_specs=[vmem] * (depth - 1),
-        scratch_shapes=[
-            pltpu.VMEM(frames.shape, jnp.bfloat16),
-            pltpu.VMEM(out, jnp.bfloat16),
-            pltpu.SemaphoreType.DMA,
-        ],
+        scratch_shapes=[pltpu.VMEM(out, jnp.bfloat16)],
         compiler_params=pltpu.CompilerParams(vmem_limit_bytes=VMEM_LIMIT),
         cost_estimate=pl.CostEstimate(
             flops=2 * vols * rows * cols * block * 16,
@@ -249,7 +230,7 @@
             transcendentals=0,
         ),
         name="warp",
-    )(place, pltpu.with_memory_space_constraint(frames, pltpu.HBM), other_frames, *bands)
+    )(place, codes, other_codes, frames, other_frames, *bands)
 
 
 def spectrum_kernel(vols, down, across, block, own, planes, depth, *refs):
@@ -258,7 +239,8 @@
     out_refs, sums_ref = refs[15 : 15 + 2 * planes], refs[15 + 2 * planes]
     cross, sums, found = refs[16 + 2 * planes :]
     frame_refs = (frames_ref, other_frames_ref)
-    totals = warp_step(place_ref, 0, frame_refs, band_refs, down, across, block, own)
+    code_refs = (codes_ref, other_codes_ref)
+    totals = warp_step(place_ref, 0, code_refs, frame_refs, band_refs, down, across, block, own)
     for count, total in enumerate(totals):
         sums_ref[count] = total
 
@@ -452,16 +434,14 @@
         [template] + [exchange(template, "z", depth, turn) for turn in range(1, depth)], axis=0
     )
     far = exchange(near, "y", 2, 1)
-    bands = warp_bands(place, shift_codes, other_codes, img_cols // block, depth, block, own)
+    staged, *bands = stage([frames, *tap_constants(block)], other_codes)
     averages, window = [], [0.0, 0.0]
     volumes = vol_dev * depth * 4
     for p in range(pl_dev):
-        work = (frames[:, p], other_frames[:, p])
-        warped = warp_sums(place, *work, bands, depth, block, own)
+        work = (place, shift_codes, other_codes, staged[:, p], other_frames[:, p])
+        warped = warp_sums(*work, bands, depth, block, own)
         templates = (near[:, p], far[:, p])
-        *found, kept = lag_windows(
-            place, shift_codes, other_codes, *work, templates, bands, warped[0], planes, depth, own
-        )
+        *found, kept = lag_windows(*work, templates, bands, warped[0], planes, depth, own)
         warped = [exchange(one, "z", depth, turn + 1) for turn, one in enumerate(warped)]
         found, warped[0] = lax.optimization_barrier((found, warped[0]))
         warped.append(kept)

time: 45.2 us -> 38.2 us (0.85)
  Pallas kernels: 19.3 us -> 13.9 us
  local copies, waits for them, and re-layouts: 2.34 us -> 0.7 us
  waiting for transfers between devices: 6.43 us -> 8 us
  other arithmetic: 1.73 us -> 0.89 us
  starting transfers between devices: 14.4 us -> 13.8 us
    pallas_call x1, Pallas kernels: 6.32 us -> 2.49 us  [stage(): pl.pallas_call(functools.partial(stage_kernel, count), out_shape=[jax.Sha...]
    pallas_call x1, Pallas kernels: 5.97 us -> 4.32 us  [warp_sums(): pl.pallas_call(functools.partial(warp_kernel, down, across, block, own, d...]
    unnamed x16 -> x12, local copies, waits for them, and re-layouts: 1.66 us -> 0.03 us
    ppermute x13, waiting for transfers between devices: 6.43 us -> 8 us  [exchange(): return lax.ppermute(value, axes, [(at, at ^ turn) for at in range(size)])]
    concatenate x1, other arithmetic: 0.89 us -> 0.05 us  [on_device(): jnp.concatenate([template] + [exchange(template, 'z', depth, turn) for tu...]
    ppermute x13, starting transfers between devices: 14.4 us -> 13.8 us  [exchange(): return lax.ppermute(value, axes, [(at, at ^ turn) for at in range(size)])]
  transfers between devices with their start and end apart: 13 -> 13, of which waited for: 5 -> 6; matrix products, arithmetic and copies ran while one was open for 4% -> 2% of each run, Pallas kernels for 43% -> 36%
where the time goes in v8:
time: 38.2 us; the launch traced here: 38.1 us
  Pallas kernels  13.9 us (36%)
  starting transfers between devices  13.8 us (36%)
  waiting for transfers between devices  8 us (21%)
  other arithmetic  0.89 us (2%)
  between operations  0.76 us (2%)
  local copies, waits for them, and re-layouts  0.7 us (2%)
    ppermute x13, starting transfers between devices, exchange(): return lax.ppermute(value, axes, [(at, at ^ turn) for at in range(size)])  13.8 us
    ppermute x13, waiting for transfers between devices, exchange(): return lax.ppermute(value, axes, [(at, at ^ turn) for at in range(size)])  8 us
    pallas_call x1, Pallas kernels, lag_windows(): pl.pallas_call(functools.partial(spectrum_kernel, vols, down, across, blo...  7.09 us
    pallas_call x1, Pallas kernels, warp_sums(): pl.pallas_call(functools.partial(warp_kernel, down, across, block, own, d...  4.32 us
    pallas_call x1, Pallas kernels, stage(): pl.pallas_call(functools.partial(stage_kernel, count), out_shape=[jax.Sha...  2.49 us
  transfers between devices with their start and end apart: 13, of which 6 were waited for; matrix products, arithmetic and copies ran while one was open for 2% of the time, Pallas kernels for 36%

profile of v8, /device:TPU:0, one launch (start us, length us, event | category | flops | bytes accessed | tf_op | source)
XLA Modules:
  0.0 38.1 jit_solution(8552976620667636620)
XLA Ops:
  0.6 0.5 %collective-permute-start.1 = (bf16[2,1,512,1024]{3,2,0,1:T(8,128)(2,1)}, bf16[2,1,512,1024]{3,2,0,1:T(8,128)(2,1)S(1)}, u32[]{:S(2)}, u32[]{:S(2)}) collective-permute-start(bf16[2,1,512,1024]{3,2,0,1:T(8,128)(2,1)} %bitcast.20), channel_id=1, source_target_pairs={{0,2},{2,0},{1,3},{3,1},{4,6},{6,4},{5,7},{7,5},{8,10},{10,8},{9,1... | collective-permute-start | bytes 6291464 | tf_op jit(solution)/shard_map/ppermute | solution.py:421
  1.1 4.7 %collective-permute-start.4 = (bf16[2,1,128,128]{3,2,0,1:T(8,128)(2,1)}, bf16[2,1,128,128]{3,2,0,1:T(8,128)(2,1)S(1)}, u32[]{:S(2)}, u32[]{:S(2)}) collective-permute-start(bf16[2,1,128,128]{3,2,0,1:T(8,128)(2,1)} %bitcast.21), channel_id=1, source_target_pairs={{0,24},{8,16},{16,8},{24,0},{1,25},{9,17},{17,9},{25,1},{2,26},{10... | collective-permute-start | bytes 196616 | tf_op jit(solution)/shard_map/ppermute | solution.py:421
  5.8 0.0 collective-permute-start.3
  5.8 0.6 %collective-permute-start.2 = (bf16[2,1,128,128]{3,2,0,1:T(8,128)(2,1)}, bf16[2,1,128,128]{3,2,0,1:T(8,128)(2,1)S(1)}, u32[]{:S(2)}, u32[]{:S(2)}) collective-permute-start(bf16[2,1,128,128]{3,2,0,1:T(8,128)(2,1)} %bitcast.23), channel_id=1, source_target_pairs={{0,8},{8,0},{16,24},{24,16},{1,9},{9,1},{17,25},{25,17},{2,10},{10... | collective-permute-start | bytes 196616 | tf_op jit(solution)/shard_map/ppermute | solution.py:421
  6.5 0.1 pad_add_fusion.refs_0_
  6.6 1.3 %collective-permute-done.refs_4_.refs_2_ = s32[2,2,32]{2,1,0:T(2,128)S(1)} collective-permute-done((s32[2,2,32]{2,1,0:T(2,128)}, s32[2,2,32]{2,1,0:T(2,128)S(1)}, u32[]{:S(2)}, u32[]{:S(2)}) %collective-permute-start) | collective-permute-done | bytes 544 | tf_op jit(solution)/shard_map/ppermute | solution.py:421
  7.8 2.5 %stage.1 = (bf16[2,1,512,1024]{3,2,1,0:T(8,128)(2,1)S(1)}, f32[16,176,128]{2,1,0:T(8,128)S(1)}, f32[16,144,128]{2,1,0:T(8,128)S(1)}, f32[16,2,32,128]{3,2,1,0:T(8,128)S(1)}) custom-call(bf16[2,1,512,1024]{3,2,1,0:T(8,128)(2,1)} %refs_0_.1, f32[16,176,128]{2,1,0:T(8,128)} %constant.32.clone.refs_1_, f32[16,144,128]{2,1,0:T(8,128)} %constant.33.clone.refs_2_, ...), custom_call_target="tpu_custom_call" | custom-call | tf_op jit(solution)/shard_map/stage/pallas_call | solution.py:102
  10.4 1.7 %collective-permute-done.3 = bf16[2,1,128,128]{3,2,0,1:T(8,128)(2,1)S(1)} collective-permute-done((bf16[2,1,128,128]{3,2,0,1:T(8,128)(2,1)}, bf16[2,1,128,128]{3,2,0,1:T(8,128)(2,1)S(1)}, u32[]{:S(2)}, u32[]{:S(2)}) %collective-permute-start.3) | collective-permute-done | bytes 65568 | tf_op jit(solution)/shard_map/ppermute | solution.py:421
  12.2 1.6 %collective-permute-start.5 = (bf16[8,1,128,128]{3,2,0,1:T(8,128)(2,1)S(1)}, bf16[8,1,128,128]{3,2,0,1:T(8,128)(2,1)S(1)}, u32[]{:S(2)}, u32[]{:S(2)}) collective-permute-start(bf16[8,1,128,128]{3,2,0,1:T(8,128)(2,1)S(1)} %get-tuple-element.38), channel_id=1, source_target_pairs={{0,4},{4,0},{1,5},{5,1},{2,6},{6,2},{3,7},{7,3},{8,12},{12,8},{9,1... | collective-permute-start | bytes 786440 | tf_op jit(solution)/shard_map/ppermute | solution.py:421
  13.8 0.0 copy-start.3
  13.8 0.0 copy-start.4
  13.8 4.3 %warp.1 = (bf16[4,128,128]{2,1,0:T(8,128)(2,1)S(1)}, bf16[4,128,128]{2,1,0:T(8,128)(2,1)S(1)}, bf16[4,128,128]{2,1,0:T(8,128)(2,1)S(1)}) custom-call(s32[4]{0:T(128)S(1)} %pad_add_fusion.refs_0_, s32[2,2,32]{2,1,0:T(2,128)S(1)} %copy-done, s32[2,2,32]{2,1,0:T(2,128)S(1)} %collective-permute-done.refs_4_.refs_2_, bf16[2,512,1024]{2,1,0:T(8,128)(2,1)S(1)} %bitcast.17, ...), custom_call_target="tpu_custom_call" | custom-call | flops 4294967296 | bytes 4718592 | tf_op jit(solution)/shard_map/warp/pallas_call | solution.py:220
  18.1 1.2 %collective-permute-start.10 = (bf16[4,128,128]{2,1,0:T(8,128)(2,1)S(1)}, bf16[4,128,128]{2,1,0:T(8,128)(2,1)S(1)}, u32[]{:S(2)}, u32[]{:S(2)}) collective-permute-start(bf16[4,128,128]{2,1,0:T(8,128)(2,1)S(1)} %get-tuple-element.33), channel_id=1, source_target_pairs={{0,16},{8,24},{16,0},{24,8},{1,17},{9,25},{17,1},{25,9},{2,18},{10... | collective-permute-start | bytes 393224 | tf_op jit(solution)/shard_map/ppermute | solution.py:421
  19.4 2.4 %collective-permute-start.11 = (bf16[4,128,128]{2,1,0:T(8,128)(2,1)S(1)}, bf16[4,128,128]{2,1,0:T(8,128)(2,1)S(1)}, u32[]{:S(2)}, u32[]{:S(2)}) collective-permute-start(bf16[4,128,128]{2,1,0:T(8,128)(2,1)S(1)} %get-tuple-element.34), channel_id=1, source_target_pairs={{0,24},{8,16},{16,8},{24,0},{1,25},{9,17},{17,9},{25,1},{2,26},{10... | collective-permute-start | bytes 393224 | tf_op jit(solution)/shard_map/ppermute | solution.py:421
  21.8 7.1 %lag_windows.1 = (f32[2,8,256]{2,1,0:T(8,128)S(1)}, f32[2,8,256]{2,1,0:T(8,128)S(1)}, f32[2,8,256]{2,1,0:T(8,128)S(1)}, f32[2,8,256]{2,1,0:T(8,128)S(1)}, bf16[4,128,128]{2,1,0:T(8,128)(2,1)S(1)}) custom-call(s32[4]{0:T(128)S(1)} %pad_add_fusion.refs_0_, s32[2,2,32]{2,1,0:T(2,128)S(1)} %copy-done, s32[2,2,32]{2,1,0:T(2,128)S(1)} %collective-permute-done.refs_4_.refs_2_, ...), custom_call_target="tpu_custom_call" | custom-call | flops 6442450944 | bytes 4718592 | tf_op jit(solution)/shard_map/lag_windows/pallas_call | solution.py:397
  28.9 1.9 %collective-permute-done.6 = bf16[4,128,128]{2,1,0:T(8,128)(2,1)S(1)} collective-permute-done((bf16[4,128,128]{2,1,0:T(8,128)(2,1)S(1)}, bf16[4,128,128]{2,1,0:T(8,128)(2,1)S(1)}, u32[]{:S(2)}, u32[]{:S(2)}) %collective-permute-start.6) | collective-permute-done | bytes 131104 | tf_op jit(solution)/shard_map/ppermute | solution.py:421
  30.8 1.5 %collective-permute-start.7 = (f32[2,8,256]{2,1,0:T(8,128)S(1)}, f32[2,8,256]{2,1,0:T(8,128)S(1)}, u32[]{:S(2)}, u32[]{:S(2)}) collective-permute-start(f32[2,8,256]{2,1,0:T(8,128)S(1)} %get-tuple-element.29), channel_id=1, source_target_pairs={{0,1},{1,0},{2,3},{3,2},{4,5},{5,4},{6,7},{7,6},{8,9},{9,8},{10,11... | collective-permute-start | bytes 49160 | tf_op jit(solution)/shard_map/ppermute | solution.py:421
  32.3 0.6 %collective-permute-start.9 = (f32[2,8,256]{2,1,0:T(8,128)S(1)}, f32[2,8,256]{2,1,0:T(8,128)S(1)}, u32[]{:S(2)}, u32[]{:S(2)}) collective-permute-start(f32[2,8,256]{2,1,0:T(8,128)S(1)} %get-tuple-element.31), channel_id=1, source_target_pairs={{0,3},{1,2},{2,1},{3,0},{4,7},{5,6},{6,5},{7,4},{8,11},{9,10},{10,... | collective-permute-start | bytes 49160 | tf_op jit(solution)/shard_map/ppermute | solution.py:421
  33.0 0.6 %collective-permute-start.12 = (bf16[2,128,128]{2,1,0:T(8,128)(2,1)S(1)}, bf16[2,128,128]{2,1,0:T(8,128)(2,1)S(1)}, u32[]{:S(2)}, u32[]{:S(2)}) collective-permute-start(bf16[2,128,128]{2,1,0:T(8,128)(2,1)S(1)} %add_convert_fusion), channel_id=1, source_target_pairs={{0,4},{4,0},{1,5},{5,1},{2,6},{6,2},{3,7},{7,3},{8,12},{12,8},{9,1... | collective-permute-start | bytes 196616 | tf_op jit(solution)/shard_map/ppermute | solution.py:421
  33.6 1.0 %collective-permute-done.7 = f32[2,8,256]{2,1,0:T(8,128)S(1)} collective-permute-done((f32[2,8,256]{2,1,0:T(8,128)S(1)}, f32[2,8,256]{2,1,0:T(8,128)S(1)}, u32[]{:S(2)}, u32[]{:S(2)}) %collective-permute-start.7) | collective-permute-done | bytes 16416 | tf_op jit(solution)/shard_map/ppermute | solution.py:421
  34.6 0.9 %collective-permute-done.9 = f32[2,8,256]{2,1,0:T(8,128)S(1)} collective-permute-done((f32[2,8,256]{2,1,0:T(8,128)S(1)}, f32[2,8,256]{2,1,0:T(8,128)S(1)}, u32[]{:S(2)}, u32[]{:S(2)}) %collective-permute-start.9) | collective-permute-done | bytes 16416 | tf_op jit(solution)/shard_map/ppermute | solution.py:421
  35.6 0.6 %reshape.15 = f32[2,16,256]{2,1,0:T(8,128)} reshape(f32[2,4,2,2,256]{4,3,2,1,0:T(2,128)S(1)} %copy.17) | data formatting | bytes 65536 | tf_op jit(solution)/shard_map/reshape | solution.py:458
  36.2 1.1 %collective-permute-done.12 = bf16[2,128,128]{2,1,0:T(8,128)(2,1)S(1)} collective-permute-done((bf16[2,128,128]{2,1,0:T(8,128)(2,1)S(1)}, bf16[2,128,128]{2,1,0:T(8,128)(2,1)S(1)}, u32[]{:S(2)}, u32[]{:S(2)}) %collective-permute-start.12) | collective-permute-done | bytes 65568 | tf_op jit(solution)/shard_map/ppermute | solution.py:421
  37.4 0.7 %multiply_bitcast_fusion = f32[2,1,128,128]{3,2,1,0:T(8,128)} fusion(bf16[2,128,128]{2,1,0:T(8,128)(2,1)S(1)} %collective-permute-done.12, bf16[4,128,128]{2,1,0:T(8,128)(2,1)S(1)} %collective-permute-done.11, bf16[4,128,128]{2,1,0:T(8,128)(2,1)S(1)} %collective-permute-done.10, bf16[4,128,128]{2,1,0:T(8,128)(2,1)S(1)} %get-tuple-element.35, ...), kind=kLoop, calls=%fused_computation.1 | loop fusion | flops 327680 | bytes 458752
  (27 shorter events, 0.2 us)
Async XLA Ops:
  0.6 13.1 %collective-permute-start.1 = (bf16[2,1,512,1024]{3,2,0,1:T(8,128)(2,1)}, bf16[2,1,512,1024]{3,2,0,1:T(8,128)(2,1)S(1)}, u32[]{:S(2)}, u32[]{:S(2)}) collective-permute-start(bf16[2,1,512,1024]{3,2,0,1:T(8,128)(2,1)} %bitcast.20), channel_id=1, source_target_pairs={{0,2},{2,0},{1,3},{3,1},{4,6},{6,4},{5,7},{7,5},{8,10},{10,8},{9,1... | collective-permute-start | bytes 6291464 | tf_op jit(solution)/shard_map/ppermute | solution.py:421
  1.1 9.2 %collective-permute-start.4 = (bf16[2,1,128,128]{3,2,0,1:T(8,128)(2,1)}, bf16[2,1,128,128]{3,2,0,1:T(8,128)(2,1)S(1)}, u32[]{:S(2)}, u32[]{:S(2)}) collective-permute-start(bf16[2,1,128,128]{3,2,0,1:T(8,128)(2,1)} %bitcast.21), channel_id=1, source_target_pairs={{0,24},{8,16},{16,8},{24,0},{1,25},{9,17},{17,9},{25,1},{2,26},{10... | collective-permute-start | bytes 196616 | tf_op jit(solution)/shard_map/ppermute | solution.py:421
  5.8 6.3 %collective-permute-start.3 = (bf16[2,1,128,128]{3,2,0,1:T(8,128)(2,1)}, bf16[2,1,128,128]{3,2,0,1:T(8,128)(2,1)S(1)}, u32[]{:S(2)}, u32[]{:S(2)}) collective-permute-start(bf16[2,1,128,128]{3,2,0,1:T(8,128)(2,1)} %bitcast.22), channel_id=1, source_target_pairs={{0,16},{8,24},{16,0},{24,8},{1,17},{9,25},{17,1},{25,9},{2,18},{10... | collective-permute-start | bytes 196616 | tf_op jit(solution)/shard_map/ppermute | solution.py:421
  5.8 6.3 %collective-permute-start.2 = (bf16[2,1,128,128]{3,2,0,1:T(8,128)(2,1)}, bf16[2,1,128,128]{3,2,0,1:T(8,128)(2,1)S(1)}, u32[]{:S(2)}, u32[]{:S(2)}) collective-permute-start(bf16[2,1,128,128]{3,2,0,1:T(8,128)(2,1)} %bitcast.23), channel_id=1, source_target_pairs={{0,8},{8,0},{16,24},{24,16},{1,9},{9,1},{17,25},{25,17},{2,10},{10... | collective-permute-start | bytes 196616 | tf_op jit(solution)/shard_map/ppermute | solution.py:421
  6.5 1.4 %collective-permute-start = (s32[2,2,32]{2,1,0:T(2,128)}, s32[2,2,32]{2,1,0:T(2,128)S(1)}, u32[]{:S(2)}, u32[]{:S(2)}) collective-permute-start(s32[2,2,32]{2,1,0:T(2,128)} %refs_1_.4), channel_id=1, source_target_pairs={{0,2},{2,0},{1,3},{3,1},{4,6},{6,4},{5,7},{7,5},{8,10},{10,8},{9,1... | collective-permute-start | bytes 1544 | tf_op jit(solution)/shard_map/ppermute | solution.py:421
  6.5 5.6 %copy-start.5 = (bf16[2,1,128,128]{3,2,1,0:T(8,128)(2,1)S(1)}, bf16[2,1,128,128]{3,2,1,0:T(8,128)(2,1)}, u32[]{:S(2)}) copy-start(bf16[2,1,128,128]{3,2,1,0:T(8,128)(2,1)} %param.11) | copy-start | bytes 196612
  6.6 7.2 %copy-start = (s32[2,2,32]{2,1,0:T(2,128)S(1)}, s32[2,2,32]{2,1,0:T(2,128)}, u32[]{:S(2)}) copy-start(s32[2,2,32]{2,1,0:T(2,128)} %refs_1_.4) | copy-start | bytes 1540
  12.2 9.6 %collective-permute-start.5 = (bf16[8,1,128,128]{3,2,0,1:T(8,128)(2,1)S(1)}, bf16[8,1,128,128]{3,2,0,1:T(8,128)(2,1)S(1)}, u32[]{:S(2)}, u32[]{:S(2)}) collective-permute-start(bf16[8,1,128,128]{3,2,0,1:T(8,128)(2,1)S(1)} %get-tuple-element.38), channel_id=1, source_target_pairs={{0,4},{4,0},{1,5},{5,1},{2,6},{6,2},{3,7},{7,3},{8,12},{12,8},{9,1... | collective-permute-start | bytes 786440 | tf_op jit(solution)/shard_map/ppermute | solution.py:421
  13.7 8.0 %copy-start.1 = (bf16[256,256]{1,0:T(8,128)(2,1)S(1)}, bf16[256,256]{1,0:T(8,128)(2,1)}, u32[]{:S(2)}) copy-start(bf16[256,256]{1,0:T(8,128)(2,1)} %constant.36.clone.refs_4_) | copy-start | bytes 393220
  13.8 8.0 %copy-start.2 = (bf16[256,128]{1,0:T(8,128)(2,1)S(1)}, bf16[256,128]{1,0:T(8,128)(2,1)}, u32[]{:S(2)}) copy-start(bf16[256,128]{1,0:T(8,128)(2,1)} %constant.38.clone.refs_6_) | copy-start | bytes 196612
  13.8 8.0 %copy-start.3 = (bf16[160,128]{1,0:T(8,128)(2,1)S(1)}, bf16[160,128]{1,0:T(8,128)(2,1)}, u32[]{:S(2)}) copy-start(bf16[160,128]{1,0:T(8,128)(2,1)} %constant.35.clone.refs_3_) | copy-start | bytes 122884
  13.8 8.0 %copy-start.4 = (bf16[64,160]{1,0:T(8,128)(2,1)S(1)}, bf16[64,160]{1,0:T(8,128)(2,1)}, u32[]{:S(2)}) copy-start(bf16[64,160]{1,0:T(8,128)(2,1)} %constant.37.clone.refs_5_) | copy-start | bytes 61444
  18.1 14.9 %collective-permute-start.10 = (bf16[4,128,128]{2,1,0:T(8,128)(2,1)S(1)}, bf16[4,128,128]{2,1,0:T(8,128)(2,1)S(1)}, u32[]{:S(2)}, u32[]{:S(2)}) collective-permute-start(bf16[4,128,128]{2,1,0:T(8,128)(2,1)S(1)} %get-tuple-element.33), channel_id=1, source_target_pairs={{0,16},{8,24},{16,0},{24,8},{1,17},{9,25},{17,1},{25,9},{2,18},{10... | collective-permute-start | bytes 393224 | tf_op jit(solution)/shard_map/ppermute | solution.py:421
  19.4 13.6 %collective-permute-start.11 = (bf16[4,128,128]{2,1,0:T(8,128)(2,1)S(1)}, bf16[4,128,128]{2,1,0:T(8,128)(2,1)S(1)}, u32[]{:S(2)}, u32[]{:S(2)}) collective-permute-start(bf16[4,128,128]{2,1,0:T(8,128)(2,1)S(1)} %get-tuple-element.34), channel_id=1, source_target_pairs={{0,24},{8,16},{16,8},{24,0},{1,25},{9,17},{17,9},{25,1},{2,26},{10... | collective-permute-start | bytes 393224 | tf_op jit(solution)/shard_map/ppermute | solution.py:421
  21.8 9.1 %collective-permute-start.6 = (bf16[4,128,128]{2,1,0:T(8,128)(2,1)S(1)}, bf16[4,128,128]{2,1,0:T(8,128)(2,1)S(1)}, u32[]{:S(2)}, u32[]{:S(2)}) collective-permute-start(bf16[4,128,128]{2,1,0:T(8,128)(2,1)S(1)} %get-tuple-element.23.refs_14_), channel_id=1, source_target_pairs={{0,8},{8,0},{16,24},{24,16},{1,9},{9,1},{17,25},{25,17},{2,10},{10... | collective-permute-start | bytes 393224 | tf_op jit(solution)/shard_map/ppermute | solution.py:421
  30.8 3.7 %collective-permute-start.7 = (f32[2,8,256]{2,1,0:T(8,128)S(1)}, f32[2,8,256]{2,1,0:T(8,128)S(1)}, u32[]{:S(2)}, u32[]{:S(2)}) collective-permute-start(f32[2,8,256]{2,1,0:T(8,128)S(1)} %get-tuple-element.29), channel_id=1, source_target_pairs={{0,1},{1,0},{2,3},{3,2},{4,5},{5,4},{6,7},{7,6},{8,9},{9,8},{10,11... | collective-permute-start | bytes 49160 | tf_op jit(solution)/shard_map/ppermute | solution.py:421
  32.3 2.3 %collective-permute-start.8 = (f32[2,8,256]{2,1,0:T(8,128)S(1)}, f32[2,8,256]{2,1,0:T(8,128)S(1)}, u32[]{:S(2)}, u32[]{:S(2)}) collective-permute-start(f32[2,8,256]{2,1,0:T(8,128)S(1)} %get-tuple-element.30), channel_id=1, source_target_pairs={{0,2},{1,3},{2,0},{3,1},{4,6},{5,7},{6,4},{7,5},{8,10},{9,11},{10,... | collective-permute-start | bytes 49160 | tf_op jit(solution)/shard_map/ppermute | solution.py:421
  32.3 3.2 %collective-permute-start.9 = (f32[2,8,256]{2,1,0:T(8,128)S(1)}, f32[2,8,256]{2,1,0:T(8,128)S(1)}, u32[]{:S(2)}, u32[]{:S(2)}) collective-permute-start(f32[2,8,256]{2,1,0:T(8,128)S(1)} %get-tuple-element.31), channel_id=1, source_target_pairs={{0,3},{1,2},{2,1},{3,0},{4,7},{5,6},{6,5},{7,4},{8,11},{9,10},{10,... | collective-permute-start | bytes 49160 | tf_op jit(solution)/shard_map/ppermute | solution.py:421
  33.0 4.3 %collective-permute-start.12 = (bf16[2,128,128]{2,1,0:T(8,128)(2,1)S(1)}, bf16[2,128,128]{2,1,0:T(8,128)(2,1)S(1)}, u32[]{:S(2)}, u32[]{:S(2)}) collective-permute-start(bf16[2,128,128]{2,1,0:T(8,128)(2,1)S(1)} %add_convert_fusion), channel_id=1, source_target_pairs={{0,4},{4,0},{1,5},{5,1},{2,6},{6,2},{3,7},{7,3},{8,12},{12,8},{9,1... | collective-permute-start | bytes 196616 | tf_op jit(solution)/shard_map/ppermute | solution.py:421

commit v9 on v8

--- a/solution.py
+++ b/solution.py
@@ -108,7 +108,7 @@
         scratch_shapes=[pltpu.SemaphoreType.DMA((count,))],
         compiler_params=pltpu.CompilerParams(vmem_limit_bytes=VMEM_LIMIT),
         name="stage",
-    )(*kept, after)
+    )(*kept, pltpu.with_memory_space_constraint(after, pltpu.HBM))
 
 
 def warp_step(place_ref, step, code_refs, frame_refs, band_refs, down, across, block, own):
@@ -233,16 +233,21 @@
     )(place, codes, other_codes, frames, other_frames, *bands)
 
 
-def spectrum_kernel(vols, down, across, block, own, planes, depth, *refs):
+def spectrum_kernel(vols, down, across, block, own, planes, depth, other, *refs):
     place_ref, codes_ref, other_codes_ref, row_ref, col_ref, lag_ref, span_ref = refs[:7]
-    frames_ref, other_frames_ref, near_ref, far_ref, *band_refs = refs[7:14]
-    out_refs, sums_ref = refs[15 : 15 + 2 * planes], refs[15 + 2 * planes]
-    cross, sums, found = refs[16 + 2 * planes :]
-    frame_refs = (frames_ref, other_frames_ref)
-    code_refs = (codes_ref, other_codes_ref)
-    totals = warp_step(place_ref, 0, code_refs, frame_refs, band_refs, down, across, block, own)
-    for count, total in enumerate(totals):
-        sums_ref[count] = total
+    frames_ref, other_frames_ref, template_ref = refs[7:10]
+    cross, sums = refs[-2:]
+    if other:
+        found_ref, out_refs, found = refs[10], refs[11:-3], refs[-3]
+        found[...] = found_ref[...]
+    else:
+        band_refs, found, sums_ref = refs[10:13], refs[14], refs[15]
+        code_refs, frame_refs = (codes_ref, other_codes_ref), (frames_ref, other_frames_ref)
+        totals = warp_step(
+            place_ref, 0, code_refs, frame_refs, band_refs, down, across, block, own
+        )
+        for count, total in enumerate(totals):
+            sums_ref[count] = total
 
     row_table = row_ref[...]
     col_table = col_ref[...]
@@ -257,24 +262,21 @@
     local = 2 * own
     no_rows = jnp.zeros((half - kept, LANES), jnp.float32)
 
-    def one_step(step, _):
-        places = step_places(place_ref, step, across, own)
-        band = step_band(place_ref, step, across, own)
-        band_rows = pl.ds(pl.multiple_of(band * block, block), block)
+    def two_steps(half_step, _):
+        places = []
+        for step in (2 * half_step, 2 * half_step + 1):
+            band = step_band(place_ref, step, across, own)
+            band_rows = pl.ds(pl.multiple_of(band * block, block), block)
+            chosen = step_places(place_ref, step, across, own)[other * own : (other + 1) * own]
+            for one, (index, at) in enumerate(chosen):
+                lanes = pl.ds(pl.multiple_of(at * block, block), block)
+                places.append((index, band_rows, lanes, step * own + one))
 
         for pair in range(local // 2):
             pair_places = places[2 * pair : 2 * pair + 2]
-            counts = (2 * pair, 2 * pair + 1)
-            sources = [
-                [(far_ref if count // own else near_ref)[step * own + count % own] for count in counts]
-            ]
+            sources = [[template_ref[at] for _, _, _, at in pair_places]]
             for _, frames, v in volumes:
-                sources.append(
-                    [
-                        frames[v, band_rows, pl.ds(pl.multiple_of(at * block, block), block)]
-                        for _, at in pair_places
-                    ]
-                )
+                sources.append([frames[v, rows, lanes] for _, rows, lanes, _ in pair_places])
             parts = []
             for source in sources:
                 rows = jnp.dot(
@@ -348,7 +350,7 @@
         for pair in range(local // 2):
             for order, (codes, _, v) in enumerate(volumes):
                 for side in range(2):
-                    index, _ = places[2 * pair + side]
+                    index = places[2 * pair + side][0]
                     row_shift = codes[v, 0, index] >> 4
                     col_shift = codes[v, 1, index] >> 4
                     at = (pair * many + order) * 2 + side
@@ -360,7 +362,9 @@
                     )
         return 0
 
-    lax.fori_loop(0, depth, one_step, 0)
+    lax.fori_loop(0, depth // 2, two_steps, 0)
+    if not other:
+        return
 
     share = depth * local // planes
     per_tile = LANES // WIN
@@ -381,10 +385,10 @@
 
 
 def lag_windows(
-    place, codes, other_codes, frames, other_frames, templates, bands, after, planes, depth, own
+    place, codes, other_codes, frames, other_frames, template, bands, other, planes, depth, own, more
 ):
     vols, rows, cols = frames.shape
-    block = templates[0].shape[-1]
+    block = template.shape[-1]
     down, across = rows // block, cols // block
     tables = dft_constants(block)
     kept = -(-(block // 2 + 1) // 8) * 8
@@ -392,29 +396,34 @@
     vmem = pl.BlockSpec(memory_space=pltpu.VMEM)
     local = depth * 2 * own
     many = 2 * vols * 2 * own
-    out = (vols, local // planes, WIN * WIN)
-    kept_sums = (2 * own, block, block)
+    found = jax.ShapeDtypeStruct((2 * vols, local * WIN, LANES), jnp.float32)
+    if other:
+        out = (vols, local // planes, WIN * WIN)
+        out_shape = [jax.ShapeDtypeStruct(out, jnp.float32)] * (2 * planes)
+        scratch_shapes = [pltpu.VMEM(found.shape, found.dtype)]
+        bands, last = [], vmem
+    else:
+        out_shape = [found, jax.ShapeDtypeStruct((2 * own, block, block), jnp.bfloat16)]
+        scratch_shapes = []
+        last = pl.BlockSpec(memory_space=pl.ANY)
     return pl.pallas_call(
-        functools.partial(spectrum_kernel, vols, down, across, block, own, planes, depth),
-        out_shape=[jax.ShapeDtypeStruct(out, jnp.float32)] * (2 * planes)
-        + [jax.ShapeDtypeStruct(kept_sums, jnp.bfloat16)],
-        in_specs=[smem] * 3
-        + [vmem] * (len(tables) + 4 + len(bands))
-        + [pl.BlockSpec(memory_space=pl.ANY)],
-        out_specs=[vmem] * (2 * planes + 1),
-        scratch_shapes=[
+        functools.partial(spectrum_kernel, vols, down, across, block, own, planes, depth, other),
+        out_shape=out_shape,
+        in_specs=[smem] * 3 + [vmem] * (len(tables) + 3 + len(bands)) + [last],
+        out_specs=[vmem] * len(out_shape),
+        scratch_shapes=scratch_shapes
+        + [
             pltpu.VMEM((many, 3 * kept, LANES), jnp.float32),
             pltpu.VMEM((many, 1, LANES), jnp.float32),
-            pltpu.VMEM((2 * vols, local * WIN, LANES), jnp.float32),
         ],
         compiler_params=pltpu.CompilerParams(vmem_limit_bytes=VMEM_LIMIT),
         cost_estimate=pl.CostEstimate(
-            flops=2 * 3 * rows * cols * block * 16,
+            flops=2 * 3 * rows * cols * block * 8,
             bytes_accessed=vols * rows * cols * 4 + rows * cols,
             transcendentals=0,
         ),
         name="lag_windows",
-    )(place, codes, other_codes, *tables, frames, other_frames, *templates, *bands, after)
+    )(place, codes, other_codes, *tables, frames, other_frames, template, *bands, more)
 
 
 def exchange(value, axes, size, turn):
@@ -430,20 +439,21 @@
     place = jnp.stack([lax.axis_index(axis) for axis in ("z", "y", "core", "plane")])
     other_codes = exchange(shift_codes, "core", 2, 1)
     other_frames = exchange(frames, "core", 2, 1)
-    near = jnp.concatenate(
-        [template] + [exchange(template, "z", depth, turn) for turn in range(1, depth)], axis=0
-    )
-    far = exchange(near, "y", 2, 1)
-    staged, *bands = stage([frames, *tap_constants(block)], other_codes)
+    pieces = [template] + [exchange(template, "z", depth, turn) for turn in range(1, depth)]
+    staged, *bands = stage([frames, *tap_constants(block)], template)
     averages, window = [], [0.0, 0.0]
     volumes = vol_dev * depth * 4
     for p in range(pl_dev):
         work = (place, shift_codes, other_codes, staged[:, p], other_frames[:, p])
-        warped = warp_sums(*work, bands, depth, block, own)
-        templates = (near[:, p], far[:, p])
-        *found, kept = lag_windows(*work, templates, bands, warped[0], planes, depth, own)
+        warped = list(warp_sums(*work, bands, depth, block, own))
+        pieces, warped[0] = lax.optimization_barrier((pieces, warped[0]))
+        near = jnp.concatenate([piece[:, p] for piece in pieces], axis=0)
+        far = exchange(near, "y", 2, 1)
+        sizes = (planes, depth, own)
+        part, kept = lag_windows(*work, near, bands, 0, *sizes, warped[0])
+        found = lag_windows(*work, far, bands, 1, *sizes, part)
         warped = [exchange(one, "z", depth, turn + 1) for turn, one in enumerate(warped)]
-        found, warped[0] = lax.optimization_barrier((found, warped[0]))
+        found, warped = lax.optimization_barrier((found, warped))
         warped.append(kept)
         sums = [sum(one[at : at + own].astype(jnp.float32) for one in warped) for at in (0, own)]
         taken = exchange(sums[1].astype(jnp.bfloat16), "y", 2, 1)

time: 38.2 us -> 37 us (0.969)
  waiting for transfers between devices: 8 us -> 4.13 us
  starting transfers between devices: 13.8 us -> 15.8 us
  Pallas kernels: 13.9 us -> 14.6 us
    ppermute x13, waiting for transfers between devices: 8 us -> 4.13 us  [exchange(): return lax.ppermute(value, axes, [(at, at ^ turn) for at in range(size)])]
    ppermute x13, starting transfers between devices: 13.8 us -> 15.8 us  [exchange(): return lax.ppermute(value, axes, [(at, at ^ turn) for at in range(size)])]
    pallas_call x1 -> x2, Pallas kernels: 7.09 us -> 7.74 us  [lag_windows(): pl.pallas_call(functools.partial(spectrum_kernel, vols, down, across, blo...]
  transfers between devices with their start and end apart: 13 -> 13, of which waited for: 6 -> 3; matrix products, arithmetic and copies ran while one was open for 2% -> 2% of each run, Pallas kernels for 36% -> 40%
where the time goes in v9:
time: 37 us; the launch traced here: 36.9 us
  starting transfers between devices  15.8 us (43%)
  Pallas kernels  14.6 us (39%)
  waiting for transfers between devices  4.13 us (11%)
  other arithmetic  0.88 us (2%)
  between operations  0.81 us (2%)
  local copies, waits for them, and re-layouts  0.71 us (2%)
    ppermute x13, starting transfers between devices, exchange(): return lax.ppermute(value, axes, [(at, at ^ turn) for at in range(size)])  15.8 us
    pallas_call x2, Pallas kernels, lag_windows(): pl.pallas_call(functools.partial(spectrum_kernel, vols, down, across, blo...  7.74 us
    pallas_call x1, Pallas kernels, warp_sums(): pl.pallas_call(functools.partial(warp_kernel, down, across, block, own, d...  4.33 us
    ppermute x13, waiting for transfers between devices, exchange(): return lax.ppermute(value, axes, [(at, at ^ turn) for at in range(size)])  4.13 us
    pallas_call x1, Pallas kernels, stage(): pl.pallas_call(functools.partial(stage_kernel, count), out_shape=[jax.Sha...  2.51 us
  transfers between devices with their start and end apart: 13, of which 3 were waited for; matrix products, arithmetic and copies ran while one was open for 2% of the time, Pallas kernels for 40%

profile of v9, /device:TPU:0, one launch (start us, length us, event | category | flops | bytes accessed | tf_op | source)
XLA Modules:
  0.0 36.9 jit_solution(14060826292655268187)
XLA Ops:
  0.6 0.5 %collective-permute-start.1 = (bf16[2,1,512,1024]{3,2,0,1:T(8,128)(2,1)}, bf16[2,1,512,1024]{3,2,0,1:T(8,128)(2,1)S(1)}, u32[]{:S(2)}, u32[]{:S(2)}) collective-permute-start(bf16[2,1,512,1024]{3,2,0,1:T(8,128)(2,1)} %bitcast.22), channel_id=1, source_target_pairs={{0,2},{2,0},{1,3},{3,1},{4,6},{6,4},{5,7},{7,5},{8,10},{10,8},{9,1... | collective-permute-start | bytes 6291464 | tf_op jit(solution)/shard_map/ppermute | solution.py:430
  1.1 4.7 %collective-permute-start.4 = (bf16[2,1,128,128]{3,2,0,1:T(8,128)(2,1)}, bf16[2,1,128,128]{3,2,0,1:T(8,128)(2,1)S(1)}, u32[]{:S(2)}, u32[]{:S(2)}) collective-permute-start(bf16[2,1,128,128]{3,2,0,1:T(8,128)(2,1)} %bitcast.23), channel_id=1, source_target_pairs={{0,24},{8,16},{16,8},{24,0},{1,25},{9,17},{17,9},{25,1},{2,26},{10... | collective-permute-start | bytes 196616 | tf_op jit(solution)/shard_map/ppermute | solution.py:430
  5.8 0.6 %collective-permute-start.2 = (bf16[2,1,128,128]{3,2,0,1:T(8,128)(2,1)}, bf16[2,1,128,128]{3,2,0,1:T(8,128)(2,1)S(1)}, u32[]{:S(2)}, u32[]{:S(2)}) collective-permute-start(bf16[2,1,128,128]{3,2,0,1:T(8,128)(2,1)} %bitcast.25), channel_id=1, source_target_pairs={{0,8},{8,0},{16,24},{24,16},{1,9},{9,1},{17,25},{25,17},{2,10},{10... | collective-permute-start | bytes 196616 | tf_op jit(solution)/shard_map/ppermute | solution.py:430
  6.5 0.1 pad_add_fusion.refs_0_
  6.6 2.5 %stage.1 = (bf16[2,1,512,1024]{3,2,1,0:T(8,128)(2,1)S(1)}, f32[16,176,128]{2,1,0:T(8,128)S(1)}, f32[16,144,128]{2,1,0:T(8,128)S(1)}, f32[16,2,32,128]{3,2,1,0:T(8,128)S(1)}) custom-call(bf16[2,1,512,1024]{3,2,1,0:T(8,128)(2,1)} %refs_0_.1, f32[16,176,128]{2,1,0:T(8,128)} %constant.32.clone.refs_1_, f32[16,144,128]{2,1,0:T(8,128)} %constant.33.clone.refs_2_, ...), custom_call_target="tpu_custom_call" | custom-call | tf_op jit(solution)/shard_map/stage/pallas_call | solution.py:102
  9.1 0.0 copy-start.1
  9.1 0.0 copy-start.2
  9.1 0.0 copy-start.3
  9.2 0.0 copy-start.4
  9.2 4.3 %warp.1 = (bf16[4,128,128]{2,1,0:T(8,128)(2,1)S(1)}, bf16[4,128,128]{2,1,0:T(8,128)(2,1)S(1)}, bf16[4,128,128]{2,1,0:T(8,128)(2,1)S(1)}) custom-call(s32[4]{0:T(128)S(1)} %pad_add_fusion.refs_0_, s32[2,2,32]{2,1,0:T(2,128)S(1)} %copy-done, s32[2,2,32]{2,1,0:T(2,128)S(1)} %collective-permute-done.refs_2_, bf16[2,512,1024]{2,1,0:T(8,128)(2,1)S(1)} %bitcast.19, ...), custom_call_target="tpu_custom_call" | custom-call | flops 4294967296 | bytes 4718592 | tf_op jit(solution)/shard_map/warp/pallas_call | solution.py:220
  13.5 1.4 %collective-permute-start.6 = (bf16[4,128,128]{2,1,0:T(8,128)(2,1)S(1)}, bf16[4,128,128]{2,1,0:T(8,128)(2,1)S(1)}, u32[]{:S(2)}, u32[]{:S(2)}) collective-permute-start(bf16[4,128,128]{2,1,0:T(8,128)(2,1)S(1)} %get-tuple-element.36.refs_13_), channel_id=1, source_target_pairs={{0,8},{8,0},{16,24},{24,16},{1,9},{9,1},{17,25},{25,17},{2,10},{10... | collective-permute-start | bytes 393224 | tf_op jit(solution)/shard_map/ppermute | solution.py:430
  15.0 2.9 %collective-permute-start.7 = (bf16[4,128,128]{2,1,0:T(8,128)(2,1)S(1)}, bf16[4,128,128]{2,1,0:T(8,128)(2,1)S(1)}, u32[]{:S(2)}, u32[]{:S(2)}) collective-permute-start(bf16[4,128,128]{2,1,0:T(8,128)(2,1)S(1)} %get-tuple-element.42), channel_id=1, source_target_pairs={{0,16},{8,24},{16,0},{24,8},{1,17},{9,25},{17,1},{25,9},{2,18},{10... | collective-permute-start | bytes 393224 | tf_op jit(solution)/shard_map/ppermute | solution.py:430
  17.9 0.1 collective-permute-start.8
  18.0 1.7 %collective-permute-start.5 = (bf16[8,128,128]{2,1,0:T(8,128)(2,1)S(1)}, bf16[8,128,128]{2,1,0:T(8,128)(2,1)S(1)}, u32[]{:S(2)}, u32[]{:S(2)}) collective-permute-start(bf16[8,128,128]{2,1,0:T(8,128)(2,1)S(1)} %pad_maximum_fusion.refs_9_), channel_id=1, source_target_pairs={{0,4},{4,0},{1,5},{5,1},{2,6},{6,2},{3,7},{7,3},{8,12},{12,8},{9,1... | collective-permute-start | bytes 786440 | tf_op jit(solution)/shard_map/ppermute | solution.py:430
  19.8 4.4 %lag_windows.2 = (f32[4,256,128]{2,1,0:T(8,128)S(1)}, bf16[4,128,128]{2,1,0:T(8,128)(2,1)S(1)}) custom-call(s32[4]{0:T(128)S(1)} %pad_add_fusion.refs_0_, s32[2,2,32]{2,1,0:T(2,128)S(1)} %copy-done, s32[2,2,32]{2,1,0:T(2,128)S(1)} %collective-permute-done.refs_2_, bf16[160,128]{1,0:T(8,128)(2,1)S(1)} %copy-done.3, bf16[256,256]{1,0:T(8,128)(2,1)S(1)} %copy-done.1, ...), custom_call_target="tpu_custom_call" | custom-call | flops 3221225472 | bytes 4718592 | tf_op jit(solution)/shard_map/lag_windows/pallas_call | solution.py:409
  24.1 2.1 %collective-permute-done.5.refs_9_ = bf16[8,128,128]{2,1,0:T(8,128)(2,1)S(1)} collective-permute-done((bf16[8,128,128]{2,1,0:T(8,128)(2,1)S(1)}, bf16[8,128,128]{2,1,0:T(8,128)(2,1)S(1)}, u32[]{:S(2)}, u32[]{:S(2)}) %collective-permute-start.5) | collective-permute-done | bytes 262176 | tf_op jit(solution)/shard_map/ppermute | solution.py:430
  26.2 3.4 %lag_windows.3 = (f32[2,8,256]{2,1,0:T(8,128)S(1)}, f32[2,8,256]{2,1,0:T(8,128)S(1)}, f32[2,8,256]{2,1,0:T(8,128)S(1)}, f32[2,8,256]{2,1,0:T(8,128)S(1)}) custom-call(s32[4]{0:T(128)S(1)} %pad_add_fusion.refs_0_, s32[2,2,32]{2,1,0:T(2,128)S(1)} %copy-done, s32[2,2,32]{2,1,0:T(2,128)S(1)} %collective-permute-done.refs_2_, bf16[160,128]{1,0:T(8,128)(2,1)S(1)} %copy-done.3, ...), custom_call_target="tpu_custom_call" | custom-call | flops 3221225472 | bytes 4718592 | tf_op jit(solution)/shard_map/lag_windows/pallas_call | solution.py:409
  29.6 1.6 %collective-permute-start.9 = (f32[2,8,256]{2,1,0:T(8,128)S(1)}, f32[2,8,256]{2,1,0:T(8,128)S(1)}, u32[]{:S(2)}, u32[]{:S(2)}) collective-permute-start(f32[2,8,256]{2,1,0:T(8,128)S(1)} %get-tuple-element.45), channel_id=1, source_target_pairs={{0,1},{1,0},{2,3},{3,2},{4,5},{5,4},{6,7},{7,6},{8,9},{9,8},{10,11... | collective-permute-start | bytes 49160 | tf_op jit(solution)/shard_map/ppermute | solution.py:430
  31.2 0.6 %collective-permute-start.11 = (f32[2,8,256]{2,1,0:T(8,128)S(1)}, f32[2,8,256]{2,1,0:T(8,128)S(1)}, u32[]{:S(2)}, u32[]{:S(2)}) collective-permute-start(f32[2,8,256]{2,1,0:T(8,128)S(1)} %get-tuple-element.47), channel_id=1, source_target_pairs={{0,3},{1,2},{2,1},{3,0},{4,7},{5,6},{6,5},{7,4},{8,11},{9,10},{10,... | collective-permute-start | bytes 49160 | tf_op jit(solution)/shard_map/ppermute | solution.py:430
  31.8 1.6 %collective-permute-start.12 = (bf16[2,128,128]{2,1,0:T(8,128)(2,1)S(1)}, bf16[2,128,128]{2,1,0:T(8,128)(2,1)S(1)}, u32[]{:S(2)}, u32[]{:S(2)}) collective-permute-start(bf16[2,128,128]{2,1,0:T(8,128)(2,1)S(1)} %add_convert_fusion), channel_id=1, source_target_pairs={{0,4},{4,0},{1,5},{5,1},{2,6},{6,2},{3,7},{7,3},{8,12},{12,8},{9,1... | collective-permute-start | bytes 196616 | tf_op jit(solution)/shard_map/ppermute | solution.py:430
  33.4 0.9 %collective-permute-done.11 = f32[2,8,256]{2,1,0:T(8,128)S(1)} collective-permute-done((f32[2,8,256]{2,1,0:T(8,128)S(1)}, f32[2,8,256]{2,1,0:T(8,128)S(1)}, u32[]{:S(2)}, u32[]{:S(2)}) %collective-permute-start.11) | collective-permute-done | bytes 16416 | tf_op jit(solution)/shard_map/ppermute | solution.py:430
  34.4 0.6 %reshape.15 = f32[2,16,256]{2,1,0:T(8,128)} reshape(f32[2,4,2,2,256]{4,3,2,1,0:T(2,128)S(1)} %copy.20) | data formatting | bytes 65536 | tf_op jit(solution)/shard_map/reshape | solution.py:468
  35.0 1.1 %collective-permute-done.12 = bf16[2,128,128]{2,1,0:T(8,128)(2,1)S(1)} collective-permute-done((bf16[2,128,128]{2,1,0:T(8,128)(2,1)S(1)}, bf16[2,128,128]{2,1,0:T(8,128)(2,1)S(1)}, u32[]{:S(2)}, u32[]{:S(2)}) %collective-permute-start.12) | collective-permute-done | bytes 65568 | tf_op jit(solution)/shard_map/ppermute | solution.py:430
  36.2 0.7 %multiply_bitcast_fusion = f32[2,1,128,128]{3,2,1,0:T(8,128)} fusion(bf16[2,128,128]{2,1,0:T(8,128)(2,1)S(1)} %collective-permute-done.12, bf16[4,128,128]{2,1,0:T(8,128)(2,1)S(1)} %get-tuple-element.51, bf16[4,128,128]{2,1,0:T(8,128)(2,1)S(1)} %collective-permute-done.8, bf16[4,128,128]{2,1,0:T(8,128)(2,1)S(1)} %collective-permute-done.7, ...), kind=kLoop, calls=%fused_computation.1 | loop fusion | flops 327680 | bytes 458752
  (28 shorter events, 0.2 us)
Async XLA Ops:
  0.6 8.5 %collective-permute-start.1 = (bf16[2,1,512,1024]{3,2,0,1:T(8,128)(2,1)}, bf16[2,1,512,1024]{3,2,0,1:T(8,128)(2,1)S(1)}, u32[]{:S(2)}, u32[]{:S(2)}) collective-permute-start(bf16[2,1,512,1024]{3,2,0,1:T(8,128)(2,1)} %bitcast.22), channel_id=1, source_target_pairs={{0,2},{2,0},{1,3},{3,1},{4,6},{6,4},{5,7},{7,5},{8,10},{10,8},{9,1... | collective-permute-start | bytes 6291464 | tf_op jit(solution)/shard_map/ppermute | solution.py:430
  1.1 12.4 %collective-permute-start.4 = (bf16[2,1,128,128]{3,2,0,1:T(8,128)(2,1)}, bf16[2,1,128,128]{3,2,0,1:T(8,128)(2,1)S(1)}, u32[]{:S(2)}, u32[]{:S(2)}) collective-permute-start(bf16[2,1,128,128]{3,2,0,1:T(8,128)(2,1)} %bitcast.23), channel_id=1, source_target_pairs={{0,24},{8,16},{16,8},{24,0},{1,25},{9,17},{17,9},{25,1},{2,26},{10... | collective-permute-start | bytes 196616 | tf_op jit(solution)/shard_map/ppermute | solution.py:430
  5.8 7.7 %collective-permute-start.3 = (bf16[2,1,128,128]{3,2,0,1:T(8,128)(2,1)}, bf16[2,1,128,128]{3,2,0,1:T(8,128)(2,1)S(1)}, u32[]{:S(2)}, u32[]{:S(2)}) collective-permute-start(bf16[2,1,128,128]{3,2,0,1:T(8,128)(2,1)} %bitcast.24), channel_id=1, source_target_pairs={{0,16},{8,24},{16,0},{24,8},{1,17},{9,25},{17,1},{25,9},{2,18},{10... | collective-permute-start | bytes 196616 | tf_op jit(solution)/shard_map/ppermute | solution.py:430
  5.8 7.7 %collective-permute-start.2 = (bf16[2,1,128,128]{3,2,0,1:T(8,128)(2,1)}, bf16[2,1,128,128]{3,2,0,1:T(8,128)(2,1)S(1)}, u32[]{:S(2)}, u32[]{:S(2)}) collective-permute-start(bf16[2,1,128,128]{3,2,0,1:T(8,128)(2,1)} %bitcast.25), channel_id=1, source_target_pairs={{0,8},{8,0},{16,24},{24,16},{1,9},{9,1},{17,25},{25,17},{2,10},{10... | collective-permute-start | bytes 196616 | tf_op jit(solution)/shard_map/ppermute | solution.py:430
  6.5 2.6 %collective-permute-start = (s32[2,2,32]{2,1,0:T(2,128)}, s32[2,2,32]{2,1,0:T(2,128)S(1)}, u32[]{:S(2)}, u32[]{:S(2)}) collective-permute-start(s32[2,2,32]{2,1,0:T(2,128)} %refs_1_.6), channel_id=1, source_target_pairs={{0,2},{2,0},{1,3},{3,1},{4,6},{6,4},{5,7},{7,5},{8,10},{10,8},{9,1... | collective-permute-start | bytes 1544 | tf_op jit(solution)/shard_map/ppermute | solution.py:430
  6.5 2.5 %copy-start = (s32[2,2,32]{2,1,0:T(2,128)S(1)}, s32[2,2,32]{2,1,0:T(2,128)}, u32[]{:S(2)}) copy-start(s32[2,2,32]{2,1,0:T(2,128)} %refs_1_.6) | copy-start | bytes 1540
  9.1 8.9 %copy-start.5 = (bf16[2,1,128,128]{3,2,1,0:T(8,128)(2,1)S(1)}, bf16[2,1,128,128]{3,2,1,0:T(8,128)(2,1)}, u32[]{:S(2)}) copy-start(bf16[2,1,128,128]{3,2,1,0:T(8,128)(2,1)} %refs_4_.3) | copy-start | bytes 196612
  9.1 10.6 %copy-start.1 = (bf16[256,256]{1,0:T(8,128)(2,1)S(1)}, bf16[256,256]{1,0:T(8,128)(2,1)}, u32[]{:S(2)}) copy-start(bf16[256,256]{1,0:T(8,128)(2,1)} %constant.36.clone.refs_4_) | copy-start | bytes 393220
  9.1 10.6 %copy-start.2 = (bf16[256,128]{1,0:T(8,128)(2,1)S(1)}, bf16[256,128]{1,0:T(8,128)(2,1)}, u32[]{:S(2)}) copy-start(bf16[256,128]{1,0:T(8,128)(2,1)} %constant.38.clone.refs_6_) | copy-start | bytes 196612
  9.1 10.6 %copy-start.3 = (bf16[160,128]{1,0:T(8,128)(2,1)S(1)}, bf16[160,128]{1,0:T(8,128)(2,1)}, u32[]{:S(2)}) copy-start(bf16[160,128]{1,0:T(8,128)(2,1)} %constant.35.clone.refs_3_) | copy-start | bytes 122884
  9.2 10.6 %copy-start.4 = (bf16[64,160]{1,0:T(8,128)(2,1)S(1)}, bf16[64,160]{1,0:T(8,128)(2,1)}, u32[]{:S(2)}) copy-start(bf16[64,160]{1,0:T(8,128)(2,1)} %constant.37.clone.refs_5_) | copy-start | bytes 61444
  13.5 16.0 %collective-permute-start.6 = (bf16[4,128,128]{2,1,0:T(8,128)(2,1)S(1)}, bf16[4,128,128]{2,1,0:T(8,128)(2,1)S(1)}, u32[]{:S(2)}, u32[]{:S(2)}) collective-permute-start(bf16[4,128,128]{2,1,0:T(8,128)(2,1)S(1)} %get-tuple-element.36.refs_13_), channel_id=1, source_target_pairs={{0,8},{8,0},{16,24},{24,16},{1,9},{9,1},{17,25},{25,17},{2,10},{10... | collective-permute-start | bytes 393224 | tf_op jit(solution)/shard_map/ppermute | solution.py:430
  15.0 14.6 %collective-permute-start.7 = (bf16[4,128,128]{2,1,0:T(8,128)(2,1)S(1)}, bf16[4,128,128]{2,1,0:T(8,128)(2,1)S(1)}, u32[]{:S(2)}, u32[]{:S(2)}) collective-permute-start(bf16[4,128,128]{2,1,0:T(8,128)(2,1)S(1)} %get-tuple-element.42), channel_id=1, source_target_pairs={{0,16},{8,24},{16,0},{24,8},{1,17},{9,25},{17,1},{25,9},{2,18},{10... | collective-permute-start | bytes 393224 | tf_op jit(solution)/shard_map/ppermute | solution.py:430
  17.9 11.7 %collective-permute-start.8 = (bf16[4,128,128]{2,1,0:T(8,128)(2,1)S(1)}, bf16[4,128,128]{2,1,0:T(8,128)(2,1)S(1)}, u32[]{:S(2)}, u32[]{:S(2)}) collective-permute-start(bf16[4,128,128]{2,1,0:T(8,128)(2,1)S(1)} %get-tuple-element.43), channel_id=1, source_target_pairs={{0,24},{8,16},{16,8},{24,0},{1,25},{9,17},{17,9},{25,1},{2,26},{10... | collective-permute-start | bytes 393224 | tf_op jit(solution)/shard_map/ppermute | solution.py:430
  18.0 8.1 %collective-permute-start.5 = (bf16[8,128,128]{2,1,0:T(8,128)(2,1)S(1)}, bf16[8,128,128]{2,1,0:T(8,128)(2,1)S(1)}, u32[]{:S(2)}, u32[]{:S(2)}) collective-permute-start(bf16[8,128,128]{2,1,0:T(8,128)(2,1)S(1)} %pad_maximum_fusion.refs_9_), channel_id=1, source_target_pairs={{0,4},{4,0},{1,5},{5,1},{2,6},{6,2},{3,7},{7,3},{8,12},{12,8},{9,1... | collective-permute-start | bytes 786440 | tf_op jit(solution)/shard_map/ppermute | solution.py:430
  29.6 3.8 %collective-permute-start.9 = (f32[2,8,256]{2,1,0:T(8,128)S(1)}, f32[2,8,256]{2,1,0:T(8,128)S(1)}, u32[]{:S(2)}, u32[]{:S(2)}) collective-permute-start(f32[2,8,256]{2,1,0:T(8,128)S(1)} %get-tuple-element.45), channel_id=1, source_target_pairs={{0,1},{1,0},{2,3},{3,2},{4,5},{5,4},{6,7},{7,6},{8,9},{9,8},{10,11... | collective-permute-start | bytes 49160 | tf_op jit(solution)/shard_map/ppermute | solution.py:430
  31.1 2.3 %collective-permute-start.10 = (f32[2,8,256]{2,1,0:T(8,128)S(1)}, f32[2,8,256]{2,1,0:T(8,128)S(1)}, u32[]{:S(2)}, u32[]{:S(2)}) collective-permute-start(f32[2,8,256]{2,1,0:T(8,128)S(1)} %get-tuple-element.46), channel_id=1, source_target_pairs={{0,2},{1,3},{2,0},{3,1},{4,6},{5,7},{6,4},{7,5},{8,10},{9,11},{10,... | collective-permute-start | bytes 49160 | tf_op jit(solution)/shard_map/ppermute | solution.py:430
  31.2 3.2 %collective-permute-start.11 = (f32[2,8,256]{2,1,0:T(8,128)S(1)}, f32[2,8,256]{2,1,0:T(8,128)S(1)}, u32[]{:S(2)}, u32[]{:S(2)}) collective-permute-start(f32[2,8,256]{2,1,0:T(8,128)S(1)} %get-tuple-element.47), channel_id=1, source_target_pairs={{0,3},{1,2},{2,1},{3,0},{4,7},{5,6},{6,5},{7,4},{8,11},{9,10},{10,... | collective-permute-start | bytes 49160 | tf_op jit(solution)/shard_map/ppermute | solution.py:430
  31.8 4.3 %collective-permute-start.12 = (bf16[2,128,128]{2,1,0:T(8,128)(2,1)S(1)}, bf16[2,128,128]{2,1,0:T(8,128)(2,1)S(1)}, u32[]{:S(2)}, u32[]{:S(2)}) collective-permute-start(bf16[2,128,128]{2,1,0:T(8,128)(2,1)S(1)} %add_convert_fusion), channel_id=1, source_target_pairs={{0,4},{4,0},{1,5},{5,1},{2,6},{6,2},{3,7},{7,3},{8,12},{12,8},{9,1... | collective-permute-start | bytes 196616 | tf_op jit(solution)/shard_map/ppermute | solution.py:430

commit v10 on v9

--- a/solution.py
+++ b/solution.py
@@ -192,23 +192,14 @@
 def warp_kernel(down, across, block, own, depth, *refs):
     place_ref, *code_refs = refs[:3]
     frame_refs, band_refs = refs[3:5], refs[5:8]
-    out_refs, sums = refs[8 : 7 + depth], refs[7 + depth]
-
-    def one_step(step, _):
+    out_refs = refs[8:]
+
+    for at, out_ref in enumerate(out_refs):
         totals = warp_step(
-            place_ref, step, code_refs, frame_refs, band_refs, down, across, block, own
+            place_ref, at + 1, code_refs, frame_refs, band_refs, down, across, block, own
         )
         for count, total in enumerate(totals):
-            sums[count] = total
-        for at, out_ref in enumerate(out_refs):
-
-            @pl.when(step == at + 1)
-            def _():
-                out_ref[...] = sums[...]
-
-        return 0
-
-    lax.fori_loop(1, depth, one_step, 0)
+            out_ref[count] = total
 
 
 def warp_sums(place, codes, other_codes, frames, other_frames, bands, depth, block, own):
@@ -222,7 +213,6 @@
         out_shape=[jax.ShapeDtypeStruct(out, jnp.bfloat16)] * (depth - 1),
         in_specs=[smem] * 3 + [vmem] * 5,
         out_specs=[vmem] * (depth - 1),
-        scratch_shapes=[pltpu.VMEM(out, jnp.bfloat16)],
         compiler_params=pltpu.CompilerParams(vmem_limit_bytes=VMEM_LIMIT),
         cost_estimate=pl.CostEstimate(
             flops=2 * vols * rows * cols * block * 16,
@@ -236,7 +226,7 @@
 def spectrum_kernel(vols, down, across, block, own, planes, depth, other, *refs):
     place_ref, codes_ref, other_codes_ref, row_ref, col_ref, lag_ref, span_ref = refs[:7]
     frames_ref, other_frames_ref, template_ref = refs[7:10]
-    cross, sums = refs[-2:]
+    all_cross, all_sums = refs[-2:]
     if other:
         found_ref, out_refs, found = refs[10], refs[11:-3], refs[-3]
         found[...] = found_ref[...]
@@ -248,6 +238,7 @@
         )
         for count, total in enumerate(totals):
             sums_ref[count] = total
+        found[...] = jnp.zeros(found.shape, jnp.float32)
 
     row_table = row_ref[...]
     col_table = col_ref[...]
@@ -262,7 +253,8 @@
     local = 2 * own
     no_rows = jnp.zeros((half - kept, LANES), jnp.float32)
 
-    def two_steps(half_step, _):
+    for half_step in range(depth // 2):
+        cross, sums = all_cross.at[half_step], all_sums.at[half_step]
         places = []
         for step in (2 * half_step, 2 * half_step + 1):
             band = step_band(place_ref, step, across, own)
@@ -356,23 +348,20 @@
                     at = (pair * many + order) * 2 + side
                     one = lags[at * span : (at + 1) * span]
                     one = pltpu.roll(one, span - SHIFT - row_shift, 0)[:WIN]
-                    place = index // (2 * own) * own + (2 * pair + side) % own
-                    found[order, pl.ds(pl.multiple_of(place * WIN, WIN), WIN), :] = pltpu.roll(
+                    found[order, pl.ds(pl.multiple_of(index * WIN, WIN), WIN), :] = pltpu.roll(
                         one, LANES - SHIFT - col_shift, 1
                     )
-        return 0
-
-    lax.fori_loop(0, depth // 2, two_steps, 0)
+
     if not other:
         return
 
-    share = depth * local // planes
+    keep_refs, give_ref = out_refs[:-1], out_refs[-1]
+    share = found.shape[1] // WIN // planes
     per_tile = LANES // WIN
     lane = lax.broadcasted_iota(jnp.int32, (share, LANES), 1) // WIN
-    for turn, out_ref in enumerate(out_refs):
-        plane = place_ref[3] ^ (turn % planes)
-        for v in range(vols):
-            order = turn // planes * vols + v
+    for turn, keep_ref in enumerate(keep_refs):
+        plane = place_ref[3] ^ turn
+        for order in range(many):
             for tile in range(WIN // per_tile):
                 total = jnp.zeros((share, LANES), jnp.float32)
                 for part in range(per_tile):
@@ -381,7 +370,12 @@
                     if part:
                         one = pltpu.roll(one, part * WIN, 1)
                     total = jnp.where(lane == part, one, total)
-                out_ref[v, :, tile * LANES : (tile + 1) * LANES] = total * (1.0 / block)
+                lanes = slice(tile * LANES, (tile + 1) * LANES)
+                total = total * (1.0 / block)
+                if order < vols:
+                    keep_ref[order, :, lanes] = total
+                else:
+                    give_ref[turn, order - vols, :, lanes] = total
 
 
 def lag_windows(
@@ -394,12 +388,13 @@
     kept = -(-(block // 2 + 1) // 8) * 8
     smem = pl.BlockSpec(memory_space=pltpu.SMEM)
     vmem = pl.BlockSpec(memory_space=pltpu.VMEM)
-    local = depth * 2 * own
+    blocks = down * across
     many = 2 * vols * 2 * own
-    found = jax.ShapeDtypeStruct((2 * vols, local * WIN, LANES), jnp.float32)
+    found = jax.ShapeDtypeStruct((2 * vols, blocks * WIN, LANES), jnp.float32)
     if other:
-        out = (vols, local // planes, WIN * WIN)
-        out_shape = [jax.ShapeDtypeStruct(out, jnp.float32)] * (2 * planes)
+        out = (vols, blocks // planes, WIN * WIN)
+        out_shape = [jax.ShapeDtypeStruct(out, jnp.float32)] * planes
+        out_shape.append(jax.ShapeDtypeStruct((planes, *out), jnp.float32))
         scratch_shapes = [pltpu.VMEM(found.shape, found.dtype)]
         bands, last = [], vmem
     else:
@@ -413,8 +408,8 @@
         out_specs=[vmem] * len(out_shape),
         scratch_shapes=scratch_shapes
         + [
-            pltpu.VMEM((many, 3 * kept, LANES), jnp.float32),
-            pltpu.VMEM((many, 1, LANES), jnp.float32),
+            pltpu.VMEM((depth // 2, many, 3 * kept, LANES), jnp.float32),
+            pltpu.VMEM((depth // 2, many, 1, LANES), jnp.float32),
         ],
         compiler_params=pltpu.CompilerParams(vmem_limit_bytes=VMEM_LIMIT),
         cost_estimate=pl.CostEstimate(
@@ -435,13 +430,13 @@
     own, block = template.shape[0], template.shape[-1]
     depth = lax.axis_size("z")
     planes = lax.axis_size("plane")
-    share = 4 * depth * own // planes
     place = jnp.stack([lax.axis_index(axis) for axis in ("z", "y", "core", "plane")])
     other_codes = exchange(shift_codes, "core", 2, 1)
     other_frames = exchange(frames, "core", 2, 1)
-    pieces = [template] + [exchange(template, "z", depth, turn) for turn in range(1, depth)]
     staged, *bands = stage([frames, *tap_constants(block)], template)
-    averages, window = [], [0.0, 0.0]
+    later, staged = lax.optimization_barrier((template, staged))
+    pieces = [template] + [exchange(later, "z", depth, turn) for turn in range(1, depth)]
+    averages, correlation = [], 0.0
     volumes = vol_dev * depth * 4
     for p in range(pl_dev):
         work = (place, shift_codes, other_codes, staged[:, p], other_frames[:, p])
@@ -458,14 +453,10 @@
         sums = [sum(one[at : at + own].astype(jnp.float32) for one in warped) for at in (0, own)]
         taken = exchange(sums[1].astype(jnp.bfloat16), "y", 2, 1)
         averages.append((sums[0] + taken.astype(jnp.float32)) * (1.0 / volumes))
-        for turn, one in enumerate(found):
-            if turn:
-                one = exchange(one, ("core", "plane"), 2 * planes, turn)
-            window[turn // planes] += one
-    core = place[2]
-    window = [jnp.where(core == 0, *window), jnp.where(core == 0, *window[::-1])]
-    window = [one.reshape(vol_dev, share // (2 * own), 1, own, WIN * WIN) for one in window]
-    correlation = jnp.concatenate(window, axis=2).reshape(vol_dev, share, WIN * WIN)
+        got = exchange(found[-1], "core", 2, 1)
+        for turn, one in enumerate(found[:-1]):
+            one = one + got[turn]
+            correlation += exchange(one, "plane", planes, turn) if turn else one
     return (correlation, jnp.stack(averages, axis=1))
 
 

time: 37 us -> 44.2 us (1.19)
  local copies, waits for them, and re-layouts: 0.71 us -> 7.08 us
  other arithmetic: 0.88 us -> 2.42 us
  Pallas kernels: 14.6 us -> 13.6 us
  waiting for transfers between devices: 4.13 us -> 4.89 us
  starting transfers between devices: 15.8 us -> 15.2 us
    unnamed x12 -> x22, local copies, waits for them, and re-layouts: 0.04 us -> 7.08 us
    concatenate x1, other arithmetic: 0.04 us -> 0.97 us  [on_device(): near = jnp.concatenate([piece[:, p] for piece in pieces], axis=0)]
    ppermute x13 -> x12, waiting for transfers between devices: 4.13 us -> 4.89 us  [exchange(): return lax.ppermute(value, axes, [(at, at ^ turn) for at in range(size)])]
    reshape x3 -> x0, local copies, waits for them, and re-layouts: 0.67 us -> none  [the longest x1 0.64 us: on_device(): jnp.concatenate(window, axis=2).reshape(vol_dev, share, WIN * WIN)]
    add x0 -> x2, other arithmetic: none -> 0.63 us  [the longest x1 0.62 us: on_device(): correlation += exchange(one, 'plane', planes, turn) if turn else one]
    ppermute x13 -> x12, starting transfers between devices: 15.8 us -> 15.2 us  [exchange(): return lax.ppermute(value, axes, [(at, at ^ turn) for at in range(size)])]
    pallas_call x2, Pallas kernels: 7.74 us -> 7.17 us  [lag_windows(): pl.pallas_call(functools.partial(spectrum_kernel, vols, down, across, blo...]
  transfers between devices with their start and end apart: 13 -> 12, of which waited for: 3 -> 4; matrix products, arithmetic and copies ran while one was open for 2% -> 4% of each run, Pallas kernels for 40% -> 31%
where the time goes in v10:
time: 44.2 us; the launch traced here: 43.9 us
  starting transfers between devices  15.2 us (34%)
  Pallas kernels  13.6 us (31%)
  local copies, waits for them, and re-layouts  7.08 us (16%)
  waiting for transfers between devices  4.89 us (11%)
  other arithmetic  2.42 us (5%)
  between operations  0.76 us (2%)
    ppermute x12, starting transfers between devices, exchange(): return lax.ppermute(value, axes, [(at, at ^ turn) for at in range(size)])  15.2 us
    pallas_call x2, Pallas kernels, lag_windows(): pl.pallas_call(functools.partial(spectrum_kernel, vols, down, across, blo...  7.17 us
    unnamed x22, local copies, waits for them, and re-layouts  7.08 us
    ppermute x12, waiting for transfers between devices, exchange(): return lax.ppermute(value, axes, [(at, at ^ turn) for at in range(size)])  4.89 us
    pallas_call x1, Pallas kernels, warp_sums(): pl.pallas_call(functools.partial(warp_kernel, down, across, block, own, d...  3.89 us
    pallas_call x1, Pallas kernels, stage(): pl.pallas_call(functools.partial(stage_kernel, count), out_shape=[jax.Sha...  2.49 us
    concatenate x1, other arithmetic, on_device(): near = jnp.concatenate([piece[:, p] for piece in pieces], axis=0)  0.97 us
  transfers between devices with their start and end apart: 12, of which 4 were waited for; matrix products, arithmetic and copies ran while one was open for 4% of the time, Pallas kernels for 31%

profile of v10, /device:TPU:0, one launch (start us, length us, event | category | flops | bytes accessed | tf_op | source)
XLA Modules:
  0.0 43.9 jit_solution(11313448879134727682)
XLA Ops:
  0.6 0.5 %collective-permute-start.1 = (bf16[2,1,512,1024]{3,2,0,1:T(8,128)(2,1)}, bf16[2,1,512,1024]{3,2,0,1:T(8,128)(2,1)S(1)}, u32[]{:S(2)}, u32[]{:S(2)}) collective-permute-start(bf16[2,1,512,1024]{3,2,0,1:T(8,128)(2,1)} %bitcast.32), channel_id=1, source_target_pairs={{0,2},{2,0},{1,3},{3,1},{4,6},{6,4},{5,7},{7,5},{8,10},{10,8},{9,1... | collective-permute-start | bytes 6291464 | tf_op jit(solution)/shard_map/ppermute | solution.py:425
  1.2 2.5 %stage.1 = (bf16[2,1,512,1024]{3,2,1,0:T(8,128)(2,1)S(1)}, f32[16,176,128]{2,1,0:T(8,128)S(1)}, f32[16,144,128]{2,1,0:T(8,128)S(1)}, f32[16,2,32,128]{3,2,1,0:T(8,128)S(1)}) custom-call(bf16[2,1,512,1024]{3,2,1,0:T(8,128)(2,1)} %refs_0_.1, f32[16,176,128]{2,1,0:T(8,128)} %constant.30.clone.refs_1_, f32[16,144,128]{2,1,0:T(8,128)} %constant.31.clone.refs_2_, ...), custom_call_target="tpu_custom_call" | custom-call | tf_op jit(solution)/shard_map/stage/pallas_call | solution.py:102
  3.7 1.3 %copy-done = bf16[2,1,512,1024]{3,2,1,0:T(8,128)(2,1)} copy-done((bf16[2,1,512,1024]{3,2,1,0:T(8,128)(2,1)}, bf16[2,1,512,1024]{3,2,1,0:T(8,128)(2,1)S(1)}, u32[]{:S(2)}) %copy-start) | copy-done | bytes 2097176
  5.0 1.0 %copy-done.2 = f32[16,144,128]{2,1,0:T(8,128)} copy-done((f32[16,144,128]{2,1,0:T(8,128)}, f32[16,144,128]{2,1,0:T(8,128)S(1)}, u32[]{:S(2)}) %copy-start.2) | copy-done | bytes 1179672
  6.0 0.8 %copy-done.4 = f32[16,2,32,128]{3,2,1,0:T(8,128)} copy-done((f32[16,2,32,128]{3,2,1,0:T(8,128)}, f32[16,2,32,128]{3,2,1,0:T(8,128)S(1)}, u32[]{:S(2)}) %copy-start.4) | copy-done | bytes 524312
  6.8 4.6 %collective-permute-start.4 = (bf16[2,1,128,128]{3,2,0,1:T(8,128)(2,1)}, bf16[2,1,128,128]{3,2,0,1:T(8,128)(2,1)}, u32[]{:S(2)}, u32[]{:S(2)}) collective-permute-start(bf16[2,1,128,128]{3,2,0,1:T(8,128)(2,1)} %bitcast.7), channel_id=1, source_target_pairs={{0,24},{8,16},{16,8},{24,0},{1,25},{9,17},{17,9},{25,1},{2,26},{10... | collective-permute-start | bytes 196616 | tf_op jit(solution)/shard_map/ppermute | solution.py:425
  11.4 0.6 %collective-permute-start.2 = (bf16[2,1,128,128]{3,2,0,1:T(8,128)(2,1)}, bf16[2,1,128,128]{3,2,0,1:T(8,128)(2,1)}, u32[]{:S(2)}, u32[]{:S(2)}) collective-permute-start(bf16[2,1,128,128]{3,2,0,1:T(8,128)(2,1)} %bitcast.7), channel_id=1, source_target_pairs={{0,8},{8,0},{16,24},{24,16},{1,9},{9,1},{17,25},{25,17},{2,10},{10... | collective-permute-start | bytes 196616 | tf_op jit(solution)/shard_map/ppermute | solution.py:425
  12.1 1.1 %collective-permute-done.refs_2_ = s32[2,2,32]{2,1,0:T(2,128)S(1)} collective-permute-done((s32[2,2,32]{2,1,0:T(2,128)S(1)}, s32[2,2,32]{2,1,0:T(2,128)S(1)}, u32[]{:S(2)}, u32[]{:S(2)}) %collective-permute-start) | collective-permute-done | bytes 544 | tf_op jit(solution)/shard_map/ppermute | solution.py:425
  13.2 1.6 %copy-done.1 = bf16[2,1,512,1024]{3,2,1,0:T(8,128)(2,1)S(1)} copy-done((bf16[2,1,512,1024]{3,2,1,0:T(8,128)(2,1)S(1)}, bf16[2,1,512,1024]{3,2,1,0:T(8,128)(2,1)}, u32[]{:S(2)}) %copy-start.1) | copy-done | bytes 2097176
  14.8 1.3 %copy-done.3 = f32[16,144,128]{2,1,0:T(8,128)S(1)} copy-done((f32[16,144,128]{2,1,0:T(8,128)S(1)}, f32[16,144,128]{2,1,0:T(8,128)}, u32[]{:S(2)}) %copy-start.3) | copy-done | bytes 1179672
  16.0 1.0 %copy-done.5 = f32[16,2,32,128]{3,2,1,0:T(8,128)S(1)} copy-done((f32[16,2,32,128]{3,2,1,0:T(8,128)S(1)}, f32[16,2,32,128]{3,2,1,0:T(8,128)}, u32[]{:S(2)}) %copy-start.5) | copy-done | bytes 524312
  17.1 3.9 %warp.1 = (bf16[4,128,128]{2,1,0:T(8,128)(2,1)S(1)}, bf16[4,128,128]{2,1,0:T(8,128)(2,1)S(1)}, bf16[4,128,128]{2,1,0:T(8,128)(2,1)S(1)}) custom-call(s32[4]{0:T(128)S(1)} %pad_add_fusion.refs_0_, s32[2,2,32]{2,1,0:T(2,128)S(1)} %copy-done.6, s32[2,2,32]{2,1,0:T(2,128)S(1)} %collective-permute-done.refs_2_, bf16[2,512,1024]{2,1,0:T(8,128)(2,1)S(1)} %bitcast.29, ...), custom_call_target="tpu_custom_call" | custom-call | flops 4294967296 | bytes 4718592 | tf_op jit(solution)/shard_map/warp/pallas_call | solution.py:211
  21.0 1.5 %collective-permute-start.6 = (bf16[4,128,128]{2,1,0:T(8,128)(2,1)S(1)}, bf16[4,128,128]{2,1,0:T(8,128)(2,1)S(1)}, u32[]{:S(2)}, u32[]{:S(2)}) collective-permute-start(bf16[4,128,128]{2,1,0:T(8,128)(2,1)S(1)} %get-tuple-element.38.refs_13_), channel_id=1, source_target_pairs={{0,8},{8,0},{16,24},{24,16},{1,9},{9,1},{17,25},{25,17},{2,10},{10... | collective-permute-start | bytes 393224 | tf_op jit(solution)/shard_map/ppermute | solution.py:425
  22.5 2.9 %collective-permute-start.7 = (bf16[4,128,128]{2,1,0:T(8,128)(2,1)S(1)}, bf16[4,128,128]{2,1,0:T(8,128)(2,1)S(1)}, u32[]{:S(2)}, u32[]{:S(2)}) collective-permute-start(bf16[4,128,128]{2,1,0:T(8,128)(2,1)S(1)} %get-tuple-element.43), channel_id=1, source_target_pairs={{0,16},{8,24},{16,0},{24,8},{1,17},{9,25},{17,1},{25,9},{2,18},{10... | collective-permute-start | bytes 393224 | tf_op jit(solution)/shard_map/ppermute | solution.py:425
  25.5 1.0 %pad_maximum_fusion.refs_9_ = bf16[8,128,128]{2,1,0:T(8,128)(2,1)S(1)} fusion(bf16[2,128,128]{2,1,0:T(8,128)(2,1)} %bitcast.11, bf16[2,128,128]{2,1,0:T(8,128)(2,1)} %bitcast.10, bf16[2,128,128]{2,1,0:T(8,128)(2,1)} %bitcast.9, bf16[2,128,128]{2,1,0:T(8,128)(2,1)} %bitcast.8), kind=kLoop, calls=%fused_computation | loop fusion | flops 393216 | bytes 524288 | tf_op jit(solution)/shard_map/concatenate | solution.py:445
  26.4 1.8 %collective-permute-start.5 = (bf16[8,128,128]{2,1,0:T(8,128)(2,1)S(1)}, bf16[8,128,128]{2,1,0:T(8,128)(2,1)S(1)}, u32[]{:S(2)}, u32[]{:S(2)}) collective-permute-start(bf16[8,128,128]{2,1,0:T(8,128)(2,1)S(1)} %pad_maximum_fusion.refs_9_), channel_id=1, source_target_pairs={{0,4},{4,0},{1,5},{5,1},{2,6},{6,2},{3,7},{7,3},{8,12},{12,8},{9,1... | collective-permute-start | bytes 786440 | tf_op jit(solution)/shard_map/ppermute | solution.py:425
  28.3 4.0 %lag_windows.2 = (f32[4,512,128]{2,1,0:T(8,128)S(1)}, bf16[4,128,128]{2,1,0:T(8,128)(2,1)S(1)}) custom-call(s32[4]{0:T(128)S(1)} %pad_add_fusion.refs_0_, s32[2,2,32]{2,1,0:T(2,128)S(1)} %copy-done.6, s32[2,2,32]{2,1,0:T(2,128)S(1)} %collective-permute-done.refs_2_, bf16[160,128]{1,0:T(8,128)(2,1)S(1)} %copy-done.9, bf16[256,256]{1,0:T(8,128)(2,1)S(1)} %copy-done.7, ...), custom_call_target="tpu_custom_call" | custom-call | flops 3221225472 | bytes 4718592 | tf_op jit(solution)/shard_map/lag_windows/pallas_call | solution.py:404
  32.2 2.1 %collective-permute-done.5.refs_9_ = bf16[8,128,128]{2,1,0:T(8,128)(2,1)S(1)} collective-permute-done((bf16[8,128,128]{2,1,0:T(8,128)(2,1)S(1)}, bf16[8,128,128]{2,1,0:T(8,128)(2,1)S(1)}, u32[]{:S(2)}, u32[]{:S(2)}) %collective-permute-start.5) | collective-permute-done | bytes 262176 | tf_op jit(solution)/shard_map/ppermute | solution.py:425
  34.3 3.2 %lag_windows.3 = (f32[2,16,256]{2,1,0:T(8,128)S(1)}, f32[2,16,256]{2,1,0:T(8,128)S(1)}, f32[2,2,16,256]{3,2,1,0:T(8,128)S(1)}) custom-call(s32[4]{0:T(128)S(1)} %pad_add_fusion.refs_0_, s32[2,2,32]{2,1,0:T(2,128)S(1)} %copy-done.6, s32[2,2,32]{2,1,0:T(2,128)S(1)} %collective-permute-done.refs_2_, bf16[160,128]{1,0:T(8,128)(2,1)S(1)} %copy-done.9, ...), custom_call_target="tpu_custom_call" | custom-call | flops 3221225472 | bytes 4718592 | tf_op jit(solution)/shard_map/lag_windows/pallas_call | solution.py:404
  37.7 1.6 %collective-permute-start.11 = (bf16[2,128,128]{2,1,0:T(8,128)(2,1)S(1)}, bf16[2,128,128]{2,1,0:T(8,128)(2,1)S(1)}, u32[]{:S(2)}, u32[]{:S(2)}) collective-permute-start(bf16[2,128,128]{2,1,0:T(8,128)(2,1)S(1)} %add_convert_fusion), channel_id=1, source_target_pairs={{0,4},{4,0},{1,5},{5,1},{2,6},{6,2},{3,7},{7,3},{8,12},{12,8},{9,1... | collective-permute-start | bytes 196616 | tf_op jit(solution)/shard_map/ppermute | solution.py:425
  39.3 1.6 %collective-permute-start.10 = (f32[2,16,256]{2,1,0:T(8,128)S(1)}, f32[2,16,256]{2,1,0:T(8,128)S(1)}, u32[]{:S(2)}, u32[]{:S(2)}) collective-permute-start(f32[2,16,256]{2,1,0:T(8,128)S(1)} %fusion), channel_id=1, source_target_pairs={{0,1},{1,0},{2,3},{3,2},{4,5},{5,4},{6,7},{7,6},{8,9},{9,8},{10,11... | collective-permute-start | bytes 98312 | tf_op jit(solution)/shard_map/ppermute | solution.py:425
  40.8 1.4 %collective-permute-done.11 = bf16[2,128,128]{2,1,0:T(8,128)(2,1)S(1)} collective-permute-done((bf16[2,128,128]{2,1,0:T(8,128)(2,1)S(1)}, bf16[2,128,128]{2,1,0:T(8,128)(2,1)S(1)}, u32[]{:S(2)}, u32[]{:S(2)}) %collective-permute-start.11) | collective-permute-done | bytes 65568 | tf_op jit(solution)/shard_map/ppermute | solution.py:425
  42.2 0.7 %multiply_bitcast_fusion = f32[2,1,128,128]{3,2,1,0:T(8,128)} fusion(bf16[2,128,128]{2,1,0:T(8,128)(2,1)S(1)} %collective-permute-done.11, bf16[4,128,128]{2,1,0:T(8,128)(2,1)S(1)} %get-tuple-element.51, bf16[4,128,128]{2,1,0:T(8,128)(2,1)S(1)} %collective-permute-done.8, bf16[4,128,128]{2,1,0:T(8,128)(2,1)S(1)} %collective-permute-done.7, ...), kind=kLoop, calls=%fused_computation.1 | loop fusion | flops 327680 | bytes 458752
  43.3 0.6 %fusion.2 = f32[2,16,256]{2,1,0:T(8,128)} fusion(f32[2,16,256]{2,1,0:T(8,128)S(1)} %collective-permute-done.10, f32[2,16,256]{2,1,0:T(8,128)S(1)} %get-tuple-element.45, f32[2,2,16,256]{3,2,1,0:T(8,128)S(1)} %collective-permute-done.9), kind=kLoop, calls=%fused_computation.7 | loop fusion | flops 16384 | bytes 131072 | tf_op jit(solution)/shard_map/add | solution.py:459
  (32 shorter events, 0.6 us)
Async XLA Ops:
  0.6 11.4 %copy-start.6 = (s32[2,2,32]{2,1,0:T(2,128)S(1)}, s32[2,2,32]{2,1,0:T(2,128)}, u32[]{:S(2)}) copy-start(s32[2,2,32]{2,1,0:T(2,128)} %refs_1_.6) | copy-start | bytes 1540
  0.6 12.5 %collective-permute-start.1 = (bf16[2,1,512,1024]{3,2,0,1:T(8,128)(2,1)}, bf16[2,1,512,1024]{3,2,0,1:T(8,128)(2,1)S(1)}, u32[]{:S(2)}, u32[]{:S(2)}) collective-permute-start(bf16[2,1,512,1024]{3,2,0,1:T(8,128)(2,1)} %bitcast.32), channel_id=1, source_target_pairs={{0,2},{2,0},{1,3},{3,1},{4,6},{6,4},{5,7},{7,5},{8,10},{10,8},{9,1... | collective-permute-start | bytes 6291464 | tf_op jit(solution)/shard_map/ppermute | solution.py:425
  3.7 1.3 %copy-start = (bf16[2,1,512,1024]{3,2,1,0:T(8,128)(2,1)}, bf16[2,1,512,1024]{3,2,1,0:T(8,128)(2,1)S(1)}, u32[]{:S(2)}) copy-start(bf16[2,1,512,1024]{3,2,1,0:T(8,128)(2,1)S(1)} %get-tuple-element.28) | copy-start | bytes 6291460
  5.0 1.0 %copy-start.2 = (f32[16,144,128]{2,1,0:T(8,128)}, f32[16,144,128]{2,1,0:T(8,128)S(1)}, u32[]{:S(2)}) copy-start(f32[16,144,128]{2,1,0:T(8,128)S(1)} %get-tuple-element.31.refs_6_.refs_11_) | copy-start | bytes 3538948
  6.0 0.8 %copy-start.4 = (f32[16,2,32,128]{3,2,1,0:T(8,128)}, f32[16,2,32,128]{3,2,1,0:T(8,128)S(1)}, u32[]{:S(2)}) copy-start(f32[16,2,32,128]{3,2,1,0:T(8,128)S(1)} %get-tuple-element.32.refs_7_.refs_12_) | copy-start | bytes 1572868
  6.8 14.2 %collective-permute-start.4 = (bf16[2,1,128,128]{3,2,0,1:T(8,128)(2,1)}, bf16[2,1,128,128]{3,2,0,1:T(8,128)(2,1)}, u32[]{:S(2)}, u32[]{:S(2)}) collective-permute-start(bf16[2,1,128,128]{3,2,0,1:T(8,128)(2,1)} %bitcast.7), channel_id=1, source_target_pairs={{0,24},{8,16},{16,8},{24,0},{1,25},{9,17},{17,9},{25,1},{2,26},{10... | collective-permute-start | bytes 196616 | tf_op jit(solution)/shard_map/ppermute | solution.py:425
  11.4 9.6 %collective-permute-start.3 = (bf16[2,1,128,128]{3,2,0,1:T(8,128)(2,1)}, bf16[2,1,128,128]{3,2,0,1:T(8,128)(2,1)}, u32[]{:S(2)}, u32[]{:S(2)}) collective-permute-start(bf16[2,1,128,128]{3,2,0,1:T(8,128)(2,1)} %bitcast.7), channel_id=1, source_target_pairs={{0,16},{8,24},{16,0},{24,8},{1,17},{9,25},{17,1},{25,9},{2,18},{10... | collective-permute-start | bytes 196616 | tf_op jit(solution)/shard_map/ppermute | solution.py:425
  11.4 9.6 %collective-permute-start.2 = (bf16[2,1,128,128]{3,2,0,1:T(8,128)(2,1)}, bf16[2,1,128,128]{3,2,0,1:T(8,128)(2,1)}, u32[]{:S(2)}, u32[]{:S(2)}) collective-permute-start(bf16[2,1,128,128]{3,2,0,1:T(8,128)(2,1)} %bitcast.7), channel_id=1, source_target_pairs={{0,8},{8,0},{16,24},{24,16},{1,9},{9,1},{17,25},{25,17},{2,10},{10... | collective-permute-start | bytes 196616 | tf_op jit(solution)/shard_map/ppermute | solution.py:425
  12.0 1.2 %collective-permute-start = (s32[2,2,32]{2,1,0:T(2,128)S(1)}, s32[2,2,32]{2,1,0:T(2,128)S(1)}, u32[]{:S(2)}, u32[]{:S(2)}) collective-permute-start(s32[2,2,32]{2,1,0:T(2,128)S(1)} %copy-done.6), channel_id=1, source_target_pairs={{0,2},{2,0},{1,3},{3,1},{4,6},{6,4},{5,7},{7,5},{8,10},{10,8},{9,1... | collective-permute-start | bytes 1544 | tf_op jit(solution)/shard_map/ppermute | solution.py:425
  13.2 1.6 %copy-start.1 = (bf16[2,1,512,1024]{3,2,1,0:T(8,128)(2,1)S(1)}, bf16[2,1,512,1024]{3,2,1,0:T(8,128)(2,1)}, u32[]{:S(2)}) copy-start(bf16[2,1,512,1024]{3,2,1,0:T(8,128)(2,1)} %copy-done) | copy-start | bytes 6291460
  14.8 1.3 %copy-start.3 = (f32[16,144,128]{2,1,0:T(8,128)S(1)}, f32[16,144,128]{2,1,0:T(8,128)}, u32[]{:S(2)}) copy-start(f32[16,144,128]{2,1,0:T(8,128)} %copy-done.2) | copy-start | bytes 3538948
  16.0 1.0 %copy-start.5 = (f32[16,2,32,128]{3,2,1,0:T(8,128)S(1)}, f32[16,2,32,128]{3,2,1,0:T(8,128)}, u32[]{:S(2)}) copy-start(f32[16,2,32,128]{3,2,1,0:T(8,128)} %copy-done.4) | copy-start | bytes 1572868
  17.1 11.2 %copy-start.7 = (bf16[256,256]{1,0:T(8,128)(2,1)S(1)}, bf16[256,256]{1,0:T(8,128)(2,1)}, u32[]{:S(2)}) copy-start(bf16[256,256]{1,0:T(8,128)(2,1)} %constant.34.clone.refs_4_) | copy-start | bytes 393220
  17.1 11.2 %copy-start.8 = (bf16[256,128]{1,0:T(8,128)(2,1)S(1)}, bf16[256,128]{1,0:T(8,128)(2,1)}, u32[]{:S(2)}) copy-start(bf16[256,128]{1,0:T(8,128)(2,1)} %constant.36.clone.refs_6_) | copy-start | bytes 196612
  17.1 11.2 %copy-start.9 = (bf16[160,128]{1,0:T(8,128)(2,1)S(1)}, bf16[160,128]{1,0:T(8,128)(2,1)}, u32[]{:S(2)}) copy-start(bf16[160,128]{1,0:T(8,128)(2,1)} %constant.33.clone.refs_3_) | copy-start | bytes 122884
  17.1 11.2 %copy-start.10 = (bf16[64,160]{1,0:T(8,128)(2,1)S(1)}, bf16[64,160]{1,0:T(8,128)(2,1)}, u32[]{:S(2)}) copy-start(bf16[64,160]{1,0:T(8,128)(2,1)} %constant.35.clone.refs_5_) | copy-start | bytes 61444
  21.0 16.5 %collective-permute-start.6 = (bf16[4,128,128]{2,1,0:T(8,128)(2,1)S(1)}, bf16[4,128,128]{2,1,0:T(8,128)(2,1)S(1)}, u32[]{:S(2)}, u32[]{:S(2)}) collective-permute-start(bf16[4,128,128]{2,1,0:T(8,128)(2,1)S(1)} %get-tuple-element.38.refs_13_), channel_id=1, source_target_pairs={{0,8},{8,0},{16,24},{24,16},{1,9},{9,1},{17,25},{25,17},{2,10},{10... | collective-permute-start | bytes 393224 | tf_op jit(solution)/shard_map/ppermute | solution.py:425
  22.5 15.0 %collective-permute-start.7 = (bf16[4,128,128]{2,1,0:T(8,128)(2,1)S(1)}, bf16[4,128,128]{2,1,0:T(8,128)(2,1)S(1)}, u32[]{:S(2)}, u32[]{:S(2)}) collective-permute-start(bf16[4,128,128]{2,1,0:T(8,128)(2,1)S(1)} %get-tuple-element.43), channel_id=1, source_target_pairs={{0,16},{8,24},{16,0},{24,8},{1,17},{9,25},{17,1},{25,9},{2,18},{10... | collective-permute-start | bytes 393224 | tf_op jit(solution)/shard_map/ppermute | solution.py:425
  25.5 12.1 %collective-permute-start.8 = (bf16[4,128,128]{2,1,0:T(8,128)(2,1)S(1)}, bf16[4,128,128]{2,1,0:T(8,128)(2,1)S(1)}, u32[]{:S(2)}, u32[]{:S(2)}) collective-permute-start(bf16[4,128,128]{2,1,0:T(8,128)(2,1)S(1)} %get-tuple-element.44), channel_id=1, source_target_pairs={{0,24},{8,16},{16,8},{24,0},{1,25},{9,17},{17,9},{25,1},{2,26},{10... | collective-permute-start | bytes 393224 | tf_op jit(solution)/shard_map/ppermute | solution.py:425
  26.4 7.9 %collective-permute-start.5 = (bf16[8,128,128]{2,1,0:T(8,128)(2,1)S(1)}, bf16[8,128,128]{2,1,0:T(8,128)(2,1)S(1)}, u32[]{:S(2)}, u32[]{:S(2)}) collective-permute-start(bf16[8,128,128]{2,1,0:T(8,128)(2,1)S(1)} %pad_maximum_fusion.refs_9_), channel_id=1, source_target_pairs={{0,4},{4,0},{1,5},{5,1},{2,6},{6,2},{3,7},{7,3},{8,12},{12,8},{9,1... | collective-permute-start | bytes 786440 | tf_op jit(solution)/shard_map/ppermute | solution.py:425
  37.5 1.7 %collective-permute-start.9 = (f32[2,2,16,256]{3,2,1,0:T(8,128)S(1)}, f32[2,2,16,256]{3,2,1,0:T(8,128)S(1)}, u32[]{:S(2)}, u32[]{:S(2)}) collective-permute-start(f32[2,2,16,256]{3,2,1,0:T(8,128)S(1)} %get-tuple-element.46), channel_id=1, source_target_pairs={{0,2},{2,0},{1,3},{3,1},{4,6},{6,4},{5,7},{7,5},{8,10},{10,8},{9,1... | collective-permute-start | bytes 196616 | tf_op jit(solution)/shard_map/ppermute | solution.py:425
  37.7 4.6 %collective-permute-start.11 = (bf16[2,128,128]{2,1,0:T(8,128)(2,1)S(1)}, bf16[2,128,128]{2,1,0:T(8,128)(2,1)S(1)}, u32[]{:S(2)}, u32[]{:S(2)}) collective-permute-start(bf16[2,128,128]{2,1,0:T(8,128)(2,1)S(1)} %add_convert_fusion), channel_id=1, source_target_pairs={{0,4},{4,0},{1,5},{5,1},{2,6},{6,2},{3,7},{7,3},{8,12},{12,8},{9,1... | collective-permute-start | bytes 196616 | tf_op jit(solution)/shard_map/ppermute | solution.py:425
  39.3 4.0 %collective-permute-start.10 = (f32[2,16,256]{2,1,0:T(8,128)S(1)}, f32[2,16,256]{2,1,0:T(8,128)S(1)}, u32[]{:S(2)}, u32[]{:S(2)}) collective-permute-start(f32[2,16,256]{2,1,0:T(8,128)S(1)} %fusion), channel_id=1, source_target_pairs={{0,1},{1,0},{2,3},{3,2},{4,5},{5,4},{6,7},{7,6},{8,9},{9,8},{10,11... | collective-permute-start | bytes 98312 | tf_op jit(solution)/shard_map/ppermute | solution.py:425

commit v11 on v10

--- a/solution.py
+++ b/solution.py
@@ -62,11 +62,11 @@
 
     lanes = np.arange(block_size)[None, :]
     inputs = np.arange(block_size + 3 * EDGE)[:, None] - EDGE - SHIFT
-    outputs = np.arange(block_size + EDGE)[:, None] - SHIFT
+    outputs = np.arange(2 * EDGE)[:, None] - SHIFT
     spare = np.arange(LANES)[None, :] % (2 * EDGE)
-    first = band(spare - 2 * EDGE, outputs[: 2 * EDGE]) * (spare >= EDGE)
-    last = band(spare + EDGE, outputs[: 2 * EDGE]) * (spare < EDGE)
-    tables = band(inputs, lanes), band(lanes, outputs), np.stack([first, last], axis=1)
+    first = band(spare - 2 * EDGE, outputs) * (spare >= EDGE)
+    last = band(spare + EDGE, outputs) * (spare < EDGE)
+    tables = band(inputs, lanes), np.stack([first, last], axis=1)
     return [jnp.asarray(table, jnp.float32) for table in tables]
 
 
@@ -111,8 +111,8 @@
     )(*kept, pltpu.with_memory_space_constraint(after, pltpu.HBM))
 
 
-def warp_step(place_ref, step, code_refs, frame_refs, band_refs, down, across, block, own):
-    cols_ref, rows_ref, edges_ref = band_refs
+def warp_step(place_ref, step, other, code_refs, frame_refs, band_refs, down, across, block, own):
+    cols_ref, edges_ref = band_refs
     band = step_band(place_ref, step, across, own)
     row = pl.multiple_of(band * block, block)
     row_above = pl.multiple_of(jnp.maximum(row - EDGE, 0), EDGE)
@@ -135,95 +135,102 @@
         below = jnp.where(band < down - 1, frames[v, pl.ds(row_below, EDGE), lanes], zero)
         return jnp.concatenate([frames[v, pl.ds(row, block), lanes], below, above], axis=0)
 
-    places = step_places(place_ref, step, across, own)
+    places = step_places(place_ref, step, across, own)[other * own : (other + 1) * own]
+    start = places[0][1]
+    tiles = []
+    for _, frames, v in volumes:
+        left = jnp.where(start > 0, tile(frames, v, jnp.maximum(start - 1, 0)), no_tile)
+        right = jnp.where(
+            start + own < across, tile(frames, v, jnp.minimum(start + own, across - 1)), no_tile
+        )
+        tiles.append([left] + [tile(frames, v, start + one) for one in range(own)] + [right])
     totals = []
-    for group in range(0, len(places), own):
-        start = places[group][1]
-        tiles = []
-        for _, frames, v in volumes:
-            left = jnp.where(start > 0, tile(frames, v, jnp.maximum(start - 1, 0)), no_tile)
-            right = jnp.where(
-                start + own < across,
-                tile(frames, v, jnp.minimum(start + own, across - 1)),
-                no_tile,
-            )
-            tiles.append([left] + [tile(frames, v, start + one) for one in range(own)] + [right])
-        for one in range(own):
-            index = places[group + one][0]
-            row_tiles, partials, edges = [], [], []
-            firsts, lasts = [], []
-            for order, (codes, _, v) in enumerate(volumes):
-                row_code, col_code = codes[v, 0, index], codes[v, 1, index]
-                left, middle, right = tiles[order][one : one + 3]
-                sides = jnp.concatenate([right[:, : block // 2], left[:, block // 2 :]], axis=1)
-                col_start = SHIFT - (col_code >> 4)
-                cols = cols_ref[col_code & (SUB - 1), pl.ds(col_start, block + 2 * EDGE), :]
-                cols = cols.astype(jnp.bfloat16)
-                partial = jnp.dot(
-                    jnp.concatenate([middle, sides], axis=1),
-                    jnp.concatenate([cols[EDGE:], gap, cols[:EDGE]], axis=0),
-                    preferred_element_type=jnp.float32,
-                ).astype(jnp.bfloat16)
-                partials.append(partial[:block])
-                edges.append(partial[block:])
-                row_start = SHIFT + (row_code >> 4)
-                step_at = row_code & (SUB - 1)
-                row_tiles.append(rows_ref[step_at, pl.ds(row_start, block), :].astype(jnp.bfloat16))
-                first = edges_ref[step_at, 0, pl.ds(row_start, EDGE), :]
-                last = edges_ref[step_at, 1, pl.ds(row_start, EDGE), :]
-                if order % per_tile:
-                    first = jnp.where(lane == order % per_tile, first, firsts.pop())
-                    last = jnp.where(lane == order % per_tile, last, lasts.pop())
-                firsts.append(first)
-                lasts.append(last)
-            for first, last in zip(firsts, lasts):
-                both = [first.astype(jnp.bfloat16), gap, last.astype(jnp.bfloat16)]
-                row_tiles.append(jnp.concatenate(both, axis=0))
-            deep = many * (block + 2 * EDGE)
-            total = jnp.dot(
-                jnp.concatenate(row_tiles, axis=1)[:, :deep],
-                jnp.concatenate(partials + edges, axis=0),
+    for one, (index, _) in enumerate(places):
+        row_tiles, partials, edges = [], [], []
+        firsts, lasts = [], []
+        for order, (codes, _, v) in enumerate(volumes):
+            row_code, col_code = codes[v, 0, index], codes[v, 1, index]
+            left, middle, right = tiles[order][one : one + 3]
+            sides = jnp.concatenate([right[:, : block // 2], left[:, block // 2 :]], axis=1)
+            col_start = SHIFT - (col_code >> 4)
+            cols = cols_ref[col_code & (SUB - 1), pl.ds(col_start, block + 2 * EDGE), :]
+            cols = cols.astype(jnp.bfloat16)
+            partial = jnp.dot(
+                jnp.concatenate([middle, sides], axis=1),
+                jnp.concatenate([cols[EDGE:], gap, cols[:EDGE]], axis=0),
                 preferred_element_type=jnp.float32,
-            )
-            totals.append(total.astype(jnp.bfloat16))
+            ).astype(jnp.bfloat16)
+            partials.append(partial[:block])
+            edges.append(partial[block:])
+            back = -row_code
+            back_start = SHIFT + EDGE - (back >> 4)
+            rows = cols_ref[back & (SUB - 1), pl.ds(back_start, block), :]
+            row_tiles.append(rows.astype(jnp.bfloat16))
+            row_start, step_at = SHIFT + (row_code >> 4), row_code & (SUB - 1)
+            first = edges_ref[step_at, 0, pl.ds(row_start, EDGE), :]
+            last = edges_ref[step_at, 1, pl.ds(row_start, EDGE), :]
+            if order % per_tile:
+                first = jnp.where(lane == order % per_tile, first, firsts.pop())
+                last = jnp.where(lane == order % per_tile, last, lasts.pop())
+            firsts.append(first)
+            lasts.append(last)
+        for first, last in zip(firsts, lasts):
+            both = [first.astype(jnp.bfloat16), gap, last.astype(jnp.bfloat16)]
+            row_tiles.append(jnp.concatenate(both, axis=0))
+        deep = many * (block + 2 * EDGE)
+        total = jnp.dot(
+            jnp.concatenate(row_tiles, axis=1)[:, :deep],
+            jnp.concatenate(partials + edges, axis=0),
+            preferred_element_type=jnp.float32,
+        )
+        totals.append(total.astype(jnp.bfloat16))
     return totals
 
 
-def warp_kernel(down, across, block, own, depth, *refs):
+def warp_kernel(down, across, block, own, other, *refs):
     place_ref, *code_refs = refs[:3]
-    frame_refs, band_refs = refs[3:5], refs[5:8]
-    out_refs = refs[8:]
-
-    for at, out_ref in enumerate(out_refs):
+    frame_refs, band_refs, out_refs = refs[3:5], refs[5:7], refs[8:]
+    depth = out_refs[0].shape[0] // own if other else len(out_refs)
+    for step in range(depth):
         totals = warp_step(
-            place_ref, at + 1, code_refs, frame_refs, band_refs, down, across, block, own
+            place_ref, step, other, code_refs, frame_refs, band_refs, down, across, block, own
         )
-        for count, total in enumerate(totals):
-            out_ref[count] = total
-
-
-def warp_sums(place, codes, other_codes, frames, other_frames, bands, depth, block, own):
+        for one, total in enumerate(totals):
+            if other:
+                out_refs[0][step * own + one] = total
+            else:
+                out_refs[step][one] = total
+
+
+def warp_sums(
+    place, codes, other_codes, frames, other_frames, bands, after, other, depth, block, own
+):
     vols, rows, cols = frames.shape
     down, across = rows // block, cols // block
-    out = (2 * own, block, block)
     smem = pl.BlockSpec(memory_space=pltpu.SMEM)
     vmem = pl.BlockSpec(memory_space=pltpu.VMEM)
+    if other:
+        out_shape = [jax.ShapeDtypeStruct((depth * own, block, block), jnp.bfloat16)]
+    else:
+        out_shape = [jax.ShapeDtypeStruct((own, block, block), jnp.bfloat16)] * depth
     return pl.pallas_call(
-        functools.partial(warp_kernel, down, across, block, own, depth),
-        out_shape=[jax.ShapeDtypeStruct(out, jnp.bfloat16)] * (depth - 1),
-        in_specs=[smem] * 3 + [vmem] * 5,
-        out_specs=[vmem] * (depth - 1),
+        functools.partial(warp_kernel, down, across, block, own, other),
+        out_shape=out_shape,
+        in_specs=[smem] * 3
+        + [vmem] * (2 + len(bands))
+        + [pl.BlockSpec(memory_space=pl.ANY)],
+        out_specs=[vmem] * len(out_shape),
         compiler_params=pltpu.CompilerParams(vmem_limit_bytes=VMEM_LIMIT),
         cost_estimate=pl.CostEstimate(
-            flops=2 * vols * rows * cols * block * 16,
+            flops=2 * vols * rows * cols * block * 8,
             bytes_accessed=vols * rows * cols * 4 + rows * cols,
             transcendentals=0,
         ),
         name="warp",
-    )(place, codes, other_codes, frames, other_frames, *bands)
-
-
-def spectrum_kernel(vols, down, across, block, own, planes, depth, other, *refs):
+    )(place, codes, other_codes, frames, other_frames, *bands, after)
+
+
+def spectrum_kernel(vols, across, block, own, planes, depth, other, *refs):
     place_ref, codes_ref, other_codes_ref, row_ref, col_ref, lag_ref, span_ref = refs[:7]
     frames_ref, other_frames_ref, template_ref = refs[7:10]
     all_cross, all_sums = refs[-2:]
@@ -231,13 +238,7 @@
         found_ref, out_refs, found = refs[10], refs[11:-3], refs[-3]
         found[...] = found_ref[...]
     else:
-        band_refs, found, sums_ref = refs[10:13], refs[14], refs[15]
-        code_refs, frame_refs = (codes_ref, other_codes_ref), (frames_ref, other_frames_ref)
-        totals = warp_step(
-            place_ref, 0, code_refs, frame_refs, band_refs, down, across, block, own
-        )
-        for count, total in enumerate(totals):
-            sums_ref[count] = total
+        found = refs[11]
         found[...] = jnp.zeros(found.shape, jnp.float32)
 
     row_table = row_ref[...]
@@ -379,7 +380,7 @@
 
 
 def lag_windows(
-    place, codes, other_codes, frames, other_frames, template, bands, other, planes, depth, own, more
+    place, codes, other_codes, frames, other_frames, template, more, other, planes, depth, own
 ):
     vols, rows, cols = frames.shape
     block = template.shape[-1]
@@ -396,15 +397,15 @@
         out_shape = [jax.ShapeDtypeStruct(out, jnp.float32)] * planes
         out_shape.append(jax.ShapeDtypeStruct((planes, *out), jnp.float32))
         scratch_shapes = [pltpu.VMEM(found.shape, found.dtype)]
-        bands, last = [], vmem
+        last = vmem
     else:
-        out_shape = [found, jax.ShapeDtypeStruct((2 * own, block, block), jnp.bfloat16)]
+        out_shape = [found]
         scratch_shapes = []
         last = pl.BlockSpec(memory_space=pl.ANY)
     return pl.pallas_call(
-        functools.partial(spectrum_kernel, vols, down, across, block, own, planes, depth, other),
+        functools.partial(spectrum_kernel, vols, across, block, own, planes, depth, other),
         out_shape=out_shape,
-        in_specs=[smem] * 3 + [vmem] * (len(tables) + 3 + len(bands)) + [last],
+        in_specs=[smem] * 3 + [vmem] * (len(tables) + 3) + [last],
         out_specs=[vmem] * len(out_shape),
         scratch_shapes=scratch_shapes
         + [
@@ -413,12 +414,12 @@
         ],
         compiler_params=pltpu.CompilerParams(vmem_limit_bytes=VMEM_LIMIT),
         cost_estimate=pl.CostEstimate(
-            flops=2 * 3 * rows * cols * block * 8,
+            flops=2 * 3 * rows * cols * block * (2 if other else 8),
             bytes_accessed=vols * rows * cols * 4 + rows * cols,
             transcendentals=0,
         ),
         name="lag_windows",
-    )(place, codes, other_codes, *tables, frames, other_frames, template, *bands, more)
+    )(place, codes, other_codes, *tables, frames, other_frames, template, more)
 
 
 def exchange(value, axes, size, turn):
@@ -434,27 +435,33 @@
     other_codes = exchange(shift_codes, "core", 2, 1)
     other_frames = exchange(frames, "core", 2, 1)
     staged, *bands = stage([frames, *tap_constants(block)], template)
-    later, staged = lax.optimization_barrier((template, staged))
-    pieces = [template] + [exchange(later, "z", depth, turn) for turn in range(1, depth)]
+    pieces = [template] + [exchange(template, "z", depth, turn) for turn in range(1, depth)]
     averages, correlation = [], 0.0
     volumes = vol_dev * depth * 4
     for p in range(pl_dev):
         work = (place, shift_codes, other_codes, staged[:, p], other_frames[:, p])
-        warped = list(warp_sums(*work, bands, depth, block, own))
-        pieces, warped[0] = lax.optimization_barrier((pieces, warped[0]))
+        sizes = (depth, block, own)
+        (far_sums,) = warp_sums(*work, bands, template, 1, *sizes)
+        taken = exchange(far_sums, "y", 2, 1)
+        near_sums = warp_sums(*work, bands, far_sums, 0, *sizes)
+        pieces, near_sums = lax.optimization_barrier((pieces, near_sums))
         near = jnp.concatenate([piece[:, p] for piece in pieces], axis=0)
         far = exchange(near, "y", 2, 1)
+        sums = [
+            one.astype(jnp.float32) + taken[step * own : (step + 1) * own].astype(jnp.float32)
+            for step, one in enumerate(near_sums)
+        ]
+        moved = [
+            exchange(sums[turn].astype(jnp.bfloat16), "z", depth, turn) for turn in range(1, depth)
+        ]
         sizes = (planes, depth, own)
-        part, kept = lag_windows(*work, near, bands, 0, *sizes, warped[0])
-        found = lag_windows(*work, far, bands, 1, *sizes, part)
-        warped = [exchange(one, "z", depth, turn + 1) for turn, one in enumerate(warped)]
-        found, warped = lax.optimization_barrier((found, warped))
-        warped.append(kept)
-        sums = [sum(one[at : at + own].astype(jnp.float32) for one in warped) for at in (0, own)]
-        taken = exchange(sums[1].astype(jnp.bfloat16), "y", 2, 1)
-        averages.append((sums[0] + taken.astype(jnp.float32)) * (1.0 / volumes))
-        got = exchange(found[-1], "core", 2, 1)
-        for turn, one in enumerate(found[:-1]):
+        (part,) = lag_windows(*work, near, sums[0], 0, *sizes)
+        *keep, give = lag_windows(*work, far, part, 1, *sizes)
+        keep, moved = lax.optimization_barrier((keep, moved))
+        total = sum((one.astype(jnp.float32) for one in moved), sums[0])
+        averages.append(total * (1.0 / volumes))
+        got = exchange(give, "core", 2, 1)
+        for turn, one in enumerate(keep):
             one = one + got[turn]
             correlation += exchange(one, "plane", planes, turn) if turn else one
     return (correlation, jnp.stack(averages, axis=1))

time: 44.2 us -> 37.4 us (0.85)
  local copies, waits for them, and re-layouts: 7.08 us -> 0.04 us
  waiting for transfers between devices: 4.89 us -> 6.86 us
  starting transfers between devices: 15.2 us -> 14.1 us
  other arithmetic: 2.42 us -> 1.51 us
    unnamed x22 -> x12, local copies, waits for them, and re-layouts: 7.08 us -> 0.04 us
    ppermute x12, waiting for transfers between devices: 4.89 us -> 6.86 us  [exchange(): return lax.ppermute(value, axes, [(at, at ^ turn) for at in range(size)])]
    ppermute x12, starting transfers between devices: 15.2 us -> 14.1 us  [exchange(): return lax.ppermute(value, axes, [(at, at ^ turn) for at in range(size)])]
    concatenate x1, other arithmetic: 0.97 us -> 0.04 us  [on_device(): near = jnp.concatenate([piece[:, p] for piece in pieces], axis=0)]
    pallas_call x3 -> x4, Pallas kernels: 11.1 us -> 11.8 us  [the longest x2 6.08 us: lag_windows(): pl.pallas_call(functools.partial(spectrum_kernel, vols, across, block, ow...]
  transfers between devices with their start and end apart: 12 -> 12, of which waited for: 4 -> 3; matrix products, arithmetic and copies ran while one was open for 4% -> 2% of each run, Pallas kernels for 31% -> 37%
where the time goes in v11:
time: 37.4 us; the launch traced here: 37.3 us
  starting transfers between devices  14.1 us (38%)
  Pallas kernels  13.9 us (37%)
  waiting for transfers between devices  6.86 us (18%)
  other arithmetic  1.51 us (4%)
  between operations  0.82 us (2%)
    ppermute x12, starting transfers between devices, exchange(): return lax.ppermute(value, axes, [(at, at ^ turn) for at in range(size)])  14.1 us
    ppermute x12, waiting for transfers between devices, exchange(): return lax.ppermute(value, axes, [(at, at ^ turn) for at in range(size)])  6.86 us
    pallas_call x2, Pallas kernels, lag_windows(): pl.pallas_call(functools.partial(spectrum_kernel, vols, across, block, ow...  6.08 us
    pallas_call x2, Pallas kernels, warp_sums(): pl.pallas_call(functools.partial(warp_kernel, down, across, block, own, o...  5.68 us
    pallas_call x1, Pallas kernels, stage(): pl.pallas_call(functools.partial(stage_kernel, count), out_shape=[jax.Sha...  2.13 us
  transfers between devices with their start and end apart: 12, of which 3 were waited for; matrix products, arithmetic and copies ran while one was open for 2% of the time, Pallas kernels for 37%

profile of v11, /device:TPU:0, one launch (start us, length us, event | category | flops | bytes accessed | tf_op | source)
XLA Modules:
  0.0 37.3 jit_solution(15752969497867648402)
XLA Ops:
  0.6 0.0 copy-start
  0.7 0.5 %collective-permute-start.1 = (bf16[2,1,512,1024]{3,2,0,1:T(8,128)(2,1)}, bf16[2,1,512,1024]{3,2,0,1:T(8,128)(2,1)S(1)}, u32[]{:S(2)}, u32[]{:S(2)}) collective-permute-start(bf16[2,1,512,1024]{3,2,0,1:T(8,128)(2,1)} %bitcast.38), channel_id=1, source_target_pairs={{0,2},{2,0},{1,3},{3,1},{4,6},{6,4},{5,7},{7,5},{8,10},{10,8},{9,1... | collective-permute-start | bytes 6291464 | tf_op jit(solution)/shard_map/ppermute | solution.py:426
  1.2 2.7 %collective-permute-start.2 = (bf16[2,1,128,128]{3,2,0,1:T(8,128)(2,1)}, bf16[2,1,128,128]{3,2,0,1:T(8,128)(2,1)S(1)}, u32[]{:S(2)}, u32[]{:S(2)}) collective-permute-start(bf16[2,1,128,128]{3,2,0,1:T(8,128)(2,1)} %bitcast.34), channel_id=1, source_target_pairs={{0,8},{8,0},{16,24},{24,16},{1,9},{9,1},{17,25},{25,17},{2,10},{10... | collective-permute-start | bytes 196616 | tf_op jit(solution)/shard_map/ppermute | solution.py:426
  3.8 2.6 %collective-permute-start.3 = (bf16[2,1,128,128]{3,2,0,1:T(8,128)(2,1)}, bf16[2,1,128,128]{3,2,0,1:T(8,128)(2,1)S(1)}, u32[]{:S(2)}, u32[]{:S(2)}) collective-permute-start(bf16[2,1,128,128]{3,2,0,1:T(8,128)(2,1)} %bitcast.35), channel_id=1, source_target_pairs={{0,16},{8,24},{16,0},{24,8},{1,17},{9,25},{17,1},{25,9},{2,18},{10... | collective-permute-start | bytes 196616 | tf_op jit(solution)/shard_map/ppermute | solution.py:426
  6.4 0.1 pad_add_fusion.refs_0_
  6.5 2.1 %stage.1 = (bf16[2,1,512,1024]{3,2,1,0:T(8,128)(2,1)S(1)}, f32[16,176,128]{2,1,0:T(8,128)S(1)}, f32[16,2,32,128]{3,2,1,0:T(8,128)S(1)}) custom-call(bf16[2,1,512,1024]{3,2,1,0:T(8,128)(2,1)} %refs_0_.1, f32[16,176,128]{2,1,0:T(8,128)} %constant.28.clone.refs_1_, f32[16,2,32,128]{3,2,1,0:T(8,128)} %constant.29.clone.refs_2_, bf16[2,1,128,128]{3,2,1,0:T(8,128)(2,1)} %refs_7_.1), custom_call_target="tpu_custom_call" | custom-call | tf_op jit(solution)/shard_map/stage/pallas_call | solution.py:102
  8.7 2.8 %warp.2.refs_7_ = bf16[8,128,128]{2,1,0:T(8,128)(2,1)S(1)} custom-call(s32[4]{0:T(128)S(1)} %pad_add_fusion.refs_0_, s32[2,2,32]{2,1,0:T(2,128)S(1)} %copy-done.5, s32[2,2,32]{2,1,0:T(2,128)S(1)} %collective-permute-done.refs_2_, bf16[2,512,1024]{2,1,0:T(8,128)(2,1)S(1)} %bitcast.30, bf16[2,512,1024]{2,1,0:T(8,128)(2,1)S(1)} %bitcast.26, ...), custom_call_target="tpu_custom_call" | custom-call | flops 2147483648 | bytes 4718592 | tf_op jit(solution)/shard_map/warp/pallas_call | solution.py:216
  11.5 0.0 copy-start.2
  11.5 0.0 copy-start.3
  11.6 1.8 %collective-permute-start.6 = (bf16[8,128,128]{2,1,0:T(8,128)(2,1)S(1)}, bf16[8,128,128]{2,1,0:T(8,128)(2,1)S(1)}, u32[]{:S(2)}, u32[]{:S(2)}) collective-permute-start(bf16[8,128,128]{2,1,0:T(8,128)(2,1)S(1)} %warp.2.refs_7_), channel_id=1, source_target_pairs={{0,4},{4,0},{1,5},{5,1},{2,6},{6,2},{3,7},{7,3},{8,12},{12,8},{9,1... | collective-permute-start | bytes 786440 | tf_op jit(solution)/shard_map/ppermute | solution.py:426
  13.4 2.8 %warp.3 = (bf16[2,128,128]{2,1,0:T(8,128)(2,1)S(1)}, bf16[2,128,128]{2,1,0:T(8,128)(2,1)S(1)}, bf16[2,128,128]{2,1,0:T(8,128)(2,1)S(1)}, bf16[2,128,128]{2,1,0:T(8,128)(2,1)S(1)}) custom-call(s32[4]{0:T(128)S(1)} %pad_add_fusion.refs_0_, s32[2,2,32]{2,1,0:T(2,128)S(1)} %copy-done.5, s32[2,2,32]{2,1,0:T(2,128)S(1)} %collective-permute-done.refs_2_, ...), custom_call_target="tpu_custom_call" | custom-call | flops 2147483648 | bytes 4718592 | tf_op jit(solution)/shard_map/warp/pallas_call | solution.py:216
  16.3 0.4 collective-permute-start.5
  16.6 4.1 %collective-permute-done.6 = bf16[8,128,128]{2,1,0:T(8,128)(2,1)S(1)} collective-permute-done((bf16[8,128,128]{2,1,0:T(8,128)(2,1)S(1)}, bf16[8,128,128]{2,1,0:T(8,128)(2,1)S(1)}, u32[]{:S(2)}, u32[]{:S(2)}) %collective-permute-start.6) | collective-permute-done | bytes 262176 | tf_op jit(solution)/shard_map/ppermute | solution.py:426
  20.7 0.1 add_convert_fusion
  20.8 1.0 %collective-permute-start.7 = (bf16[2,128,128]{2,1,0:T(8,128)(2,1)S(1)}, bf16[2,128,128]{2,1,0:T(8,128)(2,1)S(1)}, u32[]{:S(2)}, u32[]{:S(2)}) collective-permute-start(bf16[2,128,128]{2,1,0:T(8,128)(2,1)S(1)} %get-tuple-element.52), channel_id=1, source_target_pairs={{0,8},{8,0},{16,24},{24,16},{1,9},{9,1},{17,25},{25,17},{2,10},{10... | collective-permute-start | bytes 196616 | tf_op jit(solution)/shard_map/ppermute | solution.py:426
  21.8 3.5 %collective-permute-start.8 = (bf16[2,128,128]{2,1,0:T(8,128)(2,1)S(1)}, bf16[2,128,128]{2,1,0:T(8,128)(2,1)S(1)}, u32[]{:S(2)}, u32[]{:S(2)}) collective-permute-start(bf16[2,128,128]{2,1,0:T(8,128)(2,1)S(1)} %get-tuple-element.51), channel_id=1, source_target_pairs={{0,16},{8,24},{16,0},{24,8},{1,17},{9,25},{17,1},{25,9},{2,18},{10... | collective-permute-start | bytes 196616 | tf_op jit(solution)/shard_map/ppermute | solution.py:426
  25.3 2.9 %lag_windows.2.refs_10_ = f32[4,512,128]{2,1,0:T(8,128)S(1)} custom-call(s32[4]{0:T(128)S(1)} %pad_add_fusion.refs_0_, s32[2,2,32]{2,1,0:T(2,128)S(1)} %copy-done.5, s32[2,2,32]{2,1,0:T(2,128)S(1)} %collective-permute-done.refs_2_, bf16[160,128]{1,0:T(8,128)(2,1)S(1)} %copy-done.3, bf16[256,256]{1,0:T(8,128)(2,1)S(1)} %copy-done.1, ...), custom_call_target="tpu_custom_call" | custom-call | flops 3221225472 | bytes 4718592 | tf_op jit(solution)/shard_map/lag_windows/pallas_call | solution.py:405
  28.2 3.2 %lag_windows.3 = (f32[2,16,256]{2,1,0:T(8,128)S(1)}, f32[2,16,256]{2,1,0:T(8,128)S(1)}, f32[2,2,16,256]{3,2,1,0:T(8,128)S(1)}) custom-call(s32[4]{0:T(128)S(1)} %pad_add_fusion.refs_0_, s32[2,2,32]{2,1,0:T(2,128)S(1)} %copy-done.5, s32[2,2,32]{2,1,0:T(2,128)S(1)} %collective-permute-done.refs_2_, bf16[160,128]{1,0:T(8,128)(2,1)S(1)} %copy-done.3, ...), custom_call_target="tpu_custom_call" | custom-call | flops 805306368 | bytes 4718592 | tf_op jit(solution)/shard_map/lag_windows/pallas_call | solution.py:405
  31.4 0.1 collective-permute-start.10
  31.5 1.2 %collective-permute-done.10 = f32[2,2,16,256]{3,2,1,0:T(8,128)S(1)} collective-permute-done((f32[2,2,16,256]{3,2,1,0:T(8,128)S(1)}, f32[2,2,16,256]{3,2,1,0:T(8,128)S(1)}, u32[]{:S(2)}, u32[]{:S(2)}) %collective-permute-start.10) | collective-permute-done | bytes 65568 | tf_op jit(solution)/shard_map/ppermute | solution.py:426
  32.7 1.7 %collective-permute-start.11 = (f32[2,16,256]{2,1,0:T(8,128)S(1)}, f32[2,16,256]{2,1,0:T(8,128)S(1)}, u32[]{:S(2)}, u32[]{:S(2)}) collective-permute-start(f32[2,16,256]{2,1,0:T(8,128)S(1)} %fusion), channel_id=1, source_target_pairs={{0,1},{1,0},{2,3},{3,2},{4,5},{5,4},{6,7},{7,6},{8,9},{9,8},{10,11... | collective-permute-start | bytes 98312 | tf_op jit(solution)/shard_map/ppermute | solution.py:426
  34.4 0.7 %multiply_bitcast_fusion = f32[2,1,128,128]{3,2,1,0:T(8,128)} fusion(bf16[2,128,128]{2,1,0:T(8,128)(2,1)S(1)} %collective-permute-done.9, bf16[2,128,128]{2,1,0:T(8,128)(2,1)S(1)} %collective-permute-done.8, bf16[2,128,128]{2,1,0:T(8,128)(2,1)S(1)} %collective-permute-done.7, bf16[8,128,128]{2,1,0:T(8,128)(2,1)S(1)} %collective-permute-done.6, ...), kind=kLoop, calls=%fused_computation.1 | loop fusion | flops 327680 | bytes 458752
  35.1 1.5 %collective-permute-done.11 = f32[2,16,256]{2,1,0:T(8,128)S(1)} collective-permute-done((f32[2,16,256]{2,1,0:T(8,128)S(1)}, f32[2,16,256]{2,1,0:T(8,128)S(1)}, u32[]{:S(2)}, u32[]{:S(2)}) %collective-permute-start.11) | collective-permute-done | bytes 32800 | tf_op jit(solution)/shard_map/ppermute | solution.py:426
  36.6 0.6 %fusion.2 = f32[2,16,256]{2,1,0:T(8,128)} fusion(f32[2,16,256]{2,1,0:T(8,128)S(1)} %collective-permute-done.11, f32[2,16,256]{2,1,0:T(8,128)S(1)} %get-tuple-element.42, f32[2,2,16,256]{3,2,1,0:T(8,128)S(1)} %collective-permute-done.10), kind=kLoop, calls=%fused_computation.10 | loop fusion | flops 16384 | bytes 131072 | tf_op jit(solution)/shard_map/add | solution.py:466
  (23 shorter events, 0.1 us)
Async XLA Ops:
  0.6 8.0 %copy-start = (bf16[2,1,128,128]{3,2,1,0:T(8,128)(2,1)S(1)}, bf16[2,1,128,128]{3,2,1,0:T(8,128)(2,1)}, u32[]{:S(2)}) copy-start(bf16[2,1,128,128]{3,2,1,0:T(8,128)(2,1)} %refs_7_.1) | copy-start | bytes 196612
  0.6 8.0 %copy-start.5 = (s32[2,2,32]{2,1,0:T(2,128)S(1)}, s32[2,2,32]{2,1,0:T(2,128)}, u32[]{:S(2)}) copy-start(s32[2,2,32]{2,1,0:T(2,128)} %refs_1_.8) | copy-start | bytes 1540
  0.7 8.0 %collective-permute-start.1 = (bf16[2,1,512,1024]{3,2,0,1:T(8,128)(2,1)}, bf16[2,1,512,1024]{3,2,0,1:T(8,128)(2,1)S(1)}, u32[]{:S(2)}, u32[]{:S(2)}) collective-permute-start(bf16[2,1,512,1024]{3,2,0,1:T(8,128)(2,1)} %bitcast.38), channel_id=1, source_target_pairs={{0,2},{2,0},{1,3},{3,1},{4,6},{6,4},{5,7},{7,5},{8,10},{10,8},{9,1... | collective-permute-start | bytes 6291464 | tf_op jit(solution)/shard_map/ppermute | solution.py:426
  1.2 15.0 %collective-permute-start.2 = (bf16[2,1,128,128]{3,2,0,1:T(8,128)(2,1)}, bf16[2,1,128,128]{3,2,0,1:T(8,128)(2,1)S(1)}, u32[]{:S(2)}, u32[]{:S(2)}) collective-permute-start(bf16[2,1,128,128]{3,2,0,1:T(8,128)(2,1)} %bitcast.34), channel_id=1, source_target_pairs={{0,8},{8,0},{16,24},{24,16},{1,9},{9,1},{17,25},{25,17},{2,10},{10... | collective-permute-start | bytes 196616 | tf_op jit(solution)/shard_map/ppermute | solution.py:426
  3.8 12.4 %collective-permute-start.3 = (bf16[2,1,128,128]{3,2,0,1:T(8,128)(2,1)}, bf16[2,1,128,128]{3,2,0,1:T(8,128)(2,1)S(1)}, u32[]{:S(2)}, u32[]{:S(2)}) collective-permute-start(bf16[2,1,128,128]{3,2,0,1:T(8,128)(2,1)} %bitcast.35), channel_id=1, source_target_pairs={{0,16},{8,24},{16,0},{24,8},{1,17},{9,25},{17,1},{25,9},{2,18},{10... | collective-permute-start | bytes 196616 | tf_op jit(solution)/shard_map/ppermute | solution.py:426
  6.4 9.8 %collective-permute-start.4 = (bf16[2,1,128,128]{3,2,0,1:T(8,128)(2,1)}, bf16[2,1,128,128]{3,2,0,1:T(8,128)(2,1)S(1)}, u32[]{:S(2)}, u32[]{:S(2)}) collective-permute-start(bf16[2,1,128,128]{3,2,0,1:T(8,128)(2,1)} %bitcast.36), channel_id=1, source_target_pairs={{0,24},{8,16},{16,8},{24,0},{1,25},{9,17},{17,9},{25,1},{2,26},{10... | collective-permute-start | bytes 196616 | tf_op jit(solution)/shard_map/ppermute | solution.py:426
  6.4 2.2 %collective-permute-start = (s32[2,2,32]{2,1,0:T(2,128)}, s32[2,2,32]{2,1,0:T(2,128)S(1)}, u32[]{:S(2)}, u32[]{:S(2)}) collective-permute-start(s32[2,2,32]{2,1,0:T(2,128)} %refs_1_.8), channel_id=1, source_target_pairs={{0,2},{2,0},{1,3},{3,1},{4,6},{6,4},{5,7},{7,5},{8,10},{10,8},{9,1... | collective-permute-start | bytes 1544 | tf_op jit(solution)/shard_map/ppermute | solution.py:426
  11.5 13.8 %copy-start.1 = (bf16[256,256]{1,0:T(8,128)(2,1)S(1)}, bf16[256,256]{1,0:T(8,128)(2,1)}, u32[]{:S(2)}) copy-start(bf16[256,256]{1,0:T(8,128)(2,1)} %constant.31.clone.refs_4_) | copy-start | bytes 393220
  11.5 13.7 %copy-start.2 = (bf16[256,128]{1,0:T(8,128)(2,1)S(1)}, bf16[256,128]{1,0:T(8,128)(2,1)}, u32[]{:S(2)}) copy-start(bf16[256,128]{1,0:T(8,128)(2,1)} %constant.33.clone.refs_6_) | copy-start | bytes 196612
  11.5 13.7 %copy-start.3 = (bf16[160,128]{1,0:T(8,128)(2,1)S(1)}, bf16[160,128]{1,0:T(8,128)(2,1)}, u32[]{:S(2)}) copy-start(bf16[160,128]{1,0:T(8,128)(2,1)} %constant.30.clone.refs_3_) | copy-start | bytes 122884
  11.6 13.7 %copy-start.4 = (bf16[64,160]{1,0:T(8,128)(2,1)S(1)}, bf16[64,160]{1,0:T(8,128)(2,1)}, u32[]{:S(2)}) copy-start(bf16[64,160]{1,0:T(8,128)(2,1)} %constant.32.clone.refs_5_) | copy-start | bytes 61444
  11.6 9.2 %collective-permute-start.6 = (bf16[8,128,128]{2,1,0:T(8,128)(2,1)S(1)}, bf16[8,128,128]{2,1,0:T(8,128)(2,1)S(1)}, u32[]{:S(2)}, u32[]{:S(2)}) collective-permute-start(bf16[8,128,128]{2,1,0:T(8,128)(2,1)S(1)} %warp.2.refs_7_), channel_id=1, source_target_pairs={{0,4},{4,0},{1,5},{5,1},{2,6},{6,2},{3,7},{7,3},{8,12},{12,8},{9,1... | collective-permute-start | bytes 786440 | tf_op jit(solution)/shard_map/ppermute | solution.py:426
  16.3 11.9 %collective-permute-start.5 = (bf16[8,128,128]{2,1,0:T(8,128)(2,1)S(1)}, bf16[8,128,128]{2,1,0:T(8,128)(2,1)S(1)}, u32[]{:S(2)}, u32[]{:S(2)}) collective-permute-start(bf16[8,128,128]{2,1,0:T(8,128)(2,1)S(1)} %pad_maximum_fusion.refs_9_), channel_id=1, source_target_pairs={{0,4},{4,0},{1,5},{5,1},{2,6},{6,2},{3,7},{7,3},{8,12},{12,8},{9,1... | collective-permute-start | bytes 786440 | tf_op jit(solution)/shard_map/ppermute | solution.py:426
  20.8 10.7 %collective-permute-start.7 = (bf16[2,128,128]{2,1,0:T(8,128)(2,1)S(1)}, bf16[2,128,128]{2,1,0:T(8,128)(2,1)S(1)}, u32[]{:S(2)}, u32[]{:S(2)}) collective-permute-start(bf16[2,128,128]{2,1,0:T(8,128)(2,1)S(1)} %get-tuple-element.52), channel_id=1, source_target_pairs={{0,8},{8,0},{16,24},{24,16},{1,9},{9,1},{17,25},{25,17},{2,10},{10... | collective-permute-start | bytes 196616 | tf_op jit(solution)/shard_map/ppermute | solution.py:426
  21.8 9.7 %collective-permute-start.8 = (bf16[2,128,128]{2,1,0:T(8,128)(2,1)S(1)}, bf16[2,128,128]{2,1,0:T(8,128)(2,1)S(1)}, u32[]{:S(2)}, u32[]{:S(2)}) collective-permute-start(bf16[2,128,128]{2,1,0:T(8,128)(2,1)S(1)} %get-tuple-element.51), channel_id=1, source_target_pairs={{0,16},{8,24},{16,0},{24,8},{1,17},{9,25},{17,1},{25,9},{2,18},{10... | collective-permute-start | bytes 196616 | tf_op jit(solution)/shard_map/ppermute | solution.py:426
  25.3 6.2 %collective-permute-start.9 = (bf16[2,128,128]{2,1,0:T(8,128)(2,1)S(1)}, bf16[2,128,128]{2,1,0:T(8,128)(2,1)S(1)}, u32[]{:S(2)}, u32[]{:S(2)}) collective-permute-start(bf16[2,128,128]{2,1,0:T(8,128)(2,1)S(1)} %get-tuple-element.50), channel_id=1, source_target_pairs={{0,24},{8,16},{16,8},{24,0},{1,25},{9,17},{17,9},{25,1},{2,26},{10... | collective-permute-start | bytes 196616 | tf_op jit(solution)/shard_map/ppermute | solution.py:426
  31.4 1.3 %collective-permute-start.10 = (f32[2,2,16,256]{3,2,1,0:T(8,128)S(1)}, f32[2,2,16,256]{3,2,1,0:T(8,128)S(1)}, u32[]{:S(2)}, u32[]{:S(2)}) collective-permute-start(f32[2,2,16,256]{3,2,1,0:T(8,128)S(1)} %get-tuple-element.43), channel_id=1, source_target_pairs={{0,2},{2,0},{1,3},{3,1},{4,6},{6,4},{5,7},{7,5},{8,10},{10,8},{9,1... | collective-permute-start | bytes 196616 | tf_op jit(solution)/shard_map/ppermute | solution.py:426
  32.7 3.9 %collective-permute-start.11 = (f32[2,16,256]{2,1,0:T(8,128)S(1)}, f32[2,16,256]{2,1,0:T(8,128)S(1)}, u32[]{:S(2)}, u32[]{:S(2)}) collective-permute-start(f32[2,16,256]{2,1,0:T(8,128)S(1)} %fusion), channel_id=1, source_target_pairs={{0,1},{1,0},{2,3},{3,2},{4,5},{5,4},{6,7},{7,6},{8,9},{9,8},{10,11... | collective-permute-start | bytes 98312 | tf_op jit(solution)/shard_map/ppermute | solution.py:426

commit v12 on v11

--- a/solution.py
+++ b/solution.py
@@ -92,6 +92,7 @@
     ]
     for copy in copies:
         copy.start()
+    refs[2 * count + 1][...] = jnp.zeros((8, LANES), jnp.float32)
     for copy in copies:
         copy.wait()
 
@@ -101,12 +102,16 @@
     count = len(arrays)
     return pl.pallas_call(
         functools.partial(stage_kernel, count),
-        out_shape=[jax.ShapeDtypeStruct(one.shape, one.dtype) for one in arrays],
+        out_shape=[jax.ShapeDtypeStruct(one.shape, one.dtype) for one in arrays]
+        + [jax.ShapeDtypeStruct((8, LANES), jnp.float32)],
         in_specs=[pl.BlockSpec(memory_space=pltpu.HBM)] * count
         + [pl.BlockSpec(memory_space=pl.ANY)],
-        out_specs=[pl.BlockSpec(memory_space=pltpu.VMEM)] * count,
+        out_specs=[pl.BlockSpec(memory_space=pltpu.VMEM)] * (count + 1),
         scratch_shapes=[pltpu.SemaphoreType.DMA((count,))],
         compiler_params=pltpu.CompilerParams(vmem_limit_bytes=VMEM_LIMIT),
+        cost_estimate=pl.CostEstimate(
+            flops=0, bytes_accessed=2 * sum(one.nbytes for one in arrays), transcendentals=0
+        ),
         name="stage",
     )(*kept, pltpu.with_memory_space_constraint(after, pltpu.HBM))
 
@@ -434,8 +439,16 @@
     place = jnp.stack([lax.axis_index(axis) for axis in ("z", "y", "core", "plane")])
     other_codes = exchange(shift_codes, "core", 2, 1)
     other_frames = exchange(frames, "core", 2, 1)
-    staged, *bands = stage([frames, *tap_constants(block)], template)
-    pieces = [template] + [exchange(template, "z", depth, turn) for turn in range(1, depth)]
+    staged, *bands, token = stage([frames, *tap_constants(block)], template)
+    pieces, turn = [template], depth // 2
+    while turn:
+        held = pieces[0] if len(pieces) == 1 else jnp.concatenate(pieces, axis=0)
+        fetched = exchange(held, "z", depth, turn)
+        if turn > 1:
+            fetched, token = lax.optimization_barrier((fetched, token))
+            fetched = [fetched[at * own : (at + 1) * own] for at in range(len(pieces))]
+            pieces = [piece for pair in zip(pieces, fetched) for piece in pair]
+        turn //= 2
     averages, correlation = [], 0.0
     volumes = vol_dev * depth * 4
     for p in range(pl_dev):
@@ -444,8 +457,10 @@
         (far_sums,) = warp_sums(*work, bands, template, 1, *sizes)
         taken = exchange(far_sums, "y", 2, 1)
         near_sums = warp_sums(*work, bands, far_sums, 0, *sizes)
-        pieces, near_sums = lax.optimization_barrier((pieces, near_sums))
-        near = jnp.concatenate([piece[:, p] for piece in pieces], axis=0)
+        kept, got, near_sums = lax.optimization_barrier((held, fetched, near_sums))
+        near = jnp.stack(
+            [one[:, p].reshape(depth // 2, own, block, block) for one in (kept, got)], axis=1
+        ).reshape(depth * own, block, block)
         far = exchange(near, "y", 2, 1)
         sums = [
             one.astype(jnp.float32) + taken[step * own : (step + 1) * own].astype(jnp.float32)
@@ -455,7 +470,7 @@
             exchange(sums[turn].astype(jnp.bfloat16), "z", depth, turn) for turn in range(1, depth)
         ]
         sizes = (planes, depth, own)
-        (part,) = lag_windows(*work, near, sums[0], 0, *sizes)
+        (part,) = lag_windows(*work, near, near_sums[0], 0, *sizes)
         *keep, give = lag_windows(*work, far, part, 1, *sizes)
         keep, moved = lax.optimization_barrier((keep, moved))
         total = sum((one.astype(jnp.float32) for one in moved), sums[0])

time: 37.4 us -> 36.7 us (0.981)
  waiting for transfers between devices: 6.86 us -> 5.69 us
  Pallas kernels: 13.9 us -> 14.5 us
    ppermute x12 -> x11, waiting for transfers between devices: 6.86 us -> 5.69 us  [exchange(): return lax.ppermute(value, axes, [(at, at ^ turn) for at in range(size)])]
    pallas_call x1, Pallas kernels: 2.13 us -> 2.74 us  [stage(): pl.pallas_call(functools.partial(stage_kernel, count), out_shape=[jax.Sha...]
    ppermute x12 -> x11, starting transfers between devices: 14.1 us -> 14.1 us  [exchange(): return lax.ppermute(value, axes, [(at, at ^ turn) for at in range(size)])]
  transfers between devices with their start and end apart: 12 -> 11, of which waited for: 3 -> 4; matrix products, arithmetic and copies ran while one was open for 2% -> 2% of each run, Pallas kernels for 37% -> 40%
where the time goes in v12:
time: 36.7 us; the launch traced here: 36.6 us
  Pallas kernels  14.5 us (40%)
  starting transfers between devices  14.1 us (38%)
  waiting for transfers between devices  5.69 us (16%)
  other arithmetic  1.51 us (4%)
  between operations  0.75 us (2%)
    ppermute x11, starting transfers between devices, exchange(): return lax.ppermute(value, axes, [(at, at ^ turn) for at in range(size)])  14.1 us
    pallas_call x2, Pallas kernels, lag_windows(): pl.pallas_call(functools.partial(spectrum_kernel, vols, across, block, ow...  6.07 us
    ppermute x11, waiting for transfers between devices, exchange(): return lax.ppermute(value, axes, [(at, at ^ turn) for at in range(size)])  5.69 us
    pallas_call x2, Pallas kernels, warp_sums(): pl.pallas_call(functools.partial(warp_kernel, down, across, block, own, o...  5.67 us
    pallas_call x1, Pallas kernels, stage(): pl.pallas_call(functools.partial(stage_kernel, count), out_shape=[jax.Sha...  2.74 us
  transfers between devices with their start and end apart: 11, of which 4 were waited for; matrix products, arithmetic and copies ran while one was open for 2% of the time, Pallas kernels for 40%

profile of v12, /device:TPU:0, one launch (start us, length us, event | category | flops | bytes accessed | tf_op | source)
XLA Modules:
  0.0 36.6 jit_solution(6028786585662750332)
XLA Ops:
  0.6 0.5 %collective-permute-start.1 = (bf16[2,1,512,1024]{3,2,0,1:T(8,128)(2,1)}, bf16[2,1,512,1024]{3,2,0,1:T(8,128)(2,1)S(1)}, u32[]{:S(2)}, u32[]{:S(2)}) collective-permute-start(bf16[2,1,512,1024]{3,2,0,1:T(8,128)(2,1)} %bitcast.38), channel_id=1, source_target_pairs={{0,2},{2,0},{1,3},{3,1},{4,6},{6,4},{5,7},{7,5},{8,10},{10,8},{9,1... | collective-permute-start | bytes 6291464 | tf_op jit(solution)/shard_map/ppermute | solution.py:431
  1.2 0.1 collective-permute-start
  1.2 4.0 %collective-permute-start.2 = (bf16[2,1,128,128]{3,2,1,0:T(8,128)(2,1)}, bf16[2,1,128,128]{3,2,1,0:T(8,128)(2,1)S(1)}, u32[]{:S(2)}, u32[]{:S(2)}) collective-permute-start(bf16[2,1,128,128]{3,2,1,0:T(8,128)(2,1)} %refs_7_.1), channel_id=1, source_target_pairs={{0,16},{8,24},{16,0},{24,8},{1,17},{9,25},{17,1},{25,9},{2,18},{10... | collective-permute-start | bytes 196616 | tf_op jit(solution)/shard_map/ppermute | solution.py:431
  5.3 2.7 %stage.1 = (bf16[2,1,512,1024]{3,2,1,0:T(8,128)(2,1)S(1)}, f32[16,176,128]{2,1,0:T(8,128)S(1)}, f32[16,2,32,128]{3,2,1,0:T(8,128)S(1)}, f32[8,128]{1,0:T(8,128)}) custom-call(bf16[2,1,512,1024]{3,2,1,0:T(8,128)(2,1)} %refs_0_.1, f32[16,176,128]{2,1,0:T(8,128)} %constant.28.clone.refs_1_, f32[16,2,32,128]{3,2,1,0:T(8,128)} %constant.29.clone.refs_2_, ...), custom_call_target="tpu_custom_call" | custom-call | bytes 8126464 | tf_op jit(solution)/shard_map/stage/pallas_call | solution.py:103
  8.0 0.1 pad_add_fusion.refs_0_
  8.1 1.1 %collective-permute-done.2 = bf16[2,1,128,128]{3,2,1,0:T(8,128)(2,1)S(1)} collective-permute-done((bf16[2,1,128,128]{3,2,1,0:T(8,128)(2,1)}, bf16[2,1,128,128]{3,2,1,0:T(8,128)(2,1)S(1)}, u32[]{:S(2)}, u32[]{:S(2)}) %collective-permute-start.2) | collective-permute-done | bytes 65568 | tf_op jit(solution)/shard_map/ppermute | solution.py:431
  9.2 0.9 %collective-permute-start.3 = (bf16[4,1,128,128]{3,2,1,0:T(8,128)(2,1)S(1)}, bf16[4,1,128,128]{3,2,1,0:T(8,128)(2,1)S(1)}, u32[]{:S(2)}, u32[]{:S(2)}) collective-permute-start(bf16[4,1,128,128]{3,2,1,0:T(8,128)(2,1)S(1)} %pad_maximum_fusion.1), channel_id=1, source_target_pairs={{0,8},{8,0},{16,24},{24,16},{1,9},{9,1},{17,25},{25,17},{2,10},{10... | collective-permute-start | bytes 393224 | tf_op jit(solution)/shard_map/ppermute | solution.py:431
  10.1 2.8 %warp.2.refs_7_ = bf16[8,128,128]{2,1,0:T(8,128)(2,1)S(1)} custom-call(s32[4]{0:T(128)S(1)} %pad_add_fusion.refs_0_, s32[2,2,32]{2,1,0:T(2,128)S(1)} %copy-done.5, s32[2,2,32]{2,1,0:T(2,128)S(1)} %collective-permute-done.refs_2_, bf16[2,512,1024]{2,1,0:T(8,128)(2,1)S(1)} %bitcast.32, bf16[2,512,1024]{2,1,0:T(8,128)(2,1)S(1)} %bitcast.28, ...), custom_call_target="tpu_custom_call" | custom-call | flops 2147483648 | bytes 4718592 | tf_op jit(solution)/shard_map/warp/pallas_call | solution.py:221
  13.0 1.6 %collective-permute-start.5 = (bf16[8,128,128]{2,1,0:T(8,128)(2,1)S(1)}, bf16[8,128,128]{2,1,0:T(8,128)(2,1)S(1)}, u32[]{:S(2)}, u32[]{:S(2)}) collective-permute-start(bf16[8,128,128]{2,1,0:T(8,128)(2,1)S(1)} %warp.2.refs_7_), channel_id=1, source_target_pairs={{0,4},{4,0},{1,5},{5,1},{2,6},{6,2},{3,7},{7,3},{8,12},{12,8},{9,1... | collective-permute-start | bytes 786440 | tf_op jit(solution)/shard_map/ppermute | solution.py:431
  14.6 2.8 %warp.3 = (bf16[2,128,128]{2,1,0:T(8,128)(2,1)S(1)}, bf16[2,128,128]{2,1,0:T(8,128)(2,1)S(1)}, bf16[2,128,128]{2,1,0:T(8,128)(2,1)S(1)}, bf16[2,128,128]{2,1,0:T(8,128)(2,1)S(1)}) custom-call(s32[4]{0:T(128)S(1)} %pad_add_fusion.refs_0_, s32[2,2,32]{2,1,0:T(2,128)S(1)} %copy-done.5, s32[2,2,32]{2,1,0:T(2,128)S(1)} %collective-permute-done.refs_2_, ...), custom_call_target="tpu_custom_call" | custom-call | flops 2147483648 | bytes 4718592 | tf_op jit(solution)/shard_map/warp/pallas_call | solution.py:221
  17.5 0.6 %collective-permute-start.4 = (bf16[8,128,128]{2,1,0:T(8,128)(2,1)S(1)}, bf16[8,128,128]{2,1,0:T(8,128)(2,1)S(1)}, u32[]{:S(2)}, u32[]{:S(2)}) collective-permute-start(bf16[8,128,128]{2,1,0:T(8,128)(2,1)S(1)} %bitcast.36), channel_id=1, source_target_pairs={{0,4},{4,0},{1,5},{5,1},{2,6},{6,2},{3,7},{7,3},{8,12},{12,8},{9,1... | collective-permute-start | bytes 786440 | tf_op jit(solution)/shard_map/ppermute | solution.py:431
  18.1 2.9 %lag_windows.2.refs_10_ = f32[4,512,128]{2,1,0:T(8,128)S(1)} custom-call(s32[4]{0:T(128)S(1)} %pad_add_fusion.refs_0_, s32[2,2,32]{2,1,0:T(2,128)S(1)} %copy-done.5, s32[2,2,32]{2,1,0:T(2,128)S(1)} %collective-permute-done.refs_2_, bf16[160,128]{1,0:T(8,128)(2,1)S(1)} %copy-done.3, bf16[256,256]{1,0:T(8,128)(2,1)S(1)} %copy-done.1, ...), custom_call_target="tpu_custom_call" | custom-call | flops 3221225472 | bytes 4718592 | tf_op jit(solution)/shard_map/lag_windows/pallas_call | solution.py:410
  21.0 1.3 %collective-permute-done.5 = bf16[8,128,128]{2,1,0:T(8,128)(2,1)S(1)} collective-permute-done((bf16[8,128,128]{2,1,0:T(8,128)(2,1)S(1)}, bf16[8,128,128]{2,1,0:T(8,128)(2,1)S(1)}, u32[]{:S(2)}, u32[]{:S(2)}) %collective-permute-start.5) | collective-permute-done | bytes 262176 | tf_op jit(solution)/shard_map/ppermute | solution.py:431
  22.3 0.1 add_convert_fusion
  22.4 0.5 %collective-permute-start.6 = (bf16[2,128,128]{2,1,0:T(8,128)(2,1)S(1)}, bf16[2,128,128]{2,1,0:T(8,128)(2,1)S(1)}, u32[]{:S(2)}, u32[]{:S(2)}) collective-permute-start(bf16[2,128,128]{2,1,0:T(8,128)(2,1)S(1)} %get-tuple-element.48), channel_id=1, source_target_pairs={{0,8},{8,0},{16,24},{24,16},{1,9},{9,1},{17,25},{25,17},{2,10},{10... | collective-permute-start | bytes 196616 | tf_op jit(solution)/shard_map/ppermute | solution.py:431
  22.9 2.9 %collective-permute-start.7 = (bf16[2,128,128]{2,1,0:T(8,128)(2,1)S(1)}, bf16[2,128,128]{2,1,0:T(8,128)(2,1)S(1)}, u32[]{:S(2)}, u32[]{:S(2)}) collective-permute-start(bf16[2,128,128]{2,1,0:T(8,128)(2,1)S(1)} %get-tuple-element.47), channel_id=1, source_target_pairs={{0,16},{8,24},{16,0},{24,8},{1,17},{9,25},{17,1},{25,9},{2,18},{10... | collective-permute-start | bytes 196616 | tf_op jit(solution)/shard_map/ppermute | solution.py:431
  25.8 1.4 %collective-permute-start.8 = (bf16[2,128,128]{2,1,0:T(8,128)(2,1)S(1)}, bf16[2,128,128]{2,1,0:T(8,128)(2,1)S(1)}, u32[]{:S(2)}, u32[]{:S(2)}) collective-permute-start(bf16[2,128,128]{2,1,0:T(8,128)(2,1)S(1)} %get-tuple-element.46), channel_id=1, source_target_pairs={{0,24},{8,16},{16,8},{24,0},{1,25},{9,17},{17,9},{25,1},{2,26},{10... | collective-permute-start | bytes 196616 | tf_op jit(solution)/shard_map/ppermute | solution.py:431
  27.2 3.2 %lag_windows.3 = (f32[2,16,256]{2,1,0:T(8,128)S(1)}, f32[2,16,256]{2,1,0:T(8,128)S(1)}, f32[2,2,16,256]{3,2,1,0:T(8,128)S(1)}) custom-call(s32[4]{0:T(128)S(1)} %pad_add_fusion.refs_0_, s32[2,2,32]{2,1,0:T(2,128)S(1)} %copy-done.5, s32[2,2,32]{2,1,0:T(2,128)S(1)} %collective-permute-done.refs_2_, bf16[160,128]{1,0:T(8,128)(2,1)S(1)} %copy-done.3, ...), custom_call_target="tpu_custom_call" | custom-call | flops 805306368 | bytes 4718592 | tf_op jit(solution)/shard_map/lag_windows/pallas_call | solution.py:410
  30.4 0.1 collective-permute-start.9
  30.5 1.5 %collective-permute-done.8 = bf16[2,128,128]{2,1,0:T(8,128)(2,1)S(1)} collective-permute-done((bf16[2,128,128]{2,1,0:T(8,128)(2,1)S(1)}, bf16[2,128,128]{2,1,0:T(8,128)(2,1)S(1)}, u32[]{:S(2)}, u32[]{:S(2)}) %collective-permute-start.8) | collective-permute-done | bytes 65568 | tf_op jit(solution)/shard_map/ppermute | solution.py:431
  32.0 1.6 %collective-permute-start.10 = (f32[2,16,256]{2,1,0:T(8,128)S(1)}, f32[2,16,256]{2,1,0:T(8,128)S(1)}, u32[]{:S(2)}, u32[]{:S(2)}) collective-permute-start(f32[2,16,256]{2,1,0:T(8,128)S(1)} %fusion), channel_id=1, source_target_pairs={{0,1},{1,0},{2,3},{3,2},{4,5},{5,4},{6,7},{7,6},{8,9},{9,8},{10,11... | collective-permute-start | bytes 98312 | tf_op jit(solution)/shard_map/ppermute | solution.py:431
  33.5 0.7 %multiply_bitcast_fusion = f32[2,1,128,128]{3,2,1,0:T(8,128)} fusion(bf16[2,128,128]{2,1,0:T(8,128)(2,1)S(1)} %collective-permute-done.8, bf16[2,128,128]{2,1,0:T(8,128)(2,1)S(1)} %collective-permute-done.7, bf16[2,128,128]{2,1,0:T(8,128)(2,1)S(1)} %collective-permute-done.6, bf16[2,128,128]{2,1,0:T(8,128)(2,1)S(1)} %get-tuple-element.32.refs_10_, ...), kind=kLoop, calls=%fused_computation.2 | loop fusion | flops 327680 | bytes 458752
  34.2 1.7 %collective-permute-done.10 = f32[2,16,256]{2,1,0:T(8,128)S(1)} collective-permute-done((f32[2,16,256]{2,1,0:T(8,128)S(1)}, f32[2,16,256]{2,1,0:T(8,128)S(1)}, u32[]{:S(2)}, u32[]{:S(2)}) %collective-permute-start.10) | collective-permute-done | bytes 32800 | tf_op jit(solution)/shard_map/ppermute | solution.py:431
  36.0 0.6 %fusion.2 = f32[2,16,256]{2,1,0:T(8,128)} fusion(f32[2,16,256]{2,1,0:T(8,128)S(1)} %collective-permute-done.10, f32[2,16,256]{2,1,0:T(8,128)S(1)} %get-tuple-element.38, f32[2,2,16,256]{3,2,1,0:T(8,128)S(1)} %collective-permute-done.9), kind=kLoop, calls=%fused_computation.10 | loop fusion | flops 16384 | bytes 131072 | tf_op jit(solution)/shard_map/add | solution.py:481
  (22 shorter events, 0.1 us)
Async XLA Ops:
  0.6 8.6 %copy-start = (bf16[2,1,128,128]{3,2,1,0:T(8,128)(2,1)S(1)}, bf16[2,1,128,128]{3,2,1,0:T(8,128)(2,1)}, u32[]{:S(2)}) copy-start(bf16[2,1,128,128]{3,2,1,0:T(8,128)(2,1)} %refs_7_.1) | copy-start | bytes 196612
  0.6 9.5 %collective-permute-start.1 = (bf16[2,1,512,1024]{3,2,0,1:T(8,128)(2,1)}, bf16[2,1,512,1024]{3,2,0,1:T(8,128)(2,1)S(1)}, u32[]{:S(2)}, u32[]{:S(2)}) collective-permute-start(bf16[2,1,512,1024]{3,2,0,1:T(8,128)(2,1)} %bitcast.38), channel_id=1, source_target_pairs={{0,2},{2,0},{1,3},{3,1},{4,6},{6,4},{5,7},{7,5},{8,10},{10,8},{9,1... | collective-permute-start | bytes 6291464 | tf_op jit(solution)/shard_map/ppermute | solution.py:431
  1.2 9.0 %collective-permute-start = (s32[2,2,32]{2,1,0:T(2,128)}, s32[2,2,32]{2,1,0:T(2,128)S(1)}, u32[]{:S(2)}, u32[]{:S(2)}) collective-permute-start(s32[2,2,32]{2,1,0:T(2,128)} %refs_1_.8), channel_id=1, source_target_pairs={{0,2},{2,0},{1,3},{3,1},{4,6},{6,4},{5,7},{7,5},{8,10},{10,8},{9,1... | collective-permute-start | bytes 1544 | tf_op jit(solution)/shard_map/ppermute | solution.py:431
  1.2 8.0 %collective-permute-start.2 = (bf16[2,1,128,128]{3,2,1,0:T(8,128)(2,1)}, bf16[2,1,128,128]{3,2,1,0:T(8,128)(2,1)S(1)}, u32[]{:S(2)}, u32[]{:S(2)}) collective-permute-start(bf16[2,1,128,128]{3,2,1,0:T(8,128)(2,1)} %refs_7_.1), channel_id=1, source_target_pairs={{0,16},{8,24},{16,0},{24,8},{1,17},{9,25},{17,1},{25,9},{2,18},{10... | collective-permute-start | bytes 196616 | tf_op jit(solution)/shard_map/ppermute | solution.py:431
  5.3 4.9 %copy-start.5 = (s32[2,2,32]{2,1,0:T(2,128)S(1)}, s32[2,2,32]{2,1,0:T(2,128)}, u32[]{:S(2)}) copy-start(s32[2,2,32]{2,1,0:T(2,128)} %refs_1_.8) | copy-start | bytes 1540
  9.2 8.2 %collective-permute-start.3 = (bf16[4,1,128,128]{3,2,1,0:T(8,128)(2,1)S(1)}, bf16[4,1,128,128]{3,2,1,0:T(8,128)(2,1)S(1)}, u32[]{:S(2)}, u32[]{:S(2)}) collective-permute-start(bf16[4,1,128,128]{3,2,1,0:T(8,128)(2,1)S(1)} %pad_maximum_fusion.1), channel_id=1, source_target_pairs={{0,8},{8,0},{16,24},{24,16},{1,9},{9,1},{17,25},{25,17},{2,10},{10... | collective-permute-start | bytes 393224 | tf_op jit(solution)/shard_map/ppermute | solution.py:431
  13.0 5.1 %copy-start.1 = (bf16[256,256]{1,0:T(8,128)(2,1)S(1)}, bf16[256,256]{1,0:T(8,128)(2,1)}, u32[]{:S(2)}) copy-start(bf16[256,256]{1,0:T(8,128)(2,1)} %constant.31.clone.refs_4_) | copy-start | bytes 393220
  13.0 5.1 %copy-start.2 = (bf16[256,128]{1,0:T(8,128)(2,1)S(1)}, bf16[256,128]{1,0:T(8,128)(2,1)}, u32[]{:S(2)}) copy-start(bf16[256,128]{1,0:T(8,128)(2,1)} %constant.33.clone.refs_6_) | copy-start | bytes 196612
  13.0 5.1 %copy-start.3 = (bf16[160,128]{1,0:T(8,128)(2,1)S(1)}, bf16[160,128]{1,0:T(8,128)(2,1)}, u32[]{:S(2)}) copy-start(bf16[160,128]{1,0:T(8,128)(2,1)} %constant.30.clone.refs_3_) | copy-start | bytes 122884
  13.0 5.1 %copy-start.4 = (bf16[64,160]{1,0:T(8,128)(2,1)S(1)}, bf16[64,160]{1,0:T(8,128)(2,1)}, u32[]{:S(2)}) copy-start(bf16[64,160]{1,0:T(8,128)(2,1)} %constant.32.clone.refs_5_) | copy-start | bytes 61444
  13.0 9.3 %collective-permute-start.5 = (bf16[8,128,128]{2,1,0:T(8,128)(2,1)S(1)}, bf16[8,128,128]{2,1,0:T(8,128)(2,1)S(1)}, u32[]{:S(2)}, u32[]{:S(2)}) collective-permute-start(bf16[8,128,128]{2,1,0:T(8,128)(2,1)S(1)} %warp.2.refs_7_), channel_id=1, source_target_pairs={{0,4},{4,0},{1,5},{5,1},{2,6},{6,2},{3,7},{7,3},{8,12},{12,8},{9,1... | collective-permute-start | bytes 786440 | tf_op jit(solution)/shard_map/ppermute | solution.py:431
  17.5 9.7 %collective-permute-start.4 = (bf16[8,128,128]{2,1,0:T(8,128)(2,1)S(1)}, bf16[8,128,128]{2,1,0:T(8,128)(2,1)S(1)}, u32[]{:S(2)}, u32[]{:S(2)}) collective-permute-start(bf16[8,128,128]{2,1,0:T(8,128)(2,1)S(1)} %bitcast.36), channel_id=1, source_target_pairs={{0,4},{4,0},{1,5},{5,1},{2,6},{6,2},{3,7},{7,3},{8,12},{12,8},{9,1... | collective-permute-start | bytes 786440 | tf_op jit(solution)/shard_map/ppermute | solution.py:431
  22.4 8.1 %collective-permute-start.6 = (bf16[2,128,128]{2,1,0:T(8,128)(2,1)S(1)}, bf16[2,128,128]{2,1,0:T(8,128)(2,1)S(1)}, u32[]{:S(2)}, u32[]{:S(2)}) collective-permute-start(bf16[2,128,128]{2,1,0:T(8,128)(2,1)S(1)} %get-tuple-element.48), channel_id=1, source_target_pairs={{0,8},{8,0},{16,24},{24,16},{1,9},{9,1},{17,25},{25,17},{2,10},{10... | collective-permute-start | bytes 196616 | tf_op jit(solution)/shard_map/ppermute | solution.py:431
  22.9 7.6 %collective-permute-start.7 = (bf16[2,128,128]{2,1,0:T(8,128)(2,1)S(1)}, bf16[2,128,128]{2,1,0:T(8,128)(2,1)S(1)}, u32[]{:S(2)}, u32[]{:S(2)}) collective-permute-start(bf16[2,128,128]{2,1,0:T(8,128)(2,1)S(1)} %get-tuple-element.47), channel_id=1, source_target_pairs={{0,16},{8,24},{16,0},{24,8},{1,17},{9,25},{17,1},{25,9},{2,18},{10... | collective-permute-start | bytes 196616 | tf_op jit(solution)/shard_map/ppermute | solution.py:431
  25.8 6.2 %collective-permute-start.8 = (bf16[2,128,128]{2,1,0:T(8,128)(2,1)S(1)}, bf16[2,128,128]{2,1,0:T(8,128)(2,1)S(1)}, u32[]{:S(2)}, u32[]{:S(2)}) collective-permute-start(bf16[2,128,128]{2,1,0:T(8,128)(2,1)S(1)} %get-tuple-element.46), channel_id=1, source_target_pairs={{0,24},{8,16},{16,8},{24,0},{1,25},{9,17},{17,9},{25,1},{2,26},{10... | collective-permute-start | bytes 196616 | tf_op jit(solution)/shard_map/ppermute | solution.py:431
  30.4 1.6 %collective-permute-start.9 = (f32[2,2,16,256]{3,2,1,0:T(8,128)S(1)}, f32[2,2,16,256]{3,2,1,0:T(8,128)S(1)}, u32[]{:S(2)}, u32[]{:S(2)}) collective-permute-start(f32[2,2,16,256]{3,2,1,0:T(8,128)S(1)} %get-tuple-element.39), channel_id=1, source_target_pairs={{0,2},{2,0},{1,3},{3,1},{4,6},{6,4},{5,7},{7,5},{8,10},{10,8},{9,1... | collective-permute-start | bytes 196616 | tf_op jit(solution)/shard_map/ppermute | solution.py:431
  32.0 4.0 %collective-permute-start.10 = (f32[2,16,256]{2,1,0:T(8,128)S(1)}, f32[2,16,256]{2,1,0:T(8,128)S(1)}, u32[]{:S(2)}, u32[]{:S(2)}) collective-permute-start(f32[2,16,256]{2,1,0:T(8,128)S(1)} %fusion), channel_id=1, source_target_pairs={{0,1},{1,0},{2,3},{3,2},{4,5},{5,4},{6,7},{7,6},{8,9},{9,8},{10,11... | collective-permute-start | bytes 98312 | tf_op jit(solution)/shard_map/ppermute | solution.py:431

commit v13 on v11

--- a/solution.py
+++ b/solution.py
@@ -92,6 +92,7 @@
     ]
     for copy in copies:
         copy.start()
+    refs[2 * count + 1][...] = jnp.zeros((8, LANES), jnp.float32)
     for copy in copies:
         copy.wait()
 
@@ -101,12 +102,16 @@
     count = len(arrays)
     return pl.pallas_call(
         functools.partial(stage_kernel, count),
-        out_shape=[jax.ShapeDtypeStruct(one.shape, one.dtype) for one in arrays],
+        out_shape=[jax.ShapeDtypeStruct(one.shape, one.dtype) for one in arrays]
+        + [jax.ShapeDtypeStruct((8, LANES), jnp.float32)],
         in_specs=[pl.BlockSpec(memory_space=pltpu.HBM)] * count
         + [pl.BlockSpec(memory_space=pl.ANY)],
-        out_specs=[pl.BlockSpec(memory_space=pltpu.VMEM)] * count,
+        out_specs=[pl.BlockSpec(memory_space=pltpu.VMEM)] * (count + 1),
         scratch_shapes=[pltpu.SemaphoreType.DMA((count,))],
         compiler_params=pltpu.CompilerParams(vmem_limit_bytes=VMEM_LIMIT),
+        cost_estimate=pl.CostEstimate(
+            flops=0, bytes_accessed=2 * sum(one.nbytes for one in arrays), transcendentals=0
+        ),
         name="stage",
     )(*kept, pltpu.with_memory_space_constraint(after, pltpu.HBM))
 
@@ -434,14 +439,17 @@
     place = jnp.stack([lax.axis_index(axis) for axis in ("z", "y", "core", "plane")])
     other_codes = exchange(shift_codes, "core", 2, 1)
     other_frames = exchange(frames, "core", 2, 1)
-    staged, *bands = stage([frames, *tap_constants(block)], template)
-    pieces = [template] + [exchange(template, "z", depth, turn) for turn in range(1, depth)]
+    staged, *bands, token = stage([frames, *tap_constants(block)], template)
+    later, token = lax.optimization_barrier((template, token))
+    pieces = [template]
+    for turn in range(1, depth):
+        pieces.append(exchange(later if turn == depth - 1 else template, "z", depth, turn))
     averages, correlation = [], 0.0
     volumes = vol_dev * depth * 4
     for p in range(pl_dev):
         work = (place, shift_codes, other_codes, staged[:, p], other_frames[:, p])
         sizes = (depth, block, own)
-        (far_sums,) = warp_sums(*work, bands, template, 1, *sizes)
+        (far_sums,) = warp_sums(*work, bands, token, 1, *sizes)
         taken = exchange(far_sums, "y", 2, 1)
         near_sums = warp_sums(*work, bands, far_sums, 0, *sizes)
         pieces, near_sums = lax.optimization_barrier((pieces, near_sums))
@@ -455,7 +463,7 @@
             exchange(sums[turn].astype(jnp.bfloat16), "z", depth, turn) for turn in range(1, depth)
         ]
         sizes = (planes, depth, own)
-        (part,) = lag_windows(*work, near, sums[0], 0, *sizes)
+        (part,) = lag_windows(*work, near, near_sums[0], 0, *sizes)
         *keep, give = lag_windows(*work, far, part, 1, *sizes)
         keep, moved = lax.optimization_barrier((keep, moved))
         total = sum((one.astype(jnp.float32) for one in moved), sums[0])

time: 37.4 us -> 40.6 us (1.086)
  local copies, waits for them, and re-layouts: 0.04 us -> 4.79 us
  waiting for transfers between devices: 6.86 us -> 4.45 us
  other arithmetic: 1.51 us -> 2.44 us
    unnamed x12 -> x18, local copies, waits for them, and re-layouts: 0.04 us -> 4.79 us
    ppermute x12, waiting for transfers between devices: 6.86 us -> 4.45 us  [exchange(): return lax.ppermute(value, axes, [(at, at ^ turn) for at in range(size)])]
    concatenate x1, other arithmetic: 0.04 us -> 0.97 us  [on_device(): near = jnp.concatenate([piece[:, p] for piece in pieces], axis=0)]
  transfers between devices with their start and end apart: 12 -> 12, of which waited for: 3 -> 5; matrix products, arithmetic and copies ran while one was open for 2% -> 4% of each run, Pallas kernels for 37% -> 34%
where the time goes in v13:
time: 40.6 us; the launch traced here: 40.4 us
  starting transfers between devices  14.1 us (35%)
  Pallas kernels  13.9 us (34%)
  local copies, waits for them, and re-layouts  4.79 us (12%)
  waiting for transfers between devices  4.45 us (11%)
  other arithmetic  2.44 us (6%)
  between operations  0.77 us (2%)
    ppermute x12, starting transfers between devices, exchange(): return lax.ppermute(value, axes, [(at, at ^ turn) for at in range(size)])  14.1 us
    pallas_call x2, Pallas kernels, lag_windows(): pl.pallas_call(functools.partial(spectrum_kernel, vols, across, block, ow...  6.08 us
    pallas_call x2, Pallas kernels, warp_sums(): pl.pallas_call(functools.partial(warp_kernel, down, across, block, own, o...  5.68 us
    unnamed x18, local copies, waits for them, and re-layouts  4.79 us
    ppermute x12, waiting for transfers between devices, exchange(): return lax.ppermute(value, axes, [(at, at ^ turn) for at in range(size)])  4.45 us
    pallas_call x1, Pallas kernels, stage(): pl.pallas_call(functools.partial(stage_kernel, count), out_shape=[jax.Sha...  2.13 us
    concatenate x1, other arithmetic, on_device(): near = jnp.concatenate([piece[:, p] for piece in pieces], axis=0)  0.97 us
  transfers between devices with their start and end apart: 12, of which 5 were waited for; matrix products, arithmetic and copies ran while one was open for 4% of the time, Pallas kernels for 34%

profile of v13, /device:TPU:0, one launch (start us, length us, event | category | flops | bytes accessed | tf_op | source)
XLA Modules:
  0.0 40.4 jit_solution(728788919902773565)
XLA Ops:
  0.6 0.5 %collective-permute-start.1 = (bf16[2,1,512,1024]{3,2,0,1:T(8,128)(2,1)}, bf16[2,1,512,1024]{3,2,0,1:T(8,128)(2,1)S(1)}, u32[]{:S(2)}, u32[]{:S(2)}) collective-permute-start(bf16[2,1,512,1024]{3,2,0,1:T(8,128)(2,1)} %bitcast.35), channel_id=1, source_target_pairs={{0,2},{2,0},{1,3},{3,1},{4,6},{6,4},{5,7},{7,5},{8,10},{10,8},{9,1... | collective-permute-start | bytes 6291464 | tf_op jit(solution)/shard_map/ppermute | solution.py:431
  1.2 2.6 %collective-permute-start.2 = (bf16[2,1,128,128]{3,2,0,1:T(8,128)(2,1)}, bf16[2,1,128,128]{3,2,0,1:T(8,128)(2,1)}, u32[]{:S(2)}, u32[]{:S(2)}) collective-permute-start(bf16[2,1,128,128]{3,2,0,1:T(8,128)(2,1)} %bitcast.7), channel_id=1, source_target_pairs={{0,8},{8,0},{16,24},{24,16},{1,9},{9,1},{17,25},{25,17},{2,10},{10... | collective-permute-start | bytes 196616 | tf_op jit(solution)/shard_map/ppermute | solution.py:431
  3.8 2.6 %collective-permute-start.3 = (bf16[2,1,128,128]{3,2,0,1:T(8,128)(2,1)}, bf16[2,1,128,128]{3,2,0,1:T(8,128)(2,1)}, u32[]{:S(2)}, u32[]{:S(2)}) collective-permute-start(bf16[2,1,128,128]{3,2,0,1:T(8,128)(2,1)} %bitcast.7), channel_id=1, source_target_pairs={{0,16},{8,24},{16,0},{24,8},{1,17},{9,25},{17,1},{25,9},{2,18},{10... | collective-permute-start | bytes 196616 | tf_op jit(solution)/shard_map/ppermute | solution.py:431
  6.4 2.1 %stage.1 = (bf16[2,1,512,1024]{3,2,1,0:T(8,128)(2,1)S(1)}, f32[16,176,128]{2,1,0:T(8,128)S(1)}, f32[16,2,32,128]{3,2,1,0:T(8,128)S(1)}, f32[8,128]{1,0:T(8,128)S(1)}) custom-call(bf16[2,1,512,1024]{3,2,1,0:T(8,128)(2,1)} %refs_0_.1, f32[16,176,128]{2,1,0:T(8,128)} %constant.28.clone.refs_1_, f32[16,2,32,128]{3,2,1,0:T(8,128)} %constant.29.clone.refs_2_, ...), custom_call_target="tpu_custom_call" | custom-call | bytes 8126464 | tf_op jit(solution)/shard_map/stage/pallas_call | solution.py:103
  8.5 1.3 %copy-done = bf16[2,1,512,1024]{3,2,1,0:T(8,128)(2,1)} copy-done((bf16[2,1,512,1024]{3,2,1,0:T(8,128)(2,1)}, bf16[2,1,512,1024]{3,2,1,0:T(8,128)(2,1)S(1)}, u32[]{:S(2)}) %copy-start) | copy-done | bytes 2097176
  9.9 0.8 %copy-done.7 = f32[16,2,32,128]{3,2,1,0:T(8,128)} copy-done((f32[16,2,32,128]{3,2,1,0:T(8,128)}, f32[16,2,32,128]{3,2,1,0:T(8,128)S(1)}, u32[]{:S(2)}) %copy-start.7) | copy-done | bytes 524312
  10.8 1.6 %copy-done.1 = bf16[2,1,512,1024]{3,2,1,0:T(8,128)(2,1)S(1)} copy-done((bf16[2,1,512,1024]{3,2,1,0:T(8,128)(2,1)S(1)}, bf16[2,1,512,1024]{3,2,1,0:T(8,128)(2,1)}, u32[]{:S(2)}) %copy-start.1) | copy-done | bytes 2097176
  12.4 1.0 %copy-done.8 = f32[16,2,32,128]{3,2,1,0:T(8,128)S(1)} copy-done((f32[16,2,32,128]{3,2,1,0:T(8,128)S(1)}, f32[16,2,32,128]{3,2,1,0:T(8,128)}, u32[]{:S(2)}) %copy-start.8) | copy-done | bytes 524312
  13.5 2.8 %warp.2.refs_7_ = bf16[8,128,128]{2,1,0:T(8,128)(2,1)S(1)} custom-call(s32[4]{0:T(128)S(1)} %pad_add_fusion.refs_0_, s32[2,2,32]{2,1,0:T(2,128)S(1)} %copy-done.6, s32[2,2,32]{2,1,0:T(2,128)S(1)} %collective-permute-done.refs_2_, bf16[2,512,1024]{2,1,0:T(8,128)(2,1)S(1)} %bitcast.31, bf16[2,512,1024]{2,1,0:T(8,128)(2,1)S(1)} %bitcast.27, ...), custom_call_target="tpu_custom_call" | custom-call | flops 2147483648 | bytes 4718592 | tf_op jit(solution)/shard_map/warp/pallas_call | solution.py:221
  16.3 1.8 %collective-permute-start.6 = (bf16[8,128,128]{2,1,0:T(8,128)(2,1)S(1)}, bf16[8,128,128]{2,1,0:T(8,128)(2,1)S(1)}, u32[]{:S(2)}, u32[]{:S(2)}) collective-permute-start(bf16[8,128,128]{2,1,0:T(8,128)(2,1)S(1)} %warp.2.refs_7_), channel_id=1, source_target_pairs={{0,4},{4,0},{1,5},{5,1},{2,6},{6,2},{3,7},{7,3},{8,12},{12,8},{9,1... | collective-permute-start | bytes 786440 | tf_op jit(solution)/shard_map/ppermute | solution.py:431
  18.1 2.8 %warp.3 = (bf16[2,128,128]{2,1,0:T(8,128)(2,1)S(1)}, bf16[2,128,128]{2,1,0:T(8,128)(2,1)S(1)}, bf16[2,128,128]{2,1,0:T(8,128)(2,1)S(1)}, bf16[2,128,128]{2,1,0:T(8,128)(2,1)S(1)}) custom-call(s32[4]{0:T(128)S(1)} %pad_add_fusion.refs_0_, s32[2,2,32]{2,1,0:T(2,128)S(1)} %copy-done.6, s32[2,2,32]{2,1,0:T(2,128)S(1)} %collective-permute-done.refs_2_, ...), custom_call_target="tpu_custom_call" | custom-call | flops 2147483648 | bytes 4718592 | tf_op jit(solution)/shard_map/warp/pallas_call | solution.py:221
  21.0 1.0 %pad_maximum_fusion.refs_9_ = bf16[8,128,128]{2,1,0:T(8,128)(2,1)S(1)} fusion(bf16[2,128,128]{2,1,0:T(8,128)(2,1)} %bitcast.12, bf16[2,128,128]{2,1,0:T(8,128)(2,1)} %bitcast.11, bf16[2,128,128]{2,1,0:T(8,128)(2,1)} %bitcast.10, bf16[2,128,128]{2,1,0:T(8,128)(2,1)} %bitcast.9), kind=kLoop, calls=%fused_computation | loop fusion | flops 393216 | bytes 524288 | tf_op jit(solution)/shard_map/concatenate | solution.py:456
  21.9 0.4 %collective-permute-start.5 = (bf16[8,128,128]{2,1,0:T(8,128)(2,1)S(1)}, bf16[8,128,128]{2,1,0:T(8,128)(2,1)S(1)}, u32[]{:S(2)}, u32[]{:S(2)}) collective-permute-start(bf16[8,128,128]{2,1,0:T(8,128)(2,1)S(1)} %pad_maximum_fusion.refs_9_), channel_id=1, source_target_pairs={{0,4},{4,0},{1,5},{5,1},{2,6},{6,2},{3,7},{7,3},{8,12},{12,8},{9,1... | collective-permute-start | bytes 786440 | tf_op jit(solution)/shard_map/ppermute | solution.py:431
  22.4 2.9 %lag_windows.2.refs_10_ = f32[4,512,128]{2,1,0:T(8,128)S(1)} custom-call(s32[4]{0:T(128)S(1)} %pad_add_fusion.refs_0_, s32[2,2,32]{2,1,0:T(2,128)S(1)} %copy-done.6, s32[2,2,32]{2,1,0:T(2,128)S(1)} %collective-permute-done.refs_2_, bf16[160,128]{1,0:T(8,128)(2,1)S(1)} %copy-done.4, bf16[256,256]{1,0:T(8,128)(2,1)S(1)} %copy-done.2, ...), custom_call_target="tpu_custom_call" | custom-call | flops 3221225472 | bytes 4718592 | tf_op jit(solution)/shard_map/lag_windows/pallas_call | solution.py:410
  25.6 0.7 %collective-permute-start.7 = (bf16[2,128,128]{2,1,0:T(8,128)(2,1)S(1)}, bf16[2,128,128]{2,1,0:T(8,128)(2,1)S(1)}, u32[]{:S(2)}, u32[]{:S(2)}) collective-permute-start(bf16[2,128,128]{2,1,0:T(8,128)(2,1)S(1)} %get-tuple-element.58), channel_id=1, source_target_pairs={{0,8},{8,0},{16,24},{24,16},{1,9},{9,1},{17,25},{25,17},{2,10},{10... | collective-permute-start | bytes 196616 | tf_op jit(solution)/shard_map/ppermute | solution.py:431
  26.3 3.5 %collective-permute-start.8 = (bf16[2,128,128]{2,1,0:T(8,128)(2,1)S(1)}, bf16[2,128,128]{2,1,0:T(8,128)(2,1)S(1)}, u32[]{:S(2)}, u32[]{:S(2)}) collective-permute-start(bf16[2,128,128]{2,1,0:T(8,128)(2,1)S(1)} %get-tuple-element.57), channel_id=1, source_target_pairs={{0,16},{8,24},{16,0},{24,8},{1,17},{9,25},{17,1},{25,9},{2,18},{10... | collective-permute-start | bytes 196616 | tf_op jit(solution)/shard_map/ppermute | solution.py:431
  29.7 0.3 collective-permute-start.9
  30.0 0.7 %collective-permute-done.5.refs_9_ = bf16[8,128,128]{2,1,0:T(8,128)(2,1)S(1)} collective-permute-done((bf16[8,128,128]{2,1,0:T(8,128)(2,1)S(1)}, bf16[8,128,128]{2,1,0:T(8,128)(2,1)S(1)}, u32[]{:S(2)}, u32[]{:S(2)}) %collective-permute-start.5) | collective-permute-done | bytes 262176 | tf_op jit(solution)/shard_map/ppermute | solution.py:431
  30.7 3.2 %lag_windows.3 = (f32[2,16,256]{2,1,0:T(8,128)S(1)}, f32[2,16,256]{2,1,0:T(8,128)S(1)}, f32[2,2,16,256]{3,2,1,0:T(8,128)S(1)}) custom-call(s32[4]{0:T(128)S(1)} %pad_add_fusion.refs_0_, s32[2,2,32]{2,1,0:T(2,128)S(1)} %copy-done.6, s32[2,2,32]{2,1,0:T(2,128)S(1)} %collective-permute-done.refs_2_, bf16[160,128]{1,0:T(8,128)(2,1)S(1)} %copy-done.4, ...), custom_call_target="tpu_custom_call" | custom-call | flops 805306368 | bytes 4718592 | tf_op jit(solution)/shard_map/lag_windows/pallas_call | solution.py:410
  34.2 1.6 %collective-permute-done.9 = bf16[2,128,128]{2,1,0:T(8,128)(2,1)S(1)} collective-permute-done((bf16[2,128,128]{2,1,0:T(8,128)(2,1)S(1)}, bf16[2,128,128]{2,1,0:T(8,128)(2,1)S(1)}, u32[]{:S(2)}, u32[]{:S(2)}) %collective-permute-start.9) | collective-permute-done | bytes 65568 | tf_op jit(solution)/shard_map/ppermute | solution.py:431
  35.8 1.6 %collective-permute-start.11 = (f32[2,16,256]{2,1,0:T(8,128)S(1)}, f32[2,16,256]{2,1,0:T(8,128)S(1)}, u32[]{:S(2)}, u32[]{:S(2)}) collective-permute-start(f32[2,16,256]{2,1,0:T(8,128)S(1)} %fusion), channel_id=1, source_target_pairs={{0,1},{1,0},{2,3},{3,2},{4,5},{5,4},{6,7},{7,6},{8,9},{9,8},{10,11... | collective-permute-start | bytes 98312 | tf_op jit(solution)/shard_map/ppermute | solution.py:431
  37.3 0.7 %multiply_bitcast_fusion = f32[2,1,128,128]{3,2,1,0:T(8,128)} fusion(bf16[2,128,128]{2,1,0:T(8,128)(2,1)S(1)} %collective-permute-done.9, bf16[2,128,128]{2,1,0:T(8,128)(2,1)S(1)} %collective-permute-done.8, bf16[2,128,128]{2,1,0:T(8,128)(2,1)S(1)} %collective-permute-done.7, bf16[2,128,128]{2,1,0:T(8,128)(2,1)S(1)} %get-tuple-element.42.refs_10_, ...), kind=kLoop, calls=%fused_computation.1 | loop fusion | flops 327680 | bytes 458752
  38.0 1.7 %collective-permute-done.11 = f32[2,16,256]{2,1,0:T(8,128)S(1)} collective-permute-done((f32[2,16,256]{2,1,0:T(8,128)S(1)}, f32[2,16,256]{2,1,0:T(8,128)S(1)}, u32[]{:S(2)}, u32[]{:S(2)}) %collective-permute-start.11) | collective-permute-done | bytes 32800 | tf_op jit(solution)/shard_map/ppermute | solution.py:431
  39.8 0.6 %fusion.2 = f32[2,16,256]{2,1,0:T(8,128)} fusion(f32[2,16,256]{2,1,0:T(8,128)S(1)} %collective-permute-done.11, f32[2,16,256]{2,1,0:T(8,128)S(1)} %get-tuple-element.48, f32[2,2,16,256]{3,2,1,0:T(8,128)S(1)} %collective-permute-done.10), kind=kLoop, calls=%fused_computation.9 | loop fusion | flops 16384 | bytes 131072 | tf_op jit(solution)/shard_map/add | solution.py:474
  (29 shorter events, 0.7 us)
Async XLA Ops:
  0.6 10.2 %copy-start.6 = (s32[2,2,32]{2,1,0:T(2,128)S(1)}, s32[2,2,32]{2,1,0:T(2,128)}, u32[]{:S(2)}) copy-start(s32[2,2,32]{2,1,0:T(2,128)} %refs_1_.8) | copy-start | bytes 1540
  0.6 10.2 %collective-permute-start.1 = (bf16[2,1,512,1024]{3,2,0,1:T(8,128)(2,1)}, bf16[2,1,512,1024]{3,2,0,1:T(8,128)(2,1)S(1)}, u32[]{:S(2)}, u32[]{:S(2)}) collective-permute-start(bf16[2,1,512,1024]{3,2,0,1:T(8,128)(2,1)} %bitcast.35), channel_id=1, source_target_pairs={{0,2},{2,0},{1,3},{3,1},{4,6},{6,4},{5,7},{7,5},{8,10},{10,8},{9,1... | collective-permute-start | bytes 6291464 | tf_op jit(solution)/shard_map/ppermute | solution.py:431
  1.2 19.8 %collective-permute-start.2 = (bf16[2,1,128,128]{3,2,0,1:T(8,128)(2,1)}, bf16[2,1,128,128]{3,2,0,1:T(8,128)(2,1)}, u32[]{:S(2)}, u32[]{:S(2)}) collective-permute-start(bf16[2,1,128,128]{3,2,0,1:T(8,128)(2,1)} %bitcast.7), channel_id=1, source_target_pairs={{0,8},{8,0},{16,24},{24,16},{1,9},{9,1},{17,25},{25,17},{2,10},{10... | collective-permute-start | bytes 196616 | tf_op jit(solution)/shard_map/ppermute | solution.py:431
  3.8 17.2 %collective-permute-start.3 = (bf16[2,1,128,128]{3,2,0,1:T(8,128)(2,1)}, bf16[2,1,128,128]{3,2,0,1:T(8,128)(2,1)}, u32[]{:S(2)}, u32[]{:S(2)}) collective-permute-start(bf16[2,1,128,128]{3,2,0,1:T(8,128)(2,1)} %bitcast.7), channel_id=1, source_target_pairs={{0,16},{8,24},{16,0},{24,8},{1,17},{9,25},{17,1},{25,9},{2,18},{10... | collective-permute-start | bytes 196616 | tf_op jit(solution)/shard_map/ppermute | solution.py:431
  6.4 4.4 %collective-permute-start = (s32[2,2,32]{2,1,0:T(2,128)}, s32[2,2,32]{2,1,0:T(2,128)S(1)}, u32[]{:S(2)}, u32[]{:S(2)}) collective-permute-start(s32[2,2,32]{2,1,0:T(2,128)} %refs_1_.8), channel_id=1, source_target_pairs={{0,2},{2,0},{1,3},{3,1},{4,6},{6,4},{5,7},{7,5},{8,10},{10,8},{9,1... | collective-permute-start | bytes 1544 | tf_op jit(solution)/shard_map/ppermute | solution.py:431
  8.5 1.3 %copy-start = (bf16[2,1,512,1024]{3,2,1,0:T(8,128)(2,1)}, bf16[2,1,512,1024]{3,2,1,0:T(8,128)(2,1)S(1)}, u32[]{:S(2)}) copy-start(bf16[2,1,512,1024]{3,2,1,0:T(8,128)(2,1)S(1)} %get-tuple-element.28) | copy-start | bytes 6291460
  9.9 0.8 %copy-start.7 = (f32[16,2,32,128]{3,2,1,0:T(8,128)}, f32[16,2,32,128]{3,2,1,0:T(8,128)S(1)}, u32[]{:S(2)}) copy-start(f32[16,2,32,128]{3,2,1,0:T(8,128)S(1)} %get-tuple-element.32.refs_6_) | copy-start | bytes 1572868
  10.7 10.3 %collective-permute-start.4 = (bf16[2,1,128,128]{3,2,0,1:T(8,128)(2,1)}, bf16[2,1,128,128]{3,2,0,1:T(8,128)(2,1)}, u32[]{:S(2)}, u32[]{:S(2)}) collective-permute-start(bf16[2,1,128,128]{3,2,0,1:T(8,128)(2,1)} %bitcast.8), channel_id=1, source_target_pairs={{0,24},{8,16},{16,8},{24,0},{1,25},{9,17},{17,9},{25,1},{2,26},{10... | collective-permute-start | bytes 196616 | tf_op jit(solution)/shard_map/ppermute | solution.py:431
  10.8 1.6 %copy-start.1 = (bf16[2,1,512,1024]{3,2,1,0:T(8,128)(2,1)S(1)}, bf16[2,1,512,1024]{3,2,1,0:T(8,128)(2,1)}, u32[]{:S(2)}) copy-start(bf16[2,1,512,1024]{3,2,1,0:T(8,128)(2,1)} %copy-done) | copy-start | bytes 6291460
  12.4 1.0 %copy-start.8 = (f32[16,2,32,128]{3,2,1,0:T(8,128)S(1)}, f32[16,2,32,128]{3,2,1,0:T(8,128)}, u32[]{:S(2)}) copy-start(f32[16,2,32,128]{3,2,1,0:T(8,128)} %copy-done.7) | copy-start | bytes 1572868
  16.3 6.1 %copy-start.2 = (bf16[256,256]{1,0:T(8,128)(2,1)S(1)}, bf16[256,256]{1,0:T(8,128)(2,1)}, u32[]{:S(2)}) copy-start(bf16[256,256]{1,0:T(8,128)(2,1)} %constant.31.clone.refs_4_) | copy-start | bytes 393220
  16.3 6.1 %copy-start.3 = (bf16[256,128]{1,0:T(8,128)(2,1)S(1)}, bf16[256,128]{1,0:T(8,128)(2,1)}, u32[]{:S(2)}) copy-start(bf16[256,128]{1,0:T(8,128)(2,1)} %constant.33.clone.refs_6_) | copy-start | bytes 196612
  16.3 6.0 %copy-start.4 = (bf16[160,128]{1,0:T(8,128)(2,1)S(1)}, bf16[160,128]{1,0:T(8,128)(2,1)}, u32[]{:S(2)}) copy-start(bf16[160,128]{1,0:T(8,128)(2,1)} %constant.30.clone.refs_3_) | copy-start | bytes 122884
  16.3 6.0 %copy-start.5 = (bf16[64,160]{1,0:T(8,128)(2,1)S(1)}, bf16[64,160]{1,0:T(8,128)(2,1)}, u32[]{:S(2)}) copy-start(bf16[64,160]{1,0:T(8,128)(2,1)} %constant.32.clone.refs_5_) | copy-start | bytes 61444
  16.3 9.2 %collective-permute-start.6 = (bf16[8,128,128]{2,1,0:T(8,128)(2,1)S(1)}, bf16[8,128,128]{2,1,0:T(8,128)(2,1)S(1)}, u32[]{:S(2)}, u32[]{:S(2)}) collective-permute-start(bf16[8,128,128]{2,1,0:T(8,128)(2,1)S(1)} %warp.2.refs_7_), channel_id=1, source_target_pairs={{0,4},{4,0},{1,5},{5,1},{2,6},{6,2},{3,7},{7,3},{8,12},{12,8},{9,1... | collective-permute-start | bytes 786440 | tf_op jit(solution)/shard_map/ppermute | solution.py:431
  21.9 8.8 %collective-permute-start.5 = (bf16[8,128,128]{2,1,0:T(8,128)(2,1)S(1)}, bf16[8,128,128]{2,1,0:T(8,128)(2,1)S(1)}, u32[]{:S(2)}, u32[]{:S(2)}) collective-permute-start(bf16[8,128,128]{2,1,0:T(8,128)(2,1)S(1)} %pad_maximum_fusion.refs_9_), channel_id=1, source_target_pairs={{0,4},{4,0},{1,5},{5,1},{2,6},{6,2},{3,7},{7,3},{8,12},{12,8},{9,1... | collective-permute-start | bytes 786440 | tf_op jit(solution)/shard_map/ppermute | solution.py:431
  25.6 8.4 %collective-permute-start.7 = (bf16[2,128,128]{2,1,0:T(8,128)(2,1)S(1)}, bf16[2,128,128]{2,1,0:T(8,128)(2,1)S(1)}, u32[]{:S(2)}, u32[]{:S(2)}) collective-permute-start(bf16[2,128,128]{2,1,0:T(8,128)(2,1)S(1)} %get-tuple-element.58), channel_id=1, source_target_pairs={{0,8},{8,0},{16,24},{24,16},{1,9},{9,1},{17,25},{25,17},{2,10},{10... | collective-permute-start | bytes 196616 | tf_op jit(solution)/shard_map/ppermute | solution.py:431
  26.3 7.9 %collective-permute-start.8 = (bf16[2,128,128]{2,1,0:T(8,128)(2,1)S(1)}, bf16[2,128,128]{2,1,0:T(8,128)(2,1)S(1)}, u32[]{:S(2)}, u32[]{:S(2)}) collective-permute-start(bf16[2,128,128]{2,1,0:T(8,128)(2,1)S(1)} %get-tuple-element.57), channel_id=1, source_target_pairs={{0,16},{8,24},{16,0},{24,8},{1,17},{9,25},{17,1},{25,9},{2,18},{10... | collective-permute-start | bytes 196616 | tf_op jit(solution)/shard_map/ppermute | solution.py:431
  29.7 6.1 %collective-permute-start.9 = (bf16[2,128,128]{2,1,0:T(8,128)(2,1)S(1)}, bf16[2,128,128]{2,1,0:T(8,128)(2,1)S(1)}, u32[]{:S(2)}, u32[]{:S(2)}) collective-permute-start(bf16[2,128,128]{2,1,0:T(8,128)(2,1)S(1)} %get-tuple-element.56), channel_id=1, source_target_pairs={{0,24},{8,16},{16,8},{24,0},{1,25},{9,17},{17,9},{25,1},{2,26},{10... | collective-permute-start | bytes 196616 | tf_op jit(solution)/shard_map/ppermute | solution.py:431
  33.9 1.9 %collective-permute-start.10 = (f32[2,2,16,256]{3,2,1,0:T(8,128)S(1)}, f32[2,2,16,256]{3,2,1,0:T(8,128)S(1)}, u32[]{:S(2)}, u32[]{:S(2)}) collective-permute-start(f32[2,2,16,256]{3,2,1,0:T(8,128)S(1)} %get-tuple-element.49), channel_id=1, source_target_pairs={{0,2},{2,0},{1,3},{3,1},{4,6},{6,4},{5,7},{7,5},{8,10},{10,8},{9,1... | collective-permute-start | bytes 196616 | tf_op jit(solution)/shard_map/ppermute | solution.py:431
  35.8 4.0 %collective-permute-start.11 = (f32[2,16,256]{2,1,0:T(8,128)S(1)}, f32[2,16,256]{2,1,0:T(8,128)S(1)}, u32[]{:S(2)}, u32[]{:S(2)}) collective-permute-start(f32[2,16,256]{2,1,0:T(8,128)S(1)} %fusion), channel_id=1, source_target_pairs={{0,1},{1,0},{2,3},{3,2},{4,5},{5,4},{6,7},{7,6},{8,9},{9,8},{10,11... | collective-permute-start | bytes 98312 | tf_op jit(solution)/shard_map/ppermute | solution.py:431

commit v14 on v11

--- a/solution.py
+++ b/solution.py
@@ -107,6 +107,9 @@
         out_specs=[pl.BlockSpec(memory_space=pltpu.VMEM)] * count,
         scratch_shapes=[pltpu.SemaphoreType.DMA((count,))],
         compiler_params=pltpu.CompilerParams(vmem_limit_bytes=VMEM_LIMIT),
+        cost_estimate=pl.CostEstimate(
+            flops=0, bytes_accessed=2 * sum(one.nbytes for one in arrays), transcendentals=0
+        ),
         name="stage",
     )(*kept, pltpu.with_memory_space_constraint(after, pltpu.HBM))
 
@@ -455,7 +458,7 @@
             exchange(sums[turn].astype(jnp.bfloat16), "z", depth, turn) for turn in range(1, depth)
         ]
         sizes = (planes, depth, own)
-        (part,) = lag_windows(*work, near, sums[0], 0, *sizes)
+        (part,) = lag_windows(*work, near, near_sums[0], 0, *sizes)
         *keep, give = lag_windows(*work, far, part, 1, *sizes)
         keep, moved = lax.optimization_barrier((keep, moved))
         total = sum((one.astype(jnp.float32) for one in moved), sums[0])

time: 37.4 us -> 36.1 us (0.965)
  waiting for transfers between devices: 6.86 us -> 5.71 us
    ppermute x12, waiting for transfers between devices: 6.86 us -> 5.71 us  [exchange(): return lax.ppermute(value, axes, [(at, at ^ turn) for at in range(size)])]
  transfers between devices with their start and end apart: 12 -> 12, of which waited for: 3 -> 5; matrix products, arithmetic and copies ran while one was open for 2% -> 2% of each run, Pallas kernels for 37% -> 39%
where the time goes in v14:
time: 36.1 us; the launch traced here: 35.9 us
  starting transfers between devices  14 us (39%)
  Pallas kernels  13.9 us (39%)
  waiting for transfers between devices  5.71 us (16%)
  other arithmetic  1.5 us (4%)
  between operations  0.79 us (2%)
    ppermute x12, starting transfers between devices, exchange(): return lax.ppermute(value, axes, [(at, at ^ turn) for at in range(size)])  14 us
    pallas_call x2, Pallas kernels, lag_windows(): pl.pallas_call(functools.partial(spectrum_kernel, vols, across, block, ow...  6.08 us
    ppermute x12, waiting for transfers between devices, exchange(): return lax.ppermute(value, axes, [(at, at ^ turn) for at in range(size)])  5.71 us
    pallas_call x2, Pallas kernels, warp_sums(): pl.pallas_call(functools.partial(warp_kernel, down, across, block, own, o...  5.68 us
    pallas_call x1, Pallas kernels, stage(): pl.pallas_call(functools.partial(stage_kernel, count), out_shape=[jax.Sha...  2.13 us
  transfers between devices with their start and end apart: 12, of which 5 were waited for; matrix products, arithmetic and copies ran while one was open for 2% of the time, Pallas kernels for 39%

profile of v14, /device:TPU:0, one launch (start us, length us, event | category | flops | bytes accessed | tf_op | source)
XLA Modules:
  0.0 35.9 jit_solution(13765525211053884628)
XLA Ops:
  0.6 0.0 copy-start
  0.7 0.5 %collective-permute-start.1 = (bf16[2,1,512,1024]{3,2,0,1:T(8,128)(2,1)}, bf16[2,1,512,1024]{3,2,0,1:T(8,128)(2,1)S(1)}, u32[]{:S(2)}, u32[]{:S(2)}) collective-permute-start(bf16[2,1,512,1024]{3,2,0,1:T(8,128)(2,1)} %bitcast.38), channel_id=1, source_target_pairs={{0,2},{2,0},{1,3},{3,1},{4,6},{6,4},{5,7},{7,5},{8,10},{10,8},{9,1... | collective-permute-start | bytes 6291464 | tf_op jit(solution)/shard_map/ppermute | solution.py:429
  1.2 2.7 %collective-permute-start.2 = (bf16[2,1,128,128]{3,2,0,1:T(8,128)(2,1)}, bf16[2,1,128,128]{3,2,0,1:T(8,128)(2,1)S(1)}, u32[]{:S(2)}, u32[]{:S(2)}) collective-permute-start(bf16[2,1,128,128]{3,2,0,1:T(8,128)(2,1)} %bitcast.34), channel_id=1, source_target_pairs={{0,8},{8,0},{16,24},{24,16},{1,9},{9,1},{17,25},{25,17},{2,10},{10... | collective-permute-start | bytes 196616 | tf_op jit(solution)/shard_map/ppermute | solution.py:429
  3.8 2.6 %collective-permute-start.3 = (bf16[2,1,128,128]{3,2,0,1:T(8,128)(2,1)}, bf16[2,1,128,128]{3,2,0,1:T(8,128)(2,1)S(1)}, u32[]{:S(2)}, u32[]{:S(2)}) collective-permute-start(bf16[2,1,128,128]{3,2,0,1:T(8,128)(2,1)} %bitcast.35), channel_id=1, source_target_pairs={{0,16},{8,24},{16,0},{24,8},{1,17},{9,25},{17,1},{25,9},{2,18},{10... | collective-permute-start | bytes 196616 | tf_op jit(solution)/shard_map/ppermute | solution.py:429
  6.4 0.1 pad_add_fusion.refs_0_
  6.5 2.1 %stage.1 = (bf16[2,1,512,1024]{3,2,1,0:T(8,128)(2,1)S(1)}, f32[16,176,128]{2,1,0:T(8,128)S(1)}, f32[16,2,32,128]{3,2,1,0:T(8,128)S(1)}) custom-call(bf16[2,1,512,1024]{3,2,1,0:T(8,128)(2,1)} %refs_0_.1, f32[16,176,128]{2,1,0:T(8,128)} %constant.28.clone.refs_1_, f32[16,2,32,128]{3,2,1,0:T(8,128)} %constant.29.clone.refs_2_, bf16[2,1,128,128]{3,2,1,0:T(8,128)(2,1)} %refs_7_.1), custom_call_target="tpu_custom_call" | custom-call | bytes 8126464 | tf_op jit(solution)/shard_map/stage/pallas_call | solution.py:102
  8.7 2.8 %warp.2.refs_7_ = bf16[8,128,128]{2,1,0:T(8,128)(2,1)S(1)} custom-call(s32[4]{0:T(128)S(1)} %pad_add_fusion.refs_0_, s32[2,2,32]{2,1,0:T(2,128)S(1)} %copy-done.5, s32[2,2,32]{2,1,0:T(2,128)S(1)} %collective-permute-done.refs_2_, bf16[2,512,1024]{2,1,0:T(8,128)(2,1)S(1)} %bitcast.30, bf16[2,512,1024]{2,1,0:T(8,128)(2,1)S(1)} %bitcast.26, ...), custom_call_target="tpu_custom_call" | custom-call | flops 2147483648 | bytes 4718592 | tf_op jit(solution)/shard_map/warp/pallas_call | solution.py:219
  11.6 1.8 %collective-permute-start.6 = (bf16[8,128,128]{2,1,0:T(8,128)(2,1)S(1)}, bf16[8,128,128]{2,1,0:T(8,128)(2,1)S(1)}, u32[]{:S(2)}, u32[]{:S(2)}) collective-permute-start(bf16[8,128,128]{2,1,0:T(8,128)(2,1)S(1)} %warp.2.refs_7_), channel_id=1, source_target_pairs={{0,4},{4,0},{1,5},{5,1},{2,6},{6,2},{3,7},{7,3},{8,12},{12,8},{9,1... | collective-permute-start | bytes 786440 | tf_op jit(solution)/shard_map/ppermute | solution.py:429
  13.4 2.8 %warp.3 = (bf16[2,128,128]{2,1,0:T(8,128)(2,1)S(1)}, bf16[2,128,128]{2,1,0:T(8,128)(2,1)S(1)}, bf16[2,128,128]{2,1,0:T(8,128)(2,1)S(1)}, bf16[2,128,128]{2,1,0:T(8,128)(2,1)S(1)}) custom-call(s32[4]{0:T(128)S(1)} %pad_add_fusion.refs_0_, s32[2,2,32]{2,1,0:T(2,128)S(1)} %copy-done.5, s32[2,2,32]{2,1,0:T(2,128)S(1)} %collective-permute-done.refs_2_, ...), custom_call_target="tpu_custom_call" | custom-call | flops 2147483648 | bytes 4718592 | tf_op jit(solution)/shard_map/warp/pallas_call | solution.py:219
  16.3 0.4 collective-permute-start.5
  16.7 2.9 %lag_windows.2.refs_10_ = f32[4,512,128]{2,1,0:T(8,128)S(1)} custom-call(s32[4]{0:T(128)S(1)} %pad_add_fusion.refs_0_, s32[2,2,32]{2,1,0:T(2,128)S(1)} %copy-done.5, s32[2,2,32]{2,1,0:T(2,128)S(1)} %collective-permute-done.refs_2_, bf16[160,128]{1,0:T(8,128)(2,1)S(1)} %copy-done.3, bf16[256,256]{1,0:T(8,128)(2,1)S(1)} %copy-done.1, ...), custom_call_target="tpu_custom_call" | custom-call | flops 3221225472 | bytes 4718592 | tf_op jit(solution)/shard_map/lag_windows/pallas_call | solution.py:408
  19.5 1.2 %collective-permute-done.6 = bf16[8,128,128]{2,1,0:T(8,128)(2,1)S(1)} collective-permute-done((bf16[8,128,128]{2,1,0:T(8,128)(2,1)S(1)}, bf16[8,128,128]{2,1,0:T(8,128)(2,1)S(1)}, u32[]{:S(2)}, u32[]{:S(2)}) %collective-permute-start.6) | collective-permute-done | bytes 262176 | tf_op jit(solution)/shard_map/ppermute | solution.py:429
  20.7 0.1 add_convert_fusion
  20.8 1.0 %collective-permute-start.7 = (bf16[2,128,128]{2,1,0:T(8,128)(2,1)S(1)}, bf16[2,128,128]{2,1,0:T(8,128)(2,1)S(1)}, u32[]{:S(2)}, u32[]{:S(2)}) collective-permute-start(bf16[2,128,128]{2,1,0:T(8,128)(2,1)S(1)} %get-tuple-element.52), channel_id=1, source_target_pairs={{0,8},{8,0},{16,24},{24,16},{1,9},{9,1},{17,25},{25,17},{2,10},{10... | collective-permute-start | bytes 196616 | tf_op jit(solution)/shard_map/ppermute | solution.py:429
  21.8 3.5 %collective-permute-start.8 = (bf16[2,128,128]{2,1,0:T(8,128)(2,1)S(1)}, bf16[2,128,128]{2,1,0:T(8,128)(2,1)S(1)}, u32[]{:S(2)}, u32[]{:S(2)}) collective-permute-start(bf16[2,128,128]{2,1,0:T(8,128)(2,1)S(1)} %get-tuple-element.51), channel_id=1, source_target_pairs={{0,16},{8,24},{16,0},{24,8},{1,17},{9,25},{17,1},{25,9},{2,18},{10... | collective-permute-start | bytes 196616 | tf_op jit(solution)/shard_map/ppermute | solution.py:429
  25.3 0.7 %collective-permute-done.5.refs_9_ = bf16[8,128,128]{2,1,0:T(8,128)(2,1)S(1)} collective-permute-done((bf16[8,128,128]{2,1,0:T(8,128)(2,1)S(1)}, bf16[8,128,128]{2,1,0:T(8,128)(2,1)S(1)}, u32[]{:S(2)}, u32[]{:S(2)}) %collective-permute-start.5) | collective-permute-done | bytes 262176 | tf_op jit(solution)/shard_map/ppermute | solution.py:429
  26.0 3.2 %lag_windows.3 = (f32[2,16,256]{2,1,0:T(8,128)S(1)}, f32[2,16,256]{2,1,0:T(8,128)S(1)}, f32[2,2,16,256]{3,2,1,0:T(8,128)S(1)}) custom-call(s32[4]{0:T(128)S(1)} %pad_add_fusion.refs_0_, s32[2,2,32]{2,1,0:T(2,128)S(1)} %copy-done.5, s32[2,2,32]{2,1,0:T(2,128)S(1)} %collective-permute-done.refs_2_, bf16[160,128]{1,0:T(8,128)(2,1)S(1)} %copy-done.3, ...), custom_call_target="tpu_custom_call" | custom-call | flops 805306368 | bytes 4718592 | tf_op jit(solution)/shard_map/lag_windows/pallas_call | solution.py:408
  29.2 0.1 collective-permute-start.10
  29.3 0.1 collective-permute-done.8
  29.4 2.0 %collective-permute-done.9 = bf16[2,128,128]{2,1,0:T(8,128)(2,1)S(1)} collective-permute-done((bf16[2,128,128]{2,1,0:T(8,128)(2,1)S(1)}, bf16[2,128,128]{2,1,0:T(8,128)(2,1)S(1)}, u32[]{:S(2)}, u32[]{:S(2)}) %collective-permute-start.9) | collective-permute-done | bytes 65568 | tf_op jit(solution)/shard_map/ppermute | solution.py:429
  31.3 1.6 %collective-permute-start.11 = (f32[2,16,256]{2,1,0:T(8,128)S(1)}, f32[2,16,256]{2,1,0:T(8,128)S(1)}, u32[]{:S(2)}, u32[]{:S(2)}) collective-permute-start(f32[2,16,256]{2,1,0:T(8,128)S(1)} %fusion), channel_id=1, source_target_pairs={{0,1},{1,0},{2,3},{3,2},{4,5},{5,4},{6,7},{7,6},{8,9},{9,8},{10,11... | collective-permute-start | bytes 98312 | tf_op jit(solution)/shard_map/ppermute | solution.py:429
  32.9 0.7 %multiply_bitcast_fusion = f32[2,1,128,128]{3,2,1,0:T(8,128)} fusion(bf16[2,128,128]{2,1,0:T(8,128)(2,1)S(1)} %collective-permute-done.9, bf16[2,128,128]{2,1,0:T(8,128)(2,1)S(1)} %collective-permute-done.8, bf16[2,128,128]{2,1,0:T(8,128)(2,1)S(1)} %collective-permute-done.7, bf16[2,128,128]{2,1,0:T(8,128)(2,1)S(1)} %get-tuple-element.36.refs_10_, ...), kind=kLoop, calls=%fused_computation.1 | loop fusion | flops 327680 | bytes 458752
  33.6 1.7 %collective-permute-done.11 = f32[2,16,256]{2,1,0:T(8,128)S(1)} collective-permute-done((f32[2,16,256]{2,1,0:T(8,128)S(1)}, f32[2,16,256]{2,1,0:T(8,128)S(1)}, u32[]{:S(2)}, u32[]{:S(2)}) %collective-permute-start.11) | collective-permute-done | bytes 32800 | tf_op jit(solution)/shard_map/ppermute | solution.py:429
  35.3 0.6 %fusion.2 = f32[2,16,256]{2,1,0:T(8,128)} fusion(f32[2,16,256]{2,1,0:T(8,128)S(1)} %collective-permute-done.11, f32[2,16,256]{2,1,0:T(8,128)S(1)} %get-tuple-element.42, f32[2,2,16,256]{3,2,1,0:T(8,128)S(1)} %collective-permute-done.10), kind=kLoop, calls=%fused_computation.9 | loop fusion | flops 16384 | bytes 131072 | tf_op jit(solution)/shard_map/add | solution.py:469
  (23 shorter events, 0.1 us)
Async XLA Ops:
  0.6 8.0 %copy-start = (bf16[2,1,128,128]{3,2,1,0:T(8,128)(2,1)S(1)}, bf16[2,1,128,128]{3,2,1,0:T(8,128)(2,1)}, u32[]{:S(2)}) copy-start(bf16[2,1,128,128]{3,2,1,0:T(8,128)(2,1)} %refs_7_.1) | copy-start | bytes 196612
  0.6 8.0 %copy-start.5 = (s32[2,2,32]{2,1,0:T(2,128)S(1)}, s32[2,2,32]{2,1,0:T(2,128)}, u32[]{:S(2)}) copy-start(s32[2,2,32]{2,1,0:T(2,128)} %refs_1_.8) | copy-start | bytes 1540
  0.7 8.0 %collective-permute-start.1 = (bf16[2,1,512,1024]{3,2,0,1:T(8,128)(2,1)}, bf16[2,1,512,1024]{3,2,0,1:T(8,128)(2,1)S(1)}, u32[]{:S(2)}, u32[]{:S(2)}) collective-permute-start(bf16[2,1,512,1024]{3,2,0,1:T(8,128)(2,1)} %bitcast.38), channel_id=1, source_target_pairs={{0,2},{2,0},{1,3},{3,1},{4,6},{6,4},{5,7},{7,5},{8,10},{10,8},{9,1... | collective-permute-start | bytes 6291464 | tf_op jit(solution)/shard_map/ppermute | solution.py:429
  1.2 15.0 %collective-permute-start.2 = (bf16[2,1,128,128]{3,2,0,1:T(8,128)(2,1)}, bf16[2,1,128,128]{3,2,0,1:T(8,128)(2,1)S(1)}, u32[]{:S(2)}, u32[]{:S(2)}) collective-permute-start(bf16[2,1,128,128]{3,2,0,1:T(8,128)(2,1)} %bitcast.34), channel_id=1, source_target_pairs={{0,8},{8,0},{16,24},{24,16},{1,9},{9,1},{17,25},{25,17},{2,10},{10... | collective-permute-start | bytes 196616 | tf_op jit(solution)/shard_map/ppermute | solution.py:429
  3.8 12.4 %collective-permute-start.3 = (bf16[2,1,128,128]{3,2,0,1:T(8,128)(2,1)}, bf16[2,1,128,128]{3,2,0,1:T(8,128)(2,1)S(1)}, u32[]{:S(2)}, u32[]{:S(2)}) collective-permute-start(bf16[2,1,128,128]{3,2,0,1:T(8,128)(2,1)} %bitcast.35), channel_id=1, source_target_pairs={{0,16},{8,24},{16,0},{24,8},{1,17},{9,25},{17,1},{25,9},{2,18},{10... | collective-permute-start | bytes 196616 | tf_op jit(solution)/shard_map/ppermute | solution.py:429
  6.4 9.8 %collective-permute-start.4 = (bf16[2,1,128,128]{3,2,0,1:T(8,128)(2,1)}, bf16[2,1,128,128]{3,2,0,1:T(8,128)(2,1)S(1)}, u32[]{:S(2)}, u32[]{:S(2)}) collective-permute-start(bf16[2,1,128,128]{3,2,0,1:T(8,128)(2,1)} %bitcast.36), channel_id=1, source_target_pairs={{0,24},{8,16},{16,8},{24,0},{1,25},{9,17},{17,9},{25,1},{2,26},{10... | collective-permute-start | bytes 196616 | tf_op jit(solution)/shard_map/ppermute | solution.py:429
  6.4 2.2 %collective-permute-start = (s32[2,2,32]{2,1,0:T(2,128)}, s32[2,2,32]{2,1,0:T(2,128)S(1)}, u32[]{:S(2)}, u32[]{:S(2)}) collective-permute-start(s32[2,2,32]{2,1,0:T(2,128)} %refs_1_.8), channel_id=1, source_target_pairs={{0,2},{2,0},{1,3},{3,1},{4,6},{6,4},{5,7},{7,5},{8,10},{10,8},{9,1... | collective-permute-start | bytes 1544 | tf_op jit(solution)/shard_map/ppermute | solution.py:429
  11.5 5.1 %copy-start.1 = (bf16[256,256]{1,0:T(8,128)(2,1)S(1)}, bf16[256,256]{1,0:T(8,128)(2,1)}, u32[]{:S(2)}) copy-start(bf16[256,256]{1,0:T(8,128)(2,1)} %constant.31.clone.refs_4_) | copy-start | bytes 393220
  11.5 5.1 %copy-start.2 = (bf16[256,128]{1,0:T(8,128)(2,1)S(1)}, bf16[256,128]{1,0:T(8,128)(2,1)}, u32[]{:S(2)}) copy-start(bf16[256,128]{1,0:T(8,128)(2,1)} %constant.33.clone.refs_6_) | copy-start | bytes 196612
  11.5 5.1 %copy-start.3 = (bf16[160,128]{1,0:T(8,128)(2,1)S(1)}, bf16[160,128]{1,0:T(8,128)(2,1)}, u32[]{:S(2)}) copy-start(bf16[160,128]{1,0:T(8,128)(2,1)} %constant.30.clone.refs_3_) | copy-start | bytes 122884
  11.6 5.1 %copy-start.4 = (bf16[64,160]{1,0:T(8,128)(2,1)S(1)}, bf16[64,160]{1,0:T(8,128)(2,1)}, u32[]{:S(2)}) copy-start(bf16[64,160]{1,0:T(8,128)(2,1)} %constant.32.clone.refs_5_) | copy-start | bytes 61444
  11.6 9.2 %collective-permute-start.6 = (bf16[8,128,128]{2,1,0:T(8,128)(2,1)S(1)}, bf16[8,128,128]{2,1,0:T(8,128)(2,1)S(1)}, u32[]{:S(2)}, u32[]{:S(2)}) collective-permute-start(bf16[8,128,128]{2,1,0:T(8,128)(2,1)S(1)} %warp.2.refs_7_), channel_id=1, source_target_pairs={{0,4},{4,0},{1,5},{5,1},{2,6},{6,2},{3,7},{7,3},{8,12},{12,8},{9,1... | collective-permute-start | bytes 786440 | tf_op jit(solution)/shard_map/ppermute | solution.py:429
  16.3 9.7 %collective-permute-start.5 = (bf16[8,128,128]{2,1,0:T(8,128)(2,1)S(1)}, bf16[8,128,128]{2,1,0:T(8,128)(2,1)S(1)}, u32[]{:S(2)}, u32[]{:S(2)}) collective-permute-start(bf16[8,128,128]{2,1,0:T(8,128)(2,1)S(1)} %pad_maximum_fusion.refs_9_), channel_id=1, source_target_pairs={{0,4},{4,0},{1,5},{5,1},{2,6},{6,2},{3,7},{7,3},{8,12},{12,8},{9,1... | collective-permute-start | bytes 786440 | tf_op jit(solution)/shard_map/ppermute | solution.py:429
  20.8 8.5 %collective-permute-start.7 = (bf16[2,128,128]{2,1,0:T(8,128)(2,1)S(1)}, bf16[2,128,128]{2,1,0:T(8,128)(2,1)S(1)}, u32[]{:S(2)}, u32[]{:S(2)}) collective-permute-start(bf16[2,128,128]{2,1,0:T(8,128)(2,1)S(1)} %get-tuple-element.52), channel_id=1, source_target_pairs={{0,8},{8,0},{16,24},{24,16},{1,9},{9,1},{17,25},{25,17},{2,10},{10... | collective-permute-start | bytes 196616 | tf_op jit(solution)/shard_map/ppermute | solution.py:429
  21.8 7.6 %collective-permute-start.8 = (bf16[2,128,128]{2,1,0:T(8,128)(2,1)S(1)}, bf16[2,128,128]{2,1,0:T(8,128)(2,1)S(1)}, u32[]{:S(2)}, u32[]{:S(2)}) collective-permute-start(bf16[2,128,128]{2,1,0:T(8,128)(2,1)S(1)} %get-tuple-element.51), channel_id=1, source_target_pairs={{0,16},{8,24},{16,0},{24,8},{1,17},{9,25},{17,1},{25,9},{2,18},{10... | collective-permute-start | bytes 196616 | tf_op jit(solution)/shard_map/ppermute | solution.py:429
  25.3 6.1 %collective-permute-start.9 = (bf16[2,128,128]{2,1,0:T(8,128)(2,1)S(1)}, bf16[2,128,128]{2,1,0:T(8,128)(2,1)S(1)}, u32[]{:S(2)}, u32[]{:S(2)}) collective-permute-start(bf16[2,128,128]{2,1,0:T(8,128)(2,1)S(1)} %get-tuple-element.50), channel_id=1, source_target_pairs={{0,24},{8,16},{16,8},{24,0},{1,25},{9,17},{17,9},{25,1},{2,26},{10... | collective-permute-start | bytes 196616 | tf_op jit(solution)/shard_map/ppermute | solution.py:429
  29.2 2.2 %collective-permute-start.10 = (f32[2,2,16,256]{3,2,1,0:T(8,128)S(1)}, f32[2,2,16,256]{3,2,1,0:T(8,128)S(1)}, u32[]{:S(2)}, u32[]{:S(2)}) collective-permute-start(f32[2,2,16,256]{3,2,1,0:T(8,128)S(1)} %get-tuple-element.43), channel_id=1, source_target_pairs={{0,2},{2,0},{1,3},{3,1},{4,6},{6,4},{5,7},{7,5},{8,10},{10,8},{9,1... | collective-permute-start | bytes 196616 | tf_op jit(solution)/shard_map/ppermute | solution.py:429
  31.3 4.0 %collective-permute-start.11 = (f32[2,16,256]{2,1,0:T(8,128)S(1)}, f32[2,16,256]{2,1,0:T(8,128)S(1)}, u32[]{:S(2)}, u32[]{:S(2)}) collective-permute-start(f32[2,16,256]{2,1,0:T(8,128)S(1)} %fusion), channel_id=1, source_target_pairs={{0,1},{1,0},{2,3},{3,2},{4,5},{5,4},{6,7},{7,6},{8,9},{9,8},{10,11... | collective-permute-start | bytes 98312 | tf_op jit(solution)/shard_map/ppermute | solution.py:429

commit v15 on v14

--- a/solution.py
+++ b/solution.py
@@ -359,11 +359,10 @@
     if not other:
         return
 
-    keep_refs, give_ref = out_refs[:-1], out_refs[-1]
     share = found.shape[1] // WIN // planes
     per_tile = LANES // WIN
     lane = lax.broadcasted_iota(jnp.int32, (share, LANES), 1) // WIN
-    for turn, keep_ref in enumerate(keep_refs):
+    for turn, out_ref in enumerate(out_refs):
         plane = place_ref[3] ^ turn
         for order in range(many):
             for tile in range(WIN // per_tile):
@@ -375,11 +374,7 @@
                         one = pltpu.roll(one, part * WIN, 1)
                     total = jnp.where(lane == part, one, total)
                 lanes = slice(tile * LANES, (tile + 1) * LANES)
-                total = total * (1.0 / block)
-                if order < vols:
-                    keep_ref[order, :, lanes] = total
-                else:
-                    give_ref[turn, order - vols, :, lanes] = total
+                out_ref[order // vols, order % vols, :, lanes] = total * (1.0 / block)
 
 
 def lag_windows(
@@ -396,9 +391,8 @@
     many = 2 * vols * 2 * own
     found = jax.ShapeDtypeStruct((2 * vols, blocks * WIN, LANES), jnp.float32)
     if other:
-        out = (vols, blocks // planes, WIN * WIN)
+        out = (2, vols, blocks // planes, WIN * WIN)
         out_shape = [jax.ShapeDtypeStruct(out, jnp.float32)] * planes
-        out_shape.append(jax.ShapeDtypeStruct((planes, *out), jnp.float32))
         scratch_shapes = [pltpu.VMEM(found.shape, found.dtype)]
         last = vmem
     else:
@@ -438,7 +432,9 @@
     other_codes = exchange(shift_codes, "core", 2, 1)
     other_frames = exchange(frames, "core", 2, 1)
     staged, *bands = stage([frames, *tap_constants(block)], template)
-    pieces = [template] + [exchange(template, "z", depth, turn) for turn in range(1, depth)]
+    turns = [depth - 1, *range(1, depth - 1)]
+    fetched = {turn: exchange(template, "z", depth, turn) for turn in turns}
+    pieces = [template] + [fetched[turn] for turn in range(1, depth)]
     averages, correlation = [], 0.0
     volumes = vol_dev * depth * 4
     for p in range(pl_dev):
@@ -454,19 +450,16 @@
             one.astype(jnp.float32) + taken[step * own : (step + 1) * own].astype(jnp.float32)
             for step, one in enumerate(near_sums)
         ]
-        moved = [
-            exchange(sums[turn].astype(jnp.bfloat16), "z", depth, turn) for turn in range(1, depth)
-        ]
+        moved = [exchange(sums[turn].astype(jnp.bfloat16), "z", depth, turn) for turn in turns]
         sizes = (planes, depth, own)
         (part,) = lag_windows(*work, near, near_sums[0], 0, *sizes)
-        *keep, give = lag_windows(*work, far, part, 1, *sizes)
-        keep, moved = lax.optimization_barrier((keep, moved))
+        found, *given = lag_windows(*work, far, part, 1, *sizes)
+        found, moved = lax.optimization_barrier((found, moved))
         total = sum((one.astype(jnp.float32) for one in moved), sums[0])
         averages.append(total * (1.0 / volumes))
-        got = exchange(give, "core", 2, 1)
-        for turn, one in enumerate(keep):
-            one = one + got[turn]
-            correlation += exchange(one, "plane", planes, turn) if turn else one
+        for turn, one in enumerate(given):
+            found = found + exchange(one, "plane", planes, turn + 1)
+        correlation += found[0] + exchange(found[1], "core", 2, 1)
     return (correlation, jnp.stack(averages, axis=1))
 
 

time: 36.1 us -> 35.6 us (0.986)
  waiting for transfers between devices: 5.71 us -> 4.91 us
    ppermute x12, waiting for transfers between devices: 5.71 us -> 4.91 us  [exchange(): return lax.ppermute(value, axes, [(at, at ^ turn) for at in range(size)])]
  transfers between devices with their start and end apart: 12 -> 12, of which waited for: 5 -> 4; matrix products, arithmetic and copies ran while one was open for 2% -> 2% of each run, Pallas kernels for 39% -> 39%
where the time goes in v15:
time: 35.6 us; the launch traced here: 35.4 us
  starting transfers between devices  14.3 us (40%)
  Pallas kernels  13.9 us (39%)
  waiting for transfers between devices  4.91 us (14%)
  other arithmetic  1.5 us (4%)
  between operations  0.8 us (2%)
    ppermute x12, starting transfers between devices, exchange(): return lax.ppermute(value, axes, [(at, at ^ turn) for at in range(size)])  14.3 us
    pallas_call x2, Pallas kernels, lag_windows(): pl.pallas_call(functools.partial(spectrum_kernel, vols, across, block, ow...  6.07 us
    pallas_call x2, Pallas kernels, warp_sums(): pl.pallas_call(functools.partial(warp_kernel, down, across, block, own, o...  5.68 us
    ppermute x12, waiting for transfers between devices, exchange(): return lax.ppermute(value, axes, [(at, at ^ turn) for at in range(size)])  4.91 us
    pallas_call x1, Pallas kernels, stage(): pl.pallas_call(functools.partial(stage_kernel, count), out_shape=[jax.Sha...  2.13 us
  transfers between devices with their start and end apart: 12, of which 4 were waited for; matrix products, arithmetic and copies ran while one was open for 2% of the time, Pallas kernels for 39%

profile of v15, /device:TPU:0, one launch (start us, length us, event | category | flops | bytes accessed | tf_op | source)
XLA Modules:
  0.0 35.4 jit_solution(2420328051241782439)
XLA Ops:
  0.6 0.0 copy-start
  0.7 0.5 %collective-permute-start.1 = (bf16[2,1,512,1024]{3,2,0,1:T(8,128)(2,1)}, bf16[2,1,512,1024]{3,2,0,1:T(8,128)(2,1)S(1)}, u32[]{:S(2)}, u32[]{:S(2)}) collective-permute-start(bf16[2,1,512,1024]{3,2,0,1:T(8,128)(2,1)} %bitcast.34), channel_id=1, source_target_pairs={{0,2},{2,0},{1,3},{3,1},{4,6},{6,4},{5,7},{7,5},{8,10},{10,8},{9,1... | collective-permute-start | bytes 6291464 | tf_op jit(solution)/shard_map/ppermute | solution.py:423
  1.2 2.7 %collective-permute-start.2 = (bf16[2,1,128,128]{3,2,0,1:T(8,128)(2,1)}, bf16[2,1,128,128]{3,2,0,1:T(8,128)(2,1)S(1)}, u32[]{:S(2)}, u32[]{:S(2)}) collective-permute-start(bf16[2,1,128,128]{3,2,0,1:T(8,128)(2,1)} %bitcast.30), channel_id=1, source_target_pairs={{0,8},{8,0},{16,24},{24,16},{1,9},{9,1},{17,25},{25,17},{2,10},{10... | collective-permute-start | bytes 196616 | tf_op jit(solution)/shard_map/ppermute | solution.py:423
  3.8 2.6 %collective-permute-start.3 = (bf16[2,1,128,128]{3,2,0,1:T(8,128)(2,1)}, bf16[2,1,128,128]{3,2,0,1:T(8,128)(2,1)S(1)}, u32[]{:S(2)}, u32[]{:S(2)}) collective-permute-start(bf16[2,1,128,128]{3,2,0,1:T(8,128)(2,1)} %bitcast.31), channel_id=1, source_target_pairs={{0,16},{8,24},{16,0},{24,8},{1,17},{9,25},{17,1},{25,9},{2,18},{10... | collective-permute-start | bytes 196616 | tf_op jit(solution)/shard_map/ppermute | solution.py:423
  6.4 0.1 pad_add_fusion.refs_0_
  6.5 2.1 %stage.1 = (bf16[2,1,512,1024]{3,2,1,0:T(8,128)(2,1)S(1)}, f32[16,176,128]{2,1,0:T(8,128)S(1)}, f32[16,2,32,128]{3,2,1,0:T(8,128)S(1)}) custom-call(bf16[2,1,512,1024]{3,2,1,0:T(8,128)(2,1)} %refs_0_.1, f32[16,176,128]{2,1,0:T(8,128)} %constant.28.clone.refs_1_, f32[16,2,32,128]{3,2,1,0:T(8,128)} %constant.29.clone.refs_2_, bf16[2,1,128,128]{3,2,1,0:T(8,128)(2,1)} %refs_7_.1), custom_call_target="tpu_custom_call" | custom-call | bytes 8126464 | tf_op jit(solution)/shard_map/stage/pallas_call | solution.py:102
  8.7 2.8 %warp.2.refs_7_ = bf16[8,128,128]{2,1,0:T(8,128)(2,1)S(1)} custom-call(s32[4]{0:T(128)S(1)} %pad_add_fusion.refs_0_, s32[2,2,32]{2,1,0:T(2,128)S(1)} %copy-done.5, s32[2,2,32]{2,1,0:T(2,128)S(1)} %collective-permute-done.refs_2_, bf16[2,512,1024]{2,1,0:T(8,128)(2,1)S(1)} %bitcast.26, bf16[2,512,1024]{2,1,0:T(8,128)(2,1)S(1)} %bitcast.22, ...), custom_call_target="tpu_custom_call" | custom-call | flops 2147483648 | bytes 4718592 | tf_op jit(solution)/shard_map/warp/pallas_call | solution.py:219
  11.5 0.0 copy-start.3
  11.6 1.8 %collective-permute-start.6 = (bf16[8,128,128]{2,1,0:T(8,128)(2,1)S(1)}, bf16[8,128,128]{2,1,0:T(8,128)(2,1)S(1)}, u32[]{:S(2)}, u32[]{:S(2)}) collective-permute-start(bf16[8,128,128]{2,1,0:T(8,128)(2,1)S(1)} %warp.2.refs_7_), channel_id=1, source_target_pairs={{0,4},{4,0},{1,5},{5,1},{2,6},{6,2},{3,7},{7,3},{8,12},{12,8},{9,1... | collective-permute-start | bytes 786440 | tf_op jit(solution)/shard_map/ppermute | solution.py:423
  13.4 2.8 %warp.3 = (bf16[2,128,128]{2,1,0:T(8,128)(2,1)S(1)}, bf16[2,128,128]{2,1,0:T(8,128)(2,1)S(1)}, bf16[2,128,128]{2,1,0:T(8,128)(2,1)S(1)}, bf16[2,128,128]{2,1,0:T(8,128)(2,1)S(1)}) custom-call(s32[4]{0:T(128)S(1)} %pad_add_fusion.refs_0_, s32[2,2,32]{2,1,0:T(2,128)S(1)} %copy-done.5, s32[2,2,32]{2,1,0:T(2,128)S(1)} %collective-permute-done.refs_2_, ...), custom_call_target="tpu_custom_call" | custom-call | flops 2147483648 | bytes 4718592 | tf_op jit(solution)/shard_map/warp/pallas_call | solution.py:219
  16.3 0.3 collective-permute-start.5
  16.6 2.9 %lag_windows.2.refs_10_ = f32[4,512,128]{2,1,0:T(8,128)S(1)} custom-call(s32[4]{0:T(128)S(1)} %pad_add_fusion.refs_0_, s32[2,2,32]{2,1,0:T(2,128)S(1)} %copy-done.5, s32[2,2,32]{2,1,0:T(2,128)S(1)} %collective-permute-done.refs_2_, bf16[160,128]{1,0:T(8,128)(2,1)S(1)} %copy-done.3, bf16[256,256]{1,0:T(8,128)(2,1)S(1)} %copy-done.1, ...), custom_call_target="tpu_custom_call" | custom-call | flops 3221225472 | bytes 4718592 | tf_op jit(solution)/shard_map/lag_windows/pallas_call | solution.py:402
  19.5 1.2 %collective-permute-done.6 = bf16[8,128,128]{2,1,0:T(8,128)(2,1)S(1)} collective-permute-done((bf16[8,128,128]{2,1,0:T(8,128)(2,1)S(1)}, bf16[8,128,128]{2,1,0:T(8,128)(2,1)S(1)}, u32[]{:S(2)}, u32[]{:S(2)}) %collective-permute-start.6) | collective-permute-done | bytes 262176 | tf_op jit(solution)/shard_map/ppermute | solution.py:423
  20.7 0.1 add_convert_fusion
  20.8 3.9 %collective-permute-start.7 = (bf16[2,128,128]{2,1,0:T(8,128)(2,1)S(1)}, bf16[2,128,128]{2,1,0:T(8,128)(2,1)S(1)}, u32[]{:S(2)}, u32[]{:S(2)}) collective-permute-start(bf16[2,128,128]{2,1,0:T(8,128)(2,1)S(1)} %get-tuple-element.48), channel_id=1, source_target_pairs={{0,24},{8,16},{16,8},{24,0},{1,25},{9,17},{17,9},{25,1},{2,26},{10... | collective-permute-start | bytes 196616 | tf_op jit(solution)/shard_map/ppermute | solution.py:423
  24.7 0.6 %collective-permute-start.9 = (bf16[2,128,128]{2,1,0:T(8,128)(2,1)S(1)}, bf16[2,128,128]{2,1,0:T(8,128)(2,1)S(1)}, u32[]{:S(2)}, u32[]{:S(2)}) collective-permute-start(bf16[2,128,128]{2,1,0:T(8,128)(2,1)S(1)} %get-tuple-element.46), channel_id=1, source_target_pairs={{0,16},{8,24},{16,0},{24,8},{1,17},{9,25},{17,1},{25,9},{2,18},{10... | collective-permute-start | bytes 196616 | tf_op jit(solution)/shard_map/ppermute | solution.py:423
  25.3 0.6 %collective-permute-done.5.refs_9_ = bf16[8,128,128]{2,1,0:T(8,128)(2,1)S(1)} collective-permute-done((bf16[8,128,128]{2,1,0:T(8,128)(2,1)S(1)}, bf16[8,128,128]{2,1,0:T(8,128)(2,1)S(1)}, u32[]{:S(2)}, u32[]{:S(2)}) %collective-permute-start.5) | collective-permute-done | bytes 262176 | tf_op jit(solution)/shard_map/ppermute | solution.py:423
  26.0 3.2 %lag_windows.3 = (f32[2,2,16,256]{3,2,1,0:T(8,128)S(1)}, f32[2,2,16,256]{3,2,1,0:T(8,128)S(1)}) custom-call(s32[4]{0:T(128)S(1)} %pad_add_fusion.refs_0_, s32[2,2,32]{2,1,0:T(2,128)S(1)} %copy-done.5, s32[2,2,32]{2,1,0:T(2,128)S(1)} %collective-permute-done.refs_2_, bf16[160,128]{1,0:T(8,128)(2,1)S(1)} %copy-done.3, bf16[256,256]{1,0:T(8,128)(2,1)S(1)} %copy-done.1, ...), custom_call_target="tpu_custom_call" | custom-call | flops 805306368 | bytes 4718592 | tf_op jit(solution)/shard_map/lag_windows/pallas_call | solution.py:402
  29.2 1.8 %collective-permute-start.10 = (f32[2,2,16,256]{3,2,1,0:T(8,128)S(1)}, f32[2,2,16,256]{3,2,1,0:T(8,128)S(1)}, u32[]{:S(2)}, u32[]{:S(2)}) collective-permute-start(f32[2,2,16,256]{3,2,1,0:T(8,128)S(1)} %get-tuple-element.40), channel_id=1, source_target_pairs={{0,1},{1,0},{2,3},{3,2},{4,5},{5,4},{6,7},{7,6},{8,9},{9,8},{10,11... | collective-permute-start | bytes 196616 | tf_op jit(solution)/shard_map/ppermute | solution.py:423
  31.0 2.5 %collective-permute-done.10 = f32[2,2,16,256]{3,2,1,0:T(8,128)S(1)} collective-permute-done((f32[2,2,16,256]{3,2,1,0:T(8,128)S(1)}, f32[2,2,16,256]{3,2,1,0:T(8,128)S(1)}, u32[]{:S(2)}, u32[]{:S(2)}) %collective-permute-start.10) | collective-permute-done | bytes 65568 | tf_op jit(solution)/shard_map/ppermute | solution.py:423
  33.5 0.1 collective-permute-start.11
  33.6 0.7 %multiply_bitcast_fusion = f32[2,1,128,128]{3,2,1,0:T(8,128)} fusion(bf16[2,128,128]{2,1,0:T(8,128)(2,1)S(1)} %collective-permute-done.9, bf16[2,128,128]{2,1,0:T(8,128)(2,1)S(1)} %collective-permute-done.8, bf16[2,128,128]{2,1,0:T(8,128)(2,1)S(1)} %collective-permute-done.7, bf16[2,128,128]{2,1,0:T(8,128)(2,1)S(1)} %get-tuple-element.34.refs_10_, ...), kind=kLoop, calls=%fused_computation.1 | loop fusion | flops 327680 | bytes 458752
  34.3 0.5 %collective-permute-done.11 = f32[2,16,256]{2,1,0:T(8,128)S(1)} collective-permute-done((f32[2,16,256]{2,1,0:T(8,128)S(1)}, f32[2,16,256]{2,1,0:T(8,128)S(1)}, u32[]{:S(2)}, u32[]{:S(2)}) %collective-permute-start.11) | collective-permute-done | bytes 32800 | tf_op jit(solution)/shard_map/ppermute | solution.py:423
  34.8 0.6 %fusion = f32[2,16,256]{2,1,0:T(8,128)} fusion(f32[2,16,256]{2,1,0:T(8,128)S(1)} %collective-permute-done.11, f32[2,2,16,256]{3,2,1,0:T(8,128)S(1)} %add.30), kind=kLoop, calls=%fused_computation.7 | loop fusion | flops 8192 | bytes 98304 | tf_op jit(solution)/shard_map/add | solution.py:462
  (24 shorter events, 0.1 us)
Async XLA Ops:
  0.6 8.0 %copy-start = (bf16[2,1,128,128]{3,2,1,0:T(8,128)(2,1)S(1)}, bf16[2,1,128,128]{3,2,1,0:T(8,128)(2,1)}, u32[]{:S(2)}) copy-start(bf16[2,1,128,128]{3,2,1,0:T(8,128)(2,1)} %refs_7_.1) | copy-start | bytes 196612
  0.6 8.0 %copy-start.5 = (s32[2,2,32]{2,1,0:T(2,128)S(1)}, s32[2,2,32]{2,1,0:T(2,128)}, u32[]{:S(2)}) copy-start(s32[2,2,32]{2,1,0:T(2,128)} %refs_1_.8) | copy-start | bytes 1540
  0.7 8.0 %collective-permute-start.1 = (bf16[2,1,512,1024]{3,2,0,1:T(8,128)(2,1)}, bf16[2,1,512,1024]{3,2,0,1:T(8,128)(2,1)S(1)}, u32[]{:S(2)}, u32[]{:S(2)}) collective-permute-start(bf16[2,1,512,1024]{3,2,0,1:T(8,128)(2,1)} %bitcast.34), channel_id=1, source_target_pairs={{0,2},{2,0},{1,3},{3,1},{4,6},{6,4},{5,7},{7,5},{8,10},{10,8},{9,1... | collective-permute-start | bytes 6291464 | tf_op jit(solution)/shard_map/ppermute | solution.py:423
  1.2 15.1 %collective-permute-start.2 = (bf16[2,1,128,128]{3,2,0,1:T(8,128)(2,1)}, bf16[2,1,128,128]{3,2,0,1:T(8,128)(2,1)S(1)}, u32[]{:S(2)}, u32[]{:S(2)}) collective-permute-start(bf16[2,1,128,128]{3,2,0,1:T(8,128)(2,1)} %bitcast.30), channel_id=1, source_target_pairs={{0,8},{8,0},{16,24},{24,16},{1,9},{9,1},{17,25},{25,17},{2,10},{10... | collective-permute-start | bytes 196616 | tf_op jit(solution)/shard_map/ppermute | solution.py:423
  3.8 12.4 %collective-permute-start.3 = (bf16[2,1,128,128]{3,2,0,1:T(8,128)(2,1)}, bf16[2,1,128,128]{3,2,0,1:T(8,128)(2,1)S(1)}, u32[]{:S(2)}, u32[]{:S(2)}) collective-permute-start(bf16[2,1,128,128]{3,2,0,1:T(8,128)(2,1)} %bitcast.31), channel_id=1, source_target_pairs={{0,16},{8,24},{16,0},{24,8},{1,17},{9,25},{17,1},{25,9},{2,18},{10... | collective-permute-start | bytes 196616 | tf_op jit(solution)/shard_map/ppermute | solution.py:423
  6.4 9.8 %collective-permute-start.4 = (bf16[2,1,128,128]{3,2,0,1:T(8,128)(2,1)}, bf16[2,1,128,128]{3,2,0,1:T(8,128)(2,1)S(1)}, u32[]{:S(2)}, u32[]{:S(2)}) collective-permute-start(bf16[2,1,128,128]{3,2,0,1:T(8,128)(2,1)} %bitcast.32), channel_id=1, source_target_pairs={{0,24},{8,16},{16,8},{24,0},{1,25},{9,17},{17,9},{25,1},{2,26},{10... | collective-permute-start | bytes 196616 | tf_op jit(solution)/shard_map/ppermute | solution.py:423
  6.4 2.2 %collective-permute-start = (s32[2,2,32]{2,1,0:T(2,128)}, s32[2,2,32]{2,1,0:T(2,128)S(1)}, u32[]{:S(2)}, u32[]{:S(2)}) collective-permute-start(s32[2,2,32]{2,1,0:T(2,128)} %refs_1_.8), channel_id=1, source_target_pairs={{0,2},{2,0},{1,3},{3,1},{4,6},{6,4},{5,7},{7,5},{8,10},{10,8},{9,1... | collective-permute-start | bytes 1544 | tf_op jit(solution)/shard_map/ppermute | solution.py:423
  11.5 5.1 %copy-start.1 = (bf16[256,256]{1,0:T(8,128)(2,1)S(1)}, bf16[256,256]{1,0:T(8,128)(2,1)}, u32[]{:S(2)}) copy-start(bf16[256,256]{1,0:T(8,128)(2,1)} %constant.31.clone.refs_4_) | copy-start | bytes 393220
  11.5 5.1 %copy-start.2 = (bf16[256,128]{1,0:T(8,128)(2,1)S(1)}, bf16[256,128]{1,0:T(8,128)(2,1)}, u32[]{:S(2)}) copy-start(bf16[256,128]{1,0:T(8,128)(2,1)} %constant.33.clone.refs_6_) | copy-start | bytes 196612
  11.5 5.1 %copy-start.3 = (bf16[160,128]{1,0:T(8,128)(2,1)S(1)}, bf16[160,128]{1,0:T(8,128)(2,1)}, u32[]{:S(2)}) copy-start(bf16[160,128]{1,0:T(8,128)(2,1)} %constant.30.clone.refs_3_) | copy-start | bytes 122884
  11.5 5.1 %copy-start.4 = (bf16[64,160]{1,0:T(8,128)(2,1)S(1)}, bf16[64,160]{1,0:T(8,128)(2,1)}, u32[]{:S(2)}) copy-start(bf16[64,160]{1,0:T(8,128)(2,1)} %constant.32.clone.refs_5_) | copy-start | bytes 61444
  11.6 9.2 %collective-permute-start.6 = (bf16[8,128,128]{2,1,0:T(8,128)(2,1)S(1)}, bf16[8,128,128]{2,1,0:T(8,128)(2,1)S(1)}, u32[]{:S(2)}, u32[]{:S(2)}) collective-permute-start(bf16[8,128,128]{2,1,0:T(8,128)(2,1)S(1)} %warp.2.refs_7_), channel_id=1, source_target_pairs={{0,4},{4,0},{1,5},{5,1},{2,6},{6,2},{3,7},{7,3},{8,12},{12,8},{9,1... | collective-permute-start | bytes 786440 | tf_op jit(solution)/shard_map/ppermute | solution.py:423
  16.3 9.7 %collective-permute-start.5 = (bf16[8,128,128]{2,1,0:T(8,128)(2,1)S(1)}, bf16[8,128,128]{2,1,0:T(8,128)(2,1)S(1)}, u32[]{:S(2)}, u32[]{:S(2)}) collective-permute-start(bf16[8,128,128]{2,1,0:T(8,128)(2,1)S(1)} %pad_maximum_fusion.refs_9_), channel_id=1, source_target_pairs={{0,4},{4,0},{1,5},{5,1},{2,6},{6,2},{3,7},{7,3},{8,12},{12,8},{9,1... | collective-permute-start | bytes 786440 | tf_op jit(solution)/shard_map/ppermute | solution.py:423
  20.8 10.2 %collective-permute-start.7 = (bf16[2,128,128]{2,1,0:T(8,128)(2,1)S(1)}, bf16[2,128,128]{2,1,0:T(8,128)(2,1)S(1)}, u32[]{:S(2)}, u32[]{:S(2)}) collective-permute-start(bf16[2,128,128]{2,1,0:T(8,128)(2,1)S(1)} %get-tuple-element.48), channel_id=1, source_target_pairs={{0,24},{8,16},{16,8},{24,0},{1,25},{9,17},{17,9},{25,1},{2,26},{10... | collective-permute-start | bytes 196616 | tf_op jit(solution)/shard_map/ppermute | solution.py:423
  24.7 6.3 %collective-permute-start.8 = (bf16[2,128,128]{2,1,0:T(8,128)(2,1)S(1)}, bf16[2,128,128]{2,1,0:T(8,128)(2,1)S(1)}, u32[]{:S(2)}, u32[]{:S(2)}) collective-permute-start(bf16[2,128,128]{2,1,0:T(8,128)(2,1)S(1)} %get-tuple-element.47), channel_id=1, source_target_pairs={{0,8},{8,0},{16,24},{24,16},{1,9},{9,1},{17,25},{25,17},{2,10},{10... | collective-permute-start | bytes 196616 | tf_op jit(solution)/shard_map/ppermute | solution.py:423
  24.7 6.3 %collective-permute-start.9 = (bf16[2,128,128]{2,1,0:T(8,128)(2,1)S(1)}, bf16[2,128,128]{2,1,0:T(8,128)(2,1)S(1)}, u32[]{:S(2)}, u32[]{:S(2)}) collective-permute-start(bf16[2,128,128]{2,1,0:T(8,128)(2,1)S(1)} %get-tuple-element.46), channel_id=1, source_target_pairs={{0,16},{8,24},{16,0},{24,8},{1,17},{9,25},{17,1},{25,9},{2,18},{10... | collective-permute-start | bytes 196616 | tf_op jit(solution)/shard_map/ppermute | solution.py:423
  29.2 4.3 %collective-permute-start.10 = (f32[2,2,16,256]{3,2,1,0:T(8,128)S(1)}, f32[2,2,16,256]{3,2,1,0:T(8,128)S(1)}, u32[]{:S(2)}, u32[]{:S(2)}) collective-permute-start(f32[2,2,16,256]{3,2,1,0:T(8,128)S(1)} %get-tuple-element.40), channel_id=1, source_target_pairs={{0,1},{1,0},{2,3},{3,2},{4,5},{5,4},{6,7},{7,6},{8,9},{9,8},{10,11... | collective-permute-start | bytes 196616 | tf_op jit(solution)/shard_map/ppermute | solution.py:423
  33.5 1.3 %collective-permute-start.11 = (f32[2,16,256]{2,1,0:T(8,128)S(1)}, f32[2,16,256]{2,1,0:T(8,128)S(1)}, u32[]{:S(2)}, u32[]{:S(2)}) collective-permute-start(f32[2,16,256]{2,1,0:T(8,128)S(1)} %slice_bitcast_fusion), channel_id=1, source_target_pairs={{0,2},{2,0},{1,3},{3,1},{4,6},{6,4},{5,7},{7,5},{8,10},{10,8},{9,1... | collective-permute-start | bytes 98312 | tf_op jit(solution)/shard_map/ppermute | solution.py:423

commit v16 on v15

--- a/solution.py
+++ b/solution.py
@@ -82,36 +82,6 @@
 
 def step_band(place_ref, step, across, own):
     return (place_ref[0] ^ step) * (4 * own) // across
-
-
-def stage_kernel(count, *refs):
-    sources, targets, sems = refs[:count], refs[count + 1 : 2 * count + 1], refs[-1]
-    copies = [
-        pltpu.make_async_copy(source, target, sems.at[at])
-        for at, (source, target) in enumerate(zip(sources, targets))
-    ]
-    for copy in copies:
-        copy.start()
-    for copy in copies:
-        copy.wait()
-
-
-def stage(arrays, after):
-    kept = [pltpu.with_memory_space_constraint(one, pltpu.HBM) for one in arrays]
-    count = len(arrays)
-    return pl.pallas_call(
-        functools.partial(stage_kernel, count),
-        out_shape=[jax.ShapeDtypeStruct(one.shape, one.dtype) for one in arrays],
-        in_specs=[pl.BlockSpec(memory_space=pltpu.HBM)] * count
-        + [pl.BlockSpec(memory_space=pl.ANY)],
-        out_specs=[pl.BlockSpec(memory_space=pltpu.VMEM)] * count,
-        scratch_shapes=[pltpu.SemaphoreType.DMA((count,))],
-        compiler_params=pltpu.CompilerParams(vmem_limit_bytes=VMEM_LIMIT),
-        cost_estimate=pl.CostEstimate(
-            flops=0, bytes_accessed=2 * sum(one.nbytes for one in arrays), transcendentals=0
-        ),
-        name="stage",
-    )(*kept, pltpu.with_memory_space_constraint(after, pltpu.HBM))
 
 
 def warp_step(place_ref, step, other, code_refs, frame_refs, band_refs, down, across, block, own):
@@ -186,43 +156,103 @@
             jnp.concatenate(partials + edges, axis=0),
             preferred_element_type=jnp.float32,
         )
-        totals.append(total.astype(jnp.bfloat16))
+        totals.append(total)
     return totals
 
 
-def warp_kernel(down, across, block, own, other, *refs):
-    place_ref, *code_refs = refs[:3]
-    frame_refs, band_refs, out_refs = refs[3:5], refs[5:7], refs[8:]
-    depth = out_refs[0].shape[0] // own if other else len(out_refs)
-    for step in range(depth):
+def first_kernel(down, across, block, own, place_ref, codes_ref, *refs):
+    sources, (out_ref, token_ref) = refs[:3], refs[3:5]
+    frames_ref, *band_refs = targets = refs[5:8]
+    copies = [
+        pltpu.make_async_copy(source, target, refs[8].at[at])
+        for at, (source, target) in enumerate(zip(sources, targets))
+    ]
+    for copy in copies:
+        copy.start()
+    token_ref[...] = jnp.zeros(token_ref.shape, jnp.float32)
+    for copy in copies:
+        copy.wait()
+    for step in range(out_ref.shape[0] // own):
         totals = warp_step(
-            place_ref, step, other, code_refs, frame_refs, band_refs, down, across, block, own
+            place_ref, step, 1, [codes_ref], [frames_ref], band_refs, down, across, block, own
         )
         for one, total in enumerate(totals):
-            if other:
-                out_refs[0][step * own + one] = total
-            else:
-                out_refs[step][one] = total
-
-
-def warp_sums(
-    place, codes, other_codes, frames, other_frames, bands, after, other, depth, block, own
-):
+            out_ref[step * own + one] = total
+
+
+def first_sums(place, codes, frames, bands, depth, block, own):
+    rows, cols = frames.shape[1:]
+    down, across = rows // block, cols // block
+    sources = [pltpu.with_memory_space_constraint(one, pltpu.HBM) for one in (frames, *bands)]
+    smem = pl.BlockSpec(memory_space=pltpu.SMEM)
+    return pl.pallas_call(
+        functools.partial(first_kernel, down, across, block, own),
+        out_shape=[
+            jax.ShapeDtypeStruct((depth * own, block, block), jnp.float32),
+            jax.ShapeDtypeStruct((8, LANES), jnp.float32),
+        ],
+        in_specs=[smem] * 2 + [pl.BlockSpec(memory_space=pltpu.HBM)] * len(sources),
+        out_specs=[pl.BlockSpec(memory_space=pltpu.VMEM)] * 2,
+        scratch_shapes=[pltpu.VMEM(one.shape, one.dtype) for one in sources]
+        + [pltpu.SemaphoreType.DMA((len(sources),))],
+        compiler_params=pltpu.CompilerParams(vmem_limit_bytes=VMEM_LIMIT),
+        cost_estimate=pl.CostEstimate(
+            flops=2 * frames.size * block * 8, bytes_accessed=frames.size * 4, transcendentals=0
+        ),
+        name="first_warp",
+    )(place, codes, *sources)
+
+
+def second_kernel(down, across, block, own, place_ref, codes_ref, frames_ref, *refs):
+    band_refs, first_ref, out_ref = refs[:2], refs[2], refs[4]
+    for step in range(out_ref.shape[0] // own):
+        totals = warp_step(
+            place_ref, step, 1, [codes_ref], [frames_ref], band_refs, down, across, block, own
+        )
+        for one, total in enumerate(totals):
+            at = step * own + one
+            out_ref[at] = (first_ref[at] + total).astype(jnp.bfloat16)
+
+
+def second_sums(place, codes, frames, bands, first, after, block, own):
+    rows, cols = frames.shape[1:]
+    down, across = rows // block, cols // block
+    smem = pl.BlockSpec(memory_space=pltpu.SMEM)
+    vmem = pl.BlockSpec(memory_space=pltpu.VMEM)
+    return pl.pallas_call(
+        functools.partial(second_kernel, down, across, block, own),
+        out_shape=jax.ShapeDtypeStruct(first.shape, jnp.bfloat16),
+        in_specs=[smem] * 2 + [vmem] * (2 + len(bands)) + [pl.BlockSpec(memory_space=pl.ANY)],
+        out_specs=vmem,
+        compiler_params=pltpu.CompilerParams(vmem_limit_bytes=VMEM_LIMIT),
+        cost_estimate=pl.CostEstimate(
+            flops=2 * frames.size * block * 8, bytes_accessed=frames.size * 4, transcendentals=0
+        ),
+        name="second_warp",
+    )(place, codes, frames, *bands, first, after)
+
+
+def warp_kernel(down, across, block, own, place_ref, codes_ref, other_codes_ref, *refs):
+    code_refs, frame_refs = (codes_ref, other_codes_ref), refs[:2]
+    band_refs, out_refs = refs[2:4], refs[5:]
+    for step, out_ref in enumerate(out_refs):
+        totals = warp_step(
+            place_ref, step, 0, code_refs, frame_refs, band_refs, down, across, block, own
+        )
+        for one, total in enumerate(totals):
+            out_ref[one] = total.astype(jnp.bfloat16)
+
+
+def warp_sums(place, codes, other_codes, frames, other_frames, bands, after, depth, block, own):
     vols, rows, cols = frames.shape
     down, across = rows // block, cols // block
     smem = pl.BlockSpec(memory_space=pltpu.SMEM)
     vmem = pl.BlockSpec(memory_space=pltpu.VMEM)
-    if other:
-        out_shape = [jax.ShapeDtypeStruct((depth * own, block, block), jnp.bfloat16)]
-    else:
-        out_shape = [jax.ShapeDtypeStruct((own, block, block), jnp.bfloat16)] * depth
     return pl.pallas_call(
-        functools.partial(warp_kernel, down, across, block, own, other),
-        out_shape=out_shape,
-        in_specs=[smem] * 3
-        + [vmem] * (2 + len(bands))
-        + [pl.BlockSpec(memory_space=pl.ANY)],
-        out_specs=[vmem] * len(out_shape),
+        functools.partial(warp_kernel, down, across, block, own),
+        out_shape=[jax.ShapeDtypeStruct((own, block, block), jnp.bfloat16)] * depth,
+        in_specs=[smem] * 3 + [vmem] * (2 + len(bands)) + [pl.BlockSpec(memory_space=pl.ANY)],
+        out_specs=[vmem] * depth,
         compiler_params=pltpu.CompilerParams(vmem_limit_bytes=VMEM_LIMIT),
         cost_estimate=pl.CostEstimate(
             flops=2 * vols * rows * cols * block * 8,
@@ -242,7 +272,6 @@
         found[...] = found_ref[...]
     else:
         found = refs[11]
-        found[...] = jnp.zeros(found.shape, jnp.float32)
 
     row_table = row_ref[...]
     col_table = col_ref[...]
@@ -352,7 +381,8 @@
                     at = (pair * many + order) * 2 + side
                     one = lags[at * span : (at + 1) * span]
                     one = pltpu.roll(one, span - SHIFT - row_shift, 0)[:WIN]
-                    found[order, pl.ds(pl.multiple_of(index * WIN, WIN), WIN), :] = pltpu.roll(
+                    at = index // (2 * own) * own + (2 * pair + side) % own
+                    found[order, pl.ds(pl.multiple_of(at * WIN, WIN), WIN), :] = pltpu.roll(
                         one, LANES - SHIFT - col_shift, 1
                     )
 
@@ -387,7 +417,7 @@
     kept = -(-(block // 2 + 1) // 8) * 8
     smem = pl.BlockSpec(memory_space=pltpu.SMEM)
     vmem = pl.BlockSpec(memory_space=pltpu.VMEM)
-    blocks = down * across
+    blocks = down * across // 2
     many = 2 * vols * 2 * own
     found = jax.ShapeDtypeStruct((2 * vols, blocks * WIN, LANES), jnp.float32)
     if other:
@@ -429,20 +459,27 @@
     depth = lax.axis_size("z")
     planes = lax.axis_size("plane")
     place = jnp.stack([lax.axis_index(axis) for axis in ("z", "y", "core", "plane")])
+    core = place[2]
     other_codes = exchange(shift_codes, "core", 2, 1)
     other_frames = exchange(frames, "core", 2, 1)
-    staged, *bands = stage([frames, *tap_constants(block)], template)
-    turns = [depth - 1, *range(1, depth - 1)]
-    fetched = {turn: exchange(template, "z", depth, turn) for turn in turns}
+    bands = tap_constants(block)
+    sizes = (depth, block, own)
+    first = [first_sums(place, shift_codes, frames[:, p], bands, *sizes) for p in range(pl_dev)]
+    later, token = lax.optimization_barrier((template, first[0][1]))
+    fetched = {depth - 1: exchange(template, "z", depth, depth - 1)}
+    for turn in range(1, depth - 1):
+        fetched[turn] = exchange(later, "z", depth, turn)
     pieces = [template] + [fetched[turn] for turn in range(1, depth)]
     averages, correlation = [], 0.0
     volumes = vol_dev * depth * 4
     for p in range(pl_dev):
-        work = (place, shift_codes, other_codes, staged[:, p], other_frames[:, p])
+        work = (place, shift_codes, other_codes, frames[:, p], other_frames[:, p])
         sizes = (depth, block, own)
-        (far_sums,) = warp_sums(*work, bands, template, 1, *sizes)
+        far_sums = second_sums(
+            place, other_codes, other_frames[:, p], bands, first[p][0], token, block, own
+        )
         taken = exchange(far_sums, "y", 2, 1)
-        near_sums = warp_sums(*work, bands, far_sums, 0, *sizes)
+        near_sums = warp_sums(*work, bands, far_sums, *sizes)
         pieces, near_sums = lax.optimization_barrier((pieces, near_sums))
         near = jnp.concatenate([piece[:, p] for piece in pieces], axis=0)
         far = exchange(near, "y", 2, 1)
@@ -450,7 +487,7 @@
             one.astype(jnp.float32) + taken[step * own : (step + 1) * own].astype(jnp.float32)
             for step, one in enumerate(near_sums)
         ]
-        moved = [exchange(sums[turn].astype(jnp.bfloat16), "z", depth, turn) for turn in turns]
+        moved = [exchange(sums[turn].astype(jnp.bfloat16), "z", depth, turn) for turn in [depth - 1, *range(1, depth - 1)]]
         sizes = (planes, depth, own)
         (part,) = lag_windows(*work, near, near_sums[0], 0, *sizes)
         found, *given = lag_windows(*work, far, part, 1, *sizes)
@@ -459,7 +496,9 @@
         averages.append(total * (1.0 / volumes))
         for turn, one in enumerate(given):
             found = found + exchange(one, "plane", planes, turn + 1)
-        correlation += found[0] + exchange(found[1], "core", 2, 1)
+        pair = (found[0], exchange(found[1], "core", 2, 1))
+        pair = [jnp.where(core == at, *pair).reshape(vol_dev, -1, 1, own, WIN * WIN) for at in (0, 1)]
+        correlation += jnp.concatenate(pair, axis=2).reshape(vol_dev, -1, WIN * WIN)
     return (correlation, jnp.stack(averages, axis=1))
 
 

time: 35.6 us -> 37.5 us (1.053)
  Pallas kernels: 13.9 us -> 15.6 us
  local copies, waits for them, and re-layouts: 0.04 us -> 1.42 us
  waiting for transfers between devices: 4.91 us -> 3.87 us
  other arithmetic: 1.5 us -> 0.9 us
  starting transfers between devices: 14.3 us -> 14.7 us
    pallas_call x3, Pallas kernels: 7.81 us -> 9.79 us  [the longest x1 4.55 us: first_sums(): pl.pallas_call(functools.partial(first_kernel, down, across, block, own),...]
    ppermute x12, waiting for transfers between devices: 4.91 us -> 3.87 us  [exchange(): return lax.ppermute(value, axes, [(at, at ^ turn) for at in range(size)])]
    unnamed x12 -> x20, local copies, waits for them, and re-layouts: 0.04 us -> 0.73 us
    reshape x0 -> x3, local copies, waits for them, and re-layouts: none -> 0.67 us  [the longest x1 0.64 us: on_device(): correlation += jnp.concatenate(pair, axis=2).reshape(vol_dev, -1, WIN * WIN)]
    add x1 -> x0, other arithmetic: 0.62 us -> none  [on_device(): correlation += found[0] + exchange(found[1], 'core', 2, 1)]
    ppermute x12, starting transfers between devices: 14.3 us -> 14.7 us  [exchange(): return lax.ppermute(value, axes, [(at, at ^ turn) for at in range(size)])]
  transfers between devices with their start and end apart: 12 -> 12, of which waited for: 4 -> 3; matrix products, arithmetic and copies ran while one was open for 2% -> 2% of each run, Pallas kernels for 39% -> 42%
where the time goes in v16:
time: 37.5 us; the launch traced here: 37.3 us
  Pallas kernels  15.6 us (42%)
  starting transfers between devices  14.7 us (39%)
  waiting for transfers between devices  3.87 us (10%)
  local copies, waits for them, and re-layouts  1.42 us (4%)
  other arithmetic  0.9 us (2%)
  between operations  0.82 us (2%)
    ppermute x12, starting transfers between devices, exchange(): return lax.ppermute(value, axes, [(at, at ^ turn) for at in range(size)])  14.7 us
    pallas_call x2, Pallas kernels, lag_windows(): pl.pallas_call(functools.partial(spectrum_kernel, vols, across, block, ow...  5.83 us
    pallas_call x1, Pallas kernels, first_sums(): pl.pallas_call(functools.partial(first_kernel, down, across, block, own),...  4.55 us
    ppermute x12, waiting for transfers between devices, exchange(): return lax.ppermute(value, axes, [(at, at ^ turn) for at in range(size)])  3.87 us
    pallas_call x1, Pallas kernels, warp_sums(): pl.pallas_call(functools.partial(warp_kernel, down, across, block, own),...  2.84 us
    pallas_call x1, Pallas kernels, second_sums(): pl.pallas_call(functools.partial(second_kernel, down, across, block, own)...  2.39 us
  transfers between devices with their start and end apart: 12, of which 3 were waited for; matrix products, arithmetic and copies ran while one was open for 2% of the time, Pallas kernels for 42%

profile of v16, /device:TPU:0, one launch (start us, length us, event | category | flops | bytes accessed | tf_op | source)
XLA Modules:
  0.0 37.3 jit_solution(16066730244078098335)
XLA Ops:
  0.6 0.5 %collective-permute-start.1 = (bf16[2,1,512,1024]{3,2,0,1:T(8,128)(2,1)}, bf16[2,1,512,1024]{3,2,0,1:T(8,128)(2,1)S(1)}, u32[]{:S(2)}, u32[]{:S(2)}) collective-permute-start(bf16[2,1,512,1024]{3,2,0,1:T(8,128)(2,1)} %bitcast.25), channel_id=1, source_target_pairs={{0,2},{2,0},{1,3},{3,1},{4,6},{6,4},{5,7},{7,5},{8,10},{10,8},{9,1... | collective-permute-start | bytes 6291464 | tf_op jit(solution)/shard_map/ppermute | solution.py:453
  1.1 0.1 collective-permute-start
  1.2 0.1 pad_add_fusion.place_ref.refs_0_
  1.3 0.7 %copy-done.5 = s32[2,2,32]{2,1,0:T(2,128)S(1)} copy-done((s32[2,2,32]{2,1,0:T(2,128)S(1)}, s32[2,2,32]{2,1,0:T(2,128)}, u32[]{:S(2)}) %copy-start.5) | copy-done | bytes 536
  2.0 4.5 %first_warp.1 = (f32[8,128,128]{2,1,0:T(8,128)S(1)}, f32[8,128]{1,0:T(8,128)S(1)}) custom-call(s32[4]{0:T(128)S(1)} %pad_add_fusion.place_ref.refs_0_, s32[2,2,32]{2,1,0:T(2,128)S(1)} %copy-done.5, bf16[2,512,1024]{2,1,0:T(8,128)(2,1)} %bitcast.26, f32[16,176,128]{2,1,0:T(8,128)} %constant.32.clone.refs_1_.refs_0_.refs_2_, ...), custom_call_target="tpu_custom_call" | custom-call | flops 2147483648 | bytes 4194304 | tf_op jit(solution)/shard_map/first_warp/pallas_call | solution.py:188
  6.6 3.1 %collective-permute-start.2 = (bf16[2,1,128,128]{3,2,0,1:T(8,128)(2,1)S(1)}, bf16[2,1,128,128]{3,2,0,1:T(8,128)(2,1)S(1)}, u32[]{:S(2)}, u32[]{:S(2)}) collective-permute-start(bf16[2,1,128,128]{3,2,0,1:T(8,128)(2,1)S(1)} %bitcast.34), channel_id=1, source_target_pairs={{0,8},{8,0},{16,24},{24,16},{1,9},{9,1},{17,25},{25,17},{2,10},{10... | collective-permute-start | bytes 196616 | tf_op jit(solution)/shard_map/ppermute | solution.py:453
  9.6 2.6 %collective-permute-start.3 = (bf16[2,1,128,128]{3,2,0,1:T(8,128)(2,1)S(1)}, bf16[2,1,128,128]{3,2,0,1:T(8,128)(2,1)S(1)}, u32[]{:S(2)}, u32[]{:S(2)}) collective-permute-start(bf16[2,1,128,128]{3,2,0,1:T(8,128)(2,1)S(1)} %bitcast.35), channel_id=1, source_target_pairs={{0,16},{8,24},{16,0},{24,8},{1,17},{9,25},{17,1},{25,9},{2,18},{10... | collective-permute-start | bytes 196616 | tf_op jit(solution)/shard_map/ppermute | solution.py:453
  12.3 2.4 %second_warp.1.refs_4_ = bf16[8,128,128]{2,1,0:T(8,128)(2,1)S(1)} custom-call(s32[4]{0:T(128)S(1)} %pad_add_fusion.place_ref.refs_0_, s32[2,2,32]{2,1,0:T(2,128)S(1)} %collective-permute-done.codes_ref.other_codes_ref.refs_2_, bf16[2,512,1024]{2,1,0:T(8,128)(2,1)S(1)} %bitcast.30, f32[16,176,128]{2,1,0:T(8,128)S(1)} %copy-done.7, ...), custom_call_target="tpu_custom_call" | custom-call | flops 2147483648 | bytes 4194304 | tf_op jit(solution)/shard_map/second_warp/pallas_call | solution.py:222
  14.7 0.0 copy-start.1
  14.7 1.8 %collective-permute-start.6 = (bf16[8,128,128]{2,1,0:T(8,128)(2,1)S(1)}, bf16[8,128,128]{2,1,0:T(8,128)(2,1)S(1)}, u32[]{:S(2)}, u32[]{:S(2)}) collective-permute-start(bf16[8,128,128]{2,1,0:T(8,128)(2,1)S(1)} %second_warp.1.refs_4_), channel_id=1, source_target_pairs={{0,4},{4,0},{1,5},{5,1},{2,6},{6,2},{3,7},{7,3},{8,12},{12,8},{9,1... | collective-permute-start | bytes 786440 | tf_op jit(solution)/shard_map/ppermute | solution.py:453
  16.5 2.8 %warp.1 = (bf16[2,128,128]{2,1,0:T(8,128)(2,1)S(1)}, bf16[2,128,128]{2,1,0:T(8,128)(2,1)S(1)}, bf16[2,128,128]{2,1,0:T(8,128)(2,1)S(1)}, bf16[2,128,128]{2,1,0:T(8,128)(2,1)S(1)}) custom-call(s32[4]{0:T(128)S(1)} %pad_add_fusion.place_ref.refs_0_, s32[2,2,32]{2,1,0:T(2,128)S(1)} %copy-done.6, ...), custom_call_target="tpu_custom_call" | custom-call | flops 2147483648 | bytes 4718592 | tf_op jit(solution)/shard_map/warp/pallas_call | solution.py:251
  19.4 0.6 %collective-permute-start.5 = (bf16[8,128,128]{2,1,0:T(8,128)(2,1)S(1)}, bf16[8,128,128]{2,1,0:T(8,128)(2,1)S(1)}, u32[]{:S(2)}, u32[]{:S(2)}) collective-permute-start(bf16[8,128,128]{2,1,0:T(8,128)(2,1)S(1)} %pad_maximum_fusion.refs_9_), channel_id=1, source_target_pairs={{0,4},{4,0},{1,5},{5,1},{2,6},{6,2},{3,7},{7,3},{8,12},{12,8},{9,1... | collective-permute-start | bytes 786440 | tf_op jit(solution)/shard_map/ppermute | solution.py:453
  20.0 2.8 %lag_windows.2.refs_10_ = f32[4,256,128]{2,1,0:T(8,128)S(1)} custom-call(s32[4]{0:T(128)S(1)} %pad_add_fusion.place_ref.refs_0_, s32[2,2,32]{2,1,0:T(2,128)S(1)} %copy-done.6, s32[2,2,32]{2,1,0:T(2,128)S(1)} %collective-permute-done.codes_ref.other_codes_ref.refs_2_, bf16[160,128]{1,0:T(8,128)(2,1)S(1)} %copy-done.3, bf16[256,256]{1,0:T(8,128)(2,1)S(1)} %copy-done.1, ...), custom_call_target="tpu_custom_call" | custom-call | flops 3221225472 | bytes 4718592 | tf_op jit(solution)/shard_map/lag_windows/pallas_call | solution.py:432
  22.8 1.0 %collective-permute-done.6 = bf16[8,128,128]{2,1,0:T(8,128)(2,1)S(1)} collective-permute-done((bf16[8,128,128]{2,1,0:T(8,128)(2,1)S(1)}, bf16[8,128,128]{2,1,0:T(8,128)(2,1)S(1)}, u32[]{:S(2)}, u32[]{:S(2)}) %collective-permute-start.6) | collective-permute-done | bytes 262176 | tf_op jit(solution)/shard_map/ppermute | solution.py:453
  23.8 0.1 add_convert_fusion
  23.9 3.6 %collective-permute-start.7 = (bf16[2,128,128]{2,1,0:T(8,128)(2,1)S(1)}, bf16[2,128,128]{2,1,0:T(8,128)(2,1)S(1)}, u32[]{:S(2)}, u32[]{:S(2)}) collective-permute-start(bf16[2,128,128]{2,1,0:T(8,128)(2,1)S(1)} %get-tuple-element.50), channel_id=1, source_target_pairs={{0,24},{8,16},{16,8},{24,0},{1,25},{9,17},{17,9},{25,1},{2,26},{10... | collective-permute-start | bytes 196616 | tf_op jit(solution)/shard_map/ppermute | solution.py:453
  27.5 0.9 %collective-permute-start.9 = (bf16[2,128,128]{2,1,0:T(8,128)(2,1)S(1)}, bf16[2,128,128]{2,1,0:T(8,128)(2,1)S(1)}, u32[]{:S(2)}, u32[]{:S(2)}) collective-permute-start(bf16[2,128,128]{2,1,0:T(8,128)(2,1)S(1)} %get-tuple-element.48), channel_id=1, source_target_pairs={{0,16},{8,24},{16,0},{24,8},{1,17},{9,25},{17,1},{25,9},{2,18},{10... | collective-permute-start | bytes 196616 | tf_op jit(solution)/shard_map/ppermute | solution.py:453
  28.3 3.0 %lag_windows.3 = (f32[2,2,8,256]{3,2,1,0:T(8,128)S(1)}, f32[2,2,8,256]{3,2,1,0:T(8,128)S(1)}) custom-call(s32[4]{0:T(128)S(1)} %pad_add_fusion.place_ref.refs_0_, s32[2,2,32]{2,1,0:T(2,128)S(1)} %copy-done.6, s32[2,2,32]{2,1,0:T(2,128)S(1)} %collective-permute-done.codes_ref.other_codes_ref.refs_2_, bf16[160,128]{1,0:T(8,128)(2,1)S(1)} %copy-done.3, ...), custom_call_target="tpu_custom_call" | custom-call | flops 805306368 | bytes 4718592 | tf_op jit(solution)/shard_map/lag_windows/pallas_call | solution.py:432
  31.4 1.6 %collective-permute-start.10 = (f32[2,2,8,256]{3,2,1,0:T(8,128)S(1)}, f32[2,2,8,256]{3,2,1,0:T(8,128)S(1)}, u32[]{:S(2)}, u32[]{:S(2)}) collective-permute-start(f32[2,2,8,256]{3,2,1,0:T(8,128)S(1)} %get-tuple-element.42), channel_id=1, source_target_pairs={{0,1},{1,0},{2,3},{3,2},{4,5},{5,4},{6,7},{7,6},{8,9},{9,8},{10,11... | collective-permute-start | bytes 98312 | tf_op jit(solution)/shard_map/ppermute | solution.py:453
  33.0 2.4 %collective-permute-done.10 = f32[2,2,8,256]{3,2,1,0:T(8,128)S(1)} collective-permute-done((f32[2,2,8,256]{3,2,1,0:T(8,128)S(1)}, f32[2,2,8,256]{3,2,1,0:T(8,128)S(1)}, u32[]{:S(2)}, u32[]{:S(2)}) %collective-permute-start.10) | collective-permute-done | bytes 32800 | tf_op jit(solution)/shard_map/ppermute | solution.py:453
  35.4 0.1 collective-permute-start.11
  35.4 0.7 %multiply_bitcast_fusion = f32[2,1,128,128]{3,2,1,0:T(8,128)} fusion(bf16[2,128,128]{2,1,0:T(8,128)(2,1)S(1)} %collective-permute-done.9, bf16[2,128,128]{2,1,0:T(8,128)(2,1)S(1)} %collective-permute-done.8, bf16[2,128,128]{2,1,0:T(8,128)(2,1)S(1)} %collective-permute-done.7, bf16[2,128,128]{2,1,0:T(8,128)(2,1)S(1)} %get-tuple-element.36.refs_10_, ...), kind=kLoop, calls=%fused_computation.1 | loop fusion | flops 327680 | bytes 458752
  36.1 0.5 %collective-permute-done.11 = f32[2,8,256]{2,1,0:T(8,128)S(1)} collective-permute-done((f32[2,8,256]{2,1,0:T(8,128)S(1)}, f32[2,8,256]{2,1,0:T(8,128)S(1)}, u32[]{:S(2)}, u32[]{:S(2)}) %collective-permute-start.11) | collective-permute-done | bytes 16416 | tf_op jit(solution)/shard_map/ppermute | solution.py:453
  36.7 0.6 %reshape.15 = f32[2,16,256]{2,1,0:T(8,128)} reshape(f32[2,4,2,2,256]{4,3,2,1,0:T(2,128)S(1)} %copy.19) | data formatting | bytes 65536 | tf_op jit(solution)/shard_map/reshape | solution.py:501
  (37 shorter events, 0.2 us)
Async XLA Ops:
  0.6 11.6 %collective-permute-start.1 = (bf16[2,1,512,1024]{3,2,0,1:T(8,128)(2,1)}, bf16[2,1,512,1024]{3,2,0,1:T(8,128)(2,1)S(1)}, u32[]{:S(2)}, u32[]{:S(2)}) collective-permute-start(bf16[2,1,512,1024]{3,2,0,1:T(8,128)(2,1)} %bitcast.25), channel_id=1, source_target_pairs={{0,2},{2,0},{1,3},{3,1},{4,6},{6,4},{5,7},{7,5},{8,10},{10,8},{9,1... | collective-permute-start | bytes 6291464 | tf_op jit(solution)/shard_map/ppermute | solution.py:453
  1.1 11.1 %collective-permute-start = (s32[2,2,32]{2,1,0:T(2,128)}, s32[2,2,32]{2,1,0:T(2,128)S(1)}, u32[]{:S(2)}, u32[]{:S(2)}) collective-permute-start(s32[2,2,32]{2,1,0:T(2,128)} %refs_1_.5), channel_id=1, source_target_pairs={{0,2},{2,0},{1,3},{3,1},{4,6},{6,4},{5,7},{7,5},{8,10},{10,8},{9,1... | collective-permute-start | bytes 1544 | tf_op jit(solution)/shard_map/ppermute | solution.py:453
  1.3 0.7 %copy-start.5 = (s32[2,2,32]{2,1,0:T(2,128)S(1)}, s32[2,2,32]{2,1,0:T(2,128)}, u32[]{:S(2)}) copy-start(s32[2,2,32]{2,1,0:T(2,128)} %refs_1_.5) | copy-start | bytes 1540
  2.0 4.6 %copy-start.9 = (bf16[2,1,128,128]{3,2,1,0:T(8,128)(2,1)S(1)}, bf16[2,1,128,128]{3,2,1,0:T(8,128)(2,1)}, u32[]{:S(2)}) copy-start(bf16[2,1,128,128]{3,2,1,0:T(8,128)(2,1)} %param.14) | copy-start | bytes 196612
  2.0 10.2 %copy-start.7 = (f32[16,176,128]{2,1,0:T(8,128)S(1)}, f32[16,176,128]{2,1,0:T(8,128)}, u32[]{:S(2)}) copy-start(f32[16,176,128]{2,1,0:T(8,128)} %constant.32.clone.refs_1_.refs_0_.refs_2_) | copy-start | bytes 4325380
  2.0 10.3 %copy-start.8 = (f32[16,2,32,128]{3,2,1,0:T(8,128)S(1)}, f32[16,2,32,128]{3,2,1,0:T(8,128)}, u32[]{:S(2)}) copy-start(f32[16,2,32,128]{3,2,1,0:T(8,128)} %constant.33.clone.refs_2_.refs_1_.refs_3_) | copy-start | bytes 1572868
  6.6 12.8 %collective-permute-start.2 = (bf16[2,1,128,128]{3,2,0,1:T(8,128)(2,1)S(1)}, bf16[2,1,128,128]{3,2,0,1:T(8,128)(2,1)S(1)}, u32[]{:S(2)}, u32[]{:S(2)}) collective-permute-start(bf16[2,1,128,128]{3,2,0,1:T(8,128)(2,1)S(1)} %bitcast.34), channel_id=1, source_target_pairs={{0,8},{8,0},{16,24},{24,16},{1,9},{9,1},{17,25},{25,17},{2,10},{10... | collective-permute-start | bytes 196616 | tf_op jit(solution)/shard_map/ppermute | solution.py:453
  9.6 9.7 %collective-permute-start.3 = (bf16[2,1,128,128]{3,2,0,1:T(8,128)(2,1)S(1)}, bf16[2,1,128,128]{3,2,0,1:T(8,128)(2,1)S(1)}, u32[]{:S(2)}, u32[]{:S(2)}) collective-permute-start(bf16[2,1,128,128]{3,2,0,1:T(8,128)(2,1)S(1)} %bitcast.35), channel_id=1, source_target_pairs={{0,16},{8,24},{16,0},{24,8},{1,17},{9,25},{17,1},{25,9},{2,18},{10... | collective-permute-start | bytes 196616 | tf_op jit(solution)/shard_map/ppermute | solution.py:453
  12.2 7.2 %collective-permute-start.4 = (bf16[2,1,128,128]{3,2,0,1:T(8,128)(2,1)S(1)}, bf16[2,1,128,128]{3,2,0,1:T(8,128)(2,1)S(1)}, u32[]{:S(2)}, u32[]{:S(2)}) collective-permute-start(bf16[2,1,128,128]{3,2,0,1:T(8,128)(2,1)S(1)} %bitcast.36), channel_id=1, source_target_pairs={{0,24},{8,16},{16,8},{24,0},{1,25},{9,17},{17,9},{25,1},{2,26},{10... | collective-permute-start | bytes 196616 | tf_op jit(solution)/shard_map/ppermute | solution.py:453
  12.3 4.3 %copy-start = (bf16[2,1,512,1024]{3,2,1,0:T(8,128)(2,1)S(1)}, bf16[2,1,512,1024]{3,2,1,0:T(8,128)(2,1)}, u32[]{:S(2)}) copy-start(bf16[2,1,512,1024]{3,2,1,0:T(8,128)(2,1)} %param.13) | copy-start | bytes 6291460
  12.3 4.2 %copy-start.6 = (s32[2,2,32]{2,1,0:T(2,128)S(1)}, s32[2,2,32]{2,1,0:T(2,128)}, u32[]{:S(2)}) copy-start(s32[2,2,32]{2,1,0:T(2,128)} %refs_1_.5) | copy-start | bytes 1540
  14.7 5.3 %copy-start.1 = (bf16[256,256]{1,0:T(8,128)(2,1)S(1)}, bf16[256,256]{1,0:T(8,128)(2,1)}, u32[]{:S(2)}) copy-start(bf16[256,256]{1,0:T(8,128)(2,1)} %constant.35.clone.refs_4_) | copy-start | bytes 393220
  14.7 5.3 %copy-start.2 = (bf16[256,128]{1,0:T(8,128)(2,1)S(1)}, bf16[256,128]{1,0:T(8,128)(2,1)}, u32[]{:S(2)}) copy-start(bf16[256,128]{1,0:T(8,128)(2,1)} %constant.37.clone.refs_6_) | copy-start | bytes 196612
  14.7 5.3 %copy-start.3 = (bf16[160,128]{1,0:T(8,128)(2,1)S(1)}, bf16[160,128]{1,0:T(8,128)(2,1)}, u32[]{:S(2)}) copy-start(bf16[160,128]{1,0:T(8,128)(2,1)} %constant.34.clone.refs_3_) | copy-start | bytes 122884
  14.7 5.3 %copy-start.4 = (bf16[64,160]{1,0:T(8,128)(2,1)S(1)}, bf16[64,160]{1,0:T(8,128)(2,1)}, u32[]{:S(2)}) copy-start(bf16[64,160]{1,0:T(8,128)(2,1)} %constant.36.clone.refs_5_) | copy-start | bytes 61444
  14.7 9.1 %collective-permute-start.6 = (bf16[8,128,128]{2,1,0:T(8,128)(2,1)S(1)}, bf16[8,128,128]{2,1,0:T(8,128)(2,1)S(1)}, u32[]{:S(2)}, u32[]{:S(2)}) collective-permute-start(bf16[8,128,128]{2,1,0:T(8,128)(2,1)S(1)} %second_warp.1.refs_4_), channel_id=1, source_target_pairs={{0,4},{4,0},{1,5},{5,1},{2,6},{6,2},{3,7},{7,3},{8,12},{12,8},{9,1... | collective-permute-start | bytes 786440 | tf_op jit(solution)/shard_map/ppermute | solution.py:453
  19.4 8.9 %collective-permute-start.5 = (bf16[8,128,128]{2,1,0:T(8,128)(2,1)S(1)}, bf16[8,128,128]{2,1,0:T(8,128)(2,1)S(1)}, u32[]{:S(2)}, u32[]{:S(2)}) collective-permute-start(bf16[8,128,128]{2,1,0:T(8,128)(2,1)S(1)} %pad_maximum_fusion.refs_9_), channel_id=1, source_target_pairs={{0,4},{4,0},{1,5},{5,1},{2,6},{6,2},{3,7},{7,3},{8,12},{12,8},{9,1... | collective-permute-start | bytes 786440 | tf_op jit(solution)/shard_map/ppermute | solution.py:453
  23.9 9.1 %collective-permute-start.7 = (bf16[2,128,128]{2,1,0:T(8,128)(2,1)S(1)}, bf16[2,128,128]{2,1,0:T(8,128)(2,1)S(1)}, u32[]{:S(2)}, u32[]{:S(2)}) collective-permute-start(bf16[2,128,128]{2,1,0:T(8,128)(2,1)S(1)} %get-tuple-element.50), channel_id=1, source_target_pairs={{0,24},{8,16},{16,8},{24,0},{1,25},{9,17},{17,9},{25,1},{2,26},{10... | collective-permute-start | bytes 196616 | tf_op jit(solution)/shard_map/ppermute | solution.py:453
  27.5 5.5 %collective-permute-start.8 = (bf16[2,128,128]{2,1,0:T(8,128)(2,1)S(1)}, bf16[2,128,128]{2,1,0:T(8,128)(2,1)S(1)}, u32[]{:S(2)}, u32[]{:S(2)}) collective-permute-start(bf16[2,128,128]{2,1,0:T(8,128)(2,1)S(1)} %get-tuple-element.49), channel_id=1, source_target_pairs={{0,8},{8,0},{16,24},{24,16},{1,9},{9,1},{17,25},{25,17},{2,10},{10... | collective-permute-start | bytes 196616 | tf_op jit(solution)/shard_map/ppermute | solution.py:453
  27.5 5.5 %collective-permute-start.9 = (bf16[2,128,128]{2,1,0:T(8,128)(2,1)S(1)}, bf16[2,128,128]{2,1,0:T(8,128)(2,1)S(1)}, u32[]{:S(2)}, u32[]{:S(2)}) collective-permute-start(bf16[2,128,128]{2,1,0:T(8,128)(2,1)S(1)} %get-tuple-element.48), channel_id=1, source_target_pairs={{0,16},{8,24},{16,0},{24,8},{1,17},{9,25},{17,1},{25,9},{2,18},{10... | collective-permute-start | bytes 196616 | tf_op jit(solution)/shard_map/ppermute | solution.py:453
  31.4 4.0 %collective-permute-start.10 = (f32[2,2,8,256]{3,2,1,0:T(8,128)S(1)}, f32[2,2,8,256]{3,2,1,0:T(8,128)S(1)}, u32[]{:S(2)}, u32[]{:S(2)}) collective-permute-start(f32[2,2,8,256]{3,2,1,0:T(8,128)S(1)} %get-tuple-element.42), channel_id=1, source_target_pairs={{0,1},{1,0},{2,3},{3,2},{4,5},{5,4},{6,7},{7,6},{8,9},{9,8},{10,11... | collective-permute-start | bytes 98312 | tf_op jit(solution)/shard_map/ppermute | solution.py:453
  35.4 1.2 %collective-permute-start.11 = (f32[2,8,256]{2,1,0:T(8,128)S(1)}, f32[2,8,256]{2,1,0:T(8,128)S(1)}, u32[]{:S(2)}, u32[]{:S(2)}) collective-permute-start(f32[2,8,256]{2,1,0:T(8,128)S(1)} %slice_bitcast_fusion), channel_id=1, source_target_pairs={{0,2},{2,0},{1,3},{3,1},{4,6},{6,4},{5,7},{7,5},{8,10},{10,8},{9,1... | collective-permute-start | bytes 49160 | tf_op jit(solution)/shard_map/ppermute | solution.py:453

commit v17 on v15

--- a/solution.py
+++ b/solution.py
@@ -242,7 +242,6 @@
         found[...] = found_ref[...]
     else:
         found = refs[11]
-        found[...] = jnp.zeros(found.shape, jnp.float32)
 
     row_table = row_ref[...]
     col_table = col_ref[...]
@@ -352,7 +351,8 @@
                     at = (pair * many + order) * 2 + side
                     one = lags[at * span : (at + 1) * span]
                     one = pltpu.roll(one, span - SHIFT - row_shift, 0)[:WIN]
-                    found[order, pl.ds(pl.multiple_of(index * WIN, WIN), WIN), :] = pltpu.roll(
+                    at = index // (2 * own) * own + (2 * pair + side) % own
+                    found[order, pl.ds(pl.multiple_of(at * WIN, WIN), WIN), :] = pltpu.roll(
                         one, LANES - SHIFT - col_shift, 1
                     )
 
@@ -387,7 +387,7 @@
     kept = -(-(block // 2 + 1) // 8) * 8
     smem = pl.BlockSpec(memory_space=pltpu.SMEM)
     vmem = pl.BlockSpec(memory_space=pltpu.VMEM)
-    blocks = down * across
+    blocks = down * across // 2
     many = 2 * vols * 2 * own
     found = jax.ShapeDtypeStruct((2 * vols, blocks * WIN, LANES), jnp.float32)
     if other:
@@ -429,6 +429,7 @@
     depth = lax.axis_size("z")
     planes = lax.axis_size("plane")
     place = jnp.stack([lax.axis_index(axis) for axis in ("z", "y", "core", "plane")])
+    core = place[2]
     other_codes = exchange(shift_codes, "core", 2, 1)
     other_frames = exchange(frames, "core", 2, 1)
     staged, *bands = stage([frames, *tap_constants(block)], template)
@@ -459,7 +460,9 @@
         averages.append(total * (1.0 / volumes))
         for turn, one in enumerate(given):
             found = found + exchange(one, "plane", planes, turn + 1)
-        correlation += found[0] + exchange(found[1], "core", 2, 1)
+        pair = (found[0], exchange(found[1], "core", 2, 1))
+        pair = [jnp.where(core == at, *pair).reshape(vol_dev, -1, 1, own, WIN * WIN) for at in (0, 1)]
+        correlation += jnp.concatenate(pair, axis=2).reshape(vol_dev, -1, WIN * WIN)
     return (correlation, jnp.stack(averages, axis=1))
 
 

time: 35.6 us -> 35.1 us (0.986)
  local copies, waits for them, and re-layouts: 0.04 us -> 0.72 us
  other arithmetic: 1.5 us -> 0.9 us
    reshape x0 -> x3, local copies, waits for them, and re-layouts: none -> 0.67 us  [the longest x1 0.64 us: on_device(): correlation += jnp.concatenate(pair, axis=2).reshape(vol_dev, -1, WIN * WIN)]
    add x1 -> x0, other arithmetic: 0.62 us -> none  [on_device(): correlation += found[0] + exchange(found[1], 'core', 2, 1)]
where the time goes in v17:
time: 35.1 us; the launch traced here: 35 us
  starting transfers between devices  14.2 us (40%)
  Pallas kernels  13.7 us (39%)
  waiting for transfers between devices  4.62 us (13%)
  other arithmetic  0.9 us (3%)
  between operations  0.82 us (2%)
  local copies, waits for them, and re-layouts  0.72 us (2%)
    ppermute x12, starting transfers between devices, exchange(): return lax.ppermute(value, axes, [(at, at ^ turn) for at in range(size)])  14.2 us
    pallas_call x2, Pallas kernels, lag_windows(): pl.pallas_call(functools.partial(spectrum_kernel, vols, across, block, ow...  5.83 us
    pallas_call x2, Pallas kernels, warp_sums(): pl.pallas_call(functools.partial(warp_kernel, down, across, block, own, o...  5.69 us
    ppermute x12, waiting for transfers between devices, exchange(): return lax.ppermute(value, axes, [(at, at ^ turn) for at in range(size)])  4.62 us
    pallas_call x1, Pallas kernels, stage(): pl.pallas_call(functools.partial(stage_kernel, count), out_shape=[jax.Sha...  2.13 us
    unnamed x1, other arithmetic  0.7 us
  transfers between devices with their start and end apart: 12, of which 4 were waited for; matrix products, arithmetic and copies ran while one was open for 2% of the time, Pallas kernels for 39%

profile of v17, /device:TPU:0, one launch (start us, length us, event | category | flops | bytes accessed | tf_op | source)
XLA Modules:
  0.0 35.0 jit_solution(16638862994193410378)
XLA Ops:
  0.6 0.0 copy-start
  0.7 0.5 %collective-permute-start.1 = (bf16[2,1,512,1024]{3,2,0,1:T(8,128)(2,1)}, bf16[2,1,512,1024]{3,2,0,1:T(8,128)(2,1)S(1)}, u32[]{:S(2)}, u32[]{:S(2)}) collective-permute-start(bf16[2,1,512,1024]{3,2,0,1:T(8,128)(2,1)} %bitcast.36), channel_id=1, source_target_pairs={{0,2},{2,0},{1,3},{3,1},{4,6},{6,4},{5,7},{7,5},{8,10},{10,8},{9,1... | collective-permute-start | bytes 6291464 | tf_op jit(solution)/shard_map/ppermute | solution.py:423
  1.2 2.7 %collective-permute-start.2 = (bf16[2,1,128,128]{3,2,0,1:T(8,128)(2,1)}, bf16[2,1,128,128]{3,2,0,1:T(8,128)(2,1)S(1)}, u32[]{:S(2)}, u32[]{:S(2)}) collective-permute-start(bf16[2,1,128,128]{3,2,0,1:T(8,128)(2,1)} %bitcast.32), channel_id=1, source_target_pairs={{0,8},{8,0},{16,24},{24,16},{1,9},{9,1},{17,25},{25,17},{2,10},{10... | collective-permute-start | bytes 196616 | tf_op jit(solution)/shard_map/ppermute | solution.py:423
  3.8 2.6 %collective-permute-start.3 = (bf16[2,1,128,128]{3,2,0,1:T(8,128)(2,1)}, bf16[2,1,128,128]{3,2,0,1:T(8,128)(2,1)S(1)}, u32[]{:S(2)}, u32[]{:S(2)}) collective-permute-start(bf16[2,1,128,128]{3,2,0,1:T(8,128)(2,1)} %bitcast.33), channel_id=1, source_target_pairs={{0,16},{8,24},{16,0},{24,8},{1,17},{9,25},{17,1},{25,9},{2,18},{10... | collective-permute-start | bytes 196616 | tf_op jit(solution)/shard_map/ppermute | solution.py:423
  6.4 0.1 pad_add_fusion.refs_0_
  6.5 2.1 %stage.1 = (bf16[2,1,512,1024]{3,2,1,0:T(8,128)(2,1)S(1)}, f32[16,176,128]{2,1,0:T(8,128)S(1)}, f32[16,2,32,128]{3,2,1,0:T(8,128)S(1)}) custom-call(bf16[2,1,512,1024]{3,2,1,0:T(8,128)(2,1)} %refs_0_.1, f32[16,176,128]{2,1,0:T(8,128)} %constant.32.clone.refs_1_, f32[16,2,32,128]{3,2,1,0:T(8,128)} %constant.33.clone.refs_2_, bf16[2,1,128,128]{3,2,1,0:T(8,128)(2,1)} %refs_7_.1), custom_call_target="tpu_custom_call" | custom-call | bytes 8126464 | tf_op jit(solution)/shard_map/stage/pallas_call | solution.py:102
  8.7 2.9 %warp.2.refs_7_ = bf16[8,128,128]{2,1,0:T(8,128)(2,1)S(1)} custom-call(s32[4]{0:T(128)S(1)} %pad_add_fusion.refs_0_, s32[2,2,32]{2,1,0:T(2,128)S(1)} %copy-done.5, s32[2,2,32]{2,1,0:T(2,128)S(1)} %collective-permute-done.refs_2_, bf16[2,512,1024]{2,1,0:T(8,128)(2,1)S(1)} %bitcast.28, bf16[2,512,1024]{2,1,0:T(8,128)(2,1)S(1)} %bitcast.24, ...), custom_call_target="tpu_custom_call" | custom-call | flops 2147483648 | bytes 4718592 | tf_op jit(solution)/shard_map/warp/pallas_call | solution.py:219
  11.5 0.0 copy-start.1
  11.6 1.8 %collective-permute-start.6 = (bf16[8,128,128]{2,1,0:T(8,128)(2,1)S(1)}, bf16[8,128,128]{2,1,0:T(8,128)(2,1)S(1)}, u32[]{:S(2)}, u32[]{:S(2)}) collective-permute-start(bf16[8,128,128]{2,1,0:T(8,128)(2,1)S(1)} %warp.2.refs_7_), channel_id=1, source_target_pairs={{0,4},{4,0},{1,5},{5,1},{2,6},{6,2},{3,7},{7,3},{8,12},{12,8},{9,1... | collective-permute-start | bytes 786440 | tf_op jit(solution)/shard_map/ppermute | solution.py:423
  13.4 2.8 %warp.3 = (bf16[2,128,128]{2,1,0:T(8,128)(2,1)S(1)}, bf16[2,128,128]{2,1,0:T(8,128)(2,1)S(1)}, bf16[2,128,128]{2,1,0:T(8,128)(2,1)S(1)}, bf16[2,128,128]{2,1,0:T(8,128)(2,1)S(1)}) custom-call(s32[4]{0:T(128)S(1)} %pad_add_fusion.refs_0_, s32[2,2,32]{2,1,0:T(2,128)S(1)} %copy-done.5, s32[2,2,32]{2,1,0:T(2,128)S(1)} %collective-permute-done.refs_2_, ...), custom_call_target="tpu_custom_call" | custom-call | flops 2147483648 | bytes 4718592 | tf_op jit(solution)/shard_map/warp/pallas_call | solution.py:219
  16.3 0.3 collective-permute-start.5
  16.7 2.8 %lag_windows.2.refs_10_ = f32[4,256,128]{2,1,0:T(8,128)S(1)} custom-call(s32[4]{0:T(128)S(1)} %pad_add_fusion.refs_0_, s32[2,2,32]{2,1,0:T(2,128)S(1)} %copy-done.5, s32[2,2,32]{2,1,0:T(2,128)S(1)} %collective-permute-done.refs_2_, bf16[160,128]{1,0:T(8,128)(2,1)S(1)} %copy-done.3, bf16[256,256]{1,0:T(8,128)(2,1)S(1)} %copy-done.1, ...), custom_call_target="tpu_custom_call" | custom-call | flops 3221225472 | bytes 4718592 | tf_op jit(solution)/shard_map/lag_windows/pallas_call | solution.py:402
  19.5 1.3 %collective-permute-done.6 = bf16[8,128,128]{2,1,0:T(8,128)(2,1)S(1)} collective-permute-done((bf16[8,128,128]{2,1,0:T(8,128)(2,1)S(1)}, bf16[8,128,128]{2,1,0:T(8,128)(2,1)S(1)}, u32[]{:S(2)}, u32[]{:S(2)}) %collective-permute-start.6) | collective-permute-done | bytes 262176 | tf_op jit(solution)/shard_map/ppermute | solution.py:423
  20.7 0.1 add_convert_fusion
  20.8 3.9 %collective-permute-start.7 = (bf16[2,128,128]{2,1,0:T(8,128)(2,1)S(1)}, bf16[2,128,128]{2,1,0:T(8,128)(2,1)S(1)}, u32[]{:S(2)}, u32[]{:S(2)}) collective-permute-start(bf16[2,128,128]{2,1,0:T(8,128)(2,1)S(1)} %get-tuple-element.48), channel_id=1, source_target_pairs={{0,24},{8,16},{16,8},{24,0},{1,25},{9,17},{17,9},{25,1},{2,26},{10... | collective-permute-start | bytes 196616 | tf_op jit(solution)/shard_map/ppermute | solution.py:423
  24.7 0.6 %collective-permute-start.9 = (bf16[2,128,128]{2,1,0:T(8,128)(2,1)S(1)}, bf16[2,128,128]{2,1,0:T(8,128)(2,1)S(1)}, u32[]{:S(2)}, u32[]{:S(2)}) collective-permute-start(bf16[2,128,128]{2,1,0:T(8,128)(2,1)S(1)} %get-tuple-element.46), channel_id=1, source_target_pairs={{0,16},{8,24},{16,0},{24,8},{1,17},{9,25},{17,1},{25,9},{2,18},{10... | collective-permute-start | bytes 196616 | tf_op jit(solution)/shard_map/ppermute | solution.py:423
  25.3 0.7 %collective-permute-done.5.refs_9_ = bf16[8,128,128]{2,1,0:T(8,128)(2,1)S(1)} collective-permute-done((bf16[8,128,128]{2,1,0:T(8,128)(2,1)S(1)}, bf16[8,128,128]{2,1,0:T(8,128)(2,1)S(1)}, u32[]{:S(2)}, u32[]{:S(2)}) %collective-permute-start.5) | collective-permute-done | bytes 262176 | tf_op jit(solution)/shard_map/ppermute | solution.py:423
  26.0 3.0 %lag_windows.3 = (f32[2,2,8,256]{3,2,1,0:T(8,128)S(1)}, f32[2,2,8,256]{3,2,1,0:T(8,128)S(1)}) custom-call(s32[4]{0:T(128)S(1)} %pad_add_fusion.refs_0_, s32[2,2,32]{2,1,0:T(2,128)S(1)} %copy-done.5, s32[2,2,32]{2,1,0:T(2,128)S(1)} %collective-permute-done.refs_2_, bf16[160,128]{1,0:T(8,128)(2,1)S(1)} %copy-done.3, bf16[256,256]{1,0:T(8,128)(2,1)S(1)} %copy-done.1, ...), custom_call_target="tpu_custom_call" | custom-call | flops 805306368 | bytes 4718592 | tf_op jit(solution)/shard_map/lag_windows/pallas_call | solution.py:402
  29.0 1.8 %collective-permute-start.10 = (f32[2,2,8,256]{3,2,1,0:T(8,128)S(1)}, f32[2,2,8,256]{3,2,1,0:T(8,128)S(1)}, u32[]{:S(2)}, u32[]{:S(2)}) collective-permute-start(f32[2,2,8,256]{3,2,1,0:T(8,128)S(1)} %get-tuple-element.40), channel_id=1, source_target_pairs={{0,1},{1,0},{2,3},{3,2},{4,5},{5,4},{6,7},{7,6},{8,9},{9,8},{10,11... | collective-permute-start | bytes 98312 | tf_op jit(solution)/shard_map/ppermute | solution.py:423
  30.8 2.2 %collective-permute-done.10 = f32[2,2,8,256]{3,2,1,0:T(8,128)S(1)} collective-permute-done((f32[2,2,8,256]{3,2,1,0:T(8,128)S(1)}, f32[2,2,8,256]{3,2,1,0:T(8,128)S(1)}, u32[]{:S(2)}, u32[]{:S(2)}) %collective-permute-start.10) | collective-permute-done | bytes 32800 | tf_op jit(solution)/shard_map/ppermute | solution.py:423
  33.0 0.1 collective-permute-start.11
  33.1 0.7 %multiply_bitcast_fusion = f32[2,1,128,128]{3,2,1,0:T(8,128)} fusion(bf16[2,128,128]{2,1,0:T(8,128)(2,1)S(1)} %collective-permute-done.9, bf16[2,128,128]{2,1,0:T(8,128)(2,1)S(1)} %collective-permute-done.8, bf16[2,128,128]{2,1,0:T(8,128)(2,1)S(1)} %collective-permute-done.7, bf16[2,128,128]{2,1,0:T(8,128)(2,1)S(1)} %get-tuple-element.34.refs_10_, ...), kind=kLoop, calls=%fused_computation.1 | loop fusion | flops 327680 | bytes 458752
  33.8 0.5 %collective-permute-done.11 = f32[2,8,256]{2,1,0:T(8,128)S(1)} collective-permute-done((f32[2,8,256]{2,1,0:T(8,128)S(1)}, f32[2,8,256]{2,1,0:T(8,128)S(1)}, u32[]{:S(2)}, u32[]{:S(2)}) %collective-permute-start.11) | collective-permute-done | bytes 16416 | tf_op jit(solution)/shard_map/ppermute | solution.py:423
  34.3 0.6 %reshape.15 = f32[2,16,256]{2,1,0:T(8,128)} reshape(f32[2,4,2,2,256]{4,3,2,1,0:T(2,128)S(1)} %copy.19) | data formatting | bytes 65536 | tf_op jit(solution)/shard_map/reshape | solution.py:465
  (29 shorter events, 0.2 us)
Async XLA Ops:
  0.6 8.0 %copy-start = (bf16[2,1,128,128]{3,2,1,0:T(8,128)(2,1)S(1)}, bf16[2,1,128,128]{3,2,1,0:T(8,128)(2,1)}, u32[]{:S(2)}) copy-start(bf16[2,1,128,128]{3,2,1,0:T(8,128)(2,1)} %refs_7_.1) | copy-start | bytes 196612
  0.6 8.0 %copy-start.5 = (s32[2,2,32]{2,1,0:T(2,128)S(1)}, s32[2,2,32]{2,1,0:T(2,128)}, u32[]{:S(2)}) copy-start(s32[2,2,32]{2,1,0:T(2,128)} %refs_1_.8) | copy-start | bytes 1540
  0.7 8.0 %collective-permute-start.1 = (bf16[2,1,512,1024]{3,2,0,1:T(8,128)(2,1)}, bf16[2,1,512,1024]{3,2,0,1:T(8,128)(2,1)S(1)}, u32[]{:S(2)}, u32[]{:S(2)}) collective-permute-start(bf16[2,1,512,1024]{3,2,0,1:T(8,128)(2,1)} %bitcast.36), channel_id=1, source_target_pairs={{0,2},{2,0},{1,3},{3,1},{4,6},{6,4},{5,7},{7,5},{8,10},{10,8},{9,1... | collective-permute-start | bytes 6291464 | tf_op jit(solution)/shard_map/ppermute | solution.py:423
  1.2 15.1 %collective-permute-start.2 = (bf16[2,1,128,128]{3,2,0,1:T(8,128)(2,1)}, bf16[2,1,128,128]{3,2,0,1:T(8,128)(2,1)S(1)}, u32[]{:S(2)}, u32[]{:S(2)}) collective-permute-start(bf16[2,1,128,128]{3,2,0,1:T(8,128)(2,1)} %bitcast.32), channel_id=1, source_target_pairs={{0,8},{8,0},{16,24},{24,16},{1,9},{9,1},{17,25},{25,17},{2,10},{10... | collective-permute-start | bytes 196616 | tf_op jit(solution)/shard_map/ppermute | solution.py:423
  3.8 12.4 %collective-permute-start.3 = (bf16[2,1,128,128]{3,2,0,1:T(8,128)(2,1)}, bf16[2,1,128,128]{3,2,0,1:T(8,128)(2,1)S(1)}, u32[]{:S(2)}, u32[]{:S(2)}) collective-permute-start(bf16[2,1,128,128]{3,2,0,1:T(8,128)(2,1)} %bitcast.33), channel_id=1, source_target_pairs={{0,16},{8,24},{16,0},{24,8},{1,17},{9,25},{17,1},{25,9},{2,18},{10... | collective-permute-start | bytes 196616 | tf_op jit(solution)/shard_map/ppermute | solution.py:423
  6.4 9.8 %collective-permute-start.4 = (bf16[2,1,128,128]{3,2,0,1:T(8,128)(2,1)}, bf16[2,1,128,128]{3,2,0,1:T(8,128)(2,1)S(1)}, u32[]{:S(2)}, u32[]{:S(2)}) collective-permute-start(bf16[2,1,128,128]{3,2,0,1:T(8,128)(2,1)} %bitcast.34), channel_id=1, source_target_pairs={{0,24},{8,16},{16,8},{24,0},{1,25},{9,17},{17,9},{25,1},{2,26},{10... | collective-permute-start | bytes 196616 | tf_op jit(solution)/shard_map/ppermute | solution.py:423
  6.4 2.2 %collective-permute-start = (s32[2,2,32]{2,1,0:T(2,128)}, s32[2,2,32]{2,1,0:T(2,128)S(1)}, u32[]{:S(2)}, u32[]{:S(2)}) collective-permute-start(s32[2,2,32]{2,1,0:T(2,128)} %refs_1_.8), channel_id=1, source_target_pairs={{0,2},{2,0},{1,3},{3,1},{4,6},{6,4},{5,7},{7,5},{8,10},{10,8},{9,1... | collective-permute-start | bytes 1544 | tf_op jit(solution)/shard_map/ppermute | solution.py:423
  11.5 5.1 %copy-start.1 = (bf16[256,256]{1,0:T(8,128)(2,1)S(1)}, bf16[256,256]{1,0:T(8,128)(2,1)}, u32[]{:S(2)}) copy-start(bf16[256,256]{1,0:T(8,128)(2,1)} %constant.35.clone.refs_4_) | copy-start | bytes 393220
  11.5 5.1 %copy-start.2 = (bf16[256,128]{1,0:T(8,128)(2,1)S(1)}, bf16[256,128]{1,0:T(8,128)(2,1)}, u32[]{:S(2)}) copy-start(bf16[256,128]{1,0:T(8,128)(2,1)} %constant.37.clone.refs_6_) | copy-start | bytes 196612
  11.6 5.1 %copy-start.3 = (bf16[160,128]{1,0:T(8,128)(2,1)S(1)}, bf16[160,128]{1,0:T(8,128)(2,1)}, u32[]{:S(2)}) copy-start(bf16[160,128]{1,0:T(8,128)(2,1)} %constant.34.clone.refs_3_) | copy-start | bytes 122884
  11.6 5.1 %copy-start.4 = (bf16[64,160]{1,0:T(8,128)(2,1)S(1)}, bf16[64,160]{1,0:T(8,128)(2,1)}, u32[]{:S(2)}) copy-start(bf16[64,160]{1,0:T(8,128)(2,1)} %constant.36.clone.refs_5_) | copy-start | bytes 61444
  11.6 9.2 %collective-permute-start.6 = (bf16[8,128,128]{2,1,0:T(8,128)(2,1)S(1)}, bf16[8,128,128]{2,1,0:T(8,128)(2,1)S(1)}, u32[]{:S(2)}, u32[]{:S(2)}) collective-permute-start(bf16[8,128,128]{2,1,0:T(8,128)(2,1)S(1)} %warp.2.refs_7_), channel_id=1, source_target_pairs={{0,4},{4,0},{1,5},{5,1},{2,6},{6,2},{3,7},{7,3},{8,12},{12,8},{9,1... | collective-permute-start | bytes 786440 | tf_op jit(solution)/shard_map/ppermute | solution.py:423
  16.3 9.7 %collective-permute-start.5 = (bf16[8,128,128]{2,1,0:T(8,128)(2,1)S(1)}, bf16[8,128,128]{2,1,0:T(8,128)(2,1)S(1)}, u32[]{:S(2)}, u32[]{:S(2)}) collective-permute-start(bf16[8,128,128]{2,1,0:T(8,128)(2,1)S(1)} %pad_maximum_fusion.refs_9_), channel_id=1, source_target_pairs={{0,4},{4,0},{1,5},{5,1},{2,6},{6,2},{3,7},{7,3},{8,12},{12,8},{9,1... | collective-permute-start | bytes 786440 | tf_op jit(solution)/shard_map/ppermute | solution.py:423
  20.8 10.0 %collective-permute-start.7 = (bf16[2,128,128]{2,1,0:T(8,128)(2,1)S(1)}, bf16[2,128,128]{2,1,0:T(8,128)(2,1)S(1)}, u32[]{:S(2)}, u32[]{:S(2)}) collective-permute-start(bf16[2,128,128]{2,1,0:T(8,128)(2,1)S(1)} %get-tuple-element.48), channel_id=1, source_target_pairs={{0,24},{8,16},{16,8},{24,0},{1,25},{9,17},{17,9},{25,1},{2,26},{10... | collective-permute-start | bytes 196616 | tf_op jit(solution)/shard_map/ppermute | solution.py:423
  24.7 6.1 %collective-permute-start.8 = (bf16[2,128,128]{2,1,0:T(8,128)(2,1)S(1)}, bf16[2,128,128]{2,1,0:T(8,128)(2,1)S(1)}, u32[]{:S(2)}, u32[]{:S(2)}) collective-permute-start(bf16[2,128,128]{2,1,0:T(8,128)(2,1)S(1)} %get-tuple-element.47), channel_id=1, source_target_pairs={{0,8},{8,0},{16,24},{24,16},{1,9},{9,1},{17,25},{25,17},{2,10},{10... | collective-permute-start | bytes 196616 | tf_op jit(solution)/shard_map/ppermute | solution.py:423
  24.7 6.1 %collective-permute-start.9 = (bf16[2,128,128]{2,1,0:T(8,128)(2,1)S(1)}, bf16[2,128,128]{2,1,0:T(8,128)(2,1)S(1)}, u32[]{:S(2)}, u32[]{:S(2)}) collective-permute-start(bf16[2,128,128]{2,1,0:T(8,128)(2,1)S(1)} %get-tuple-element.46), channel_id=1, source_target_pairs={{0,16},{8,24},{16,0},{24,8},{1,17},{9,25},{17,1},{25,9},{2,18},{10... | collective-permute-start | bytes 196616 | tf_op jit(solution)/shard_map/ppermute | solution.py:423
  29.0 4.0 %collective-permute-start.10 = (f32[2,2,8,256]{3,2,1,0:T(8,128)S(1)}, f32[2,2,8,256]{3,2,1,0:T(8,128)S(1)}, u32[]{:S(2)}, u32[]{:S(2)}) collective-permute-start(f32[2,2,8,256]{3,2,1,0:T(8,128)S(1)} %get-tuple-element.40), channel_id=1, source_target_pairs={{0,1},{1,0},{2,3},{3,2},{4,5},{5,4},{6,7},{7,6},{8,9},{9,8},{10,11... | collective-permute-start | bytes 98312 | tf_op jit(solution)/shard_map/ppermute | solution.py:423
  33.0 1.2 %collective-permute-start.11 = (f32[2,8,256]{2,1,0:T(8,128)S(1)}, f32[2,8,256]{2,1,0:T(8,128)S(1)}, u32[]{:S(2)}, u32[]{:S(2)}) collective-permute-start(f32[2,8,256]{2,1,0:T(8,128)S(1)} %slice_bitcast_fusion), channel_id=1, source_target_pairs={{0,2},{2,0},{1,3},{3,1},{4,6},{6,4},{5,7},{7,5},{8,10},{10,8},{9,1... | collective-permute-start | bytes 49160 | tf_op jit(solution)/shard_map/ppermute | solution.py:423

commit v18 on v17

--- a/solution.py
+++ b/solution.py
@@ -84,12 +84,16 @@
     return (place_ref[0] ^ step) * (4 * own) // across
 
 
-def stage_kernel(count, *refs):
+def stage_kernel(count, chunks, *refs):
     sources, targets, sems = refs[:count], refs[count + 1 : 2 * count + 1], refs[-1]
-    copies = [
-        pltpu.make_async_copy(source, target, sems.at[at])
-        for at, (source, target) in enumerate(zip(sources, targets))
-    ]
+    copies = []
+    for source, target in zip(sources, targets):
+        size = source.shape[0] // chunks
+        for at in range(chunks):
+            part = pl.ds(at * size, size)
+            copies.append(
+                pltpu.make_async_copy(source.at[part], target.at[part], sems.at[len(copies)])
+            )
     for copy in copies:
         copy.start()
     for copy in copies:
@@ -97,15 +101,16 @@
 
 
 def stage(arrays, after):
+    chunks = 4
     kept = [pltpu.with_memory_space_constraint(one, pltpu.HBM) for one in arrays]
     count = len(arrays)
     return pl.pallas_call(
-        functools.partial(stage_kernel, count),
+        functools.partial(stage_kernel, count, chunks),
         out_shape=[jax.ShapeDtypeStruct(one.shape, one.dtype) for one in arrays],
         in_specs=[pl.BlockSpec(memory_space=pltpu.HBM)] * count
         + [pl.BlockSpec(memory_space=pl.ANY)],
         out_specs=[pl.BlockSpec(memory_space=pltpu.VMEM)] * count,
-        scratch_shapes=[pltpu.SemaphoreType.DMA((count,))],
+        scratch_shapes=[pltpu.SemaphoreType.DMA((chunks * count,))],
         compiler_params=pltpu.CompilerParams(vmem_limit_bytes=VMEM_LIMIT),
         cost_estimate=pl.CostEstimate(
             flops=0, bytes_accessed=2 * sum(one.nbytes for one in arrays), transcendentals=0
@@ -305,12 +310,11 @@
                         cross[one, kept + row : kept + row + 8, :] = cross_imag
                         cross[one, 2 * kept + row : 2 * kept + row + 8, :] = magnitude
                         if row == 0:
-                            total = jnp.where(top, magnitude, 2.0 * magnitude)
+                            once = jnp.where(top, magnitude, 0.0)
                         elif row == block // 2:
-                            total += magnitude
-                        else:
-                            total += 2.0 * magnitude
-                    sums[one] = jnp.sum(total, axis=0, keepdims=True)
+                            once += magnitude
+                        total += magnitude
+                    sums[one] = jnp.sum(total + total - once, axis=0, keepdims=True)
 
         means = jnp.sum(sums[...], axis=2, keepdims=True) * (1.0 / (block * block)) + 1e-06
         lag_sums = []
@@ -432,7 +436,9 @@
     core = place[2]
     other_codes = exchange(shift_codes, "core", 2, 1)
     other_frames = exchange(frames, "core", 2, 1)
-    staged, *bands = stage([frames, *tap_constants(block)], template)
+    halves = frames.reshape(4, pl_dev * vol_dev * img_rows // 4, img_cols)
+    staged, *bands = stage([halves, *tap_constants(block)], template)
+    staged = staged.reshape(frames.shape)
     turns = [depth - 1, *range(1, depth - 1)]
     fetched = {turn: exchange(template, "z", depth, turn) for turn in turns}
     pieces = [template] + [fetched[turn] for turn in range(1, depth)]

time: 35.1 us -> 35.2 us (level)
  no operation moved by 1% of the time
where the time goes in v18:
time: 35.2 us; the launch traced here: 35 us
  starting transfers between devices  14.3 us (41%)
  Pallas kernels  13.7 us (39%)
  waiting for transfers between devices  4.6 us (13%)
  other arithmetic  0.9 us (3%)
  between operations  0.82 us (2%)
  local copies, waits for them, and re-layouts  0.72 us (2%)
    ppermute x12, starting transfers between devices, exchange(): return lax.ppermute(value, axes, [(at, at ^ turn) for at in range(size)])  14.3 us
    pallas_call x2, Pallas kernels, lag_windows(): pl.pallas_call(functools.partial(spectrum_kernel, vols, across, block, ow...  5.85 us
    pallas_call x2, Pallas kernels, warp_sums(): pl.pallas_call(functools.partial(warp_kernel, down, across, block, own, o...  5.68 us
    ppermute x12, waiting for transfers between devices, exchange(): return lax.ppermute(value, axes, [(at, at ^ turn) for at in range(size)])  4.6 us
    pallas_call x1, Pallas kernels, stage(): pl.pallas_call(functools.partial(stage_kernel, count, chunks), out_shape=...  2.19 us
    unnamed x1, other arithmetic  0.7 us
  transfers between devices with their start and end apart: 12, of which 4 were waited for; matrix products, arithmetic and copies ran while one was open for 2% of the time, Pallas kernels for 39%

profile of v18, /device:TPU:0, one launch (start us, length us, event | category | flops | bytes accessed | tf_op | source)
XLA Modules:
  0.0 35.0 jit_solution(13133990748244414342)
XLA Ops:
  0.6 0.0 copy-start
  0.7 0.5 %collective-permute-start.1 = (bf16[2,1,512,1024]{3,2,0,1:T(8,128)(2,1)}, bf16[2,1,512,1024]{3,2,0,1:T(8,128)(2,1)S(1)}, u32[]{:S(2)}, u32[]{:S(2)}) collective-permute-start(bf16[2,1,512,1024]{3,2,0,1:T(8,128)(2,1)} %bitcast.37), channel_id=1, source_target_pairs={{0,2},{2,0},{1,3},{3,1},{4,6},{6,4},{5,7},{7,5},{8,10},{10,8},{9,1... | collective-permute-start | bytes 6291464 | tf_op jit(solution)/shard_map/ppermute | solution.py:427
  1.2 2.7 %collective-permute-start.2 = (bf16[2,1,128,128]{3,2,0,1:T(8,128)(2,1)}, bf16[2,1,128,128]{3,2,0,1:T(8,128)(2,1)S(1)}, u32[]{:S(2)}, u32[]{:S(2)}) collective-permute-start(bf16[2,1,128,128]{3,2,0,1:T(8,128)(2,1)} %bitcast.33), channel_id=1, source_target_pairs={{0,8},{8,0},{16,24},{24,16},{1,9},{9,1},{17,25},{25,17},{2,10},{10... | collective-permute-start | bytes 196616 | tf_op jit(solution)/shard_map/ppermute | solution.py:427
  3.8 2.6 %collective-permute-start.3 = (bf16[2,1,128,128]{3,2,0,1:T(8,128)(2,1)}, bf16[2,1,128,128]{3,2,0,1:T(8,128)(2,1)S(1)}, u32[]{:S(2)}, u32[]{:S(2)}) collective-permute-start(bf16[2,1,128,128]{3,2,0,1:T(8,128)(2,1)} %bitcast.34), channel_id=1, source_target_pairs={{0,16},{8,24},{16,0},{24,8},{1,17},{9,25},{17,1},{25,9},{2,18},{10... | collective-permute-start | bytes 196616 | tf_op jit(solution)/shard_map/ppermute | solution.py:427
  6.4 0.1 pad_add_fusion.refs_0_
  6.5 2.2 %stage.1 = (bf16[4,256,1024]{2,1,0:T(8,128)(2,1)S(1)}, f32[16,176,128]{2,1,0:T(8,128)S(1)}, f32[16,2,32,128]{3,2,1,0:T(8,128)S(1)}) custom-call(bf16[4,256,1024]{2,1,0:T(8,128)(2,1)} %bitcast.38, f32[16,176,128]{2,1,0:T(8,128)} %constant.32.clone.refs_1_, f32[16,2,32,128]{3,2,1,0:T(8,128)} %constant.33.clone.refs_2_, bf16[2,1,128,128]{3,2,1,0:T(8,128)(2,1)} %refs_7_.1), custom_call_target="tpu_custom_call" | custom-call | bytes 8126464 | tf_op jit(solution)/shard_map/stage/pallas_call | solution.py:107
  8.7 2.8 %warp.2.refs_7_ = bf16[8,128,128]{2,1,0:T(8,128)(2,1)S(1)} custom-call(s32[4]{0:T(128)S(1)} %pad_add_fusion.refs_0_, s32[2,2,32]{2,1,0:T(2,128)S(1)} %copy-done.5, s32[2,2,32]{2,1,0:T(2,128)S(1)} %collective-permute-done.refs_2_, bf16[2,512,1024]{2,1,0:T(8,128)(2,1)S(1)} %bitcast.29, bf16[2,512,1024]{2,1,0:T(8,128)(2,1)S(1)} %bitcast.25, ...), custom_call_target="tpu_custom_call" | custom-call | flops 2147483648 | bytes 4718592 | tf_op jit(solution)/shard_map/warp/pallas_call | solution.py:224
  11.6 0.0 copy-start.1
  11.6 1.8 %collective-permute-start.6 = (bf16[8,128,128]{2,1,0:T(8,128)(2,1)S(1)}, bf16[8,128,128]{2,1,0:T(8,128)(2,1)S(1)}, u32[]{:S(2)}, u32[]{:S(2)}) collective-permute-start(bf16[8,128,128]{2,1,0:T(8,128)(2,1)S(1)} %warp.2.refs_7_), channel_id=1, source_target_pairs={{0,4},{4,0},{1,5},{5,1},{2,6},{6,2},{3,7},{7,3},{8,12},{12,8},{9,1... | collective-permute-start | bytes 786440 | tf_op jit(solution)/shard_map/ppermute | solution.py:427
  13.4 2.8 %warp.3 = (bf16[2,128,128]{2,1,0:T(8,128)(2,1)S(1)}, bf16[2,128,128]{2,1,0:T(8,128)(2,1)S(1)}, bf16[2,128,128]{2,1,0:T(8,128)(2,1)S(1)}, bf16[2,128,128]{2,1,0:T(8,128)(2,1)S(1)}) custom-call(s32[4]{0:T(128)S(1)} %pad_add_fusion.refs_0_, s32[2,2,32]{2,1,0:T(2,128)S(1)} %copy-done.5, s32[2,2,32]{2,1,0:T(2,128)S(1)} %collective-permute-done.refs_2_, ...), custom_call_target="tpu_custom_call" | custom-call | flops 2147483648 | bytes 4718592 | tf_op jit(solution)/shard_map/warp/pallas_call | solution.py:224
  16.4 0.3 collective-permute-start.5
  16.7 2.8 %lag_windows.2.refs_10_ = f32[4,256,128]{2,1,0:T(8,128)S(1)} custom-call(s32[4]{0:T(128)S(1)} %pad_add_fusion.refs_0_, s32[2,2,32]{2,1,0:T(2,128)S(1)} %copy-done.5, s32[2,2,32]{2,1,0:T(2,128)S(1)} %collective-permute-done.refs_2_, bf16[160,128]{1,0:T(8,128)(2,1)S(1)} %copy-done.3, bf16[256,256]{1,0:T(8,128)(2,1)S(1)} %copy-done.1, ...), custom_call_target="tpu_custom_call" | custom-call | flops 3221225472 | bytes 4718592 | tf_op jit(solution)/shard_map/lag_windows/pallas_call | solution.py:406
  19.5 1.3 %collective-permute-done.6 = bf16[8,128,128]{2,1,0:T(8,128)(2,1)S(1)} collective-permute-done((bf16[8,128,128]{2,1,0:T(8,128)(2,1)S(1)}, bf16[8,128,128]{2,1,0:T(8,128)(2,1)S(1)}, u32[]{:S(2)}, u32[]{:S(2)}) %collective-permute-start.6) | collective-permute-done | bytes 262176 | tf_op jit(solution)/shard_map/ppermute | solution.py:427
  20.8 0.1 add_convert_fusion
  20.8 3.9 %collective-permute-start.7 = (bf16[2,128,128]{2,1,0:T(8,128)(2,1)S(1)}, bf16[2,128,128]{2,1,0:T(8,128)(2,1)S(1)}, u32[]{:S(2)}, u32[]{:S(2)}) collective-permute-start(bf16[2,128,128]{2,1,0:T(8,128)(2,1)S(1)} %get-tuple-element.48), channel_id=1, source_target_pairs={{0,24},{8,16},{16,8},{24,0},{1,25},{9,17},{17,9},{25,1},{2,26},{10... | collective-permute-start | bytes 196616 | tf_op jit(solution)/shard_map/ppermute | solution.py:427
  24.7 0.6 %collective-permute-start.9 = (bf16[2,128,128]{2,1,0:T(8,128)(2,1)S(1)}, bf16[2,128,128]{2,1,0:T(8,128)(2,1)S(1)}, u32[]{:S(2)}, u32[]{:S(2)}) collective-permute-start(bf16[2,128,128]{2,1,0:T(8,128)(2,1)S(1)} %get-tuple-element.46), channel_id=1, source_target_pairs={{0,16},{8,24},{16,0},{24,8},{1,17},{9,25},{17,1},{25,9},{2,18},{10... | collective-permute-start | bytes 196616 | tf_op jit(solution)/shard_map/ppermute | solution.py:427
  25.4 0.7 %collective-permute-done.5.refs_9_ = bf16[8,128,128]{2,1,0:T(8,128)(2,1)S(1)} collective-permute-done((bf16[8,128,128]{2,1,0:T(8,128)(2,1)S(1)}, bf16[8,128,128]{2,1,0:T(8,128)(2,1)S(1)}, u32[]{:S(2)}, u32[]{:S(2)}) %collective-permute-start.5) | collective-permute-done | bytes 262176 | tf_op jit(solution)/shard_map/ppermute | solution.py:427
  26.0 3.0 %lag_windows.3 = (f32[2,2,8,256]{3,2,1,0:T(8,128)S(1)}, f32[2,2,8,256]{3,2,1,0:T(8,128)S(1)}) custom-call(s32[4]{0:T(128)S(1)} %pad_add_fusion.refs_0_, s32[2,2,32]{2,1,0:T(2,128)S(1)} %copy-done.5, s32[2,2,32]{2,1,0:T(2,128)S(1)} %collective-permute-done.refs_2_, bf16[160,128]{1,0:T(8,128)(2,1)S(1)} %copy-done.3, bf16[256,256]{1,0:T(8,128)(2,1)S(1)} %copy-done.1, ...), custom_call_target="tpu_custom_call" | custom-call | flops 805306368 | bytes 4718592 | tf_op jit(solution)/shard_map/lag_windows/pallas_call | solution.py:406
  29.1 1.8 %collective-permute-start.10 = (f32[2,2,8,256]{3,2,1,0:T(8,128)S(1)}, f32[2,2,8,256]{3,2,1,0:T(8,128)S(1)}, u32[]{:S(2)}, u32[]{:S(2)}) collective-permute-start(f32[2,2,8,256]{3,2,1,0:T(8,128)S(1)} %get-tuple-element.40), channel_id=1, source_target_pairs={{0,1},{1,0},{2,3},{3,2},{4,5},{5,4},{6,7},{7,6},{8,9},{9,8},{10,11... | collective-permute-start | bytes 98312 | tf_op jit(solution)/shard_map/ppermute | solution.py:427
  30.9 2.2 %collective-permute-done.10 = f32[2,2,8,256]{3,2,1,0:T(8,128)S(1)} collective-permute-done((f32[2,2,8,256]{3,2,1,0:T(8,128)S(1)}, f32[2,2,8,256]{3,2,1,0:T(8,128)S(1)}, u32[]{:S(2)}, u32[]{:S(2)}) %collective-permute-start.10) | collective-permute-done | bytes 32800 | tf_op jit(solution)/shard_map/ppermute | solution.py:427
  33.1 0.1 collective-permute-start.11
  33.2 0.7 %multiply_bitcast_fusion = f32[2,1,128,128]{3,2,1,0:T(8,128)} fusion(bf16[2,128,128]{2,1,0:T(8,128)(2,1)S(1)} %collective-permute-done.9, bf16[2,128,128]{2,1,0:T(8,128)(2,1)S(1)} %collective-permute-done.8, bf16[2,128,128]{2,1,0:T(8,128)(2,1)S(1)} %collective-permute-done.7, bf16[2,128,128]{2,1,0:T(8,128)(2,1)S(1)} %get-tuple-element.34.refs_10_, ...), kind=kLoop, calls=%fused_computation.1 | loop fusion | flops 327680 | bytes 458752
  33.9 0.5 %collective-permute-done.11 = f32[2,8,256]{2,1,0:T(8,128)S(1)} collective-permute-done((f32[2,8,256]{2,1,0:T(8,128)S(1)}, f32[2,8,256]{2,1,0:T(8,128)S(1)}, u32[]{:S(2)}, u32[]{:S(2)}) %collective-permute-start.11) | collective-permute-done | bytes 16416 | tf_op jit(solution)/shard_map/ppermute | solution.py:427
  34.4 0.6 %reshape.19 = f32[2,16,256]{2,1,0:T(8,128)} reshape(f32[2,4,2,2,256]{4,3,2,1,0:T(2,128)S(1)} %copy.19) | data formatting | bytes 65536 | tf_op jit(solution)/shard_map/reshape | solution.py:471
  (29 shorter events, 0.2 us)
Async XLA Ops:
  0.6 8.1 %copy-start = (bf16[2,1,128,128]{3,2,1,0:T(8,128)(2,1)S(1)}, bf16[2,1,128,128]{3,2,1,0:T(8,128)(2,1)}, u32[]{:S(2)}) copy-start(bf16[2,1,128,128]{3,2,1,0:T(8,128)(2,1)} %refs_7_.1) | copy-start | bytes 196612
  0.6 8.1 %copy-start.5 = (s32[2,2,32]{2,1,0:T(2,128)S(1)}, s32[2,2,32]{2,1,0:T(2,128)}, u32[]{:S(2)}) copy-start(s32[2,2,32]{2,1,0:T(2,128)} %refs_1_.8) | copy-start | bytes 1540
  0.7 8.1 %collective-permute-start.1 = (bf16[2,1,512,1024]{3,2,0,1:T(8,128)(2,1)}, bf16[2,1,512,1024]{3,2,0,1:T(8,128)(2,1)S(1)}, u32[]{:S(2)}, u32[]{:S(2)}) collective-permute-start(bf16[2,1,512,1024]{3,2,0,1:T(8,128)(2,1)} %bitcast.37), channel_id=1, source_target_pairs={{0,2},{2,0},{1,3},{3,1},{4,6},{6,4},{5,7},{7,5},{8,10},{10,8},{9,1... | collective-permute-start | bytes 6291464 | tf_op jit(solution)/shard_map/ppermute | solution.py:427
  1.2 15.1 %collective-permute-start.2 = (bf16[2,1,128,128]{3,2,0,1:T(8,128)(2,1)}, bf16[2,1,128,128]{3,2,0,1:T(8,128)(2,1)S(1)}, u32[]{:S(2)}, u32[]{:S(2)}) collective-permute-start(bf16[2,1,128,128]{3,2,0,1:T(8,128)(2,1)} %bitcast.33), channel_id=1, source_target_pairs={{0,8},{8,0},{16,24},{24,16},{1,9},{9,1},{17,25},{25,17},{2,10},{10... | collective-permute-start | bytes 196616 | tf_op jit(solution)/shard_map/ppermute | solution.py:427
  3.8 12.5 %collective-permute-start.3 = (bf16[2,1,128,128]{3,2,0,1:T(8,128)(2,1)}, bf16[2,1,128,128]{3,2,0,1:T(8,128)(2,1)S(1)}, u32[]{:S(2)}, u32[]{:S(2)}) collective-permute-start(bf16[2,1,128,128]{3,2,0,1:T(8,128)(2,1)} %bitcast.34), channel_id=1, source_target_pairs={{0,16},{8,24},{16,0},{24,8},{1,17},{9,25},{17,1},{25,9},{2,18},{10... | collective-permute-start | bytes 196616 | tf_op jit(solution)/shard_map/ppermute | solution.py:427
  6.4 9.9 %collective-permute-start.4 = (bf16[2,1,128,128]{3,2,0,1:T(8,128)(2,1)}, bf16[2,1,128,128]{3,2,0,1:T(8,128)(2,1)S(1)}, u32[]{:S(2)}, u32[]{:S(2)}) collective-permute-start(bf16[2,1,128,128]{3,2,0,1:T(8,128)(2,1)} %bitcast.35), channel_id=1, source_target_pairs={{0,24},{8,16},{16,8},{24,0},{1,25},{9,17},{17,9},{25,1},{2,26},{10... | collective-permute-start | bytes 196616 | tf_op jit(solution)/shard_map/ppermute | solution.py:427
  6.4 2.3 %collective-permute-start = (s32[2,2,32]{2,1,0:T(2,128)}, s32[2,2,32]{2,1,0:T(2,128)S(1)}, u32[]{:S(2)}, u32[]{:S(2)}) collective-permute-start(s32[2,2,32]{2,1,0:T(2,128)} %refs_1_.8), channel_id=1, source_target_pairs={{0,2},{2,0},{1,3},{3,1},{4,6},{6,4},{5,7},{7,5},{8,10},{10,8},{9,1... | collective-permute-start | bytes 1544 | tf_op jit(solution)/shard_map/ppermute | solution.py:427
  11.6 5.1 %copy-start.1 = (bf16[256,256]{1,0:T(8,128)(2,1)S(1)}, bf16[256,256]{1,0:T(8,128)(2,1)}, u32[]{:S(2)}) copy-start(bf16[256,256]{1,0:T(8,128)(2,1)} %constant.35.clone.refs_4_) | copy-start | bytes 393220
  11.6 5.1 %copy-start.2 = (bf16[256,128]{1,0:T(8,128)(2,1)S(1)}, bf16[256,128]{1,0:T(8,128)(2,1)}, u32[]{:S(2)}) copy-start(bf16[256,128]{1,0:T(8,128)(2,1)} %constant.37.clone.refs_6_) | copy-start | bytes 196612
  11.6 5.1 %copy-start.3 = (bf16[160,128]{1,0:T(8,128)(2,1)S(1)}, bf16[160,128]{1,0:T(8,128)(2,1)}, u32[]{:S(2)}) copy-start(bf16[160,128]{1,0:T(8,128)(2,1)} %constant.34.clone.refs_3_) | copy-start | bytes 122884
  11.6 5.1 %copy-start.4 = (bf16[64,160]{1,0:T(8,128)(2,1)S(1)}, bf16[64,160]{1,0:T(8,128)(2,1)}, u32[]{:S(2)}) copy-start(bf16[64,160]{1,0:T(8,128)(2,1)} %constant.36.clone.refs_5_) | copy-start | bytes 61444
  11.6 9.2 %collective-permute-start.6 = (bf16[8,128,128]{2,1,0:T(8,128)(2,1)S(1)}, bf16[8,128,128]{2,1,0:T(8,128)(2,1)S(1)}, u32[]{:S(2)}, u32[]{:S(2)}) collective-permute-start(bf16[8,128,128]{2,1,0:T(8,128)(2,1)S(1)} %warp.2.refs_7_), channel_id=1, source_target_pairs={{0,4},{4,0},{1,5},{5,1},{2,6},{6,2},{3,7},{7,3},{8,12},{12,8},{9,1... | collective-permute-start | bytes 786440 | tf_op jit(solution)/shard_map/ppermute | solution.py:427
  16.4 9.7 %collective-permute-start.5 = (bf16[8,128,128]{2,1,0:T(8,128)(2,1)S(1)}, bf16[8,128,128]{2,1,0:T(8,128)(2,1)S(1)}, u32[]{:S(2)}, u32[]{:S(2)}) collective-permute-start(bf16[8,128,128]{2,1,0:T(8,128)(2,1)S(1)} %pad_maximum_fusion.refs_9_), channel_id=1, source_target_pairs={{0,4},{4,0},{1,5},{5,1},{2,6},{6,2},{3,7},{7,3},{8,12},{12,8},{9,1... | collective-permute-start | bytes 786440 | tf_op jit(solution)/shard_map/ppermute | solution.py:427
  20.8 10.0 %collective-permute-start.7 = (bf16[2,128,128]{2,1,0:T(8,128)(2,1)S(1)}, bf16[2,128,128]{2,1,0:T(8,128)(2,1)S(1)}, u32[]{:S(2)}, u32[]{:S(2)}) collective-permute-start(bf16[2,128,128]{2,1,0:T(8,128)(2,1)S(1)} %get-tuple-element.48), channel_id=1, source_target_pairs={{0,24},{8,16},{16,8},{24,0},{1,25},{9,17},{17,9},{25,1},{2,26},{10... | collective-permute-start | bytes 196616 | tf_op jit(solution)/shard_map/ppermute | solution.py:427
  24.7 6.1 %collective-permute-start.8 = (bf16[2,128,128]{2,1,0:T(8,128)(2,1)S(1)}, bf16[2,128,128]{2,1,0:T(8,128)(2,1)S(1)}, u32[]{:S(2)}, u32[]{:S(2)}) collective-permute-start(bf16[2,128,128]{2,1,0:T(8,128)(2,1)S(1)} %get-tuple-element.47), channel_id=1, source_target_pairs={{0,8},{8,0},{16,24},{24,16},{1,9},{9,1},{17,25},{25,17},{2,10},{10... | collective-permute-start | bytes 196616 | tf_op jit(solution)/shard_map/ppermute | solution.py:427
  24.7 6.1 %collective-permute-start.9 = (bf16[2,128,128]{2,1,0:T(8,128)(2,1)S(1)}, bf16[2,128,128]{2,1,0:T(8,128)(2,1)S(1)}, u32[]{:S(2)}, u32[]{:S(2)}) collective-permute-start(bf16[2,128,128]{2,1,0:T(8,128)(2,1)S(1)} %get-tuple-element.46), channel_id=1, source_target_pairs={{0,16},{8,24},{16,0},{24,8},{1,17},{9,25},{17,1},{25,9},{2,18},{10... | collective-permute-start | bytes 196616 | tf_op jit(solution)/shard_map/ppermute | solution.py:427
  29.1 4.0 %collective-permute-start.10 = (f32[2,2,8,256]{3,2,1,0:T(8,128)S(1)}, f32[2,2,8,256]{3,2,1,0:T(8,128)S(1)}, u32[]{:S(2)}, u32[]{:S(2)}) collective-permute-start(f32[2,2,8,256]{3,2,1,0:T(8,128)S(1)} %get-tuple-element.40), channel_id=1, source_target_pairs={{0,1},{1,0},{2,3},{3,2},{4,5},{5,4},{6,7},{7,6},{8,9},{9,8},{10,11... | collective-permute-start | bytes 98312 | tf_op jit(solution)/shard_map/ppermute | solution.py:427
  33.1 1.2 %collective-permute-start.11 = (f32[2,8,256]{2,1,0:T(8,128)S(1)}, f32[2,8,256]{2,1,0:T(8,128)S(1)}, u32[]{:S(2)}, u32[]{:S(2)}) collective-permute-start(f32[2,8,256]{2,1,0:T(8,128)S(1)} %slice_bitcast_fusion), channel_id=1, source_target_pairs={{0,2},{2,0},{1,3},{3,1},{4,6},{6,4},{5,7},{7,5},{8,10},{10,8},{9,1... | collective-permute-start | bytes 49160 | tf_op jit(solution)/shard_map/ppermute | solution.py:427

commit v19 on v17

--- a/solution.py
+++ b/solution.py
@@ -66,8 +66,8 @@
     spare = np.arange(LANES)[None, :] % (2 * EDGE)
     first = band(spare - 2 * EDGE, outputs) * (spare >= EDGE)
     last = band(spare + EDGE, outputs) * (spare < EDGE)
-    tables = band(inputs, lanes), np.stack([first, last], axis=1)
-    return [jnp.asarray(table, jnp.float32) for table in tables]
+    tables = band(inputs, lanes), np.concatenate([first, last], axis=1)
+    return [jnp.asarray(table, jnp.bfloat16) for table in tables]
 
 
 def step_places(place_ref, step, across, own):
@@ -85,33 +85,46 @@
 
 
 def stage_kernel(count, *refs):
-    sources, targets, sems = refs[:count], refs[count + 1 : 2 * count + 1], refs[-1]
+    sources, targets = refs[:count], refs[count + 1 : 2 * count + 1]
+    held, sems = refs[2 * count + 1 : 3 * count], refs[-1]
     copies = [
         pltpu.make_async_copy(source, target, sems.at[at])
-        for at, (source, target) in enumerate(zip(sources, targets))
+        for at, (source, target) in enumerate(zip(sources, (*held, targets[-1])))
     ]
     for copy in copies:
         copy.start()
-    for copy in copies:
+    for copy, one, target in zip(copies, held, targets):
         copy.wait()
 
-
-def stage(arrays, after):
-    kept = [pltpu.with_memory_space_constraint(one, pltpu.HBM) for one in arrays]
-    count = len(arrays)
+        def widen(at, _):
+            target[at] = one[at].astype(jnp.float32)
+            return 0
+
+        lax.fori_loop(0, one.shape[0], widen, 0)
+    copies[-1].wait()
+
+
+def stage(tables, frames, after):
+    arrays = [
+        pltpu.with_memory_space_constraint(one, pltpu.HBM) for one in (*tables, frames, after)
+    ]
+    count = len(tables) + 1
+    vmem = pl.BlockSpec(memory_space=pltpu.VMEM)
     return pl.pallas_call(
         functools.partial(stage_kernel, count),
-        out_shape=[jax.ShapeDtypeStruct(one.shape, one.dtype) for one in arrays],
+        out_shape=[jax.ShapeDtypeStruct(one.shape, jnp.float32) for one in tables]
+        + [jax.ShapeDtypeStruct(frames.shape, frames.dtype)],
         in_specs=[pl.BlockSpec(memory_space=pltpu.HBM)] * count
         + [pl.BlockSpec(memory_space=pl.ANY)],
-        out_specs=[pl.BlockSpec(memory_space=pltpu.VMEM)] * count,
-        scratch_shapes=[pltpu.SemaphoreType.DMA((count,))],
+        out_specs=[vmem] * count,
+        scratch_shapes=[pltpu.VMEM(one.shape, one.dtype) for one in tables]
+        + [pltpu.SemaphoreType.DMA((count,))],
         compiler_params=pltpu.CompilerParams(vmem_limit_bytes=VMEM_LIMIT),
         cost_estimate=pl.CostEstimate(
-            flops=0, bytes_accessed=2 * sum(one.nbytes for one in arrays), transcendentals=0
+            flops=0, bytes_accessed=2 * frames.nbytes, transcendentals=0
         ),
         name="stage",
-    )(*kept, pltpu.with_memory_space_constraint(after, pltpu.HBM))
+    )(*arrays)
 
 
 def warp_step(place_ref, step, other, code_refs, frame_refs, band_refs, down, across, block, own):
@@ -170,8 +183,8 @@
             rows = cols_ref[back & (SUB - 1), pl.ds(back_start, block), :]
             row_tiles.append(rows.astype(jnp.bfloat16))
             row_start, step_at = SHIFT + (row_code >> 4), row_code & (SUB - 1)
-            first = edges_ref[step_at, 0, pl.ds(row_start, EDGE), :]
-            last = edges_ref[step_at, 1, pl.ds(row_start, EDGE), :]
+            first = edges_ref[step_at, pl.ds(row_start, EDGE), :]
+            last = edges_ref[step_at, pl.ds(2 * EDGE + row_start, EDGE), :]
             if order % per_tile:
                 first = jnp.where(lane == order % per_tile, first, firsts.pop())
                 last = jnp.where(lane == order % per_tile, last, lasts.pop())
@@ -305,12 +318,11 @@
                         cross[one, kept + row : kept + row + 8, :] = cross_imag
                         cross[one, 2 * kept + row : 2 * kept + row + 8, :] = magnitude
                         if row == 0:
-                            total = jnp.where(top, magnitude, 2.0 * magnitude)
+                            once = jnp.where(top, magnitude, 0.0)
                         elif row == block // 2:
-                            total += magnitude
-                        else:
-                            total += 2.0 * magnitude
-                    sums[one] = jnp.sum(total, axis=0, keepdims=True)
+                            once += magnitude
+                        total += magnitude
+                    sums[one] = jnp.sum(total + total - once, axis=0, keepdims=True)
 
         means = jnp.sum(sums[...], axis=2, keepdims=True) * (1.0 / (block * block)) + 1e-06
         lag_sums = []
@@ -374,7 +386,8 @@
                         one = pltpu.roll(one, part * WIN, 1)
                     total = jnp.where(lane == part, one, total)
                 lanes = slice(tile * LANES, (tile + 1) * LANES)
-                out_ref[order // vols, order % vols, :, lanes] = total * (1.0 / block)
+                total = (total * (1.0 / block)).astype(out_ref.dtype)
+                out_ref[order // vols, order % vols, :, lanes] = total
 
 
 def lag_windows(
@@ -392,7 +405,8 @@
     found = jax.ShapeDtypeStruct((2 * vols, blocks * WIN, LANES), jnp.float32)
     if other:
         out = (2, vols, blocks // planes, WIN * WIN)
-        out_shape = [jax.ShapeDtypeStruct(out, jnp.float32)] * planes
+        out_shape = [jax.ShapeDtypeStruct(out, jnp.float32)]
+        out_shape += [jax.ShapeDtypeStruct(out, jnp.bfloat16)] * (planes - 1)
         scratch_shapes = [pltpu.VMEM(found.shape, found.dtype)]
         last = vmem
     else:
@@ -432,7 +446,7 @@
     core = place[2]
     other_codes = exchange(shift_codes, "core", 2, 1)
     other_frames = exchange(frames, "core", 2, 1)
-    staged, *bands = stage([frames, *tap_constants(block)], template)
+    *bands, staged = stage(tap_constants(block), frames, template)
     turns = [depth - 1, *range(1, depth - 1)]
     fetched = {turn: exchange(template, "z", depth, turn) for turn in turns}
     pieces = [template] + [fetched[turn] for turn in range(1, depth)]
@@ -459,8 +473,9 @@
         total = sum((one.astype(jnp.float32) for one in moved), sums[0])
         averages.append(total * (1.0 / volumes))
         for turn, one in enumerate(given):
-            found = found + exchange(one, "plane", planes, turn + 1)
-        pair = (found[0], exchange(found[1], "core", 2, 1))
+            found = found + exchange(one, "plane", planes, turn + 1).astype(jnp.float32)
+        given = exchange(found[1].astype(jnp.bfloat16), "core", 2, 1)
+        pair = (found[0], given.astype(jnp.float32))
         pair = [jnp.where(core == at, *pair).reshape(vol_dev, -1, 1, own, WIN * WIN) for at in (0, 1)]
         correlation += jnp.concatenate(pair, axis=2).reshape(vol_dev, -1, WIN * WIN)
     return (correlation, jnp.stack(averages, axis=1))

time: 35.1 us -> 34.7 us (0.989)
  transfers between devices with their start and end apart: 12 -> 12, of which waited for: 4 -> 4; matrix products, arithmetic and copies ran while one was open for 2% -> 3% of each run, Pallas kernels for 39% -> 39%
where the time goes in v19:
time: 34.7 us; the launch traced here: 34.6 us
  starting transfers between devices  14.3 us (41%)
  Pallas kernels  13.4 us (39%)
  waiting for transfers between devices  4.43 us (13%)
  other arithmetic  0.9 us (3%)
  between operations  0.81 us (2%)
  local copies, waits for them, and re-layouts  0.72 us (2%)
    ppermute x12, starting transfers between devices, exchange(): return lax.ppermute(value, axes, [(at, at ^ turn) for at in range(size)])  14.3 us
    pallas_call x2, Pallas kernels, lag_windows(): pl.pallas_call(functools.partial(spectrum_kernel, vols, across, block, ow...  5.85 us
    pallas_call x2, Pallas kernels, warp_sums(): pl.pallas_call(functools.partial(warp_kernel, down, across, block, own, o...  5.67 us
    ppermute x12, waiting for transfers between devices, exchange(): return lax.ppermute(value, axes, [(at, at ^ turn) for at in range(size)])  4.43 us
    pallas_call x1, Pallas kernels, stage(): pl.pallas_call(functools.partial(stage_kernel, count), out_shape=[jax.Sha...  1.93 us
    unnamed x1, other arithmetic  0.7 us
  transfers between devices with their start and end apart: 12, of which 4 were waited for; matrix products, arithmetic and copies ran while one was open for 3% of the time, Pallas kernels for 39%

profile of v19, /device:TPU:0, one launch (start us, length us, event | category | flops | bytes accessed | tf_op | source)
XLA Modules:
  0.0 34.6 jit_solution(15095810895786774272)
XLA Ops:
  0.6 0.0 copy-start
  0.7 0.5 %collective-permute-start.1 = (bf16[2,1,512,1024]{3,2,0,1:T(8,128)(2,1)}, bf16[2,1,512,1024]{3,2,0,1:T(8,128)(2,1)S(1)}, u32[]{:S(2)}, u32[]{:S(2)}) collective-permute-start(bf16[2,1,512,1024]{3,2,0,1:T(8,128)(2,1)} %bitcast.36), channel_id=1, source_target_pairs={{0,2},{2,0},{1,3},{3,1},{4,6},{6,4},{5,7},{7,5},{8,10},{10,8},{9,1... | collective-permute-start | bytes 6291464 | tf_op jit(solution)/shard_map/ppermute | solution.py:437
  1.2 2.7 %collective-permute-start.2 = (bf16[2,1,128,128]{3,2,0,1:T(8,128)(2,1)}, bf16[2,1,128,128]{3,2,0,1:T(8,128)(2,1)S(1)}, u32[]{:S(2)}, u32[]{:S(2)}) collective-permute-start(bf16[2,1,128,128]{3,2,0,1:T(8,128)(2,1)} %bitcast.32), channel_id=1, source_target_pairs={{0,8},{8,0},{16,24},{24,16},{1,9},{9,1},{17,25},{25,17},{2,10},{10... | collective-permute-start | bytes 196616 | tf_op jit(solution)/shard_map/ppermute | solution.py:437
  3.8 2.6 %collective-permute-start.3 = (bf16[2,1,128,128]{3,2,0,1:T(8,128)(2,1)}, bf16[2,1,128,128]{3,2,0,1:T(8,128)(2,1)S(1)}, u32[]{:S(2)}, u32[]{:S(2)}) collective-permute-start(bf16[2,1,128,128]{3,2,0,1:T(8,128)(2,1)} %bitcast.33), channel_id=1, source_target_pairs={{0,16},{8,24},{16,0},{24,8},{1,17},{9,25},{17,1},{25,9},{2,18},{10... | collective-permute-start | bytes 196616 | tf_op jit(solution)/shard_map/ppermute | solution.py:437
  6.4 0.1 pad_add_fusion.refs_0_
  6.5 1.9 %stage.1 = (f32[16,176,128]{2,1,0:T(8,128)S(1)}, f32[16,64,128]{2,1,0:T(8,128)S(1)}, bf16[2,1,512,1024]{3,2,1,0:T(8,128)(2,1)S(1)}) custom-call(bf16[16,176,128]{2,1,0:T(8,128)(2,1)} %constant.32.clone.refs_0_, bf16[16,64,128]{2,1,0:T(8,128)(2,1)} %constant.33.clone.refs_1_, bf16[2,1,512,1024]{3,2,1,0:T(8,128)(2,1)} %refs_2_.1, bf16[2,1,128,128]{3,2,1,0:T(8,128)(2,1)} %refs_7_.1), custom_call_target="tpu_custom_call" | custom-call | bytes 4194304 | tf_op jit(solution)/shard_map/stage/pallas_call | solution.py:113
  8.5 2.8 %warp.2.refs_7_ = bf16[8,128,128]{2,1,0:T(8,128)(2,1)S(1)} custom-call(s32[4]{0:T(128)S(1)} %pad_add_fusion.refs_0_, s32[2,2,32]{2,1,0:T(2,128)S(1)} %copy-done.5, s32[2,2,32]{2,1,0:T(2,128)S(1)} %collective-permute-done.refs_2_, bf16[2,512,1024]{2,1,0:T(8,128)(2,1)S(1)} %bitcast.28, bf16[2,512,1024]{2,1,0:T(8,128)(2,1)S(1)} %bitcast.24, ...), custom_call_target="tpu_custom_call" | custom-call | flops 2147483648 | bytes 4718592 | tf_op jit(solution)/shard_map/warp/pallas_call | solution.py:232
  11.3 0.0 copy-start.2
  11.4 1.8 %collective-permute-start.6 = (bf16[8,128,128]{2,1,0:T(8,128)(2,1)S(1)}, bf16[8,128,128]{2,1,0:T(8,128)(2,1)S(1)}, u32[]{:S(2)}, u32[]{:S(2)}) collective-permute-start(bf16[8,128,128]{2,1,0:T(8,128)(2,1)S(1)} %warp.2.refs_7_), channel_id=1, source_target_pairs={{0,4},{4,0},{1,5},{5,1},{2,6},{6,2},{3,7},{7,3},{8,12},{12,8},{9,1... | collective-permute-start | bytes 786440 | tf_op jit(solution)/shard_map/ppermute | solution.py:437
  13.2 2.8 %warp.3 = (bf16[2,128,128]{2,1,0:T(8,128)(2,1)S(1)}, bf16[2,128,128]{2,1,0:T(8,128)(2,1)S(1)}, bf16[2,128,128]{2,1,0:T(8,128)(2,1)S(1)}, bf16[2,128,128]{2,1,0:T(8,128)(2,1)S(1)}) custom-call(s32[4]{0:T(128)S(1)} %pad_add_fusion.refs_0_, s32[2,2,32]{2,1,0:T(2,128)S(1)} %copy-done.5, s32[2,2,32]{2,1,0:T(2,128)S(1)} %collective-permute-done.refs_2_, ...), custom_call_target="tpu_custom_call" | custom-call | flops 2147483648 | bytes 4718592 | tf_op jit(solution)/shard_map/warp/pallas_call | solution.py:232
  16.1 0.4 %collective-permute-start.5 = (bf16[8,128,128]{2,1,0:T(8,128)(2,1)S(1)}, bf16[8,128,128]{2,1,0:T(8,128)(2,1)S(1)}, u32[]{:S(2)}, u32[]{:S(2)}) collective-permute-start(bf16[8,128,128]{2,1,0:T(8,128)(2,1)S(1)} %pad_maximum_fusion.refs_9_), channel_id=1, source_target_pairs={{0,4},{4,0},{1,5},{5,1},{2,6},{6,2},{3,7},{7,3},{8,12},{12,8},{9,1... | collective-permute-start | bytes 786440 | tf_op jit(solution)/shard_map/ppermute | solution.py:437
  16.4 2.8 %lag_windows.2.refs_10_ = f32[4,256,128]{2,1,0:T(8,128)S(1)} custom-call(s32[4]{0:T(128)S(1)} %pad_add_fusion.refs_0_, s32[2,2,32]{2,1,0:T(2,128)S(1)} %copy-done.5, s32[2,2,32]{2,1,0:T(2,128)S(1)} %collective-permute-done.refs_2_, bf16[160,128]{1,0:T(8,128)(2,1)S(1)} %copy-done.3, bf16[256,256]{1,0:T(8,128)(2,1)S(1)} %copy-done.1, ...), custom_call_target="tpu_custom_call" | custom-call | flops 3221225472 | bytes 4718592 | tf_op jit(solution)/shard_map/lag_windows/pallas_call | solution.py:416
  19.3 1.3 %collective-permute-done.6 = bf16[8,128,128]{2,1,0:T(8,128)(2,1)S(1)} collective-permute-done((bf16[8,128,128]{2,1,0:T(8,128)(2,1)S(1)}, bf16[8,128,128]{2,1,0:T(8,128)(2,1)S(1)}, u32[]{:S(2)}, u32[]{:S(2)}) %collective-permute-start.6) | collective-permute-done | bytes 262176 | tf_op jit(solution)/shard_map/ppermute | solution.py:437
  20.5 0.1 add_convert_fusion
  20.6 3.9 %collective-permute-start.7 = (bf16[2,128,128]{2,1,0:T(8,128)(2,1)S(1)}, bf16[2,128,128]{2,1,0:T(8,128)(2,1)S(1)}, u32[]{:S(2)}, u32[]{:S(2)}) collective-permute-start(bf16[2,128,128]{2,1,0:T(8,128)(2,1)S(1)} %get-tuple-element.48), channel_id=1, source_target_pairs={{0,24},{8,16},{16,8},{24,0},{1,25},{9,17},{17,9},{25,1},{2,26},{10... | collective-permute-start | bytes 196616 | tf_op jit(solution)/shard_map/ppermute | solution.py:437
  24.5 0.6 %collective-permute-start.9 = (bf16[2,128,128]{2,1,0:T(8,128)(2,1)S(1)}, bf16[2,128,128]{2,1,0:T(8,128)(2,1)S(1)}, u32[]{:S(2)}, u32[]{:S(2)}) collective-permute-start(bf16[2,128,128]{2,1,0:T(8,128)(2,1)S(1)} %get-tuple-element.46), channel_id=1, source_target_pairs={{0,16},{8,24},{16,0},{24,8},{1,17},{9,25},{17,1},{25,9},{2,18},{10... | collective-permute-start | bytes 196616 | tf_op jit(solution)/shard_map/ppermute | solution.py:437
  25.1 0.7 %collective-permute-done.5.refs_9_ = bf16[8,128,128]{2,1,0:T(8,128)(2,1)S(1)} collective-permute-done((bf16[8,128,128]{2,1,0:T(8,128)(2,1)S(1)}, bf16[8,128,128]{2,1,0:T(8,128)(2,1)S(1)}, u32[]{:S(2)}, u32[]{:S(2)}) %collective-permute-start.5) | collective-permute-done | bytes 262176 | tf_op jit(solution)/shard_map/ppermute | solution.py:437
  25.8 3.0 %lag_windows.3 = (f32[2,2,8,256]{3,2,1,0:T(8,128)S(1)}, bf16[2,2,8,256]{3,2,1,0:T(8,128)(2,1)S(1)}) custom-call(s32[4]{0:T(128)S(1)} %pad_add_fusion.refs_0_, s32[2,2,32]{2,1,0:T(2,128)S(1)} %copy-done.5, s32[2,2,32]{2,1,0:T(2,128)S(1)} %collective-permute-done.refs_2_, bf16[160,128]{1,0:T(8,128)(2,1)S(1)} %copy-done.3, bf16[256,256]{1,0:T(8,128)(2,1)S(1)} %copy-done.1, ...), custom_call_target="tpu_custom_call" | custom-call | flops 805306368 | bytes 4718592 | tf_op jit(solution)/shard_map/lag_windows/pallas_call | solution.py:416
  28.8 1.7 %collective-permute-start.10 = (bf16[2,2,8,256]{3,2,1,0:T(8,128)(2,1)S(1)}, bf16[2,2,8,256]{3,2,1,0:T(8,128)(2,1)S(1)}, u32[]{:S(2)}, u32[]{:S(2)}) collective-permute-start(bf16[2,2,8,256]{3,2,1,0:T(8,128)(2,1)S(1)} %get-tuple-element.40), channel_id=1, source_target_pairs={{0,1},{1,0},{2,3},{3,2},{4,5},{5,4},{6,7},{7,6},{8,9},{9,8},{10,11... | collective-permute-start | bytes 49160 | tf_op jit(solution)/shard_map/ppermute | solution.py:437
  30.6 2.0 %collective-permute-done.10 = bf16[2,2,8,256]{3,2,1,0:T(8,128)(2,1)S(1)} collective-permute-done((bf16[2,2,8,256]{3,2,1,0:T(8,128)(2,1)S(1)}, bf16[2,2,8,256]{3,2,1,0:T(8,128)(2,1)S(1)}, u32[]{:S(2)}, u32[]{:S(2)}) %collective-permute-start.10) | collective-permute-done | bytes 16416 | tf_op jit(solution)/shard_map/ppermute | solution.py:437
  32.6 0.1 collective-permute-start.11
  32.7 0.7 %multiply_bitcast_fusion = f32[2,1,128,128]{3,2,1,0:T(8,128)} fusion(bf16[2,128,128]{2,1,0:T(8,128)(2,1)S(1)} %collective-permute-done.9, bf16[2,128,128]{2,1,0:T(8,128)(2,1)S(1)} %collective-permute-done.8, bf16[2,128,128]{2,1,0:T(8,128)(2,1)S(1)} %collective-permute-done.7, bf16[2,128,128]{2,1,0:T(8,128)(2,1)S(1)} %get-tuple-element.34.refs_10_, ...), kind=kLoop, calls=%fused_computation.1 | loop fusion | flops 327680 | bytes 458752
  33.4 0.5 %collective-permute-done.11 = bf16[2,8,256]{2,1,0:T(8,128)(2,1)S(1)} collective-permute-done((bf16[2,8,256]{2,1,0:T(8,128)(2,1)S(1)}, bf16[2,8,256]{2,1,0:T(8,128)(2,1)S(1)}, u32[]{:S(2)}, u32[]{:S(2)}) %collective-permute-start.11) | collective-permute-done | bytes 8224 | tf_op jit(solution)/shard_map/ppermute | solution.py:437
  34.0 0.6 %reshape.16 = f32[2,16,256]{2,1,0:T(8,128)} reshape(f32[2,4,2,2,256]{4,3,2,1,0:T(2,128)S(1)} %copy.19) | data formatting | bytes 65536 | tf_op jit(solution)/shard_map/reshape | solution.py:480
  (29 shorter events, 0.2 us)
Async XLA Ops:
  0.6 7.8 %copy-start = (bf16[2,1,128,128]{3,2,1,0:T(8,128)(2,1)S(1)}, bf16[2,1,128,128]{3,2,1,0:T(8,128)(2,1)}, u32[]{:S(2)}) copy-start(bf16[2,1,128,128]{3,2,1,0:T(8,128)(2,1)} %refs_7_.1) | copy-start | bytes 196612
  0.6 7.8 %copy-start.5 = (s32[2,2,32]{2,1,0:T(2,128)S(1)}, s32[2,2,32]{2,1,0:T(2,128)}, u32[]{:S(2)}) copy-start(s32[2,2,32]{2,1,0:T(2,128)} %refs_1_.8) | copy-start | bytes 1540
  0.7 7.8 %collective-permute-start.1 = (bf16[2,1,512,1024]{3,2,0,1:T(8,128)(2,1)}, bf16[2,1,512,1024]{3,2,0,1:T(8,128)(2,1)S(1)}, u32[]{:S(2)}, u32[]{:S(2)}) collective-permute-start(bf16[2,1,512,1024]{3,2,0,1:T(8,128)(2,1)} %bitcast.36), channel_id=1, source_target_pairs={{0,2},{2,0},{1,3},{3,1},{4,6},{6,4},{5,7},{7,5},{8,10},{10,8},{9,1... | collective-permute-start | bytes 6291464 | tf_op jit(solution)/shard_map/ppermute | solution.py:437
  1.2 14.8 %collective-permute-start.2 = (bf16[2,1,128,128]{3,2,0,1:T(8,128)(2,1)}, bf16[2,1,128,128]{3,2,0,1:T(8,128)(2,1)S(1)}, u32[]{:S(2)}, u32[]{:S(2)}) collective-permute-start(bf16[2,1,128,128]{3,2,0,1:T(8,128)(2,1)} %bitcast.32), channel_id=1, source_target_pairs={{0,8},{8,0},{16,24},{24,16},{1,9},{9,1},{17,25},{25,17},{2,10},{10... | collective-permute-start | bytes 196616 | tf_op jit(solution)/shard_map/ppermute | solution.py:437
  3.8 12.2 %collective-permute-start.3 = (bf16[2,1,128,128]{3,2,0,1:T(8,128)(2,1)}, bf16[2,1,128,128]{3,2,0,1:T(8,128)(2,1)S(1)}, u32[]{:S(2)}, u32[]{:S(2)}) collective-permute-start(bf16[2,1,128,128]{3,2,0,1:T(8,128)(2,1)} %bitcast.33), channel_id=1, source_target_pairs={{0,16},{8,24},{16,0},{24,8},{1,17},{9,25},{17,1},{25,9},{2,18},{10... | collective-permute-start | bytes 196616 | tf_op jit(solution)/shard_map/ppermute | solution.py:437
  6.4 9.6 %collective-permute-start.4 = (bf16[2,1,128,128]{3,2,0,1:T(8,128)(2,1)}, bf16[2,1,128,128]{3,2,0,1:T(8,128)(2,1)S(1)}, u32[]{:S(2)}, u32[]{:S(2)}) collective-permute-start(bf16[2,1,128,128]{3,2,0,1:T(8,128)(2,1)} %bitcast.34), channel_id=1, source_target_pairs={{0,24},{8,16},{16,8},{24,0},{1,25},{9,17},{17,9},{25,1},{2,26},{10... | collective-permute-start | bytes 196616 | tf_op jit(solution)/shard_map/ppermute | solution.py:437
  6.4 2.0 %collective-permute-start = (s32[2,2,32]{2,1,0:T(2,128)}, s32[2,2,32]{2,1,0:T(2,128)S(1)}, u32[]{:S(2)}, u32[]{:S(2)}) collective-permute-start(s32[2,2,32]{2,1,0:T(2,128)} %refs_1_.8), channel_id=1, source_target_pairs={{0,2},{2,0},{1,3},{3,1},{4,6},{6,4},{5,7},{7,5},{8,10},{10,8},{9,1... | collective-permute-start | bytes 1544 | tf_op jit(solution)/shard_map/ppermute | solution.py:437
  11.3 5.1 %copy-start.1 = (bf16[256,256]{1,0:T(8,128)(2,1)S(1)}, bf16[256,256]{1,0:T(8,128)(2,1)}, u32[]{:S(2)}) copy-start(bf16[256,256]{1,0:T(8,128)(2,1)} %constant.35.clone.refs_4_) | copy-start | bytes 393220
  11.3 5.1 %copy-start.2 = (bf16[256,128]{1,0:T(8,128)(2,1)S(1)}, bf16[256,128]{1,0:T(8,128)(2,1)}, u32[]{:S(2)}) copy-start(bf16[256,128]{1,0:T(8,128)(2,1)} %constant.37.clone.refs_6_) | copy-start | bytes 196612
  11.3 5.1 %copy-start.3 = (bf16[160,128]{1,0:T(8,128)(2,1)S(1)}, bf16[160,128]{1,0:T(8,128)(2,1)}, u32[]{:S(2)}) copy-start(bf16[160,128]{1,0:T(8,128)(2,1)} %constant.34.clone.refs_3_) | copy-start | bytes 122884
  11.4 5.1 %copy-start.4 = (bf16[64,160]{1,0:T(8,128)(2,1)S(1)}, bf16[64,160]{1,0:T(8,128)(2,1)}, u32[]{:S(2)}) copy-start(bf16[64,160]{1,0:T(8,128)(2,1)} %constant.36.clone.refs_5_) | copy-start | bytes 61444
  11.4 9.2 %collective-permute-start.6 = (bf16[8,128,128]{2,1,0:T(8,128)(2,1)S(1)}, bf16[8,128,128]{2,1,0:T(8,128)(2,1)S(1)}, u32[]{:S(2)}, u32[]{:S(2)}) collective-permute-start(bf16[8,128,128]{2,1,0:T(8,128)(2,1)S(1)} %warp.2.refs_7_), channel_id=1, source_target_pairs={{0,4},{4,0},{1,5},{5,1},{2,6},{6,2},{3,7},{7,3},{8,12},{12,8},{9,1... | collective-permute-start | bytes 786440 | tf_op jit(solution)/shard_map/ppermute | solution.py:437
  16.1 9.7 %collective-permute-start.5 = (bf16[8,128,128]{2,1,0:T(8,128)(2,1)S(1)}, bf16[8,128,128]{2,1,0:T(8,128)(2,1)S(1)}, u32[]{:S(2)}, u32[]{:S(2)}) collective-permute-start(bf16[8,128,128]{2,1,0:T(8,128)(2,1)S(1)} %pad_maximum_fusion.refs_9_), channel_id=1, source_target_pairs={{0,4},{4,0},{1,5},{5,1},{2,6},{6,2},{3,7},{7,3},{8,12},{12,8},{9,1... | collective-permute-start | bytes 786440 | tf_op jit(solution)/shard_map/ppermute | solution.py:437
  20.6 10.0 %collective-permute-start.7 = (bf16[2,128,128]{2,1,0:T(8,128)(2,1)S(1)}, bf16[2,128,128]{2,1,0:T(8,128)(2,1)S(1)}, u32[]{:S(2)}, u32[]{:S(2)}) collective-permute-start(bf16[2,128,128]{2,1,0:T(8,128)(2,1)S(1)} %get-tuple-element.48), channel_id=1, source_target_pairs={{0,24},{8,16},{16,8},{24,0},{1,25},{9,17},{17,9},{25,1},{2,26},{10... | collective-permute-start | bytes 196616 | tf_op jit(solution)/shard_map/ppermute | solution.py:437
  24.5 6.1 %collective-permute-start.8 = (bf16[2,128,128]{2,1,0:T(8,128)(2,1)S(1)}, bf16[2,128,128]{2,1,0:T(8,128)(2,1)S(1)}, u32[]{:S(2)}, u32[]{:S(2)}) collective-permute-start(bf16[2,128,128]{2,1,0:T(8,128)(2,1)S(1)} %get-tuple-element.47), channel_id=1, source_target_pairs={{0,8},{8,0},{16,24},{24,16},{1,9},{9,1},{17,25},{25,17},{2,10},{10... | collective-permute-start | bytes 196616 | tf_op jit(solution)/shard_map/ppermute | solution.py:437
  24.5 6.1 %collective-permute-start.9 = (bf16[2,128,128]{2,1,0:T(8,128)(2,1)S(1)}, bf16[2,128,128]{2,1,0:T(8,128)(2,1)S(1)}, u32[]{:S(2)}, u32[]{:S(2)}) collective-permute-start(bf16[2,128,128]{2,1,0:T(8,128)(2,1)S(1)} %get-tuple-element.46), channel_id=1, source_target_pairs={{0,16},{8,24},{16,0},{24,8},{1,17},{9,25},{17,1},{25,9},{2,18},{10... | collective-permute-start | bytes 196616 | tf_op jit(solution)/shard_map/ppermute | solution.py:437
  28.8 3.8 %collective-permute-start.10 = (bf16[2,2,8,256]{3,2,1,0:T(8,128)(2,1)S(1)}, bf16[2,2,8,256]{3,2,1,0:T(8,128)(2,1)S(1)}, u32[]{:S(2)}, u32[]{:S(2)}) collective-permute-start(bf16[2,2,8,256]{3,2,1,0:T(8,128)(2,1)S(1)} %get-tuple-element.40), channel_id=1, source_target_pairs={{0,1},{1,0},{2,3},{3,2},{4,5},{5,4},{6,7},{7,6},{8,9},{9,8},{10,11... | collective-permute-start | bytes 49160 | tf_op jit(solution)/shard_map/ppermute | solution.py:437
  32.6 1.2 %collective-permute-start.11 = (bf16[2,8,256]{2,1,0:T(8,128)(2,1)S(1)}, bf16[2,8,256]{2,1,0:T(8,128)(2,1)S(1)}, u32[]{:S(2)}, u32[]{:S(2)}) collective-permute-start(bf16[2,8,256]{2,1,0:T(8,128)(2,1)S(1)} %fusion), channel_id=1, source_target_pairs={{0,2},{2,0},{1,3},{3,1},{4,6},{6,4},{5,7},{7,5},{8,10},{10,8},{9,1... | collective-permute-start | bytes 24584 | tf_op jit(solution)/shard_map/ppermute | solution.py:437

commit v20 on v19

--- a/solution.py
+++ b/solution.py
@@ -425,7 +425,7 @@
         ],
         compiler_params=pltpu.CompilerParams(vmem_limit_bytes=VMEM_LIMIT),
         cost_estimate=pl.CostEstimate(
-            flops=2 * 3 * rows * cols * block * (2 if other else 8),
+            flops=2 * 3 * rows * cols * block * (2 if other else 2),
             bytes_accessed=vols * rows * cols * 4 + rows * cols,
             transcendentals=0,
         ),
@@ -448,7 +448,10 @@
     other_frames = exchange(frames, "core", 2, 1)
     *bands, staged = stage(tap_constants(block), frames, template)
     turns = [depth - 1, *range(1, depth - 1)]
-    fetched = {turn: exchange(template, "z", depth, turn) for turn in turns}
+    later, other_codes = lax.optimization_barrier((template, other_codes))
+    fetched = {
+        turn: exchange(later if turn == depth - 1 else template, "z", depth, turn) for turn in turns
+    }
     pieces = [template] + [fetched[turn] for turn in range(1, depth)]
     averages, correlation = [], 0.0
     volumes = vol_dev * depth * 4

time: 34.7 us -> 35.8 us (1.032)
  starting transfers between devices: 14.3 us -> 15.7 us
  waiting for transfers between devices: 4.43 us -> 4.06 us
    ppermute x12, starting transfers between devices: 14.3 us -> 15.7 us  [exchange(): return lax.ppermute(value, axes, [(at, at ^ turn) for at in range(size)])]
    ppermute x12, waiting for transfers between devices: 4.43 us -> 4.06 us  [exchange(): return lax.ppermute(value, axes, [(at, at ^ turn) for at in range(size)])]
  transfers between devices with their start and end apart: 12 -> 12, of which waited for: 4 -> 3; matrix products, arithmetic and copies ran while one was open for 3% -> 2% of each run, Pallas kernels for 39% -> 38%
where the time goes in v20:
time: 35.8 us; the launch traced here: 35.6 us
  starting transfers between devices  15.7 us (44%)
  Pallas kernels  13.5 us (38%)
  waiting for transfers between devices  4.06 us (11%)
  other arithmetic  0.9 us (3%)
  between operations  0.79 us (2%)
  local copies, waits for them, and re-layouts  0.72 us (2%)
    ppermute x12, starting transfers between devices, exchange(): return lax.ppermute(value, axes, [(at, at ^ turn) for at in range(size)])  15.7 us
    pallas_call x2, Pallas kernels, lag_windows(): pl.pallas_call(functools.partial(spectrum_kernel, vols, across, block, ow...  5.85 us
    pallas_call x2, Pallas kernels, warp_sums(): pl.pallas_call(functools.partial(warp_kernel, down, across, block, own, o...  5.67 us
    ppermute x12, waiting for transfers between devices, exchange(): return lax.ppermute(value, axes, [(at, at ^ turn) for at in range(size)])  4.06 us
    pallas_call x1, Pallas kernels, stage(): pl.pallas_call(functools.partial(stage_kernel, count), out_shape=[jax.Sha...  1.93 us
  transfers between devices with their start and end apart: 12, of which 3 were waited for; matrix products, arithmetic and copies ran while one was open for 2% of the time, Pallas kernels for 38%

profile of v20, /device:TPU:0, one launch (start us, length us, event | category | flops | bytes accessed | tf_op | source)
XLA Modules:
  0.0 35.6 jit_solution(6710356678049319510)
XLA Ops:
  0.7 0.5 %collective-permute-start.1 = (bf16[2,1,512,1024]{3,2,0,1:T(8,128)(2,1)}, bf16[2,1,512,1024]{3,2,0,1:T(8,128)(2,1)S(1)}, u32[]{:S(2)}, u32[]{:S(2)}) collective-permute-start(bf16[2,1,512,1024]{3,2,0,1:T(8,128)(2,1)} %bitcast.37), channel_id=1, source_target_pairs={{0,2},{2,0},{1,3},{3,1},{4,6},{6,4},{5,7},{7,5},{8,10},{10,8},{9,1... | collective-permute-start | bytes 6291464 | tf_op jit(solution)/shard_map/ppermute | solution.py:437
  1.2 2.7 %collective-permute-start.2 = (bf16[2,1,128,128]{3,2,0,1:T(8,128)(2,1)}, bf16[2,1,128,128]{3,2,0,1:T(8,128)(2,1)S(1)}, u32[]{:S(2)}, u32[]{:S(2)}) collective-permute-start(bf16[2,1,128,128]{3,2,0,1:T(8,128)(2,1)} %bitcast.33), channel_id=1, source_target_pairs={{0,8},{8,0},{16,24},{24,16},{1,9},{9,1},{17,25},{25,17},{2,10},{10... | collective-permute-start | bytes 196616 | tf_op jit(solution)/shard_map/ppermute | solution.py:437
  3.8 2.6 %collective-permute-start.3 = (bf16[2,1,128,128]{3,2,0,1:T(8,128)(2,1)}, bf16[2,1,128,128]{3,2,0,1:T(8,128)(2,1)S(1)}, u32[]{:S(2)}, u32[]{:S(2)}) collective-permute-start(bf16[2,1,128,128]{3,2,0,1:T(8,128)(2,1)} %bitcast.34), channel_id=1, source_target_pairs={{0,16},{8,24},{16,0},{24,8},{1,17},{9,25},{17,1},{25,9},{2,18},{10... | collective-permute-start | bytes 196616 | tf_op jit(solution)/shard_map/ppermute | solution.py:437
  6.4 0.1 pad_add_fusion.refs_0_
  6.5 1.9 %stage.1 = (f32[16,176,128]{2,1,0:T(8,128)S(1)}, f32[16,64,128]{2,1,0:T(8,128)S(1)}, bf16[2,1,512,1024]{3,2,1,0:T(8,128)(2,1)S(1)}) custom-call(bf16[16,176,128]{2,1,0:T(8,128)(2,1)} %constant.32.clone.refs_0_, bf16[16,64,128]{2,1,0:T(8,128)(2,1)} %constant.33.clone.refs_1_, bf16[2,1,512,1024]{3,2,1,0:T(8,128)(2,1)} %refs_2_.1, bf16[2,1,128,128]{3,2,1,0:T(8,128)(2,1)} %refs_7_.1), custom_call_target="tpu_custom_call" | custom-call | bytes 4194304 | tf_op jit(solution)/shard_map/stage/pallas_call | solution.py:113
  8.4 1.7 %collective-permute-start.4 = (bf16[2,1,128,128]{3,2,0,1:T(8,128)(2,1)S(1)}, bf16[2,1,128,128]{3,2,0,1:T(8,128)(2,1)S(1)}, u32[]{:S(2)}, u32[]{:S(2)}) collective-permute-start(bf16[2,1,128,128]{3,2,0,1:T(8,128)(2,1)S(1)} %bitcast.35), channel_id=1, source_target_pairs={{0,24},{8,16},{16,8},{24,0},{1,25},{9,17},{17,9},{25,1},{2,26},{10... | collective-permute-start | bytes 196616 | tf_op jit(solution)/shard_map/ppermute | solution.py:437
  10.1 2.8 %warp.2.refs_7_ = bf16[8,128,128]{2,1,0:T(8,128)(2,1)S(1)} custom-call(s32[4]{0:T(128)S(1)} %pad_add_fusion.refs_0_, s32[2,2,32]{2,1,0:T(2,128)S(1)} %copy-done.5, s32[2,2,32]{2,1,0:T(2,128)S(1)} %collective-permute-done.refs_2_, bf16[2,512,1024]{2,1,0:T(8,128)(2,1)S(1)} %bitcast.29, bf16[2,512,1024]{2,1,0:T(8,128)(2,1)S(1)} %bitcast.25, ...), custom_call_target="tpu_custom_call" | custom-call | flops 2147483648 | bytes 4718592 | tf_op jit(solution)/shard_map/warp/pallas_call | solution.py:232
  13.0 0.0 copy-start.1
  13.0 0.0 copy-start.3
  13.0 1.6 %collective-permute-start.6 = (bf16[8,128,128]{2,1,0:T(8,128)(2,1)S(1)}, bf16[8,128,128]{2,1,0:T(8,128)(2,1)S(1)}, u32[]{:S(2)}, u32[]{:S(2)}) collective-permute-start(bf16[8,128,128]{2,1,0:T(8,128)(2,1)S(1)} %warp.2.refs_7_), channel_id=1, source_target_pairs={{0,4},{4,0},{1,5},{5,1},{2,6},{6,2},{3,7},{7,3},{8,12},{12,8},{9,1... | collective-permute-start | bytes 786440 | tf_op jit(solution)/shard_map/ppermute | solution.py:437
  14.6 2.8 %warp.3 = (bf16[2,128,128]{2,1,0:T(8,128)(2,1)S(1)}, bf16[2,128,128]{2,1,0:T(8,128)(2,1)S(1)}, bf16[2,128,128]{2,1,0:T(8,128)(2,1)S(1)}, bf16[2,128,128]{2,1,0:T(8,128)(2,1)S(1)}) custom-call(s32[4]{0:T(128)S(1)} %pad_add_fusion.refs_0_, s32[2,2,32]{2,1,0:T(2,128)S(1)} %copy-done.5, s32[2,2,32]{2,1,0:T(2,128)S(1)} %collective-permute-done.refs_2_, ...), custom_call_target="tpu_custom_call" | custom-call | flops 2147483648 | bytes 4718592 | tf_op jit(solution)/shard_map/warp/pallas_call | solution.py:232
  17.5 0.6 %collective-permute-start.5 = (bf16[8,128,128]{2,1,0:T(8,128)(2,1)S(1)}, bf16[8,128,128]{2,1,0:T(8,128)(2,1)S(1)}, u32[]{:S(2)}, u32[]{:S(2)}) collective-permute-start(bf16[8,128,128]{2,1,0:T(8,128)(2,1)S(1)} %pad_maximum_fusion.refs_9_), channel_id=1, source_target_pairs={{0,4},{4,0},{1,5},{5,1},{2,6},{6,2},{3,7},{7,3},{8,12},{12,8},{9,1... | collective-permute-start | bytes 786440 | tf_op jit(solution)/shard_map/ppermute | solution.py:437
  18.1 2.8 %lag_windows.2.refs_10_ = f32[4,256,128]{2,1,0:T(8,128)S(1)} custom-call(s32[4]{0:T(128)S(1)} %pad_add_fusion.refs_0_, s32[2,2,32]{2,1,0:T(2,128)S(1)} %copy-done.5, s32[2,2,32]{2,1,0:T(2,128)S(1)} %collective-permute-done.refs_2_, bf16[160,128]{1,0:T(8,128)(2,1)S(1)} %copy-done.3, bf16[256,256]{1,0:T(8,128)(2,1)S(1)} %copy-done, ...), custom_call_target="tpu_custom_call" | custom-call | flops 805306368 | bytes 4718592 | tf_op jit(solution)/shard_map/lag_windows/pallas_call | solution.py:416
  20.9 1.3 %collective-permute-done.6 = bf16[8,128,128]{2,1,0:T(8,128)(2,1)S(1)} collective-permute-done((bf16[8,128,128]{2,1,0:T(8,128)(2,1)S(1)}, bf16[8,128,128]{2,1,0:T(8,128)(2,1)S(1)}, u32[]{:S(2)}, u32[]{:S(2)}) %collective-permute-start.6) | collective-permute-done | bytes 262176 | tf_op jit(solution)/shard_map/ppermute | solution.py:437
  22.3 0.1 add_convert_fusion
  22.3 2.2 %collective-permute-start.7 = (bf16[2,128,128]{2,1,0:T(8,128)(2,1)S(1)}, bf16[2,128,128]{2,1,0:T(8,128)(2,1)S(1)}, u32[]{:S(2)}, u32[]{:S(2)}) collective-permute-start(bf16[2,128,128]{2,1,0:T(8,128)(2,1)S(1)} %get-tuple-element.52), channel_id=1, source_target_pairs={{0,24},{8,16},{16,8},{24,0},{1,25},{9,17},{17,9},{25,1},{2,26},{10... | collective-permute-start | bytes 196616 | tf_op jit(solution)/shard_map/ppermute | solution.py:437
  24.6 2.2 %collective-permute-start.9 = (bf16[2,128,128]{2,1,0:T(8,128)(2,1)S(1)}, bf16[2,128,128]{2,1,0:T(8,128)(2,1)S(1)}, u32[]{:S(2)}, u32[]{:S(2)}) collective-permute-start(bf16[2,128,128]{2,1,0:T(8,128)(2,1)S(1)} %get-tuple-element.50), channel_id=1, source_target_pairs={{0,16},{8,24},{16,0},{24,8},{1,17},{9,25},{17,1},{25,9},{2,18},{10... | collective-permute-start | bytes 196616 | tf_op jit(solution)/shard_map/ppermute | solution.py:437
  26.8 3.0 %lag_windows.3 = (f32[2,2,8,256]{3,2,1,0:T(8,128)S(1)}, bf16[2,2,8,256]{3,2,1,0:T(8,128)(2,1)S(1)}) custom-call(s32[4]{0:T(128)S(1)} %pad_add_fusion.refs_0_, s32[2,2,32]{2,1,0:T(2,128)S(1)} %copy-done.5, s32[2,2,32]{2,1,0:T(2,128)S(1)} %collective-permute-done.refs_2_, bf16[160,128]{1,0:T(8,128)(2,1)S(1)} %copy-done.3, bf16[256,256]{1,0:T(8,128)(2,1)S(1)} %copy-done, ...), custom_call_target="tpu_custom_call" | custom-call | flops 805306368 | bytes 4718592 | tf_op jit(solution)/shard_map/lag_windows/pallas_call | solution.py:416
  29.8 1.6 %collective-permute-start.10 = (bf16[2,2,8,256]{3,2,1,0:T(8,128)(2,1)S(1)}, bf16[2,2,8,256]{3,2,1,0:T(8,128)(2,1)S(1)}, u32[]{:S(2)}, u32[]{:S(2)}) collective-permute-start(bf16[2,2,8,256]{3,2,1,0:T(8,128)(2,1)S(1)} %get-tuple-element.44), channel_id=1, source_target_pairs={{0,1},{1,0},{2,3},{3,2},{4,5},{5,4},{6,7},{7,6},{8,9},{9,8},{10,11... | collective-permute-start | bytes 49160 | tf_op jit(solution)/shard_map/ppermute | solution.py:437
  31.4 2.2 %collective-permute-done.10 = bf16[2,2,8,256]{3,2,1,0:T(8,128)(2,1)S(1)} collective-permute-done((bf16[2,2,8,256]{3,2,1,0:T(8,128)(2,1)S(1)}, bf16[2,2,8,256]{3,2,1,0:T(8,128)(2,1)S(1)}, u32[]{:S(2)}, u32[]{:S(2)}) %collective-permute-start.10) | collective-permute-done | bytes 16416 | tf_op jit(solution)/shard_map/ppermute | solution.py:437
  33.7 0.1 collective-permute-start.11
  33.7 0.7 %multiply_bitcast_fusion = f32[2,1,128,128]{3,2,1,0:T(8,128)} fusion(bf16[2,128,128]{2,1,0:T(8,128)(2,1)S(1)} %collective-permute-done.9, bf16[2,128,128]{2,1,0:T(8,128)(2,1)S(1)} %collective-permute-done.8, bf16[2,128,128]{2,1,0:T(8,128)(2,1)S(1)} %collective-permute-done.7, bf16[2,128,128]{2,1,0:T(8,128)(2,1)S(1)} %get-tuple-element.38.refs_10_, ...), kind=kLoop, calls=%fused_computation.1 | loop fusion | flops 327680 | bytes 458752
  34.4 0.5 %collective-permute-done.11 = bf16[2,8,256]{2,1,0:T(8,128)(2,1)S(1)} collective-permute-done((bf16[2,8,256]{2,1,0:T(8,128)(2,1)S(1)}, bf16[2,8,256]{2,1,0:T(8,128)(2,1)S(1)}, u32[]{:S(2)}, u32[]{:S(2)}) %collective-permute-start.11) | collective-permute-done | bytes 8224 | tf_op jit(solution)/shard_map/ppermute | solution.py:437
  35.0 0.6 %reshape.16 = f32[2,16,256]{2,1,0:T(8,128)} reshape(f32[2,4,2,2,256]{4,3,2,1,0:T(2,128)S(1)} %copy.19) | data formatting | bytes 65536 | tf_op jit(solution)/shard_map/reshape | solution.py:483
  (29 shorter events, 0.2 us)
Async XLA Ops:
  0.6 7.8 %copy-start.2 = (bf16[2,1,128,128]{3,2,1,0:T(8,128)(2,1)S(1)}, bf16[2,1,128,128]{3,2,1,0:T(8,128)(2,1)}, u32[]{:S(2)}) copy-start(bf16[2,1,128,128]{3,2,1,0:T(8,128)(2,1)} %refs_7_.1) | copy-start | bytes 196612
  0.6 9.5 %copy-start.5 = (s32[2,2,32]{2,1,0:T(2,128)S(1)}, s32[2,2,32]{2,1,0:T(2,128)}, u32[]{:S(2)}) copy-start(s32[2,2,32]{2,1,0:T(2,128)} %refs_1_.8) | copy-start | bytes 1540
  0.7 9.5 %collective-permute-start.1 = (bf16[2,1,512,1024]{3,2,0,1:T(8,128)(2,1)}, bf16[2,1,512,1024]{3,2,0,1:T(8,128)(2,1)S(1)}, u32[]{:S(2)}, u32[]{:S(2)}) collective-permute-start(bf16[2,1,512,1024]{3,2,0,1:T(8,128)(2,1)} %bitcast.37), channel_id=1, source_target_pairs={{0,2},{2,0},{1,3},{3,1},{4,6},{6,4},{5,7},{7,5},{8,10},{10,8},{9,1... | collective-permute-start | bytes 6291464 | tf_op jit(solution)/shard_map/ppermute | solution.py:437
  1.2 16.3 %collective-permute-start.2 = (bf16[2,1,128,128]{3,2,0,1:T(8,128)(2,1)}, bf16[2,1,128,128]{3,2,0,1:T(8,128)(2,1)S(1)}, u32[]{:S(2)}, u32[]{:S(2)}) collective-permute-start(bf16[2,1,128,128]{3,2,0,1:T(8,128)(2,1)} %bitcast.33), channel_id=1, source_target_pairs={{0,8},{8,0},{16,24},{24,16},{1,9},{9,1},{17,25},{25,17},{2,10},{10... | collective-permute-start | bytes 196616 | tf_op jit(solution)/shard_map/ppermute | solution.py:437
  3.8 13.6 %collective-permute-start.3 = (bf16[2,1,128,128]{3,2,0,1:T(8,128)(2,1)}, bf16[2,1,128,128]{3,2,0,1:T(8,128)(2,1)S(1)}, u32[]{:S(2)}, u32[]{:S(2)}) collective-permute-start(bf16[2,1,128,128]{3,2,0,1:T(8,128)(2,1)} %bitcast.34), channel_id=1, source_target_pairs={{0,16},{8,24},{16,0},{24,8},{1,17},{9,25},{17,1},{25,9},{2,18},{10... | collective-permute-start | bytes 196616 | tf_op jit(solution)/shard_map/ppermute | solution.py:437
  6.4 2.0 %collective-permute-start = (s32[2,2,32]{2,1,0:T(2,128)}, s32[2,2,32]{2,1,0:T(2,128)S(1)}, u32[]{:S(2)}, u32[]{:S(2)}) collective-permute-start(s32[2,2,32]{2,1,0:T(2,128)} %refs_1_.8), channel_id=1, source_target_pairs={{0,2},{2,0},{1,3},{3,1},{4,6},{6,4},{5,7},{7,5},{8,10},{10,8},{9,1... | collective-permute-start | bytes 1544 | tf_op jit(solution)/shard_map/ppermute | solution.py:437
  8.4 9.0 %collective-permute-start.4 = (bf16[2,1,128,128]{3,2,0,1:T(8,128)(2,1)S(1)}, bf16[2,1,128,128]{3,2,0,1:T(8,128)(2,1)S(1)}, u32[]{:S(2)}, u32[]{:S(2)}) collective-permute-start(bf16[2,1,128,128]{3,2,0,1:T(8,128)(2,1)S(1)} %bitcast.35), channel_id=1, source_target_pairs={{0,24},{8,16},{16,8},{24,0},{1,25},{9,17},{17,9},{25,1},{2,26},{10... | collective-permute-start | bytes 196616 | tf_op jit(solution)/shard_map/ppermute | solution.py:437
  13.0 5.1 %copy-start = (bf16[256,256]{1,0:T(8,128)(2,1)S(1)}, bf16[256,256]{1,0:T(8,128)(2,1)}, u32[]{:S(2)}) copy-start(bf16[256,256]{1,0:T(8,128)(2,1)} %constant.35.clone.refs_4_) | copy-start | bytes 393220
  13.0 5.1 %copy-start.1 = (bf16[256,128]{1,0:T(8,128)(2,1)S(1)}, bf16[256,128]{1,0:T(8,128)(2,1)}, u32[]{:S(2)}) copy-start(bf16[256,128]{1,0:T(8,128)(2,1)} %constant.37.clone.refs_6_) | copy-start | bytes 196612
  13.0 5.1 %copy-start.3 = (bf16[160,128]{1,0:T(8,128)(2,1)S(1)}, bf16[160,128]{1,0:T(8,128)(2,1)}, u32[]{:S(2)}) copy-start(bf16[160,128]{1,0:T(8,128)(2,1)} %constant.34.clone.refs_3_) | copy-start | bytes 122884
  13.0 5.1 %copy-start.4 = (bf16[64,160]{1,0:T(8,128)(2,1)S(1)}, bf16[64,160]{1,0:T(8,128)(2,1)}, u32[]{:S(2)}) copy-start(bf16[64,160]{1,0:T(8,128)(2,1)} %constant.36.clone.refs_5_) | copy-start | bytes 61444
  13.0 9.3 %collective-permute-start.6 = (bf16[8,128,128]{2,1,0:T(8,128)(2,1)S(1)}, bf16[8,128,128]{2,1,0:T(8,128)(2,1)S(1)}, u32[]{:S(2)}, u32[]{:S(2)}) collective-permute-start(bf16[8,128,128]{2,1,0:T(8,128)(2,1)S(1)} %warp.2.refs_7_), channel_id=1, source_target_pairs={{0,4},{4,0},{1,5},{5,1},{2,6},{6,2},{3,7},{7,3},{8,12},{12,8},{9,1... | collective-permute-start | bytes 786440 | tf_op jit(solution)/shard_map/ppermute | solution.py:437
  17.5 9.3 %collective-permute-start.5 = (bf16[8,128,128]{2,1,0:T(8,128)(2,1)S(1)}, bf16[8,128,128]{2,1,0:T(8,128)(2,1)S(1)}, u32[]{:S(2)}, u32[]{:S(2)}) collective-permute-start(bf16[8,128,128]{2,1,0:T(8,128)(2,1)S(1)} %pad_maximum_fusion.refs_9_), channel_id=1, source_target_pairs={{0,4},{4,0},{1,5},{5,1},{2,6},{6,2},{3,7},{7,3},{8,12},{12,8},{9,1... | collective-permute-start | bytes 786440 | tf_op jit(solution)/shard_map/ppermute | solution.py:437
  22.3 9.1 %collective-permute-start.7 = (bf16[2,128,128]{2,1,0:T(8,128)(2,1)S(1)}, bf16[2,128,128]{2,1,0:T(8,128)(2,1)S(1)}, u32[]{:S(2)}, u32[]{:S(2)}) collective-permute-start(bf16[2,128,128]{2,1,0:T(8,128)(2,1)S(1)} %get-tuple-element.52), channel_id=1, source_target_pairs={{0,24},{8,16},{16,8},{24,0},{1,25},{9,17},{17,9},{25,1},{2,26},{10... | collective-permute-start | bytes 196616 | tf_op jit(solution)/shard_map/ppermute | solution.py:437
  24.6 6.8 %collective-permute-start.8 = (bf16[2,128,128]{2,1,0:T(8,128)(2,1)S(1)}, bf16[2,128,128]{2,1,0:T(8,128)(2,1)S(1)}, u32[]{:S(2)}, u32[]{:S(2)}) collective-permute-start(bf16[2,128,128]{2,1,0:T(8,128)(2,1)S(1)} %get-tuple-element.51), channel_id=1, source_target_pairs={{0,8},{8,0},{16,24},{24,16},{1,9},{9,1},{17,25},{25,17},{2,10},{10... | collective-permute-start | bytes 196616 | tf_op jit(solution)/shard_map/ppermute | solution.py:437
  24.6 6.8 %collective-permute-start.9 = (bf16[2,128,128]{2,1,0:T(8,128)(2,1)S(1)}, bf16[2,128,128]{2,1,0:T(8,128)(2,1)S(1)}, u32[]{:S(2)}, u32[]{:S(2)}) collective-permute-start(bf16[2,128,128]{2,1,0:T(8,128)(2,1)S(1)} %get-tuple-element.50), channel_id=1, source_target_pairs={{0,16},{8,24},{16,0},{24,8},{1,17},{9,25},{17,1},{25,9},{2,18},{10... | collective-permute-start | bytes 196616 | tf_op jit(solution)/shard_map/ppermute | solution.py:437
  29.8 3.8 %collective-permute-start.10 = (bf16[2,2,8,256]{3,2,1,0:T(8,128)(2,1)S(1)}, bf16[2,2,8,256]{3,2,1,0:T(8,128)(2,1)S(1)}, u32[]{:S(2)}, u32[]{:S(2)}) collective-permute-start(bf16[2,2,8,256]{3,2,1,0:T(8,128)(2,1)S(1)} %get-tuple-element.44), channel_id=1, source_target_pairs={{0,1},{1,0},{2,3},{3,2},{4,5},{5,4},{6,7},{7,6},{8,9},{9,8},{10,11... | collective-permute-start | bytes 49160 | tf_op jit(solution)/shard_map/ppermute | solution.py:437
  33.7 1.2 %collective-permute-start.11 = (bf16[2,8,256]{2,1,0:T(8,128)(2,1)S(1)}, bf16[2,8,256]{2,1,0:T(8,128)(2,1)S(1)}, u32[]{:S(2)}, u32[]{:S(2)}) collective-permute-start(bf16[2,8,256]{2,1,0:T(8,128)(2,1)S(1)} %fusion), channel_id=1, source_target_pairs={{0,2},{2,0},{1,3},{3,1},{4,6},{6,4},{5,7},{7,5},{8,10},{10,8},{9,1... | collective-permute-start | bytes 24584 | tf_op jit(solution)/shard_map/ppermute | solution.py:437

commit v21 on v19

--- a/solution.py
+++ b/solution.py
@@ -250,11 +250,13 @@
     place_ref, codes_ref, other_codes_ref, row_ref, col_ref, lag_ref, span_ref = refs[:7]
     frames_ref, other_frames_ref, template_ref = refs[7:10]
     all_cross, all_sums = refs[-2:]
+    ready = []
     if other:
-        found_ref, out_refs, found = refs[10], refs[11:-3], refs[-3]
+        found_ref, spectra_ref, out_refs, found = refs[10], refs[11], refs[12:-3], refs[-3]
         found[...] = found_ref[...]
+        ready.append(spectra_ref)
     else:
-        found = refs[11]
+        found, spectra_ref = refs[11:13]
 
     row_table = row_ref[...]
     col_table = col_ref[...]
@@ -269,35 +271,47 @@
     local = 2 * own
     no_rows = jnp.zeros((half - kept, LANES), jnp.float32)
 
-    for half_step in range(depth // 2):
-        cross, sums = all_cross.at[half_step], all_sums.at[half_step]
+    def find_places(half_step, row):
         places = []
         for step in (2 * half_step, 2 * half_step + 1):
             band = step_band(place_ref, step, across, own)
             band_rows = pl.ds(pl.multiple_of(band * block, block), block)
-            chosen = step_places(place_ref, step, across, own)[other * own : (other + 1) * own]
+            chosen = step_places(place_ref, step, across, own)[row * own : (row + 1) * own]
             for one, (index, at) in enumerate(chosen):
                 lanes = pl.ds(pl.multiple_of(at * block, block), block)
                 places.append((index, band_rows, lanes, step * own + one))
-
+        return places
+
+    def frame_sources(pair_places):
+        return [
+            [frames[v, rows, lanes] for _, rows, lanes, _ in pair_places]
+            for _, frames, v in volumes
+        ]
+
+    def transform(sources):
+        parts = []
+        for source in sources:
+            rows = jnp.dot(
+                row_table, jnp.concatenate(source, axis=1), preferred_element_type=jnp.float32
+            ).astype(jnp.bfloat16)
+            for side in range(2):
+                lanes = slice(side * block, (side + 1) * block)
+                parts.append(jnp.concatenate([rows[:half, lanes], rows[half:, lanes]], axis=1))
+        return jnp.dot(
+            jnp.concatenate(parts, axis=0), col_table, preferred_element_type=jnp.float32
+        )
+
+    for half_step in range(depth // 2):
+        cross, sums = all_cross.at[half_step], all_sums.at[half_step]
+        places = find_places(half_step, other)
         for pair in range(local // 2):
             pair_places = places[2 * pair : 2 * pair + 2]
             sources = [[template_ref[at] for _, _, _, at in pair_places]]
-            for _, frames, v in volumes:
-                sources.append([frames[v, rows, lanes] for _, rows, lanes, _ in pair_places])
-            parts = []
-            for source in sources:
-                rows = jnp.dot(
-                    row_table,
-                    jnp.concatenate(source, axis=1),
-                    preferred_element_type=jnp.float32,
-                ).astype(jnp.bfloat16)
-                for side in range(2):
-                    lanes = slice(side * block, (side + 1) * block)
-                    parts.append(jnp.concatenate([rows[:half, lanes], rows[half:, lanes]], axis=1))
-            spectra = jnp.dot(
-                jnp.concatenate(parts, axis=0), col_table, preferred_element_type=jnp.float32
-            )
+            sources += frame_sources(pair_places)
+            if ready and half_step == 0:
+                spectra = jnp.concatenate([transform(sources[:1]), ready[0][pair]], axis=0)
+            else:
+                spectra = transform(sources)
             temp = spectra[: 2 * half].astype(jnp.bfloat16).astype(jnp.float32)
             for order in range(many):
                 for side in range(2):
@@ -369,6 +383,9 @@
                     )
 
     if not other:
+        places = find_places(0, 1)
+        for pair in range(local // 2):
+            spectra_ref[pair] = transform(frame_sources(places[2 * pair : 2 * pair + 2]))
         return
 
     share = found.shape[1] // WIN // planes
@@ -408,15 +425,17 @@
         out_shape = [jax.ShapeDtypeStruct(out, jnp.float32)]
         out_shape += [jax.ShapeDtypeStruct(out, jnp.bfloat16)] * (planes - 1)
         scratch_shapes = [pltpu.VMEM(found.shape, found.dtype)]
-        last = vmem
+        last = [vmem, vmem]
     else:
-        out_shape = [found]
+        half = tables[0].shape[0] // 2
+        spectra = (own, 2 * vols * 2 * half, 2 * block)
+        out_shape = [found, jax.ShapeDtypeStruct(spectra, jnp.float32)]
         scratch_shapes = []
-        last = pl.BlockSpec(memory_space=pl.ANY)
+        last = [pl.BlockSpec(memory_space=pl.ANY)]
     return pl.pallas_call(
         functools.partial(spectrum_kernel, vols, across, block, own, planes, depth, other),
         out_shape=out_shape,
-        in_specs=[smem] * 3 + [vmem] * (len(tables) + 3) + [last],
+        in_specs=[smem] * 3 + [vmem] * (len(tables) + 3) + last,
         out_specs=[vmem] * len(out_shape),
         scratch_shapes=scratch_shapes
         + [
@@ -430,7 +449,7 @@
             transcendentals=0,
         ),
         name="lag_windows",
-    )(place, codes, other_codes, *tables, frames, other_frames, template, more)
+    )(place, codes, other_codes, *tables, frames, other_frames, template, *more)
 
 
 def exchange(value, axes, size, turn):
@@ -467,7 +486,7 @@
         ]
         moved = [exchange(sums[turn].astype(jnp.bfloat16), "z", depth, turn) for turn in turns]
         sizes = (planes, depth, own)
-        (part,) = lag_windows(*work, near, near_sums[0], 0, *sizes)
+        part = lag_windows(*work, near, near_sums[:1], 0, *sizes)
         found, *given = lag_windows(*work, far, part, 1, *sizes)
         found, moved = lax.optimization_barrier((found, moved))
         total = sum((one.astype(jnp.float32) for one in moved), sums[0])

time: 34.7 us -> 34.5 us (level)
  waiting for transfers between devices: 4.43 us -> 3.98 us
    ppermute x12, waiting for transfers between devices: 4.43 us -> 3.98 us  [exchange(): return lax.ppermute(value, axes, [(at, at ^ turn) for at in range(size)])]
  transfers between devices with their start and end apart: 12 -> 12, of which waited for: 4 -> 4; matrix products, arithmetic and copies ran while one was open for 3% -> 3% of each run, Pallas kernels for 39% -> 40%
where the time goes in v21:
time: 34.5 us; the launch traced here: 34.4 us
  starting transfers between devices  14.3 us (41%)
  Pallas kernels  13.7 us (40%)
  waiting for transfers between devices  3.98 us (12%)
  other arithmetic  0.9 us (3%)
  between operations  0.82 us (2%)
  local copies, waits for them, and re-layouts  0.72 us (2%)
    ppermute x12, starting transfers between devices, exchange(): return lax.ppermute(value, axes, [(at, at ^ turn) for at in range(size)])  14.3 us
    pallas_call x2, Pallas kernels, lag_windows(): pl.pallas_call(functools.partial(spectrum_kernel, vols, across, block, ow...  6.06 us
    pallas_call x2, Pallas kernels, warp_sums(): pl.pallas_call(functools.partial(warp_kernel, down, across, block, own, o...  5.67 us
    ppermute x12, waiting for transfers between devices, exchange(): return lax.ppermute(value, axes, [(at, at ^ turn) for at in range(size)])  3.98 us
    pallas_call x1, Pallas kernels, stage(): pl.pallas_call(functools.partial(stage_kernel, count), out_shape=[jax.Sha...  1.93 us
    unnamed x1, other arithmetic  0.7 us
  transfers between devices with their start and end apart: 12, of which 4 were waited for; matrix products, arithmetic and copies ran while one was open for 3% of the time, Pallas kernels for 40%

profile of v21, /device:TPU:0, one launch (start us, length us, event | category | flops | bytes accessed | tf_op | source)
XLA Modules:
  0.0 34.4 jit_solution(17406644031338985526)
XLA Ops:
  0.6 0.0 copy-start
  0.7 0.5 %collective-permute-start.1 = (bf16[2,1,512,1024]{3,2,0,1:T(8,128)(2,1)}, bf16[2,1,512,1024]{3,2,0,1:T(8,128)(2,1)S(1)}, u32[]{:S(2)}, u32[]{:S(2)}) collective-permute-start(bf16[2,1,512,1024]{3,2,0,1:T(8,128)(2,1)} %bitcast.36), channel_id=1, source_target_pairs={{0,2},{2,0},{1,3},{3,1},{4,6},{6,4},{5,7},{7,5},{8,10},{10,8},{9,1... | collective-permute-start | bytes 6291464 | tf_op jit(solution)/shard_map/ppermute | solution.py:456
  1.2 2.7 %collective-permute-start.2 = (bf16[2,1,128,128]{3,2,0,1:T(8,128)(2,1)}, bf16[2,1,128,128]{3,2,0,1:T(8,128)(2,1)S(1)}, u32[]{:S(2)}, u32[]{:S(2)}) collective-permute-start(bf16[2,1,128,128]{3,2,0,1:T(8,128)(2,1)} %bitcast.32), channel_id=1, source_target_pairs={{0,8},{8,0},{16,24},{24,16},{1,9},{9,1},{17,25},{25,17},{2,10},{10... | collective-permute-start | bytes 196616 | tf_op jit(solution)/shard_map/ppermute | solution.py:456
  3.8 2.6 %collective-permute-start.3 = (bf16[2,1,128,128]{3,2,0,1:T(8,128)(2,1)}, bf16[2,1,128,128]{3,2,0,1:T(8,128)(2,1)S(1)}, u32[]{:S(2)}, u32[]{:S(2)}) collective-permute-start(bf16[2,1,128,128]{3,2,0,1:T(8,128)(2,1)} %bitcast.33), channel_id=1, source_target_pairs={{0,16},{8,24},{16,0},{24,8},{1,17},{9,25},{17,1},{25,9},{2,18},{10... | collective-permute-start | bytes 196616 | tf_op jit(solution)/shard_map/ppermute | solution.py:456
  6.4 0.1 pad_add_fusion.refs_0_
  6.5 1.9 %stage.1 = (f32[16,176,128]{2,1,0:T(8,128)S(1)}, f32[16,64,128]{2,1,0:T(8,128)S(1)}, bf16[2,1,512,1024]{3,2,1,0:T(8,128)(2,1)S(1)}) custom-call(bf16[16,176,128]{2,1,0:T(8,128)(2,1)} %constant.32.clone.refs_0_, bf16[16,64,128]{2,1,0:T(8,128)(2,1)} %constant.33.clone.refs_1_, bf16[2,1,512,1024]{3,2,1,0:T(8,128)(2,1)} %refs_2_.1, bf16[2,1,128,128]{3,2,1,0:T(8,128)(2,1)} %refs_7_.1), custom_call_target="tpu_custom_call" | custom-call | bytes 4194304 | tf_op jit(solution)/shard_map/stage/pallas_call | solution.py:113
  8.5 2.8 %warp.2.refs_7_ = bf16[8,128,128]{2,1,0:T(8,128)(2,1)S(1)} custom-call(s32[4]{0:T(128)S(1)} %pad_add_fusion.refs_0_, s32[2,2,32]{2,1,0:T(2,128)S(1)} %copy-done.5, s32[2,2,32]{2,1,0:T(2,128)S(1)} %collective-permute-done.refs_2_, bf16[2,512,1024]{2,1,0:T(8,128)(2,1)S(1)} %bitcast.28, bf16[2,512,1024]{2,1,0:T(8,128)(2,1)S(1)} %bitcast.24, ...), custom_call_target="tpu_custom_call" | custom-call | flops 2147483648 | bytes 4718592 | tf_op jit(solution)/shard_map/warp/pallas_call | solution.py:232
  11.3 0.0 copy-start.1
  11.4 1.8 %collective-permute-start.6 = (bf16[8,128,128]{2,1,0:T(8,128)(2,1)S(1)}, bf16[8,128,128]{2,1,0:T(8,128)(2,1)S(1)}, u32[]{:S(2)}, u32[]{:S(2)}) collective-permute-start(bf16[8,128,128]{2,1,0:T(8,128)(2,1)S(1)} %warp.2.refs_7_), channel_id=1, source_target_pairs={{0,4},{4,0},{1,5},{5,1},{2,6},{6,2},{3,7},{7,3},{8,12},{12,8},{9,1... | collective-permute-start | bytes 786440 | tf_op jit(solution)/shard_map/ppermute | solution.py:456
  13.2 2.8 %warp.3 = (bf16[2,128,128]{2,1,0:T(8,128)(2,1)S(1)}, bf16[2,128,128]{2,1,0:T(8,128)(2,1)S(1)}, bf16[2,128,128]{2,1,0:T(8,128)(2,1)S(1)}, bf16[2,128,128]{2,1,0:T(8,128)(2,1)S(1)}) custom-call(s32[4]{0:T(128)S(1)} %pad_add_fusion.refs_0_, s32[2,2,32]{2,1,0:T(2,128)S(1)} %copy-done.5, s32[2,2,32]{2,1,0:T(2,128)S(1)} %collective-permute-done.refs_2_, ...), custom_call_target="tpu_custom_call" | custom-call | flops 2147483648 | bytes 4718592 | tf_op jit(solution)/shard_map/warp/pallas_call | solution.py:232
  16.1 0.4 %collective-permute-start.5 = (bf16[8,128,128]{2,1,0:T(8,128)(2,1)S(1)}, bf16[8,128,128]{2,1,0:T(8,128)(2,1)S(1)}, u32[]{:S(2)}, u32[]{:S(2)}) collective-permute-start(bf16[8,128,128]{2,1,0:T(8,128)(2,1)S(1)} %pad_maximum_fusion.refs_9_), channel_id=1, source_target_pairs={{0,4},{4,0},{1,5},{5,1},{2,6},{6,2},{3,7},{7,3},{8,12},{12,8},{9,1... | collective-permute-start | bytes 786440 | tf_op jit(solution)/shard_map/ppermute | solution.py:456
  16.5 3.2 %lag_windows.2 = (f32[4,256,128]{2,1,0:T(8,128)S(1)}, f32[2,640,256]{2,1,0:T(8,128)S(1)}) custom-call(s32[4]{0:T(128)S(1)} %pad_add_fusion.refs_0_, s32[2,2,32]{2,1,0:T(2,128)S(1)} %copy-done.5, s32[2,2,32]{2,1,0:T(2,128)S(1)} %collective-permute-done.refs_2_, bf16[160,128]{1,0:T(8,128)(2,1)S(1)} %copy-done.3, bf16[256,256]{1,0:T(8,128)(2,1)S(1)} %copy-done.1, ...), custom_call_target="tpu_custom_call" | custom-call | flops 3221225472 | bytes 4718592 | tf_op jit(solution)/shard_map/lag_windows/pallas_call | solution.py:435
  19.7 0.8 %collective-permute-done.6 = bf16[8,128,128]{2,1,0:T(8,128)(2,1)S(1)} collective-permute-done((bf16[8,128,128]{2,1,0:T(8,128)(2,1)S(1)}, bf16[8,128,128]{2,1,0:T(8,128)(2,1)S(1)}, u32[]{:S(2)}, u32[]{:S(2)}) %collective-permute-start.6) | collective-permute-done | bytes 262176 | tf_op jit(solution)/shard_map/ppermute | solution.py:456
  20.5 0.1 add_convert_fusion
  20.6 3.9 %collective-permute-start.7 = (bf16[2,128,128]{2,1,0:T(8,128)(2,1)S(1)}, bf16[2,128,128]{2,1,0:T(8,128)(2,1)S(1)}, u32[]{:S(2)}, u32[]{:S(2)}) collective-permute-start(bf16[2,128,128]{2,1,0:T(8,128)(2,1)S(1)} %get-tuple-element.52), channel_id=1, source_target_pairs={{0,24},{8,16},{16,8},{24,0},{1,25},{9,17},{17,9},{25,1},{2,26},{10... | collective-permute-start | bytes 196616 | tf_op jit(solution)/shard_map/ppermute | solution.py:456
  24.5 0.6 %collective-permute-start.9 = (bf16[2,128,128]{2,1,0:T(8,128)(2,1)S(1)}, bf16[2,128,128]{2,1,0:T(8,128)(2,1)S(1)}, u32[]{:S(2)}, u32[]{:S(2)}) collective-permute-start(bf16[2,128,128]{2,1,0:T(8,128)(2,1)S(1)} %get-tuple-element.50), channel_id=1, source_target_pairs={{0,16},{8,24},{16,0},{24,8},{1,17},{9,25},{17,1},{25,9},{2,18},{10... | collective-permute-start | bytes 196616 | tf_op jit(solution)/shard_map/ppermute | solution.py:456
  25.1 0.6 %collective-permute-done.5.refs_9_ = bf16[8,128,128]{2,1,0:T(8,128)(2,1)S(1)} collective-permute-done((bf16[8,128,128]{2,1,0:T(8,128)(2,1)S(1)}, bf16[8,128,128]{2,1,0:T(8,128)(2,1)S(1)}, u32[]{:S(2)}, u32[]{:S(2)}) %collective-permute-start.5) | collective-permute-done | bytes 262176 | tf_op jit(solution)/shard_map/ppermute | solution.py:456
  25.8 2.8 %lag_windows.3 = (f32[2,2,8,256]{3,2,1,0:T(8,128)S(1)}, bf16[2,2,8,256]{3,2,1,0:T(8,128)(2,1)S(1)}) custom-call(s32[4]{0:T(128)S(1)} %pad_add_fusion.refs_0_, s32[2,2,32]{2,1,0:T(2,128)S(1)} %copy-done.5, s32[2,2,32]{2,1,0:T(2,128)S(1)} %collective-permute-done.refs_2_, bf16[160,128]{1,0:T(8,128)(2,1)S(1)} %copy-done.3, bf16[256,256]{1,0:T(8,128)(2,1)S(1)} %copy-done.1, ...), custom_call_target="tpu_custom_call" | custom-call | flops 805306368 | bytes 4718592 | tf_op jit(solution)/shard_map/lag_windows/pallas_call | solution.py:435
  28.6 1.8 %collective-permute-start.10 = (bf16[2,2,8,256]{3,2,1,0:T(8,128)(2,1)S(1)}, bf16[2,2,8,256]{3,2,1,0:T(8,128)(2,1)S(1)}, u32[]{:S(2)}, u32[]{:S(2)}) collective-permute-start(bf16[2,2,8,256]{3,2,1,0:T(8,128)(2,1)S(1)} %get-tuple-element.44), channel_id=1, source_target_pairs={{0,1},{1,0},{2,3},{3,2},{4,5},{5,4},{6,7},{7,6},{8,9},{9,8},{10,11... | collective-permute-start | bytes 49160 | tf_op jit(solution)/shard_map/ppermute | solution.py:456
  30.4 2.0 %collective-permute-done.10 = bf16[2,2,8,256]{3,2,1,0:T(8,128)(2,1)S(1)} collective-permute-done((bf16[2,2,8,256]{3,2,1,0:T(8,128)(2,1)S(1)}, bf16[2,2,8,256]{3,2,1,0:T(8,128)(2,1)S(1)}, u32[]{:S(2)}, u32[]{:S(2)}) %collective-permute-start.10) | collective-permute-done | bytes 16416 | tf_op jit(solution)/shard_map/ppermute | solution.py:456
  32.4 0.1 collective-permute-start.11
  32.5 0.7 %multiply_bitcast_fusion = f32[2,1,128,128]{3,2,1,0:T(8,128)} fusion(bf16[2,128,128]{2,1,0:T(8,128)(2,1)S(1)} %collective-permute-done.9, bf16[2,128,128]{2,1,0:T(8,128)(2,1)S(1)} %collective-permute-done.8, bf16[2,128,128]{2,1,0:T(8,128)(2,1)S(1)} %collective-permute-done.7, bf16[2,128,128]{2,1,0:T(8,128)(2,1)S(1)} %get-tuple-element.36.refs_10_, ...), kind=kLoop, calls=%fused_computation.1 | loop fusion | flops 327680 | bytes 458752
  33.2 0.5 %collective-permute-done.11 = bf16[2,8,256]{2,1,0:T(8,128)(2,1)S(1)} collective-permute-done((bf16[2,8,256]{2,1,0:T(8,128)(2,1)S(1)}, bf16[2,8,256]{2,1,0:T(8,128)(2,1)S(1)}, u32[]{:S(2)}, u32[]{:S(2)}) %collective-permute-start.11) | collective-permute-done | bytes 8224 | tf_op jit(solution)/shard_map/ppermute | solution.py:456
  33.8 0.6 %reshape.16 = f32[2,16,256]{2,1,0:T(8,128)} reshape(f32[2,4,2,2,256]{4,3,2,1,0:T(2,128)S(1)} %copy.19) | data formatting | bytes 65536 | tf_op jit(solution)/shard_map/reshape | solution.py:499
  (29 shorter events, 0.2 us)
Async XLA Ops:
  0.6 7.8 %copy-start = (bf16[2,1,128,128]{3,2,1,0:T(8,128)(2,1)S(1)}, bf16[2,1,128,128]{3,2,1,0:T(8,128)(2,1)}, u32[]{:S(2)}) copy-start(bf16[2,1,128,128]{3,2,1,0:T(8,128)(2,1)} %refs_7_.1) | copy-start | bytes 196612
  0.6 7.8 %copy-start.5 = (s32[2,2,32]{2,1,0:T(2,128)S(1)}, s32[2,2,32]{2,1,0:T(2,128)}, u32[]{:S(2)}) copy-start(s32[2,2,32]{2,1,0:T(2,128)} %refs_1_.8) | copy-start | bytes 1540
  0.7 7.8 %collective-permute-start.1 = (bf16[2,1,512,1024]{3,2,0,1:T(8,128)(2,1)}, bf16[2,1,512,1024]{3,2,0,1:T(8,128)(2,1)S(1)}, u32[]{:S(2)}, u32[]{:S(2)}) collective-permute-start(bf16[2,1,512,1024]{3,2,0,1:T(8,128)(2,1)} %bitcast.36), channel_id=1, source_target_pairs={{0,2},{2,0},{1,3},{3,1},{4,6},{6,4},{5,7},{7,5},{8,10},{10,8},{9,1... | collective-permute-start | bytes 6291464 | tf_op jit(solution)/shard_map/ppermute | solution.py:456
  1.2 14.8 %collective-permute-start.2 = (bf16[2,1,128,128]{3,2,0,1:T(8,128)(2,1)}, bf16[2,1,128,128]{3,2,0,1:T(8,128)(2,1)S(1)}, u32[]{:S(2)}, u32[]{:S(2)}) collective-permute-start(bf16[2,1,128,128]{3,2,0,1:T(8,128)(2,1)} %bitcast.32), channel_id=1, source_target_pairs={{0,8},{8,0},{16,24},{24,16},{1,9},{9,1},{17,25},{25,17},{2,10},{10... | collective-permute-start | bytes 196616 | tf_op jit(solution)/shard_map/ppermute | solution.py:456
  3.8 12.2 %collective-permute-start.3 = (bf16[2,1,128,128]{3,2,0,1:T(8,128)(2,1)}, bf16[2,1,128,128]{3,2,0,1:T(8,128)(2,1)S(1)}, u32[]{:S(2)}, u32[]{:S(2)}) collective-permute-start(bf16[2,1,128,128]{3,2,0,1:T(8,128)(2,1)} %bitcast.33), channel_id=1, source_target_pairs={{0,16},{8,24},{16,0},{24,8},{1,17},{9,25},{17,1},{25,9},{2,18},{10... | collective-permute-start | bytes 196616 | tf_op jit(solution)/shard_map/ppermute | solution.py:456
  6.4 9.6 %collective-permute-start.4 = (bf16[2,1,128,128]{3,2,0,1:T(8,128)(2,1)}, bf16[2,1,128,128]{3,2,0,1:T(8,128)(2,1)S(1)}, u32[]{:S(2)}, u32[]{:S(2)}) collective-permute-start(bf16[2,1,128,128]{3,2,0,1:T(8,128)(2,1)} %bitcast.34), channel_id=1, source_target_pairs={{0,24},{8,16},{16,8},{24,0},{1,25},{9,17},{17,9},{25,1},{2,26},{10... | collective-permute-start | bytes 196616 | tf_op jit(solution)/shard_map/ppermute | solution.py:456
  6.4 2.0 %collective-permute-start = (s32[2,2,32]{2,1,0:T(2,128)}, s32[2,2,32]{2,1,0:T(2,128)S(1)}, u32[]{:S(2)}, u32[]{:S(2)}) collective-permute-start(s32[2,2,32]{2,1,0:T(2,128)} %refs_1_.8), channel_id=1, source_target_pairs={{0,2},{2,0},{1,3},{3,1},{4,6},{6,4},{5,7},{7,5},{8,10},{10,8},{9,1... | collective-permute-start | bytes 1544 | tf_op jit(solution)/shard_map/ppermute | solution.py:456
  11.3 5.1 %copy-start.1 = (bf16[256,256]{1,0:T(8,128)(2,1)S(1)}, bf16[256,256]{1,0:T(8,128)(2,1)}, u32[]{:S(2)}) copy-start(bf16[256,256]{1,0:T(8,128)(2,1)} %constant.35.clone.refs_4_) | copy-start | bytes 393220
  11.3 5.1 %copy-start.2 = (bf16[256,128]{1,0:T(8,128)(2,1)S(1)}, bf16[256,128]{1,0:T(8,128)(2,1)}, u32[]{:S(2)}) copy-start(bf16[256,128]{1,0:T(8,128)(2,1)} %constant.37.clone.refs_6_) | copy-start | bytes 196612
  11.3 5.1 %copy-start.3 = (bf16[160,128]{1,0:T(8,128)(2,1)S(1)}, bf16[160,128]{1,0:T(8,128)(2,1)}, u32[]{:S(2)}) copy-start(bf16[160,128]{1,0:T(8,128)(2,1)} %constant.34.clone.refs_3_) | copy-start | bytes 122884
  11.4 5.1 %copy-start.4 = (bf16[64,160]{1,0:T(8,128)(2,1)S(1)}, bf16[64,160]{1,0:T(8,128)(2,1)}, u32[]{:S(2)}) copy-start(bf16[64,160]{1,0:T(8,128)(2,1)} %constant.36.clone.refs_5_) | copy-start | bytes 61444
  11.4 9.2 %collective-permute-start.6 = (bf16[8,128,128]{2,1,0:T(8,128)(2,1)S(1)}, bf16[8,128,128]{2,1,0:T(8,128)(2,1)S(1)}, u32[]{:S(2)}, u32[]{:S(2)}) collective-permute-start(bf16[8,128,128]{2,1,0:T(8,128)(2,1)S(1)} %warp.2.refs_7_), channel_id=1, source_target_pairs={{0,4},{4,0},{1,5},{5,1},{2,6},{6,2},{3,7},{7,3},{8,12},{12,8},{9,1... | collective-permute-start | bytes 786440 | tf_op jit(solution)/shard_map/ppermute | solution.py:456
  16.1 9.7 %collective-permute-start.5 = (bf16[8,128,128]{2,1,0:T(8,128)(2,1)S(1)}, bf16[8,128,128]{2,1,0:T(8,128)(2,1)S(1)}, u32[]{:S(2)}, u32[]{:S(2)}) collective-permute-start(bf16[8,128,128]{2,1,0:T(8,128)(2,1)S(1)} %pad_maximum_fusion.refs_9_), channel_id=1, source_target_pairs={{0,4},{4,0},{1,5},{5,1},{2,6},{6,2},{3,7},{7,3},{8,12},{12,8},{9,1... | collective-permute-start | bytes 786440 | tf_op jit(solution)/shard_map/ppermute | solution.py:456
  20.6 9.8 %collective-permute-start.7 = (bf16[2,128,128]{2,1,0:T(8,128)(2,1)S(1)}, bf16[2,128,128]{2,1,0:T(8,128)(2,1)S(1)}, u32[]{:S(2)}, u32[]{:S(2)}) collective-permute-start(bf16[2,128,128]{2,1,0:T(8,128)(2,1)S(1)} %get-tuple-element.52), channel_id=1, source_target_pairs={{0,24},{8,16},{16,8},{24,0},{1,25},{9,17},{17,9},{25,1},{2,26},{10... | collective-permute-start | bytes 196616 | tf_op jit(solution)/shard_map/ppermute | solution.py:456
  24.5 5.9 %collective-permute-start.8 = (bf16[2,128,128]{2,1,0:T(8,128)(2,1)S(1)}, bf16[2,128,128]{2,1,0:T(8,128)(2,1)S(1)}, u32[]{:S(2)}, u32[]{:S(2)}) collective-permute-start(bf16[2,128,128]{2,1,0:T(8,128)(2,1)S(1)} %get-tuple-element.51), channel_id=1, source_target_pairs={{0,8},{8,0},{16,24},{24,16},{1,9},{9,1},{17,25},{25,17},{2,10},{10... | collective-permute-start | bytes 196616 | tf_op jit(solution)/shard_map/ppermute | solution.py:456
  24.5 5.9 %collective-permute-start.9 = (bf16[2,128,128]{2,1,0:T(8,128)(2,1)S(1)}, bf16[2,128,128]{2,1,0:T(8,128)(2,1)S(1)}, u32[]{:S(2)}, u32[]{:S(2)}) collective-permute-start(bf16[2,128,128]{2,1,0:T(8,128)(2,1)S(1)} %get-tuple-element.50), channel_id=1, source_target_pairs={{0,16},{8,24},{16,0},{24,8},{1,17},{9,25},{17,1},{25,9},{2,18},{10... | collective-permute-start | bytes 196616 | tf_op jit(solution)/shard_map/ppermute | solution.py:456
  28.6 3.8 %collective-permute-start.10 = (bf16[2,2,8,256]{3,2,1,0:T(8,128)(2,1)S(1)}, bf16[2,2,8,256]{3,2,1,0:T(8,128)(2,1)S(1)}, u32[]{:S(2)}, u32[]{:S(2)}) collective-permute-start(bf16[2,2,8,256]{3,2,1,0:T(8,128)(2,1)S(1)} %get-tuple-element.44), channel_id=1, source_target_pairs={{0,1},{1,0},{2,3},{3,2},{4,5},{5,4},{6,7},{7,6},{8,9},{9,8},{10,11... | collective-permute-start | bytes 49160 | tf_op jit(solution)/shard_map/ppermute | solution.py:456
  32.4 1.2 %collective-permute-start.11 = (bf16[2,8,256]{2,1,0:T(8,128)(2,1)S(1)}, bf16[2,8,256]{2,1,0:T(8,128)(2,1)S(1)}, u32[]{:S(2)}, u32[]{:S(2)}) collective-permute-start(bf16[2,8,256]{2,1,0:T(8,128)(2,1)S(1)} %fusion), channel_id=1, source_target_pairs={{0,2},{2,0},{1,3},{3,1},{4,6},{6,4},{5,7},{7,5},{8,10},{10,8},{9,1... | collective-permute-start | bytes 24584 | tf_op jit(solution)/shard_map/ppermute | solution.py:456

commit v22 on v21

--- a/solution.py
+++ b/solution.py
@@ -388,7 +388,7 @@
             spectra_ref[pair] = transform(frame_sources(places[2 * pair : 2 * pair + 2]))
         return
 
-    share = found.shape[1] // WIN // planes
+    share = (found.shape[1] // WIN - 1) // planes
     per_tile = LANES // WIN
     lane = lax.broadcasted_iota(jnp.int32, (share, LANES), 1) // WIN
     for turn, out_ref in enumerate(out_refs):
@@ -419,7 +419,7 @@
     vmem = pl.BlockSpec(memory_space=pltpu.VMEM)
     blocks = down * across // 2
     many = 2 * vols * 2 * own
-    found = jax.ShapeDtypeStruct((2 * vols, blocks * WIN, LANES), jnp.float32)
+    found = jax.ShapeDtypeStruct((2 * vols, (blocks + 1) * WIN, LANES), jnp.float32)
     if other:
         out = (2, vols, blocks // planes, WIN * WIN)
         out_shape = [jax.ShapeDtypeStruct(out, jnp.float32)]

time: 34.5 us -> 34.6 us (level)
  no operation moved by 1% of the time
where the time goes in v22:
time: 34.6 us; the launch traced here: 34.4 us
  starting transfers between devices  14.3 us (41%)
  Pallas kernels  13.7 us (40%)
  waiting for transfers between devices  4.02 us (12%)
  other arithmetic  0.9 us (3%)
  between operations  0.81 us (2%)
  local copies, waits for them, and re-layouts  0.72 us (2%)
    ppermute x12, starting transfers between devices, exchange(): return lax.ppermute(value, axes, [(at, at ^ turn) for at in range(size)])  14.3 us
    pallas_call x2, Pallas kernels, lag_windows(): pl.pallas_call(functools.partial(spectrum_kernel, vols, across, block, ow...  6.06 us
    pallas_call x2, Pallas kernels, warp_sums(): pl.pallas_call(functools.partial(warp_kernel, down, across, block, own, o...  5.68 us
    ppermute x12, waiting for transfers between devices, exchange(): return lax.ppermute(value, axes, [(at, at ^ turn) for at in range(size)])  4.02 us
    pallas_call x1, Pallas kernels, stage(): pl.pallas_call(functools.partial(stage_kernel, count), out_shape=[jax.Sha...  1.93 us
    unnamed x1, other arithmetic  0.7 us
  transfers between devices with their start and end apart: 12, of which 4 were waited for; matrix products, arithmetic and copies ran while one was open for 3% of the time, Pallas kernels for 40%

profile of v22, /device:TPU:0, one launch (start us, length us, event | category | flops | bytes accessed | tf_op | source)
XLA Modules:
  0.0 34.4 jit_solution(12724526121229078875)
XLA Ops:
  0.6 0.0 copy-start
  0.7 0.5 %collective-permute-start.1 = (bf16[2,1,512,1024]{3,2,0,1:T(8,128)(2,1)}, bf16[2,1,512,1024]{3,2,0,1:T(8,128)(2,1)S(1)}, u32[]{:S(2)}, u32[]{:S(2)}) collective-permute-start(bf16[2,1,512,1024]{3,2,0,1:T(8,128)(2,1)} %bitcast.36), channel_id=1, source_target_pairs={{0,2},{2,0},{1,3},{3,1},{4,6},{6,4},{5,7},{7,5},{8,10},{10,8},{9,1... | collective-permute-start | bytes 6291464 | tf_op jit(solution)/shard_map/ppermute | solution.py:456
  1.2 2.7 %collective-permute-start.2 = (bf16[2,1,128,128]{3,2,0,1:T(8,128)(2,1)}, bf16[2,1,128,128]{3,2,0,1:T(8,128)(2,1)S(1)}, u32[]{:S(2)}, u32[]{:S(2)}) collective-permute-start(bf16[2,1,128,128]{3,2,0,1:T(8,128)(2,1)} %bitcast.32), channel_id=1, source_target_pairs={{0,8},{8,0},{16,24},{24,16},{1,9},{9,1},{17,25},{25,17},{2,10},{10... | collective-permute-start | bytes 196616 | tf_op jit(solution)/shard_map/ppermute | solution.py:456
  3.8 2.6 %collective-permute-start.3 = (bf16[2,1,128,128]{3,2,0,1:T(8,128)(2,1)}, bf16[2,1,128,128]{3,2,0,1:T(8,128)(2,1)S(1)}, u32[]{:S(2)}, u32[]{:S(2)}) collective-permute-start(bf16[2,1,128,128]{3,2,0,1:T(8,128)(2,1)} %bitcast.33), channel_id=1, source_target_pairs={{0,16},{8,24},{16,0},{24,8},{1,17},{9,25},{17,1},{25,9},{2,18},{10... | collective-permute-start | bytes 196616 | tf_op jit(solution)/shard_map/ppermute | solution.py:456
  6.4 0.1 pad_add_fusion.refs_0_
  6.5 1.9 %stage.1 = (f32[16,176,128]{2,1,0:T(8,128)S(1)}, f32[16,64,128]{2,1,0:T(8,128)S(1)}, bf16[2,1,512,1024]{3,2,1,0:T(8,128)(2,1)S(1)}) custom-call(bf16[16,176,128]{2,1,0:T(8,128)(2,1)} %constant.32.clone.refs_0_, bf16[16,64,128]{2,1,0:T(8,128)(2,1)} %constant.33.clone.refs_1_, bf16[2,1,512,1024]{3,2,1,0:T(8,128)(2,1)} %refs_2_.1, bf16[2,1,128,128]{3,2,1,0:T(8,128)(2,1)} %refs_7_.1), custom_call_target="tpu_custom_call" | custom-call | bytes 4194304 | tf_op jit(solution)/shard_map/stage/pallas_call | solution.py:113
  8.5 2.8 %warp.2.refs_7_ = bf16[8,128,128]{2,1,0:T(8,128)(2,1)S(1)} custom-call(s32[4]{0:T(128)S(1)} %pad_add_fusion.refs_0_, s32[2,2,32]{2,1,0:T(2,128)S(1)} %copy-done.5, s32[2,2,32]{2,1,0:T(2,128)S(1)} %collective-permute-done.refs_2_, bf16[2,512,1024]{2,1,0:T(8,128)(2,1)S(1)} %bitcast.28, bf16[2,512,1024]{2,1,0:T(8,128)(2,1)S(1)} %bitcast.24, ...), custom_call_target="tpu_custom_call" | custom-call | flops 2147483648 | bytes 4718592 | tf_op jit(solution)/shard_map/warp/pallas_call | solution.py:232
  11.3 0.0 copy-start.2
  11.4 1.8 %collective-permute-start.6 = (bf16[8,128,128]{2,1,0:T(8,128)(2,1)S(1)}, bf16[8,128,128]{2,1,0:T(8,128)(2,1)S(1)}, u32[]{:S(2)}, u32[]{:S(2)}) collective-permute-start(bf16[8,128,128]{2,1,0:T(8,128)(2,1)S(1)} %warp.2.refs_7_), channel_id=1, source_target_pairs={{0,4},{4,0},{1,5},{5,1},{2,6},{6,2},{3,7},{7,3},{8,12},{12,8},{9,1... | collective-permute-start | bytes 786440 | tf_op jit(solution)/shard_map/ppermute | solution.py:456
  13.2 2.8 %warp.3 = (bf16[2,128,128]{2,1,0:T(8,128)(2,1)S(1)}, bf16[2,128,128]{2,1,0:T(8,128)(2,1)S(1)}, bf16[2,128,128]{2,1,0:T(8,128)(2,1)S(1)}, bf16[2,128,128]{2,1,0:T(8,128)(2,1)S(1)}) custom-call(s32[4]{0:T(128)S(1)} %pad_add_fusion.refs_0_, s32[2,2,32]{2,1,0:T(2,128)S(1)} %copy-done.5, s32[2,2,32]{2,1,0:T(2,128)S(1)} %collective-permute-done.refs_2_, ...), custom_call_target="tpu_custom_call" | custom-call | flops 2147483648 | bytes 4718592 | tf_op jit(solution)/shard_map/warp/pallas_call | solution.py:232
  16.1 0.3 collective-permute-start.5
  16.4 3.2 %lag_windows.2 = (f32[4,272,128]{2,1,0:T(8,128)S(1)}, f32[2,640,256]{2,1,0:T(8,128)S(1)}) custom-call(s32[4]{0:T(128)S(1)} %pad_add_fusion.refs_0_, s32[2,2,32]{2,1,0:T(2,128)S(1)} %copy-done.5, s32[2,2,32]{2,1,0:T(2,128)S(1)} %collective-permute-done.refs_2_, bf16[160,128]{1,0:T(8,128)(2,1)S(1)} %copy-done.3, bf16[256,256]{1,0:T(8,128)(2,1)S(1)} %copy-done.1, ...), custom_call_target="tpu_custom_call" | custom-call | flops 3221225472 | bytes 4718592 | tf_op jit(solution)/shard_map/lag_windows/pallas_call | solution.py:435
  19.7 0.9 %collective-permute-done.6 = bf16[8,128,128]{2,1,0:T(8,128)(2,1)S(1)} collective-permute-done((bf16[8,128,128]{2,1,0:T(8,128)(2,1)S(1)}, bf16[8,128,128]{2,1,0:T(8,128)(2,1)S(1)}, u32[]{:S(2)}, u32[]{:S(2)}) %collective-permute-start.6) | collective-permute-done | bytes 262176 | tf_op jit(solution)/shard_map/ppermute | solution.py:456
  20.5 0.1 add_convert_fusion
  20.6 3.9 %collective-permute-start.7 = (bf16[2,128,128]{2,1,0:T(8,128)(2,1)S(1)}, bf16[2,128,128]{2,1,0:T(8,128)(2,1)S(1)}, u32[]{:S(2)}, u32[]{:S(2)}) collective-permute-start(bf16[2,128,128]{2,1,0:T(8,128)(2,1)S(1)} %get-tuple-element.52), channel_id=1, source_target_pairs={{0,24},{8,16},{16,8},{24,0},{1,25},{9,17},{17,9},{25,1},{2,26},{10... | collective-permute-start | bytes 196616 | tf_op jit(solution)/shard_map/ppermute | solution.py:456
  24.5 0.6 %collective-permute-start.9 = (bf16[2,128,128]{2,1,0:T(8,128)(2,1)S(1)}, bf16[2,128,128]{2,1,0:T(8,128)(2,1)S(1)}, u32[]{:S(2)}, u32[]{:S(2)}) collective-permute-start(bf16[2,128,128]{2,1,0:T(8,128)(2,1)S(1)} %get-tuple-element.50), channel_id=1, source_target_pairs={{0,16},{8,24},{16,0},{24,8},{1,17},{9,25},{17,1},{25,9},{2,18},{10... | collective-permute-start | bytes 196616 | tf_op jit(solution)/shard_map/ppermute | solution.py:456
  25.1 0.7 %collective-permute-done.5.refs_9_ = bf16[8,128,128]{2,1,0:T(8,128)(2,1)S(1)} collective-permute-done((bf16[8,128,128]{2,1,0:T(8,128)(2,1)S(1)}, bf16[8,128,128]{2,1,0:T(8,128)(2,1)S(1)}, u32[]{:S(2)}, u32[]{:S(2)}) %collective-permute-start.5) | collective-permute-done | bytes 262176 | tf_op jit(solution)/shard_map/ppermute | solution.py:456
  25.8 2.8 %lag_windows.3 = (f32[2,2,8,256]{3,2,1,0:T(8,128)S(1)}, bf16[2,2,8,256]{3,2,1,0:T(8,128)(2,1)S(1)}) custom-call(s32[4]{0:T(128)S(1)} %pad_add_fusion.refs_0_, s32[2,2,32]{2,1,0:T(2,128)S(1)} %copy-done.5, s32[2,2,32]{2,1,0:T(2,128)S(1)} %collective-permute-done.refs_2_, bf16[160,128]{1,0:T(8,128)(2,1)S(1)} %copy-done.3, bf16[256,256]{1,0:T(8,128)(2,1)S(1)} %copy-done.1, ...), custom_call_target="tpu_custom_call" | custom-call | flops 805306368 | bytes 4718592 | tf_op jit(solution)/shard_map/lag_windows/pallas_call | solution.py:435
  28.6 1.8 %collective-permute-start.10 = (bf16[2,2,8,256]{3,2,1,0:T(8,128)(2,1)S(1)}, bf16[2,2,8,256]{3,2,1,0:T(8,128)(2,1)S(1)}, u32[]{:S(2)}, u32[]{:S(2)}) collective-permute-start(bf16[2,2,8,256]{3,2,1,0:T(8,128)(2,1)S(1)} %get-tuple-element.44), channel_id=1, source_target_pairs={{0,1},{1,0},{2,3},{3,2},{4,5},{5,4},{6,7},{7,6},{8,9},{9,8},{10,11... | collective-permute-start | bytes 49160 | tf_op jit(solution)/shard_map/ppermute | solution.py:456
  30.4 2.0 %collective-permute-done.10 = bf16[2,2,8,256]{3,2,1,0:T(8,128)(2,1)S(1)} collective-permute-done((bf16[2,2,8,256]{3,2,1,0:T(8,128)(2,1)S(1)}, bf16[2,2,8,256]{3,2,1,0:T(8,128)(2,1)S(1)}, u32[]{:S(2)}, u32[]{:S(2)}) %collective-permute-start.10) | collective-permute-done | bytes 16416 | tf_op jit(solution)/shard_map/ppermute | solution.py:456
  32.4 0.1 collective-permute-start.11
  32.5 0.7 %multiply_bitcast_fusion = f32[2,1,128,128]{3,2,1,0:T(8,128)} fusion(bf16[2,128,128]{2,1,0:T(8,128)(2,1)S(1)} %collective-permute-done.9, bf16[2,128,128]{2,1,0:T(8,128)(2,1)S(1)} %collective-permute-done.8, bf16[2,128,128]{2,1,0:T(8,128)(2,1)S(1)} %collective-permute-done.7, bf16[2,128,128]{2,1,0:T(8,128)(2,1)S(1)} %get-tuple-element.36.refs_10_, ...), kind=kLoop, calls=%fused_computation.1 | loop fusion | flops 327680 | bytes 458752
  33.2 0.5 %collective-permute-done.11 = bf16[2,8,256]{2,1,0:T(8,128)(2,1)S(1)} collective-permute-done((bf16[2,8,256]{2,1,0:T(8,128)(2,1)S(1)}, bf16[2,8,256]{2,1,0:T(8,128)(2,1)S(1)}, u32[]{:S(2)}, u32[]{:S(2)}) %collective-permute-start.11) | collective-permute-done | bytes 8224 | tf_op jit(solution)/shard_map/ppermute | solution.py:456
  33.8 0.6 %reshape.16 = f32[2,16,256]{2,1,0:T(8,128)} reshape(f32[2,4,2,2,256]{4,3,2,1,0:T(2,128)S(1)} %copy.19) | data formatting | bytes 65536 | tf_op jit(solution)/shard_map/reshape | solution.py:499
  (29 shorter events, 0.2 us)
Async XLA Ops:
  0.6 7.8 %copy-start = (bf16[2,1,128,128]{3,2,1,0:T(8,128)(2,1)S(1)}, bf16[2,1,128,128]{3,2,1,0:T(8,128)(2,1)}, u32[]{:S(2)}) copy-start(bf16[2,1,128,128]{3,2,1,0:T(8,128)(2,1)} %refs_7_.1) | copy-start | bytes 196612
  0.6 7.8 %copy-start.5 = (s32[2,2,32]{2,1,0:T(2,128)S(1)}, s32[2,2,32]{2,1,0:T(2,128)}, u32[]{:S(2)}) copy-start(s32[2,2,32]{2,1,0:T(2,128)} %refs_1_.8) | copy-start | bytes 1540
  0.7 7.8 %collective-permute-start.1 = (bf16[2,1,512,1024]{3,2,0,1:T(8,128)(2,1)}, bf16[2,1,512,1024]{3,2,0,1:T(8,128)(2,1)S(1)}, u32[]{:S(2)}, u32[]{:S(2)}) collective-permute-start(bf16[2,1,512,1024]{3,2,0,1:T(8,128)(2,1)} %bitcast.36), channel_id=1, source_target_pairs={{0,2},{2,0},{1,3},{3,1},{4,6},{6,4},{5,7},{7,5},{8,10},{10,8},{9,1... | collective-permute-start | bytes 6291464 | tf_op jit(solution)/shard_map/ppermute | solution.py:456
  1.2 14.9 %collective-permute-start.2 = (bf16[2,1,128,128]{3,2,0,1:T(8,128)(2,1)}, bf16[2,1,128,128]{3,2,0,1:T(8,128)(2,1)S(1)}, u32[]{:S(2)}, u32[]{:S(2)}) collective-permute-start(bf16[2,1,128,128]{3,2,0,1:T(8,128)(2,1)} %bitcast.32), channel_id=1, source_target_pairs={{0,8},{8,0},{16,24},{24,16},{1,9},{9,1},{17,25},{25,17},{2,10},{10... | collective-permute-start | bytes 196616 | tf_op jit(solution)/shard_map/ppermute | solution.py:456
  3.8 12.2 %collective-permute-start.3 = (bf16[2,1,128,128]{3,2,0,1:T(8,128)(2,1)}, bf16[2,1,128,128]{3,2,0,1:T(8,128)(2,1)S(1)}, u32[]{:S(2)}, u32[]{:S(2)}) collective-permute-start(bf16[2,1,128,128]{3,2,0,1:T(8,128)(2,1)} %bitcast.33), channel_id=1, source_target_pairs={{0,16},{8,24},{16,0},{24,8},{1,17},{9,25},{17,1},{25,9},{2,18},{10... | collective-permute-start | bytes 196616 | tf_op jit(solution)/shard_map/ppermute | solution.py:456
  6.4 9.6 %collective-permute-start.4 = (bf16[2,1,128,128]{3,2,0,1:T(8,128)(2,1)}, bf16[2,1,128,128]{3,2,0,1:T(8,128)(2,1)S(1)}, u32[]{:S(2)}, u32[]{:S(2)}) collective-permute-start(bf16[2,1,128,128]{3,2,0,1:T(8,128)(2,1)} %bitcast.34), channel_id=1, source_target_pairs={{0,24},{8,16},{16,8},{24,0},{1,25},{9,17},{17,9},{25,1},{2,26},{10... | collective-permute-start | bytes 196616 | tf_op jit(solution)/shard_map/ppermute | solution.py:456
  6.4 2.0 %collective-permute-start = (s32[2,2,32]{2,1,0:T(2,128)}, s32[2,2,32]{2,1,0:T(2,128)S(1)}, u32[]{:S(2)}, u32[]{:S(2)}) collective-permute-start(s32[2,2,32]{2,1,0:T(2,128)} %refs_1_.8), channel_id=1, source_target_pairs={{0,2},{2,0},{1,3},{3,1},{4,6},{6,4},{5,7},{7,5},{8,10},{10,8},{9,1... | collective-permute-start | bytes 1544 | tf_op jit(solution)/shard_map/ppermute | solution.py:456
  11.3 5.1 %copy-start.1 = (bf16[256,256]{1,0:T(8,128)(2,1)S(1)}, bf16[256,256]{1,0:T(8,128)(2,1)}, u32[]{:S(2)}) copy-start(bf16[256,256]{1,0:T(8,128)(2,1)} %constant.35.clone.refs_4_) | copy-start | bytes 393220
  11.3 5.1 %copy-start.2 = (bf16[256,128]{1,0:T(8,128)(2,1)S(1)}, bf16[256,128]{1,0:T(8,128)(2,1)}, u32[]{:S(2)}) copy-start(bf16[256,128]{1,0:T(8,128)(2,1)} %constant.37.clone.refs_6_) | copy-start | bytes 196612
  11.3 5.1 %copy-start.3 = (bf16[160,128]{1,0:T(8,128)(2,1)S(1)}, bf16[160,128]{1,0:T(8,128)(2,1)}, u32[]{:S(2)}) copy-start(bf16[160,128]{1,0:T(8,128)(2,1)} %constant.34.clone.refs_3_) | copy-start | bytes 122884
  11.4 5.1 %copy-start.4 = (bf16[64,160]{1,0:T(8,128)(2,1)S(1)}, bf16[64,160]{1,0:T(8,128)(2,1)}, u32[]{:S(2)}) copy-start(bf16[64,160]{1,0:T(8,128)(2,1)} %constant.36.clone.refs_5_) | copy-start | bytes 61444
  11.4 9.2 %collective-permute-start.6 = (bf16[8,128,128]{2,1,0:T(8,128)(2,1)S(1)}, bf16[8,128,128]{2,1,0:T(8,128)(2,1)S(1)}, u32[]{:S(2)}, u32[]{:S(2)}) collective-permute-start(bf16[8,128,128]{2,1,0:T(8,128)(2,1)S(1)} %warp.2.refs_7_), channel_id=1, source_target_pairs={{0,4},{4,0},{1,5},{5,1},{2,6},{6,2},{3,7},{7,3},{8,12},{12,8},{9,1... | collective-permute-start | bytes 786440 | tf_op jit(solution)/shard_map/ppermute | solution.py:456
  16.1 9.7 %collective-permute-start.5 = (bf16[8,128,128]{2,1,0:T(8,128)(2,1)S(1)}, bf16[8,128,128]{2,1,0:T(8,128)(2,1)S(1)}, u32[]{:S(2)}, u32[]{:S(2)}) collective-permute-start(bf16[8,128,128]{2,1,0:T(8,128)(2,1)S(1)} %pad_maximum_fusion.refs_9_), channel_id=1, source_target_pairs={{0,4},{4,0},{1,5},{5,1},{2,6},{6,2},{3,7},{7,3},{8,12},{12,8},{9,1... | collective-permute-start | bytes 786440 | tf_op jit(solution)/shard_map/ppermute | solution.py:456
  20.6 9.8 %collective-permute-start.7 = (bf16[2,128,128]{2,1,0:T(8,128)(2,1)S(1)}, bf16[2,128,128]{2,1,0:T(8,128)(2,1)S(1)}, u32[]{:S(2)}, u32[]{:S(2)}) collective-permute-start(bf16[2,128,128]{2,1,0:T(8,128)(2,1)S(1)} %get-tuple-element.52), channel_id=1, source_target_pairs={{0,24},{8,16},{16,8},{24,0},{1,25},{9,17},{17,9},{25,1},{2,26},{10... | collective-permute-start | bytes 196616 | tf_op jit(solution)/shard_map/ppermute | solution.py:456
  24.5 5.9 %collective-permute-start.8 = (bf16[2,128,128]{2,1,0:T(8,128)(2,1)S(1)}, bf16[2,128,128]{2,1,0:T(8,128)(2,1)S(1)}, u32[]{:S(2)}, u32[]{:S(2)}) collective-permute-start(bf16[2,128,128]{2,1,0:T(8,128)(2,1)S(1)} %get-tuple-element.51), channel_id=1, source_target_pairs={{0,8},{8,0},{16,24},{24,16},{1,9},{9,1},{17,25},{25,17},{2,10},{10... | collective-permute-start | bytes 196616 | tf_op jit(solution)/shard_map/ppermute | solution.py:456
  24.5 5.9 %collective-permute-start.9 = (bf16[2,128,128]{2,1,0:T(8,128)(2,1)S(1)}, bf16[2,128,128]{2,1,0:T(8,128)(2,1)S(1)}, u32[]{:S(2)}, u32[]{:S(2)}) collective-permute-start(bf16[2,128,128]{2,1,0:T(8,128)(2,1)S(1)} %get-tuple-element.50), channel_id=1, source_target_pairs={{0,16},{8,24},{16,0},{24,8},{1,17},{9,25},{17,1},{25,9},{2,18},{10... | collective-permute-start | bytes 196616 | tf_op jit(solution)/shard_map/ppermute | solution.py:456
  28.6 3.8 %collective-permute-start.10 = (bf16[2,2,8,256]{3,2,1,0:T(8,128)(2,1)S(1)}, bf16[2,2,8,256]{3,2,1,0:T(8,128)(2,1)S(1)}, u32[]{:S(2)}, u32[]{:S(2)}) collective-permute-start(bf16[2,2,8,256]{3,2,1,0:T(8,128)(2,1)S(1)} %get-tuple-element.44), channel_id=1, source_target_pairs={{0,1},{1,0},{2,3},{3,2},{4,5},{5,4},{6,7},{7,6},{8,9},{9,8},{10,11... | collective-permute-start | bytes 49160 | tf_op jit(solution)/shard_map/ppermute | solution.py:456
  32.4 1.2 %collective-permute-start.11 = (bf16[2,8,256]{2,1,0:T(8,128)(2,1)S(1)}, bf16[2,8,256]{2,1,0:T(8,128)(2,1)S(1)}, u32[]{:S(2)}, u32[]{:S(2)}) collective-permute-start(bf16[2,8,256]{2,1,0:T(8,128)(2,1)S(1)} %fusion), channel_id=1, source_target_pairs={{0,2},{2,0},{1,3},{3,1},{4,6},{6,4},{5,7},{7,5},{8,10},{10,8},{9,1... | collective-permute-start | bytes 24584 | tf_op jit(solution)/shard_map/ppermute | solution.py:456

commit v23 on v22

--- a/solution.py
+++ b/solution.py
@@ -338,14 +338,16 @@
                         total += magnitude
                     sums[one] = jnp.sum(total + total - once, axis=0, keepdims=True)
 
-        means = jnp.sum(sums[...], axis=2, keepdims=True) * (1.0 / (block * block)) + 1e-06
         lag_sums = []
         for pair in range(local // 2):
+            first = 2 * pair * many
+            magnitudes = jnp.sum(sums[first : first + 2 * many], axis=2, keepdims=True)
+            means = magnitudes * (1.0 / (block * block)) + 1e-06
             for order in range(many):
                 norms = []
                 for side in range(2):
                     one = (2 * pair + side) * many + order
-                    scale = pl.reciprocal(cross[one, 2 * kept :, :] + means[one], approx=True)
+                    scale = pl.reciprocal(cross[one, 2 * kept :, :] + means[one - first], approx=True)
                     norms.append(
                         jnp.concatenate(
                             [

time: 34.6 us -> 34.5 us (level)
  no operation moved by 1% of the time
where the time goes in v23:
time: 34.5 us; the launch traced here: 34.4 us
  starting transfers between devices  14.3 us (41%)
  Pallas kernels  13.7 us (40%)
  waiting for transfers between devices  4 us (12%)
  other arithmetic  0.9 us (3%)
  between operations  0.81 us (2%)
  local copies, waits for them, and re-layouts  0.72 us (2%)
    ppermute x12, starting transfers between devices, exchange(): return lax.ppermute(value, axes, [(at, at ^ turn) for at in range(size)])  14.3 us
    pallas_call x2, Pallas kernels, lag_windows(): pl.pallas_call(functools.partial(spectrum_kernel, vols, across, block, ow...  6.06 us
    pallas_call x2, Pallas kernels, warp_sums(): pl.pallas_call(functools.partial(warp_kernel, down, across, block, own, o...  5.68 us
    ppermute x12, waiting for transfers between devices, exchange(): return lax.ppermute(value, axes, [(at, at ^ turn) for at in range(size)])  4 us
    pallas_call x1, Pallas kernels, stage(): pl.pallas_call(functools.partial(stage_kernel, count), out_shape=[jax.Sha...  1.93 us
    unnamed x1, other arithmetic  0.7 us
  transfers between devices with their start and end apart: 12, of which 4 were waited for; matrix products, arithmetic and copies ran while one was open for 3% of the time, Pallas kernels for 40%

profile of v23, /device:TPU:0, one launch (start us, length us, event | category | flops | bytes accessed | tf_op | source)
XLA Modules:
  0.0 34.4 jit_solution(12724526121229078875)
XLA Ops:
  0.6 0.0 copy-start
  0.7 0.5 %collective-permute-start.1 = (bf16[2,1,512,1024]{3,2,0,1:T(8,128)(2,1)}, bf16[2,1,512,1024]{3,2,0,1:T(8,128)(2,1)S(1)}, u32[]{:S(2)}, u32[]{:S(2)}) collective-permute-start(bf16[2,1,512,1024]{3,2,0,1:T(8,128)(2,1)} %bitcast.36), channel_id=1, source_target_pairs={{0,2},{2,0},{1,3},{3,1},{4,6},{6,4},{5,7},{7,5},{8,10},{10,8},{9,1... | collective-permute-start | bytes 6291464 | tf_op jit(solution)/shard_map/ppermute | solution.py:458
  1.2 2.7 %collective-permute-start.2 = (bf16[2,1,128,128]{3,2,0,1:T(8,128)(2,1)}, bf16[2,1,128,128]{3,2,0,1:T(8,128)(2,1)S(1)}, u32[]{:S(2)}, u32[]{:S(2)}) collective-permute-start(bf16[2,1,128,128]{3,2,0,1:T(8,128)(2,1)} %bitcast.32), channel_id=1, source_target_pairs={{0,8},{8,0},{16,24},{24,16},{1,9},{9,1},{17,25},{25,17},{2,10},{10... | collective-permute-start | bytes 196616 | tf_op jit(solution)/shard_map/ppermute | solution.py:458
  3.8 2.6 %collective-permute-start.3 = (bf16[2,1,128,128]{3,2,0,1:T(8,128)(2,1)}, bf16[2,1,128,128]{3,2,0,1:T(8,128)(2,1)S(1)}, u32[]{:S(2)}, u32[]{:S(2)}) collective-permute-start(bf16[2,1,128,128]{3,2,0,1:T(8,128)(2,1)} %bitcast.33), channel_id=1, source_target_pairs={{0,16},{8,24},{16,0},{24,8},{1,17},{9,25},{17,1},{25,9},{2,18},{10... | collective-permute-start | bytes 196616 | tf_op jit(solution)/shard_map/ppermute | solution.py:458
  6.4 0.1 pad_add_fusion.refs_0_
  6.5 1.9 %stage.1 = (f32[16,176,128]{2,1,0:T(8,128)S(1)}, f32[16,64,128]{2,1,0:T(8,128)S(1)}, bf16[2,1,512,1024]{3,2,1,0:T(8,128)(2,1)S(1)}) custom-call(bf16[16,176,128]{2,1,0:T(8,128)(2,1)} %constant.32.clone.refs_0_, bf16[16,64,128]{2,1,0:T(8,128)(2,1)} %constant.33.clone.refs_1_, bf16[2,1,512,1024]{3,2,1,0:T(8,128)(2,1)} %refs_2_.1, bf16[2,1,128,128]{3,2,1,0:T(8,128)(2,1)} %refs_7_.1), custom_call_target="tpu_custom_call" | custom-call | bytes 4194304 | tf_op jit(solution)/shard_map/stage/pallas_call | solution.py:113
  8.5 2.8 %warp.2.refs_7_ = bf16[8,128,128]{2,1,0:T(8,128)(2,1)S(1)} custom-call(s32[4]{0:T(128)S(1)} %pad_add_fusion.refs_0_, s32[2,2,32]{2,1,0:T(2,128)S(1)} %copy-done.5, s32[2,2,32]{2,1,0:T(2,128)S(1)} %collective-permute-done.refs_2_, bf16[2,512,1024]{2,1,0:T(8,128)(2,1)S(1)} %bitcast.28, bf16[2,512,1024]{2,1,0:T(8,128)(2,1)S(1)} %bitcast.24, ...), custom_call_target="tpu_custom_call" | custom-call | flops 2147483648 | bytes 4718592 | tf_op jit(solution)/shard_map/warp/pallas_call | solution.py:232
  11.3 0.0 copy-start.3
  11.4 1.8 %collective-permute-start.6 = (bf16[8,128,128]{2,1,0:T(8,128)(2,1)S(1)}, bf16[8,128,128]{2,1,0:T(8,128)(2,1)S(1)}, u32[]{:S(2)}, u32[]{:S(2)}) collective-permute-start(bf16[8,128,128]{2,1,0:T(8,128)(2,1)S(1)} %warp.2.refs_7_), channel_id=1, source_target_pairs={{0,4},{4,0},{1,5},{5,1},{2,6},{6,2},{3,7},{7,3},{8,12},{12,8},{9,1... | collective-permute-start | bytes 786440 | tf_op jit(solution)/shard_map/ppermute | solution.py:458
  13.2 2.8 %warp.3 = (bf16[2,128,128]{2,1,0:T(8,128)(2,1)S(1)}, bf16[2,128,128]{2,1,0:T(8,128)(2,1)S(1)}, bf16[2,128,128]{2,1,0:T(8,128)(2,1)S(1)}, bf16[2,128,128]{2,1,0:T(8,128)(2,1)S(1)}) custom-call(s32[4]{0:T(128)S(1)} %pad_add_fusion.refs_0_, s32[2,2,32]{2,1,0:T(2,128)S(1)} %copy-done.5, s32[2,2,32]{2,1,0:T(2,128)S(1)} %collective-permute-done.refs_2_, ...), custom_call_target="tpu_custom_call" | custom-call | flops 2147483648 | bytes 4718592 | tf_op jit(solution)/shard_map/warp/pallas_call | solution.py:232
  16.1 0.3 collective-permute-start.5
  16.4 3.2 %lag_windows.2 = (f32[4,272,128]{2,1,0:T(8,128)S(1)}, f32[2,640,256]{2,1,0:T(8,128)S(1)}) custom-call(s32[4]{0:T(128)S(1)} %pad_add_fusion.refs_0_, s32[2,2,32]{2,1,0:T(2,128)S(1)} %copy-done.5, s32[2,2,32]{2,1,0:T(2,128)S(1)} %collective-permute-done.refs_2_, bf16[160,128]{1,0:T(8,128)(2,1)S(1)} %copy-done.3, bf16[256,256]{1,0:T(8,128)(2,1)S(1)} %copy-done.1, ...), custom_call_target="tpu_custom_call" | custom-call | flops 3221225472 | bytes 4718592 | tf_op jit(solution)/shard_map/lag_windows/pallas_call | solution.py:437
  19.7 0.9 %collective-permute-done.6 = bf16[8,128,128]{2,1,0:T(8,128)(2,1)S(1)} collective-permute-done((bf16[8,128,128]{2,1,0:T(8,128)(2,1)S(1)}, bf16[8,128,128]{2,1,0:T(8,128)(2,1)S(1)}, u32[]{:S(2)}, u32[]{:S(2)}) %collective-permute-start.6) | collective-permute-done | bytes 262176 | tf_op jit(solution)/shard_map/ppermute | solution.py:458
  20.5 0.1 add_convert_fusion
  20.6 3.9 %collective-permute-start.7 = (bf16[2,128,128]{2,1,0:T(8,128)(2,1)S(1)}, bf16[2,128,128]{2,1,0:T(8,128)(2,1)S(1)}, u32[]{:S(2)}, u32[]{:S(2)}) collective-permute-start(bf16[2,128,128]{2,1,0:T(8,128)(2,1)S(1)} %get-tuple-element.52), channel_id=1, source_target_pairs={{0,24},{8,16},{16,8},{24,0},{1,25},{9,17},{17,9},{25,1},{2,26},{10... | collective-permute-start | bytes 196616 | tf_op jit(solution)/shard_map/ppermute | solution.py:458
  24.5 0.6 %collective-permute-start.9 = (bf16[2,128,128]{2,1,0:T(8,128)(2,1)S(1)}, bf16[2,128,128]{2,1,0:T(8,128)(2,1)S(1)}, u32[]{:S(2)}, u32[]{:S(2)}) collective-permute-start(bf16[2,128,128]{2,1,0:T(8,128)(2,1)S(1)} %get-tuple-element.50), channel_id=1, source_target_pairs={{0,16},{8,24},{16,0},{24,8},{1,17},{9,25},{17,1},{25,9},{2,18},{10... | collective-permute-start | bytes 196616 | tf_op jit(solution)/shard_map/ppermute | solution.py:458
  25.1 0.6 %collective-permute-done.5.refs_9_ = bf16[8,128,128]{2,1,0:T(8,128)(2,1)S(1)} collective-permute-done((bf16[8,128,128]{2,1,0:T(8,128)(2,1)S(1)}, bf16[8,128,128]{2,1,0:T(8,128)(2,1)S(1)}, u32[]{:S(2)}, u32[]{:S(2)}) %collective-permute-start.5) | collective-permute-done | bytes 262176 | tf_op jit(solution)/shard_map/ppermute | solution.py:458
  25.8 2.8 %lag_windows.3 = (f32[2,2,8,256]{3,2,1,0:T(8,128)S(1)}, bf16[2,2,8,256]{3,2,1,0:T(8,128)(2,1)S(1)}) custom-call(s32[4]{0:T(128)S(1)} %pad_add_fusion.refs_0_, s32[2,2,32]{2,1,0:T(2,128)S(1)} %copy-done.5, s32[2,2,32]{2,1,0:T(2,128)S(1)} %collective-permute-done.refs_2_, bf16[160,128]{1,0:T(8,128)(2,1)S(1)} %copy-done.3, bf16[256,256]{1,0:T(8,128)(2,1)S(1)} %copy-done.1, ...), custom_call_target="tpu_custom_call" | custom-call | flops 805306368 | bytes 4718592 | tf_op jit(solution)/shard_map/lag_windows/pallas_call | solution.py:437
  28.6 1.8 %collective-permute-start.10 = (bf16[2,2,8,256]{3,2,1,0:T(8,128)(2,1)S(1)}, bf16[2,2,8,256]{3,2,1,0:T(8,128)(2,1)S(1)}, u32[]{:S(2)}, u32[]{:S(2)}) collective-permute-start(bf16[2,2,8,256]{3,2,1,0:T(8,128)(2,1)S(1)} %get-tuple-element.44), channel_id=1, source_target_pairs={{0,1},{1,0},{2,3},{3,2},{4,5},{5,4},{6,7},{7,6},{8,9},{9,8},{10,11... | collective-permute-start | bytes 49160 | tf_op jit(solution)/shard_map/ppermute | solution.py:458
  30.4 2.0 %collective-permute-done.10 = bf16[2,2,8,256]{3,2,1,0:T(8,128)(2,1)S(1)} collective-permute-done((bf16[2,2,8,256]{3,2,1,0:T(8,128)(2,1)S(1)}, bf16[2,2,8,256]{3,2,1,0:T(8,128)(2,1)S(1)}, u32[]{:S(2)}, u32[]{:S(2)}) %collective-permute-start.10) | collective-permute-done | bytes 16416 | tf_op jit(solution)/shard_map/ppermute | solution.py:458
  32.4 0.1 collective-permute-start.11
  32.5 0.7 %multiply_bitcast_fusion = f32[2,1,128,128]{3,2,1,0:T(8,128)} fusion(bf16[2,128,128]{2,1,0:T(8,128)(2,1)S(1)} %collective-permute-done.9, bf16[2,128,128]{2,1,0:T(8,128)(2,1)S(1)} %collective-permute-done.8, bf16[2,128,128]{2,1,0:T(8,128)(2,1)S(1)} %collective-permute-done.7, bf16[2,128,128]{2,1,0:T(8,128)(2,1)S(1)} %get-tuple-element.36.refs_10_, ...), kind=kLoop, calls=%fused_computation.1 | loop fusion | flops 327680 | bytes 458752
  33.2 0.5 %collective-permute-done.11 = bf16[2,8,256]{2,1,0:T(8,128)(2,1)S(1)} collective-permute-done((bf16[2,8,256]{2,1,0:T(8,128)(2,1)S(1)}, bf16[2,8,256]{2,1,0:T(8,128)(2,1)S(1)}, u32[]{:S(2)}, u32[]{:S(2)}) %collective-permute-start.11) | collective-permute-done | bytes 8224 | tf_op jit(solution)/shard_map/ppermute | solution.py:458
  33.7 0.6 %reshape.16 = f32[2,16,256]{2,1,0:T(8,128)} reshape(f32[2,4,2,2,256]{4,3,2,1,0:T(2,128)S(1)} %copy.19) | data formatting | bytes 65536 | tf_op jit(solution)/shard_map/reshape | solution.py:501
  (29 shorter events, 0.2 us)
Async XLA Ops:
  0.6 7.8 %copy-start = (bf16[2,1,128,128]{3,2,1,0:T(8,128)(2,1)S(1)}, bf16[2,1,128,128]{3,2,1,0:T(8,128)(2,1)}, u32[]{:S(2)}) copy-start(bf16[2,1,128,128]{3,2,1,0:T(8,128)(2,1)} %refs_7_.1) | copy-start | bytes 196612
  0.6 7.8 %copy-start.5 = (s32[2,2,32]{2,1,0:T(2,128)S(1)}, s32[2,2,32]{2,1,0:T(2,128)}, u32[]{:S(2)}) copy-start(s32[2,2,32]{2,1,0:T(2,128)} %refs_1_.8) | copy-start | bytes 1540
  0.7 7.8 %collective-permute-start.1 = (bf16[2,1,512,1024]{3,2,0,1:T(8,128)(2,1)}, bf16[2,1,512,1024]{3,2,0,1:T(8,128)(2,1)S(1)}, u32[]{:S(2)}, u32[]{:S(2)}) collective-permute-start(bf16[2,1,512,1024]{3,2,0,1:T(8,128)(2,1)} %bitcast.36), channel_id=1, source_target_pairs={{0,2},{2,0},{1,3},{3,1},{4,6},{6,4},{5,7},{7,5},{8,10},{10,8},{9,1... | collective-permute-start | bytes 6291464 | tf_op jit(solution)/shard_map/ppermute | solution.py:458
  1.2 14.8 %collective-permute-start.2 = (bf16[2,1,128,128]{3,2,0,1:T(8,128)(2,1)}, bf16[2,1,128,128]{3,2,0,1:T(8,128)(2,1)S(1)}, u32[]{:S(2)}, u32[]{:S(2)}) collective-permute-start(bf16[2,1,128,128]{3,2,0,1:T(8,128)(2,1)} %bitcast.32), channel_id=1, source_target_pairs={{0,8},{8,0},{16,24},{24,16},{1,9},{9,1},{17,25},{25,17},{2,10},{10... | collective-permute-start | bytes 196616 | tf_op jit(solution)/shard_map/ppermute | solution.py:458
  3.8 12.2 %collective-permute-start.3 = (bf16[2,1,128,128]{3,2,0,1:T(8,128)(2,1)}, bf16[2,1,128,128]{3,2,0,1:T(8,128)(2,1)S(1)}, u32[]{:S(2)}, u32[]{:S(2)}) collective-permute-start(bf16[2,1,128,128]{3,2,0,1:T(8,128)(2,1)} %bitcast.33), channel_id=1, source_target_pairs={{0,16},{8,24},{16,0},{24,8},{1,17},{9,25},{17,1},{25,9},{2,18},{10... | collective-permute-start | bytes 196616 | tf_op jit(solution)/shard_map/ppermute | solution.py:458
  6.4 9.6 %collective-permute-start.4 = (bf16[2,1,128,128]{3,2,0,1:T(8,128)(2,1)}, bf16[2,1,128,128]{3,2,0,1:T(8,128)(2,1)S(1)}, u32[]{:S(2)}, u32[]{:S(2)}) collective-permute-start(bf16[2,1,128,128]{3,2,0,1:T(8,128)(2,1)} %bitcast.34), channel_id=1, source_target_pairs={{0,24},{8,16},{16,8},{24,0},{1,25},{9,17},{17,9},{25,1},{2,26},{10... | collective-permute-start | bytes 196616 | tf_op jit(solution)/shard_map/ppermute | solution.py:458
  6.4 2.0 %collective-permute-start = (s32[2,2,32]{2,1,0:T(2,128)}, s32[2,2,32]{2,1,0:T(2,128)S(1)}, u32[]{:S(2)}, u32[]{:S(2)}) collective-permute-start(s32[2,2,32]{2,1,0:T(2,128)} %refs_1_.8), channel_id=1, source_target_pairs={{0,2},{2,0},{1,3},{3,1},{4,6},{6,4},{5,7},{7,5},{8,10},{10,8},{9,1... | collective-permute-start | bytes 1544 | tf_op jit(solution)/shard_map/ppermute | solution.py:458
  11.3 5.1 %copy-start.1 = (bf16[256,256]{1,0:T(8,128)(2,1)S(1)}, bf16[256,256]{1,0:T(8,128)(2,1)}, u32[]{:S(2)}) copy-start(bf16[256,256]{1,0:T(8,128)(2,1)} %constant.35.clone.refs_4_) | copy-start | bytes 393220
  11.3 5.1 %copy-start.2 = (bf16[256,128]{1,0:T(8,128)(2,1)S(1)}, bf16[256,128]{1,0:T(8,128)(2,1)}, u32[]{:S(2)}) copy-start(bf16[256,128]{1,0:T(8,128)(2,1)} %constant.37.clone.refs_6_) | copy-start | bytes 196612
  11.3 5.1 %copy-start.3 = (bf16[160,128]{1,0:T(8,128)(2,1)S(1)}, bf16[160,128]{1,0:T(8,128)(2,1)}, u32[]{:S(2)}) copy-start(bf16[160,128]{1,0:T(8,128)(2,1)} %constant.34.clone.refs_3_) | copy-start | bytes 122884
  11.4 5.1 %copy-start.4 = (bf16[64,160]{1,0:T(8,128)(2,1)S(1)}, bf16[64,160]{1,0:T(8,128)(2,1)}, u32[]{:S(2)}) copy-start(bf16[64,160]{1,0:T(8,128)(2,1)} %constant.36.clone.refs_5_) | copy-start | bytes 61444
  11.4 9.2 %collective-permute-start.6 = (bf16[8,128,128]{2,1,0:T(8,128)(2,1)S(1)}, bf16[8,128,128]{2,1,0:T(8,128)(2,1)S(1)}, u32[]{:S(2)}, u32[]{:S(2)}) collective-permute-start(bf16[8,128,128]{2,1,0:T(8,128)(2,1)S(1)} %warp.2.refs_7_), channel_id=1, source_target_pairs={{0,4},{4,0},{1,5},{5,1},{2,6},{6,2},{3,7},{7,3},{8,12},{12,8},{9,1... | collective-permute-start | bytes 786440 | tf_op jit(solution)/shard_map/ppermute | solution.py:458
  16.1 9.7 %collective-permute-start.5 = (bf16[8,128,128]{2,1,0:T(8,128)(2,1)S(1)}, bf16[8,128,128]{2,1,0:T(8,128)(2,1)S(1)}, u32[]{:S(2)}, u32[]{:S(2)}) collective-permute-start(bf16[8,128,128]{2,1,0:T(8,128)(2,1)S(1)} %pad_maximum_fusion.refs_9_), channel_id=1, source_target_pairs={{0,4},{4,0},{1,5},{5,1},{2,6},{6,2},{3,7},{7,3},{8,12},{12,8},{9,1... | collective-permute-start | bytes 786440 | tf_op jit(solution)/shard_map/ppermute | solution.py:458
  20.6 9.8 %collective-permute-start.7 = (bf16[2,128,128]{2,1,0:T(8,128)(2,1)S(1)}, bf16[2,128,128]{2,1,0:T(8,128)(2,1)S(1)}, u32[]{:S(2)}, u32[]{:S(2)}) collective-permute-start(bf16[2,128,128]{2,1,0:T(8,128)(2,1)S(1)} %get-tuple-element.52), channel_id=1, source_target_pairs={{0,24},{8,16},{16,8},{24,0},{1,25},{9,17},{17,9},{25,1},{2,26},{10... | collective-permute-start | bytes 196616 | tf_op jit(solution)/shard_map/ppermute | solution.py:458
  24.5 5.9 %collective-permute-start.8 = (bf16[2,128,128]{2,1,0:T(8,128)(2,1)S(1)}, bf16[2,128,128]{2,1,0:T(8,128)(2,1)S(1)}, u32[]{:S(2)}, u32[]{:S(2)}) collective-permute-start(bf16[2,128,128]{2,1,0:T(8,128)(2,1)S(1)} %get-tuple-element.51), channel_id=1, source_target_pairs={{0,8},{8,0},{16,24},{24,16},{1,9},{9,1},{17,25},{25,17},{2,10},{10... | collective-permute-start | bytes 196616 | tf_op jit(solution)/shard_map/ppermute | solution.py:458
  24.5 5.9 %collective-permute-start.9 = (bf16[2,128,128]{2,1,0:T(8,128)(2,1)S(1)}, bf16[2,128,128]{2,1,0:T(8,128)(2,1)S(1)}, u32[]{:S(2)}, u32[]{:S(2)}) collective-permute-start(bf16[2,128,128]{2,1,0:T(8,128)(2,1)S(1)} %get-tuple-element.50), channel_id=1, source_target_pairs={{0,16},{8,24},{16,0},{24,8},{1,17},{9,25},{17,1},{25,9},{2,18},{10... | collective-permute-start | bytes 196616 | tf_op jit(solution)/shard_map/ppermute | solution.py:458
  28.6 3.8 %collective-permute-start.10 = (bf16[2,2,8,256]{3,2,1,0:T(8,128)(2,1)S(1)}, bf16[2,2,8,256]{3,2,1,0:T(8,128)(2,1)S(1)}, u32[]{:S(2)}, u32[]{:S(2)}) collective-permute-start(bf16[2,2,8,256]{3,2,1,0:T(8,128)(2,1)S(1)} %get-tuple-element.44), channel_id=1, source_target_pairs={{0,1},{1,0},{2,3},{3,2},{4,5},{5,4},{6,7},{7,6},{8,9},{9,8},{10,11... | collective-permute-start | bytes 49160 | tf_op jit(solution)/shard_map/ppermute | solution.py:458
  32.4 1.2 %collective-permute-start.11 = (bf16[2,8,256]{2,1,0:T(8,128)(2,1)S(1)}, bf16[2,8,256]{2,1,0:T(8,128)(2,1)S(1)}, u32[]{:S(2)}, u32[]{:S(2)}) collective-permute-start(bf16[2,8,256]{2,1,0:T(8,128)(2,1)S(1)} %fusion), channel_id=1, source_target_pairs={{0,2},{2,0},{1,3},{3,1},{4,6},{6,4},{5,7},{7,5},{8,10},{10,8},{9,1... | collective-permute-start | bytes 24584 | tf_op jit(solution)/shard_map/ppermute | solution.py:458

commit v24 on v22

--- a/solution.py
+++ b/solution.py
@@ -301,86 +301,96 @@
             jnp.concatenate(parts, axis=0), col_table, preferred_element_type=jnp.float32
         )
 
-    for half_step in range(depth // 2):
+    def first_pass(half_step, pair):
         cross, sums = all_cross.at[half_step], all_sums.at[half_step]
         places = find_places(half_step, other)
-        for pair in range(local // 2):
-            pair_places = places[2 * pair : 2 * pair + 2]
-            sources = [[template_ref[at] for _, _, _, at in pair_places]]
-            sources += frame_sources(pair_places)
-            if ready and half_step == 0:
-                spectra = jnp.concatenate([transform(sources[:1]), ready[0][pair]], axis=0)
-            else:
-                spectra = transform(sources)
-            temp = spectra[: 2 * half].astype(jnp.bfloat16).astype(jnp.float32)
-            for order in range(many):
-                for side in range(2):
-                    one = (2 * pair + side) * many + order
-                    base = (2 * (order + 1) + side) * half
-                    total = jnp.zeros((8, LANES), jnp.float32)
-                    for row in range(0, kept, 8):
-                        at = side * half + row
-                        temp_real = temp[at : at + 8, :block]
-                        temp_imag = temp[at : at + 8, block:]
-                        real = spectra[base + row : base + row + 8, :block]
-                        imag = spectra[base + row : base + row + 8, block:]
-                        cross_real = real * temp_real + imag * temp_imag
-                        cross_imag = imag * temp_real - real * temp_imag
-                        power = cross_real * cross_real + cross_imag * cross_imag
-                        magnitude = power * lax.rsqrt(jnp.maximum(power, 1e-36))
-                        cross[one, row : row + 8, :] = cross_real
-                        cross[one, kept + row : kept + row + 8, :] = cross_imag
-                        cross[one, 2 * kept + row : 2 * kept + row + 8, :] = magnitude
-                        if row == 0:
-                            once = jnp.where(top, magnitude, 0.0)
-                        elif row == block // 2:
-                            once += magnitude
-                        total += magnitude
-                    sums[one] = jnp.sum(total + total - once, axis=0, keepdims=True)
-
-        means = jnp.sum(sums[...], axis=2, keepdims=True) * (1.0 / (block * block)) + 1e-06
+        pair_places = places[2 * pair : 2 * pair + 2]
+        sources = [[template_ref[at] for _, _, _, at in pair_places]]
+        sources += frame_sources(pair_places)
+        if ready and half_step == 0:
+            spectra = jnp.concatenate([transform(sources[:1]), ready[0][pair]], axis=0)
+        else:
+            spectra = transform(sources)
+        temp = spectra[: 2 * half].astype(jnp.bfloat16).astype(jnp.float32)
+        for order in range(many):
+            for side in range(2):
+                one = (2 * pair + side) * many + order
+                base = (2 * (order + 1) + side) * half
+                total = jnp.zeros((8, LANES), jnp.float32)
+                for row in range(0, kept, 8):
+                    at = side * half + row
+                    temp_real = temp[at : at + 8, :block]
+                    temp_imag = temp[at : at + 8, block:]
+                    real = spectra[base + row : base + row + 8, :block]
+                    imag = spectra[base + row : base + row + 8, block:]
+                    cross_real = real * temp_real + imag * temp_imag
+                    cross_imag = imag * temp_real - real * temp_imag
+                    power = cross_real * cross_real + cross_imag * cross_imag
+                    magnitude = power * lax.rsqrt(jnp.maximum(power, 1e-36))
+                    cross[one, row : row + 8, :] = cross_real
+                    cross[one, kept + row : kept + row + 8, :] = cross_imag
+                    cross[one, 2 * kept + row : 2 * kept + row + 8, :] = magnitude
+                    if row == 0:
+                        once = jnp.where(top, magnitude, 0.0)
+                    elif row == block // 2:
+                        once += magnitude
+                    total += magnitude
+                sums[one] = jnp.sum(total + total - once, axis=0, keepdims=True)
+
+
+    def second_pass(half_step, pair):
+        cross, sums = all_cross.at[half_step], all_sums.at[half_step]
+        places = find_places(half_step, other)
         lag_sums = []
-        for pair in range(local // 2):
-            for order in range(many):
-                norms = []
-                for side in range(2):
-                    one = (2 * pair + side) * many + order
-                    scale = pl.reciprocal(cross[one, 2 * kept :, :] + means[one], approx=True)
-                    norms.append(
-                        jnp.concatenate(
-                            [
-                                cross[one, :kept, :] * scale,
-                                no_rows,
-                                cross[one, kept : 2 * kept, :] * scale,
-                                no_rows,
-                            ],
-                            axis=0,
-                        ).astype(jnp.bfloat16)
-                    )
-                lag_rows = jnp.dot(
-                    lag_table, jnp.concatenate(norms, axis=1), preferred_element_type=jnp.float32
-                ).astype(jnp.bfloat16)
-                for side in range(2):
-                    lanes = slice(side * block, (side + 1) * block)
-                    lag_sums.append(
-                        jnp.concatenate([lag_rows[:span, lanes], lag_rows[span:, lanes]], axis=1)
-                    )
+        first = 2 * pair * many
+        magnitudes = jnp.sum(sums[first : first + 2 * many], axis=2, keepdims=True)
+        means = magnitudes * (1.0 / (block * block)) + 1e-06
+        for order in range(many):
+            norms = []
+            for side in range(2):
+                one = (2 * pair + side) * many + order
+                scale = pl.reciprocal(cross[one, 2 * kept :, :] + means[one - first], approx=True)
+                norms.append(
+                    jnp.concatenate(
+                        [
+                            cross[one, :kept, :] * scale,
+                            no_rows,
+                            cross[one, kept : 2 * kept, :] * scale,
+                            no_rows,
+                        ],
+                        axis=0,
+                    ).astype(jnp.bfloat16)
+                )
+            lag_rows = jnp.dot(
+                lag_table, jnp.concatenate(norms, axis=1), preferred_element_type=jnp.float32
+            ).astype(jnp.bfloat16)
+            for side in range(2):
+                lanes = slice(side * block, (side + 1) * block)
+                lag_sums.append(
+                    jnp.concatenate([lag_rows[:span, lanes], lag_rows[span:, lanes]], axis=1)
+                )
         lags = jnp.dot(
             jnp.concatenate(lag_sums, axis=0), span_ref[...], preferred_element_type=jnp.float32
         )
-        for pair in range(local // 2):
-            for order, (codes, _, v) in enumerate(volumes):
-                for side in range(2):
-                    index = places[2 * pair + side][0]
-                    row_shift = codes[v, 0, index] >> 4
-                    col_shift = codes[v, 1, index] >> 4
-                    at = (pair * many + order) * 2 + side
-                    one = lags[at * span : (at + 1) * span]
-                    one = pltpu.roll(one, span - SHIFT - row_shift, 0)[:WIN]
-                    at = index // (2 * own) * own + (2 * pair + side) % own
-                    found[order, pl.ds(pl.multiple_of(at * WIN, WIN), WIN), :] = pltpu.roll(
-                        one, LANES - SHIFT - col_shift, 1
-                    )
+        for order, (codes, _, v) in enumerate(volumes):
+            for side in range(2):
+                index = places[2 * pair + side][0]
+                row_shift = codes[v, 0, index] >> 4
+                col_shift = codes[v, 1, index] >> 4
+                at = order * 2 + side
+                one = lags[at * span : (at + 1) * span]
+                one = pltpu.roll(one, span - SHIFT - row_shift, 0)[:WIN]
+                at = index // (2 * own) * own + (2 * pair + side) % own
+                found[order, pl.ds(pl.multiple_of(at * WIN, WIN), WIN), :] = pltpu.roll(
+                    one, LANES - SHIFT - col_shift, 1
+                )
+
+    units = [(at, pair) for at in range(depth // 2) for pair in range(local // 2)]
+    first_pass(*units[0])
+    for before, unit in zip(units, units[1:]):
+        first_pass(*unit)
+        second_pass(*before)
+    second_pass(*units[-1])
 
     if not other:
         places = find_places(0, 1)

time: 34.6 us -> 34.7 us (level)
  no operation moved by 1% of the time
where the time goes in v24:
time: 34.7 us; the launch traced here: 34.5 us
  starting transfers between devices  14.3 us (41%)
  Pallas kernels  13.7 us (39%)
  waiting for transfers between devices  4.08 us (12%)
  other arithmetic  0.9 us (3%)
  between operations  0.81 us (2%)
  local copies, waits for them, and re-layouts  0.72 us (2%)
    ppermute x12, starting transfers between devices, exchange(): return lax.ppermute(value, axes, [(at, at ^ turn) for at in range(size)])  14.3 us
    pallas_call x2, Pallas kernels, lag_windows(): pl.pallas_call(functools.partial(spectrum_kernel, vols, across, block, ow...  6.09 us
    pallas_call x2, Pallas kernels, warp_sums(): pl.pallas_call(functools.partial(warp_kernel, down, across, block, own, o...  5.68 us
    ppermute x12, waiting for transfers between devices, exchange(): return lax.ppermute(value, axes, [(at, at ^ turn) for at in range(size)])  4.08 us
    pallas_call x1, Pallas kernels, stage(): pl.pallas_call(functools.partial(stage_kernel, count), out_shape=[jax.Sha...  1.93 us
    unnamed x1, other arithmetic  0.7 us
  transfers between devices with their start and end apart: 12, of which 4 were waited for; matrix products, arithmetic and copies ran while one was open for 3% of the time, Pallas kernels for 40%

profile of v24, /device:TPU:0, one launch (start us, length us, event | category | flops | bytes accessed | tf_op | source)
XLA Modules:
  0.0 34.5 jit_solution(11491112128819289636)
XLA Ops:
  0.7 0.5 %collective-permute-start.1 = (bf16[2,1,512,1024]{3,2,0,1:T(8,128)(2,1)}, bf16[2,1,512,1024]{3,2,0,1:T(8,128)(2,1)S(1)}, u32[]{:S(2)}, u32[]{:S(2)}) collective-permute-start(bf16[2,1,512,1024]{3,2,0,1:T(8,128)(2,1)} %bitcast.36), channel_id=1, source_target_pairs={{0,2},{2,0},{1,3},{3,1},{4,6},{6,4},{5,7},{7,5},{8,10},{10,8},{9,1... | collective-permute-start | bytes 6291464 | tf_op jit(solution)/shard_map/ppermute | solution.py:466
  1.2 2.7 %collective-permute-start.2 = (bf16[2,1,128,128]{3,2,0,1:T(8,128)(2,1)}, bf16[2,1,128,128]{3,2,0,1:T(8,128)(2,1)S(1)}, u32[]{:S(2)}, u32[]{:S(2)}) collective-permute-start(bf16[2,1,128,128]{3,2,0,1:T(8,128)(2,1)} %bitcast.32), channel_id=1, source_target_pairs={{0,8},{8,0},{16,24},{24,16},{1,9},{9,1},{17,25},{25,17},{2,10},{10... | collective-permute-start | bytes 196616 | tf_op jit(solution)/shard_map/ppermute | solution.py:466
  3.8 2.6 %collective-permute-start.3 = (bf16[2,1,128,128]{3,2,0,1:T(8,128)(2,1)}, bf16[2,1,128,128]{3,2,0,1:T(8,128)(2,1)S(1)}, u32[]{:S(2)}, u32[]{:S(2)}) collective-permute-start(bf16[2,1,128,128]{3,2,0,1:T(8,128)(2,1)} %bitcast.33), channel_id=1, source_target_pairs={{0,16},{8,24},{16,0},{24,8},{1,17},{9,25},{17,1},{25,9},{2,18},{10... | collective-permute-start | bytes 196616 | tf_op jit(solution)/shard_map/ppermute | solution.py:466
  6.4 0.1 pad_add_fusion.refs_0_
  6.5 1.9 %stage.1 = (f32[16,176,128]{2,1,0:T(8,128)S(1)}, f32[16,64,128]{2,1,0:T(8,128)S(1)}, bf16[2,1,512,1024]{3,2,1,0:T(8,128)(2,1)S(1)}) custom-call(bf16[16,176,128]{2,1,0:T(8,128)(2,1)} %constant.32.clone.refs_0_, bf16[16,64,128]{2,1,0:T(8,128)(2,1)} %constant.33.clone.refs_1_, bf16[2,1,512,1024]{3,2,1,0:T(8,128)(2,1)} %refs_2_.1, bf16[2,1,128,128]{3,2,1,0:T(8,128)(2,1)} %refs_7_.1), custom_call_target="tpu_custom_call" | custom-call | bytes 4194304 | tf_op jit(solution)/shard_map/stage/pallas_call | solution.py:113
  8.5 2.8 %warp.2.refs_7_ = bf16[8,128,128]{2,1,0:T(8,128)(2,1)S(1)} custom-call(s32[4]{0:T(128)S(1)} %pad_add_fusion.refs_0_, s32[2,2,32]{2,1,0:T(2,128)S(1)} %copy-done.5, s32[2,2,32]{2,1,0:T(2,128)S(1)} %collective-permute-done.refs_2_, bf16[2,512,1024]{2,1,0:T(8,128)(2,1)S(1)} %bitcast.28, bf16[2,512,1024]{2,1,0:T(8,128)(2,1)S(1)} %bitcast.24, ...), custom_call_target="tpu_custom_call" | custom-call | flops 2147483648 | bytes 4718592 | tf_op jit(solution)/shard_map/warp/pallas_call | solution.py:232
  11.3 0.0 copy-start.2
  11.3 0.0 copy-start.3
  11.4 1.8 %collective-permute-start.6 = (bf16[8,128,128]{2,1,0:T(8,128)(2,1)S(1)}, bf16[8,128,128]{2,1,0:T(8,128)(2,1)S(1)}, u32[]{:S(2)}, u32[]{:S(2)}) collective-permute-start(bf16[8,128,128]{2,1,0:T(8,128)(2,1)S(1)} %warp.2.refs_7_), channel_id=1, source_target_pairs={{0,4},{4,0},{1,5},{5,1},{2,6},{6,2},{3,7},{7,3},{8,12},{12,8},{9,1... | collective-permute-start | bytes 786440 | tf_op jit(solution)/shard_map/ppermute | solution.py:466
  13.2 2.8 %warp.3 = (bf16[2,128,128]{2,1,0:T(8,128)(2,1)S(1)}, bf16[2,128,128]{2,1,0:T(8,128)(2,1)S(1)}, bf16[2,128,128]{2,1,0:T(8,128)(2,1)S(1)}, bf16[2,128,128]{2,1,0:T(8,128)(2,1)S(1)}) custom-call(s32[4]{0:T(128)S(1)} %pad_add_fusion.refs_0_, s32[2,2,32]{2,1,0:T(2,128)S(1)} %copy-done.5, s32[2,2,32]{2,1,0:T(2,128)S(1)} %collective-permute-done.refs_2_, ...), custom_call_target="tpu_custom_call" | custom-call | flops 2147483648 | bytes 4718592 | tf_op jit(solution)/shard_map/warp/pallas_call | solution.py:232
  16.1 0.3 collective-permute-start.5
  16.4 3.1 %lag_windows.2 = (f32[4,272,128]{2,1,0:T(8,128)S(1)}, f32[2,640,256]{2,1,0:T(8,128)S(1)}) custom-call(s32[4]{0:T(128)S(1)} %pad_add_fusion.refs_0_, s32[2,2,32]{2,1,0:T(2,128)S(1)} %copy-done.5, s32[2,2,32]{2,1,0:T(2,128)S(1)} %collective-permute-done.refs_2_, bf16[160,128]{1,0:T(8,128)(2,1)S(1)} %copy-done.3, bf16[256,256]{1,0:T(8,128)(2,1)S(1)} %copy-done.1, ...), custom_call_target="tpu_custom_call" | custom-call | flops 3221225472 | bytes 4718592 | tf_op jit(solution)/shard_map/lag_windows/pallas_call | solution.py:445
  19.6 1.0 %collective-permute-done.6 = bf16[8,128,128]{2,1,0:T(8,128)(2,1)S(1)} collective-permute-done((bf16[8,128,128]{2,1,0:T(8,128)(2,1)S(1)}, bf16[8,128,128]{2,1,0:T(8,128)(2,1)S(1)}, u32[]{:S(2)}, u32[]{:S(2)}) %collective-permute-start.6) | collective-permute-done | bytes 262176 | tf_op jit(solution)/shard_map/ppermute | solution.py:466
  20.5 0.1 add_convert_fusion
  20.6 3.9 %collective-permute-start.7 = (bf16[2,128,128]{2,1,0:T(8,128)(2,1)S(1)}, bf16[2,128,128]{2,1,0:T(8,128)(2,1)S(1)}, u32[]{:S(2)}, u32[]{:S(2)}) collective-permute-start(bf16[2,128,128]{2,1,0:T(8,128)(2,1)S(1)} %get-tuple-element.52), channel_id=1, source_target_pairs={{0,24},{8,16},{16,8},{24,0},{1,25},{9,17},{17,9},{25,1},{2,26},{10... | collective-permute-start | bytes 196616 | tf_op jit(solution)/shard_map/ppermute | solution.py:466
  24.5 0.6 %collective-permute-start.9 = (bf16[2,128,128]{2,1,0:T(8,128)(2,1)S(1)}, bf16[2,128,128]{2,1,0:T(8,128)(2,1)S(1)}, u32[]{:S(2)}, u32[]{:S(2)}) collective-permute-start(bf16[2,128,128]{2,1,0:T(8,128)(2,1)S(1)} %get-tuple-element.50), channel_id=1, source_target_pairs={{0,16},{8,24},{16,0},{24,8},{1,17},{9,25},{17,1},{25,9},{2,18},{10... | collective-permute-start | bytes 196616 | tf_op jit(solution)/shard_map/ppermute | solution.py:466
  25.1 0.6 %collective-permute-done.5.refs_9_ = bf16[8,128,128]{2,1,0:T(8,128)(2,1)S(1)} collective-permute-done((bf16[8,128,128]{2,1,0:T(8,128)(2,1)S(1)}, bf16[8,128,128]{2,1,0:T(8,128)(2,1)S(1)}, u32[]{:S(2)}, u32[]{:S(2)}) %collective-permute-start.5) | collective-permute-done | bytes 262176 | tf_op jit(solution)/shard_map/ppermute | solution.py:466
  25.8 3.0 %lag_windows.3 = (f32[2,2,8,256]{3,2,1,0:T(8,128)S(1)}, bf16[2,2,8,256]{3,2,1,0:T(8,128)(2,1)S(1)}) custom-call(s32[4]{0:T(128)S(1)} %pad_add_fusion.refs_0_, s32[2,2,32]{2,1,0:T(2,128)S(1)} %copy-done.5, s32[2,2,32]{2,1,0:T(2,128)S(1)} %collective-permute-done.refs_2_, bf16[160,128]{1,0:T(8,128)(2,1)S(1)} %copy-done.3, bf16[256,256]{1,0:T(8,128)(2,1)S(1)} %copy-done.1, ...), custom_call_target="tpu_custom_call" | custom-call | flops 805306368 | bytes 4718592 | tf_op jit(solution)/shard_map/lag_windows/pallas_call | solution.py:445
  28.7 1.8 %collective-permute-start.10 = (bf16[2,2,8,256]{3,2,1,0:T(8,128)(2,1)S(1)}, bf16[2,2,8,256]{3,2,1,0:T(8,128)(2,1)S(1)}, u32[]{:S(2)}, u32[]{:S(2)}) collective-permute-start(bf16[2,2,8,256]{3,2,1,0:T(8,128)(2,1)S(1)} %get-tuple-element.44), channel_id=1, source_target_pairs={{0,1},{1,0},{2,3},{3,2},{4,5},{5,4},{6,7},{7,6},{8,9},{9,8},{10,11... | collective-permute-start | bytes 49160 | tf_op jit(solution)/shard_map/ppermute | solution.py:466
  30.5 2.0 %collective-permute-done.10 = bf16[2,2,8,256]{3,2,1,0:T(8,128)(2,1)S(1)} collective-permute-done((bf16[2,2,8,256]{3,2,1,0:T(8,128)(2,1)S(1)}, bf16[2,2,8,256]{3,2,1,0:T(8,128)(2,1)S(1)}, u32[]{:S(2)}, u32[]{:S(2)}) %collective-permute-start.10) | collective-permute-done | bytes 16416 | tf_op jit(solution)/shard_map/ppermute | solution.py:466
  32.6 0.1 collective-permute-start.11
  32.6 0.7 %multiply_bitcast_fusion = f32[2,1,128,128]{3,2,1,0:T(8,128)} fusion(bf16[2,128,128]{2,1,0:T(8,128)(2,1)S(1)} %collective-permute-done.9, bf16[2,128,128]{2,1,0:T(8,128)(2,1)S(1)} %collective-permute-done.8, bf16[2,128,128]{2,1,0:T(8,128)(2,1)S(1)} %collective-permute-done.7, bf16[2,128,128]{2,1,0:T(8,128)(2,1)S(1)} %get-tuple-element.36.refs_10_, ...), kind=kLoop, calls=%fused_computation.1 | loop fusion | flops 327680 | bytes 458752
  33.3 0.5 %collective-permute-done.11 = bf16[2,8,256]{2,1,0:T(8,128)(2,1)S(1)} collective-permute-done((bf16[2,8,256]{2,1,0:T(8,128)(2,1)S(1)}, bf16[2,8,256]{2,1,0:T(8,128)(2,1)S(1)}, u32[]{:S(2)}, u32[]{:S(2)}) %collective-permute-start.11) | collective-permute-done | bytes 8224 | tf_op jit(solution)/shard_map/ppermute | solution.py:466
  33.9 0.6 %reshape.16 = f32[2,16,256]{2,1,0:T(8,128)} reshape(f32[2,4,2,2,256]{4,3,2,1,0:T(2,128)S(1)} %copy.19) | data formatting | bytes 65536 | tf_op jit(solution)/shard_map/reshape | solution.py:509
  (29 shorter events, 0.2 us)
Async XLA Ops:
  0.6 7.8 %copy-start = (bf16[2,1,128,128]{3,2,1,0:T(8,128)(2,1)S(1)}, bf16[2,1,128,128]{3,2,1,0:T(8,128)(2,1)}, u32[]{:S(2)}) copy-start(bf16[2,1,128,128]{3,2,1,0:T(8,128)(2,1)} %refs_7_.1) | copy-start | bytes 196612
  0.6 7.8 %copy-start.5 = (s32[2,2,32]{2,1,0:T(2,128)S(1)}, s32[2,2,32]{2,1,0:T(2,128)}, u32[]{:S(2)}) copy-start(s32[2,2,32]{2,1,0:T(2,128)} %refs_1_.8) | copy-start | bytes 1540
  0.7 7.8 %collective-permute-start.1 = (bf16[2,1,512,1024]{3,2,0,1:T(8,128)(2,1)}, bf16[2,1,512,1024]{3,2,0,1:T(8,128)(2,1)S(1)}, u32[]{:S(2)}, u32[]{:S(2)}) collective-permute-start(bf16[2,1,512,1024]{3,2,0,1:T(8,128)(2,1)} %bitcast.36), channel_id=1, source_target_pairs={{0,2},{2,0},{1,3},{3,1},{4,6},{6,4},{5,7},{7,5},{8,10},{10,8},{9,1... | collective-permute-start | bytes 6291464 | tf_op jit(solution)/shard_map/ppermute | solution.py:466
  1.2 14.9 %collective-permute-start.2 = (bf16[2,1,128,128]{3,2,0,1:T(8,128)(2,1)}, bf16[2,1,128,128]{3,2,0,1:T(8,128)(2,1)S(1)}, u32[]{:S(2)}, u32[]{:S(2)}) collective-permute-start(bf16[2,1,128,128]{3,2,0,1:T(8,128)(2,1)} %bitcast.32), channel_id=1, source_target_pairs={{0,8},{8,0},{16,24},{24,16},{1,9},{9,1},{17,25},{25,17},{2,10},{10... | collective-permute-start | bytes 196616 | tf_op jit(solution)/shard_map/ppermute | solution.py:466
  3.8 12.2 %collective-permute-start.3 = (bf16[2,1,128,128]{3,2,0,1:T(8,128)(2,1)}, bf16[2,1,128,128]{3,2,0,1:T(8,128)(2,1)S(1)}, u32[]{:S(2)}, u32[]{:S(2)}) collective-permute-start(bf16[2,1,128,128]{3,2,0,1:T(8,128)(2,1)} %bitcast.33), channel_id=1, source_target_pairs={{0,16},{8,24},{16,0},{24,8},{1,17},{9,25},{17,1},{25,9},{2,18},{10... | collective-permute-start | bytes 196616 | tf_op jit(solution)/shard_map/ppermute | solution.py:466
  6.4 9.6 %collective-permute-start.4 = (bf16[2,1,128,128]{3,2,0,1:T(8,128)(2,1)}, bf16[2,1,128,128]{3,2,0,1:T(8,128)(2,1)S(1)}, u32[]{:S(2)}, u32[]{:S(2)}) collective-permute-start(bf16[2,1,128,128]{3,2,0,1:T(8,128)(2,1)} %bitcast.34), channel_id=1, source_target_pairs={{0,24},{8,16},{16,8},{24,0},{1,25},{9,17},{17,9},{25,1},{2,26},{10... | collective-permute-start | bytes 196616 | tf_op jit(solution)/shard_map/ppermute | solution.py:466
  6.4 2.0 %collective-permute-start = (s32[2,2,32]{2,1,0:T(2,128)}, s32[2,2,32]{2,1,0:T(2,128)S(1)}, u32[]{:S(2)}, u32[]{:S(2)}) collective-permute-start(s32[2,2,32]{2,1,0:T(2,128)} %refs_1_.8), channel_id=1, source_target_pairs={{0,2},{2,0},{1,3},{3,1},{4,6},{6,4},{5,7},{7,5},{8,10},{10,8},{9,1... | collective-permute-start | bytes 1544 | tf_op jit(solution)/shard_map/ppermute | solution.py:466
  11.3 5.1 %copy-start.1 = (bf16[256,256]{1,0:T(8,128)(2,1)S(1)}, bf16[256,256]{1,0:T(8,128)(2,1)}, u32[]{:S(2)}) copy-start(bf16[256,256]{1,0:T(8,128)(2,1)} %constant.35.clone.refs_4_) | copy-start | bytes 393220
  11.3 5.1 %copy-start.2 = (bf16[256,128]{1,0:T(8,128)(2,1)S(1)}, bf16[256,128]{1,0:T(8,128)(2,1)}, u32[]{:S(2)}) copy-start(bf16[256,128]{1,0:T(8,128)(2,1)} %constant.37.clone.refs_6_) | copy-start | bytes 196612
  11.3 5.1 %copy-start.3 = (bf16[160,128]{1,0:T(8,128)(2,1)S(1)}, bf16[160,128]{1,0:T(8,128)(2,1)}, u32[]{:S(2)}) copy-start(bf16[160,128]{1,0:T(8,128)(2,1)} %constant.34.clone.refs_3_) | copy-start | bytes 122884
  11.3 5.1 %copy-start.4 = (bf16[64,160]{1,0:T(8,128)(2,1)S(1)}, bf16[64,160]{1,0:T(8,128)(2,1)}, u32[]{:S(2)}) copy-start(bf16[64,160]{1,0:T(8,128)(2,1)} %constant.36.clone.refs_5_) | copy-start | bytes 61444
  11.4 9.2 %collective-permute-start.6 = (bf16[8,128,128]{2,1,0:T(8,128)(2,1)S(1)}, bf16[8,128,128]{2,1,0:T(8,128)(2,1)S(1)}, u32[]{:S(2)}, u32[]{:S(2)}) collective-permute-start(bf16[8,128,128]{2,1,0:T(8,128)(2,1)S(1)} %warp.2.refs_7_), channel_id=1, source_target_pairs={{0,4},{4,0},{1,5},{5,1},{2,6},{6,2},{3,7},{7,3},{8,12},{12,8},{9,1... | collective-permute-start | bytes 786440 | tf_op jit(solution)/shard_map/ppermute | solution.py:466
  16.1 9.7 %collective-permute-start.5 = (bf16[8,128,128]{2,1,0:T(8,128)(2,1)S(1)}, bf16[8,128,128]{2,1,0:T(8,128)(2,1)S(1)}, u32[]{:S(2)}, u32[]{:S(2)}) collective-permute-start(bf16[8,128,128]{2,1,0:T(8,128)(2,1)S(1)} %pad_maximum_fusion.refs_9_), channel_id=1, source_target_pairs={{0,4},{4,0},{1,5},{5,1},{2,6},{6,2},{3,7},{7,3},{8,12},{12,8},{9,1... | collective-permute-start | bytes 786440 | tf_op jit(solution)/shard_map/ppermute | solution.py:466
  20.6 9.9 %collective-permute-start.7 = (bf16[2,128,128]{2,1,0:T(8,128)(2,1)S(1)}, bf16[2,128,128]{2,1,0:T(8,128)(2,1)S(1)}, u32[]{:S(2)}, u32[]{:S(2)}) collective-permute-start(bf16[2,128,128]{2,1,0:T(8,128)(2,1)S(1)} %get-tuple-element.52), channel_id=1, source_target_pairs={{0,24},{8,16},{16,8},{24,0},{1,25},{9,17},{17,9},{25,1},{2,26},{10... | collective-permute-start | bytes 196616 | tf_op jit(solution)/shard_map/ppermute | solution.py:466
  24.5 6.0 %collective-permute-start.8 = (bf16[2,128,128]{2,1,0:T(8,128)(2,1)S(1)}, bf16[2,128,128]{2,1,0:T(8,128)(2,1)S(1)}, u32[]{:S(2)}, u32[]{:S(2)}) collective-permute-start(bf16[2,128,128]{2,1,0:T(8,128)(2,1)S(1)} %get-tuple-element.51), channel_id=1, source_target_pairs={{0,8},{8,0},{16,24},{24,16},{1,9},{9,1},{17,25},{25,17},{2,10},{10... | collective-permute-start | bytes 196616 | tf_op jit(solution)/shard_map/ppermute | solution.py:466
  24.5 6.0 %collective-permute-start.9 = (bf16[2,128,128]{2,1,0:T(8,128)(2,1)S(1)}, bf16[2,128,128]{2,1,0:T(8,128)(2,1)S(1)}, u32[]{:S(2)}, u32[]{:S(2)}) collective-permute-start(bf16[2,128,128]{2,1,0:T(8,128)(2,1)S(1)} %get-tuple-element.50), channel_id=1, source_target_pairs={{0,16},{8,24},{16,0},{24,8},{1,17},{9,25},{17,1},{25,9},{2,18},{10... | collective-permute-start | bytes 196616 | tf_op jit(solution)/shard_map/ppermute | solution.py:466
  28.7 3.8 %collective-permute-start.10 = (bf16[2,2,8,256]{3,2,1,0:T(8,128)(2,1)S(1)}, bf16[2,2,8,256]{3,2,1,0:T(8,128)(2,1)S(1)}, u32[]{:S(2)}, u32[]{:S(2)}) collective-permute-start(bf16[2,2,8,256]{3,2,1,0:T(8,128)(2,1)S(1)} %get-tuple-element.44), channel_id=1, source_target_pairs={{0,1},{1,0},{2,3},{3,2},{4,5},{5,4},{6,7},{7,6},{8,9},{9,8},{10,11... | collective-permute-start | bytes 49160 | tf_op jit(solution)/shard_map/ppermute | solution.py:466
  32.6 1.2 %collective-permute-start.11 = (bf16[2,8,256]{2,1,0:T(8,128)(2,1)S(1)}, bf16[2,8,256]{2,1,0:T(8,128)(2,1)S(1)}, u32[]{:S(2)}, u32[]{:S(2)}) collective-permute-start(bf16[2,8,256]{2,1,0:T(8,128)(2,1)S(1)} %fusion), channel_id=1, source_target_pairs={{0,2},{2,0},{1,3},{3,1},{4,6},{6,4},{5,7},{7,5},{8,10},{10,8},{9,1... | collective-permute-start | bytes 24584 | tf_op jit(solution)/shard_map/ppermute | solution.py:466

commit v25 on v24

--- a/solution.py
+++ b/solution.py
@@ -386,11 +386,14 @@
                 )
 
     units = [(at, pair) for at in range(depth // 2) for pair in range(local // 2)]
-    first_pass(*units[0])
-    for before, unit in zip(units, units[1:]):
-        first_pass(*unit)
-        second_pass(*before)
-    second_pass(*units[-1])
+    lead = local // 2 if other else 1
+    for at in range(0, len(units), lead):
+        for unit in units[at : at + lead]:
+            first_pass(*unit)
+        for unit in units[at : at + lead] if other else units[max(at - 1, 0) : at]:
+            second_pass(*unit)
+    if not other:
+        second_pass(*units[-1])
 
     if not other:
         places = find_places(0, 1)

time: 34.7 us -> 34.6 us (level)
  no operation moved by 1% of the time
where the time goes in v25:
time: 34.6 us; the launch traced here: 34.5 us
  starting transfers between devices  14.3 us (41%)
  Pallas kernels  13.6 us (39%)
  waiting for transfers between devices  4.1 us (12%)
  other arithmetic  0.9 us (3%)
  between operations  0.81 us (2%)
  local copies, waits for them, and re-layouts  0.72 us (2%)
    ppermute x12, starting transfers between devices, exchange(): return lax.ppermute(value, axes, [(at, at ^ turn) for at in range(size)])  14.3 us
    pallas_call x2, Pallas kernels, lag_windows(): pl.pallas_call(functools.partial(spectrum_kernel, vols, across, block, ow...  6.04 us
    pallas_call x2, Pallas kernels, warp_sums(): pl.pallas_call(functools.partial(warp_kernel, down, across, block, own, o...  5.67 us
    ppermute x12, waiting for transfers between devices, exchange(): return lax.ppermute(value, axes, [(at, at ^ turn) for at in range(size)])  4.1 us
    pallas_call x1, Pallas kernels, stage(): pl.pallas_call(functools.partial(stage_kernel, count), out_shape=[jax.Sha...  1.93 us
    unnamed x1, other arithmetic  0.7 us
  transfers between devices with their start and end apart: 12, of which 4 were waited for; matrix products, arithmetic and copies ran while one was open for 3% of the time, Pallas kernels for 40%

profile of v25, /device:TPU:0, one launch (start us, length us, event | category | flops | bytes accessed | tf_op | source)
XLA Modules:
  0.0 34.5 jit_solution(18395997985211424251)
XLA Ops:
  0.6 0.0 copy-start
  0.7 0.5 %collective-permute-start.1 = (bf16[2,1,512,1024]{3,2,0,1:T(8,128)(2,1)}, bf16[2,1,512,1024]{3,2,0,1:T(8,128)(2,1)S(1)}, u32[]{:S(2)}, u32[]{:S(2)}) collective-permute-start(bf16[2,1,512,1024]{3,2,0,1:T(8,128)(2,1)} %bitcast.36), channel_id=1, source_target_pairs={{0,2},{2,0},{1,3},{3,1},{4,6},{6,4},{5,7},{7,5},{8,10},{10,8},{9,1... | collective-permute-start | bytes 6291464 | tf_op jit(solution)/shard_map/ppermute | solution.py:469
  1.2 2.7 %collective-permute-start.2 = (bf16[2,1,128,128]{3,2,0,1:T(8,128)(2,1)}, bf16[2,1,128,128]{3,2,0,1:T(8,128)(2,1)S(1)}, u32[]{:S(2)}, u32[]{:S(2)}) collective-permute-start(bf16[2,1,128,128]{3,2,0,1:T(8,128)(2,1)} %bitcast.32), channel_id=1, source_target_pairs={{0,8},{8,0},{16,24},{24,16},{1,9},{9,1},{17,25},{25,17},{2,10},{10... | collective-permute-start | bytes 196616 | tf_op jit(solution)/shard_map/ppermute | solution.py:469
  3.8 2.6 %collective-permute-start.3 = (bf16[2,1,128,128]{3,2,0,1:T(8,128)(2,1)}, bf16[2,1,128,128]{3,2,0,1:T(8,128)(2,1)S(1)}, u32[]{:S(2)}, u32[]{:S(2)}) collective-permute-start(bf16[2,1,128,128]{3,2,0,1:T(8,128)(2,1)} %bitcast.33), channel_id=1, source_target_pairs={{0,16},{8,24},{16,0},{24,8},{1,17},{9,25},{17,1},{25,9},{2,18},{10... | collective-permute-start | bytes 196616 | tf_op jit(solution)/shard_map/ppermute | solution.py:469
  6.4 0.1 pad_add_fusion.refs_0_
  6.5 1.9 %stage.1 = (f32[16,176,128]{2,1,0:T(8,128)S(1)}, f32[16,64,128]{2,1,0:T(8,128)S(1)}, bf16[2,1,512,1024]{3,2,1,0:T(8,128)(2,1)S(1)}) custom-call(bf16[16,176,128]{2,1,0:T(8,128)(2,1)} %constant.32.clone.refs_0_, bf16[16,64,128]{2,1,0:T(8,128)(2,1)} %constant.33.clone.refs_1_, bf16[2,1,512,1024]{3,2,1,0:T(8,128)(2,1)} %refs_2_.1, bf16[2,1,128,128]{3,2,1,0:T(8,128)(2,1)} %refs_7_.1), custom_call_target="tpu_custom_call" | custom-call | bytes 4194304 | tf_op jit(solution)/shard_map/stage/pallas_call | solution.py:113
  8.5 2.8 %warp.2.refs_7_ = bf16[8,128,128]{2,1,0:T(8,128)(2,1)S(1)} custom-call(s32[4]{0:T(128)S(1)} %pad_add_fusion.refs_0_, s32[2,2,32]{2,1,0:T(2,128)S(1)} %copy-done.5, s32[2,2,32]{2,1,0:T(2,128)S(1)} %collective-permute-done.refs_2_, bf16[2,512,1024]{2,1,0:T(8,128)(2,1)S(1)} %bitcast.28, bf16[2,512,1024]{2,1,0:T(8,128)(2,1)S(1)} %bitcast.24, ...), custom_call_target="tpu_custom_call" | custom-call | flops 2147483648 | bytes 4718592 | tf_op jit(solution)/shard_map/warp/pallas_call | solution.py:232
  11.3 0.0 copy-start.2
  11.4 1.8 %collective-permute-start.6 = (bf16[8,128,128]{2,1,0:T(8,128)(2,1)S(1)}, bf16[8,128,128]{2,1,0:T(8,128)(2,1)S(1)}, u32[]{:S(2)}, u32[]{:S(2)}) collective-permute-start(bf16[8,128,128]{2,1,0:T(8,128)(2,1)S(1)} %warp.2.refs_7_), channel_id=1, source_target_pairs={{0,4},{4,0},{1,5},{5,1},{2,6},{6,2},{3,7},{7,3},{8,12},{12,8},{9,1... | collective-permute-start | bytes 786440 | tf_op jit(solution)/shard_map/ppermute | solution.py:469
  13.2 2.8 %warp.3 = (bf16[2,128,128]{2,1,0:T(8,128)(2,1)S(1)}, bf16[2,128,128]{2,1,0:T(8,128)(2,1)S(1)}, bf16[2,128,128]{2,1,0:T(8,128)(2,1)S(1)}, bf16[2,128,128]{2,1,0:T(8,128)(2,1)S(1)}) custom-call(s32[4]{0:T(128)S(1)} %pad_add_fusion.refs_0_, s32[2,2,32]{2,1,0:T(2,128)S(1)} %copy-done.5, s32[2,2,32]{2,1,0:T(2,128)S(1)} %collective-permute-done.refs_2_, ...), custom_call_target="tpu_custom_call" | custom-call | flops 2147483648 | bytes 4718592 | tf_op jit(solution)/shard_map/warp/pallas_call | solution.py:232
  16.1 0.3 %collective-permute-start.5 = (bf16[8,128,128]{2,1,0:T(8,128)(2,1)S(1)}, bf16[8,128,128]{2,1,0:T(8,128)(2,1)S(1)}, u32[]{:S(2)}, u32[]{:S(2)}) collective-permute-start(bf16[8,128,128]{2,1,0:T(8,128)(2,1)S(1)} %pad_maximum_fusion.refs_9_), channel_id=1, source_target_pairs={{0,4},{4,0},{1,5},{5,1},{2,6},{6,2},{3,7},{7,3},{8,12},{12,8},{9,1... | collective-permute-start | bytes 786440 | tf_op jit(solution)/shard_map/ppermute | solution.py:469
  16.4 3.1 %lag_windows.2 = (f32[4,272,128]{2,1,0:T(8,128)S(1)}, f32[2,640,256]{2,1,0:T(8,128)S(1)}) custom-call(s32[4]{0:T(128)S(1)} %pad_add_fusion.refs_0_, s32[2,2,32]{2,1,0:T(2,128)S(1)} %copy-done.5, s32[2,2,32]{2,1,0:T(2,128)S(1)} %collective-permute-done.refs_2_, bf16[160,128]{1,0:T(8,128)(2,1)S(1)} %copy-done.3, bf16[256,256]{1,0:T(8,128)(2,1)S(1)} %copy-done.1, ...), custom_call_target="tpu_custom_call" | custom-call | flops 3221225472 | bytes 4718592 | tf_op jit(solution)/shard_map/lag_windows/pallas_call | solution.py:448
  19.6 1.0 %collective-permute-done.6 = bf16[8,128,128]{2,1,0:T(8,128)(2,1)S(1)} collective-permute-done((bf16[8,128,128]{2,1,0:T(8,128)(2,1)S(1)}, bf16[8,128,128]{2,1,0:T(8,128)(2,1)S(1)}, u32[]{:S(2)}, u32[]{:S(2)}) %collective-permute-start.6) | collective-permute-done | bytes 262176 | tf_op jit(solution)/shard_map/ppermute | solution.py:469
  20.5 0.1 add_convert_fusion
  20.6 3.9 %collective-permute-start.7 = (bf16[2,128,128]{2,1,0:T(8,128)(2,1)S(1)}, bf16[2,128,128]{2,1,0:T(8,128)(2,1)S(1)}, u32[]{:S(2)}, u32[]{:S(2)}) collective-permute-start(bf16[2,128,128]{2,1,0:T(8,128)(2,1)S(1)} %get-tuple-element.52), channel_id=1, source_target_pairs={{0,24},{8,16},{16,8},{24,0},{1,25},{9,17},{17,9},{25,1},{2,26},{10... | collective-permute-start | bytes 196616 | tf_op jit(solution)/shard_map/ppermute | solution.py:469
  24.5 0.6 %collective-permute-start.9 = (bf16[2,128,128]{2,1,0:T(8,128)(2,1)S(1)}, bf16[2,128,128]{2,1,0:T(8,128)(2,1)S(1)}, u32[]{:S(2)}, u32[]{:S(2)}) collective-permute-start(bf16[2,128,128]{2,1,0:T(8,128)(2,1)S(1)} %get-tuple-element.50), channel_id=1, source_target_pairs={{0,16},{8,24},{16,0},{24,8},{1,17},{9,25},{17,1},{25,9},{2,18},{10... | collective-permute-start | bytes 196616 | tf_op jit(solution)/shard_map/ppermute | solution.py:469
  25.1 0.7 %collective-permute-done.5.refs_9_ = bf16[8,128,128]{2,1,0:T(8,128)(2,1)S(1)} collective-permute-done((bf16[8,128,128]{2,1,0:T(8,128)(2,1)S(1)}, bf16[8,128,128]{2,1,0:T(8,128)(2,1)S(1)}, u32[]{:S(2)}, u32[]{:S(2)}) %collective-permute-start.5) | collective-permute-done | bytes 262176 | tf_op jit(solution)/shard_map/ppermute | solution.py:469
  25.8 2.9 %lag_windows.3 = (f32[2,2,8,256]{3,2,1,0:T(8,128)S(1)}, bf16[2,2,8,256]{3,2,1,0:T(8,128)(2,1)S(1)}) custom-call(s32[4]{0:T(128)S(1)} %pad_add_fusion.refs_0_, s32[2,2,32]{2,1,0:T(2,128)S(1)} %copy-done.5, s32[2,2,32]{2,1,0:T(2,128)S(1)} %collective-permute-done.refs_2_, bf16[160,128]{1,0:T(8,128)(2,1)S(1)} %copy-done.3, bf16[256,256]{1,0:T(8,128)(2,1)S(1)} %copy-done.1, ...), custom_call_target="tpu_custom_call" | custom-call | flops 805306368 | bytes 4718592 | tf_op jit(solution)/shard_map/lag_windows/pallas_call | solution.py:448
  28.7 1.8 %collective-permute-start.10 = (bf16[2,2,8,256]{3,2,1,0:T(8,128)(2,1)S(1)}, bf16[2,2,8,256]{3,2,1,0:T(8,128)(2,1)S(1)}, u32[]{:S(2)}, u32[]{:S(2)}) collective-permute-start(bf16[2,2,8,256]{3,2,1,0:T(8,128)(2,1)S(1)} %get-tuple-element.44), channel_id=1, source_target_pairs={{0,1},{1,0},{2,3},{3,2},{4,5},{5,4},{6,7},{7,6},{8,9},{9,8},{10,11... | collective-permute-start | bytes 49160 | tf_op jit(solution)/shard_map/ppermute | solution.py:469
  30.5 2.0 %collective-permute-done.10 = bf16[2,2,8,256]{3,2,1,0:T(8,128)(2,1)S(1)} collective-permute-done((bf16[2,2,8,256]{3,2,1,0:T(8,128)(2,1)S(1)}, bf16[2,2,8,256]{3,2,1,0:T(8,128)(2,1)S(1)}, u32[]{:S(2)}, u32[]{:S(2)}) %collective-permute-start.10) | collective-permute-done | bytes 16416 | tf_op jit(solution)/shard_map/ppermute | solution.py:469
  32.5 0.1 collective-permute-start.11
  32.6 0.7 %multiply_bitcast_fusion = f32[2,1,128,128]{3,2,1,0:T(8,128)} fusion(bf16[2,128,128]{2,1,0:T(8,128)(2,1)S(1)} %collective-permute-done.9, bf16[2,128,128]{2,1,0:T(8,128)(2,1)S(1)} %collective-permute-done.8, bf16[2,128,128]{2,1,0:T(8,128)(2,1)S(1)} %collective-permute-done.7, bf16[2,128,128]{2,1,0:T(8,128)(2,1)S(1)} %get-tuple-element.36.refs_10_, ...), kind=kLoop, calls=%fused_computation.1 | loop fusion | flops 327680 | bytes 458752
  33.3 0.5 %collective-permute-done.11 = bf16[2,8,256]{2,1,0:T(8,128)(2,1)S(1)} collective-permute-done((bf16[2,8,256]{2,1,0:T(8,128)(2,1)S(1)}, bf16[2,8,256]{2,1,0:T(8,128)(2,1)S(1)}, u32[]{:S(2)}, u32[]{:S(2)}) %collective-permute-start.11) | collective-permute-done | bytes 8224 | tf_op jit(solution)/shard_map/ppermute | solution.py:469
  33.8 0.6 %reshape.16 = f32[2,16,256]{2,1,0:T(8,128)} reshape(f32[2,4,2,2,256]{4,3,2,1,0:T(2,128)S(1)} %copy.19) | data formatting | bytes 65536 | tf_op jit(solution)/shard_map/reshape | solution.py:512
  (29 shorter events, 0.2 us)
Async XLA Ops:
  0.6 7.8 %copy-start = (bf16[2,1,128,128]{3,2,1,0:T(8,128)(2,1)S(1)}, bf16[2,1,128,128]{3,2,1,0:T(8,128)(2,1)}, u32[]{:S(2)}) copy-start(bf16[2,1,128,128]{3,2,1,0:T(8,128)(2,1)} %refs_7_.1) | copy-start | bytes 196612
  0.6 7.8 %copy-start.5 = (s32[2,2,32]{2,1,0:T(2,128)S(1)}, s32[2,2,32]{2,1,0:T(2,128)}, u32[]{:S(2)}) copy-start(s32[2,2,32]{2,1,0:T(2,128)} %refs_1_.8) | copy-start | bytes 1540
  0.7 7.8 %collective-permute-start.1 = (bf16[2,1,512,1024]{3,2,0,1:T(8,128)(2,1)}, bf16[2,1,512,1024]{3,2,0,1:T(8,128)(2,1)S(1)}, u32[]{:S(2)}, u32[]{:S(2)}) collective-permute-start(bf16[2,1,512,1024]{3,2,0,1:T(8,128)(2,1)} %bitcast.36), channel_id=1, source_target_pairs={{0,2},{2,0},{1,3},{3,1},{4,6},{6,4},{5,7},{7,5},{8,10},{10,8},{9,1... | collective-permute-start | bytes 6291464 | tf_op jit(solution)/shard_map/ppermute | solution.py:469
  1.2 14.8 %collective-permute-start.2 = (bf16[2,1,128,128]{3,2,0,1:T(8,128)(2,1)}, bf16[2,1,128,128]{3,2,0,1:T(8,128)(2,1)S(1)}, u32[]{:S(2)}, u32[]{:S(2)}) collective-permute-start(bf16[2,1,128,128]{3,2,0,1:T(8,128)(2,1)} %bitcast.32), channel_id=1, source_target_pairs={{0,8},{8,0},{16,24},{24,16},{1,9},{9,1},{17,25},{25,17},{2,10},{10... | collective-permute-start | bytes 196616 | tf_op jit(solution)/shard_map/ppermute | solution.py:469
  3.8 12.2 %collective-permute-start.3 = (bf16[2,1,128,128]{3,2,0,1:T(8,128)(2,1)}, bf16[2,1,128,128]{3,2,0,1:T(8,128)(2,1)S(1)}, u32[]{:S(2)}, u32[]{:S(2)}) collective-permute-start(bf16[2,1,128,128]{3,2,0,1:T(8,128)(2,1)} %bitcast.33), channel_id=1, source_target_pairs={{0,16},{8,24},{16,0},{24,8},{1,17},{9,25},{17,1},{25,9},{2,18},{10... | collective-permute-start | bytes 196616 | tf_op jit(solution)/shard_map/ppermute | solution.py:469
  6.4 9.6 %collective-permute-start.4 = (bf16[2,1,128,128]{3,2,0,1:T(8,128)(2,1)}, bf16[2,1,128,128]{3,2,0,1:T(8,128)(2,1)S(1)}, u32[]{:S(2)}, u32[]{:S(2)}) collective-permute-start(bf16[2,1,128,128]{3,2,0,1:T(8,128)(2,1)} %bitcast.34), channel_id=1, source_target_pairs={{0,24},{8,16},{16,8},{24,0},{1,25},{9,17},{17,9},{25,1},{2,26},{10... | collective-permute-start | bytes 196616 | tf_op jit(solution)/shard_map/ppermute | solution.py:469
  6.4 2.0 %collective-permute-start = (s32[2,2,32]{2,1,0:T(2,128)}, s32[2,2,32]{2,1,0:T(2,128)S(1)}, u32[]{:S(2)}, u32[]{:S(2)}) collective-permute-start(s32[2,2,32]{2,1,0:T(2,128)} %refs_1_.8), channel_id=1, source_target_pairs={{0,2},{2,0},{1,3},{3,1},{4,6},{6,4},{5,7},{7,5},{8,10},{10,8},{9,1... | collective-permute-start | bytes 1544 | tf_op jit(solution)/shard_map/ppermute | solution.py:469
  11.3 5.1 %copy-start.1 = (bf16[256,256]{1,0:T(8,128)(2,1)S(1)}, bf16[256,256]{1,0:T(8,128)(2,1)}, u32[]{:S(2)}) copy-start(bf16[256,256]{1,0:T(8,128)(2,1)} %constant.35.clone.refs_4_) | copy-start | bytes 393220
  11.3 5.1 %copy-start.2 = (bf16[256,128]{1,0:T(8,128)(2,1)S(1)}, bf16[256,128]{1,0:T(8,128)(2,1)}, u32[]{:S(2)}) copy-start(bf16[256,128]{1,0:T(8,128)(2,1)} %constant.37.clone.refs_6_) | copy-start | bytes 196612
  11.3 5.1 %copy-start.3 = (bf16[160,128]{1,0:T(8,128)(2,1)S(1)}, bf16[160,128]{1,0:T(8,128)(2,1)}, u32[]{:S(2)}) copy-start(bf16[160,128]{1,0:T(8,128)(2,1)} %constant.34.clone.refs_3_) | copy-start | bytes 122884
  11.3 5.1 %copy-start.4 = (bf16[64,160]{1,0:T(8,128)(2,1)S(1)}, bf16[64,160]{1,0:T(8,128)(2,1)}, u32[]{:S(2)}) copy-start(bf16[64,160]{1,0:T(8,128)(2,1)} %constant.36.clone.refs_5_) | copy-start | bytes 61444
  11.4 9.2 %collective-permute-start.6 = (bf16[8,128,128]{2,1,0:T(8,128)(2,1)S(1)}, bf16[8,128,128]{2,1,0:T(8,128)(2,1)S(1)}, u32[]{:S(2)}, u32[]{:S(2)}) collective-permute-start(bf16[8,128,128]{2,1,0:T(8,128)(2,1)S(1)} %warp.2.refs_7_), channel_id=1, source_target_pairs={{0,4},{4,0},{1,5},{5,1},{2,6},{6,2},{3,7},{7,3},{8,12},{12,8},{9,1... | collective-permute-start | bytes 786440 | tf_op jit(solution)/shard_map/ppermute | solution.py:469
  16.1 9.7 %collective-permute-start.5 = (bf16[8,128,128]{2,1,0:T(8,128)(2,1)S(1)}, bf16[8,128,128]{2,1,0:T(8,128)(2,1)S(1)}, u32[]{:S(2)}, u32[]{:S(2)}) collective-permute-start(bf16[8,128,128]{2,1,0:T(8,128)(2,1)S(1)} %pad_maximum_fusion.refs_9_), channel_id=1, source_target_pairs={{0,4},{4,0},{1,5},{5,1},{2,6},{6,2},{3,7},{7,3},{8,12},{12,8},{9,1... | collective-permute-start | bytes 786440 | tf_op jit(solution)/shard_map/ppermute | solution.py:469
  20.6 9.9 %collective-permute-start.7 = (bf16[2,128,128]{2,1,0:T(8,128)(2,1)S(1)}, bf16[2,128,128]{2,1,0:T(8,128)(2,1)S(1)}, u32[]{:S(2)}, u32[]{:S(2)}) collective-permute-start(bf16[2,128,128]{2,1,0:T(8,128)(2,1)S(1)} %get-tuple-element.52), channel_id=1, source_target_pairs={{0,24},{8,16},{16,8},{24,0},{1,25},{9,17},{17,9},{25,1},{2,26},{10... | collective-permute-start | bytes 196616 | tf_op jit(solution)/shard_map/ppermute | solution.py:469
  24.5 6.0 %collective-permute-start.8 = (bf16[2,128,128]{2,1,0:T(8,128)(2,1)S(1)}, bf16[2,128,128]{2,1,0:T(8,128)(2,1)S(1)}, u32[]{:S(2)}, u32[]{:S(2)}) collective-permute-start(bf16[2,128,128]{2,1,0:T(8,128)(2,1)S(1)} %get-tuple-element.51), channel_id=1, source_target_pairs={{0,8},{8,0},{16,24},{24,16},{1,9},{9,1},{17,25},{25,17},{2,10},{10... | collective-permute-start | bytes 196616 | tf_op jit(solution)/shard_map/ppermute | solution.py:469
  24.5 6.0 %collective-permute-start.9 = (bf16[2,128,128]{2,1,0:T(8,128)(2,1)S(1)}, bf16[2,128,128]{2,1,0:T(8,128)(2,1)S(1)}, u32[]{:S(2)}, u32[]{:S(2)}) collective-permute-start(bf16[2,128,128]{2,1,0:T(8,128)(2,1)S(1)} %get-tuple-element.50), channel_id=1, source_target_pairs={{0,16},{8,24},{16,0},{24,8},{1,17},{9,25},{17,1},{25,9},{2,18},{10... | collective-permute-start | bytes 196616 | tf_op jit(solution)/shard_map/ppermute | solution.py:469
  28.7 3.8 %collective-permute-start.10 = (bf16[2,2,8,256]{3,2,1,0:T(8,128)(2,1)S(1)}, bf16[2,2,8,256]{3,2,1,0:T(8,128)(2,1)S(1)}, u32[]{:S(2)}, u32[]{:S(2)}) collective-permute-start(bf16[2,2,8,256]{3,2,1,0:T(8,128)(2,1)S(1)} %get-tuple-element.44), channel_id=1, source_target_pairs={{0,1},{1,0},{2,3},{3,2},{4,5},{5,4},{6,7},{7,6},{8,9},{9,8},{10,11... | collective-permute-start | bytes 49160 | tf_op jit(solution)/shard_map/ppermute | solution.py:469
  32.5 1.2 %collective-permute-start.11 = (bf16[2,8,256]{2,1,0:T(8,128)(2,1)S(1)}, bf16[2,8,256]{2,1,0:T(8,128)(2,1)S(1)}, u32[]{:S(2)}, u32[]{:S(2)}) collective-permute-start(bf16[2,8,256]{2,1,0:T(8,128)(2,1)S(1)} %fusion), channel_id=1, source_target_pairs={{0,2},{2,0},{1,3},{3,1},{4,6},{6,4},{5,7},{7,5},{8,10},{10,8},{9,1... | collective-permute-start | bytes 24584 | tf_op jit(solution)/shard_map/ppermute | solution.py:469
